TPU v7x, 32 devices: a whole 2x2x4 slice. The times are simulated.
32 devices in a mesh: replica: 2 (over x), shard: 8 (over z, y), tensor: 2 (over core).
Axes of the slice: x: 2, y: 2, z: 4, core: 2. Of those that a mesh axis runs over, the one named last changes fastest.
Arguments:
- latent: bfloat16 [8192, 3072], P(('replica', 'shard'), 'tensor'), parts along dimension 0, may hold values from -6 to 6
- row_adapter_index: int32 [8192, 1], P(('replica', 'shard')), parts along dimension 0, may hold values from 0 to 7; in each aligned block of 512 rows (0 to 511, 512 to 1023, ...) at most 128 rows name the same one
- shared_weight: bfloat16 [3072, 3072], P(None, 'tensor'), may hold values from -0.109375 to 0.109375
- adapter_down_weight: bfloat16 [8, 3072, 64], P('shard', 'tensor'), may hold values from -0.109375 to 0.109375
- adapter_up_weight: bfloat16 [8, 64, 3072], P('shard', None, 'tensor'), may hold values from -0.75 to 0.75
Outputs:
- output_rows: bfloat16 [8192, 3072], P(('replica', 'shard'), 'tensor'), parts along dimension 0
There are 2 independent parts, one for each index of `replica`. A program takes and returns all parts, laid end to end along the dimension named above; an argument that names none is the same for every part. Nothing has to cross between parts.
Inputs may be any that keep to these rules, and one draw needn't show every extreme that they name: `row_adapter_index`: among the 512 rows of one request group, no adapter is named by more than 128 rows, a bound that some block reaches.
All inputs are finite; a program needn't handle non-finite values.
Results may differ from a plain program's by a relative error of at most 0.005.
Values may be sent and summed in bfloat16 or wider, within the bound.
No kernel may reach another device: no remote copies, remote signals or barrier semaphores. Data moves between devices by JAX's collectives and lax.ppermute only.
A program may use at most 128 MiB of HBM per device.

v0:
```python
import jax
import jax.numpy as jnp
from jax import lax
from jax.sharding import PartitionSpec as P


def slot_targets(adapter_ids, adapters, capacity):
    onehot = (adapter_ids[:, None] == jnp.arange(adapters, dtype=jnp.int32)[None, :]).astype(
        jnp.int32
    )
    position = jnp.sum((jnp.cumsum(onehot, axis=0) - 1) * onehot, axis=1)
    return adapter_ids * capacity + position


def on_device(latent, row_adapter_index, shared_weight, adapter_down_weight, adapter_up_weight):
    row_count, half_width = latent.shape
    per_request_rows = adapter_down_weight.shape[0]
    owners = lax.axis_size("shard")
    adapters = per_request_rows * owners
    capacity = 2 * row_count // adapters
    adapter_ids = row_adapter_index[:, 0]
    target = slot_targets(adapter_ids, adapters, capacity)
    packed = jnp.zeros((adapters * capacity, half_width), latent.dtype).at[target].set(latent)
    base_part = jnp.dot(
        lax.all_gather(latent, "tensor", axis=1, tiled=True),
        shared_weight,
        preferred_element_type=jnp.float32,
    )
    slot_rows = packed.reshape(adapters, capacity, half_width)
    chosen = slot_rows
    partial_value = jnp.einsum(
        "kmd,kde->kme",
        chosen,
        lax.all_gather(adapter_down_weight, "shard", axis=0, tiled=True),
        preferred_element_type=jnp.float32,
    )
    lowrank = lax.psum(partial_value, "tensor").astype(jnp.bfloat16)
    chosen = lowrank
    corrections = jnp.einsum(
        "kme,kef->kmf",
        chosen,
        lax.all_gather(adapter_up_weight, "shard", axis=0, tiled=True),
        preferred_element_type=jnp.float32,
    ).astype(jnp.bfloat16)
    delta_slots = corrections.reshape(adapters * capacity, half_width)
    delta_rows = jnp.take(delta_slots, target, axis=0)
    return (base_part + delta_rows.astype(jnp.float32)).astype(jnp.bfloat16)


def solution(mesh):
    return jax.shard_map(
        on_device,
        mesh=mesh,
        in_specs=(
            P(("replica", "shard"), "tensor"),
            P(("replica", "shard"), None),
            P(None, "tensor"),
            P("shard", "tensor", None),
            P("shard", None, "tensor"),
        ),
        out_specs=P(("replica", "shard"), "tensor"),
        check_vma=False,
    )
```

profile of v0, /device:TPU:0, one launch (start us, length us, event | category | flops | bytes accessed | tf_op | source)
XLA Modules:
  0.0 131.2 jit_solution(2761258087062121417)
XLA Ops:
  6.5 0.0 all-gather.6.cloned.1.call-start
  6.5 0.7 all-gather.6.cloned.1.call-update
  7.3 0.0 all-gather.8.cloned.1.call-start
  7.3 0.7 all-gather.8.cloned.1.call-update
  8.0 0.0 all-gather.4.cloned.1.call-start
  8.1 0.7 all-gather.4.cloned.1.call-update
  8.7 0.7 fusion.5
  9.4 1.1 reduce-window.6
  10.6 0.2 slice_reduce_fusion
  10.8 0.8 fusion.4
  11.6 0.7 and_reduce_fusion
  12.3 4.9 %scatter_custom_fusion = bf16[1024,1536]{1,0:T(8,128)(2,1)S(1)} fusion(s32[512]{0:T(512)S(1)} %bitcast.22, bf16[512,1536]{1,0:T(8,128)(2,1)} %param.5, bf16[]{:T(256)} %constant.28.clone.1), kind=kCustom, calls=%fused_computation.5 | custom fusion | bytes 3146240 | tf_op jit(solution)/shard_map/scatter | solution.py:23
  17.2 39.2 %all-gather.6.cloned.1.call-done = bf16[8,1536,64]{1,2,0:T(8,128)(2,1)} async-done(((bf16[1,1536,64]{1,2,0:T(8,128)(2,1)}), bf16[8,1536,64]{1,2,0:T(8,128)(2,1)}) %all-gather.6.cloned.1.call-update) | async-done | bytes 1572880 | tf_op jit(solution)/shard_map/all_gather | solution.py:34
  56.5 2.6 %fusion.6 = f32[8,128,64]{1,2,0:T(8,128)S(1)} fusion(bf16[8,128,1536]{2,1,0:T(8,128)(2,1)S(1)} %bitcast.19, bf16[8,1536,64]{1,2,0:T(8,128)(2,1)} %all-gather.6.cloned.1.call-done), kind=kOutput, calls=%fused_computation.17 | convolution fusion | flops 201326592 | bytes 4980736 | tf_op jit(solution)/shard_map/kmd,kde->kme/dot_general | solution.py:31
  59.0 4.2 %all-reduce.1 = bf16[8,128,64]{1,2,0:T(8,128)(2,1)S(1)} all-reduce(f32[8,128,64]{1,2,0:T(8,128)S(1)} %fusion.6), channel_id=1, replica_groups=mesh['replica'=2,'shard'=8,'tensor'=2] {'tensor'}, use_global_device_ids=true, to_apply=%region_4.5 | all-reduce | flops 65536 | bytes 393216 | tf_op jit(solution)/shard_map/psum | solution.py:37
  63.2 38.5 %all-gather.8.cloned.1.call-done = bf16[8,64,1536]{2,1,0:T(8,128)(2,1)} async-done(((bf16[1,64,1536]{2,1,0:T(8,128)(2,1)}), bf16[8,64,1536]{2,1,0:T(8,128)(2,1)}) %all-gather.8.cloned.1.call-update) | async-done | bytes 1572880 | tf_op jit(solution)/shard_map/all_gather | solution.py:42
  101.7 2.4 %convolution_convert_fusion = bf16[8,128,1536]{2,1,0:T(8,128)(2,1)S(1)} fusion(bf16[8,64,1536]{2,1,0:T(8,128)(2,1)} %all-gather.8.cloned.1.call-done, bf16[8,128,64]{1,2,0:T(8,128)(2,1)S(1)} %all-reduce.1), kind=kOutput, calls=%fused_computation.2 | convolution fusion | flops 202899456 | bytes 4849664 | tf_op jit(solution)/shard_map/kme,kef->kmf/dot_general | solution.py:39
  104.1 2.9 %gather_fusion = bf16[512,1536]{1,0:T(8,128)(2,1)} fusion(bf16[1024,1536]{1,0:T(8,128)(2,1)S(1)} %bitcast.18, s32[1024]{0:T(1024)S(1)} %pad_clamp_fusion), kind=kCustom, calls=%fused_computation | custom fusion | bytes 3147776 | tf_op jit(solution)/shard_map/jit(_take)/gather | solution.py:46
  107.0 7.2 %all-gather.4.cloned.1.call-done = bf16[512,3072]{1,0:T(8,128)(2,1)} async-done(((bf16[512,1536]{1,0:T(8,128)(2,1)}), bf16[512,3072]{1,0:T(8,128)(2,1)}) %all-gather.4.cloned.1.call-update) | async-done | bytes 3145744 | tf_op jit(solution)/shard_map/all_gather | solution.py:25
  114.2 10.5 %fusion = bf16[512,1536]{1,0:T(8,128)(2,1)} fusion(bf16[512,3072]{1,0:T(8,128)(2,1)} %all-gather.4.cloned.1.call-done, bf16[3072,1536]{1,0:T(8,128)(2,1)} %param.7, bf16[512,1536]{1,0:T(8,128)(2,1)} %gather_fusion, pred[512]{0:T(512)(128)(4,1)S(1)} %get-tuple-element.5), kind=kOutput, calls=%fused_computation.4 | convolution fusion | flops 4834983936 | bytes 15729152 | tf_op jit(solution)/shard_map/dot_general | solution.py:24
  (3 shorter events, 0.0 us)
Async XLA Ops:
  6.5 49.9 %all-gather.6.cloned.1.call-start = ((), (), s32[]{:S(2)}) async-start(), calls=%async_computation.1 | async-start | bytes 1769472 | tf_op jit(solution)/shard_map/all_gather | solution.py:34
  7.3 94.4 %all-gather.8.cloned.1.call-start = ((), (), s32[]{:S(2)}) async-start(), calls=%async_computation.2 | async-start | bytes 1769472 | tf_op jit(solution)/shard_map/all_gather | solution.py:42
  8.0 106.2 %all-gather.4.cloned.1.call-start = ((), (), s32[]{:S(2)}) async-start(), calls=%async_computation | async-start | bytes 4718592 | tf_op jit(solution)/shard_map/all_gather | solution.py:25
Sparse Core Ops, SparseCore 0:
  9.5 46.8 all-gather.5
  58.6 42.9 all-gather.7
  103.2 10.9 all-gather.3
where the time goes:
time: 132 us; the launch traced here: 131 us
  waiting for transfers between devices  86.9 us (66%)
  matrix products  15.5 us (12%)
  between operations  13.1 us (10%)
  local copies, waits for them, and re-layouts  8.06 us (6%)
  blocking collectives  4.17 us (3%)
  other arithmetic  3.34 us (3%)
    all_gather x1, waiting for transfers between devices, on_device(): lax.all_gather(adapter_down_weight, 'shard', axis=0, tiled=True)  39.2 us
    all_gather x1, waiting for transfers between devices, on_device(): lax.all_gather(adapter_up_weight, 'shard', axis=0, tiled=True)  38.5 us
    dot_general x1, matrix products, on_device(): jnp.dot(lax.all_gather(latent, 'tensor', axis=1, tiled=True), shared_weig...  10.5 us
    all_gather x1, waiting for transfers between devices, on_device(): lax.all_gather(latent, 'tensor', axis=1, tiled=True)  7.15 us
    scatter x1, local copies, waits for them, and re-layouts, on_device(): jnp.zeros((adapters * capacity, half_width), latent.dtype).at[target]  4.9 us
    psum x1, blocking collectives, on_device(): lowrank = lax.psum(partial_value, 'tensor').astype(jnp.bfloat16)  4.17 us
    gather x1, local copies, waits for them, and re-layouts, on_device(): delta_rows = jnp.take(delta_slots, target, axis=0)  2.94 us
  transfers between devices with their start and end apart: 3, of which 3 were waited for; matrix products, arithmetic and copies ran while one was open for 12% of the time, Pallas kernels for 0%

commit v1 on v0

v1 whole, which is shorter than its diff:
```python
import jax
import jax.numpy as jnp
from jax import lax
from jax.experimental import pallas as pl
from jax.experimental.pallas import tpu as pltpu
from jax.sharding import PartitionSpec as P

VMEM_BYTES = 60 * 1024 * 1024
CHUNK = 512


def swap(value, axis):
    return lax.ppermute(value, axis, [(0, 1), (1, 0)])


def neighbour(value, shards):
    return lax.ppermute(value, "shard", [(i, i ^ 1) for i in range(shards)])


def along_line(value, shards, step):
    return lax.ppermute(value, "shard", [(i, (i + 2 * step) % shards) for i in range(shards)])


def routed_gather(block, shards, replica):
    half = block.shape[0] // 2
    own_half = lax.dynamic_slice_in_dim(block, replica * half, half, axis=0)
    pieces = [block, neighbour(block, shards)]
    arrived = [along_line(own_half, shards, step) for step in range(1, shards // 2)]
    for piece in arrived:
        beside = neighbour(piece, shards)
        pieces += [piece, swap(piece, "replica"), beside, swap(beside, "replica")]
    return pieces


def routed_owners(shards, index):
    owners = [index, index ^ 1]
    for step in range(1, shards // 2):
        source = (index - 2 * step) % shards
        owners += [source, source ^ 1]
    return jnp.stack(owners)


def stack_pieces(info, pieces, stack):
    offset = 0
    half = pieces[0].shape[0] // 2
    for number, piece in enumerate(pieces):
        rows = piece.shape[0]
        if number < 2 and len(pieces) > 2:
            first = pl.multiple_of(info[0] * half, half)
            second = pl.multiple_of((1 - info[0]) * half, half)
            stack[offset : offset + half, :] = piece[pl.ds(first, half), :]
            stack[offset + half : offset + rows, :] = piece[pl.ds(second, half), :]
        else:
            stack[offset : offset + rows, :] = piece[...]
        offset += rows


def down_kernel(info, ids, owners, latent, *refs):
    pieces, out, stack = refs[:-2], refs[-2], refs[-1]
    stack_pieces(info, pieces, stack)
    total = jnp.zeros(out.shape, jnp.float32)
    width = out.shape[1]
    for begin in range(0, stack.shape[0], CHUNK):
        part = lax.dot_general(
            latent[...],
            stack[begin : begin + CHUNK, :],
            (((1,), (1,)), ((), ())),
            preferred_element_type=jnp.float32,
        )
        part = jnp.where(ids[...] == owners[:, begin : begin + CHUNK], part, 0.0)
        for lane in range(0, CHUNK, width):
            total += part[:, lane : lane + width]
    out[...] = total


def base_kernel(info, own, other, own_weight, other_weight, out):
    out[...] = jnp.dot(
        own[...], own_weight[...], preferred_element_type=jnp.float32
    ) + jnp.dot(other[...], other_weight[...], preferred_element_type=jnp.float32)


def up_kernel(info, ids, owners, mine, theirs, base, *refs):
    pieces, out, stack = refs[:-2], refs[-2], refs[-1]
    stack_pieces(info, pieces, stack)
    lowrank = (mine[...] + theirs[...]).astype(jnp.bfloat16).astype(jnp.float32)
    delta = jnp.zeros(out.shape, jnp.float32)
    for begin in range(0, stack.shape[0], CHUNK):
        wide = jnp.concatenate([lowrank] * (CHUNK // lowrank.shape[1]), axis=1)
        wide = jnp.where(ids[...] == owners[:, begin : begin + CHUNK], wide, 0.0)
        delta += jnp.dot(
            wide.astype(jnp.bfloat16),
            stack[begin : begin + CHUNK, :],
            preferred_element_type=jnp.float32,
        )
    out[...] = (base[...] + delta.astype(jnp.bfloat16).astype(jnp.float32)).astype(out.dtype)


def on_device(latent, row_adapter_index, shared_weight, adapter_down_weight, adapter_up_weight):
    rows, half_width = latent.shape
    out_width = shared_weight.shape[1]
    local_adapters, _, rank = adapter_down_weight.shape
    shards = lax.axis_size("shard")
    adapters = shards * local_adapters
    replica, index = lax.axis_index("replica"), lax.axis_index("shard")
    core = lax.axis_index("tensor")
    info = jnp.stack([replica, core]).astype(jnp.int32)

    down = jnp.swapaxes(adapter_down_weight, 1, 2).reshape(local_adapters * rank, half_width)
    up = adapter_up_weight.reshape(local_adapters * rank, out_width)
    if shards == 8 and local_adapters == 1 and lax.axis_size("replica") == 2:
        down_pieces = routed_gather(down, shards, replica)
        up_pieces = routed_gather(up, shards, replica)
        owner_ids = routed_owners(shards, index)
    else:
        down_pieces = [lax.all_gather(down, "shard", axis=0, tiled=True)]
        up_pieces = [lax.all_gather(up, "shard", axis=0, tiled=True)]
        owner_ids = jnp.arange(adapters)
    owners = jnp.repeat(owner_ids.astype(jnp.int32), rank)[None, :]
    other = swap(latent, "tensor")

    smem = pl.BlockSpec(memory_space=pltpu.SMEM)
    vmem = pl.BlockSpec(memory_space=pltpu.VMEM)
    params = pltpu.CompilerParams(vmem_limit_bytes=VMEM_BYTES)
    columns = adapters * rank
    mine = pl.pallas_call(
        down_kernel,
        out_shape=jax.ShapeDtypeStruct((rows, 2 * rank), jnp.float32),
        in_specs=[smem] + [vmem] * (3 + len(down_pieces)),
        out_specs=vmem,
        scratch_shapes=[pltpu.VMEM((columns, half_width), jnp.bfloat16)],
        compiler_params=params,
        cost_estimate=pl.CostEstimate(
            flops=2 * rows * columns * half_width,
            bytes_accessed=2 * (rows + columns) * half_width,
            transcendentals=0,
        ),
    )(info, row_adapter_index, owners, latent, *down_pieces)
    theirs = swap(mine, "tensor")

    tile = 512
    base = pl.pallas_call(
        base_kernel,
        out_shape=jax.ShapeDtypeStruct((rows, out_width), jnp.float32),
        grid_spec=pltpu.PrefetchScalarGridSpec(
            num_scalar_prefetch=1,
            grid=(out_width // tile,),
            in_specs=[
                pl.BlockSpec((rows, half_width), lambda j, info: (0, 0)),
                pl.BlockSpec((rows, half_width), lambda j, info: (0, 0)),
                pl.BlockSpec((half_width, tile), lambda j, info: (info[1], j)),
                pl.BlockSpec((half_width, tile), lambda j, info: (1 - info[1], j)),
            ],
            out_specs=pl.BlockSpec((rows, tile), lambda j, info: (0, j)),
        ),
        compiler_params=params,
        cost_estimate=pl.CostEstimate(
            flops=4 * rows * half_width * out_width,
            bytes_accessed=4 * half_width * (rows + out_width) + 4 * rows * out_width,
            transcendentals=0,
        ),
    )(info, latent, other, shared_weight, shared_weight)

    return pl.pallas_call(
        up_kernel,
        out_shape=jax.ShapeDtypeStruct((rows, out_width), jnp.bfloat16),
        in_specs=[smem] + [vmem] * (5 + len(up_pieces)),
        out_specs=vmem,
        scratch_shapes=[pltpu.VMEM((columns, out_width), jnp.bfloat16)],
        compiler_params=params,
        cost_estimate=pl.CostEstimate(
            flops=2 * rows * columns * out_width,
            bytes_accessed=6 * rows * out_width + 2 * columns * out_width,
            transcendentals=0,
        ),
    )(info, row_adapter_index, owners, mine, theirs, base, *up_pieces)


def solution(mesh):
    return jax.shard_map(
        on_device,
        mesh=mesh,
        in_specs=(
            P(("replica", "shard"), "tensor"),
            P(("replica", "shard"), None),
            P(None, "tensor"),
            P("shard", "tensor", None),
            P("shard", None, "tensor"),
        ),
        out_specs=P(("replica", "shard"), "tensor"),
        check_vma=False,
    )
```

time: 132 us -> 76 us (0.58)
  waiting for transfers between devices: 86.9 us -> 13.1 us
  starting transfers between devices: 0.08 us -> 35.9 us
  Pallas kernels: 0 us -> 19 us
  matrix products: 15.5 us -> 0 us
  between operations: 13.1 us -> 0.27 us
  blocking collectives: 4.17 us -> 0 us
  other arithmetic: 3.34 us -> 0.65 us
    all_gather x3 -> x0, waiting for transfers between devices: 84.8 us -> none  [the longest x1 39.2 us: on_device(): lax.all_gather(adapter_down_weight, 'shard', axis=0, tiled=True)]
    ppermute x0 -> x28, starting transfers between devices: none -> 35.9 us  [the longest x14 15.3 us: swap(): return lax.ppermute(value, axis, [(0, 1), (1, 0)])]
    pallas_call x0 -> x3, Pallas kernels: none -> 19 us  [the longest x1 10.4 us: on_device(): pl.pallas_call(base_kernel, out_shape=jax.ShapeDtypeStruct((rows, out_wid...]
    dot_general x3 -> x0, matrix products: 15.5 us -> none  [the longest x1 10.5 us: on_device(): jnp.dot(lax.all_gather(latent, 'tensor', axis=1, tiled=True), shared_weig...]
    ppermute x0 -> x28, waiting for transfers between devices: none -> 13.1 us  [the longest x6 9.32 us: along_line(): lax.ppermute(value, 'shard', [(i, (i + 2 * step) % shards) for i in range...]
    scatter x1 -> x0, local copies, waits for them, and re-layouts: 4.9 us -> none  [on_device(): jnp.zeros((adapters * capacity, half_width), latent.dtype).at[target]]
    unnamed x0 -> x53, local copies, waits for them, and re-layouts: none -> 4.18 us
    psum x1 -> x0, blocking collectives: 4.17 us -> none  [on_device(): lowrank = lax.psum(partial_value, 'tensor').astype(jnp.bfloat16)]
  transfers between devices with their start and end apart: 3 -> 28, of which waited for: 3 -> 7; matrix products, arithmetic and copies ran while one was open for 12% -> 6% of each run, Pallas kernels for 0% -> 19%
where the time goes in v1:
time: 76 us; the launch traced here: 75.7 us
  starting transfers between devices  35.9 us (47%)
  Pallas kernels  19 us (25%)
  waiting for transfers between devices  13.1 us (17%)
  local copies, waits for them, and re-layouts  6.8 us (9%)
    ppermute x14, starting transfers between devices, swap(): return lax.ppermute(value, axis, [(0, 1), (1, 0)])  15.3 us
    ppermute x8, starting transfers between devices, neighbour(): return lax.ppermute(value, 'shard', [(i, i ^ 1) for i in range(shards)])  11.1 us
    pallas_call x1, Pallas kernels, on_device(): pl.pallas_call(base_kernel, out_shape=jax.ShapeDtypeStruct((rows, out_wid...  10.4 us
    ppermute x6, starting transfers between devices, along_line(): lax.ppermute(value, 'shard', [(i, (i + 2 * step) % shards) for i in range...  9.55 us
    ppermute x6, waiting for transfers between devices, along_line(): lax.ppermute(value, 'shard', [(i, (i + 2 * step) % shards) for i in range...  9.32 us
    pallas_call x1, Pallas kernels, on_device(): pl.pallas_call(up_kernel, out_shape=jax.ShapeDtypeStruct((rows, out_width...  4.78 us
    unnamed x53, local copies, waits for them, and re-layouts  4.18 us
    pallas_call x1, Pallas kernels, on_device(): pl.pallas_call(down_kernel, out_shape=jax.ShapeDtypeStruct((rows, 2 * ran...  3.78 us
  transfers between devices with their start and end apart: 28, of which 7 were waited for; matrix products, arithmetic and copies ran while one was open for 6% of the time, Pallas kernels for 19%

profile of v1, /device:TPU:0, one launch (start us, length us, event | category | flops | bytes accessed | tf_op | source)
XLA Modules:
  0.0 75.7 jit_solution(2764480005361252488)
XLA Ops:
  0.0 0.5 collective-permute-start.14
  0.5 0.9 %dynamic-slice_bitcast_fusion = bf16[32,1536]{1,0:T(8,128)(2,1)S(1)} fusion(bf16[1,64,1536]{2,1,0:T(8,128)(2,1)} %param.9, s32[]{:T(128)S(6)} %select_n.22), kind=kLoop, calls=%fused_computation | loop fusion | bytes 196612 | tf_op jit(solution)/shard_map/dynamic_slice | solution.py:26
  1.4 4.6 %collective-permute-start.24 = (bf16[32,1536]{1,0:T(8,128)(2,1)S(1)}, bf16[32,1536]{1,0:T(8,128)(2,1)S(1)}, u32[]{:S(2)}, u32[]{:S(2)}) collective-permute-start(bf16[32,1536]{1,0:T(8,128)(2,1)S(1)} %dynamic-slice_bitcast_fusion), channel_id=1, source_target_pairs={{0,12},{2,14},{4,0},{6,2},{8,4},{10,6},{12,8},{14,10},{1,13},{3,15... | collective-permute-start | bytes 294920 | tf_op jit(solution)/shard_map/ppermute | solution.py:21
  6.0 1.0 %collective-permute-start.16 = (bf16[32,1536]{1,0:T(8,128)(2,1)S(1)}, bf16[32,1536]{1,0:T(8,128)(2,1)S(1)}, u32[]{:S(2)}, u32[]{:S(2)}) collective-permute-start(bf16[32,1536]{1,0:T(8,128)(2,1)S(1)} %dynamic-slice_bitcast_fusion), channel_id=1, source_target_pairs={{0,4},{2,6},{4,8},{6,10},{8,12},{10,14},{12,0},{14,2},{1,5},{3,7},... | collective-permute-start | bytes 294920 | tf_op jit(solution)/shard_map/ppermute | solution.py:21
  7.0 0.9 %dynamic-slice_bitcast_fusion.1 = bf16[32,1536]{1,0:T(8,128)(2,1)S(1)} fusion(bf16[1,1536,64]{1,2,0:T(8,128)(2,1)} %param.8, s32[]{:T(128)S(6)} %select_n.22), kind=kLoop, calls=%fused_computation.1 | loop fusion | bytes 196612 | tf_op jit(solution)/shard_map/dynamic_slice | solution.py:26
  7.9 2.8 %collective-permute-start.9 = (bf16[32,1536]{1,0:T(8,128)(2,1)S(1)}, bf16[32,1536]{1,0:T(8,128)(2,1)S(1)}, u32[]{:S(2)}, u32[]{:S(2)}) collective-permute-start(bf16[32,1536]{1,0:T(8,128)(2,1)S(1)} %dynamic-slice_bitcast_fusion.1), channel_id=1, source_target_pairs={{0,12},{2,14},{4,0},{6,2},{8,4},{10,6},{12,8},{14,10},{1,13},{3,15... | collective-permute-start | bytes 294920 | tf_op jit(solution)/shard_map/ppermute | solution.py:21
  10.7 1.1 %collective-permute-start.5 = (bf16[32,1536]{1,0:T(8,128)(2,1)S(1)}, bf16[32,1536]{1,0:T(8,128)(2,1)S(1)}, u32[]{:S(2)}, u32[]{:S(2)}) collective-permute-start(bf16[32,1536]{1,0:T(8,128)(2,1)S(1)} %dynamic-slice_bitcast_fusion.1), channel_id=1, source_target_pairs={{0,8},{2,10},{4,12},{6,14},{8,0},{10,2},{12,4},{14,6},{1,9},{3,11}... | collective-permute-start | bytes 294920 | tf_op jit(solution)/shard_map/ppermute | solution.py:21
  11.8 4.6 %collective-permute-done.20.refs_6_ = bf16[32,1536]{1,0:T(8,128)(2,1)S(1)} collective-permute-done((bf16[32,1536]{1,0:T(8,128)(2,1)S(1)}, bf16[32,1536]{1,0:T(8,128)(2,1)S(1)}, u32[]{:S(2)}, u32[]{:S(2)}) %collective-permute-start.20) | collective-permute-done | bytes 98336 | tf_op jit(solution)/shard_map/ppermute | solution.py:21
  16.5 1.6 %collective-permute-start.26 = (bf16[32,1536]{1,0:T(8,128)(2,1)S(1)}, bf16[32,1536]{1,0:T(8,128)(2,1)S(1)}, u32[]{:S(2)}, u32[]{:S(2)}) collective-permute-start(bf16[32,1536]{1,0:T(8,128)(2,1)S(1)} %collective-permute-done.24.refs_10_), channel_id=1, source_target_pairs={{0,2},{2,0},{4,6},{6,4},{8,10},{10,8},{12,14},{14,12},{1,3},{3,1},... | collective-permute-start | bytes 294920 | tf_op jit(solution)/shard_map/ppermute | solution.py:17
  18.1 1.5 %collective-permute-start.25 = (bf16[32,1536]{1,0:T(8,128)(2,1)S(1)}, bf16[32,1536]{1,0:T(8,128)(2,1)S(1)}, u32[]{:S(2)}, u32[]{:S(2)}) collective-permute-start(bf16[32,1536]{1,0:T(8,128)(2,1)S(1)} %collective-permute-done.24.refs_10_), channel_id=1, source_target_pairs={{0,16},{16,0},{1,17},{17,1},{2,18},{18,2},{3,19},{19,3},{4,20},{20... | collective-permute-start | bytes 294920 | tf_op jit(solution)/shard_map/ppermute | solution.py:13
  19.5 4.7 %collective-permute-done.5.refs_6_ = bf16[32,1536]{1,0:T(8,128)(2,1)S(1)} collective-permute-done((bf16[32,1536]{1,0:T(8,128)(2,1)S(1)}, bf16[32,1536]{1,0:T(8,128)(2,1)S(1)}, u32[]{:S(2)}, u32[]{:S(2)}) %collective-permute-start.5) | collective-permute-done | bytes 98336 | tf_op jit(solution)/shard_map/ppermute | solution.py:21
  24.2 1.5 %collective-permute-start.11 = (bf16[32,1536]{1,0:T(8,128)(2,1)S(1)}, bf16[32,1536]{1,0:T(8,128)(2,1)S(1)}, u32[]{:S(2)}, u32[]{:S(2)}) collective-permute-start(bf16[32,1536]{1,0:T(8,128)(2,1)S(1)} %collective-permute-done.9.refs_10_), channel_id=1, source_target_pairs={{0,2},{2,0},{4,6},{6,4},{8,10},{10,8},{12,14},{14,12},{1,3},{3,1},... | collective-permute-start | bytes 294920 | tf_op jit(solution)/shard_map/ppermute | solution.py:17
  25.8 1.5 %collective-permute-start.10 = (bf16[32,1536]{1,0:T(8,128)(2,1)S(1)}, bf16[32,1536]{1,0:T(8,128)(2,1)S(1)}, u32[]{:S(2)}, u32[]{:S(2)}) collective-permute-start(bf16[32,1536]{1,0:T(8,128)(2,1)S(1)} %collective-permute-done.9.refs_10_), channel_id=1, source_target_pairs={{0,16},{16,0},{1,17},{17,1},{2,18},{18,2},{3,19},{19,3},{4,20},{20... | collective-permute-start | bytes 294920 | tf_op jit(solution)/shard_map/ppermute | solution.py:13
  27.3 0.5 collective-permute-start.7
  27.8 1.5 %collective-permute-start = (bf16[64,1536]{1,0:T(8,128)(2,1)}, bf16[64,1536]{1,0:T(8,128)(2,1)S(1)}, u32[]{:S(2)}, u32[]{:S(2)}) collective-permute-start(bf16[64,1536]{1,0:T(8,128)(2,1)} %bitcast.20), channel_id=1, source_target_pairs={{0,2},{2,0},{4,6},{6,4},{8,10},{10,8},{12,14},{14,12},{1,3},{3,1},... | collective-permute-start | bytes 589832 | tf_op jit(solution)/shard_map/ppermute | solution.py:17
  29.3 1.8 %collective-permute-start.6 = (bf16[32,1536]{1,0:T(8,128)(2,1)S(1)}, bf16[32,1536]{1,0:T(8,128)(2,1)S(1)}, u32[]{:S(2)}, u32[]{:S(2)}) collective-permute-start(bf16[32,1536]{1,0:T(8,128)(2,1)S(1)} %collective-permute-done.5.refs_6_), channel_id=1, source_target_pairs={{0,16},{16,0},{1,17},{17,1},{2,18},{18,2},{3,19},{19,3},{4,20},{20... | collective-permute-start | bytes 294920 | tf_op jit(solution)/shard_map/ppermute | solution.py:13
  31.1 1.9 %collective-permute-start.3 = (bf16[32,1536]{1,0:T(8,128)(2,1)S(1)}, bf16[32,1536]{1,0:T(8,128)(2,1)S(1)}, u32[]{:S(2)}, u32[]{:S(2)}) collective-permute-start(bf16[32,1536]{1,0:T(8,128)(2,1)S(1)} %collective-permute-done.1.refs_2_), channel_id=1, source_target_pairs={{0,2},{2,0},{4,6},{6,4},{8,10},{10,8},{12,14},{14,12},{1,3},{3,1},... | collective-permute-start | bytes 294920 | tf_op jit(solution)/shard_map/ppermute | solution.py:17
  32.9 0.1 collective-permute-done.7.refs_8_
  33.0 0.5 collective-permute-start.2
  33.5 1.4 %collective-permute-done.6.refs_7_ = bf16[32,1536]{1,0:T(8,128)(2,1)S(1)} collective-permute-done((bf16[32,1536]{1,0:T(8,128)(2,1)S(1)}, bf16[32,1536]{1,0:T(8,128)(2,1)S(1)}, u32[]{:S(2)}, u32[]{:S(2)}) %collective-permute-start.6) | collective-permute-done | bytes 98336 | tf_op jit(solution)/shard_map/ppermute | solution.py:13
  34.9 1.8 %collective-permute-start.12 = (bf16[32,1536]{1,0:T(8,128)(2,1)S(1)}, bf16[32,1536]{1,0:T(8,128)(2,1)}, u32[]{:S(2)}, u32[]{:S(2)}) collective-permute-start(bf16[32,1536]{1,0:T(8,128)(2,1)S(1)} %collective-permute-done.11.refs_12_), channel_id=1, source_target_pairs={{0,16},{16,0},{1,17},{17,1},{2,18},{18,2},{3,19},{19,3},{4,20},{20... | collective-permute-start | bytes 294920 | tf_op jit(solution)/shard_map/ppermute | solution.py:13
  36.7 0.9 %collective-permute-done.3.refs_4_ = bf16[32,1536]{1,0:T(8,128)(2,1)S(1)} collective-permute-done((bf16[32,1536]{1,0:T(8,128)(2,1)S(1)}, bf16[32,1536]{1,0:T(8,128)(2,1)S(1)}, u32[]{:S(2)}, u32[]{:S(2)}) %collective-permute-start.3) | collective-permute-done | bytes 98336 | tf_op jit(solution)/shard_map/ppermute | solution.py:17
  37.6 1.2 %collective-permute-start.8 = (bf16[32,1536]{1,0:T(8,128)(2,1)S(1)}, bf16[32,1536]{1,0:T(8,128)(2,1)}, u32[]{:S(2)}, u32[]{:S(2)}) collective-permute-start(bf16[32,1536]{1,0:T(8,128)(2,1)S(1)} %collective-permute-done.7.refs_8_), channel_id=1, source_target_pairs={{0,16},{16,0},{1,17},{17,1},{2,18},{18,2},{3,19},{19,3},{4,20},{20... | collective-permute-start | bytes 294920 | tf_op jit(solution)/shard_map/ppermute | solution.py:13
  38.8 0.8 %collective-permute-start.4 = (bf16[32,1536]{1,0:T(8,128)(2,1)S(1)}, bf16[32,1536]{1,0:T(8,128)(2,1)}, u32[]{:S(2)}, u32[]{:S(2)}) collective-permute-start(bf16[32,1536]{1,0:T(8,128)(2,1)S(1)} %collective-permute-done.3.refs_4_), channel_id=1, source_target_pairs={{0,16},{16,0},{1,17},{17,1},{2,18},{18,2},{3,19},{19,3},{4,20},{20... | collective-permute-start | bytes 294920 | tf_op jit(solution)/shard_map/ppermute | solution.py:13
  39.6 1.2 %collective-permute-start.22 = (bf16[32,1536]{1,0:T(8,128)(2,1)S(1)}, bf16[32,1536]{1,0:T(8,128)(2,1)S(1)}, u32[]{:S(2)}, u32[]{:S(2)}) collective-permute-start(bf16[32,1536]{1,0:T(8,128)(2,1)S(1)} %collective-permute-done.20.refs_6_), channel_id=1, source_target_pairs={{0,2},{2,0},{4,6},{6,4},{8,10},{10,8},{12,14},{14,12},{1,3},{3,1},... | collective-permute-start | bytes 294920 | tf_op jit(solution)/shard_map/ppermute | solution.py:17
  40.8 1.5 %collective-permute-start.21 = (bf16[32,1536]{1,0:T(8,128)(2,1)S(1)}, bf16[32,1536]{1,0:T(8,128)(2,1)S(1)}, u32[]{:S(2)}, u32[]{:S(2)}) collective-permute-start(bf16[32,1536]{1,0:T(8,128)(2,1)S(1)} %collective-permute-done.20.refs_6_), channel_id=1, source_target_pairs={{0,16},{16,0},{1,17},{17,1},{2,18},{18,2},{3,19},{19,3},{4,20},{20... | collective-permute-start | bytes 294920 | tf_op jit(solution)/shard_map/ppermute | solution.py:13
  42.3 1.1 %collective-permute-done.8.refs_9_ = bf16[32,1536]{1,0:T(8,128)(2,1)} collective-permute-done((bf16[32,1536]{1,0:T(8,128)(2,1)S(1)}, bf16[32,1536]{1,0:T(8,128)(2,1)}, u32[]{:S(2)}, u32[]{:S(2)}) %collective-permute-start.8) | collective-permute-done | bytes 98336 | tf_op jit(solution)/shard_map/ppermute | solution.py:13
  43.4 1.2 %collective-permute-start.18 = (bf16[32,1536]{1,0:T(8,128)(2,1)S(1)}, bf16[32,1536]{1,0:T(8,128)(2,1)S(1)}, u32[]{:S(2)}, u32[]{:S(2)}) collective-permute-start(bf16[32,1536]{1,0:T(8,128)(2,1)S(1)} %collective-permute-done.16.refs_2_), channel_id=1, source_target_pairs={{0,2},{2,0},{4,6},{6,4},{8,10},{10,8},{12,14},{14,12},{1,3},{3,1},... | collective-permute-start | bytes 294920 | tf_op jit(solution)/shard_map/ppermute | solution.py:17
  44.6 0.3 collective-permute-done.4.refs_5_
  44.9 1.8 %collective-permute-start.17 = (bf16[32,1536]{1,0:T(8,128)(2,1)S(1)}, bf16[32,1536]{1,0:T(8,128)(2,1)S(1)}, u32[]{:S(2)}, u32[]{:S(2)}) collective-permute-start(bf16[32,1536]{1,0:T(8,128)(2,1)S(1)} %collective-permute-done.16.refs_2_), channel_id=1, source_target_pairs={{0,16},{16,0},{1,17},{17,1},{2,18},{18,2},{3,19},{19,3},{4,20},{20... | collective-permute-start | bytes 294920 | tf_op jit(solution)/shard_map/ppermute | solution.py:13
  46.7 0.7 pad_add_fusion.info
  47.3 0.1 stack.47
  47.4 0.1 broadcast_in_dim.3
  47.5 0.7 broadcast_in_dim_reshape.3.owners
  48.1 1.5 %copy.7.ids = s32[512,1]{1,0:T(8,128)} copy(s32[512,1]{0,1:T(1,128)} %param.6) | data formatting | bytes 4096 | tf_op args[1]
  49.8 3.8 %shard_map.55.mine = f32[512,128]{1,0:T(8,128)} custom-call(s32[2]{0:T(128)} %pad_add_fusion.info, s32[512,1]{1,0:T(8,128)} %copy.7.ids, s32[1,512]{1,0:T(1,128)} %broadcast_in_dim_reshape.3.owners, bf16[512,1536]{1,0:T(8,128)(2,1)} %own.1, bf16[64,1536]{1,0:T(8,128)(2,1)} %bitcast.21, bf16[64,1536]{1,0:T(8,128)(2,1)} %copy-done.3, ...), custom_call_target="tpu_custom_call" | custom-call | flops 805306368 | bytes 3145728 | tf_op jit(solution)/shard_map/pallas_call | solution.py:125
  53.6 1.6 %collective-permute-start.15 = (bf16[64,1536]{1,0:T(8,128)(2,1)S(1)}, bf16[64,1536]{1,0:T(8,128)(2,1)S(1)}, u32[]{:S(2)}, u32[]{:S(2)}) collective-permute-start(bf16[64,1536]{1,0:T(8,128)(2,1)S(1)} %bitcast.23), channel_id=1, source_target_pairs={{0,2},{2,0},{4,6},{6,4},{8,10},{10,8},{12,14},{14,12},{1,3},{3,1},... | collective-permute-start | bytes 589832 | tf_op jit(solution)/shard_map/ppermute | solution.py:17
  55.2 0.5 collective-permute-start.27
  55.8 1.5 %collective-permute-start.23 = (bf16[32,1536]{1,0:T(8,128)(2,1)S(1)}, bf16[32,1536]{1,0:T(8,128)(2,1)S(1)}, u32[]{:S(2)}, u32[]{:S(2)}) collective-permute-start(bf16[32,1536]{1,0:T(8,128)(2,1)S(1)} %collective-permute-done.22.refs_8_), channel_id=1, source_target_pairs={{0,16},{16,0},{1,17},{17,1},{2,18},{18,2},{3,19},{19,3},{4,20},{20... | collective-permute-start | bytes 294920 | tf_op jit(solution)/shard_map/ppermute | solution.py:13
  57.3 0.5 collective-permute-start.19
  57.8 1.1 %copy-done = bf16[512,1536]{1,0:T(8,128)(2,1)} copy-done((bf16[512,1536]{1,0:T(8,128)(2,1)}, bf16[512,1536]{1,0:T(8,128)(2,1)S(1)}, u32[]{:S(2)}) %copy-start) | copy-done | bytes 1572888
  58.9 10.4 %shard_map.56.base = f32[512,1536]{1,0:T(8,128)} custom-call(s32[2]{0:T(128)} %pad_add_fusion.info, bf16[512,1536]{1,0:T(8,128)(2,1)} %own.1, bf16[512,1536]{1,0:T(8,128)(2,1)} %copy-done, bf16[3072,1536]{1,0:T(8,128)(2,1)} %other_weight.1, bf16[3072,1536]{1,0:T(8,128)(2,1)} %other_weight.1), custom_call_target="tpu_custom_call" | custom-call | flops 4831838208 | bytes 15728640 | tf_op jit(solution)/shard_map/pallas_call | solution.py:141
  69.5 0.6 copy-done.4
  70.1 0.0 copy-done.23
  70.2 0.0 copy-done.24
  70.2 0.0 copy-done.25
  70.2 0.7 copy-done.2
  71.0 4.8 %shard_map.57 = bf16[512,1536]{1,0:T(8,128)(2,1)} custom-call(s32[2]{0:T(128)} %pad_add_fusion.info, s32[512,1]{1,0:T(8,128)} %copy.7.ids, s32[1,512]{1,0:T(1,128)} %broadcast_in_dim_reshape.3.owners, f32[512,128]{1,0:T(8,128)} %shard_map.55.mine, f32[512,128]{1,0:T(8,128)} %copy-done.2, f32[512,1536]{1,0:T(8,128)} %shard_map.56.base, ...), custom_call_target="tpu_custom_call" | custom-call | flops 805306368 | bytes 6291456 | tf_op jit(solution)/shard_map/pallas_call | solution.py:163
  (70 shorter events, 0.2 us)
Async XLA Ops:
  0.0 57.8 %collective-permute-start.14 = (bf16[512,1536]{1,0:T(8,128)(2,1)}, bf16[512,1536]{1,0:T(8,128)(2,1)S(1)}, u32[]{:S(2)}, u32[]{:S(2)}) collective-permute-start(bf16[512,1536]{1,0:T(8,128)(2,1)} %own.1), channel_id=1, source_target_pairs={{0,1},{1,0},{2,3},{3,2},{4,5},{5,4},{6,7},{7,6},{8,9},{9,8},{10,11... | collective-permute-start | bytes 4718600 | tf_op jit(solution)/shard_map/ppermute | solution.py:13
  1.4 9.3 %collective-permute-start.24 = (bf16[32,1536]{1,0:T(8,128)(2,1)S(1)}, bf16[32,1536]{1,0:T(8,128)(2,1)S(1)}, u32[]{:S(2)}, u32[]{:S(2)}) collective-permute-start(bf16[32,1536]{1,0:T(8,128)(2,1)S(1)} %dynamic-slice_bitcast_fusion), channel_id=1, source_target_pairs={{0,12},{2,14},{4,0},{6,2},{8,4},{10,6},{12,8},{14,10},{1,13},{3,15... | collective-permute-start | bytes 294920 | tf_op jit(solution)/shard_map/ppermute | solution.py:21
  6.0 10.5 %collective-permute-start.20 = (bf16[32,1536]{1,0:T(8,128)(2,1)S(1)}, bf16[32,1536]{1,0:T(8,128)(2,1)S(1)}, u32[]{:S(2)}, u32[]{:S(2)}) collective-permute-start(bf16[32,1536]{1,0:T(8,128)(2,1)S(1)} %dynamic-slice_bitcast_fusion), channel_id=1, source_target_pairs={{0,8},{2,10},{4,12},{6,14},{8,0},{10,2},{12,4},{14,6},{1,9},{3,11}... | collective-permute-start | bytes 294920 | tf_op jit(solution)/shard_map/ppermute | solution.py:21
  6.0 10.5 %collective-permute-start.16 = (bf16[32,1536]{1,0:T(8,128)(2,1)S(1)}, bf16[32,1536]{1,0:T(8,128)(2,1)S(1)}, u32[]{:S(2)}, u32[]{:S(2)}) collective-permute-start(bf16[32,1536]{1,0:T(8,128)(2,1)S(1)} %dynamic-slice_bitcast_fusion), channel_id=1, source_target_pairs={{0,4},{2,6},{4,8},{6,10},{8,12},{10,14},{12,0},{14,2},{1,5},{3,7},... | collective-permute-start | bytes 294920 | tf_op jit(solution)/shard_map/ppermute | solution.py:21
  7.9 10.2 %collective-permute-start.9 = (bf16[32,1536]{1,0:T(8,128)(2,1)S(1)}, bf16[32,1536]{1,0:T(8,128)(2,1)S(1)}, u32[]{:S(2)}, u32[]{:S(2)}) collective-permute-start(bf16[32,1536]{1,0:T(8,128)(2,1)S(1)} %dynamic-slice_bitcast_fusion.1), channel_id=1, source_target_pairs={{0,12},{2,14},{4,0},{6,2},{8,4},{10,6},{12,8},{14,10},{1,13},{3,15... | collective-permute-start | bytes 294920 | tf_op jit(solution)/shard_map/ppermute | solution.py:21
  10.7 42.9 %copy-start.5 = (bf16[32,1536]{1,0:T(8,128)(2,1)}, bf16[32,1536]{1,0:T(8,128)(2,1)S(1)}, u32[]{:S(2)}) copy-start(bf16[32,1536]{1,0:T(8,128)(2,1)S(1)} %collective-permute-done.24.refs_10_) | copy-start | bytes 294916
  10.7 13.5 %collective-permute-start.5 = (bf16[32,1536]{1,0:T(8,128)(2,1)S(1)}, bf16[32,1536]{1,0:T(8,128)(2,1)S(1)}, u32[]{:S(2)}, u32[]{:S(2)}) collective-permute-start(bf16[32,1536]{1,0:T(8,128)(2,1)S(1)} %dynamic-slice_bitcast_fusion.1), channel_id=1, source_target_pairs={{0,8},{2,10},{4,12},{6,14},{8,0},{10,2},{12,4},{14,6},{1,9},{3,11}... | collective-permute-start | bytes 294920 | tf_op jit(solution)/shard_map/ppermute | solution.py:21
  16.4 52.9 %copy-start.6 = (bf16[32,1536]{1,0:T(8,128)(2,1)}, bf16[32,1536]{1,0:T(8,128)(2,1)S(1)}, u32[]{:S(2)}) copy-start(bf16[32,1536]{1,0:T(8,128)(2,1)S(1)} %collective-permute-done.20.refs_6_) | copy-start | bytes 294916
  16.4 9.3 %collective-permute-start.1 = (bf16[32,1536]{1,0:T(8,128)(2,1)S(1)}, bf16[32,1536]{1,0:T(8,128)(2,1)S(1)}, u32[]{:S(2)}, u32[]{:S(2)}) collective-permute-start(bf16[32,1536]{1,0:T(8,128)(2,1)S(1)} %dynamic-slice_bitcast_fusion.1), channel_id=1, source_target_pairs={{0,4},{2,6},{4,8},{6,10},{8,12},{10,14},{12,0},{14,2},{1,5},{3,7},... | collective-permute-start | bytes 294920 | tf_op jit(solution)/shard_map/ppermute | solution.py:21
  16.4 52.9 %copy-start.7 = (bf16[32,1536]{1,0:T(8,128)(2,1)}, bf16[32,1536]{1,0:T(8,128)(2,1)S(1)}, u32[]{:S(2)}) copy-start(bf16[32,1536]{1,0:T(8,128)(2,1)S(1)} %collective-permute-done.16.refs_2_) | copy-start | bytes 294916
  16.5 10.8 %collective-permute-start.26 = (bf16[32,1536]{1,0:T(8,128)(2,1)S(1)}, bf16[32,1536]{1,0:T(8,128)(2,1)S(1)}, u32[]{:S(2)}, u32[]{:S(2)}) collective-permute-start(bf16[32,1536]{1,0:T(8,128)(2,1)S(1)} %collective-permute-done.24.refs_10_), channel_id=1, source_target_pairs={{0,2},{2,0},{4,6},{6,4},{8,10},{10,8},{12,14},{14,12},{1,3},{3,1},... | collective-permute-start | bytes 294920 | tf_op jit(solution)/shard_map/ppermute | solution.py:17
  18.0 31.6 %copy-start.10 = (bf16[32,1536]{1,0:T(8,128)(2,1)}, bf16[32,1536]{1,0:T(8,128)(2,1)S(1)}, u32[]{:S(2)}) copy-start(bf16[32,1536]{1,0:T(8,128)(2,1)S(1)} %collective-permute-done.9.refs_10_) | copy-start | bytes 294916
  18.1 9.7 %collective-permute-start.25 = (bf16[32,1536]{1,0:T(8,128)(2,1)S(1)}, bf16[32,1536]{1,0:T(8,128)(2,1)S(1)}, u32[]{:S(2)}, u32[]{:S(2)}) collective-permute-start(bf16[32,1536]{1,0:T(8,128)(2,1)S(1)} %collective-permute-done.24.refs_10_), channel_id=1, source_target_pairs={{0,16},{16,0},{1,17},{17,1},{2,18},{18,2},{3,19},{19,3},{4,20},{20... | collective-permute-start | bytes 294920 | tf_op jit(solution)/shard_map/ppermute | solution.py:13
  24.2 25.4 %copy-start.11 = (bf16[32,1536]{1,0:T(8,128)(2,1)}, bf16[32,1536]{1,0:T(8,128)(2,1)S(1)}, u32[]{:S(2)}) copy-start(bf16[32,1536]{1,0:T(8,128)(2,1)S(1)} %collective-permute-done.5.refs_6_) | copy-start | bytes 294916
  24.2 5.1 %collective-permute-start.11 = (bf16[32,1536]{1,0:T(8,128)(2,1)S(1)}, bf16[32,1536]{1,0:T(8,128)(2,1)S(1)}, u32[]{:S(2)}, u32[]{:S(2)}) collective-permute-start(bf16[32,1536]{1,0:T(8,128)(2,1)S(1)} %collective-permute-done.9.refs_10_), channel_id=1, source_target_pairs={{0,2},{2,0},{4,6},{6,4},{8,10},{10,8},{12,14},{14,12},{1,3},{3,1},... | collective-permute-start | bytes 294920 | tf_op jit(solution)/shard_map/ppermute | solution.py:17
  25.8 23.9 %copy-start.12 = (bf16[32,1536]{1,0:T(8,128)(2,1)}, bf16[32,1536]{1,0:T(8,128)(2,1)S(1)}, u32[]{:S(2)}) copy-start(bf16[32,1536]{1,0:T(8,128)(2,1)S(1)} %collective-permute-done.1.refs_2_) | copy-start | bytes 294916
  25.8 5.3 %collective-permute-start.10 = (bf16[32,1536]{1,0:T(8,128)(2,1)S(1)}, bf16[32,1536]{1,0:T(8,128)(2,1)S(1)}, u32[]{:S(2)}, u32[]{:S(2)}) collective-permute-start(bf16[32,1536]{1,0:T(8,128)(2,1)S(1)} %collective-permute-done.9.refs_10_), channel_id=1, source_target_pairs={{0,16},{16,0},{1,17},{17,1},{2,18},{18,2},{3,19},{19,3},{4,20},{20... | collective-permute-start | bytes 294920 | tf_op jit(solution)/shard_map/ppermute | solution.py:13
  27.3 42.1 %copy-start.8 = (bf16[32,1536]{1,0:T(8,128)(2,1)}, bf16[32,1536]{1,0:T(8,128)(2,1)S(1)}, u32[]{:S(2)}) copy-start(bf16[32,1536]{1,0:T(8,128)(2,1)S(1)} %collective-permute-done.26.refs_12_) | copy-start | bytes 294916
  27.3 5.7 %collective-permute-start.7 = (bf16[32,1536]{1,0:T(8,128)(2,1)S(1)}, bf16[32,1536]{1,0:T(8,128)(2,1)S(1)}, u32[]{:S(2)}, u32[]{:S(2)}) collective-permute-start(bf16[32,1536]{1,0:T(8,128)(2,1)S(1)} %collective-permute-done.5.refs_6_), channel_id=1, source_target_pairs={{0,2},{2,0},{4,6},{6,4},{8,10},{10,8},{12,14},{14,12},{1,3},{3,1},... | collective-permute-start | bytes 294920 | tf_op jit(solution)/shard_map/ppermute | solution.py:17
  27.8 41.6 %copy-start.9 = (bf16[32,1536]{1,0:T(8,128)(2,1)}, bf16[32,1536]{1,0:T(8,128)(2,1)S(1)}, u32[]{:S(2)}) copy-start(bf16[32,1536]{1,0:T(8,128)(2,1)S(1)} %collective-permute-done.25.refs_11_) | copy-start | bytes 294916
  27.8 11.9 %collective-permute-start = (bf16[64,1536]{1,0:T(8,128)(2,1)}, bf16[64,1536]{1,0:T(8,128)(2,1)S(1)}, u32[]{:S(2)}, u32[]{:S(2)}) collective-permute-start(bf16[64,1536]{1,0:T(8,128)(2,1)} %bitcast.20), channel_id=1, source_target_pairs={{0,2},{2,0},{4,6},{6,4},{8,10},{10,8},{12,14},{14,12},{1,3},{3,1},... | collective-permute-start | bytes 589832 | tf_op jit(solution)/shard_map/ppermute | solution.py:17
  29.3 20.4 %copy-start.13 = (bf16[32,1536]{1,0:T(8,128)(2,1)}, bf16[32,1536]{1,0:T(8,128)(2,1)S(1)}, u32[]{:S(2)}) copy-start(bf16[32,1536]{1,0:T(8,128)(2,1)S(1)} %collective-permute-done.11.refs_12_) | copy-start | bytes 294916
  29.3 5.6 %collective-permute-start.6 = (bf16[32,1536]{1,0:T(8,128)(2,1)S(1)}, bf16[32,1536]{1,0:T(8,128)(2,1)S(1)}, u32[]{:S(2)}, u32[]{:S(2)}) collective-permute-start(bf16[32,1536]{1,0:T(8,128)(2,1)S(1)} %collective-permute-done.5.refs_6_), channel_id=1, source_target_pairs={{0,16},{16,0},{1,17},{17,1},{2,18},{18,2},{3,19},{19,3},{4,20},{20... | collective-permute-start | bytes 294920 | tf_op jit(solution)/shard_map/ppermute | solution.py:13
  31.1 18.6 %copy-start.15 = (bf16[32,1536]{1,0:T(8,128)(2,1)}, bf16[32,1536]{1,0:T(8,128)(2,1)S(1)}, u32[]{:S(2)}) copy-start(bf16[32,1536]{1,0:T(8,128)(2,1)S(1)} %collective-permute-done.10.refs_11_) | copy-start | bytes 294916
  31.1 6.5 %collective-permute-start.3 = (bf16[32,1536]{1,0:T(8,128)(2,1)S(1)}, bf16[32,1536]{1,0:T(8,128)(2,1)S(1)}, u32[]{:S(2)}, u32[]{:S(2)}) collective-permute-start(bf16[32,1536]{1,0:T(8,128)(2,1)S(1)} %collective-permute-done.1.refs_2_), channel_id=1, source_target_pairs={{0,2},{2,0},{4,6},{6,4},{8,10},{10,8},{12,14},{14,12},{1,3},{3,1},... | collective-permute-start | bytes 294920 | tf_op jit(solution)/shard_map/ppermute | solution.py:17
  33.0 16.7 %copy-start.17 = (bf16[32,1536]{1,0:T(8,128)(2,1)}, bf16[32,1536]{1,0:T(8,128)(2,1)S(1)}, u32[]{:S(2)}) copy-start(bf16[32,1536]{1,0:T(8,128)(2,1)S(1)} %collective-permute-done.7.refs_8_) | copy-start | bytes 294916
  33.0 5.8 %collective-permute-start.2 = (bf16[32,1536]{1,0:T(8,128)(2,1)S(1)}, bf16[32,1536]{1,0:T(8,128)(2,1)S(1)}, u32[]{:S(2)}, u32[]{:S(2)}) collective-permute-start(bf16[32,1536]{1,0:T(8,128)(2,1)S(1)} %collective-permute-done.1.refs_2_), channel_id=1, source_target_pairs={{0,16},{16,0},{1,17},{17,1},{2,18},{18,2},{3,19},{19,3},{4,20},{20... | collective-permute-start | bytes 294920 | tf_op jit(solution)/shard_map/ppermute | solution.py:13
  34.9 14.8 %copy-start.20 = (bf16[32,1536]{1,0:T(8,128)(2,1)}, bf16[32,1536]{1,0:T(8,128)(2,1)S(1)}, u32[]{:S(2)}) copy-start(bf16[32,1536]{1,0:T(8,128)(2,1)S(1)} %collective-permute-done.6.refs_7_) | copy-start | bytes 294916
  34.9 5.9 %collective-permute-start.12 = (bf16[32,1536]{1,0:T(8,128)(2,1)S(1)}, bf16[32,1536]{1,0:T(8,128)(2,1)}, u32[]{:S(2)}, u32[]{:S(2)}) collective-permute-start(bf16[32,1536]{1,0:T(8,128)(2,1)S(1)} %collective-permute-done.11.refs_12_), channel_id=1, source_target_pairs={{0,16},{16,0},{1,17},{17,1},{2,18},{18,2},{3,19},{19,3},{4,20},{20... | collective-permute-start | bytes 294920 | tf_op jit(solution)/shard_map/ppermute | solution.py:13
  37.6 12.1 %copy-start.21 = (bf16[32,1536]{1,0:T(8,128)(2,1)}, bf16[32,1536]{1,0:T(8,128)(2,1)S(1)}, u32[]{:S(2)}) copy-start(bf16[32,1536]{1,0:T(8,128)(2,1)S(1)} %collective-permute-done.3.refs_4_) | copy-start | bytes 294916
  37.6 5.8 %collective-permute-start.8 = (bf16[32,1536]{1,0:T(8,128)(2,1)S(1)}, bf16[32,1536]{1,0:T(8,128)(2,1)}, u32[]{:S(2)}, u32[]{:S(2)}) collective-permute-start(bf16[32,1536]{1,0:T(8,128)(2,1)S(1)} %collective-permute-done.7.refs_8_), channel_id=1, source_target_pairs={{0,16},{16,0},{1,17},{17,1},{2,18},{18,2},{3,19},{19,3},{4,20},{20... | collective-permute-start | bytes 294920 | tf_op jit(solution)/shard_map/ppermute | solution.py:13
  38.8 11.0 %copy-start.22 = (bf16[32,1536]{1,0:T(8,128)(2,1)}, bf16[32,1536]{1,0:T(8,128)(2,1)S(1)}, u32[]{:S(2)}) copy-start(bf16[32,1536]{1,0:T(8,128)(2,1)S(1)} %collective-permute-done.2.refs_3_) | copy-start | bytes 294916
  38.8 6.1 %collective-permute-start.4 = (bf16[32,1536]{1,0:T(8,128)(2,1)S(1)}, bf16[32,1536]{1,0:T(8,128)(2,1)}, u32[]{:S(2)}, u32[]{:S(2)}) collective-permute-start(bf16[32,1536]{1,0:T(8,128)(2,1)S(1)} %collective-permute-done.3.refs_4_), channel_id=1, source_target_pairs={{0,16},{16,0},{1,17},{17,1},{2,18},{18,2},{3,19},{19,3},{4,20},{20... | collective-permute-start | bytes 294920 | tf_op jit(solution)/shard_map/ppermute | solution.py:13
  39.6 10.1 %copy-start.3 = (bf16[64,1536]{1,0:T(8,128)(2,1)}, bf16[64,1536]{1,0:T(8,128)(2,1)S(1)}, u32[]{:S(2)}) copy-start(bf16[64,1536]{1,0:T(8,128)(2,1)S(1)} %collective-permute-done.refs_1_) | copy-start | bytes 589828
  39.6 13.9 %collective-permute-start.22 = (bf16[32,1536]{1,0:T(8,128)(2,1)S(1)}, bf16[32,1536]{1,0:T(8,128)(2,1)S(1)}, u32[]{:S(2)}, u32[]{:S(2)}) collective-permute-start(bf16[32,1536]{1,0:T(8,128)(2,1)S(1)} %collective-permute-done.20.refs_6_), channel_id=1, source_target_pairs={{0,2},{2,0},{4,6},{6,4},{8,10},{10,8},{12,14},{14,12},{1,3},{3,1},... | collective-permute-start | bytes 294920 | tf_op jit(solution)/shard_map/ppermute | solution.py:17
  40.8 14.4 %collective-permute-start.21 = (bf16[32,1536]{1,0:T(8,128)(2,1)S(1)}, bf16[32,1536]{1,0:T(8,128)(2,1)S(1)}, u32[]{:S(2)}, u32[]{:S(2)}) collective-permute-start(bf16[32,1536]{1,0:T(8,128)(2,1)S(1)} %collective-permute-done.20.refs_6_), channel_id=1, source_target_pairs={{0,16},{16,0},{1,17},{17,1},{2,18},{18,2},{3,19},{19,3},{4,20},{20... | collective-permute-start | bytes 294920 | tf_op jit(solution)/shard_map/ppermute | solution.py:13
  43.4 12.3 %collective-permute-start.18 = (bf16[32,1536]{1,0:T(8,128)(2,1)S(1)}, bf16[32,1536]{1,0:T(8,128)(2,1)S(1)}, u32[]{:S(2)}, u32[]{:S(2)}) collective-permute-start(bf16[32,1536]{1,0:T(8,128)(2,1)S(1)} %collective-permute-done.16.refs_2_), channel_id=1, source_target_pairs={{0,2},{2,0},{4,6},{6,4},{8,10},{10,8},{12,14},{14,12},{1,3},{3,1},... | collective-permute-start | bytes 294920 | tf_op jit(solution)/shard_map/ppermute | solution.py:17
  44.9 12.3 %collective-permute-start.17 = (bf16[32,1536]{1,0:T(8,128)(2,1)S(1)}, bf16[32,1536]{1,0:T(8,128)(2,1)S(1)}, u32[]{:S(2)}, u32[]{:S(2)}) collective-permute-start(bf16[32,1536]{1,0:T(8,128)(2,1)S(1)} %collective-permute-done.16.refs_2_), channel_id=1, source_target_pairs={{0,16},{16,0},{1,17},{17,1},{2,18},{18,2},{3,19},{19,3},{4,20},{20... | collective-permute-start | bytes 294920 | tf_op jit(solution)/shard_map/ppermute | solution.py:13
  49.8 3.8 %copy-start.1 = (bf16[1,64,1536]{2,1,0:T(8,128)(2,1)S(1)}, bf16[1,64,1536]{2,1,0:T(8,128)(2,1)}, u32[]{:S(2)}) copy-start(bf16[1,64,1536]{2,1,0:T(8,128)(2,1)} %param.9) | copy-start | bytes 589828
  53.6 15.8 %copy-start.14 = (bf16[32,1536]{1,0:T(8,128)(2,1)}, bf16[32,1536]{1,0:T(8,128)(2,1)S(1)}, u32[]{:S(2)}) copy-start(bf16[32,1536]{1,0:T(8,128)(2,1)S(1)} %collective-permute-done.22.refs_8_) | copy-start | bytes 294916
  53.6 15.9 %collective-permute-start.15 = (bf16[64,1536]{1,0:T(8,128)(2,1)S(1)}, bf16[64,1536]{1,0:T(8,128)(2,1)S(1)}, u32[]{:S(2)}, u32[]{:S(2)}) collective-permute-start(bf16[64,1536]{1,0:T(8,128)(2,1)S(1)} %bitcast.23), channel_id=1, source_target_pairs={{0,2},{2,0},{4,6},{6,4},{8,10},{10,8},{12,14},{14,12},{1,3},{3,1},... | collective-permute-start | bytes 589832 | tf_op jit(solution)/shard_map/ppermute | solution.py:17
  55.2 14.2 %copy-start.16 = (bf16[32,1536]{1,0:T(8,128)(2,1)}, bf16[32,1536]{1,0:T(8,128)(2,1)S(1)}, u32[]{:S(2)}) copy-start(bf16[32,1536]{1,0:T(8,128)(2,1)S(1)} %collective-permute-done.21.refs_7_) | copy-start | bytes 294916
  55.2 14.2 %collective-permute-start.27 = (bf16[32,1536]{1,0:T(8,128)(2,1)S(1)}, bf16[32,1536]{1,0:T(8,128)(2,1)S(1)}, u32[]{:S(2)}, u32[]{:S(2)}) collective-permute-start(bf16[32,1536]{1,0:T(8,128)(2,1)S(1)} %collective-permute-done.26.refs_12_), channel_id=1, source_target_pairs={{0,16},{16,0},{1,17},{17,1},{2,18},{18,2},{3,19},{19,3},{4,20},{20... | collective-permute-start | bytes 294920 | tf_op jit(solution)/shard_map/ppermute | solution.py:13
  55.8 13.7 %copy-start.18 = (bf16[32,1536]{1,0:T(8,128)(2,1)}, bf16[32,1536]{1,0:T(8,128)(2,1)S(1)}, u32[]{:S(2)}) copy-start(bf16[32,1536]{1,0:T(8,128)(2,1)S(1)} %collective-permute-done.18.refs_4_) | copy-start | bytes 294916
  55.8 13.7 %collective-permute-start.23 = (bf16[32,1536]{1,0:T(8,128)(2,1)S(1)}, bf16[32,1536]{1,0:T(8,128)(2,1)S(1)}, u32[]{:S(2)}, u32[]{:S(2)}) collective-permute-start(bf16[32,1536]{1,0:T(8,128)(2,1)S(1)} %collective-permute-done.22.refs_8_), channel_id=1, source_target_pairs={{0,16},{16,0},{1,17},{17,1},{2,18},{18,2},{3,19},{19,3},{4,20},{20... | collective-permute-start | bytes 294920 | tf_op jit(solution)/shard_map/ppermute | solution.py:13
  57.3 12.2 %copy-start.19 = (bf16[32,1536]{1,0:T(8,128)(2,1)}, bf16[32,1536]{1,0:T(8,128)(2,1)S(1)}, u32[]{:S(2)}) copy-start(bf16[32,1536]{1,0:T(8,128)(2,1)S(1)} %collective-permute-done.17.refs_3_) | copy-start | bytes 294916
  57.3 12.2 %collective-permute-start.19 = (bf16[32,1536]{1,0:T(8,128)(2,1)S(1)}, bf16[32,1536]{1,0:T(8,128)(2,1)S(1)}, u32[]{:S(2)}, u32[]{:S(2)}) collective-permute-start(bf16[32,1536]{1,0:T(8,128)(2,1)S(1)} %collective-permute-done.18.refs_4_), channel_id=1, source_target_pairs={{0,16},{16,0},{1,17},{17,1},{2,18},{18,2},{3,19},{19,3},{4,20},{20... | collective-permute-start | bytes 294920 | tf_op jit(solution)/shard_map/ppermute | solution.py:13
  57.8 11.7 %collective-permute-start.13 = (f32[512,128]{1,0:T(8,128)}, f32[512,128]{1,0:T(8,128)S(1)}, u32[]{:S(2)}, u32[]{:S(2)}) collective-permute-start(f32[512,128]{1,0:T(8,128)} %shard_map.55.mine), channel_id=1, source_target_pairs={{0,1},{1,0},{2,3},{3,2},{4,5},{5,4},{6,7},{7,6},{8,9},{9,8},{10,11... | collective-permute-start | bytes 786440 | tf_op jit(solution)/shard_map/ppermute | solution.py:13
  (6 other events, 4.7 us)

commit v2 on v0

v2 whole, which is shorter than its diff:
```python
import jax
import jax.numpy as jnp
from jax import lax
from jax.experimental import pallas as pl
from jax.experimental.pallas import tpu as pltpu
from jax.sharding import PartitionSpec as P

MIB = 1024 * 1024
CHUNK = 512
AXES = ("replica", "shard", "tensor")
SMEM = pl.BlockSpec(memory_space=pltpu.SMEM)
VMEM = pl.BlockSpec(memory_space=pltpu.VMEM)
ANY = pl.BlockSpec(memory_space=pl.ANY)


def swap(value, axis):
    return lax.ppermute(value, axis, [(0, 1), (1, 0)])


def along_line(value, shards, step):
    return lax.ppermute(value, "shard", [(i, (i + 2 * step) % shards) for i in range(shards)])


def in_plane(value, shards, first):
    pairs = []
    for r in range(2):
        for s in range(shards):
            for t in range(2):
                to_r, to_s = (r, s ^ 1) if (t == 0) == first else (r ^ 1, s)
                pairs.append(((r * shards + s) * 2 + t, (to_r * shards + to_s) * 2 + t))
    return lax.ppermute(value, AXES, pairs)


def call(kernel, out_shape, in_specs, limit, scratch=(), flops=0, moved=0):
    return pl.pallas_call(
        kernel,
        out_shape=out_shape,
        in_specs=in_specs,
        out_specs=jax.tree.map(lambda _: VMEM, out_shape),
        scratch_shapes=list(scratch),
        compiler_params=pltpu.CompilerParams(vmem_limit_bytes=limit * MIB),
        cost_estimate=pl.CostEstimate(flops=flops, bytes_accessed=moved, transcendentals=0),
    )


def halves_kernel(info, down, up, down_half, up_half, both):
    rank = down.shape[0]
    half = rank // 2
    first = pl.multiple_of(info[0] * half, half)
    down_half[...] = down[pl.ds(first, half), :]
    up_half[...] = up[pl.ds(first, half), :]
    both[:rank, :] = down[...]
    both[rank:, :] = up[...]


def pack_kernel(*refs):
    *pieces, _, out = refs
    rows = pieces[0].shape[0]
    for number, piece in enumerate(pieces):
        out[number * rows : (number + 1) * rows, :] = piece[...]


def stack_routed(info, own, beside, line, first, second, corner, stack):
    rank = own.shape[0]
    half = rank // 2
    mine = pl.multiple_of(info[0] * half, half)
    rest = pl.multiple_of((1 - info[0]) * half, half)
    stack[0:half, :] = own[pl.ds(mine, half), :]
    stack[half : 2 * half, :] = beside[pl.ds(mine, half), :]
    stack[2 * half : 3 * half, :] = own[pl.ds(rest, half), :]
    stack[3 * half : 4 * half, :] = beside[pl.ds(rest, half), :]
    for step in range(line.shape[0] // half):
        rows = slice(step * half, (step + 1) * half)
        base = (step + 1) * 2 * rank
        stack[base : base + half, :] = line[rows, :]
        stack[pl.ds(pl.multiple_of(base + (1 + info[1]) * half, half), half), :] = first[rows, :]
        stack[pl.ds(pl.multiple_of(base + (2 - info[1]) * half, half), half), :] = second[rows, :]
        stack[base + 3 * half : base + 4 * half, :] = corner[rows, :]


def routed_owners(shards, index, rank):
    sources = [(index - 2 * step) % shards for step in range(shards // 2)]
    owners = jnp.stack([jnp.stack([s, s ^ 1, s, s ^ 1]) for s in sources])
    return jnp.repeat(owners.reshape(-1).astype(jnp.int32), rank // 2)[None, :]


def fill_stack(info, refs, stack, which):
    if len(refs) == 1:
        stack[...] = refs[0][...]
    else:
        own, beside, *others = refs
        rank = own.shape[0]
        stack_routed(info, own, beside.at[which * rank : (which + 1) * rank], *others, stack)


def down_kernel(info, ids, owners, latent, *refs):
    *pieces, _, out, stack = refs
    fill_stack(info, pieces, stack, 0)
    total = jnp.zeros(out.shape, jnp.float32)
    width = out.shape[1]
    for begin in range(0, stack.shape[0], CHUNK):
        part = lax.dot_general(
            latent[...],
            stack[begin : begin + CHUNK, :],
            (((1,), (1,)), ((), ())),
            preferred_element_type=jnp.float32,
        )
        part = jnp.where(ids[...] == owners[:, begin : begin + CHUNK], part, 0.0)
        for lane in range(0, CHUNK, width):
            total += part[:, lane : lane + width]
    out[...] = total


def base_kernel(info, own, other, own_weight, other_weight, _, out, token):
    token[...] = jnp.zeros_like(token)
    out[...] = jnp.dot(
        own[...], own_weight[...], preferred_element_type=jnp.float32
    ) + jnp.dot(other[...], other_weight[...], preferred_element_type=jnp.float32)


def base_half(info, latent, other, weight, after, number):
    rows, half_width = latent.shape
    columns = weight.shape[1] // 2
    tile = columns // 3
    skip = number * (columns // tile)
    return pl.pallas_call(
        base_kernel,
        out_shape=[
            jax.ShapeDtypeStruct((rows, columns), jnp.float32),
            jax.ShapeDtypeStruct((8, 128), jnp.float32),
        ],
        grid_spec=pltpu.PrefetchScalarGridSpec(
            num_scalar_prefetch=1,
            grid=(columns // tile,),
            in_specs=[
                pl.BlockSpec((rows, half_width), lambda j, info: (0, 0)),
                pl.BlockSpec((rows, half_width), lambda j, info: (0, 0)),
                pl.BlockSpec((half_width, tile), lambda j, info: (info[1], j + skip)),
                pl.BlockSpec((half_width, tile), lambda j, info: (1 - info[1], j + skip)),
                ANY,
            ],
            out_specs=[
                pl.BlockSpec((rows, tile), lambda j, info: (0, j)),
                pl.BlockSpec((8, 128), lambda j, info: (0, 0)),
            ],
        ),
        compiler_params=pltpu.CompilerParams(vmem_limit_bytes=54 * MIB),
        cost_estimate=pl.CostEstimate(
            flops=0,
            bytes_accessed=0,
            transcendentals=0,
        ),
    )(info, latent, other, weight, weight, after)


def up_kernel(info, ids, owners, mine, theirs, left, right, *refs):
    *pieces, out, stack = refs
    fill_stack(info, pieces, stack, 1)
    lowrank = (mine[...] + theirs[...]).astype(jnp.bfloat16).astype(jnp.float32)
    repeated = jnp.concatenate([lowrank] * (CHUNK // lowrank.shape[1]), axis=1)
    columns = left.shape[1]
    for number, base in enumerate((left, right)):
        place = slice(number * columns, (number + 1) * columns)
        delta = jnp.zeros(base.shape, jnp.float32)
        for begin in range(0, stack.shape[0], CHUNK):
            wide = jnp.where(ids[...] == owners[:, begin : begin + CHUNK], repeated, 0.0)
            delta += jnp.dot(
                wide.astype(jnp.bfloat16),
                stack[begin : begin + CHUNK, place],
                preferred_element_type=jnp.float32,
            )
        total = base[...] + delta.astype(jnp.bfloat16).astype(jnp.float32)
        out[:, place] = total.astype(out.dtype)


def on_device(latent, row_adapter_index, shared_weight, adapter_down_weight, adapter_up_weight):
    rows, half_width = latent.shape
    out_width = shared_weight.shape[1]
    local_adapters, _, rank = adapter_down_weight.shape
    shards = lax.axis_size("shard")
    adapters = shards * local_adapters
    columns = adapters * rank
    index = lax.axis_index("shard")
    info = jnp.stack([lax.axis_index("replica"), lax.axis_index("tensor")]).astype(jnp.int32)

    other = swap(latent, "tensor")
    down = jnp.swapaxes(adapter_down_weight, 1, 2).reshape(local_adapters * rank, half_width)
    up = adapter_up_weight.reshape(local_adapters * rank, out_width)
    routed = shards == 8 and local_adapters == 1 and lax.axis_size("replica") == 2
    if routed:
        half = rank // 2
        reach = shards // 2 - 1
        piece = jax.ShapeDtypeStruct((half, half_width), latent.dtype)
        packed = jax.ShapeDtypeStruct((reach * half, half_width), latent.dtype)
        down_half, up_half, both = call(
            halves_kernel,
            [piece, piece, jax.ShapeDtypeStruct((2 * rank, half_width), latent.dtype)],
            [SMEM, VMEM, VMEM],
            4,
        )(info, down, up)
        down_line = [along_line(down_half, shards, step) for step in range(1, reach + 1)]
        up_line = [along_line(up_half, shards, step) for step in range(1, reach + 1)]
        beside = lax.ppermute(both, "shard", [(i, i ^ 1) for i in range(shards)])
        left, left_token = base_half(info, latent, other, shared_weight, down_half, 0)
        pack = call(pack_kernel, packed, [VMEM] * reach + [ANY], 4)
        down_packed = pack(*down_line, left_token)
        down_first = in_plane(down_packed, shards, True)
        down_second = in_plane(down_packed, shards, False)
        right, right_token = base_half(info, latent, other, shared_weight, down_packed, 1)
        down_corner = in_plane(down_first, shards, False)
        up_packed = pack(*up_line, right_token)
        up_first = in_plane(up_packed, shards, True)
        up_second = in_plane(up_packed, shards, False)
        down_pieces = [down, beside, down_packed, down_first, down_second, down_corner]
        owners = routed_owners(shards, index, rank)
        after = up_packed
    else:
        down_pieces = [lax.all_gather(down, "shard", axis=0, tiled=True)]
        up_pieces = [lax.all_gather(up, "shard", axis=0, tiled=True)]
        left, left_token = base_half(info, latent, other, shared_weight, latent, 0)
        right, right_token = base_half(info, latent, other, shared_weight, latent, 1)
        owners = jnp.repeat(jnp.arange(adapters, dtype=jnp.int32), rank)[None, :]
        after = left

    mine = call(
        down_kernel,
        jax.ShapeDtypeStruct((rows, 2 * rank), jnp.float32),
        [SMEM] + [VMEM] * (3 + len(down_pieces)) + [ANY],
        16 if routed else 56,
        [pltpu.VMEM((columns, half_width), jnp.bfloat16)],
        2 * rows * columns * half_width,
        2 * (rows + columns) * half_width,
    )(info, row_adapter_index, owners, latent, *down_pieces, after)
    theirs = swap(mine, "tensor")
    if routed:
        up_corner = in_plane(up_first, shards, False)
        up_pieces = [up, beside, up_packed, up_first, up_second, up_corner]

    return call(
        up_kernel,
        jax.ShapeDtypeStruct((rows, out_width), jnp.bfloat16),
        [SMEM] + [VMEM] * (6 + len(up_pieces)),
        24 if routed else 56,
        [pltpu.VMEM((columns, out_width), jnp.bfloat16)],
        2 * rows * columns * out_width,
        6 * rows * out_width + 2 * columns * out_width,
    )(info, row_adapter_index, owners, mine, theirs, left, right, *up_pieces)


def solution(mesh):
    return jax.shard_map(
        on_device,
        mesh=mesh,
        in_specs=(
            P(("replica", "shard"), "tensor"),
            P(("replica", "shard"), None),
            P(None, "tensor"),
            P("shard", "tensor", None),
            P("shard", None, "tensor"),
        ),
        out_specs=P(("replica", "shard"), "tensor"),
        check_vma=False,
    )
```

time: 132 us -> 54.6 us (0.41)
  waiting for transfers between devices: 86.9 us -> 8.72 us
  Pallas kernels: 0 us -> 21.6 us
  starting transfers between devices: 0.08 us -> 17.9 us
  matrix products: 15.5 us -> 0 us
  between operations: 13.1 us -> 0.15 us
  blocking collectives: 4.17 us -> 0 us
  other arithmetic: 3.34 us -> 0.24 us
  local copies, waits for them, and re-layouts: 8.06 us -> 5.73 us
    all_gather x3 -> x0, waiting for transfers between devices: 84.8 us -> none  [the longest x1 39.2 us: on_device(): lax.all_gather(adapter_down_weight, 'shard', axis=0, tiled=True)]
    pallas_call x0 -> x7, Pallas kernels: none -> 21.6 us  [the longest x2 15.1 us: base_half(): pl.pallas_call(base_kernel, out_shape=[jax.ShapeDtypeStruct((rows, column...]
    ppermute x0 -> x15, starting transfers between devices: none -> 17.9 us  [the longest x6 9.53 us: along_line(): lax.ppermute(value, 'shard', [(i, (i + 2 * step) % shards) for i in range...]
    dot_general x3 -> x0, matrix products: 15.5 us -> none  [the longest x1 10.5 us: on_device(): jnp.dot(lax.all_gather(latent, 'tensor', axis=1, tiled=True), shared_weig...]
    ppermute x0 -> x15, waiting for transfers between devices: none -> 8.72 us  [the longest x6 8.53 us: in_plane(): return lax.ppermute(value, AXES, pairs)]
    unnamed x0 -> x33, local copies, waits for them, and re-layouts: none -> 5.49 us
    scatter x1 -> x0, local copies, waits for them, and re-layouts: 4.9 us -> none  [on_device(): jnp.zeros((adapters * capacity, half_width), latent.dtype).at[target]]
    psum x1 -> x0, blocking collectives: 4.17 us -> none  [on_device(): lowrank = lax.psum(partial_value, 'tensor').astype(jnp.bfloat16)]
  transfers between devices with their start and end apart: 3 -> 15, of which waited for: 3 -> 3; matrix products, arithmetic and copies ran while one was open for 12% -> 1% of each run, Pallas kernels for 0% -> 34%
where the time goes in v2:
time: 54.6 us; the launch traced here: 54.3 us
  Pallas kernels  21.6 us (40%)
  starting transfers between devices  17.9 us (33%)
  waiting for transfers between devices  8.72 us (16%)
  local copies, waits for them, and re-layouts  5.73 us (10%)
    pallas_call x2, Pallas kernels, base_half(): pl.pallas_call(base_kernel, out_shape=[jax.ShapeDtypeStruct((rows, column...  15.1 us
    ppermute x6, starting transfers between devices, along_line(): lax.ppermute(value, 'shard', [(i, (i + 2 * step) % shards) for i in range...  9.53 us
    ppermute x6, waiting for transfers between devices, in_plane(): return lax.ppermute(value, AXES, pairs)  8.53 us
    ppermute x6, starting transfers between devices, in_plane(): return lax.ppermute(value, AXES, pairs)  7.29 us
    unnamed x33, local copies, waits for them, and re-layouts  5.49 us
    pallas_call x1, Pallas kernels, on_device(): call(up_kernel, jax.ShapeDtypeStruct((rows, out_width), jnp.bfloat16), [S...  2.85 us
    pallas_call x1, Pallas kernels, on_device(): call(down_kernel, jax.ShapeDtypeStruct((rows, 2 * rank), jnp.float32), [S...  2.31 us
    pallas_call x1, Pallas kernels, on_device(): call(halves_kernel, [piece, piece, jax.ShapeDtypeStruct((2 * rank, half_w...  1.33 us
  transfers between devices with their start and end apart: 15, of which 3 were waited for; matrix products, arithmetic and copies ran while one was open for 1% of the time, Pallas kernels for 34%

profile of v2, /device:TPU:0, one launch (start us, length us, event | category | flops | bytes accessed | tf_op | source)
XLA Modules:
  0.0 54.3 jit_solution(1995407210453344462)
XLA Ops:
  0.0 0.5 collective-permute-start.4
  0.5 0.1 pad_add_fusion.1.info
  0.5 0.9 %copy-done.5 = bf16[1,1536,64]{1,2,0:T(8,128)(2,1)S(1)} copy-done((bf16[1,1536,64]{1,2,0:T(8,128)(2,1)S(1)}, bf16[1,1536,64]{1,2,0:T(8,128)(2,1)}, u32[]{:S(2)}) %copy-start.5) | copy-done | bytes 196632
  1.5 0.9 %copy-done.7 = bf16[1,64,1536]{2,1,0:T(8,128)(2,1)S(1)} copy-done((bf16[1,64,1536]{2,1,0:T(8,128)(2,1)S(1)}, bf16[1,64,1536]{2,1,0:T(8,128)(2,1)}, u32[]{:S(2)}) %copy-start.7) | copy-done | bytes 196632
  2.4 1.3 %shard_map.55 = (bf16[32,1536]{1,0:T(8,128)(2,1)S(1)}, bf16[32,1536]{1,0:T(8,128)(2,1)S(1)}, bf16[128,1536]{1,0:T(8,128)(2,1)}) custom-call(s32[2]{0:T(128)S(1)} %pad_add_fusion.1.info, bf16[64,1536]{1,0:T(8,128)(2,1)S(1)} %bitcast.22, bf16[64,1536]{1,0:T(8,128)(2,1)S(1)} %bitcast.24), custom_call_target="tpu_custom_call" | custom-call | tf_op jit(solution)/shard_map/pallas_call | solution.py:195
  3.7 4.6 %collective-permute-start.3 = (bf16[32,1536]{1,0:T(8,128)(2,1)S(1)}, bf16[32,1536]{1,0:T(8,128)(2,1)S(1)}, u32[]{:S(2)}, u32[]{:S(2)}) collective-permute-start(bf16[32,1536]{1,0:T(8,128)(2,1)S(1)} %get-tuple-element.13._), channel_id=1, source_target_pairs={{0,12},{2,14},{4,0},{6,2},{8,4},{10,6},{12,8},{14,10},{1,13},{3,15... | collective-permute-start | bytes 294920 | tf_op jit(solution)/shard_map/ppermute | solution.py:21
  8.3 0.0 collective-permute-start.2
  8.3 1.0 %collective-permute-start.1 = (bf16[32,1536]{1,0:T(8,128)(2,1)S(1)}, bf16[32,1536]{1,0:T(8,128)(2,1)S(1)}, u32[]{:S(2)}, u32[]{:S(2)}) collective-permute-start(bf16[32,1536]{1,0:T(8,128)(2,1)S(1)} %get-tuple-element.13._), channel_id=1, source_target_pairs={{0,4},{2,6},{4,8},{6,10},{8,12},{10,14},{12,0},{14,2},{1,5},{3,7},... | collective-permute-start | bytes 294920 | tf_op jit(solution)/shard_map/ppermute | solution.py:21
  9.3 0.0 collective-permute-done.4.other
  9.3 0.0 copy-start.14
  9.4 1.1 %copy-done.14 = bf16[512,1536]{1,0:T(8,128)(2,1)} copy-done((bf16[512,1536]{1,0:T(8,128)(2,1)}, bf16[512,1536]{1,0:T(8,128)(2,1)S(1)}, u32[]{:S(2)}) %copy-start.14) | copy-done | bytes 1572888
  10.5 7.5 %shard_map.56 = (f32[512,768]{1,0:T(8,128)}, f32[8,128]{1,0:T(8,128)}) custom-call(s32[2]{0:T(128)} %copy-done.10, bf16[512,1536]{1,0:T(8,128)(2,1)} %latent.1, bf16[512,1536]{1,0:T(8,128)(2,1)} %copy-done.14, bf16[3072,1536]{1,0:T(8,128)(2,1)} %other_weight.3, bf16[3072,1536]{1,0:T(8,128)(2,1)} %other_weight.3, bf16[32,1536]{1,0:T(8,128)(2,1)} %copy-done.9), custom_call_target="tpu_custom_call" | custom-call | tf_op jit(solution)/shard_map/pallas_call | solution.py:126
  18.0 0.0 collective-permute-done.3.refs_2_
  18.0 0.2 collective-permute-done.2.refs_1_
  18.1 0.0 collective-permute-done.1.refs_0_
  18.1 0.7 %copy-done.13 = f32[8,128]{1,0:T(8,128)S(1)} copy-done((f32[8,128]{1,0:T(8,128)S(1)}, f32[8,128]{1,0:T(8,128)}, u32[]{:S(2)}) %copy-start.13) | copy-done | bytes 4120
  18.8 1.6 %collective-permute-start.5 = (bf16[96,1536]{1,0:T(8,128)(2,1)S(1)}, bf16[96,1536]{1,0:T(8,128)(2,1)S(1)}, u32[]{:S(2)}, u32[]{:S(2)}) collective-permute-start(bf16[96,1536]{1,0:T(8,128)(2,1)S(1)} %shard_map.57._.refs_2_), channel_id=1, source_target_pairs={{0,2},{1,17},{2,0},{3,19},{4,6},{5,21},{6,4},{7,23},{8,10},{9,25},... | collective-permute-start | bytes 884744 | tf_op jit(solution)/shard_map/ppermute | solution.py:31
  20.4 2.7 %collective-permute-start.10 = (bf16[32,1536]{1,0:T(8,128)(2,1)S(1)}, bf16[32,1536]{1,0:T(8,128)(2,1)S(1)}, u32[]{:S(2)}, u32[]{:S(2)}) collective-permute-start(bf16[32,1536]{1,0:T(8,128)(2,1)S(1)} %get-tuple-element.15), channel_id=1, source_target_pairs={{0,12},{2,14},{4,0},{6,2},{8,4},{10,6},{12,8},{14,10},{1,13},{3,15... | collective-permute-start | bytes 294920 | tf_op jit(solution)/shard_map/ppermute | solution.py:21
  23.1 1.1 %collective-permute-start.9 = (bf16[32,1536]{1,0:T(8,128)(2,1)S(1)}, bf16[32,1536]{1,0:T(8,128)(2,1)S(1)}, u32[]{:S(2)}, u32[]{:S(2)}) collective-permute-start(bf16[32,1536]{1,0:T(8,128)(2,1)S(1)} %get-tuple-element.15), channel_id=1, source_target_pairs={{0,8},{2,10},{4,12},{6,14},{8,0},{10,2},{12,4},{14,6},{1,9},{3,11}... | collective-permute-start | bytes 294920 | tf_op jit(solution)/shard_map/ppermute | solution.py:21
  24.2 0.1 collective-permute-start.8
  24.3 0.5 collective-permute-start
  24.9 7.6 %shard_map.58 = (f32[512,768]{1,0:T(8,128)}, f32[8,128]{1,0:T(8,128)}) custom-call(s32[2]{0:T(128)} %copy-done.10, bf16[512,1536]{1,0:T(8,128)(2,1)} %latent.1, bf16[512,1536]{1,0:T(8,128)(2,1)} %copy-done.14, bf16[3072,1536]{1,0:T(8,128)(2,1)} %other_weight.3, bf16[3072,1536]{1,0:T(8,128)(2,1)} %other_weight.3, bf16[96,1536]{1,0:T(8,128)(2,1)} %copy-done.1), custom_call_target="tpu_custom_call" | custom-call | tf_op jit(solution)/shard_map/pallas_call | solution.py:126
  32.5 0.0 collective-permute-done.10.refs_2_
  32.5 1.5 %collective-permute-start.6 = (bf16[96,1536]{1,0:T(8,128)(2,1)}, bf16[96,1536]{1,0:T(8,128)(2,1)}, u32[]{:S(2)}, u32[]{:S(2)}) collective-permute-start(bf16[96,1536]{1,0:T(8,128)(2,1)} %copy-done.1), channel_id=1, source_target_pairs={{0,16},{1,3},{2,18},{3,1},{4,20},{5,7},{6,22},{7,5},{8,24},{9,11},... | collective-permute-start | bytes 884744 | tf_op jit(solution)/shard_map/ppermute | solution.py:31
  34.0 0.0 collective-permute-done.9.refs_1_
  34.0 0.0 collective-permute-done.8.refs_0_
  34.0 0.7 %copy-done.12 = f32[8,128]{1,0:T(8,128)S(1)} copy-done((f32[8,128]{1,0:T(8,128)S(1)}, f32[8,128]{1,0:T(8,128)}, u32[]{:S(2)}) %copy-start.12) | copy-done | bytes 4120
  34.7 1.6 %collective-permute-start.12 = (bf16[96,1536]{1,0:T(8,128)(2,1)S(1)}, bf16[96,1536]{1,0:T(8,128)(2,1)S(1)}, u32[]{:S(2)}, u32[]{:S(2)}) collective-permute-start(bf16[96,1536]{1,0:T(8,128)(2,1)S(1)} %shard_map.59.refs_6_.refs_2_), channel_id=1, source_target_pairs={{0,2},{1,17},{2,0},{3,19},{4,6},{5,21},{6,4},{7,23},{8,10},{9,25},... | collective-permute-start | bytes 884744 | tf_op jit(solution)/shard_map/ppermute | solution.py:31
  36.3 0.0 collective-permute-done.5.refs_3_
  36.3 0.5 collective-permute-start.7
  36.8 0.1 add_bitcast_fusion
  36.9 0.1 add_bitcast_fusion.2
  37.0 0.1 reshape.9
  37.0 0.1 broadcast_in_dim.3
  37.1 0.1 broadcast_in_dim_reshape.3.owners
  37.2 0.2 copy.7.ids
  37.4 1.6 %collective-permute-start.13 = (bf16[96,1536]{1,0:T(8,128)(2,1)S(1)}, bf16[96,1536]{1,0:T(8,128)(2,1)S(1)}, u32[]{:S(2)}, u32[]{:S(2)}) collective-permute-start(bf16[96,1536]{1,0:T(8,128)(2,1)S(1)} %shard_map.59.refs_6_.refs_2_), channel_id=1, source_target_pairs={{0,16},{1,3},{2,18},{3,1},{4,20},{5,7},{6,22},{7,5},{8,24},{9,11},... | collective-permute-start | bytes 884744 | tf_op jit(solution)/shard_map/ppermute | solution.py:31
  38.9 5.8 %collective-permute-done.12.refs_3_ = bf16[96,1536]{1,0:T(8,128)(2,1)S(1)} collective-permute-done((bf16[96,1536]{1,0:T(8,128)(2,1)S(1)}, bf16[96,1536]{1,0:T(8,128)(2,1)S(1)}, u32[]{:S(2)}, u32[]{:S(2)}) %collective-permute-start.12) | collective-permute-done | bytes 294944 | tf_op jit(solution)/shard_map/ppermute | solution.py:31
  44.7 0.5 collective-permute-start.14
  45.2 0.0 collective-permute-done.refs_1_
  45.2 0.0 collective-permute-done.6.refs_4_
  45.2 0.0 collective-permute-done.7.refs_5_
  45.3 1.0 %copy-done.2 = bf16[96,1536]{1,0:T(8,128)(2,1)S(1)} copy-done((bf16[96,1536]{1,0:T(8,128)(2,1)S(1)}, bf16[96,1536]{1,0:T(8,128)(2,1)}, u32[]{:S(2)}) %copy-start.2) | copy-done | bytes 294936
  46.2 2.3 %shard_map.60.mine = f32[512,128]{1,0:T(8,128)S(1)} custom-call(s32[2]{0:T(128)S(1)} %copy-done.11, s32[512,1]{1,0:T(8,128)S(1)} %copy.7.ids, s32[1,512]{1,0:T(1,128)S(1)} %broadcast_in_dim_reshape.3.owners, bf16[512,1536]{1,0:T(8,128)(2,1)S(1)} %copy-done, bf16[64,1536]{1,0:T(8,128)(2,1)S(1)} %bitcast.23, ...), custom_call_target="tpu_custom_call" | custom-call | flops 805306368 | bytes 3145728 | tf_op jit(solution)/shard_map/pallas_call | solution.py:225
  48.5 0.1 collective-permute-start.11
  48.6 0.0 collective-permute-done.13.refs_4_
  48.6 2.8 %collective-permute-done.14.refs_5_ = bf16[96,1536]{1,0:T(8,128)(2,1)S(1)} collective-permute-done((bf16[96,1536]{1,0:T(8,128)(2,1)S(1)}, bf16[96,1536]{1,0:T(8,128)(2,1)S(1)}, u32[]{:S(2)}, u32[]{:S(2)}) %collective-permute-start.14) | collective-permute-done | bytes 294944 | tf_op jit(solution)/shard_map/ppermute | solution.py:31
  51.4 2.9 %shard_map.61 = bf16[512,1536]{1,0:T(8,128)(2,1)} custom-call(s32[2]{0:T(128)S(1)} %copy-done.11, s32[512,1]{1,0:T(8,128)S(1)} %copy.7.ids, s32[1,512]{1,0:T(1,128)S(1)} %broadcast_in_dim_reshape.3.owners, f32[512,128]{1,0:T(8,128)S(1)} %shard_map.60.mine, f32[512,128]{1,0:T(8,128)S(1)} %collective-permute-done.11.theirs, f32[512,768]{1,0:T(8,128)S(1)} %copy-done.3, ...), custom_call_target="tpu_custom_call" | custom-call | flops 805306368 | bytes 6291456 | tf_op jit(solution)/shard_map/pallas_call | solution.py:239
  (29 shorter events, 0.1 us)
Async XLA Ops:
  0.0 9.3 %collective-permute-start.4 = (bf16[512,1536]{1,0:T(8,128)(2,1)}, bf16[512,1536]{1,0:T(8,128)(2,1)S(1)}, u32[]{:S(2)}, u32[]{:S(2)}) collective-permute-start(bf16[512,1536]{1,0:T(8,128)(2,1)} %latent.1), channel_id=1, source_target_pairs={{0,1},{1,0},{2,3},{3,2},{4,5},{5,4},{6,7},{7,6},{8,9},{9,8},{10,11... | collective-permute-start | bytes 4718600 | tf_op jit(solution)/shard_map/ppermute | solution.py:17
  0.5 8.8 %copy-start.10 = (s32[2]{0:T(128)}, s32[2]{0:T(128)S(1)}, u32[]{:S(2)}) copy-start(s32[2]{0:T(128)S(1)} %pad_add_fusion.1.info) | copy-start | bytes 28
  0.5 0.9 %copy-start.5 = (bf16[1,1536,64]{1,2,0:T(8,128)(2,1)S(1)}, bf16[1,1536,64]{1,2,0:T(8,128)(2,1)}, u32[]{:S(2)}) copy-start(bf16[1,1536,64]{1,2,0:T(8,128)(2,1)} %param.8) | copy-start | bytes 589828
  1.5 0.9 %copy-start.7 = (bf16[1,64,1536]{2,1,0:T(8,128)(2,1)S(1)}, bf16[1,64,1536]{2,1,0:T(8,128)(2,1)}, u32[]{:S(2)}) copy-start(bf16[1,64,1536]{2,1,0:T(8,128)(2,1)} %param.9) | copy-start | bytes 589828
  3.7 5.6 %copy-start.9 = (bf16[32,1536]{1,0:T(8,128)(2,1)}, bf16[32,1536]{1,0:T(8,128)(2,1)S(1)}, u32[]{:S(2)}) copy-start(bf16[32,1536]{1,0:T(8,128)(2,1)S(1)} %get-tuple-element.13._) | copy-start | bytes 294916
  3.7 14.2 %collective-permute-start.3 = (bf16[32,1536]{1,0:T(8,128)(2,1)S(1)}, bf16[32,1536]{1,0:T(8,128)(2,1)S(1)}, u32[]{:S(2)}, u32[]{:S(2)}) collective-permute-start(bf16[32,1536]{1,0:T(8,128)(2,1)S(1)} %get-tuple-element.13._), channel_id=1, source_target_pairs={{0,12},{2,14},{4,0},{6,2},{8,4},{10,6},{12,8},{14,10},{1,13},{3,15... | collective-permute-start | bytes 294920 | tf_op jit(solution)/shard_map/ppermute | solution.py:21
  8.3 9.8 %collective-permute-start.2 = (bf16[32,1536]{1,0:T(8,128)(2,1)S(1)}, bf16[32,1536]{1,0:T(8,128)(2,1)S(1)}, u32[]{:S(2)}, u32[]{:S(2)}) collective-permute-start(bf16[32,1536]{1,0:T(8,128)(2,1)S(1)} %get-tuple-element.13._), channel_id=1, source_target_pairs={{0,8},{2,10},{4,12},{6,14},{8,0},{10,2},{12,4},{14,6},{1,9},{3,11}... | collective-permute-start | bytes 294920 | tf_op jit(solution)/shard_map/ppermute | solution.py:21
  8.3 9.8 %collective-permute-start.1 = (bf16[32,1536]{1,0:T(8,128)(2,1)S(1)}, bf16[32,1536]{1,0:T(8,128)(2,1)S(1)}, u32[]{:S(2)}, u32[]{:S(2)}) collective-permute-start(bf16[32,1536]{1,0:T(8,128)(2,1)S(1)} %get-tuple-element.13._), channel_id=1, source_target_pairs={{0,4},{2,6},{4,8},{6,10},{8,12},{10,14},{12,0},{14,2},{1,5},{3,7},... | collective-permute-start | bytes 294920 | tf_op jit(solution)/shard_map/ppermute | solution.py:21
  9.3 1.1 %copy-start.14 = (bf16[512,1536]{1,0:T(8,128)(2,1)}, bf16[512,1536]{1,0:T(8,128)(2,1)S(1)}, u32[]{:S(2)}) copy-start(bf16[512,1536]{1,0:T(8,128)(2,1)S(1)} %collective-permute-done.4.other) | copy-start | bytes 4718596
  18.1 0.7 %copy-start.13 = (f32[8,128]{1,0:T(8,128)S(1)}, f32[8,128]{1,0:T(8,128)}, u32[]{:S(2)}) copy-start(f32[8,128]{1,0:T(8,128)} %get-tuple-element.14.refs_3_) | copy-start | bytes 12292
  18.8 6.0 %copy-start.1 = (bf16[96,1536]{1,0:T(8,128)(2,1)}, bf16[96,1536]{1,0:T(8,128)(2,1)S(1)}, u32[]{:S(2)}) copy-start(bf16[96,1536]{1,0:T(8,128)(2,1)S(1)} %shard_map.57._.refs_2_) | copy-start | bytes 884740
  18.8 17.4 %collective-permute-start.5 = (bf16[96,1536]{1,0:T(8,128)(2,1)S(1)}, bf16[96,1536]{1,0:T(8,128)(2,1)S(1)}, u32[]{:S(2)}, u32[]{:S(2)}) collective-permute-start(bf16[96,1536]{1,0:T(8,128)(2,1)S(1)} %shard_map.57._.refs_2_), channel_id=1, source_target_pairs={{0,2},{1,17},{2,0},{3,19},{4,6},{5,21},{6,4},{7,23},{8,10},{9,25},... | collective-permute-start | bytes 884744 | tf_op jit(solution)/shard_map/ppermute | solution.py:31
  20.4 12.0 %collective-permute-start.10 = (bf16[32,1536]{1,0:T(8,128)(2,1)S(1)}, bf16[32,1536]{1,0:T(8,128)(2,1)S(1)}, u32[]{:S(2)}, u32[]{:S(2)}) collective-permute-start(bf16[32,1536]{1,0:T(8,128)(2,1)S(1)} %get-tuple-element.15), channel_id=1, source_target_pairs={{0,12},{2,14},{4,0},{6,2},{8,4},{10,6},{12,8},{14,10},{1,13},{3,15... | collective-permute-start | bytes 294920 | tf_op jit(solution)/shard_map/ppermute | solution.py:21
  23.1 10.9 %collective-permute-start.9 = (bf16[32,1536]{1,0:T(8,128)(2,1)S(1)}, bf16[32,1536]{1,0:T(8,128)(2,1)S(1)}, u32[]{:S(2)}, u32[]{:S(2)}) collective-permute-start(bf16[32,1536]{1,0:T(8,128)(2,1)S(1)} %get-tuple-element.15), channel_id=1, source_target_pairs={{0,8},{2,10},{4,12},{6,14},{8,0},{10,2},{12,4},{14,6},{1,9},{3,11}... | collective-permute-start | bytes 294920 | tf_op jit(solution)/shard_map/ppermute | solution.py:21
  24.2 9.8 %collective-permute-start.8 = (bf16[32,1536]{1,0:T(8,128)(2,1)S(1)}, bf16[32,1536]{1,0:T(8,128)(2,1)S(1)}, u32[]{:S(2)}, u32[]{:S(2)}) collective-permute-start(bf16[32,1536]{1,0:T(8,128)(2,1)S(1)} %get-tuple-element.15), channel_id=1, source_target_pairs={{0,4},{2,6},{4,8},{6,10},{8,12},{10,14},{12,0},{14,2},{1,5},{3,7},... | collective-permute-start | bytes 294920 | tf_op jit(solution)/shard_map/ppermute | solution.py:21
  24.3 20.9 %collective-permute-start = (bf16[128,1536]{1,0:T(8,128)(2,1)}, bf16[128,1536]{1,0:T(8,128)(2,1)S(1)}, u32[]{:S(2)}, u32[]{:S(2)}) collective-permute-start(bf16[128,1536]{1,0:T(8,128)(2,1)} %get-tuple-element.12), channel_id=1, source_target_pairs={{0,2},{2,0},{4,6},{6,4},{8,10},{10,8},{12,14},{14,12},{1,3},{3,1},... | collective-permute-start | bytes 1179656 | tf_op jit(solution)/shard_map/ppermute | solution.py:203
  24.9 12.3 %copy-start.15 = (s32[512,1]{0,1:T(1,128)S(1)}, s32[512,1]{0,1:T(1,128)}, u32[]{:S(2)}) copy-start(s32[512,1]{0,1:T(1,128)} %param.6) | copy-start | bytes 6148
  24.9 20.4 %copy-start = (bf16[512,1536]{1,0:T(8,128)(2,1)S(1)}, bf16[512,1536]{1,0:T(8,128)(2,1)}, u32[]{:S(2)}) copy-start(bf16[512,1536]{1,0:T(8,128)(2,1)} %latent.1) | copy-start | bytes 4718596
  24.9 20.4 %copy-start.6 = (bf16[1,1536,64]{1,2,0:T(8,128)(2,1)S(1)}, bf16[1,1536,64]{1,2,0:T(8,128)(2,1)}, u32[]{:S(2)}) copy-start(bf16[1,1536,64]{1,2,0:T(8,128)(2,1)} %param.8) | copy-start | bytes 589828
  24.9 20.4 %copy-start.11 = (s32[2]{0:T(128)S(1)}, s32[2]{0:T(128)}, u32[]{:S(2)}) copy-start(s32[2]{0:T(128)} %copy-done.10) | copy-start | bytes 28
  32.5 12.7 %collective-permute-start.6 = (bf16[96,1536]{1,0:T(8,128)(2,1)}, bf16[96,1536]{1,0:T(8,128)(2,1)}, u32[]{:S(2)}, u32[]{:S(2)}) collective-permute-start(bf16[96,1536]{1,0:T(8,128)(2,1)} %copy-done.1), channel_id=1, source_target_pairs={{0,16},{1,3},{2,18},{3,1},{4,20},{5,7},{6,22},{7,5},{8,24},{9,11},... | collective-permute-start | bytes 884744 | tf_op jit(solution)/shard_map/ppermute | solution.py:31
  34.0 0.7 %copy-start.12 = (f32[8,128]{1,0:T(8,128)S(1)}, f32[8,128]{1,0:T(8,128)}, u32[]{:S(2)}) copy-start(f32[8,128]{1,0:T(8,128)} %get-tuple-element.16.refs_3_) | copy-start | bytes 12292
  34.7 10.0 %collective-permute-start.12 = (bf16[96,1536]{1,0:T(8,128)(2,1)S(1)}, bf16[96,1536]{1,0:T(8,128)(2,1)S(1)}, u32[]{:S(2)}, u32[]{:S(2)}) collective-permute-start(bf16[96,1536]{1,0:T(8,128)(2,1)S(1)} %shard_map.59.refs_6_.refs_2_), channel_id=1, source_target_pairs={{0,2},{1,17},{2,0},{3,19},{4,6},{5,21},{6,4},{7,23},{8,10},{9,25},... | collective-permute-start | bytes 884744 | tf_op jit(solution)/shard_map/ppermute | solution.py:31
  36.3 9.0 %collective-permute-start.7 = (bf16[96,1536]{1,0:T(8,128)(2,1)S(1)}, bf16[96,1536]{1,0:T(8,128)(2,1)}, u32[]{:S(2)}, u32[]{:S(2)}) collective-permute-start(bf16[96,1536]{1,0:T(8,128)(2,1)S(1)} %collective-permute-done.5.refs_3_), channel_id=1, source_target_pairs={{0,16},{1,3},{2,18},{3,1},{4,20},{5,7},{6,22},{7,5},{8,24},{9,11},... | collective-permute-start | bytes 884744 | tf_op jit(solution)/shard_map/ppermute | solution.py:31
  37.2 14.2 %copy-start.8 = (bf16[1,64,1536]{2,1,0:T(8,128)(2,1)S(1)}, bf16[1,64,1536]{2,1,0:T(8,128)(2,1)}, u32[]{:S(2)}) copy-start(bf16[1,64,1536]{2,1,0:T(8,128)(2,1)} %param.9) | copy-start | bytes 589828
  37.4 11.3 %collective-permute-start.13 = (bf16[96,1536]{1,0:T(8,128)(2,1)S(1)}, bf16[96,1536]{1,0:T(8,128)(2,1)S(1)}, u32[]{:S(2)}, u32[]{:S(2)}) collective-permute-start(bf16[96,1536]{1,0:T(8,128)(2,1)S(1)} %shard_map.59.refs_6_.refs_2_), channel_id=1, source_target_pairs={{0,16},{1,3},{2,18},{3,1},{4,20},{5,7},{6,22},{7,5},{8,24},{9,11},... | collective-permute-start | bytes 884744 | tf_op jit(solution)/shard_map/ppermute | solution.py:31
  44.7 6.7 %collective-permute-start.14 = (bf16[96,1536]{1,0:T(8,128)(2,1)S(1)}, bf16[96,1536]{1,0:T(8,128)(2,1)S(1)}, u32[]{:S(2)}, u32[]{:S(2)}) collective-permute-start(bf16[96,1536]{1,0:T(8,128)(2,1)S(1)} %collective-permute-done.12.refs_3_), channel_id=1, source_target_pairs={{0,16},{1,3},{2,18},{3,1},{4,20},{5,7},{6,22},{7,5},{8,24},{9,11},... | collective-permute-start | bytes 884744 | tf_op jit(solution)/shard_map/ppermute | solution.py:31
  45.3 1.0 %copy-start.2 = (bf16[96,1536]{1,0:T(8,128)(2,1)S(1)}, bf16[96,1536]{1,0:T(8,128)(2,1)}, u32[]{:S(2)}) copy-start(bf16[96,1536]{1,0:T(8,128)(2,1)} %copy-done.1) | copy-start | bytes 884740
  46.2 5.2 %copy-start.3 = (f32[512,768]{1,0:T(8,128)S(1)}, f32[512,768]{1,0:T(8,128)}, u32[]{:S(2)}) copy-start(f32[512,768]{1,0:T(8,128)} %get-tuple-element.17.left) | copy-start | bytes 4718596
  46.2 5.2 %copy-start.4 = (f32[512,768]{1,0:T(8,128)S(1)}, f32[512,768]{1,0:T(8,128)}, u32[]{:S(2)}) copy-start(f32[512,768]{1,0:T(8,128)} %get-tuple-element.18.right) | copy-start | bytes 4718596
  48.5 2.9 %collective-permute-start.11 = (f32[512,128]{1,0:T(8,128)S(1)}, f32[512,128]{1,0:T(8,128)S(1)}, u32[]{:S(2)}, u32[]{:S(2)}) collective-permute-start(f32[512,128]{1,0:T(8,128)S(1)} %shard_map.60.mine), channel_id=1, source_target_pairs={{0,1},{1,0},{2,3},{3,2},{4,5},{5,4},{6,7},{7,6},{8,9},{9,8},{10,11... | collective-permute-start | bytes 786440 | tf_op jit(solution)/shard_map/ppermute | solution.py:17

commit v3 on v2

v3 whole, which is shorter than its diff:
```python
import jax
import jax.numpy as jnp
import numpy as np
from jax import lax
from jax.experimental import pallas as pl
from jax.experimental.pallas import tpu as pltpu
from jax.sharding import PartitionSpec as P

MIB = 1024 * 1024
CHUNK = 512
AXES = ("replica", "shard", "tensor")
WAVES = ((1, 3), (2,))
SMEM = pl.BlockSpec(memory_space=pltpu.SMEM)
VMEM = pl.BlockSpec(memory_space=pltpu.VMEM)
ANY = pl.BlockSpec(memory_space=pl.ANY)


def swap(value, axis):
    return lax.ppermute(value, axis, [(0, 1), (1, 0)])


def neighbour(value, shards):
    return lax.ppermute(value, "shard", [(i, i ^ 1) for i in range(shards)])


def along_line(value, shards, step):
    return lax.ppermute(value, "shard", [(i, (i + 2 * step) % shards) for i in range(shards)])


def in_plane(value, shards, first):
    pairs = []
    for r in range(2):
        for s in range(shards):
            for t in range(2):
                to_r, to_s = (r, s ^ 1) if (t == 0) == first else (r ^ 1, s)
                pairs.append(((r * shards + s) * 2 + t, (to_r * shards + to_s) * 2 + t))
    return lax.ppermute(value, AXES, pairs)


def call(kernel, out_shape, in_specs, limit, scratch=(), flops=0, moved=0):
    return pl.pallas_call(
        kernel,
        out_shape=out_shape,
        in_specs=in_specs,
        out_specs=jax.tree.map(lambda _: VMEM, out_shape),
        scratch_shapes=list(scratch),
        compiler_params=pltpu.CompilerParams(vmem_limit_bytes=limit * MIB),
        cost_estimate=pl.CostEstimate(flops=flops, bytes_accessed=moved, transcendentals=0),
    )


def owner_table(shards, rank):
    table = []
    for index in range(shards):
        sources = [(index - 2 * step) % shards for step in range(shards // 2)]
        table.append([a for s in sources for a in (s, s ^ 1) for _ in range(rank)])
    return np.array(table, np.int32)


def pack(pieces, *after):
    rows, width = pieces[0].shape
    count = len(pieces)

    def kernel(*refs):
        for number in range(count):
            refs[-1][number * rows : (number + 1) * rows, :] = refs[number][...]

    return call(
        kernel,
        jax.ShapeDtypeStruct((count * rows, width), pieces[0].dtype),
        [VMEM] * count + [ANY] * len(after),
        4,
    )(*pieces, *after)


def fill_stack(info, which, refs, stack):
    if len(refs) == 1:
        stack[...] = refs[0][...]
        return
    own, beside, *received = refs
    rank = own.shape[0]
    half = rank // 2
    mine = pl.multiple_of(info[0] * half, half)
    rest = pl.multiple_of((1 - info[0]) * half, half)
    stack[0:half, :] = own[pl.ds(mine, half), :]
    stack[half:rank, :] = own[pl.ds(rest, half), :]
    stack[rank : rank + half, :] = beside[pl.ds(which * rank + mine, half), :]
    stack[rank + half : 2 * rank, :] = beside[pl.ds(which * rank + rest, half), :]
    for wave, groups in enumerate(WAVES):
        line, first, second, corner = received[4 * wave : 4 * wave + 4]
        for number, group in enumerate(groups):
            rows = slice((2 * number + which) * half, (2 * number + which + 1) * half)
            top = 2 * rank * group
            stack[top : top + half, :] = line[rows, :]
            place = pl.multiple_of(top + (2 - info[1]) * half, half)
            stack[pl.ds(place, half), :] = first[rows, :]
            place = pl.multiple_of(top + (1 + info[1]) * half, half)
            stack[pl.ds(place, half), :] = second[rows, :]
            stack[top + 3 * half : top + 4 * half, :] = corner[rows, :]


def down_kernel(info, ids, owners, latent, *refs):
    *pieces, _, out, stack = refs
    fill_stack(info, 0, pieces, stack)
    total = jnp.zeros(out.shape, jnp.float32)
    width = out.shape[1]
    for begin in range(0, stack.shape[0], CHUNK):
        part = lax.dot_general(
            latent[...],
            stack[begin : begin + CHUNK, :],
            (((1,), (1,)), ((), ())),
            preferred_element_type=jnp.float32,
        )
        part = jnp.where(ids[...] == owners[:, begin : begin + CHUNK], part, 0.0)
        for lane in range(0, CHUNK, width):
            total += part[:, lane : lane + width]
    out[...] = total


def base_kernel(info, own, other, weight, _, out, token, rows_ref, weight_ref, sems, *, skip):
    width = own.shape[1]
    tiles, _, tile = weight_ref.shape
    copies = [
        pltpu.make_async_copy(own, rows_ref.at[:, pl.ds(0, width)], sems.at[2 * tiles]),
        pltpu.make_async_copy(other, rows_ref.at[:, pl.ds(width, width)], sems.at[2 * tiles + 1]),
    ]
    for number in range(tiles):
        place = pl.ds((skip + number) * tile, tile)
        for part, owner in ((0, info[1]), (1, 1 - info[1])):
            source = pl.ds(pl.multiple_of(owner * width, width), width)
            copies.append(
                pltpu.make_async_copy(
                    weight.at[source, place],
                    weight_ref.at[number, pl.ds(part * width, width), :],
                    sems.at[2 * number + part],
                )
            )
    for copy in copies:
        copy.start()
    token[...] = jnp.zeros_like(token)
    copies[0].wait()
    copies[1].wait()
    for number in range(tiles):
        copies[2 * number + 2].wait()
        copies[2 * number + 3].wait()
        out[:, number * tile : (number + 1) * tile] = jnp.dot(
            rows_ref[...], weight_ref[number], preferred_element_type=jnp.float32
        )


def base(info, latent, other, weight, after, skip, tiles):
    rows, half_width = latent.shape
    tile = CHUNK
    columns = tiles * tile
    return pl.pallas_call(
        lambda *refs: base_kernel(*refs, skip=skip),
        out_shape=[
            jax.ShapeDtypeStruct((rows, columns), jnp.float32),
            jax.ShapeDtypeStruct((8, 128), jnp.float32),
        ],
        in_specs=[SMEM, ANY, ANY, ANY, ANY],
        out_specs=[VMEM, VMEM],
        scratch_shapes=[
            pltpu.VMEM((rows, 2 * half_width), latent.dtype),
            pltpu.VMEM((tiles, 2 * half_width, tile), weight.dtype),
            pltpu.SemaphoreType.DMA((2 * tiles + 2,)),
        ],
        compiler_params=pltpu.CompilerParams(vmem_limit_bytes=50 * MIB),
        cost_estimate=pl.CostEstimate(
            flops=4 * rows * half_width * columns,
            bytes_accessed=4 * half_width * (rows + columns) + 4 * rows * columns,
            transcendentals=0,
        ),
    )(info, latent, other, weight, after)


def up_kernel(info, ids, owners, mine, theirs, left, right, *refs):
    *pieces, out, stack = refs
    fill_stack(info, 1, pieces, stack)
    lowrank = (mine[...] + theirs[...]).astype(jnp.bfloat16).astype(jnp.float32)
    repeated = jnp.concatenate([lowrank] * (CHUNK // lowrank.shape[1]), axis=1)
    split = left.shape[1]
    for begin in range(0, out.shape[1], CHUNK):
        place = slice(begin, begin + CHUNK)
        delta = jnp.zeros((out.shape[0], CHUNK), jnp.float32)
        for depth in range(0, stack.shape[0], CHUNK):
            wide = jnp.where(ids[...] == owners[:, depth : depth + CHUNK], repeated, 0.0)
            delta += jnp.dot(
                wide.astype(jnp.bfloat16),
                stack[depth : depth + CHUNK, place],
                preferred_element_type=jnp.float32,
            )
        part = left[:, place] if begin < split else right[:, begin - split : begin - split + CHUNK]
        total = part + delta.astype(jnp.bfloat16).astype(jnp.float32)
        out[:, place] = total.astype(out.dtype)


def on_device(latent, row_adapter_index, shared_weight, adapter_down_weight, adapter_up_weight):
    rows, half_width = latent.shape
    out_width = shared_weight.shape[1]
    local_adapters, _, rank = adapter_down_weight.shape
    shards = lax.axis_size("shard")
    adapters = shards * local_adapters
    columns = adapters * rank
    index, replica = lax.axis_index("shard"), lax.axis_index("replica")
    info = jnp.stack([replica, lax.axis_index("tensor")]).astype(jnp.int32)
    tiles = out_width // CHUNK
    first_tiles = 2 * tiles // 3

    down = jnp.swapaxes(adapter_down_weight, 1, 2).reshape(local_adapters * rank, half_width)
    up = adapter_up_weight.reshape(local_adapters * rank, out_width)
    routed = shards == 8 and local_adapters == 1 and lax.axis_size("replica") == 2
    if routed:
        half = rank // 2
        piece = jnp.concatenate(
            [
                lax.dynamic_slice_in_dim(down, replica * half, half, axis=0),
                lax.dynamic_slice_in_dim(up, replica * half, half, axis=0),
            ]
        )
        line = {step: along_line(piece, shards, step) for wave in WAVES for step in wave}
        other = swap(latent, "tensor")
        beside = neighbour(jnp.concatenate([down, up]), shards)
        left, token = base(info, latent, other, shared_weight, piece, 0, first_tiles)
        held = pack([line[step] for step in WAVES[0]], token, beside)
        right, token = base(
            info, latent, other, shared_weight, held, first_tiles, tiles - first_tiles
        )
        first, second = in_plane(held, shards, True), in_plane(held, shards, False)
        received = [held, first, second, in_plane(first, shards, False)]
        held = pack([line[step] for step in WAVES[1]], token, first)
        first, second = in_plane(held, shards, True), in_plane(held, shards, False)
        received += [held, first, second, in_plane(first, shards, False)]
        down_pieces = [down, beside, *received]
        up_pieces = [up, beside, *received]
        owners = jnp.asarray(owner_table(shards, rank))[index][None, :]
    else:
        other = swap(latent, "tensor")
        down_pieces = [lax.all_gather(down, "shard", axis=0, tiled=True)]
        up_pieces = [lax.all_gather(up, "shard", axis=0, tiled=True)]
        left, token = base(info, latent, other, shared_weight, latent, 0, first_tiles)
        right, token = base(
            info, latent, other, shared_weight, latent, first_tiles, tiles - first_tiles
        )
        owners = jnp.repeat(jnp.arange(adapters, dtype=jnp.int32), rank)[None, :]

    mine = call(
        down_kernel,
        jax.ShapeDtypeStruct((rows, 2 * rank), jnp.float32),
        [SMEM] + [VMEM] * (3 + len(down_pieces)) + [ANY],
        16 if routed else 56,
        [pltpu.VMEM((columns, half_width), jnp.bfloat16)],
        2 * rows * columns * half_width,
        2 * (rows + columns) * half_width,
    )(info, row_adapter_index, owners, latent, *down_pieces, token)
    theirs = swap(mine, "tensor")

    return call(
        up_kernel,
        jax.ShapeDtypeStruct((rows, out_width), jnp.bfloat16),
        [SMEM] + [VMEM] * (6 + len(up_pieces)),
        24 if routed else 56,
        [pltpu.VMEM((columns, out_width), jnp.bfloat16)],
        2 * rows * columns * out_width,
        6 * rows * out_width + 2 * columns * out_width,
    )(info, row_adapter_index, owners, mine, theirs, left, right, *up_pieces)


def solution(mesh):
    return jax.shard_map(
        on_device,
        mesh=mesh,
        in_specs=(
            P(("replica", "shard"), "tensor"),
            P(("replica", "shard"), None),
            P(None, "tensor"),
            P("shard", "tensor", None),
            P("shard", None, "tensor"),
        ),
        out_specs=P(("replica", "shard"), "tensor"),
        check_vma=False,
    )
```

time: 54.6 us -> 58.3 us (1.068)
  waiting for transfers between devices: 8.72 us -> 15.3 us
  starting transfers between devices: 17.9 us -> 14.6 us
  other arithmetic: 0.24 us -> 2.57 us
  Pallas kernels: 21.6 us -> 19.9 us
    ppermute x6 -> x3, starting transfers between devices: 9.53 us -> 5.45 us  [along_line(): lax.ppermute(value, 'shard', [(i, (i + 2 * step) % shards) for i in range...]
    ppermute x6 -> x3, waiting for transfers between devices: 0.18 us -> 2.9 us  [along_line(): lax.ppermute(value, 'shard', [(i, (i + 2 * step) % shards) for i in range...]
    unnamed x33 -> x23, local copies, waits for them, and re-layouts: 5.49 us -> 2.89 us
    dynamic_slice x0 -> x3, local copies, waits for them, and re-layouts: none -> 2.56 us  [the longest x1 0.93 us: on_device(): lax.dynamic_slice_in_dim(down, replica * half, half, axis=0)]
    pallas_call x5 -> x4, Pallas kernels: 16.4 us -> 13.9 us  [the longest x2 12.8 us: base(): pl.pallas_call(lambda *refs: base_kernel(*refs, skip=skip), out_shape=[ja...]
    concatenate x0 -> x2, other arithmetic: none -> 2.49 us  [the longest x1 1.8 us: on_device(): beside = neighbour(jnp.concatenate([down, up]), shards)]
    ppermute x1, waiting for transfers between devices: 0.01 us -> 1.8 us  [neighbour(): return lax.ppermute(value, 'shard', [(i, i ^ 1) for i in range(shards)])]
    ppermute x2, waiting for transfers between devices: 0.01 us -> 1.52 us  [swap(): return lax.ppermute(value, axis, [(0, 1), (1, 0)])]
  transfers between devices with their start and end apart: 15 -> 12, of which waited for: 3 -> 6; matrix products, arithmetic and copies ran while one was open for 1% -> 9% of each run, Pallas kernels for 34% -> 22%
where the time goes in v3:
time: 58.3 us; the launch traced here: 58 us
  Pallas kernels  19.9 us (34%)
  waiting for transfers between devices  15.3 us (26%)
  starting transfers between devices  14.6 us (25%)
  local copies, waits for them, and re-layouts  5.45 us (9%)
  other arithmetic  2.57 us (4%)
    pallas_call x2, Pallas kernels, base(): pl.pallas_call(lambda *refs: base_kernel(*refs, skip=skip), out_shape=[ja...  12.8 us
    ppermute x6, waiting for transfers between devices, in_plane(): return lax.ppermute(value, AXES, pairs)  9.11 us
    ppermute x6, starting transfers between devices, in_plane(): return lax.ppermute(value, AXES, pairs)  7.06 us
    ppermute x3, starting transfers between devices, along_line(): lax.ppermute(value, 'shard', [(i, (i + 2 * step) % shards) for i in range...  5.45 us
    pallas_call x1, Pallas kernels, on_device(): call(up_kernel, jax.ShapeDtypeStruct((rows, out_width), jnp.bfloat16), [S...  3.62 us
    ppermute x3, waiting for transfers between devices, along_line(): lax.ppermute(value, 'shard', [(i, (i + 2 * step) % shards) for i in range...  2.9 us
    unnamed x23, local copies, waits for them, and re-layouts  2.89 us
    pallas_call x1, Pallas kernels, on_device(): call(down_kernel, jax.ShapeDtypeStruct((rows, 2 * rank), jnp.float32), [S...  2.43 us
  transfers between devices with their start and end apart: 12, of which 6 were waited for; matrix products, arithmetic and copies ran while one was open for 9% of the time, Pallas kernels for 22%

profile of v3, /device:TPU:0, one launch (start us, length us, event | category | flops | bytes accessed | tf_op | source)
XLA Modules:
  0.0 58.0 jit_solution(13854048590211608500)
XLA Ops:
  0.0 0.5 collective-permute-start.3
  0.5 0.9 %dynamic-slice_bitcast_fusion.1 = bf16[32,1536]{1,0:T(8,128)(2,1)S(1)} fusion(bf16[1,1536,64]{1,2,0:T(8,128)(2,1)} %param.9, s32[]{:T(128)S(6)} %select_n.8), kind=kLoop, calls=%fused_computation.3 | loop fusion | bytes 196612 | tf_op jit(solution)/shard_map/dynamic_slice | solution.py:217
  1.4 0.9 %dynamic-slice_bitcast_fusion = bf16[32,1536]{1,0:T(8,128)(2,1)S(1)} fusion(bf16[1,64,1536]{2,1,0:T(8,128)(2,1)} %param.10, s32[]{:T(128)S(6)} %select_n.8), kind=kLoop, calls=%fused_computation.2 | loop fusion | bytes 196612 | tf_op jit(solution)/shard_map/dynamic_slice | solution.py:218
  2.3 0.7 %pad_maximum_fusion.1.refs_4_ = bf16[64,1536]{1,0:T(8,128)(2,1)} fusion(bf16[32,1536]{1,0:T(8,128)(2,1)S(1)} %dynamic-slice_bitcast_fusion, bf16[32,1536]{1,0:T(8,128)(2,1)S(1)} %dynamic-slice_bitcast_fusion.1), kind=kLoop, calls=%fused_computation.1 | loop fusion | flops 393216 | bytes 393216 | tf_op jit(solution)/shard_map/concatenate | solution.py:215
  3.0 4.7 %collective-permute-start.2 = (bf16[64,1536]{1,0:T(8,128)(2,1)}, bf16[64,1536]{1,0:T(8,128)(2,1)}, u32[]{:S(2)}, u32[]{:S(2)}) collective-permute-start(bf16[64,1536]{1,0:T(8,128)(2,1)} %pad_maximum_fusion.1.refs_4_), channel_id=1, source_target_pairs={{0,12},{2,14},{4,0},{6,2},{8,4},{10,6},{12,8},{14,10},{1,13},{3,15... | collective-permute-start | bytes 589832 | tf_op jit(solution)/shard_map/ppermute | solution.py:27
  7.7 0.0 collective-permute-start.1
  7.7 1.8 %pad_maximum_fusion = bf16[128,1536]{1,0:T(8,128)(2,1)} fusion(bf16[64,1536]{1,0:T(8,128)(2,1)} %bitcast.14, bf16[64,1536]{1,0:T(8,128)(2,1)} %bitcast.12), kind=kLoop, calls=%fused_computation | loop fusion | flops 786432 | bytes 786432 | tf_op jit(solution)/shard_map/concatenate | solution.py:223
  9.5 1.5 %collective-permute-start = (bf16[128,1536]{1,0:T(8,128)(2,1)}, bf16[128,1536]{1,0:T(8,128)(2,1)S(1)}, u32[]{:S(2)}, u32[]{:S(2)}) collective-permute-start(bf16[128,1536]{1,0:T(8,128)(2,1)} %pad_maximum_fusion), channel_id=1, source_target_pairs={{0,2},{2,0},{4,6},{6,4},{8,10},{10,8},{12,14},{14,12},{1,3},{3,1},... | collective-permute-start | bytes 1179656 | tf_op jit(solution)/shard_map/ppermute | solution.py:23
  11.0 0.1 pad_add_fusion.refs_0_.info
  11.1 0.0 collective-permute-done.3.refs_2_
  11.1 0.0 copy-done
  11.1 7.9 %shard_map.64 = (f32[512,1024]{1,0:T(8,128)}, f32[8,128]{1,0:T(8,128)S(1)}) custom-call(s32[2]{0:T(128)S(1)} %pad_add_fusion.refs_0_.info, bf16[512,1536]{1,0:T(8,128)(2,1)S(1)} %copy-done, bf16[512,1536]{1,0:T(8,128)(2,1)S(1)} %collective-permute-done.3.refs_2_, bf16[3072,1536]{1,0:T(8,128)(2,1)} %refs_3_.3, bf16[64,1536]{1,0:T(8,128)(2,1)} %pad_maximum_fusion.1.refs_4_), custom_call_target="tpu_custom_call" | custom-call | flops 3221225472 | bytes 11534336 | tf_op jit(solution)/shard_map/pallas_call | solution.py:155
  19.0 0.0 copy-done.1
  19.0 0.0 collective-permute-done.2.refs_1_
  19.0 0.0 collective-permute-done.1.refs_0_
  19.0 1.8 %collective-permute-done.refs_3_.refs_1_ = bf16[128,1536]{1,0:T(8,128)(2,1)S(1)} collective-permute-done((bf16[128,1536]{1,0:T(8,128)(2,1)}, bf16[128,1536]{1,0:T(8,128)(2,1)S(1)}, u32[]{:S(2)}, u32[]{:S(2)}) %collective-permute-start) | collective-permute-done | bytes 393248 | tf_op jit(solution)/shard_map/ppermute | solution.py:23
  20.8 0.8 %copy-done.2 = bf16[128,1536]{1,0:T(8,128)(2,1)} copy-done((bf16[128,1536]{1,0:T(8,128)(2,1)}, bf16[128,1536]{1,0:T(8,128)(2,1)S(1)}, u32[]{:S(2)}) %copy-start.2) | copy-done | bytes 393240
  21.6 1.0 %copy-done.3 = bf16[128,1536]{1,0:T(8,128)(2,1)S(1)} copy-done((bf16[128,1536]{1,0:T(8,128)(2,1)S(1)}, bf16[128,1536]{1,0:T(8,128)(2,1)}, u32[]{:S(2)}) %copy-start.3) | copy-done | bytes 393240
  22.6 1.0 %shard_map.65.refs_4_.refs_2_ = bf16[128,1536]{1,0:T(8,128)(2,1)S(1)} custom-call(bf16[64,1536]{1,0:T(8,128)(2,1)} %collective-permute-done.1.refs_0_, bf16[64,1536]{1,0:T(8,128)(2,1)} %collective-permute-done.2.refs_1_, f32[8,128]{1,0:T(8,128)S(1)} %get-tuple-element.9.refs_2_, bf16[128,1536]{1,0:T(8,128)(2,1)S(1)} %copy-done.3), custom_call_target="tpu_custom_call" | custom-call | tf_op jit(solution)/shard_map/pallas_call | solution.py:68
  23.6 0.0 copy-start.10
  23.6 0.0 copy-start.4
  23.6 0.0 copy-start.6
  23.6 1.6 %collective-permute-start.4 = (bf16[128,1536]{1,0:T(8,128)(2,1)S(1)}, bf16[128,1536]{1,0:T(8,128)(2,1)S(1)}, u32[]{:S(2)}, u32[]{:S(2)}) collective-permute-start(bf16[128,1536]{1,0:T(8,128)(2,1)S(1)} %shard_map.65.refs_4_.refs_2_), channel_id=1, source_target_pairs={{0,2},{1,17},{2,0},{3,19},{4,6},{5,21},{6,4},{7,23},{8,10},{9,25},... | collective-permute-start | bytes 1179656 | tf_op jit(solution)/shard_map/ppermute | solution.py:37
  25.2 0.7 %collective-permute-start.7 = (bf16[64,1536]{1,0:T(8,128)(2,1)}, bf16[64,1536]{1,0:T(8,128)(2,1)S(1)}, u32[]{:S(2)}, u32[]{:S(2)}) collective-permute-start(bf16[64,1536]{1,0:T(8,128)(2,1)} %pad_maximum_fusion.1.refs_4_), channel_id=1, source_target_pairs={{0,8},{2,10},{4,12},{6,14},{8,0},{10,2},{12,4},{14,6},{1,9},{3,11}... | collective-permute-start | bytes 589832 | tf_op jit(solution)/shard_map/ppermute | solution.py:27
  26.0 1.5 %collective-permute-start.5 = (bf16[128,1536]{1,0:T(8,128)(2,1)S(1)}, bf16[128,1536]{1,0:T(8,128)(2,1)}, u32[]{:S(2)}, u32[]{:S(2)}) collective-permute-start(bf16[128,1536]{1,0:T(8,128)(2,1)S(1)} %shard_map.65.refs_4_.refs_2_), channel_id=1, source_target_pairs={{0,16},{1,3},{2,18},{3,1},{4,20},{5,7},{6,22},{7,5},{8,24},{9,11},... | collective-permute-start | bytes 1179656 | tf_op jit(solution)/shard_map/ppermute | solution.py:37
  27.4 5.0 %shard_map.66 = (f32[512,512]{1,0:T(8,128)S(1)}, f32[8,128]{1,0:T(8,128)S(1)}) custom-call(s32[2]{0:T(128)S(1)} %pad_add_fusion.refs_0_.info, bf16[512,1536]{1,0:T(8,128)(2,1)S(1)} %copy-done, bf16[512,1536]{1,0:T(8,128)(2,1)} %copy-done.1, bf16[3072,1536]{1,0:T(8,128)(2,1)} %refs_3_.3, bf16[128,1536]{1,0:T(8,128)(2,1)S(1)} %shard_map.65.refs_4_.refs_2_), custom_call_target="tpu_custom_call" | custom-call | flops 1610612736 | bytes 7340032 | tf_op jit(solution)/shard_map/pallas_call | solution.py:155
  32.4 0.0 copy-start.8
  32.4 1.0 %copy-done.8 = f32[512,512]{1,0:T(8,128)} copy-done((f32[512,512]{1,0:T(8,128)}, f32[512,512]{1,0:T(8,128)S(1)}, u32[]{:S(2)}) %copy-start.8) | copy-done | bytes 1048600
  33.4 2.9 %collective-permute-done.7.refs_0_ = bf16[64,1536]{1,0:T(8,128)(2,1)S(1)} collective-permute-done((bf16[64,1536]{1,0:T(8,128)(2,1)}, bf16[64,1536]{1,0:T(8,128)(2,1)S(1)}, u32[]{:S(2)}, u32[]{:S(2)}) %collective-permute-start.7) | collective-permute-done | bytes 196640 | tf_op jit(solution)/shard_map/ppermute | solution.py:27
  36.3 0.0 collective-permute-done.4.refs_2_.refs_3_
  36.3 1.6 %collective-permute-start.8 = (bf16[64,1536]{1,0:T(8,128)(2,1)S(1)}, bf16[64,1536]{1,0:T(8,128)(2,1)}, u32[]{:S(2)}, u32[]{:S(2)}) collective-permute-start(bf16[64,1536]{1,0:T(8,128)(2,1)S(1)} %shard_map.67.refs_6_), channel_id=1, source_target_pairs={{0,2},{1,17},{2,0},{3,19},{4,6},{5,21},{6,4},{7,23},{8,10},{9,25},... | collective-permute-start | bytes 589832 | tf_op jit(solution)/shard_map/ppermute | solution.py:37
  37.9 0.5 collective-permute-start.6
  38.4 1.5 %collective-permute-start.9 = (bf16[64,1536]{1,0:T(8,128)(2,1)S(1)}, bf16[64,1536]{1,0:T(8,128)(2,1)}, u32[]{:S(2)}, u32[]{:S(2)}) collective-permute-start(bf16[64,1536]{1,0:T(8,128)(2,1)S(1)} %shard_map.67.refs_6_), channel_id=1, source_target_pairs={{0,16},{1,3},{2,18},{3,1},{4,20},{5,7},{6,22},{7,5},{8,24},{9,11},... | collective-permute-start | bytes 589832 | tf_op jit(solution)/shard_map/ppermute | solution.py:37
  39.9 4.4 %collective-permute-done.8.refs_7_ = bf16[64,1536]{1,0:T(8,128)(2,1)} collective-permute-done((bf16[64,1536]{1,0:T(8,128)(2,1)S(1)}, bf16[64,1536]{1,0:T(8,128)(2,1)}, u32[]{:S(2)}, u32[]{:S(2)}) %collective-permute-start.8) | collective-permute-done | bytes 196640 | tf_op jit(solution)/shard_map/ppermute | solution.py:37
  44.3 0.4 collective-permute-start.10
  44.7 0.0 copy-done.10
  44.7 0.1 copy.8.ids
  44.9 0.7 %constant_dynamic-slice_fusion.owners = s32[1,512]{1,0:T(1,128)S(1)} fusion(s32[8,512]{1,0:T(8,128)} %constant.24.clone, s32[]{:T(128)S(6)} %select_n.7), kind=kLoop, calls=%fused_computation.4 | loop fusion | bytes 4100 | tf_op jit(solution)/shard_map/dynamic_slice | solution.py:236
  45.6 0.0 collective-permute-done.5.refs_4_
  45.6 2.3 %collective-permute-done.9.refs_8_ = bf16[64,1536]{1,0:T(8,128)(2,1)} collective-permute-done((bf16[64,1536]{1,0:T(8,128)(2,1)S(1)}, bf16[64,1536]{1,0:T(8,128)(2,1)}, u32[]{:S(2)}, u32[]{:S(2)}) %collective-permute-start.9) | collective-permute-done | bytes 196640 | tf_op jit(solution)/shard_map/ppermute | solution.py:37
  47.9 0.0 collective-permute-done.6.refs_5_
  47.9 2.4 %collective-permute-done.10.refs_9_ = bf16[64,1536]{1,0:T(8,128)(2,1)} collective-permute-done((bf16[64,1536]{1,0:T(8,128)(2,1)}, bf16[64,1536]{1,0:T(8,128)(2,1)}, u32[]{:S(2)}, u32[]{:S(2)}) %collective-permute-start.10) | collective-permute-done | bytes 196640 | tf_op jit(solution)/shard_map/ppermute | solution.py:37
  50.3 0.0 copy-done.4
  50.3 2.4 %shard_map.68.mine = f32[512,128]{1,0:T(8,128)S(1)} custom-call(s32[2]{0:T(128)S(1)} %pad_add_fusion.refs_0_.info, s32[512,1]{1,0:T(8,128)S(1)} %copy.8.ids, s32[1,512]{1,0:T(1,128)S(1)} %constant_dynamic-slice_fusion.owners, bf16[512,1536]{1,0:T(8,128)(2,1)S(1)} %copy-done, bf16[64,1536]{1,0:T(8,128)(2,1)S(1)} %bitcast.13, bf16[128,1536]{1,0:T(8,128)(2,1)S(1)} %copy-done.4, ...), custom_call_target="tpu_custom_call" | custom-call | flops 805306368 | bytes 3145728 | tf_op jit(solution)/shard_map/pallas_call | solution.py:247
  52.8 0.1 collective-permute-start.11
  52.8 1.5 %collective-permute-done.11.theirs = f32[512,128]{1,0:T(8,128)S(1)} collective-permute-done((f32[512,128]{1,0:T(8,128)S(1)}, f32[512,128]{1,0:T(8,128)S(1)}, u32[]{:S(2)}, u32[]{:S(2)}) %collective-permute-start.11) | collective-permute-done | bytes 262176 | tf_op jit(solution)/shard_map/ppermute | solution.py:19
  54.4 0.0 copy-done.7
  54.4 3.6 %shard_map.69 = bf16[512,1536]{1,0:T(8,128)(2,1)} custom-call(s32[2]{0:T(128)S(1)} %pad_add_fusion.refs_0_.info, s32[512,1]{1,0:T(8,128)S(1)} %copy.8.ids, s32[1,512]{1,0:T(1,128)S(1)} %constant_dynamic-slice_fusion.owners, f32[512,128]{1,0:T(8,128)S(1)} %shard_map.68.mine, f32[512,128]{1,0:T(8,128)S(1)} %collective-permute-done.11.theirs, ...), custom_call_target="tpu_custom_call" | custom-call | flops 805306368 | bytes 6291456 | tf_op jit(solution)/shard_map/pallas_call | solution.py:258
  (11 shorter events, 0.0 us)
Async XLA Ops:
  0.0 11.1 %copy-start = (bf16[512,1536]{1,0:T(8,128)(2,1)S(1)}, bf16[512,1536]{1,0:T(8,128)(2,1)}, u32[]{:S(2)}) copy-start(bf16[512,1536]{1,0:T(8,128)(2,1)} %latent.1) | copy-start | bytes 4718596
  0.0 11.1 %collective-permute-start.3 = (bf16[512,1536]{1,0:T(8,128)(2,1)}, bf16[512,1536]{1,0:T(8,128)(2,1)S(1)}, u32[]{:S(2)}, u32[]{:S(2)}) collective-permute-start(bf16[512,1536]{1,0:T(8,128)(2,1)} %latent.1), channel_id=1, source_target_pairs={{0,1},{1,0},{2,3},{3,2},{4,5},{5,4},{6,7},{7,6},{8,9},{9,8},{10,11... | collective-permute-start | bytes 4718600 | tf_op jit(solution)/shard_map/ppermute | solution.py:19
  3.0 16.0 %collective-permute-start.2 = (bf16[64,1536]{1,0:T(8,128)(2,1)}, bf16[64,1536]{1,0:T(8,128)(2,1)}, u32[]{:S(2)}, u32[]{:S(2)}) collective-permute-start(bf16[64,1536]{1,0:T(8,128)(2,1)} %pad_maximum_fusion.1.refs_4_), channel_id=1, source_target_pairs={{0,12},{2,14},{4,0},{6,2},{8,4},{10,6},{12,8},{14,10},{1,13},{3,15... | collective-permute-start | bytes 589832 | tf_op jit(solution)/shard_map/ppermute | solution.py:27
  7.7 11.3 %collective-permute-start.1 = (bf16[64,1536]{1,0:T(8,128)(2,1)}, bf16[64,1536]{1,0:T(8,128)(2,1)}, u32[]{:S(2)}, u32[]{:S(2)}) collective-permute-start(bf16[64,1536]{1,0:T(8,128)(2,1)} %pad_maximum_fusion.1.refs_4_), channel_id=1, source_target_pairs={{0,4},{2,6},{4,8},{6,10},{8,12},{10,14},{12,0},{14,2},{1,5},{3,7},... | collective-permute-start | bytes 589832 | tf_op jit(solution)/shard_map/ppermute | solution.py:27
  9.5 11.3 %collective-permute-start = (bf16[128,1536]{1,0:T(8,128)(2,1)}, bf16[128,1536]{1,0:T(8,128)(2,1)S(1)}, u32[]{:S(2)}, u32[]{:S(2)}) collective-permute-start(bf16[128,1536]{1,0:T(8,128)(2,1)} %pad_maximum_fusion), channel_id=1, source_target_pairs={{0,2},{2,0},{4,6},{6,4},{8,10},{10,8},{12,14},{14,12},{1,3},{3,1},... | collective-permute-start | bytes 1179656 | tf_op jit(solution)/shard_map/ppermute | solution.py:23
  11.1 7.9 %copy-start.1 = (bf16[512,1536]{1,0:T(8,128)(2,1)}, bf16[512,1536]{1,0:T(8,128)(2,1)S(1)}, u32[]{:S(2)}) copy-start(bf16[512,1536]{1,0:T(8,128)(2,1)S(1)} %collective-permute-done.3.refs_2_) | copy-start | bytes 4718596
  20.8 0.8 %copy-start.2 = (bf16[128,1536]{1,0:T(8,128)(2,1)}, bf16[128,1536]{1,0:T(8,128)(2,1)S(1)}, u32[]{:S(2)}) copy-start(bf16[128,1536]{1,0:T(8,128)(2,1)S(1)} %collective-permute-done.refs_3_.refs_1_) | copy-start | bytes 1179652
  21.6 1.0 %copy-start.3 = (bf16[128,1536]{1,0:T(8,128)(2,1)S(1)}, bf16[128,1536]{1,0:T(8,128)(2,1)}, u32[]{:S(2)}) copy-start(bf16[128,1536]{1,0:T(8,128)(2,1)} %copy-done.2) | copy-start | bytes 1179652
  23.6 21.1 %copy-start.10 = (s32[512,1]{0,1:T(1,128)S(1)}, s32[512,1]{0,1:T(1,128)}, u32[]{:S(2)}) copy-start(s32[512,1]{0,1:T(1,128)} %param.7) | copy-start | bytes 6148
  23.6 26.7 %copy-start.4 = (bf16[128,1536]{1,0:T(8,128)(2,1)S(1)}, bf16[128,1536]{1,0:T(8,128)(2,1)}, u32[]{:S(2)}) copy-start(bf16[128,1536]{1,0:T(8,128)(2,1)} %copy-done.2) | copy-start | bytes 1179652
  23.6 26.7 %copy-start.6 = (bf16[1,1536,64]{1,2,0:T(8,128)(2,1)S(1)}, bf16[1,1536,64]{1,2,0:T(8,128)(2,1)}, u32[]{:S(2)}) copy-start(bf16[1,1536,64]{1,2,0:T(8,128)(2,1)} %param.9) | copy-start | bytes 589828
  23.6 12.7 %collective-permute-start.4 = (bf16[128,1536]{1,0:T(8,128)(2,1)S(1)}, bf16[128,1536]{1,0:T(8,128)(2,1)S(1)}, u32[]{:S(2)}, u32[]{:S(2)}) collective-permute-start(bf16[128,1536]{1,0:T(8,128)(2,1)S(1)} %shard_map.65.refs_4_.refs_2_), channel_id=1, source_target_pairs={{0,2},{1,17},{2,0},{3,19},{4,6},{5,21},{6,4},{7,23},{8,10},{9,25},... | collective-permute-start | bytes 1179656 | tf_op jit(solution)/shard_map/ppermute | solution.py:37
  25.2 11.1 %collective-permute-start.7 = (bf16[64,1536]{1,0:T(8,128)(2,1)}, bf16[64,1536]{1,0:T(8,128)(2,1)S(1)}, u32[]{:S(2)}, u32[]{:S(2)}) collective-permute-start(bf16[64,1536]{1,0:T(8,128)(2,1)} %pad_maximum_fusion.1.refs_4_), channel_id=1, source_target_pairs={{0,8},{2,10},{4,12},{6,14},{8,0},{10,2},{12,4},{14,6},{1,9},{3,11}... | collective-permute-start | bytes 589832 | tf_op jit(solution)/shard_map/ppermute | solution.py:27
  26.0 19.6 %collective-permute-start.5 = (bf16[128,1536]{1,0:T(8,128)(2,1)S(1)}, bf16[128,1536]{1,0:T(8,128)(2,1)}, u32[]{:S(2)}, u32[]{:S(2)}) collective-permute-start(bf16[128,1536]{1,0:T(8,128)(2,1)S(1)} %shard_map.65.refs_4_.refs_2_), channel_id=1, source_target_pairs={{0,16},{1,3},{2,18},{3,1},{4,20},{5,7},{6,22},{7,5},{8,24},{9,11},... | collective-permute-start | bytes 1179656 | tf_op jit(solution)/shard_map/ppermute | solution.py:37
  32.4 1.0 %copy-start.8 = (f32[512,512]{1,0:T(8,128)}, f32[512,512]{1,0:T(8,128)S(1)}, u32[]{:S(2)}) copy-start(f32[512,512]{1,0:T(8,128)S(1)} %get-tuple-element.12.right) | copy-start | bytes 3145732
  36.3 8.0 %collective-permute-start.8 = (bf16[64,1536]{1,0:T(8,128)(2,1)S(1)}, bf16[64,1536]{1,0:T(8,128)(2,1)}, u32[]{:S(2)}, u32[]{:S(2)}) collective-permute-start(bf16[64,1536]{1,0:T(8,128)(2,1)S(1)} %shard_map.67.refs_6_), channel_id=1, source_target_pairs={{0,2},{1,17},{2,0},{3,19},{4,6},{5,21},{6,4},{7,23},{8,10},{9,25},... | collective-permute-start | bytes 589832 | tf_op jit(solution)/shard_map/ppermute | solution.py:37
  37.9 10.0 %collective-permute-start.6 = (bf16[128,1536]{1,0:T(8,128)(2,1)S(1)}, bf16[128,1536]{1,0:T(8,128)(2,1)}, u32[]{:S(2)}, u32[]{:S(2)}) collective-permute-start(bf16[128,1536]{1,0:T(8,128)(2,1)S(1)} %collective-permute-done.4.refs_2_.refs_3_), channel_id=1, source_target_pairs={{0,16},{1,3},{2,18},{3,1},{4,20},{5,7},{6,22},{7,5},{8,24},{9,11},... | collective-permute-start | bytes 1179656 | tf_op jit(solution)/shard_map/ppermute | solution.py:37
  38.4 9.5 %collective-permute-start.9 = (bf16[64,1536]{1,0:T(8,128)(2,1)S(1)}, bf16[64,1536]{1,0:T(8,128)(2,1)}, u32[]{:S(2)}, u32[]{:S(2)}) collective-permute-start(bf16[64,1536]{1,0:T(8,128)(2,1)S(1)} %shard_map.67.refs_6_), channel_id=1, source_target_pairs={{0,16},{1,3},{2,18},{3,1},{4,20},{5,7},{6,22},{7,5},{8,24},{9,11},... | collective-permute-start | bytes 589832 | tf_op jit(solution)/shard_map/ppermute | solution.py:37
  44.3 6.0 %collective-permute-start.10 = (bf16[64,1536]{1,0:T(8,128)(2,1)}, bf16[64,1536]{1,0:T(8,128)(2,1)}, u32[]{:S(2)}, u32[]{:S(2)}) collective-permute-start(bf16[64,1536]{1,0:T(8,128)(2,1)} %collective-permute-done.8.refs_7_), channel_id=1, source_target_pairs={{0,16},{1,3},{2,18},{3,1},{4,20},{5,7},{6,22},{7,5},{8,24},{9,11},... | collective-permute-start | bytes 589832 | tf_op jit(solution)/shard_map/ppermute | solution.py:37
  45.6 8.8 %copy-start.5 = (f32[512,1024]{1,0:T(8,128)S(1)}, f32[512,1024]{1,0:T(8,128)}, u32[]{:S(2)}) copy-start(f32[512,1024]{1,0:T(8,128)} %get-tuple-element.11.left) | copy-start | bytes 6291460
  45.6 8.8 %copy-start.7 = (bf16[1,64,1536]{2,1,0:T(8,128)(2,1)S(1)}, bf16[1,64,1536]{2,1,0:T(8,128)(2,1)}, u32[]{:S(2)}) copy-start(bf16[1,64,1536]{2,1,0:T(8,128)(2,1)} %param.10) | copy-start | bytes 589828
  45.6 8.8 %copy-start.9 = (f32[512,512]{1,0:T(8,128)S(1)}, f32[512,512]{1,0:T(8,128)}, u32[]{:S(2)}) copy-start(f32[512,512]{1,0:T(8,128)} %copy-done.8) | copy-start | bytes 3145732
  52.8 1.6 %collective-permute-start.11 = (f32[512,128]{1,0:T(8,128)S(1)}, f32[512,128]{1,0:T(8,128)S(1)}, u32[]{:S(2)}, u32[]{:S(2)}) collective-permute-start(f32[512,128]{1,0:T(8,128)S(1)} %shard_map.68.mine), channel_id=1, source_target_pairs={{0,1},{1,0},{2,3},{3,2},{4,5},{5,4},{6,7},{7,6},{8,9},{9,8},{10,11... | collective-permute-start | bytes 786440 | tf_op jit(solution)/shard_map/ppermute | solution.py:19

commit v4 on v3

v4 whole, which is shorter than its diff:
```python
import jax
import jax.numpy as jnp
import numpy as np
from jax import lax
from jax.experimental import pallas as pl
from jax.experimental.pallas import tpu as pltpu
from jax.sharding import PartitionSpec as P

MIB = 1024 * 1024
CHUNK = 512
AXES = ("replica", "shard", "tensor")
WAVES = ((1, 3), (2,))
BASE_COST = 1000
BASE_LIMIT = 44
LAY_OUT_LIMIT = 56
SMEM = pl.BlockSpec(memory_space=pltpu.SMEM)
VMEM = pl.BlockSpec(memory_space=pltpu.VMEM)
ANY = pl.BlockSpec(memory_space=pl.ANY)
TOKEN = jax.ShapeDtypeStruct((8, 128), jnp.float32)


def swap(value, axis):
    return lax.ppermute(value, axis, [(0, 1), (1, 0)])


def neighbour(value, shards):
    return lax.ppermute(value, "shard", [(i, i ^ 1) for i in range(shards)])


def along_line(value, shards, step):
    return lax.ppermute(value, "shard", [(i, (i + 2 * step) % shards) for i in range(shards)])


def in_plane(value, shards, first):
    pairs = []
    for r in range(2):
        for s in range(shards):
            for t in range(2):
                to_r, to_s = (r, s ^ 1) if (t == 0) == first else (r ^ 1, s)
                pairs.append(((r * shards + s) * 2 + t, (to_r * shards + to_s) * 2 + t))
    return lax.ppermute(value, AXES, pairs)


def call(kernel, out_shape, in_specs, limit, scratch=(), flops=0, moved=0):
    return pl.pallas_call(
        kernel,
        out_shape=out_shape,
        in_specs=in_specs,
        out_specs=jax.tree.map(lambda _: VMEM, out_shape),
        scratch_shapes=list(scratch),
        compiler_params=pltpu.CompilerParams(vmem_limit_bytes=limit * MIB),
        cost_estimate=pl.CostEstimate(flops=flops, bytes_accessed=moved, transcendentals=0),
    )


def owner_table(shards, rank):
    table = []
    for index in range(shards):
        sources = [(index - 2 * step) % shards for step in (0, *WAVES[0], *WAVES[1])]
        table.append([a for s in sources for a in (s, s ^ 1) for _ in range(rank)])
    return np.array(table, np.int32)


def pack(pieces, *after):
    rows, width = pieces[0].shape
    count = len(pieces)

    def kernel(*refs):
        out, token = refs[-2:]
        for number in range(count):
            out[number * rows : (number + 1) * rows, :] = refs[number][...]
        token[...] = jnp.zeros_like(token)

    return call(
        kernel,
        [jax.ShapeDtypeStruct((count * rows, width), pieces[0].dtype), TOKEN],
        [VMEM] * count + [ANY] * len(after),
        4,
    )(*pieces, *after)


def lay_out(down, up, piece, both, sems):
    rank = down.shape[0]
    half = rank // 2
    mine = pl.ds(pl.multiple_of(lax.axis_index("replica") * half, half), half)
    pairs = (
        (down.at[mine, :], piece.at[pl.ds(0, half), :]),
        (up.at[mine, :], piece.at[pl.ds(half, half), :]),
        (down, both.at[pl.ds(0, rank), :]),
        (up, both.at[pl.ds(rank, rank), :]),
    )
    copies = [pltpu.make_async_copy(*pair, sems.at[n]) for n, pair in enumerate(pairs)]
    for copy in copies:
        copy.start()
    for copy in copies:
        copy.wait()


def fill_own(info, which, own, beside, stack):
    rank = own.shape[0]
    half = rank // 2
    mine = pl.multiple_of(info[0] * half, half)
    rest = pl.multiple_of((1 - info[0]) * half, half)
    stack[0:half, :] = own[pl.ds(mine, half), :]
    stack[half:rank, :] = own[pl.ds(rest, half), :]
    stack[rank : rank + half, :] = beside[pl.ds(which * rank + mine, half), :]
    stack[rank + half : 2 * rank, :] = beside[pl.ds(which * rank + rest, half), :]


def fill_wave(info, which, pieces, half, stack, top):
    line, first, second, corner = pieces
    for number in range(line.shape[0] // (2 * half)):
        rows = slice((2 * number + which) * half, (2 * number + which + 1) * half)
        stack[top : top + half, :] = line[rows, :]
        place = pl.multiple_of(top + (2 - info[1]) * half, half)
        stack[pl.ds(place, half), :] = first[rows, :]
        place = pl.multiple_of(top + (1 + info[1]) * half, half)
        stack[pl.ds(place, half), :] = second[rows, :]
        stack[top + 3 * half : top + 4 * half, :] = corner[rows, :]
        top += 4 * half


def masked_products(ids, owners, latent, stack, width):
    total = None
    for begin in range(0, stack.shape[0], CHUNK):
        rows = slice(begin, min(begin + CHUNK, stack.shape[0]))
        part = lax.dot_general(
            latent[...],
            stack[rows, :],
            (((1,), (1,)), ((), ())),
            preferred_element_type=jnp.float32,
        )
        part = jnp.where(ids[...] == owners[:, rows], part, 0.0)
        for lane in range(0, part.shape[1], width):
            fold = part[:, lane : lane + width]
            total = fold if total is None else total + fold
    return total


def down_whole_kernel(ids, owners, latent, stack, out):
    out[...] = masked_products(ids, owners, latent, stack, out.shape[1])


def down_first_kernel(info, ids, owners, latent, own, beside, *refs):
    *pieces, _, out, stack = refs
    half = own.shape[0] // 2
    fill_own(info, 0, own, beside, stack)
    fill_wave(info, 0, pieces, half, stack, 4 * half)
    out[...] = masked_products(ids, owners, latent, stack, out.shape[1])


def down_last_kernel(info, ids, owners, latent, earlier, *refs):
    *pieces, out, stack = refs
    half = stack.shape[0] // 4
    fill_wave(info, 0, pieces, half, stack, 0)
    out[...] = earlier[...] + masked_products(ids, owners, latent, stack, out.shape[1])


def base_kernel(info, own, other, weight, _, out, token, weight_ref, sems, *, skip):
    width = own.shape[1]
    place = pl.ds(skip, out.shape[1])
    copies = []
    for part, owner in ((0, info[1]), (1, 1 - info[1])):
        source = pl.ds(pl.multiple_of(owner * width, width), width)
        copies.append(
            pltpu.make_async_copy(weight.at[source, place], weight_ref.at[part], sems.at[part])
        )
    for copy in copies:
        copy.start()
    token[...] = jnp.zeros_like(token)
    copies[0].wait()
    total = jnp.dot(own[...], weight_ref[0], preferred_element_type=jnp.float32)
    copies[1].wait()
    out[...] = total + jnp.dot(other[...], weight_ref[1], preferred_element_type=jnp.float32)


def base(info, latent, other, weight, after, number):
    rows, half_width = latent.shape
    return pl.pallas_call(
        lambda *refs: base_kernel(*refs, skip=number * CHUNK),
        out_shape=[
            jax.ShapeDtypeStruct((rows, CHUNK), jnp.float32),
            TOKEN,
        ],
        in_specs=[SMEM, VMEM, VMEM, ANY, ANY],
        out_specs=[VMEM, VMEM],
        scratch_shapes=[
            pltpu.VMEM((2, half_width, CHUNK), weight.dtype),
            pltpu.SemaphoreType.DMA((2,)),
        ],
        compiler_params=pltpu.CompilerParams(vmem_limit_bytes=BASE_LIMIT * MIB),
        cost_estimate=pl.CostEstimate(
            flops=BASE_COST, bytes_accessed=BASE_COST, transcendentals=0
        ),
    )(info, latent, other, weight, after)


def up_kernel(info, ids, owners, mine, theirs, *refs):
    tiles = refs[-1].shape[0]
    tile = refs[-1].shape[2]
    parts, pieces = refs[:tiles], refs[tiles:-5]
    out, stack, wide, sems, staged = refs[-5:]
    if len(pieces) == 1:
        stack[...] = pieces[0][...]
    else:
        half = pieces[0].shape[0] // 2
        fill_own(info, 1, pieces[0], pieces[1], stack)
        top = 4 * half
        for wave in range(2):
            fill_wave(info, 1, pieces[4 * wave + 2 : 4 * wave + 6], half, stack, top)
            top += pieces[4 * wave + 2].shape[0] * 2
    lowrank = (mine[...] + theirs[...]).astype(jnp.bfloat16)
    zeros = jnp.zeros_like(lowrank)
    width = lowrank.shape[1]
    for lane in range(0, wide.shape[1], width):
        lanes = slice(lane, lane + width)
        wide[:, lanes] = jnp.where(ids[...] == owners[:, lanes], lowrank, zeros)
    copies = []
    for number in range(tiles):
        place = pl.ds(number * tile, tile)
        delta = jnp.dot(wide[...], stack[:, place], preferred_element_type=jnp.float32)
        total = parts[number][...] + delta.astype(jnp.bfloat16).astype(jnp.float32)
        staged[number] = total.astype(out.dtype)
        copies.append(
            pltpu.make_async_copy(staged.at[number], out.at[:, place], sems.at[number])
        )
        copies[-1].start()
    for copy in copies:
        copy.wait()


def on_device(latent, row_adapter_index, shared_weight, adapter_down_weight, adapter_up_weight):
    rows, half_width = latent.shape
    out_width = shared_weight.shape[1]
    local_adapters, _, rank = adapter_down_weight.shape
    shards = lax.axis_size("shard")
    adapters = shards * local_adapters
    columns = adapters * rank
    index, replica = lax.axis_index("shard"), lax.axis_index("replica")
    info = jnp.stack([replica, lax.axis_index("tensor")]).astype(jnp.int32)
    tiles = out_width // CHUNK
    other = swap(latent, "tensor")
    down = jnp.swapaxes(adapter_down_weight, 1, 2).reshape(local_adapters * rank, half_width)
    up = adapter_up_weight.reshape(local_adapters * rank, out_width)
    ids = row_adapter_index
    routed = shards == 8 and local_adapters == 1 and lax.axis_size("replica") == 2
    lowrank = jax.ShapeDtypeStruct((rows, 2 * rank), jnp.float32)
    if routed:
        half = rank // 2
        piece, both = pl.pallas_call(
            lay_out,
            out_shape=[
                jax.ShapeDtypeStruct((rank, half_width), latent.dtype),
                jax.ShapeDtypeStruct((2 * rank, half_width), latent.dtype),
            ],
            in_specs=[ANY, ANY],
            out_specs=[ANY, ANY],
            scratch_shapes=[pltpu.SemaphoreType.DMA((4,))],
            compiler_params=pltpu.CompilerParams(vmem_limit_bytes=LAY_OUT_LIMIT * MIB),
        )(down, up)
        line = {step: along_line(piece, shards, step) for wave in WAVES for step in wave}
        beside = neighbour(both, shards)
        parts = []
        token = info
        for number in range(tiles - 1):
            part, token = base(info, latent, other, shared_weight, token, number)
            parts.append(part)
        held, token = pack([line[step] for step in WAVES[0]], token, beside)
        part, token = base(info, latent, other, shared_weight, token, tiles - 1)
        parts.append(part)
        first, second = in_plane(held, shards, True), in_plane(held, shards, False)
        wave_one = [held, first, second, in_plane(first, shards, False)]
        held, token = pack([line[step] for step in WAVES[1]], token, first)
        first, second = in_plane(held, shards, True), in_plane(held, shards, False)
        wave_two = [held, first, second, in_plane(first, shards, False)]
        owners = jnp.asarray(owner_table(shards, rank))[index][None, :]
        split = 2 * rank * (1 + len(WAVES[0]))
        mine = call(
            down_first_kernel,
            lowrank,
            [SMEM] + [VMEM] * 9 + [ANY],
            16,
            [pltpu.VMEM((split, half_width), latent.dtype)],
        )(info, ids, owners[:, :split], latent, down, beside, *wave_one, token)
        mine = call(
            down_last_kernel,
            lowrank,
            [SMEM] + [VMEM] * 8,
            16,
            [pltpu.VMEM((columns - split, half_width), latent.dtype)],
        )(info, ids, owners[:, split:], latent, mine, *wave_two)
        up_pieces = [up, beside, *wave_one, *wave_two]
    else:
        parts = []
        token = info
        for number in range(tiles):
            part, token = base(info, latent, other, shared_weight, token, number)
            parts.append(part)
        owners = jnp.repeat(jnp.arange(adapters, dtype=jnp.int32), rank)[None, :]
        mine = call(down_whole_kernel, lowrank, [VMEM] * 4, 48)(
            ids, owners, latent, lax.all_gather(down, "shard", axis=0, tiled=True)
        )
        up_pieces = [lax.all_gather(up, "shard", axis=0, tiled=True)]
    theirs = swap(mine, "tensor")

    return pl.pallas_call(
        up_kernel,
        out_shape=jax.ShapeDtypeStruct((rows, out_width), latent.dtype),
        in_specs=[SMEM] + [VMEM] * (4 + tiles + len(up_pieces)),
        out_specs=ANY,
        scratch_shapes=[
            pltpu.VMEM((columns, out_width), latent.dtype),
            pltpu.VMEM((rows, columns), latent.dtype),
            pltpu.SemaphoreType.DMA((tiles,)),
            pltpu.VMEM((tiles, rows, CHUNK), latent.dtype),
        ],
        compiler_params=pltpu.CompilerParams(vmem_limit_bytes=(24 if routed else 56) * MIB),
    )(info, ids, owners, mine, theirs, *parts, *up_pieces)


def solution(mesh):
    return jax.shard_map(
        on_device,
        mesh=mesh,
        in_specs=(
            P(("replica", "shard"), "tensor"),
            P(("replica", "shard"), None),
            P(None, "tensor"),
            P("shard", "tensor", None),
            P("shard", None, "tensor"),
        ),
        out_specs=P(("replica", "shard"), "tensor"),
        check_vma=False,
    )
```

time: 58.3 us -> 70.5 us (1.21)
  Pallas kernels: 19.9 us -> 39.3 us
  waiting for transfers between devices: 15.3 us -> 10.5 us
  other arithmetic: 2.57 us -> 0.07 us
  local copies, waits for them, and re-layouts: 5.45 us -> 6.65 us
  starting transfers between devices: 14.6 us -> 13.4 us
    pallas_call x6 -> x9, Pallas kernels: 19.9 us -> 39.3 us  [the longest x1 19 us: on_device(): pl.pallas_call(lay_out, out_shape=[jax.ShapeDtypeStruct((rank, half_width...]
    ppermute x3, waiting for transfers between devices: 2.9 us -> 0.01 us  [along_line(): lax.ppermute(value, 'shard', [(i, (i + 2 * step) % shards) for i in range...]
    concatenate x2 -> x0, other arithmetic: 2.49 us -> none  [the longest x1 1.8 us: on_device(): beside = neighbour(jnp.concatenate([down, up]), shards)]
    dynamic_slice x2 -> x0, local copies, waits for them, and re-layouts: 1.83 us -> none  [the longest x1 0.93 us: on_device(): lax.dynamic_slice_in_dim(down, replica * half, half, axis=0)]
    ppermute x1, waiting for transfers between devices: 1.8 us -> 0.01 us  [neighbour(): return lax.ppermute(value, 'shard', [(i, i ^ 1) for i in range(shards)])]
    unnamed x23 -> x25, local copies, waits for them, and re-layouts: 2.89 us -> 4.44 us
    slice x0 -> x2, local copies, waits for them, and re-layouts: none -> 1.48 us  [the longest x1 0.77 us: on_device(): owners[:, split:]]
    ppermute x6, starting transfers between devices: 7.06 us -> 5.68 us  [in_plane(): return lax.ppermute(value, AXES, pairs)]
  transfers between devices with their start and end apart: 12 -> 12, of which waited for: 6 -> 3; matrix products, arithmetic and copies ran while one was open for 9% -> 3% of each run, Pallas kernels for 22% -> 49%
where the time goes in v4:
time: 70.5 us; the launch traced here: 70.1 us
  Pallas kernels  39.3 us (56%)
  starting transfers between devices  13.4 us (19%)
  waiting for transfers between devices  10.5 us (15%)
  local copies, waits for them, and re-layouts  6.65 us (9%)
    pallas_call x1, Pallas kernels, on_device(): pl.pallas_call(lay_out, out_shape=[jax.ShapeDtypeStruct((rank, half_width...  19 us
    pallas_call x3, Pallas kernels, base(): pl.pallas_call(lambda *refs: base_kernel(*refs, skip=number * CHUNK), out...  12.7 us
    ppermute x6, waiting for transfers between devices, in_plane(): return lax.ppermute(value, AXES, pairs)  9.73 us
    ppermute x6, starting transfers between devices, in_plane(): return lax.ppermute(value, AXES, pairs)  5.68 us
    ppermute x3, starting transfers between devices, along_line(): lax.ppermute(value, 'shard', [(i, (i + 2 * step) % shards) for i in range...  4.63 us
    unnamed x25, local copies, waits for them, and re-layouts  4.44 us
    pallas_call x1, Pallas kernels, on_device(): pl.pallas_call(up_kernel, out_shape=jax.ShapeDtypeStruct((rows, out_width...  3.27 us
    ppermute x1, starting transfers between devices, neighbour(): return lax.ppermute(value, 'shard', [(i, i ^ 1) for i in range(shards)])  2.58 us
  transfers between devices with their start and end apart: 12, of which 3 were waited for; matrix products, arithmetic and copies ran while one was open for 3% of the time, Pallas kernels for 49%

profile of v4, /device:TPU:0, one launch (start us, length us, event | category | flops | bytes accessed | tf_op | source)
XLA Modules:
  0.0 70.1 jit_solution(11085888016951843785)
XLA Ops:
  0.0 0.5 collective-permute-start.3
  0.5 19.0 %shard_map.64 = (bf16[64,1536]{1,0:T(8,128)(2,1)}, bf16[128,1536]{1,0:T(8,128)(2,1)}) custom-call(bf16[64,1536]{1,0:T(8,128)(2,1)} %bitcast.6, bf16[64,1536]{1,0:T(8,128)(2,1)} %bitcast.8), custom_call_target="tpu_custom_call" | custom-call | tf_op jit(solution)/shard_map/pallas_call | solution.py:250
  19.5 2.6 %collective-permute-start = (bf16[128,1536]{1,0:T(8,128)(2,1)}, bf16[128,1536]{1,0:T(8,128)(2,1)S(1)}, u32[]{:S(2)}, u32[]{:S(2)}) collective-permute-start(bf16[128,1536]{1,0:T(8,128)(2,1)} %get-tuple-element.17), channel_id=1, source_target_pairs={{0,2},{2,0},{4,6},{6,4},{8,10},{10,8},{12,14},{14,12},{1,3},{3,1},... | collective-permute-start | bytes 1179656 | tf_op jit(solution)/shard_map/ppermute | solution.py:27
  22.0 3.6 %collective-permute-start.2 = (bf16[64,1536]{1,0:T(8,128)(2,1)}, bf16[64,1536]{1,0:T(8,128)(2,1)S(1)}, u32[]{:S(2)}, u32[]{:S(2)}) collective-permute-start(bf16[64,1536]{1,0:T(8,128)(2,1)} %get-tuple-element.18), channel_id=1, source_target_pairs={{0,12},{2,14},{4,0},{6,2},{8,4},{10,6},{12,8},{14,10},{1,13},{3,15... | collective-permute-start | bytes 589832 | tf_op jit(solution)/shard_map/ppermute | solution.py:31
  25.6 0.0 collective-permute-start.1
  25.7 0.1 pad_add_fusion.refs_0_.refs_4_.info
  25.7 0.0 collective-permute-done.3.refs_2_
  25.7 1.4 %copy-done = bf16[512,1536]{1,0:T(8,128)(2,1)S(1)} copy-done((bf16[512,1536]{1,0:T(8,128)(2,1)S(1)}, bf16[512,1536]{1,0:T(8,128)(2,1)}, u32[]{:S(2)}) %copy-start) | copy-done | bytes 1572888
  27.1 4.2 %shard_map.65 = (f32[512,512]{1,0:T(8,128)S(1)}, f32[8,128]{1,0:T(8,128)S(1)}) custom-call(s32[2]{0:T(128)S(1)} %pad_add_fusion.refs_0_.refs_4_.info, bf16[512,1536]{1,0:T(8,128)(2,1)S(1)} %copy-done, bf16[512,1536]{1,0:T(8,128)(2,1)S(1)} %collective-permute-done.3.refs_2_, bf16[3072,1536]{1,0:T(8,128)(2,1)} %refs_3_.5, s32[2]{0:T(128)S(1)} %pad_add_fusion.refs_0_.refs_4_.info), custom_call_target="tpu_custom_call" | custom-call | flops 1000 | bytes 1000 | tf_op jit(solution)/shard_map/pallas_call | solution.py:179
  31.4 0.0 copy-start.2
  31.4 0.0 copy-start.11
  31.4 4.2 %shard_map.66 = (f32[512,512]{1,0:T(8,128)S(1)}, f32[8,128]{1,0:T(8,128)S(1)}) custom-call(s32[2]{0:T(128)S(1)} %pad_add_fusion.refs_0_.refs_4_.info, bf16[512,1536]{1,0:T(8,128)(2,1)S(1)} %copy-done, bf16[512,1536]{1,0:T(8,128)(2,1)S(1)} %collective-permute-done.3.refs_2_, bf16[3072,1536]{1,0:T(8,128)(2,1)} %refs_3_.5, f32[8,128]{1,0:T(8,128)S(1)} %get-tuple-element.19.refs_4_), custom_call_target="tpu_custom_call" | custom-call | flops 1000 | bytes 1000 | tf_op jit(solution)/shard_map/pallas_call | solution.py:179
  35.7 1.0 %copy-done.4 = f32[512,512]{1,0:T(8,128)} copy-done((f32[512,512]{1,0:T(8,128)}, f32[512,512]{1,0:T(8,128)S(1)}, u32[]{:S(2)}) %copy-start.4) | copy-done | bytes 1048600
  36.7 0.0 collective-permute-done.2.refs_1_
  36.7 0.0 collective-permute-done.1.refs_0_
  36.7 0.0 collective-permute-done.refs_3_.beside.refs_4_
  36.7 0.8 %shard_map.67 = (bf16[128,1536]{1,0:T(8,128)(2,1)}, f32[8,128]{1,0:T(8,128)S(1)}) custom-call(bf16[64,1536]{1,0:T(8,128)(2,1)S(1)} %collective-permute-done.1.refs_0_, bf16[64,1536]{1,0:T(8,128)(2,1)S(1)} %collective-permute-done.2.refs_1_, f32[8,128]{1,0:T(8,128)S(1)} %get-tuple-element.20.refs_2_, ...), custom_call_target="tpu_custom_call" | custom-call | tf_op jit(solution)/shard_map/pallas_call | solution.py:74
  37.4 0.5 collective-permute-start.4
  38.0 1.0 %collective-permute-start.7 = (bf16[64,1536]{1,0:T(8,128)(2,1)S(1)}, bf16[64,1536]{1,0:T(8,128)(2,1)S(1)}, u32[]{:S(2)}, u32[]{:S(2)}) collective-permute-start(bf16[64,1536]{1,0:T(8,128)(2,1)S(1)} %copy-done.11), channel_id=1, source_target_pairs={{0,8},{2,10},{4,12},{6,14},{8,0},{10,2},{12,4},{14,6},{1,9},{3,11}... | collective-permute-start | bytes 589832 | tf_op jit(solution)/shard_map/ppermute | solution.py:31
  39.0 1.5 %collective-permute-start.5 = (bf16[128,1536]{1,0:T(8,128)(2,1)}, bf16[128,1536]{1,0:T(8,128)(2,1)}, u32[]{:S(2)}, u32[]{:S(2)}) collective-permute-start(bf16[128,1536]{1,0:T(8,128)(2,1)} %get-tuple-element.21.refs_0_.refs_5_), channel_id=1, source_target_pairs={{0,16},{1,3},{2,18},{3,1},{4,20},{5,7},{6,22},{7,5},{8,24},{9,11},... | collective-permute-start | bytes 1179656 | tf_op jit(solution)/shard_map/ppermute | solution.py:41
  40.5 4.2 %shard_map.68 = (f32[512,512]{1,0:T(8,128)S(1)}, f32[8,128]{1,0:T(8,128)S(1)}) custom-call(s32[2]{0:T(128)S(1)} %pad_add_fusion.refs_0_.refs_4_.info, bf16[512,1536]{1,0:T(8,128)(2,1)S(1)} %copy-done, bf16[512,1536]{1,0:T(8,128)(2,1)S(1)} %collective-permute-done.3.refs_2_, bf16[3072,1536]{1,0:T(8,128)(2,1)} %refs_3_.5, f32[8,128]{1,0:T(8,128)S(1)} %get-tuple-element.22.refs_4_), custom_call_target="tpu_custom_call" | custom-call | flops 1000 | bytes 1000 | tf_op jit(solution)/shard_map/pallas_call | solution.py:179
  44.7 0.9 %copy-done.6 = f32[512,512]{1,0:T(8,128)} copy-done((f32[512,512]{1,0:T(8,128)}, f32[512,512]{1,0:T(8,128)S(1)}, u32[]{:S(2)}) %copy-start.6) | copy-done | bytes 1048600
  45.7 3.5 %collective-permute-done.4.refs_2_.refs_1_.refs_6_ = bf16[128,1536]{1,0:T(8,128)(2,1)} collective-permute-done((bf16[128,1536]{1,0:T(8,128)(2,1)}, bf16[128,1536]{1,0:T(8,128)(2,1)}, u32[]{:S(2)}, u32[]{:S(2)}) %collective-permute-start.4) | collective-permute-done | bytes 393248 | tf_op jit(solution)/shard_map/ppermute | solution.py:41
  49.2 2.0 %collective-permute-start.6 = (bf16[128,1536]{1,0:T(8,128)(2,1)}, bf16[128,1536]{1,0:T(8,128)(2,1)S(1)}, u32[]{:S(2)}, u32[]{:S(2)}) collective-permute-start(bf16[128,1536]{1,0:T(8,128)(2,1)} %collective-permute-done.4.refs_2_.refs_1_.refs_6_), channel_id=1, source_target_pairs={{0,16},{1,3},{2,18},{3,1},{4,20},{5,7},{6,22},{7,5},{8,24},{9,11},... | collective-permute-start | bytes 1179656 | tf_op jit(solution)/shard_map/ppermute | solution.py:41
  51.1 0.0 collective-permute-done.7.refs_0_
  51.2 0.7 collective-permute-start.8
  51.8 0.0 collective-permute-start.9
  51.8 6.2 %collective-permute-done.8.refs_1_.refs_10_ = bf16[64,1536]{1,0:T(8,128)(2,1)S(1)} collective-permute-done((bf16[64,1536]{1,0:T(8,128)(2,1)S(1)}, bf16[64,1536]{1,0:T(8,128)(2,1)S(1)}, u32[]{:S(2)}, u32[]{:S(2)}) %collective-permute-start.8) | collective-permute-done | bytes 196640 | tf_op jit(solution)/shard_map/ppermute | solution.py:41
  58.1 1.0 %collective-permute-start.10 = (bf16[64,1536]{1,0:T(8,128)(2,1)S(1)}, bf16[64,1536]{1,0:T(8,128)(2,1)S(1)}, u32[]{:S(2)}, u32[]{:S(2)}) collective-permute-start(bf16[64,1536]{1,0:T(8,128)(2,1)S(1)} %collective-permute-done.8.refs_1_.refs_10_), channel_id=1, source_target_pairs={{0,16},{1,3},{2,18},{3,1},{4,20},{5,7},{6,22},{7,5},{8,24},{9,11},... | collective-permute-start | bytes 589832 | tf_op jit(solution)/shard_map/ppermute | solution.py:41
  59.1 0.0 copy-done.10
  59.1 0.1 copy.9.ids
  59.3 0.8 %dynamic-slice.owners = s32[1,128]{1,0:T(1,128)S(1)} dynamic-slice(s32[8,512]{1,0:T(8,128)} %constant.18.clone, s32[]{:T(128)S(6)} %select_n.3, s32[]{:T(128)S(6)} %add.5), dynamic_slice_sizes={1,128} | dynamic-slice | bytes 1028 | tf_op jit(solution)/shard_map/slice | solution.py:291
  60.0 0.7 %constant_dynamic-slice_fusion.owners = s32[1,384]{1,0:T(1,128)S(1)} fusion(s32[8,512]{1,0:T(8,128)} %constant.18.clone, s32[]{:T(128)S(6)} %select_n.3), kind=kLoop, calls=%fused_computation.1 | loop fusion | bytes 3076 | tf_op jit(solution)/shard_map/slice | solution.py:284
  60.7 0.0 collective-permute-done.5.refs_2_.refs_7_
  60.7 0.0 collective-permute-done.6.refs_3_.refs_8_
  60.8 0.0 copy-start.8
  60.8 0.9 %copy-done.8 = bf16[1,1536,64]{1,2,0:T(8,128)(2,1)S(1)} copy-done((bf16[1,1536,64]{1,2,0:T(8,128)(2,1)S(1)}, bf16[1,1536,64]{1,2,0:T(8,128)(2,1)}, u32[]{:S(2)}) %copy-start.8) | copy-done | bytes 196632
  61.7 2.3 %shard_map.70.earlier = f32[512,128]{1,0:T(8,128)S(1)} custom-call(s32[2]{0:T(128)S(1)} %pad_add_fusion.refs_0_.refs_4_.info, s32[512,1]{1,0:T(8,128)S(1)} %copy.9.ids, s32[1,384]{1,0:T(1,128)S(1)} %constant_dynamic-slice_fusion.owners, bf16[512,1536]{1,0:T(8,128)(2,1)S(1)} %copy-done.1, bf16[64,1536]{1,0:T(8,128)(2,1)S(1)} %bitcast.7, ...), custom_call_target="tpu_custom_call" | custom-call | tf_op jit(solution)/shard_map/pallas_call | solution.py:278
  64.0 0.0 copy-start.3
  64.1 0.0 copy-start.5
  64.1 0.0 copy-start.7
  64.1 0.0 collective-permute-done.9.refs_2_.refs_11_
  64.1 0.0 collective-permute-done.10.refs_3_.refs_12_
  64.1 1.1 %shard_map.71.mine = f32[512,128]{1,0:T(8,128)S(1)} custom-call(s32[2]{0:T(128)S(1)} %pad_add_fusion.refs_0_.refs_4_.info, s32[512,1]{1,0:T(8,128)S(1)} %copy.9.ids, s32[1,128]{1,0:T(1,128)S(1)} %dynamic-slice.owners, bf16[512,1536]{1,0:T(8,128)(2,1)S(1)} %copy-done.1, f32[512,128]{1,0:T(8,128)S(1)} %shard_map.70.earlier, ...), custom_call_target="tpu_custom_call" | custom-call | tf_op jit(solution)/shard_map/pallas_call | solution.py:285
  65.2 0.1 collective-permute-start.11
  65.3 0.7 %constant_dynamic-slice_fusion.1.owners = s32[1,512]{1,0:T(1,128)S(1)} fusion(s32[8,512]{1,0:T(8,128)} %constant.18.clone, s32[]{:T(128)S(6)} %select_n.3), kind=kLoop, calls=%fused_computation.2 | loop fusion | bytes 4100 | tf_op jit(solution)/shard_map/dynamic_slice | solution.py:276
  66.0 0.8 %collective-permute-done.11.theirs = f32[512,128]{1,0:T(8,128)S(1)} collective-permute-done((f32[512,128]{1,0:T(8,128)S(1)}, f32[512,128]{1,0:T(8,128)S(1)}, u32[]{:S(2)}, u32[]{:S(2)}) %collective-permute-start.11) | collective-permute-done | bytes 262176 | tf_op jit(solution)/shard_map/ppermute | solution.py:23
  66.9 3.3 %shard_map.72 = bf16[512,1536]{1,0:T(8,128)(2,1)} custom-call(s32[2]{0:T(128)S(1)} %pad_add_fusion.refs_0_.refs_4_.info, s32[512,1]{1,0:T(8,128)S(1)} %copy.9.ids, s32[1,512]{1,0:T(1,128)S(1)} %constant_dynamic-slice_fusion.1.owners, f32[512,128]{1,0:T(8,128)S(1)} %shard_map.71.mine, f32[512,128]{1,0:T(8,128)S(1)} %collective-permute-done.11.theirs, ...), custom_call_target="tpu_custom_call" | custom-call | tf_op jit(solution)/shard_map/pallas_call | solution.py:306
  (14 shorter events, 0.0 us)
Async XLA Ops:
  0.0 25.7 %collective-permute-start.3 = (bf16[512,1536]{1,0:T(8,128)(2,1)}, bf16[512,1536]{1,0:T(8,128)(2,1)S(1)}, u32[]{:S(2)}, u32[]{:S(2)}) collective-permute-start(bf16[512,1536]{1,0:T(8,128)(2,1)} %latent.3), channel_id=1, source_target_pairs={{0,1},{1,0},{2,3},{3,2},{4,5},{5,4},{6,7},{7,6},{8,9},{9,8},{10,11... | collective-permute-start | bytes 4718600 | tf_op jit(solution)/shard_map/ppermute | solution.py:23
  19.5 17.2 %collective-permute-start = (bf16[128,1536]{1,0:T(8,128)(2,1)}, bf16[128,1536]{1,0:T(8,128)(2,1)S(1)}, u32[]{:S(2)}, u32[]{:S(2)}) collective-permute-start(bf16[128,1536]{1,0:T(8,128)(2,1)} %get-tuple-element.17), channel_id=1, source_target_pairs={{0,2},{2,0},{4,6},{6,4},{8,10},{10,8},{12,14},{14,12},{1,3},{3,1},... | collective-permute-start | bytes 1179656 | tf_op jit(solution)/shard_map/ppermute | solution.py:27
  22.0 14.6 %collective-permute-start.2 = (bf16[64,1536]{1,0:T(8,128)(2,1)}, bf16[64,1536]{1,0:T(8,128)(2,1)S(1)}, u32[]{:S(2)}, u32[]{:S(2)}) collective-permute-start(bf16[64,1536]{1,0:T(8,128)(2,1)} %get-tuple-element.18), channel_id=1, source_target_pairs={{0,12},{2,14},{4,0},{6,2},{8,4},{10,6},{12,8},{14,10},{1,13},{3,15... | collective-permute-start | bytes 589832 | tf_op jit(solution)/shard_map/ppermute | solution.py:31
  25.6 11.0 %collective-permute-start.1 = (bf16[64,1536]{1,0:T(8,128)(2,1)}, bf16[64,1536]{1,0:T(8,128)(2,1)S(1)}, u32[]{:S(2)}, u32[]{:S(2)}) collective-permute-start(bf16[64,1536]{1,0:T(8,128)(2,1)} %get-tuple-element.18), channel_id=1, source_target_pairs={{0,4},{2,6},{4,8},{6,10},{8,12},{10,14},{12,0},{14,2},{1,5},{3,7},... | collective-permute-start | bytes 589832 | tf_op jit(solution)/shard_map/ppermute | solution.py:31
  25.7 1.4 %copy-start = (bf16[512,1536]{1,0:T(8,128)(2,1)S(1)}, bf16[512,1536]{1,0:T(8,128)(2,1)}, u32[]{:S(2)}) copy-start(bf16[512,1536]{1,0:T(8,128)(2,1)} %latent.3) | copy-start | bytes 4718596
  31.4 4.3 %copy-start.2 = (f32[512,512]{1,0:T(8,128)}, f32[512,512]{1,0:T(8,128)S(1)}, u32[]{:S(2)}) copy-start(f32[512,512]{1,0:T(8,128)S(1)} %get-tuple-element.26.refs_0_) | copy-start | bytes 3145732
  31.4 6.6 %copy-start.11 = (bf16[64,1536]{1,0:T(8,128)(2,1)S(1)}, bf16[64,1536]{1,0:T(8,128)(2,1)}, u32[]{:S(2)}) copy-start(bf16[64,1536]{1,0:T(8,128)(2,1)} %get-tuple-element.18) | copy-start | bytes 589828
  35.7 1.0 %copy-start.4 = (f32[512,512]{1,0:T(8,128)}, f32[512,512]{1,0:T(8,128)S(1)}, u32[]{:S(2)}) copy-start(f32[512,512]{1,0:T(8,128)S(1)} %get-tuple-element.27.refs_1_) | copy-start | bytes 3145732
  37.4 11.7 %collective-permute-start.4 = (bf16[128,1536]{1,0:T(8,128)(2,1)}, bf16[128,1536]{1,0:T(8,128)(2,1)}, u32[]{:S(2)}, u32[]{:S(2)}) collective-permute-start(bf16[128,1536]{1,0:T(8,128)(2,1)} %get-tuple-element.21.refs_0_.refs_5_), channel_id=1, source_target_pairs={{0,2},{1,17},{2,0},{3,19},{4,6},{5,21},{6,4},{7,23},{8,10},{9,25},... | collective-permute-start | bytes 1179656 | tf_op jit(solution)/shard_map/ppermute | solution.py:41
  38.0 13.2 %collective-permute-start.7 = (bf16[64,1536]{1,0:T(8,128)(2,1)S(1)}, bf16[64,1536]{1,0:T(8,128)(2,1)S(1)}, u32[]{:S(2)}, u32[]{:S(2)}) collective-permute-start(bf16[64,1536]{1,0:T(8,128)(2,1)S(1)} %copy-done.11), channel_id=1, source_target_pairs={{0,8},{2,10},{4,12},{6,14},{8,0},{10,2},{12,4},{14,6},{1,9},{3,11}... | collective-permute-start | bytes 589832 | tf_op jit(solution)/shard_map/ppermute | solution.py:31
  39.0 21.8 %collective-permute-start.5 = (bf16[128,1536]{1,0:T(8,128)(2,1)}, bf16[128,1536]{1,0:T(8,128)(2,1)}, u32[]{:S(2)}, u32[]{:S(2)}) collective-permute-start(bf16[128,1536]{1,0:T(8,128)(2,1)} %get-tuple-element.21.refs_0_.refs_5_), channel_id=1, source_target_pairs={{0,16},{1,3},{2,18},{3,1},{4,20},{5,7},{6,22},{7,5},{8,24},{9,11},... | collective-permute-start | bytes 1179656 | tf_op jit(solution)/shard_map/ppermute | solution.py:41
  40.5 18.7 %copy-start.10 = (s32[512,1]{0,1:T(1,128)S(1)}, s32[512,1]{0,1:T(1,128)}, u32[]{:S(2)}) copy-start(s32[512,1]{0,1:T(1,128)} %param.7) | copy-start | bytes 6148
  40.5 20.3 %copy-start.1 = (bf16[512,1536]{1,0:T(8,128)(2,1)S(1)}, bf16[512,1536]{1,0:T(8,128)(2,1)}, u32[]{:S(2)}) copy-start(bf16[512,1536]{1,0:T(8,128)(2,1)} %latent.3) | copy-start | bytes 4718596
  44.7 1.0 %copy-start.6 = (f32[512,512]{1,0:T(8,128)}, f32[512,512]{1,0:T(8,128)S(1)}, u32[]{:S(2)}) copy-start(f32[512,512]{1,0:T(8,128)S(1)} %get-tuple-element.28.refs_2_) | copy-start | bytes 3145732
  49.2 11.6 %collective-permute-start.6 = (bf16[128,1536]{1,0:T(8,128)(2,1)}, bf16[128,1536]{1,0:T(8,128)(2,1)S(1)}, u32[]{:S(2)}, u32[]{:S(2)}) collective-permute-start(bf16[128,1536]{1,0:T(8,128)(2,1)} %collective-permute-done.4.refs_2_.refs_1_.refs_6_), channel_id=1, source_target_pairs={{0,16},{1,3},{2,18},{3,1},{4,20},{5,7},{6,22},{7,5},{8,24},{9,11},... | collective-permute-start | bytes 1179656 | tf_op jit(solution)/shard_map/ppermute | solution.py:41
  51.2 6.9 %collective-permute-start.8 = (bf16[64,1536]{1,0:T(8,128)(2,1)S(1)}, bf16[64,1536]{1,0:T(8,128)(2,1)S(1)}, u32[]{:S(2)}, u32[]{:S(2)}) collective-permute-start(bf16[64,1536]{1,0:T(8,128)(2,1)S(1)} %get-tuple-element.25.refs_0_.refs_9_), channel_id=1, source_target_pairs={{0,2},{1,17},{2,0},{3,19},{4,6},{5,21},{6,4},{7,23},{8,10},{9,25},... | collective-permute-start | bytes 589832 | tf_op jit(solution)/shard_map/ppermute | solution.py:41
  51.8 12.2 %collective-permute-start.9 = (bf16[64,1536]{1,0:T(8,128)(2,1)S(1)}, bf16[64,1536]{1,0:T(8,128)(2,1)S(1)}, u32[]{:S(2)}, u32[]{:S(2)}) collective-permute-start(bf16[64,1536]{1,0:T(8,128)(2,1)S(1)} %get-tuple-element.25.refs_0_.refs_9_), channel_id=1, source_target_pairs={{0,16},{1,3},{2,18},{3,1},{4,20},{5,7},{6,22},{7,5},{8,24},{9,11},... | collective-permute-start | bytes 589832 | tf_op jit(solution)/shard_map/ppermute | solution.py:41
  58.1 6.0 %collective-permute-start.10 = (bf16[64,1536]{1,0:T(8,128)(2,1)S(1)}, bf16[64,1536]{1,0:T(8,128)(2,1)S(1)}, u32[]{:S(2)}, u32[]{:S(2)}) collective-permute-start(bf16[64,1536]{1,0:T(8,128)(2,1)S(1)} %collective-permute-done.8.refs_1_.refs_10_), channel_id=1, source_target_pairs={{0,16},{1,3},{2,18},{3,1},{4,20},{5,7},{6,22},{7,5},{8,24},{9,11},... | collective-permute-start | bytes 589832 | tf_op jit(solution)/shard_map/ppermute | solution.py:41
  60.8 0.9 %copy-start.8 = (bf16[1,1536,64]{1,2,0:T(8,128)(2,1)S(1)}, bf16[1,1536,64]{1,2,0:T(8,128)(2,1)}, u32[]{:S(2)}) copy-start(bf16[1,1536,64]{1,2,0:T(8,128)(2,1)} %param.9) | copy-start | bytes 589828
  61.7 5.2 %copy-start.9 = (bf16[1,64,1536]{2,1,0:T(8,128)(2,1)S(1)}, bf16[1,64,1536]{2,1,0:T(8,128)(2,1)}, u32[]{:S(2)}) copy-start(bf16[1,64,1536]{2,1,0:T(8,128)(2,1)} %param.10) | copy-start | bytes 589828
  64.0 2.8 %copy-start.3 = (f32[512,512]{1,0:T(8,128)S(1)}, f32[512,512]{1,0:T(8,128)}, u32[]{:S(2)}) copy-start(f32[512,512]{1,0:T(8,128)} %copy-done.2) | copy-start | bytes 3145732
  64.1 2.8 %copy-start.5 = (f32[512,512]{1,0:T(8,128)S(1)}, f32[512,512]{1,0:T(8,128)}, u32[]{:S(2)}) copy-start(f32[512,512]{1,0:T(8,128)} %copy-done.4) | copy-start | bytes 3145732
  64.1 2.8 %copy-start.7 = (f32[512,512]{1,0:T(8,128)S(1)}, f32[512,512]{1,0:T(8,128)}, u32[]{:S(2)}) copy-start(f32[512,512]{1,0:T(8,128)} %copy-done.6) | copy-start | bytes 3145732
  65.2 1.6 %collective-permute-start.11 = (f32[512,128]{1,0:T(8,128)S(1)}, f32[512,128]{1,0:T(8,128)S(1)}, u32[]{:S(2)}, u32[]{:S(2)}) collective-permute-start(f32[512,128]{1,0:T(8,128)S(1)} %shard_map.71.mine), channel_id=1, source_target_pairs={{0,1},{1,0},{2,3},{3,2},{4,5},{5,4},{6,7},{7,6},{8,9},{9,8},{10,11... | collective-permute-start | bytes 786440 | tf_op jit(solution)/shard_map/ppermute | solution.py:23

commit v5 on v4

v5 whole, which is shorter than its diff:
```python
import jax
import jax.numpy as jnp
import numpy as np
from jax import lax
from jax.experimental import pallas as pl
from jax.experimental.pallas import tpu as pltpu
from jax.sharding import PartitionSpec as P

MIB = 1024 * 1024
CHUNK = 512
AXES = ("replica", "shard", "tensor")
WAVES = ((1, 3), (2,))
FIRST_OWNER = 2
SMEM = pl.BlockSpec(memory_space=pltpu.SMEM)
VMEM = pl.BlockSpec(memory_space=pltpu.VMEM)
ANY = pl.BlockSpec(memory_space=pl.ANY)
TOKEN = jax.ShapeDtypeStruct((8, 128), jnp.float32)


def swap(value, axis):
    return lax.ppermute(value, axis, [(0, 1), (1, 0)])


def neighbour(value, shards):
    return lax.ppermute(value, "shard", [(i, i ^ 1) for i in range(shards)])


def along_line(value, shards, step):
    return lax.ppermute(value, "shard", [(i, (i + 2 * step) % shards) for i in range(shards)])


def in_plane(value, shards, first):
    pairs = []
    for r in range(2):
        for s in range(shards):
            for t in range(2):
                to_r, to_s = (r, s ^ 1) if (t == 0) == first else (r ^ 1, s)
                pairs.append(((r * shards + s) * 2 + t, (to_r * shards + to_s) * 2 + t))
    return lax.ppermute(value, AXES, pairs)


def call(kernel, out_shape, in_specs, limit, scratch=(), flops=0, moved=0):
    return pl.pallas_call(
        kernel,
        out_shape=out_shape,
        in_specs=in_specs,
        out_specs=jax.tree.map(lambda _: VMEM, out_shape),
        scratch_shapes=list(scratch),
        compiler_params=pltpu.CompilerParams(vmem_limit_bytes=limit * MIB),
        cost_estimate=pl.CostEstimate(flops=flops, bytes_accessed=moved, transcendentals=0),
    )


def owner_row(info, begin, count, rank):
    block = (lax.broadcasted_iota(jnp.int32, (1, count), 1) + begin) // rank
    row = jnp.zeros((1, count), jnp.int32)
    for number in range(begin // rank, (begin + count) // rank):
        row = jnp.where(block == number, info[FIRST_OWNER + number], row)
    return row


def pack(pieces, *after):
    rows, width = pieces[0].shape
    count = len(pieces)

    def kernel(*refs):
        out, token = refs[-2:]
        for number in range(count):
            out[number * rows : (number + 1) * rows, :] = refs[number][...]
        token[...] = jnp.zeros_like(token)

    return call(
        kernel,
        [jax.ShapeDtypeStruct((count * rows, width), pieces[0].dtype), TOKEN],
        [VMEM] * count + [ANY] * len(after),
        4,
    )(*pieces, *after)


def fill_wave(info, holds, pieces, stack, top, rank):
    line, first, second, corner = pieces

    def put(here, beside):
        for number in range(line.shape[0] // rank):
            rows = slice(number * rank, (number + 1) * rank)
            place = top + 2 * number * rank
            stack[place : place + rank, :] = here[rows, :]
            stack[place + rank : place + 2 * rank, :] = beside[rows, :]

    for core in range(2):
        next_line, next_replica = (first, second) if core == 0 else (second, first)
        at_core = info[0] == core
        pl.when(at_core & holds)(lambda b=next_line: put(line, b))
        pl.when(at_core & jnp.logical_not(holds))(lambda h=next_replica: put(h, corner))


def masked_products(info, ids, latent, stack, begin, rank):
    total = None
    width = 2 * rank
    for skip in range(0, stack.shape[0], CHUNK):
        count = min(CHUNK, stack.shape[0] - skip)
        part = lax.dot_general(
            latent[...],
            stack[skip : skip + count, :],
            (((1,), (1,)), ((), ())),
            preferred_element_type=jnp.float32,
        )
        mask = ids[...] == owner_row(info, begin + skip, count, rank)
        part = jnp.where(mask, part, 0.0)
        for lane in range(0, count, width):
            fold = part[:, lane : lane + width]
            total = fold if total is None else total + fold
    return total


def down_whole_kernel(info, ids, latent, stack, out):
    out[...] = masked_products(info, ids, latent, stack, 0, out.shape[1] // 2)


def down_first_kernel(info, ids, latent, own, beside, *refs):
    *pieces, _, out, stack = refs
    rank = own.shape[0]
    stack[0:rank, :] = own[...]
    stack[rank : 2 * rank, :] = beside[...]
    fill_wave(info, info[1] == 1, pieces, stack, 2 * rank, rank)
    out[...] = masked_products(info, ids, latent, stack, 0, rank)


def down_last_kernel(info, ids, latent, earlier, *refs, begin):
    *pieces, out, stack = refs
    rank = out.shape[1] // 2
    fill_wave(info, info[1] == 1, pieces, stack, 0, rank)
    out[...] = earlier[...] + masked_products(info, ids, latent, stack, begin, rank)


def base_kernel(info, own, other, weight, _, out, token, *, skip):
    token[...] = jnp.zeros_like(token)
    width = own.shape[1]
    mine = pl.ds(pl.multiple_of(info[0] * width, width), width)
    rest = pl.ds(pl.multiple_of((1 - info[0]) * width, width), width)
    for begin in range(0, out.shape[1], CHUNK):
        place = slice(begin, begin + CHUNK)
        source = slice(skip + begin, skip + begin + CHUNK)
        out[:, place] = jnp.dot(
            own[...], weight[mine, source], preferred_element_type=jnp.float32
        ) + jnp.dot(other[...], weight[rest, source], preferred_element_type=jnp.float32)


def base(info, latent, other, weight, after, skip, columns):
    rows, half_width = latent.shape
    return pl.pallas_call(
        lambda *refs: base_kernel(*refs, skip=skip),
        out_shape=[jax.ShapeDtypeStruct((rows, columns), jnp.float32), TOKEN],
        in_specs=[SMEM, VMEM, VMEM, VMEM, ANY],
        out_specs=[VMEM, VMEM],
        compiler_params=pltpu.CompilerParams(vmem_limit_bytes=24 * MIB),
        cost_estimate=pl.CostEstimate(flops=1000, bytes_accessed=1000, transcendentals=0),
    )(info, latent, other, weight, after)


def up_kernel(info, ids, mine, theirs, left, right, *refs):
    *pieces, out, stack, wide, sems, staged = refs
    rank = mine.shape[1] // 2
    if len(pieces) == 1:
        stack[...] = pieces[0][...]
    else:
        stack[0:rank, :] = pieces[0][...]
        stack[rank : 2 * rank, :] = pieces[1][...]
        top = 2 * rank
        for wave in range(2):
            received = pieces[4 * wave + 2 : 4 * wave + 6]
            fill_wave(info, info[1] == 0, received, stack, top, rank)
            top += received[0].shape[0] * 2
    lowrank = (mine[...] + theirs[...]).astype(jnp.bfloat16)
    zeros = jnp.zeros_like(lowrank)
    width = 2 * rank
    for lane in range(0, wide.shape[1], width):
        mask = ids[...] == owner_row(info, lane, width, rank)
        wide[:, lane : lane + width] = jnp.where(mask, lowrank, zeros)
    copies = []
    tiles, _, tile = staged.shape
    for number in range(tiles):
        place = pl.ds(number * tile, tile)
        delta = jnp.dot(wide[...], stack[:, place], preferred_element_type=jnp.float32)
        begin = number * tile
        if begin < left.shape[1]:
            part = left[:, begin : begin + tile]
        else:
            begin -= left.shape[1]
            part = right[:, begin : begin + tile]
        total = part + delta.astype(jnp.bfloat16).astype(jnp.float32)
        staged[number] = total.astype(out.dtype)
        copies.append(
            pltpu.make_async_copy(staged.at[number], out.at[:, place], sems.at[number])
        )
        copies[-1].start()
    for copy in copies:
        copy.wait()


def on_device(latent, row_adapter_index, shared_weight, adapter_down_weight, adapter_up_weight):
    rows, half_width = latent.shape
    out_width = shared_weight.shape[1]
    local_adapters, _, rank = adapter_down_weight.shape
    shards = lax.axis_size("shard")
    adapters = shards * local_adapters
    columns = adapters * rank
    index, core = lax.axis_index("shard"), lax.axis_index("tensor")
    holds_down = core == lax.axis_index("replica")
    tiles = out_width // CHUNK
    cut = 2 * tiles // 3 * CHUNK
    down = jnp.swapaxes(adapter_down_weight, 1, 2).reshape(local_adapters * rank, half_width)
    up = adapter_up_weight.reshape(local_adapters * rank, out_width)
    ids = row_adapter_index
    routed = shards == 8 and local_adapters == 1 and lax.axis_size("replica") == 2
    routed = routed and half_width == out_width
    lowrank = jax.ShapeDtypeStruct((rows, 2 * rank), jnp.float32)
    if routed:
        sources = [(index - 2 * step) % shards for step in (0, *WAVES[0], *WAVES[1])]
        owners = [a for source in sources for a in (source, source ^ 1)]
    else:
        owners = list(range(adapters))
    info = jnp.stack([jnp.asarray(v, jnp.int32) for v in (core, holds_down, *owners)])
    if routed:
        piece = jnp.where(holds_down, down, up)
        line = {step: along_line(piece, shards, step) for wave in WAVES for step in wave}
        other = swap(latent, "tensor")
        down_beside, up_beside = neighbour(down, shards), neighbour(up, shards)
        left, token = base(info, latent, other, shared_weight, info, 0, cut)
        held, token = pack([line[step] for step in WAVES[0]], token, down_beside, up_beside)
        right, token = base(info, latent, other, shared_weight, token, cut, out_width - cut)
        first, second = in_plane(held, shards, True), in_plane(held, shards, False)
        wave_one = [held, first, second, in_plane(first, shards, False)]
        held, token = pack([line[step] for step in WAVES[1]], token, first)
        first, second = in_plane(held, shards, True), in_plane(held, shards, False)
        wave_two = [held, first, second, in_plane(first, shards, False)]
        split = 2 * rank * (1 + len(WAVES[0]))
        mine = call(
            down_first_kernel,
            lowrank,
            [SMEM] + [VMEM] * 8 + [ANY],
            16,
            [pltpu.VMEM((split, half_width), latent.dtype)],
        )(info, ids, latent, down, down_beside, *wave_one, token)
        mine = call(
            lambda *refs: down_last_kernel(*refs, begin=split),
            lowrank,
            [SMEM] + [VMEM] * 7,
            16,
            [pltpu.VMEM((columns - split, half_width), latent.dtype)],
        )(info, ids, latent, mine, *wave_two)
        up_pieces = [up, up_beside, *wave_one, *wave_two]
    else:
        other = swap(latent, "tensor")
        left, token = base(info, latent, other, shared_weight, info, 0, cut)
        right, token = base(info, latent, other, shared_weight, token, cut, out_width - cut)
        mine = call(down_whole_kernel, lowrank, [SMEM] + [VMEM] * 3, 48)(
            info, ids, latent, lax.all_gather(down, "shard", axis=0, tiled=True)
        )
        up_pieces = [lax.all_gather(up, "shard", axis=0, tiled=True)]
    theirs = swap(mine, "tensor")

    return pl.pallas_call(
        up_kernel,
        out_shape=jax.ShapeDtypeStruct((rows, out_width), latent.dtype),
        in_specs=[SMEM] + [VMEM] * (5 + len(up_pieces)),
        out_specs=ANY,
        scratch_shapes=[
            pltpu.VMEM((columns, out_width), latent.dtype),
            pltpu.VMEM((rows, columns), latent.dtype),
            pltpu.SemaphoreType.DMA((tiles,)),
            pltpu.VMEM((tiles, rows, CHUNK), latent.dtype),
        ],
        compiler_params=pltpu.CompilerParams(vmem_limit_bytes=(24 if routed else 56) * MIB),
    )(info, ids, mine, theirs, left, right, *up_pieces)


def solution(mesh):
    return jax.shard_map(
        on_device,
        mesh=mesh,
        in_specs=(
            P(("replica", "shard"), "tensor"),
            P(("replica", "shard"), None),
            P(None, "tensor"),
            P("shard", "tensor", None),
            P("shard", None, "tensor"),
        ),
        out_specs=P(("replica", "shard"), "tensor"),
        check_vma=False,
    )
```

time: 70.5 us -> 53.5 us (0.76)
  Pallas kernels: 39.3 us -> 14.4 us
  local copies, waits for them, and re-layouts: 6.65 us -> 9.51 us
  starting transfers between devices: 13.4 us -> 15.9 us
  other arithmetic: 0.07 us -> 1.72 us
  waiting for transfers between devices: 10.5 us -> 11.5 us
    pallas_call x6 -> x4, Pallas kernels: 35.2 us -> 10.3 us  [the longest x2 6.28 us: base(): pl.pallas_call(lambda *refs: base_kernel(*refs, skip=skip), out_shape=[ja...]
    unnamed x25 -> x29, local copies, waits for them, and re-layouts: 4.44 us -> 9.42 us
    ppermute x6, starting transfers between devices: 5.68 us -> 7.74 us  [in_plane(): return lax.ppermute(value, AXES, pairs)]
    select_n x0 -> x1, other arithmetic: none -> 1.72 us  [on_device(): piece = jnp.where(holds_down, down, up)]
    slice x2 -> x0, local copies, waits for them, and re-layouts: 1.48 us -> none  [the longest x1 0.77 us: on_device(): owners[:, split:]]
    ppermute x3, starting transfers between devices: 4.63 us -> 5.61 us  [along_line(): lax.ppermute(value, 'shard', [(i, (i + 2 * step) % shards) for i in range...]
    ppermute x2, waiting for transfers between devices: 0.79 us -> 1.52 us  [swap(): return lax.ppermute(value, axis, [(0, 1), (1, 0)])]
    dynamic_slice x1 -> x0, local copies, waits for them, and re-layouts: 0.73 us -> none  [on_device(): owners = jnp.asarray(owner_table(shards, rank))[index][None, :]]
  transfers between devices with their start and end apart: 12 -> 13, of which waited for: 3 -> 4; matrix products, arithmetic and copies ran while one was open for 3% -> 4% of each run, Pallas kernels for 49% -> 16%
where the time goes in v5:
time: 53.5 us; the launch traced here: 53.2 us
  starting transfers between devices  15.9 us (30%)
  Pallas kernels  14.4 us (27%)
  waiting for transfers between devices  11.5 us (21%)
  local copies, waits for them, and re-layouts  9.51 us (18%)
  other arithmetic  1.72 us (3%)
    ppermute x6, waiting for transfers between devices, in_plane(): return lax.ppermute(value, AXES, pairs)  9.96 us
    unnamed x29, local copies, waits for them, and re-layouts  9.42 us
    ppermute x6, starting transfers between devices, in_plane(): return lax.ppermute(value, AXES, pairs)  7.74 us
    pallas_call x2, Pallas kernels, base(): pl.pallas_call(lambda *refs: base_kernel(*refs, skip=skip), out_shape=[ja...  6.28 us
    ppermute x3, starting transfers between devices, along_line(): lax.ppermute(value, 'shard', [(i, (i + 2 * step) % shards) for i in range...  5.61 us
    pallas_call x1, Pallas kernels, on_device(): pl.pallas_call(up_kernel, out_shape=jax.ShapeDtypeStruct((rows, out_width...  3.31 us
    pallas_call x1, Pallas kernels, on_device(): call(down_first_kernel, lowrank, [SMEM] + [VMEM] * 8 + [ANY], 16, [pltpu....  2.26 us
    ppermute x2, starting transfers between devices, neighbour(): return lax.ppermute(value, 'shard', [(i, i ^ 1) for i in range(shards)])  2.03 us
  transfers between devices with their start and end apart: 13, of which 4 were waited for; matrix products, arithmetic and copies ran while one was open for 4% of the time, Pallas kernels for 16%

profile of v5, /device:TPU:0, one launch (start us, length us, event | category | flops | bytes accessed | tf_op | source)
XLA Modules:
  0.0 53.2 jit_solution(13282890779648296345)
XLA Ops:
  0.0 0.5 collective-permute-start.3
  0.5 1.7 %broadcast_select_fusion = bf16[64,1536]{1,0:T(8,128)(2,1)} fusion(pred[]{:T(512)S(6)} %eq.8, bf16[1,64,1536]{2,1,0:T(8,128)(2,1)} %param.9, bf16[1,1536,64]{1,2,0:T(8,128)(2,1)} %param.8), kind=kLoop, calls=%fused_computation | loop fusion | flops 98304 | bytes 589825 | tf_op jit(solution)/shard_map/jit(_where)/select_n | solution.py:225
  2.2 4.6 %collective-permute-start.2 = (bf16[64,1536]{1,0:T(8,128)(2,1)}, bf16[64,1536]{1,0:T(8,128)(2,1)S(1)}, u32[]{:S(2)}, u32[]{:S(2)}) collective-permute-start(bf16[64,1536]{1,0:T(8,128)(2,1)} %broadcast_select_fusion), channel_id=1, source_target_pairs={{0,12},{2,14},{4,0},{6,2},{8,4},{10,6},{12,8},{14,10},{1,13},{3,15... | collective-permute-start | bytes 589832 | tf_op jit(solution)/shard_map/ppermute | solution.py:29
  6.8 0.0 collective-permute-start.1
  6.8 1.5 %collective-permute-start = (bf16[64,1536]{1,0:T(8,128)(2,1)}, bf16[64,1536]{1,0:T(8,128)(2,1)S(1)}, u32[]{:S(2)}, u32[]{:S(2)}) collective-permute-start(bf16[64,1536]{1,0:T(8,128)(2,1)} %bitcast.16), channel_id=1, source_target_pairs={{0,2},{2,0},{4,6},{6,4},{8,10},{10,8},{12,14},{14,12},{1,3},{3,1},... | collective-permute-start | bytes 589832 | tf_op jit(solution)/shard_map/ppermute | solution.py:25
  8.3 0.5 collective-permute-start.4
  8.8 0.1 stack.47.refs_0_.refs_4_.info
  8.9 0.0 collective-permute-done.3.refs_2_
  8.9 0.0 copy-start
  8.9 3.7 %copy-done = bf16[3072,1536]{1,0:T(8,128)(2,1)S(1)} copy-done((bf16[3072,1536]{1,0:T(8,128)(2,1)S(1)}, bf16[3072,1536]{1,0:T(8,128)(2,1)}, u32[]{:S(2)}) %copy-start) | copy-done | bytes 9437208
  12.6 1.4 %copy-done.1 = bf16[512,1536]{1,0:T(8,128)(2,1)S(1)} copy-done((bf16[512,1536]{1,0:T(8,128)(2,1)S(1)}, bf16[512,1536]{1,0:T(8,128)(2,1)}, u32[]{:S(2)}) %copy-start.1) | copy-done | bytes 1572888
  14.0 4.0 %shard_map.55 = (f32[512,1024]{1,0:T(8,128)S(1)}, f32[8,128]{1,0:T(8,128)S(1)}) custom-call(s32[10]{0:T(128)S(1)} %stack.47.refs_0_.refs_4_.info, bf16[512,1536]{1,0:T(8,128)(2,1)S(1)} %copy-done.1, bf16[512,1536]{1,0:T(8,128)(2,1)S(1)} %collective-permute-done.3.refs_2_, bf16[3072,1536]{1,0:T(8,128)(2,1)S(1)} %copy-done, s32[10]{0:T(128)S(1)} %stack.47.refs_0_.refs_4_.info), custom_call_target="tpu_custom_call" | custom-call | flops 1000 | bytes 1000 | tf_op jit(solution)/shard_map/pallas_call | solution.py:151
  17.9 0.0 copy-start.3
  18.0 1.3 %copy-done.3 = f32[512,1024]{1,0:T(8,128)} copy-done((f32[512,1024]{1,0:T(8,128)}, f32[512,1024]{1,0:T(8,128)S(1)}, u32[]{:S(2)}) %copy-start.3) | copy-done | bytes 2097176
  19.3 0.0 collective-permute-done.2.refs_1_
  19.3 0.0 collective-permute-done.1.refs_0_
  19.3 0.0 collective-permute-done.refs_3_.beside
  19.3 0.0 collective-permute-done.4.refs_4_.refs_1_
  19.3 0.8 %shard_map.56 = (bf16[128,1536]{1,0:T(8,128)(2,1)}, f32[8,128]{1,0:T(8,128)S(1)}) custom-call(bf16[64,1536]{1,0:T(8,128)(2,1)S(1)} %collective-permute-done.1.refs_0_, bf16[64,1536]{1,0:T(8,128)(2,1)S(1)} %collective-permute-done.2.refs_1_, f32[8,128]{1,0:T(8,128)S(1)} %get-tuple-element.13.refs_2_, ...), custom_call_target="tpu_custom_call" | custom-call | tf_op jit(solution)/shard_map/pallas_call | solution.py:72
  20.2 1.5 %collective-permute-start.5 = (bf16[128,1536]{1,0:T(8,128)(2,1)}, bf16[128,1536]{1,0:T(8,128)(2,1)S(1)}, u32[]{:S(2)}, u32[]{:S(2)}) collective-permute-start(bf16[128,1536]{1,0:T(8,128)(2,1)} %get-tuple-element.14.refs_0_.refs_2_), channel_id=1, source_target_pairs={{0,2},{1,17},{2,0},{3,19},{4,6},{5,21},{6,4},{7,23},{8,10},{9,25},... | collective-permute-start | bytes 1179656 | tf_op jit(solution)/shard_map/ppermute | solution.py:39
  21.7 1.0 %collective-permute-start.8 = (bf16[64,1536]{1,0:T(8,128)(2,1)}, bf16[64,1536]{1,0:T(8,128)(2,1)S(1)}, u32[]{:S(2)}, u32[]{:S(2)}) collective-permute-start(bf16[64,1536]{1,0:T(8,128)(2,1)} %broadcast_select_fusion), channel_id=1, source_target_pairs={{0,8},{2,10},{4,12},{6,14},{8,0},{10,2},{12,4},{14,6},{1,9},{3,11}... | collective-permute-start | bytes 589832 | tf_op jit(solution)/shard_map/ppermute | solution.py:29
  22.7 1.5 %collective-permute-start.6 = (bf16[128,1536]{1,0:T(8,128)(2,1)}, bf16[128,1536]{1,0:T(8,128)(2,1)}, u32[]{:S(2)}, u32[]{:S(2)}) collective-permute-start(bf16[128,1536]{1,0:T(8,128)(2,1)} %get-tuple-element.14.refs_0_.refs_2_), channel_id=1, source_target_pairs={{0,16},{1,3},{2,18},{3,1},{4,20},{5,7},{6,22},{7,5},{8,24},{9,11},... | collective-permute-start | bytes 1179656 | tf_op jit(solution)/shard_map/ppermute | solution.py:39
  24.2 2.3 %shard_map.57 = (f32[512,512]{1,0:T(8,128)S(1)}, f32[8,128]{1,0:T(8,128)S(1)}) custom-call(s32[10]{0:T(128)S(1)} %stack.47.refs_0_.refs_4_.info, bf16[512,1536]{1,0:T(8,128)(2,1)S(1)} %copy-done.1, bf16[512,1536]{1,0:T(8,128)(2,1)S(1)} %collective-permute-done.3.refs_2_, bf16[3072,1536]{1,0:T(8,128)(2,1)S(1)} %copy-done, f32[8,128]{1,0:T(8,128)S(1)} %get-tuple-element.15.refs_4_), custom_call_target="tpu_custom_call" | custom-call | flops 1000 | bytes 1000 | tf_op jit(solution)/shard_map/pallas_call | solution.py:151
  26.6 0.0 copy-start.5
  26.6 1.0 %copy-done.5 = f32[512,512]{1,0:T(8,128)} copy-done((f32[512,512]{1,0:T(8,128)}, f32[512,512]{1,0:T(8,128)S(1)}, u32[]{:S(2)}) %copy-start.5) | copy-done | bytes 1048600
  27.5 4.6 %collective-permute-done.5.refs_2_.refs_1_.refs_3_ = bf16[128,1536]{1,0:T(8,128)(2,1)S(1)} collective-permute-done((bf16[128,1536]{1,0:T(8,128)(2,1)}, bf16[128,1536]{1,0:T(8,128)(2,1)S(1)}, u32[]{:S(2)}, u32[]{:S(2)}) %collective-permute-start.5) | collective-permute-done | bytes 393248 | tf_op jit(solution)/shard_map/ppermute | solution.py:39
  32.1 1.7 %collective-permute-start.7 = (bf16[128,1536]{1,0:T(8,128)(2,1)S(1)}, bf16[128,1536]{1,0:T(8,128)(2,1)S(1)}, u32[]{:S(2)}, u32[]{:S(2)}) collective-permute-start(bf16[128,1536]{1,0:T(8,128)(2,1)S(1)} %collective-permute-done.5.refs_2_.refs_1_.refs_3_), channel_id=1, source_target_pairs={{0,16},{1,3},{2,18},{3,1},{4,20},{5,7},{6,22},{7,5},{8,24},{9,11},... | collective-permute-start | bytes 1179656 | tf_op jit(solution)/shard_map/ppermute | solution.py:39
  33.8 0.0 collective-permute-done.8.refs_0_
  33.9 1.6 %collective-permute-start.9 = (bf16[64,1536]{1,0:T(8,128)(2,1)S(1)}, bf16[64,1536]{1,0:T(8,128)(2,1)S(1)}, u32[]{:S(2)}, u32[]{:S(2)}) collective-permute-start(bf16[64,1536]{1,0:T(8,128)(2,1)S(1)} %get-tuple-element.18.refs_4_.refs_6_), channel_id=1, source_target_pairs={{0,2},{1,17},{2,0},{3,19},{4,6},{5,21},{6,4},{7,23},{8,10},{9,25},... | collective-permute-start | bytes 589832 | tf_op jit(solution)/shard_map/ppermute | solution.py:39
  35.4 0.3 collective-permute-start.10
  35.8 5.1 %collective-permute-done.9.refs_5_.refs_7_ = bf16[64,1536]{1,0:T(8,128)(2,1)S(1)} collective-permute-done((bf16[64,1536]{1,0:T(8,128)(2,1)S(1)}, bf16[64,1536]{1,0:T(8,128)(2,1)S(1)}, u32[]{:S(2)}, u32[]{:S(2)}) %collective-permute-start.9) | collective-permute-done | bytes 196640 | tf_op jit(solution)/shard_map/ppermute | solution.py:39
  40.8 1.1 %collective-permute-start.11 = (bf16[64,1536]{1,0:T(8,128)(2,1)S(1)}, bf16[64,1536]{1,0:T(8,128)(2,1)}, u32[]{:S(2)}, u32[]{:S(2)}) collective-permute-start(bf16[64,1536]{1,0:T(8,128)(2,1)S(1)} %collective-permute-done.9.refs_5_.refs_7_), channel_id=1, source_target_pairs={{0,16},{1,3},{2,18},{3,1},{4,20},{5,7},{6,22},{7,5},{8,24},{9,11},... | collective-permute-start | bytes 589832 | tf_op jit(solution)/shard_map/ppermute | solution.py:39
  41.9 0.1 copy.8.ids.refs_1_
  42.1 0.0 collective-permute-done.6.refs_2_.refs_4_
  42.1 0.0 collective-permute-done.7.refs_3_.refs_5_
  42.1 0.0 copy-start.7
  42.1 0.9 %copy-done.7 = bf16[1,1536,64]{1,2,0:T(8,128)(2,1)S(1)} copy-done((bf16[1,1536,64]{1,2,0:T(8,128)(2,1)S(1)}, bf16[1,1536,64]{1,2,0:T(8,128)(2,1)}, u32[]{:S(2)}) %copy-start.7) | copy-done | bytes 196632
  43.1 0.9 %copy-done.9 = bf16[64,1536]{1,0:T(8,128)(2,1)S(1)} copy-done((bf16[64,1536]{1,0:T(8,128)(2,1)S(1)}, bf16[64,1536]{1,0:T(8,128)(2,1)}, u32[]{:S(2)}) %copy-start.9) | copy-done | bytes 196632
  44.0 2.3 %shard_map.59.refs_3_ = f32[512,128]{1,0:T(8,128)S(1)} custom-call(s32[10]{0:T(128)S(1)} %stack.47.refs_0_.refs_4_.info, s32[512,1]{1,0:T(8,128)S(1)} %copy.8.ids.refs_1_, bf16[512,1536]{1,0:T(8,128)(2,1)S(1)} %copy-done.2, bf16[64,1536]{1,0:T(8,128)(2,1)S(1)} %bitcast.17, bf16[64,1536]{1,0:T(8,128)(2,1)S(1)} %copy-done.9, ...), custom_call_target="tpu_custom_call" | custom-call | tf_op jit(solution)/shard_map/pallas_call | solution.py:238
  46.3 0.0 copy-start.4
  46.3 0.0 copy-start.6
  46.3 0.0 collective-permute-done.10.refs_6_.refs_8_
  46.3 0.3 collective-permute-done.11.refs_7_.refs_9_
  46.6 1.7 %shard_map.60.mine = f32[512,128]{1,0:T(8,128)S(1)} custom-call(s32[10]{0:T(128)S(1)} %stack.47.refs_0_.refs_4_.info, s32[512,1]{1,0:T(8,128)S(1)} %copy.8.ids.refs_1_, bf16[512,1536]{1,0:T(8,128)(2,1)S(1)} %copy-done.2, f32[512,128]{1,0:T(8,128)S(1)} %shard_map.59.refs_3_, bf16[64,1536]{1,0:T(8,128)(2,1)S(1)} %get-tuple-element.18.refs_4_.refs_6_, ...), custom_call_target="tpu_custom_call" | custom-call | tf_op jit(solution)/shard_map/pallas_call | solution.py:245
  48.3 0.1 collective-permute-start.12
  48.4 1.5 %collective-permute-done.12.theirs = f32[512,128]{1,0:T(8,128)S(1)} collective-permute-done((f32[512,128]{1,0:T(8,128)S(1)}, f32[512,128]{1,0:T(8,128)S(1)}, u32[]{:S(2)}, u32[]{:S(2)}) %collective-permute-start.12) | collective-permute-done | bytes 262176 | tf_op jit(solution)/shard_map/ppermute | solution.py:21
  49.9 0.0 copy-done.6
  49.9 3.3 %shard_map.61 = bf16[512,1536]{1,0:T(8,128)(2,1)} custom-call(s32[10]{0:T(128)S(1)} %stack.47.refs_0_.refs_4_.info, s32[512,1]{1,0:T(8,128)S(1)} %copy.8.ids.refs_1_, f32[512,128]{1,0:T(8,128)S(1)} %shard_map.60.mine, f32[512,128]{1,0:T(8,128)S(1)} %collective-permute-done.12.theirs, f32[512,1024]{1,0:T(8,128)S(1)} %copy-done.4, f32[512,512]{1,0:T(8,128)S(1)} %copy-done.6, ...), custom_call_target="tpu_custom_call" | custom-call | tf_op jit(solution)/shard_map/pallas_call | solution.py:263
  (16 shorter events, 0.0 us)
Async XLA Ops:
  0.0 8.9 %collective-permute-start.3 = (bf16[512,1536]{1,0:T(8,128)(2,1)}, bf16[512,1536]{1,0:T(8,128)(2,1)S(1)}, u32[]{:S(2)}, u32[]{:S(2)}) collective-permute-start(bf16[512,1536]{1,0:T(8,128)(2,1)} %refs_2_.1), channel_id=1, source_target_pairs={{0,1},{1,0},{2,3},{3,2},{4,5},{5,4},{6,7},{7,6},{8,9},{9,8},{10,11... | collective-permute-start | bytes 4718600 | tf_op jit(solution)/shard_map/ppermute | solution.py:21
  2.2 17.1 %collective-permute-start.2 = (bf16[64,1536]{1,0:T(8,128)(2,1)}, bf16[64,1536]{1,0:T(8,128)(2,1)S(1)}, u32[]{:S(2)}, u32[]{:S(2)}) collective-permute-start(bf16[64,1536]{1,0:T(8,128)(2,1)} %broadcast_select_fusion), channel_id=1, source_target_pairs={{0,12},{2,14},{4,0},{6,2},{8,4},{10,6},{12,8},{14,10},{1,13},{3,15... | collective-permute-start | bytes 589832 | tf_op jit(solution)/shard_map/ppermute | solution.py:29
  6.8 12.5 %collective-permute-start.1 = (bf16[64,1536]{1,0:T(8,128)(2,1)}, bf16[64,1536]{1,0:T(8,128)(2,1)S(1)}, u32[]{:S(2)}, u32[]{:S(2)}) collective-permute-start(bf16[64,1536]{1,0:T(8,128)(2,1)} %broadcast_select_fusion), channel_id=1, source_target_pairs={{0,4},{2,6},{4,8},{6,10},{8,12},{10,14},{12,0},{14,2},{1,5},{3,7},... | collective-permute-start | bytes 589832 | tf_op jit(solution)/shard_map/ppermute | solution.py:29
  6.8 12.5 %collective-permute-start = (bf16[64,1536]{1,0:T(8,128)(2,1)}, bf16[64,1536]{1,0:T(8,128)(2,1)S(1)}, u32[]{:S(2)}, u32[]{:S(2)}) collective-permute-start(bf16[64,1536]{1,0:T(8,128)(2,1)} %bitcast.16), channel_id=1, source_target_pairs={{0,2},{2,0},{4,6},{6,4},{8,10},{10,8},{12,14},{14,12},{1,3},{3,1},... | collective-permute-start | bytes 589832 | tf_op jit(solution)/shard_map/ppermute | solution.py:25
  8.3 11.0 %collective-permute-start.4 = (bf16[64,1536]{1,0:T(8,128)(2,1)}, bf16[64,1536]{1,0:T(8,128)(2,1)S(1)}, u32[]{:S(2)}, u32[]{:S(2)}) collective-permute-start(bf16[64,1536]{1,0:T(8,128)(2,1)} %bitcast.18), channel_id=1, source_target_pairs={{0,2},{2,0},{4,6},{6,4},{8,10},{10,8},{12,14},{14,12},{1,3},{3,1},... | collective-permute-start | bytes 589832 | tf_op jit(solution)/shard_map/ppermute | solution.py:25
  8.9 3.7 %copy-start = (bf16[3072,1536]{1,0:T(8,128)(2,1)S(1)}, bf16[3072,1536]{1,0:T(8,128)(2,1)}, u32[]{:S(2)}) copy-start(bf16[3072,1536]{1,0:T(8,128)(2,1)} %refs_3_.3) | copy-start | bytes 28311556
  12.6 1.4 %copy-start.1 = (bf16[512,1536]{1,0:T(8,128)(2,1)S(1)}, bf16[512,1536]{1,0:T(8,128)(2,1)}, u32[]{:S(2)}) copy-start(bf16[512,1536]{1,0:T(8,128)(2,1)} %refs_2_.1) | copy-start | bytes 4718596
  17.9 1.4 %copy-start.3 = (f32[512,1024]{1,0:T(8,128)}, f32[512,1024]{1,0:T(8,128)S(1)}, u32[]{:S(2)}) copy-start(f32[512,1024]{1,0:T(8,128)S(1)} %get-tuple-element.19.left) | copy-start | bytes 6291460
  19.3 4.9 %copy-start.8 = (bf16[64,1536]{1,0:T(8,128)(2,1)}, bf16[64,1536]{1,0:T(8,128)(2,1)S(1)}, u32[]{:S(2)}) copy-start(bf16[64,1536]{1,0:T(8,128)(2,1)S(1)} %collective-permute-done.refs_3_.beside) | copy-start | bytes 589828
  19.3 4.9 %copy-start.11 = (bf16[64,1536]{1,0:T(8,128)(2,1)}, bf16[64,1536]{1,0:T(8,128)(2,1)S(1)}, u32[]{:S(2)}) copy-start(bf16[64,1536]{1,0:T(8,128)(2,1)S(1)} %collective-permute-done.4.refs_4_.refs_1_) | copy-start | bytes 589828
  20.2 11.9 %collective-permute-start.5 = (bf16[128,1536]{1,0:T(8,128)(2,1)}, bf16[128,1536]{1,0:T(8,128)(2,1)S(1)}, u32[]{:S(2)}, u32[]{:S(2)}) collective-permute-start(bf16[128,1536]{1,0:T(8,128)(2,1)} %get-tuple-element.14.refs_0_.refs_2_), channel_id=1, source_target_pairs={{0,2},{1,17},{2,0},{3,19},{4,6},{5,21},{6,4},{7,23},{8,10},{9,25},... | collective-permute-start | bytes 1179656 | tf_op jit(solution)/shard_map/ppermute | solution.py:39
  21.7 12.1 %collective-permute-start.8 = (bf16[64,1536]{1,0:T(8,128)(2,1)}, bf16[64,1536]{1,0:T(8,128)(2,1)S(1)}, u32[]{:S(2)}, u32[]{:S(2)}) collective-permute-start(bf16[64,1536]{1,0:T(8,128)(2,1)} %broadcast_select_fusion), channel_id=1, source_target_pairs={{0,8},{2,10},{4,12},{6,14},{8,0},{10,2},{12,4},{14,6},{1,9},{3,11}... | collective-permute-start | bytes 589832 | tf_op jit(solution)/shard_map/ppermute | solution.py:29
  22.7 19.4 %collective-permute-start.6 = (bf16[128,1536]{1,0:T(8,128)(2,1)}, bf16[128,1536]{1,0:T(8,128)(2,1)}, u32[]{:S(2)}, u32[]{:S(2)}) collective-permute-start(bf16[128,1536]{1,0:T(8,128)(2,1)} %get-tuple-element.14.refs_0_.refs_2_), channel_id=1, source_target_pairs={{0,16},{1,3},{2,18},{3,1},{4,20},{5,7},{6,22},{7,5},{8,24},{9,11},... | collective-permute-start | bytes 1179656 | tf_op jit(solution)/shard_map/ppermute | solution.py:39
  24.2 17.7 %copy-start.13 = (s32[512,1]{0,1:T(1,128)S(1)}, s32[512,1]{0,1:T(1,128)}, u32[]{:S(2)}) copy-start(s32[512,1]{0,1:T(1,128)} %param.6) | copy-start | bytes 6148
  24.2 17.9 %copy-start.2 = (bf16[512,1536]{1,0:T(8,128)(2,1)S(1)}, bf16[512,1536]{1,0:T(8,128)(2,1)}, u32[]{:S(2)}) copy-start(bf16[512,1536]{1,0:T(8,128)(2,1)} %refs_2_.1) | copy-start | bytes 4718596
  26.6 1.0 %copy-start.5 = (f32[512,512]{1,0:T(8,128)}, f32[512,512]{1,0:T(8,128)S(1)}, u32[]{:S(2)}) copy-start(f32[512,512]{1,0:T(8,128)S(1)} %get-tuple-element.20.right) | copy-start | bytes 3145732
  32.1 10.0 %collective-permute-start.7 = (bf16[128,1536]{1,0:T(8,128)(2,1)S(1)}, bf16[128,1536]{1,0:T(8,128)(2,1)S(1)}, u32[]{:S(2)}, u32[]{:S(2)}) collective-permute-start(bf16[128,1536]{1,0:T(8,128)(2,1)S(1)} %collective-permute-done.5.refs_2_.refs_1_.refs_3_), channel_id=1, source_target_pairs={{0,16},{1,3},{2,18},{3,1},{4,20},{5,7},{6,22},{7,5},{8,24},{9,11},... | collective-permute-start | bytes 1179656 | tf_op jit(solution)/shard_map/ppermute | solution.py:39
  33.9 7.0 %collective-permute-start.9 = (bf16[64,1536]{1,0:T(8,128)(2,1)S(1)}, bf16[64,1536]{1,0:T(8,128)(2,1)S(1)}, u32[]{:S(2)}, u32[]{:S(2)}) collective-permute-start(bf16[64,1536]{1,0:T(8,128)(2,1)S(1)} %get-tuple-element.18.refs_4_.refs_6_), channel_id=1, source_target_pairs={{0,2},{1,17},{2,0},{3,19},{4,6},{5,21},{6,4},{7,23},{8,10},{9,25},... | collective-permute-start | bytes 589832 | tf_op jit(solution)/shard_map/ppermute | solution.py:39
  35.4 10.8 %collective-permute-start.10 = (bf16[64,1536]{1,0:T(8,128)(2,1)S(1)}, bf16[64,1536]{1,0:T(8,128)(2,1)S(1)}, u32[]{:S(2)}, u32[]{:S(2)}) collective-permute-start(bf16[64,1536]{1,0:T(8,128)(2,1)S(1)} %get-tuple-element.18.refs_4_.refs_6_), channel_id=1, source_target_pairs={{0,16},{1,3},{2,18},{3,1},{4,20},{5,7},{6,22},{7,5},{8,24},{9,11},... | collective-permute-start | bytes 589832 | tf_op jit(solution)/shard_map/ppermute | solution.py:39
  40.8 5.8 %collective-permute-start.11 = (bf16[64,1536]{1,0:T(8,128)(2,1)S(1)}, bf16[64,1536]{1,0:T(8,128)(2,1)}, u32[]{:S(2)}, u32[]{:S(2)}) collective-permute-start(bf16[64,1536]{1,0:T(8,128)(2,1)S(1)} %collective-permute-done.9.refs_5_.refs_7_), channel_id=1, source_target_pairs={{0,16},{1,3},{2,18},{3,1},{4,20},{5,7},{6,22},{7,5},{8,24},{9,11},... | collective-permute-start | bytes 589832 | tf_op jit(solution)/shard_map/ppermute | solution.py:39
  42.1 0.9 %copy-start.7 = (bf16[1,1536,64]{1,2,0:T(8,128)(2,1)S(1)}, bf16[1,1536,64]{1,2,0:T(8,128)(2,1)}, u32[]{:S(2)}) copy-start(bf16[1,1536,64]{1,2,0:T(8,128)(2,1)} %param.8) | copy-start | bytes 589828
  43.1 0.9 %copy-start.9 = (bf16[64,1536]{1,0:T(8,128)(2,1)S(1)}, bf16[64,1536]{1,0:T(8,128)(2,1)}, u32[]{:S(2)}) copy-start(bf16[64,1536]{1,0:T(8,128)(2,1)} %copy-done.8) | copy-start | bytes 589828
  44.0 5.9 %copy-start.10 = (bf16[1,64,1536]{2,1,0:T(8,128)(2,1)S(1)}, bf16[1,64,1536]{2,1,0:T(8,128)(2,1)}, u32[]{:S(2)}) copy-start(bf16[1,64,1536]{2,1,0:T(8,128)(2,1)} %param.9) | copy-start | bytes 589828
  44.0 5.9 %copy-start.12 = (bf16[64,1536]{1,0:T(8,128)(2,1)S(1)}, bf16[64,1536]{1,0:T(8,128)(2,1)}, u32[]{:S(2)}) copy-start(bf16[64,1536]{1,0:T(8,128)(2,1)} %copy-done.11) | copy-start | bytes 589828
  46.3 3.7 %copy-start.4 = (f32[512,1024]{1,0:T(8,128)S(1)}, f32[512,1024]{1,0:T(8,128)}, u32[]{:S(2)}) copy-start(f32[512,1024]{1,0:T(8,128)} %copy-done.3) | copy-start | bytes 6291460
  46.3 3.7 %copy-start.6 = (f32[512,512]{1,0:T(8,128)S(1)}, f32[512,512]{1,0:T(8,128)}, u32[]{:S(2)}) copy-start(f32[512,512]{1,0:T(8,128)} %copy-done.5) | copy-start | bytes 3145732
  48.3 1.6 %collective-permute-start.12 = (f32[512,128]{1,0:T(8,128)S(1)}, f32[512,128]{1,0:T(8,128)S(1)}, u32[]{:S(2)}, u32[]{:S(2)}) collective-permute-start(f32[512,128]{1,0:T(8,128)S(1)} %shard_map.60.mine), channel_id=1, source_target_pairs={{0,1},{1,0},{2,3},{3,2},{4,5},{5,4},{6,7},{7,6},{8,9},{9,8},{10,11... | collective-permute-start | bytes 786440 | tf_op jit(solution)/shard_map/ppermute | solution.py:21

commit v6 on v5

--- a/solution.py
+++ b/solution.py
@@ -133,7 +133,8 @@
     out[...] = earlier[...] + masked_products(info, ids, latent, stack, begin, rank)
 
 
-def base_kernel(info, own, other, weight, _, out, token, *, skip):
+def base_kernel(info, own, other, weight, *refs, skip):
+    out, token = refs[-2:]
     token[...] = jnp.zeros_like(token)
     width = own.shape[1]
     mine = pl.ds(pl.multiple_of(info[0] * width, width), width)
@@ -151,11 +152,11 @@
     return pl.pallas_call(
         lambda *refs: base_kernel(*refs, skip=skip),
         out_shape=[jax.ShapeDtypeStruct((rows, columns), jnp.float32), TOKEN],
-        in_specs=[SMEM, VMEM, VMEM, VMEM, ANY],
+        in_specs=[SMEM, VMEM, VMEM, VMEM] + [ANY] * len(after),
         out_specs=[VMEM, VMEM],
         compiler_params=pltpu.CompilerParams(vmem_limit_bytes=24 * MIB),
         cost_estimate=pl.CostEstimate(flops=1000, bytes_accessed=1000, transcendentals=0),
-    )(info, latent, other, weight, after)
+    )(info, latent, other, weight, *after)
 
 
 def up_kernel(info, ids, mine, theirs, left, right, *refs):
@@ -208,7 +209,7 @@
     index, core = lax.axis_index("shard"), lax.axis_index("tensor")
     holds_down = core == lax.axis_index("replica")
     tiles = out_width // CHUNK
-    cut = 2 * tiles // 3 * CHUNK
+    cut = tiles // 3 * CHUNK
     down = jnp.swapaxes(adapter_down_weight, 1, 2).reshape(local_adapters * rank, half_width)
     up = adapter_up_weight.reshape(local_adapters * rank, out_width)
     ids = row_adapter_index
@@ -226,9 +227,9 @@
         line = {step: along_line(piece, shards, step) for wave in WAVES for step in wave}
         other = swap(latent, "tensor")
         down_beside, up_beside = neighbour(down, shards), neighbour(up, shards)
-        left, token = base(info, latent, other, shared_weight, info, 0, cut)
+        left, token = base(info, latent, other, shared_weight, [ids], 0, cut)
         held, token = pack([line[step] for step in WAVES[0]], token, down_beside, up_beside)
-        right, token = base(info, latent, other, shared_weight, token, cut, out_width - cut)
+        right, token = base(info, latent, other, shared_weight, [token], cut, out_width - cut)
         first, second = in_plane(held, shards, True), in_plane(held, shards, False)
         wave_one = [held, first, second, in_plane(first, shards, False)]
         held, token = pack([line[step] for step in WAVES[1]], token, first)
@@ -252,8 +253,8 @@
         up_pieces = [up, up_beside, *wave_one, *wave_two]
     else:
         other = swap(latent, "tensor")
-        left, token = base(info, latent, other, shared_weight, info, 0, cut)
-        right, token = base(info, latent, other, shared_weight, token, cut, out_width - cut)
+        left, token = base(info, latent, other, shared_weight, [ids], 0, cut)
+        right, token = base(info, latent, other, shared_weight, [token], cut, out_width - cut)
         mine = call(down_whole_kernel, lowrank, [SMEM] + [VMEM] * 3, 48)(
             info, ids, latent, lax.all_gather(down, "shard", axis=0, tiled=True)
         )

time: 53.5 us -> 49.2 us (0.920)
  local copies, waits for them, and re-layouts: 9.51 us -> 6.01 us
  waiting for transfers between devices: 11.5 us -> 14.8 us
  Pallas kernels: 14.4 us -> 11.8 us
  other arithmetic: 1.72 us -> 1.04 us
  starting transfers between devices: 15.9 us -> 15.3 us
    unnamed x29 -> x9, local copies, waits for them, and re-layouts: 9.42 us -> 5.91 us
    ppermute x6, waiting for transfers between devices: 9.96 us -> 12.2 us  [in_plane(): return lax.ppermute(value, AXES, pairs)]
    ppermute x2, waiting for transfers between devices: 0.01 us -> 1.05 us  [neighbour(): return lax.ppermute(value, 'shard', [(i, i ^ 1) for i in range(shards)])]
    pallas_call x2, Pallas kernels: 0.86 us -> 0.04 us  [pack(): call(kernel, [jax.ShapeDtypeStruct((count * rows, width), pieces[0].dtype...]
    select_n x1, other arithmetic: 1.72 us -> 1.04 us  [on_device(): piece = jnp.where(holds_down, down, up)]
    pallas_call x1, Pallas kernels: 3.31 us -> 2.66 us  [on_device(): pl.pallas_call(up_kernel, out_shape=jax.ShapeDtypeStruct((rows, out_width...]
    pallas_call x1, Pallas kernels: 2.26 us -> 1.63 us  [on_device(): call(down_first_kernel, lowrank, [SMEM] + [VMEM] * 8 + [ANY], 16, [pltpu....]
    pallas_call x1, Pallas kernels: 1.72 us -> 1.16 us  [on_device(): call(lambda *refs: down_last_kernel(*refs, begin=split), lowrank, [SMEM]...]
  transfers between devices with their start and end apart: 13 -> 13, of which waited for: 4 -> 6; matrix products, arithmetic and copies ran while one was open for 4% -> 4% of each run, Pallas kernels for 16% -> 16%
where the time goes in v6:
time: 49.2 us; the launch traced here: 49 us
  starting transfers between devices  15.3 us (31%)
  waiting for transfers between devices  14.8 us (30%)
  Pallas kernels  11.8 us (24%)
  local copies, waits for them, and re-layouts  6.01 us (12%)
  other arithmetic  1.04 us (2%)
    ppermute x6, waiting for transfers between devices, in_plane(): return lax.ppermute(value, AXES, pairs)  12.2 us
    ppermute x6, starting transfers between devices, in_plane(): return lax.ppermute(value, AXES, pairs)  7.34 us
    pallas_call x2, Pallas kernels, base(): pl.pallas_call(lambda *refs: base_kernel(*refs, skip=skip), out_shape=[ja...  6.28 us
    unnamed x9, local copies, waits for them, and re-layouts  5.91 us
    ppermute x3, starting transfers between devices, along_line(): lax.ppermute(value, 'shard', [(i, (i + 2 * step) % shards) for i in range...  5.39 us
    pallas_call x1, Pallas kernels, on_device(): pl.pallas_call(up_kernel, out_shape=jax.ShapeDtypeStruct((rows, out_width...  2.66 us
    ppermute x2, starting transfers between devices, neighbour(): return lax.ppermute(value, 'shard', [(i, i ^ 1) for i in range(shards)])  2.03 us
    pallas_call x1, Pallas kernels, on_device(): call(down_first_kernel, lowrank, [SMEM] + [VMEM] * 8 + [ANY], 16, [pltpu....  1.63 us
  transfers between devices with their start and end apart: 13, of which 6 were waited for; matrix products, arithmetic and copies ran while one was open for 4% of the time, Pallas kernels for 16%

profile of v6, /device:TPU:0, one launch (start us, length us, event | category | flops | bytes accessed | tf_op | source)
XLA Modules:
  0.0 49.0 jit_solution(3886519061046248564)
XLA Ops:
  0.0 0.5 collective-permute-start.3
  0.5 1.0 %broadcast_select_fusion = bf16[64,1536]{1,0:T(8,128)(2,1)S(1)} fusion(pred[]{:T(512)S(6)} %eq.8, bf16[1,64,1536]{2,1,0:T(8,128)(2,1)} %param.9, bf16[1,1536,64]{1,2,0:T(8,128)(2,1)} %param.8), kind=kLoop, calls=%fused_computation | loop fusion | flops 98304 | bytes 589825 | tf_op jit(solution)/shard_map/jit(_where)/select_n | solution.py:226
  1.5 4.7 %collective-permute-start.2 = (bf16[64,1536]{1,0:T(8,128)(2,1)S(1)}, bf16[64,1536]{1,0:T(8,128)(2,1)S(1)}, u32[]{:S(2)}, u32[]{:S(2)}) collective-permute-start(bf16[64,1536]{1,0:T(8,128)(2,1)S(1)} %broadcast_select_fusion), channel_id=1, source_target_pairs={{0,12},{2,14},{4,0},{6,2},{8,4},{10,6},{12,8},{14,10},{1,13},{3,15... | collective-permute-start | bytes 589832 | tf_op jit(solution)/shard_map/ppermute | solution.py:29
  6.2 0.0 collective-permute-start.1
  6.2 1.5 %collective-permute-start = (bf16[64,1536]{1,0:T(8,128)(2,1)}, bf16[64,1536]{1,0:T(8,128)(2,1)S(1)}, u32[]{:S(2)}, u32[]{:S(2)}) collective-permute-start(bf16[64,1536]{1,0:T(8,128)(2,1)} %bitcast.16), channel_id=1, source_target_pairs={{0,2},{2,0},{4,6},{6,4},{8,10},{10,8},{12,14},{14,12},{1,3},{3,1},... | collective-permute-start | bytes 589832 | tf_op jit(solution)/shard_map/ppermute | solution.py:25
  7.7 0.5 %collective-permute-start.4 = (bf16[64,1536]{1,0:T(8,128)(2,1)}, bf16[64,1536]{1,0:T(8,128)(2,1)S(1)}, u32[]{:S(2)}, u32[]{:S(2)}) collective-permute-start(bf16[64,1536]{1,0:T(8,128)(2,1)} %bitcast.18), channel_id=1, source_target_pairs={{0,2},{2,0},{4,6},{6,4},{8,10},{10,8},{12,14},{14,12},{1,3},{3,1},... | collective-permute-start | bytes 589832 | tf_op jit(solution)/shard_map/ppermute | solution.py:25
  8.2 0.8 %copy.9.refs_4_.ids.refs_1_ = s32[512,1]{1,0:T(8,128)S(1)} copy(s32[512,1]{0,1:T(1,128)} %param.6) | data formatting | bytes 4096 | tf_op args[1]
  9.0 0.1 stack.47.refs_0_.info
  9.1 0.0 collective-permute-done.3.refs_2_
  9.1 0.0 copy-start
  9.1 3.7 %copy-done = bf16[3072,1536]{1,0:T(8,128)(2,1)S(1)} copy-done((bf16[3072,1536]{1,0:T(8,128)(2,1)S(1)}, bf16[3072,1536]{1,0:T(8,128)(2,1)}, u32[]{:S(2)}) %copy-start) | copy-done | bytes 9437208
  12.8 0.0 copy-start.1
  12.8 1.4 %copy-done.1 = bf16[512,1536]{1,0:T(8,128)(2,1)S(1)} copy-done((bf16[512,1536]{1,0:T(8,128)(2,1)S(1)}, bf16[512,1536]{1,0:T(8,128)(2,1)}, u32[]{:S(2)}) %copy-start.1) | copy-done | bytes 1572888
  14.2 2.3 %shard_map.55 = (f32[512,512]{1,0:T(8,128)S(1)}, f32[8,128]{1,0:T(8,128)S(1)}) custom-call(s32[10]{0:T(128)S(1)} %stack.47.refs_0_.info, bf16[512,1536]{1,0:T(8,128)(2,1)S(1)} %copy-done.1, bf16[512,1536]{1,0:T(8,128)(2,1)S(1)} %collective-permute-done.3.refs_2_, bf16[3072,1536]{1,0:T(8,128)(2,1)S(1)} %copy-done, s32[512,1]{1,0:T(8,128)S(1)} %copy.9.refs_4_.ids.refs_1_), custom_call_target="tpu_custom_call" | custom-call | flops 1000 | bytes 1000 | tf_op jit(solution)/shard_map/pallas_call | solution.py:152
  16.5 0.0 collective-permute-done.2.refs_1_
  16.5 0.0 collective-permute-done.1.refs_0_
  16.6 0.0 collective-permute-done.refs_3_.beside
  16.6 1.0 %collective-permute-done.4.refs_4_.refs_1_ = bf16[64,1536]{1,0:T(8,128)(2,1)S(1)} collective-permute-done((bf16[64,1536]{1,0:T(8,128)(2,1)}, bf16[64,1536]{1,0:T(8,128)(2,1)S(1)}, u32[]{:S(2)}, u32[]{:S(2)}) %collective-permute-start.4) | collective-permute-done | bytes 196640 | tf_op jit(solution)/shard_map/ppermute | solution.py:25
  17.6 1.6 %collective-permute-start.5 = (bf16[128,1536]{1,0:T(8,128)(2,1)S(1)}, bf16[128,1536]{1,0:T(8,128)(2,1)S(1)}, u32[]{:S(2)}, u32[]{:S(2)}) collective-permute-start(bf16[128,1536]{1,0:T(8,128)(2,1)S(1)} %get-tuple-element.14.refs_0_.refs_2_), channel_id=1, source_target_pairs={{0,2},{1,17},{2,0},{3,19},{4,6},{5,21},{6,4},{7,23},{8,10},{9,25},... | collective-permute-start | bytes 1179656 | tf_op jit(solution)/shard_map/ppermute | solution.py:39
  19.2 0.7 %collective-permute-start.8 = (bf16[64,1536]{1,0:T(8,128)(2,1)S(1)}, bf16[64,1536]{1,0:T(8,128)(2,1)S(1)}, u32[]{:S(2)}, u32[]{:S(2)}) collective-permute-start(bf16[64,1536]{1,0:T(8,128)(2,1)S(1)} %broadcast_select_fusion), channel_id=1, source_target_pairs={{0,8},{2,10},{4,12},{6,14},{8,0},{10,2},{12,4},{14,6},{1,9},{3,11}... | collective-permute-start | bytes 589832 | tf_op jit(solution)/shard_map/ppermute | solution.py:29
  20.0 1.5 %collective-permute-start.6 = (bf16[128,1536]{1,0:T(8,128)(2,1)S(1)}, bf16[128,1536]{1,0:T(8,128)(2,1)S(1)}, u32[]{:S(2)}, u32[]{:S(2)}) collective-permute-start(bf16[128,1536]{1,0:T(8,128)(2,1)S(1)} %get-tuple-element.14.refs_0_.refs_2_), channel_id=1, source_target_pairs={{0,16},{1,3},{2,18},{3,1},{4,20},{5,7},{6,22},{7,5},{8,24},{9,11},... | collective-permute-start | bytes 1179656 | tf_op jit(solution)/shard_map/ppermute | solution.py:39
  21.5 0.0 copy-start.2
  21.5 4.0 %shard_map.57 = (f32[512,1024]{1,0:T(8,128)S(1)}, f32[8,128]{1,0:T(8,128)S(1)}) custom-call(s32[10]{0:T(128)S(1)} %stack.47.refs_0_.info, bf16[512,1536]{1,0:T(8,128)(2,1)S(1)} %copy-done.1, bf16[512,1536]{1,0:T(8,128)(2,1)S(1)} %collective-permute-done.3.refs_2_, bf16[3072,1536]{1,0:T(8,128)(2,1)S(1)} %copy-done, f32[8,128]{1,0:T(8,128)S(1)} %get-tuple-element.15.refs_4_), custom_call_target="tpu_custom_call" | custom-call | flops 1000 | bytes 1000 | tf_op jit(solution)/shard_map/pallas_call | solution.py:152
  25.4 4.3 %collective-permute-done.5.refs_2_.refs_1_.refs_3_ = bf16[128,1536]{1,0:T(8,128)(2,1)S(1)} collective-permute-done((bf16[128,1536]{1,0:T(8,128)(2,1)S(1)}, bf16[128,1536]{1,0:T(8,128)(2,1)S(1)}, u32[]{:S(2)}, u32[]{:S(2)}) %collective-permute-start.5) | collective-permute-done | bytes 393248 | tf_op jit(solution)/shard_map/ppermute | solution.py:39
  29.7 1.0 %collective-permute-start.7 = (bf16[128,1536]{1,0:T(8,128)(2,1)S(1)}, bf16[128,1536]{1,0:T(8,128)(2,1)S(1)}, u32[]{:S(2)}, u32[]{:S(2)}) collective-permute-start(bf16[128,1536]{1,0:T(8,128)(2,1)S(1)} %collective-permute-done.5.refs_2_.refs_1_.refs_3_), channel_id=1, source_target_pairs={{0,16},{1,3},{2,18},{3,1},{4,20},{5,7},{6,22},{7,5},{8,24},{9,11},... | collective-permute-start | bytes 1179656 | tf_op jit(solution)/shard_map/ppermute | solution.py:39
  30.7 0.0 collective-permute-done.8.refs_0_
  30.7 1.4 %collective-permute-start.9 = (bf16[64,1536]{1,0:T(8,128)(2,1)S(1)}, bf16[64,1536]{1,0:T(8,128)(2,1)S(1)}, u32[]{:S(2)}, u32[]{:S(2)}) collective-permute-start(bf16[64,1536]{1,0:T(8,128)(2,1)S(1)} %get-tuple-element.18.refs_4_.refs_6_), channel_id=1, source_target_pairs={{0,2},{1,17},{2,0},{3,19},{4,6},{5,21},{6,4},{7,23},{8,10},{9,25},... | collective-permute-start | bytes 589832 | tf_op jit(solution)/shard_map/ppermute | solution.py:39
  32.1 1.2 %collective-permute-start.10 = (bf16[64,1536]{1,0:T(8,128)(2,1)S(1)}, bf16[64,1536]{1,0:T(8,128)(2,1)S(1)}, u32[]{:S(2)}, u32[]{:S(2)}) collective-permute-start(bf16[64,1536]{1,0:T(8,128)(2,1)S(1)} %get-tuple-element.18.refs_4_.refs_6_), channel_id=1, source_target_pairs={{0,16},{1,3},{2,18},{3,1},{4,20},{5,7},{6,22},{7,5},{8,24},{9,11},... | collective-permute-start | bytes 589832 | tf_op jit(solution)/shard_map/ppermute | solution.py:39
  33.3 4.6 %collective-permute-done.9.refs_5_.refs_7_ = bf16[64,1536]{1,0:T(8,128)(2,1)S(1)} collective-permute-done((bf16[64,1536]{1,0:T(8,128)(2,1)S(1)}, bf16[64,1536]{1,0:T(8,128)(2,1)S(1)}, u32[]{:S(2)}, u32[]{:S(2)}) %collective-permute-start.9) | collective-permute-done | bytes 196640 | tf_op jit(solution)/shard_map/ppermute | solution.py:39
  37.9 0.7 %collective-permute-start.11 = (bf16[64,1536]{1,0:T(8,128)(2,1)S(1)}, bf16[64,1536]{1,0:T(8,128)(2,1)S(1)}, u32[]{:S(2)}, u32[]{:S(2)}) collective-permute-start(bf16[64,1536]{1,0:T(8,128)(2,1)S(1)} %collective-permute-done.9.refs_5_.refs_7_), channel_id=1, source_target_pairs={{0,16},{1,3},{2,18},{3,1},{4,20},{5,7},{6,22},{7,5},{8,24},{9,11},... | collective-permute-start | bytes 589832 | tf_op jit(solution)/shard_map/ppermute | solution.py:39
  38.6 0.0 collective-permute-done.6.refs_2_.refs_4_
  38.6 0.0 collective-permute-done.7.refs_3_.refs_5_
  38.6 0.0 copy-done.2
  38.6 1.6 %shard_map.59.refs_3_ = f32[512,128]{1,0:T(8,128)S(1)} custom-call(s32[10]{0:T(128)S(1)} %stack.47.refs_0_.info, s32[512,1]{1,0:T(8,128)S(1)} %copy.9.refs_4_.ids.refs_1_, bf16[512,1536]{1,0:T(8,128)(2,1)S(1)} %copy-done.1, bf16[64,1536]{1,0:T(8,128)(2,1)S(1)} %bitcast.17, bf16[64,1536]{1,0:T(8,128)(2,1)S(1)} %collective-permute-done.refs_3_.beside, ...), custom_call_target="tpu_custom_call" | custom-call | tf_op jit(solution)/shard_map/pallas_call | solution.py:239
  40.3 0.0 copy-start.3
  40.3 0.5 collective-permute-done.10.refs_6_.refs_8_
  40.7 2.9 %collective-permute-done.11.refs_7_.refs_9_ = bf16[64,1536]{1,0:T(8,128)(2,1)S(1)} collective-permute-done((bf16[64,1536]{1,0:T(8,128)(2,1)S(1)}, bf16[64,1536]{1,0:T(8,128)(2,1)S(1)}, u32[]{:S(2)}, u32[]{:S(2)}) %collective-permute-start.11) | collective-permute-done | bytes 196640 | tf_op jit(solution)/shard_map/ppermute | solution.py:39
  43.6 1.2 %shard_map.60.mine = f32[512,128]{1,0:T(8,128)S(1)} custom-call(s32[10]{0:T(128)S(1)} %stack.47.refs_0_.info, s32[512,1]{1,0:T(8,128)S(1)} %copy.9.refs_4_.ids.refs_1_, bf16[512,1536]{1,0:T(8,128)(2,1)S(1)} %copy-done.1, f32[512,128]{1,0:T(8,128)S(1)} %shard_map.59.refs_3_, bf16[64,1536]{1,0:T(8,128)(2,1)S(1)} %get-tuple-element.18.refs_4_.refs_6_, ...), custom_call_target="tpu_custom_call" | custom-call | tf_op jit(solution)/shard_map/pallas_call | solution.py:246
  44.7 0.1 collective-permute-start.12
  44.8 1.5 %collective-permute-done.12.theirs = f32[512,128]{1,0:T(8,128)S(1)} collective-permute-done((f32[512,128]{1,0:T(8,128)S(1)}, f32[512,128]{1,0:T(8,128)S(1)}, u32[]{:S(2)}, u32[]{:S(2)}) %collective-permute-start.12) | collective-permute-done | bytes 262176 | tf_op jit(solution)/shard_map/ppermute | solution.py:21
  46.3 0.0 copy-done.3
  46.3 2.7 %shard_map.61 = bf16[512,1536]{1,0:T(8,128)(2,1)} custom-call(s32[10]{0:T(128)S(1)} %stack.47.refs_0_.info, s32[512,1]{1,0:T(8,128)S(1)} %copy.9.refs_4_.ids.refs_1_, f32[512,128]{1,0:T(8,128)S(1)} %shard_map.60.mine, f32[512,128]{1,0:T(8,128)S(1)} %collective-permute-done.12.theirs, f32[512,512]{1,0:T(8,128)S(1)} %get-tuple-element.19.left, ...), custom_call_target="tpu_custom_call" | custom-call | tf_op jit(solution)/shard_map/pallas_call | solution.py:264
  (2 shorter events, 0.0 us)
Async XLA Ops:
  0.0 9.1 %collective-permute-start.3 = (bf16[512,1536]{1,0:T(8,128)(2,1)}, bf16[512,1536]{1,0:T(8,128)(2,1)S(1)}, u32[]{:S(2)}, u32[]{:S(2)}) collective-permute-start(bf16[512,1536]{1,0:T(8,128)(2,1)} %refs_2_.1), channel_id=1, source_target_pairs={{0,1},{1,0},{2,3},{3,2},{4,5},{5,4},{6,7},{7,6},{8,9},{9,8},{10,11... | collective-permute-start | bytes 4718600 | tf_op jit(solution)/shard_map/ppermute | solution.py:21
  1.5 15.0 %collective-permute-start.2 = (bf16[64,1536]{1,0:T(8,128)(2,1)S(1)}, bf16[64,1536]{1,0:T(8,128)(2,1)S(1)}, u32[]{:S(2)}, u32[]{:S(2)}) collective-permute-start(bf16[64,1536]{1,0:T(8,128)(2,1)S(1)} %broadcast_select_fusion), channel_id=1, source_target_pairs={{0,12},{2,14},{4,0},{6,2},{8,4},{10,6},{12,8},{14,10},{1,13},{3,15... | collective-permute-start | bytes 589832 | tf_op jit(solution)/shard_map/ppermute | solution.py:29
  6.2 10.4 %collective-permute-start.1 = (bf16[64,1536]{1,0:T(8,128)(2,1)S(1)}, bf16[64,1536]{1,0:T(8,128)(2,1)S(1)}, u32[]{:S(2)}, u32[]{:S(2)}) collective-permute-start(bf16[64,1536]{1,0:T(8,128)(2,1)S(1)} %broadcast_select_fusion), channel_id=1, source_target_pairs={{0,4},{2,6},{4,8},{6,10},{8,12},{10,14},{12,0},{14,2},{1,5},{3,7},... | collective-permute-start | bytes 589832 | tf_op jit(solution)/shard_map/ppermute | solution.py:29
  6.2 10.4 %collective-permute-start = (bf16[64,1536]{1,0:T(8,128)(2,1)}, bf16[64,1536]{1,0:T(8,128)(2,1)S(1)}, u32[]{:S(2)}, u32[]{:S(2)}) collective-permute-start(bf16[64,1536]{1,0:T(8,128)(2,1)} %bitcast.16), channel_id=1, source_target_pairs={{0,2},{2,0},{4,6},{6,4},{8,10},{10,8},{12,14},{14,12},{1,3},{3,1},... | collective-permute-start | bytes 589832 | tf_op jit(solution)/shard_map/ppermute | solution.py:25
  7.7 9.9 %collective-permute-start.4 = (bf16[64,1536]{1,0:T(8,128)(2,1)}, bf16[64,1536]{1,0:T(8,128)(2,1)S(1)}, u32[]{:S(2)}, u32[]{:S(2)}) collective-permute-start(bf16[64,1536]{1,0:T(8,128)(2,1)} %bitcast.18), channel_id=1, source_target_pairs={{0,2},{2,0},{4,6},{6,4},{8,10},{10,8},{12,14},{14,12},{1,3},{3,1},... | collective-permute-start | bytes 589832 | tf_op jit(solution)/shard_map/ppermute | solution.py:25
  9.1 3.7 %copy-start = (bf16[3072,1536]{1,0:T(8,128)(2,1)S(1)}, bf16[3072,1536]{1,0:T(8,128)(2,1)}, u32[]{:S(2)}) copy-start(bf16[3072,1536]{1,0:T(8,128)(2,1)} %refs_3_.3) | copy-start | bytes 28311556
  12.8 1.4 %copy-start.1 = (bf16[512,1536]{1,0:T(8,128)(2,1)S(1)}, bf16[512,1536]{1,0:T(8,128)(2,1)}, u32[]{:S(2)}) copy-start(bf16[512,1536]{1,0:T(8,128)(2,1)} %refs_2_.1) | copy-start | bytes 4718596
  17.6 12.1 %collective-permute-start.5 = (bf16[128,1536]{1,0:T(8,128)(2,1)S(1)}, bf16[128,1536]{1,0:T(8,128)(2,1)S(1)}, u32[]{:S(2)}, u32[]{:S(2)}) collective-permute-start(bf16[128,1536]{1,0:T(8,128)(2,1)S(1)} %get-tuple-element.14.refs_0_.refs_2_), channel_id=1, source_target_pairs={{0,2},{1,17},{2,0},{3,19},{4,6},{5,21},{6,4},{7,23},{8,10},{9,25},... | collective-permute-start | bytes 1179656 | tf_op jit(solution)/shard_map/ppermute | solution.py:39
  19.2 11.5 %collective-permute-start.8 = (bf16[64,1536]{1,0:T(8,128)(2,1)S(1)}, bf16[64,1536]{1,0:T(8,128)(2,1)S(1)}, u32[]{:S(2)}, u32[]{:S(2)}) collective-permute-start(bf16[64,1536]{1,0:T(8,128)(2,1)S(1)} %broadcast_select_fusion), channel_id=1, source_target_pairs={{0,8},{2,10},{4,12},{6,14},{8,0},{10,2},{12,4},{14,6},{1,9},{3,11}... | collective-permute-start | bytes 589832 | tf_op jit(solution)/shard_map/ppermute | solution.py:29
  20.0 18.6 %collective-permute-start.6 = (bf16[128,1536]{1,0:T(8,128)(2,1)S(1)}, bf16[128,1536]{1,0:T(8,128)(2,1)S(1)}, u32[]{:S(2)}, u32[]{:S(2)}) collective-permute-start(bf16[128,1536]{1,0:T(8,128)(2,1)S(1)} %get-tuple-element.14.refs_0_.refs_2_), channel_id=1, source_target_pairs={{0,16},{1,3},{2,18},{3,1},{4,20},{5,7},{6,22},{7,5},{8,24},{9,11},... | collective-permute-start | bytes 1179656 | tf_op jit(solution)/shard_map/ppermute | solution.py:39
  21.5 17.2 %copy-start.2 = (bf16[1,1536,64]{1,2,0:T(8,128)(2,1)S(1)}, bf16[1,1536,64]{1,2,0:T(8,128)(2,1)}, u32[]{:S(2)}) copy-start(bf16[1,1536,64]{1,2,0:T(8,128)(2,1)} %param.8) | copy-start | bytes 589828
  29.7 8.9 %collective-permute-start.7 = (bf16[128,1536]{1,0:T(8,128)(2,1)S(1)}, bf16[128,1536]{1,0:T(8,128)(2,1)S(1)}, u32[]{:S(2)}, u32[]{:S(2)}) collective-permute-start(bf16[128,1536]{1,0:T(8,128)(2,1)S(1)} %collective-permute-done.5.refs_2_.refs_1_.refs_3_), channel_id=1, source_target_pairs={{0,16},{1,3},{2,18},{3,1},{4,20},{5,7},{6,22},{7,5},{8,24},{9,11},... | collective-permute-start | bytes 1179656 | tf_op jit(solution)/shard_map/ppermute | solution.py:39
  30.7 7.2 %collective-permute-start.9 = (bf16[64,1536]{1,0:T(8,128)(2,1)S(1)}, bf16[64,1536]{1,0:T(8,128)(2,1)S(1)}, u32[]{:S(2)}, u32[]{:S(2)}) collective-permute-start(bf16[64,1536]{1,0:T(8,128)(2,1)S(1)} %get-tuple-element.18.refs_4_.refs_6_), channel_id=1, source_target_pairs={{0,2},{1,17},{2,0},{3,19},{4,6},{5,21},{6,4},{7,23},{8,10},{9,25},... | collective-permute-start | bytes 589832 | tf_op jit(solution)/shard_map/ppermute | solution.py:39
  32.1 8.6 %collective-permute-start.10 = (bf16[64,1536]{1,0:T(8,128)(2,1)S(1)}, bf16[64,1536]{1,0:T(8,128)(2,1)S(1)}, u32[]{:S(2)}, u32[]{:S(2)}) collective-permute-start(bf16[64,1536]{1,0:T(8,128)(2,1)S(1)} %get-tuple-element.18.refs_4_.refs_6_), channel_id=1, source_target_pairs={{0,16},{1,3},{2,18},{3,1},{4,20},{5,7},{6,22},{7,5},{8,24},{9,11},... | collective-permute-start | bytes 589832 | tf_op jit(solution)/shard_map/ppermute | solution.py:39
  37.9 5.7 %collective-permute-start.11 = (bf16[64,1536]{1,0:T(8,128)(2,1)S(1)}, bf16[64,1536]{1,0:T(8,128)(2,1)S(1)}, u32[]{:S(2)}, u32[]{:S(2)}) collective-permute-start(bf16[64,1536]{1,0:T(8,128)(2,1)S(1)} %collective-permute-done.9.refs_5_.refs_7_), channel_id=1, source_target_pairs={{0,16},{1,3},{2,18},{3,1},{4,20},{5,7},{6,22},{7,5},{8,24},{9,11},... | collective-permute-start | bytes 589832 | tf_op jit(solution)/shard_map/ppermute | solution.py:39
  40.3 6.1 %copy-start.3 = (bf16[1,64,1536]{2,1,0:T(8,128)(2,1)S(1)}, bf16[1,64,1536]{2,1,0:T(8,128)(2,1)}, u32[]{:S(2)}) copy-start(bf16[1,64,1536]{2,1,0:T(8,128)(2,1)} %param.9) | copy-start | bytes 589828
  44.7 1.6 %collective-permute-start.12 = (f32[512,128]{1,0:T(8,128)S(1)}, f32[512,128]{1,0:T(8,128)S(1)}, u32[]{:S(2)}, u32[]{:S(2)}) collective-permute-start(f32[512,128]{1,0:T(8,128)S(1)} %shard_map.60.mine), channel_id=1, source_target_pairs={{0,1},{1,0},{2,3},{3,2},{4,5},{5,4},{6,7},{7,6},{8,9},{9,8},{10,11... | collective-permute-start | bytes 786440 | tf_op jit(solution)/shard_map/ppermute | solution.py:21

commit v7 on v6

v7 whole, which is shorter than its diff:
```python
import jax
import jax.numpy as jnp
import numpy as np
from jax import lax
from jax.experimental import pallas as pl
from jax.experimental.pallas import tpu as pltpu
from jax.sharding import PartitionSpec as P

MIB = 1024 * 1024
CHUNK = 512
AXES = ("replica", "shard", "tensor")
FIRST_OWNER = 2
SMEM = pl.BlockSpec(memory_space=pltpu.SMEM)
VMEM = pl.BlockSpec(memory_space=pltpu.VMEM)
ANY = pl.BlockSpec(memory_space=pl.ANY)
TOKEN = jax.ShapeDtypeStruct((8, 128), jnp.float32)


def swap(value, axis):
    return lax.ppermute(value, axis, [(0, 1), (1, 0)])


def neighbour(value, shards):
    return lax.ppermute(value, "shard", [(i, i ^ 1) for i in range(shards)])


def along_line(value, shards, step):
    return lax.ppermute(value, "shard", [(i, (i + 2 * step) % shards) for i in range(shards)])


def in_plane(value, shards, first):
    pairs = []
    for r in range(2):
        for s in range(shards):
            for t in range(2):
                to_r, to_s = (r, s ^ 1) if (t == 0) == first else (r ^ 1, s)
                pairs.append(((r * shards + s) * 2 + t, (to_r * shards + to_s) * 2 + t))
    return lax.ppermute(value, AXES, pairs)


def call(kernel, out_shape, in_specs, limit, scratch=(), flops=0, moved=0):
    return pl.pallas_call(
        kernel,
        out_shape=out_shape,
        in_specs=in_specs,
        out_specs=jax.tree.map(lambda _: VMEM, out_shape),
        scratch_shapes=list(scratch),
        compiler_params=pltpu.CompilerParams(vmem_limit_bytes=limit * MIB),
        cost_estimate=pl.CostEstimate(flops=flops, bytes_accessed=moved, transcendentals=0),
    )


def owner_row(info, blocks, rank):
    place = lax.broadcasted_iota(jnp.int32, (1, len(blocks) * rank), 1) // rank
    row = jnp.full(place.shape, -1, jnp.int32)
    for number, block in enumerate(blocks):
        if block is not None:
            row = jnp.where(place == number, info[FIRST_OWNER + block], row)
    return row


def pack(pieces, *after):
    count = len(pieces)
    total = sum(rows for _, _, rows in pieces)
    width, dtype = pieces[0][0].shape[1], pieces[0][0].dtype

    def kernel(*refs):
        out, token = refs[-2:]
        top = 0
        for ref, (_, begin, rows) in zip(refs, pieces):
            out[top : top + rows, :] = ref[begin : begin + rows, :]
            top += rows
        token[...] = jnp.zeros_like(token)

    return call(
        kernel,
        [jax.ShapeDtypeStruct((total, width), dtype), TOKEN],
        [VMEM] * count + [ANY] * len(after),
        4,
    )(*[array for array, _, _ in pieces], *after)


def put(blocks, stack, top, rank):
    for number, parts in enumerate(blocks):
        place = top + 2 * number * rank
        for ref, begin, rows in parts:
            stack[place : place + rows, :] = ref[begin : begin + rows, :]
            place += rows


def fill_here(info, holds, received, stack, top, rank):
    early, early_first, early_second, late, late_first, late_second, _, _ = received

    def blocks(pair, single):
        return [[(pair, 0, rank)], [(pair, rank, rank)], [(single, 0, rank)]]

    swapped = ((early_second, late_second), (early_first, late_first))
    pl.when(holds)(lambda: put(blocks(early, late), stack, top, rank))
    for core in range(2):
        away = jnp.logical_not(holds) & (info[0] == core)
        pl.when(away)(lambda refs=swapped[core]: put(blocks(*refs), stack, top, rank))


def fill_beside(info, holds, received, stack, top, rank, direct=True, corner=True):
    _, early_first, early_second, _, late_first, late_second, corner_one, corner_two = received
    half = rank // 2
    swapped = ((early_first, late_first), (early_second, late_second))
    if direct:
        for core in range(2):

            def straight(refs=swapped[core]):
                pair, single = refs
                blocks = [[(pair, 0, rank)], [(pair, rank, rank)], [(single, 0, rank)]]
                put(blocks, stack, top, rank)

            pl.when(holds & (info[0] == core))(straight)
    if corner:

        def turned():
            last = [(corner_one, rank, half), (corner_two, rank, half)]
            put([[(corner_one, 0, rank)], [(corner_two, 0, rank)], last], stack, top, rank)

        pl.when(jnp.logical_not(holds))(turned)


def clear(stack, top, rank, count):
    for number in range(count):
        place = top + 2 * number * rank
        stack[place : place + rank, :] = jnp.zeros((rank, stack.shape[1]), stack.dtype)


def masked_products(info, ids, latent, stack, blocks, rank):
    total = None
    width = 2 * rank
    for skip in range(0, stack.shape[0], CHUNK):
        count = min(CHUNK, stack.shape[0] - skip)
        part = lax.dot_general(
            latent[...],
            stack[skip : skip + count, :],
            (((1,), (1,)), ((), ())),
            preferred_element_type=jnp.float32,
        )
        owners = owner_row(info, blocks[skip // rank : (skip + count) // rank], rank)
        part = jnp.where(ids[...] == owners, part, 0.0)
        for lane in range(0, count, width):
            fold = part[:, lane : lane + width]
            total = fold if total is None else total + fold
    return total


def down_whole_kernel(info, ids, latent, stack, out):
    rank = out.shape[1] // 2
    blocks = range(stack.shape[0] // rank)
    out[...] = masked_products(info, ids, latent, stack, blocks, rank)


def down_first_kernel(info, ids, latent, own, beside, *refs):
    *received, _, out, stack = refs
    rank = own.shape[0]
    holds = info[1] == 1
    stack[0:rank, :] = own[...]
    stack[rank : 2 * rank, :] = beside[...]
    fill_here(info, holds, (*received, None, None), stack, 2 * rank, rank)
    fill_beside(info, holds, (*received, None, None), stack, 3 * rank, rank, corner=False)
    pl.when(jnp.logical_not(holds))(lambda: clear(stack, 3 * rank, rank, 3))
    out[...] = masked_products(info, ids, latent, stack, range(stack.shape[0] // rank), rank)


def down_last_kernel(info, ids, latent, earlier, corner_one, corner_two, out, stack):
    rank = out.shape[1] // 2
    half = rank // 2
    holds = info[1] == 1

    @pl.when(holds)
    def _():
        out[...] = earlier[...]

    @pl.when(jnp.logical_not(holds))
    def _():
        stack[0:rank, :] = corner_one[0:rank, :]
        stack[rank : 2 * rank, :] = corner_two[0:rank, :]
        stack[2 * rank : 2 * rank + half, :] = corner_one[rank : rank + half, :]
        stack[2 * rank + half : 3 * rank, :] = corner_two[rank : rank + half, :]
        stack[3 * rank : 4 * rank, :] = jnp.zeros((rank, stack.shape[1]), stack.dtype)
        pair = masked_products(info, ids, latent, stack, (3, 5, 7, None), rank)
        fold = pair[:, :rank] + pair[:, rank:]
        out[...] = earlier[...] + jnp.concatenate([jnp.zeros_like(fold), fold], axis=1)


def base_kernel(info, own, other, weight, *refs, skip):
    out, token = refs[-2:]
    token[...] = jnp.zeros_like(token)
    width = own.shape[1]
    mine = pl.ds(pl.multiple_of(info[0] * width, width), width)
    rest = pl.ds(pl.multiple_of((1 - info[0]) * width, width), width)
    for begin in range(0, out.shape[1], CHUNK):
        place = slice(begin, begin + CHUNK)
        source = slice(skip + begin, skip + begin + CHUNK)
        out[:, place] = jnp.dot(
            own[...], weight[mine, source], preferred_element_type=jnp.float32
        ) + jnp.dot(other[...], weight[rest, source], preferred_element_type=jnp.float32)


def base(info, latent, other, weight, after, skip, end):
    rows, columns = latent.shape[0], end - skip
    return pl.pallas_call(
        lambda *refs: base_kernel(*refs, skip=skip),
        out_shape=[jax.ShapeDtypeStruct((rows, columns), jnp.float32), TOKEN],
        in_specs=[SMEM, VMEM, VMEM, VMEM] + [ANY] * len(after),
        out_specs=[VMEM, VMEM],
        compiler_params=pltpu.CompilerParams(vmem_limit_bytes=24 * MIB),
        cost_estimate=pl.CostEstimate(flops=1000, bytes_accessed=1000, transcendentals=0),
    )(info, latent, other, weight, *after)


def up_kernel(info, ids, mine, theirs, *refs, base_parts):
    *pieces, out, stack, wide, sems, staged = refs[base_parts:]
    bases = [
        part.at[:, pl.ds(begin, CHUNK)]
        for part in refs[:base_parts]
        for begin in range(0, part.shape[1], CHUNK)
    ]
    rank = mine.shape[1] // 2
    if len(pieces) == 1:
        stack[...] = pieces[0][...]
    else:
        own, beside, *received = pieces
        holds = info[1] == 0
        stack[0:rank, :] = own[...]
        stack[rank : 2 * rank, :] = beside[...]
        fill_here(info, holds, received, stack, 2 * rank, rank)
        fill_beside(info, holds, received, stack, 3 * rank, rank)
    lowrank = (mine[...] + theirs[...]).astype(jnp.bfloat16)
    zeros = jnp.zeros_like(lowrank)
    width = 2 * rank
    for lane in range(0, wide.shape[1], width):
        mask = ids[...] == owner_row(info, (lane // rank, lane // rank + 1), rank)
        wide[:, lane : lane + width] = jnp.where(mask, lowrank, zeros)
    copies = []
    tiles, _, tile = staged.shape
    for number in range(tiles):
        place = pl.ds(number * tile, tile)
        delta = jnp.dot(wide[...], stack[:, place], preferred_element_type=jnp.float32)
        total = bases[number][...] + delta.astype(jnp.bfloat16).astype(jnp.float32)
        staged[number] = total.astype(out.dtype)
        copies.append(
            pltpu.make_async_copy(staged.at[number], out.at[:, place], sems.at[number])
        )
        copies[-1].start()
    for copy in copies:
        copy.wait()


def on_device(latent, row_adapter_index, shared_weight, adapter_down_weight, adapter_up_weight):
    rows, half_width = latent.shape
    out_width = shared_weight.shape[1]
    local_adapters, _, rank = adapter_down_weight.shape
    shards = lax.axis_size("shard")
    adapters = shards * local_adapters
    columns = adapters * rank
    index, core = lax.axis_index("shard"), lax.axis_index("tensor")
    holds_down = core == lax.axis_index("replica")
    tiles = out_width // CHUNK
    cuts = [tiles * number // 3 * CHUNK for number in range(4)]
    down = jnp.swapaxes(adapter_down_weight, 1, 2).reshape(local_adapters * rank, half_width)
    up = adapter_up_weight.reshape(local_adapters * rank, out_width)
    ids = row_adapter_index
    routed = shards == 8 and local_adapters == 1 and lax.axis_size("replica") == 2
    routed = routed and half_width == out_width and tiles % 3 == 0
    lowrank = jax.ShapeDtypeStruct((rows, 2 * rank), jnp.float32)
    if routed:
        sources = [(index - 2 * step) % shards for step in (0, 1, 3, 2)]
        owners = [a for source in sources for a in (source, source ^ 1)]
    else:
        owners = list(range(adapters))
    info = jnp.stack([jnp.asarray(v, jnp.int32) for v in (core, holds_down, *owners)])
    if routed:
        piece = jnp.where(holds_down, down, up)
        line = {step: along_line(piece, shards, step) for step in (1, 3)}
        other = swap(latent, "tensor")
        down_beside, up_beside = neighbour(down, shards), neighbour(up, shards)
        parts = []
        part, token = base(info, latent, other, shared_weight, [ids], cuts[0], cuts[1])
        parts.append(part)
        relay, token = pack([(line[1], 0, rank)], token)
        line[2] = along_line(relay, shards, 1)
        early, token = pack([(line[1], 0, rank), (line[3], 0, rank)], token, down_beside, up_beside)
        part, token = base(info, latent, other, shared_weight, [token], cuts[1], cuts[2])
        parts.append(part)
        early_first, early_second = in_plane(early, shards, True), in_plane(early, shards, False)
        late, token = pack([(line[2], 0, rank)], token)
        part, token = base(info, latent, other, shared_weight, [token], cuts[2], cuts[3])
        parts.append(part)
        late_first, late_second = in_plane(late, shards, True), in_plane(late, shards, False)
        half = rank // 2
        turn_one, token = pack([(early_first, 0, rank), (late_first, 0, half)], token)
        turn_two, token = pack([(early_second, rank, rank), (late_second, half, half)], token)
        corner_one = in_plane(turn_one, shards, False)
        corner_two = in_plane(turn_two, shards, True)
        received = [early, early_first, early_second, late, late_first, late_second]
        mine = call(
            down_first_kernel,
            lowrank,
            [SMEM] + [VMEM] * 10 + [ANY],
            16,
            [pltpu.VMEM((columns, half_width), latent.dtype)],
        )(info, ids, latent, down, down_beside, *received, token)
        mine = call(
            down_last_kernel,
            lowrank,
            [SMEM] + [VMEM] * 5,
            16,
            [pltpu.VMEM((4 * rank, half_width), latent.dtype)],
        )(info, ids, latent, mine, corner_one, corner_two)
        up_pieces = [up, up_beside, *received, corner_one, corner_two]
    else:
        other = swap(latent, "tensor")
        parts, token = [], ids
        for begin, end in zip(cuts[:-1], cuts[1:]):
            part, token = base(info, latent, other, shared_weight, [token], begin, end)
            parts.append(part)
        mine = call(down_whole_kernel, lowrank, [SMEM] + [VMEM] * 3, 48)(
            info, ids, latent, lax.all_gather(down, "shard", axis=0, tiled=True)
        )
        up_pieces = [lax.all_gather(up, "shard", axis=0, tiled=True)]
    theirs = swap(mine, "tensor")

    return pl.pallas_call(
        lambda *refs: up_kernel(*refs, base_parts=len(parts)),
        out_shape=jax.ShapeDtypeStruct((rows, out_width), latent.dtype),
        in_specs=[SMEM] + [VMEM] * (3 + len(parts) + len(up_pieces)),
        out_specs=ANY,
        scratch_shapes=[
            pltpu.VMEM((columns, out_width), latent.dtype),
            pltpu.VMEM((rows, columns), latent.dtype),
            pltpu.SemaphoreType.DMA((tiles,)),
            pltpu.VMEM((tiles, rows, CHUNK), latent.dtype),
        ],
        compiler_params=pltpu.CompilerParams(vmem_limit_bytes=(24 if routed else 56) * MIB),
    )(info, ids, mine, theirs, *parts, *up_pieces)


def solution(mesh):
    return jax.shard_map(
        on_device,
        mesh=mesh,
        in_specs=(
            P(("replica", "shard"), "tensor"),
            P(("replica", "shard"), None),
            P(None, "tensor"),
            P("shard", "tensor", None),
            P("shard", None, "tensor"),
        ),
        out_specs=P(("replica", "shard"), "tensor"),
        check_vma=False,
    )
```

time: 49.2 us -> 47.3 us (0.961)
  waiting for transfers between devices: 14.8 us -> 12.2 us
    ppermute x6, waiting for transfers between devices: 12.2 us -> 7.9 us  [in_plane(): return lax.ppermute(value, AXES, pairs)]
    ppermute x3, waiting for transfers between devices: 0.01 us -> 1.85 us  [along_line(): lax.ppermute(value, 'shard', [(i, (i + 2 * step) % shards) for i in range...]
    ppermute x6, starting transfers between devices: 7.34 us -> 8.27 us  [in_plane(): return lax.ppermute(value, AXES, pairs)]
    pallas_call x2 -> x3, Pallas kernels: 6.28 us -> 6.99 us  [base(): pl.pallas_call(lambda *refs: base_kernel(*refs, skip=skip), out_shape=[ja...]
    ppermute x3, starting transfers between devices: 5.39 us -> 4.78 us  [along_line(): lax.ppermute(value, 'shard', [(i, (i + 2 * step) % shards) for i in range...]
    pallas_call x5 -> x8, Pallas kernels: 5.49 us -> 5.02 us  [the longest x1 2.67 us: on_device(): pl.pallas_call(lambda *refs: up_kernel(*refs, base_parts=len(parts)), out...]
  transfers between devices with their start and end apart: 13 -> 13, of which waited for: 6 -> 5; matrix products, arithmetic and copies ran while one was open for 4% -> 4% of each run, Pallas kernels for 16% -> 19%
where the time goes in v7:
time: 47.3 us; the launch traced here: 47 us
  starting transfers between devices  15.6 us (33%)
  waiting for transfers between devices  12.2 us (26%)
  Pallas kernels  12 us (25%)
  local copies, waits for them, and re-layouts  6.01 us (13%)
  other arithmetic  1.04 us (2%)
    ppermute x6, starting transfers between devices, in_plane(): return lax.ppermute(value, AXES, pairs)  8.27 us
    ppermute x6, waiting for transfers between devices, in_plane(): return lax.ppermute(value, AXES, pairs)  7.9 us
    pallas_call x3, Pallas kernels, base(): pl.pallas_call(lambda *refs: base_kernel(*refs, skip=skip), out_shape=[ja...  6.99 us
    unnamed x9, local copies, waits for them, and re-layouts  5.91 us
    ppermute x3, starting transfers between devices, along_line(): lax.ppermute(value, 'shard', [(i, (i + 2 * step) % shards) for i in range...  4.78 us
    pallas_call x1, Pallas kernels, on_device(): pl.pallas_call(lambda *refs: up_kernel(*refs, base_parts=len(parts)), out...  2.67 us
    ppermute x2, starting transfers between devices, neighbour(): return lax.ppermute(value, 'shard', [(i, i ^ 1) for i in range(shards)])  2.03 us
    ppermute x3, waiting for transfers between devices, along_line(): lax.ppermute(value, 'shard', [(i, (i + 2 * step) % shards) for i in range...  1.85 us
  transfers between devices with their start and end apart: 13, of which 5 were waited for; matrix products, arithmetic and copies ran while one was open for 4% of the time, Pallas kernels for 19%

profile of v7, /device:TPU:0, one launch (start us, length us, event | category | flops | bytes accessed | tf_op | source)
XLA Modules:
  0.0 47.0 jit_solution(9156003341247639487)
XLA Ops:
  0.0 0.5 collective-permute-start.3
  0.5 1.0 %broadcast_select_fusion = bf16[64,1536]{1,0:T(8,128)(2,1)S(1)} fusion(pred[]{:T(512)S(6)} %eq.8, bf16[1,64,1536]{2,1,0:T(8,128)(2,1)} %param.9, bf16[1,1536,64]{1,2,0:T(8,128)(2,1)} %param.8), kind=kLoop, calls=%fused_computation | loop fusion | flops 98304 | bytes 589825 | tf_op jit(solution)/shard_map/jit(_where)/select_n | solution.py:278
  1.5 2.6 %collective-permute-start.1 = (bf16[64,1536]{1,0:T(8,128)(2,1)S(1)}, bf16[64,1536]{1,0:T(8,128)(2,1)S(1)}, u32[]{:S(2)}, u32[]{:S(2)}) collective-permute-start(bf16[64,1536]{1,0:T(8,128)(2,1)S(1)} %broadcast_select_fusion), channel_id=1, source_target_pairs={{0,4},{2,6},{4,8},{6,10},{8,12},{10,14},{12,0},{14,2},{1,5},{3,7},... | collective-permute-start | bytes 589832 | tf_op jit(solution)/shard_map/ppermute | solution.py:28
  4.1 2.1 %collective-permute-start.2 = (bf16[64,1536]{1,0:T(8,128)(2,1)S(1)}, bf16[64,1536]{1,0:T(8,128)(2,1)S(1)}, u32[]{:S(2)}, u32[]{:S(2)}) collective-permute-start(bf16[64,1536]{1,0:T(8,128)(2,1)S(1)} %broadcast_select_fusion), channel_id=1, source_target_pairs={{0,12},{2,14},{4,0},{6,2},{8,4},{10,6},{12,8},{14,10},{1,13},{3,15... | collective-permute-start | bytes 589832 | tf_op jit(solution)/shard_map/ppermute | solution.py:28
  6.2 1.7 %collective-permute-start = (bf16[64,1536]{1,0:T(8,128)(2,1)}, bf16[64,1536]{1,0:T(8,128)(2,1)S(1)}, u32[]{:S(2)}, u32[]{:S(2)}) collective-permute-start(bf16[64,1536]{1,0:T(8,128)(2,1)} %bitcast.16), channel_id=1, source_target_pairs={{0,2},{2,0},{4,6},{6,4},{8,10},{10,8},{12,14},{14,12},{1,3},{3,1},... | collective-permute-start | bytes 589832 | tf_op jit(solution)/shard_map/ppermute | solution.py:24
  7.9 0.3 collective-permute-start.4
  8.2 0.8 %copy.9.refs_4_.ids.refs_1_ = s32[512,1]{1,0:T(8,128)S(1)} copy(s32[512,1]{0,1:T(1,128)} %param.6) | data formatting | bytes 4096 | tf_op args[1]
  9.1 0.1 stack.47.refs_0_.info
  9.2 0.0 collective-permute-done.3.refs_2_
  9.2 0.0 copy-start
  9.2 3.7 %copy-done = bf16[3072,1536]{1,0:T(8,128)(2,1)S(1)} copy-done((bf16[3072,1536]{1,0:T(8,128)(2,1)S(1)}, bf16[3072,1536]{1,0:T(8,128)(2,1)}, u32[]{:S(2)}) %copy-start) | copy-done | bytes 9437208
  12.9 0.0 copy-start.1
  12.9 1.4 %copy-done.1 = bf16[512,1536]{1,0:T(8,128)(2,1)S(1)} copy-done((bf16[512,1536]{1,0:T(8,128)(2,1)S(1)}, bf16[512,1536]{1,0:T(8,128)(2,1)}, u32[]{:S(2)}) %copy-start.1) | copy-done | bytes 1572888
  14.3 2.3 %shard_map.55 = (f32[512,512]{1,0:T(8,128)S(1)}, f32[8,128]{1,0:T(8,128)S(1)}) custom-call(s32[10]{0:T(128)S(1)} %stack.47.refs_0_.info, bf16[512,1536]{1,0:T(8,128)(2,1)S(1)} %copy-done.1, bf16[512,1536]{1,0:T(8,128)(2,1)S(1)} %collective-permute-done.3.refs_2_, bf16[3072,1536]{1,0:T(8,128)(2,1)S(1)} %copy-done, s32[512,1]{1,0:T(8,128)S(1)} %copy.9.refs_4_.ids.refs_1_), custom_call_target="tpu_custom_call" | custom-call | flops 1000 | bytes 1000 | tf_op jit(solution)/shard_map/pallas_call | solution.py:206
  16.6 0.0 collective-permute-done.1.refs_0_
  16.6 0.1 collective-permute-start.7
  16.7 0.0 collective-permute-done.2.refs_1_
  16.7 0.0 collective-permute-done.refs_3_.beside
  16.7 1.0 %collective-permute-done.4.refs_4_.refs_8_ = bf16[64,1536]{1,0:T(8,128)(2,1)S(1)} collective-permute-done((bf16[64,1536]{1,0:T(8,128)(2,1)}, bf16[64,1536]{1,0:T(8,128)(2,1)S(1)}, u32[]{:S(2)}, u32[]{:S(2)}) %collective-permute-start.4) | collective-permute-done | bytes 196640 | tf_op jit(solution)/shard_map/ppermute | solution.py:24
  17.7 1.6 %collective-permute-start.5 = (bf16[128,1536]{1,0:T(8,128)(2,1)S(1)}, bf16[128,1536]{1,0:T(8,128)(2,1)S(1)}, u32[]{:S(2)}, u32[]{:S(2)}) collective-permute-start(bf16[128,1536]{1,0:T(8,128)(2,1)S(1)} %get-tuple-element.23.refs_0_.refs_9_), channel_id=1, source_target_pairs={{0,2},{1,17},{2,0},{3,19},{4,6},{5,21},{6,4},{7,23},{8,10},{9,25},... | collective-permute-start | bytes 1179656 | tf_op jit(solution)/shard_map/ppermute | solution.py:38
  19.3 1.5 %collective-permute-start.6 = (bf16[128,1536]{1,0:T(8,128)(2,1)S(1)}, bf16[128,1536]{1,0:T(8,128)(2,1)S(1)}, u32[]{:S(2)}, u32[]{:S(2)}) collective-permute-start(bf16[128,1536]{1,0:T(8,128)(2,1)S(1)} %get-tuple-element.23.refs_0_.refs_9_), channel_id=1, source_target_pairs={{0,16},{1,3},{2,18},{3,1},{4,20},{5,7},{6,22},{7,5},{8,24},{9,11},... | collective-permute-start | bytes 1179656 | tf_op jit(solution)/shard_map/ppermute | solution.py:38
  20.8 2.3 %shard_map.58 = (f32[512,512]{1,0:T(8,128)S(1)}, f32[8,128]{1,0:T(8,128)S(1)}) custom-call(s32[10]{0:T(128)S(1)} %stack.47.refs_0_.info, bf16[512,1536]{1,0:T(8,128)(2,1)S(1)} %copy-done.1, bf16[512,1536]{1,0:T(8,128)(2,1)S(1)} %collective-permute-done.3.refs_2_, bf16[3072,1536]{1,0:T(8,128)(2,1)S(1)} %copy-done, f32[8,128]{1,0:T(8,128)S(1)} %get-tuple-element.25.refs_4_), custom_call_target="tpu_custom_call" | custom-call | flops 1000 | bytes 1000 | tf_op jit(solution)/shard_map/pallas_call | solution.py:206
  23.1 1.8 %collective-permute-done.7.refs_0_ = bf16[64,1536]{1,0:T(8,128)(2,1)S(1)} collective-permute-done((bf16[64,1536]{1,0:T(8,128)(2,1)S(1)}, bf16[64,1536]{1,0:T(8,128)(2,1)S(1)}, u32[]{:S(2)}, u32[]{:S(2)}) %collective-permute-start.7) | collective-permute-done | bytes 196640 | tf_op jit(solution)/shard_map/ppermute | solution.py:28
  25.0 1.6 %collective-permute-start.8 = (bf16[64,1536]{1,0:T(8,128)(2,1)S(1)}, bf16[64,1536]{1,0:T(8,128)(2,1)S(1)}, u32[]{:S(2)}, u32[]{:S(2)}) collective-permute-start(bf16[64,1536]{1,0:T(8,128)(2,1)S(1)} %get-tuple-element.27.refs_3_.refs_12_), channel_id=1, source_target_pairs={{0,2},{1,17},{2,0},{3,19},{4,6},{5,21},{6,4},{7,23},{8,10},{9,25},... | collective-permute-start | bytes 589832 | tf_op jit(solution)/shard_map/ppermute | solution.py:38
  26.6 1.5 %collective-permute-start.9 = (bf16[64,1536]{1,0:T(8,128)(2,1)S(1)}, bf16[64,1536]{1,0:T(8,128)(2,1)S(1)}, u32[]{:S(2)}, u32[]{:S(2)}) collective-permute-start(bf16[64,1536]{1,0:T(8,128)(2,1)S(1)} %get-tuple-element.27.refs_3_.refs_12_), channel_id=1, source_target_pairs={{0,16},{1,3},{2,18},{3,1},{4,20},{5,7},{6,22},{7,5},{8,24},{9,11},... | collective-permute-start | bytes 589832 | tf_op jit(solution)/shard_map/ppermute | solution.py:38
  28.1 0.0 copy-start.2
  28.1 2.3 %shard_map.60 = (f32[512,512]{1,0:T(8,128)S(1)}, f32[8,128]{1,0:T(8,128)S(1)}) custom-call(s32[10]{0:T(128)S(1)} %stack.47.refs_0_.info, bf16[512,1536]{1,0:T(8,128)(2,1)S(1)} %copy-done.1, bf16[512,1536]{1,0:T(8,128)(2,1)S(1)} %collective-permute-done.3.refs_2_, bf16[3072,1536]{1,0:T(8,128)(2,1)S(1)} %copy-done, f32[8,128]{1,0:T(8,128)S(1)} %get-tuple-element.28.refs_4_), custom_call_target="tpu_custom_call" | custom-call | flops 1000 | bytes 1000 | tf_op jit(solution)/shard_map/pallas_call | solution.py:206
  30.4 0.0 collective-permute-done.5.refs_0_.refs_1_.refs_10_
  30.4 3.1 %collective-permute-done.8.refs_1_.refs_4_.refs_13_ = bf16[64,1536]{1,0:T(8,128)(2,1)S(1)} collective-permute-done((bf16[64,1536]{1,0:T(8,128)(2,1)S(1)}, bf16[64,1536]{1,0:T(8,128)(2,1)S(1)}, u32[]{:S(2)}, u32[]{:S(2)}) %collective-permute-start.8) | collective-permute-done | bytes 196640 | tf_op jit(solution)/shard_map/ppermute | solution.py:38
  33.5 0.0 collective-permute-done.6.refs_0_.refs_2_.refs_11_
  33.5 0.0 collective-permute-done.9.refs_1_.refs_5_.refs_14_
  33.5 1.6 %collective-permute-start.11 = (bf16[96,1536]{1,0:T(8,128)(2,1)S(1)}, bf16[96,1536]{1,0:T(8,128)(2,1)S(1)}, u32[]{:S(2)}, u32[]{:S(2)}) collective-permute-start(bf16[96,1536]{1,0:T(8,128)(2,1)S(1)} %get-tuple-element.33), channel_id=1, source_target_pairs={{0,2},{1,17},{2,0},{3,19},{4,6},{5,21},{6,4},{7,23},{8,10},{9,25},... | collective-permute-start | bytes 884744 | tf_op jit(solution)/shard_map/ppermute | solution.py:38
  35.1 0.5 %collective-permute-start.10 = (bf16[96,1536]{1,0:T(8,128)(2,1)S(1)}, bf16[96,1536]{1,0:T(8,128)(2,1)S(1)}, u32[]{:S(2)}, u32[]{:S(2)}) collective-permute-start(bf16[96,1536]{1,0:T(8,128)(2,1)S(1)} %get-tuple-element.32), channel_id=1, source_target_pairs={{0,16},{1,3},{2,18},{3,1},{4,20},{5,7},{6,22},{7,5},{8,24},{9,11},... | collective-permute-start | bytes 884744 | tf_op jit(solution)/shard_map/ppermute | solution.py:38
  35.6 0.0 copy-done.2
  35.6 1.7 %shard_map.63.earlier = f32[512,128]{1,0:T(8,128)S(1)} custom-call(s32[10]{0:T(128)S(1)} %stack.47.refs_0_.info, s32[512,1]{1,0:T(8,128)S(1)} %copy.9.refs_4_.ids.refs_1_, bf16[512,1536]{1,0:T(8,128)(2,1)S(1)} %copy-done.1, bf16[64,1536]{1,0:T(8,128)(2,1)S(1)} %bitcast.17, bf16[64,1536]{1,0:T(8,128)(2,1)S(1)} %collective-permute-done.refs_3_.beside, ...), custom_call_target="tpu_custom_call" | custom-call | tf_op jit(solution)/shard_map/pallas_call | solution.py:301
  37.3 0.0 copy-start.3
  37.4 4.8 %collective-permute-done.11.corner_two.refs_16_ = bf16[96,1536]{1,0:T(8,128)(2,1)S(1)} collective-permute-done((bf16[96,1536]{1,0:T(8,128)(2,1)S(1)}, bf16[96,1536]{1,0:T(8,128)(2,1)S(1)}, u32[]{:S(2)}, u32[]{:S(2)}) %collective-permute-start.11) | collective-permute-done | bytes 294944 | tf_op jit(solution)/shard_map/ppermute | solution.py:38
  42.2 0.0 collective-permute-done.10.corner_one.refs_15_
  42.2 0.6 %shard_map.64.refs_2_ = f32[512,128]{1,0:T(8,128)S(1)} custom-call(s32[10]{0:T(128)S(1)} %stack.47.refs_0_.info, s32[512,1]{1,0:T(8,128)S(1)} %copy.9.refs_4_.ids.refs_1_, bf16[512,1536]{1,0:T(8,128)(2,1)S(1)} %copy-done.1, f32[512,128]{1,0:T(8,128)S(1)} %shard_map.63.earlier, bf16[96,1536]{1,0:T(8,128)(2,1)S(1)} %collective-permute-done.10.corner_one.refs_15_, ...), custom_call_target="tpu_custom_call" | custom-call | tf_op jit(solution)/shard_map/pallas_call | solution.py:308
  42.8 0.1 collective-permute-start.12
  42.8 1.5 %collective-permute-done.12.refs_3_ = f32[512,128]{1,0:T(8,128)S(1)} collective-permute-done((f32[512,128]{1,0:T(8,128)S(1)}, f32[512,128]{1,0:T(8,128)S(1)}, u32[]{:S(2)}, u32[]{:S(2)}) %collective-permute-start.12) | collective-permute-done | bytes 262176 | tf_op jit(solution)/shard_map/ppermute | solution.py:20
  44.4 0.0 copy-done.3
  44.4 2.7 %shard_map.65 = bf16[512,1536]{1,0:T(8,128)(2,1)} custom-call(s32[10]{0:T(128)S(1)} %stack.47.refs_0_.info, s32[512,1]{1,0:T(8,128)S(1)} %copy.9.refs_4_.ids.refs_1_, f32[512,128]{1,0:T(8,128)S(1)} %shard_map.64.refs_2_, f32[512,128]{1,0:T(8,128)S(1)} %collective-permute-done.12.refs_3_, f32[512,512]{1,0:T(8,128)S(1)} %get-tuple-element.34.refs_4_, ...), custom_call_target="tpu_custom_call" | custom-call | tf_op jit(solution)/shard_map/pallas_call | solution.py:328
  (5 shorter events, 0.1 us)
Async XLA Ops:
  0.0 9.2 %collective-permute-start.3 = (bf16[512,1536]{1,0:T(8,128)(2,1)}, bf16[512,1536]{1,0:T(8,128)(2,1)S(1)}, u32[]{:S(2)}, u32[]{:S(2)}) collective-permute-start(bf16[512,1536]{1,0:T(8,128)(2,1)} %latent.3), channel_id=1, source_target_pairs={{0,1},{1,0},{2,3},{3,2},{4,5},{5,4},{6,7},{7,6},{8,9},{9,8},{10,11... | collective-permute-start | bytes 4718600 | tf_op jit(solution)/shard_map/ppermute | solution.py:20
  1.5 15.1 %collective-permute-start.1 = (bf16[64,1536]{1,0:T(8,128)(2,1)S(1)}, bf16[64,1536]{1,0:T(8,128)(2,1)S(1)}, u32[]{:S(2)}, u32[]{:S(2)}) collective-permute-start(bf16[64,1536]{1,0:T(8,128)(2,1)S(1)} %broadcast_select_fusion), channel_id=1, source_target_pairs={{0,4},{2,6},{4,8},{6,10},{8,12},{10,14},{12,0},{14,2},{1,5},{3,7},... | collective-permute-start | bytes 589832 | tf_op jit(solution)/shard_map/ppermute | solution.py:28
  4.1 12.6 %collective-permute-start.2 = (bf16[64,1536]{1,0:T(8,128)(2,1)S(1)}, bf16[64,1536]{1,0:T(8,128)(2,1)S(1)}, u32[]{:S(2)}, u32[]{:S(2)}) collective-permute-start(bf16[64,1536]{1,0:T(8,128)(2,1)S(1)} %broadcast_select_fusion), channel_id=1, source_target_pairs={{0,12},{2,14},{4,0},{6,2},{8,4},{10,6},{12,8},{14,10},{1,13},{3,15... | collective-permute-start | bytes 589832 | tf_op jit(solution)/shard_map/ppermute | solution.py:28
  6.2 10.5 %collective-permute-start = (bf16[64,1536]{1,0:T(8,128)(2,1)}, bf16[64,1536]{1,0:T(8,128)(2,1)S(1)}, u32[]{:S(2)}, u32[]{:S(2)}) collective-permute-start(bf16[64,1536]{1,0:T(8,128)(2,1)} %bitcast.16), channel_id=1, source_target_pairs={{0,2},{2,0},{4,6},{6,4},{8,10},{10,8},{12,14},{14,12},{1,3},{3,1},... | collective-permute-start | bytes 589832 | tf_op jit(solution)/shard_map/ppermute | solution.py:24
  7.9 9.8 %collective-permute-start.4 = (bf16[64,1536]{1,0:T(8,128)(2,1)}, bf16[64,1536]{1,0:T(8,128)(2,1)S(1)}, u32[]{:S(2)}, u32[]{:S(2)}) collective-permute-start(bf16[64,1536]{1,0:T(8,128)(2,1)} %bitcast.18), channel_id=1, source_target_pairs={{0,2},{2,0},{4,6},{6,4},{8,10},{10,8},{12,14},{14,12},{1,3},{3,1},... | collective-permute-start | bytes 589832 | tf_op jit(solution)/shard_map/ppermute | solution.py:24
  9.2 3.7 %copy-start = (bf16[3072,1536]{1,0:T(8,128)(2,1)S(1)}, bf16[3072,1536]{1,0:T(8,128)(2,1)}, u32[]{:S(2)}) copy-start(bf16[3072,1536]{1,0:T(8,128)(2,1)} %refs_3_.5) | copy-start | bytes 28311556
  12.9 1.4 %copy-start.1 = (bf16[512,1536]{1,0:T(8,128)(2,1)S(1)}, bf16[512,1536]{1,0:T(8,128)(2,1)}, u32[]{:S(2)}) copy-start(bf16[512,1536]{1,0:T(8,128)(2,1)} %latent.3) | copy-start | bytes 4718596
  16.6 8.3 %collective-permute-start.7 = (bf16[64,1536]{1,0:T(8,128)(2,1)S(1)}, bf16[64,1536]{1,0:T(8,128)(2,1)S(1)}, u32[]{:S(2)}, u32[]{:S(2)}) collective-permute-start(bf16[64,1536]{1,0:T(8,128)(2,1)S(1)} %get-tuple-element.24), channel_id=1, source_target_pairs={{0,4},{2,6},{4,8},{6,10},{8,12},{10,14},{12,0},{14,2},{1,5},{3,7},... | collective-permute-start | bytes 589832 | tf_op jit(solution)/shard_map/ppermute | solution.py:28
  17.7 12.7 %collective-permute-start.5 = (bf16[128,1536]{1,0:T(8,128)(2,1)S(1)}, bf16[128,1536]{1,0:T(8,128)(2,1)S(1)}, u32[]{:S(2)}, u32[]{:S(2)}) collective-permute-start(bf16[128,1536]{1,0:T(8,128)(2,1)S(1)} %get-tuple-element.23.refs_0_.refs_9_), channel_id=1, source_target_pairs={{0,2},{1,17},{2,0},{3,19},{4,6},{5,21},{6,4},{7,23},{8,10},{9,25},... | collective-permute-start | bytes 1179656 | tf_op jit(solution)/shard_map/ppermute | solution.py:38
  19.3 14.2 %collective-permute-start.6 = (bf16[128,1536]{1,0:T(8,128)(2,1)S(1)}, bf16[128,1536]{1,0:T(8,128)(2,1)S(1)}, u32[]{:S(2)}, u32[]{:S(2)}) collective-permute-start(bf16[128,1536]{1,0:T(8,128)(2,1)S(1)} %get-tuple-element.23.refs_0_.refs_9_), channel_id=1, source_target_pairs={{0,16},{1,3},{2,18},{3,1},{4,20},{5,7},{6,22},{7,5},{8,24},{9,11},... | collective-permute-start | bytes 1179656 | tf_op jit(solution)/shard_map/ppermute | solution.py:38
  25.0 8.5 %collective-permute-start.8 = (bf16[64,1536]{1,0:T(8,128)(2,1)S(1)}, bf16[64,1536]{1,0:T(8,128)(2,1)S(1)}, u32[]{:S(2)}, u32[]{:S(2)}) collective-permute-start(bf16[64,1536]{1,0:T(8,128)(2,1)S(1)} %get-tuple-element.27.refs_3_.refs_12_), channel_id=1, source_target_pairs={{0,2},{1,17},{2,0},{3,19},{4,6},{5,21},{6,4},{7,23},{8,10},{9,25},... | collective-permute-start | bytes 589832 | tf_op jit(solution)/shard_map/ppermute | solution.py:38
  26.6 6.9 %collective-permute-start.9 = (bf16[64,1536]{1,0:T(8,128)(2,1)S(1)}, bf16[64,1536]{1,0:T(8,128)(2,1)S(1)}, u32[]{:S(2)}, u32[]{:S(2)}) collective-permute-start(bf16[64,1536]{1,0:T(8,128)(2,1)S(1)} %get-tuple-element.27.refs_3_.refs_12_), channel_id=1, source_target_pairs={{0,16},{1,3},{2,18},{3,1},{4,20},{5,7},{6,22},{7,5},{8,24},{9,11},... | collective-permute-start | bytes 589832 | tf_op jit(solution)/shard_map/ppermute | solution.py:38
  28.1 7.6 %copy-start.2 = (bf16[1,1536,64]{1,2,0:T(8,128)(2,1)S(1)}, bf16[1,1536,64]{1,2,0:T(8,128)(2,1)}, u32[]{:S(2)}) copy-start(bf16[1,1536,64]{1,2,0:T(8,128)(2,1)} %param.8) | copy-start | bytes 589828
  33.5 8.7 %collective-permute-start.11 = (bf16[96,1536]{1,0:T(8,128)(2,1)S(1)}, bf16[96,1536]{1,0:T(8,128)(2,1)S(1)}, u32[]{:S(2)}, u32[]{:S(2)}) collective-permute-start(bf16[96,1536]{1,0:T(8,128)(2,1)S(1)} %get-tuple-element.33), channel_id=1, source_target_pairs={{0,2},{1,17},{2,0},{3,19},{4,6},{5,21},{6,4},{7,23},{8,10},{9,25},... | collective-permute-start | bytes 884744 | tf_op jit(solution)/shard_map/ppermute | solution.py:38
  35.1 7.1 %collective-permute-start.10 = (bf16[96,1536]{1,0:T(8,128)(2,1)S(1)}, bf16[96,1536]{1,0:T(8,128)(2,1)S(1)}, u32[]{:S(2)}, u32[]{:S(2)}) collective-permute-start(bf16[96,1536]{1,0:T(8,128)(2,1)S(1)} %get-tuple-element.32), channel_id=1, source_target_pairs={{0,16},{1,3},{2,18},{3,1},{4,20},{5,7},{6,22},{7,5},{8,24},{9,11},... | collective-permute-start | bytes 884744 | tf_op jit(solution)/shard_map/ppermute | solution.py:38
  37.3 7.0 %copy-start.3 = (bf16[1,64,1536]{2,1,0:T(8,128)(2,1)S(1)}, bf16[1,64,1536]{2,1,0:T(8,128)(2,1)}, u32[]{:S(2)}) copy-start(bf16[1,64,1536]{2,1,0:T(8,128)(2,1)} %param.9) | copy-start | bytes 589828
  42.8 1.6 %collective-permute-start.12 = (f32[512,128]{1,0:T(8,128)S(1)}, f32[512,128]{1,0:T(8,128)S(1)}, u32[]{:S(2)}, u32[]{:S(2)}) collective-permute-start(f32[512,128]{1,0:T(8,128)S(1)} %shard_map.64.refs_2_), channel_id=1, source_target_pairs={{0,1},{1,0},{2,3},{3,2},{4,5},{5,4},{6,7},{7,6},{8,9},{9,8},{10,11... | collective-permute-start | bytes 786440 | tf_op jit(solution)/shard_map/ppermute | solution.py:20

commit v8 on v7

--- a/solution.py
+++ b/solution.py
@@ -8,6 +8,7 @@
 
 MIB = 1024 * 1024
 CHUNK = 512
+TILE = 256
 AXES = ("replica", "shard", "tensor")
 FIRST_OWNER = 2
 SMEM = pl.BlockSpec(memory_space=pltpu.SMEM)
@@ -193,9 +194,10 @@
     width = own.shape[1]
     mine = pl.ds(pl.multiple_of(info[0] * width, width), width)
     rest = pl.ds(pl.multiple_of((1 - info[0]) * width, width), width)
-    for begin in range(0, out.shape[1], CHUNK):
-        place = slice(begin, begin + CHUNK)
-        source = slice(skip + begin, skip + begin + CHUNK)
+    step = min(CHUNK, out.shape[1])
+    for begin in range(0, out.shape[1], step):
+        place = slice(begin, min(begin + step, out.shape[1]))
+        source = slice(skip + begin, skip + place.stop)
         out[:, place] = jnp.dot(
             own[...], weight[mine, source], preferred_element_type=jnp.float32
         ) + jnp.dot(other[...], weight[rest, source], preferred_element_type=jnp.float32)
@@ -216,9 +218,9 @@
 def up_kernel(info, ids, mine, theirs, *refs, base_parts):
     *pieces, out, stack, wide, sems, staged = refs[base_parts:]
     bases = [
-        part.at[:, pl.ds(begin, CHUNK)]
+        part.at[:, pl.ds(begin, TILE)]
         for part in refs[:base_parts]
-        for begin in range(0, part.shape[1], CHUNK)
+        for begin in range(0, part.shape[1], TILE)
     ]
     rank = mine.shape[1] // 2
     if len(pieces) == 1:
@@ -260,13 +262,13 @@
     columns = adapters * rank
     index, core = lax.axis_index("shard"), lax.axis_index("tensor")
     holds_down = core == lax.axis_index("replica")
-    tiles = out_width // CHUNK
-    cuts = [tiles * number // 3 * CHUNK for number in range(4)]
+    tiles = out_width // TILE
+    cuts = [0, out_width // 6, out_width * 2 // 3, out_width]
     down = jnp.swapaxes(adapter_down_weight, 1, 2).reshape(local_adapters * rank, half_width)
     up = adapter_up_weight.reshape(local_adapters * rank, out_width)
     ids = row_adapter_index
     routed = shards == 8 and local_adapters == 1 and lax.axis_size("replica") == 2
-    routed = routed and half_width == out_width and tiles % 3 == 0
+    routed = routed and half_width == out_width and tiles % 6 == 0
     lowrank = jax.ShapeDtypeStruct((rows, 2 * rank), jnp.float32)
     if routed:
         sources = [(index - 2 * step) % shards for step in (0, 1, 3, 2)]
@@ -284,8 +286,8 @@
         parts.append(part)
         relay, token = pack([(line[1], 0, rank)], token)
         line[2] = along_line(relay, shards, 1)
-        early, token = pack([(line[1], 0, rank), (line[3], 0, rank)], token, down_beside, up_beside)
-        part, token = base(info, latent, other, shared_weight, [token], cuts[1], cuts[2])
+        early, token = pack([(line[1], 0, rank), (line[3], 0, rank)], token, down_beside)
+        part, token = base(info, latent, other, shared_weight, [token, up_beside], cuts[1], cuts[2])
         parts.append(part)
         early_first, early_second = in_plane(early, shards, True), in_plane(early, shards, False)
         late, token = pack([(line[2], 0, rank)], token)
@@ -334,7 +336,7 @@
             pltpu.VMEM((columns, out_width), latent.dtype),
             pltpu.VMEM((rows, columns), latent.dtype),
             pltpu.SemaphoreType.DMA((tiles,)),
-            pltpu.VMEM((tiles, rows, CHUNK), latent.dtype),
+            pltpu.VMEM((tiles, rows, TILE), latent.dtype),
         ],
         compiler_params=pltpu.CompilerParams(vmem_limit_bytes=(24 if routed else 56) * MIB),
     )(info, ids, mine, theirs, *parts, *up_pieces)

time: 47.3 us -> 46.4 us (0.981)
  waiting for transfers between devices: 12.2 us -> 11.1 us
    ppermute x2, waiting for transfers between devices: 0.96 us -> 0.01 us  [neighbour(): return lax.ppermute(value, 'shard', [(i, i ^ 1) for i in range(shards)])]
  transfers between devices with their start and end apart: 13 -> 13, of which waited for: 5 -> 4; matrix products, arithmetic and copies ran while one was open for 4% -> 4% of each run, Pallas kernels for 19% -> 19%
where the time goes in v8:
time: 46.4 us; the launch traced here: 46.2 us
  starting transfers between devices  15.8 us (34%)
  Pallas kernels  12.1 us (26%)
  waiting for transfers between devices  11.1 us (24%)
  local copies, waits for them, and re-layouts  6.01 us (13%)
  other arithmetic  1.04 us (2%)
    ppermute x6, starting transfers between devices, in_plane(): return lax.ppermute(value, AXES, pairs)  8.43 us
    ppermute x6, waiting for transfers between devices, in_plane(): return lax.ppermute(value, AXES, pairs)  7.75 us
    pallas_call x3, Pallas kernels, base(): pl.pallas_call(lambda *refs: base_kernel(*refs, skip=skip), out_shape=[ja...  7.01 us
    unnamed x9, local copies, waits for them, and re-layouts  5.91 us
    ppermute x3, starting transfers between devices, along_line(): lax.ppermute(value, 'shard', [(i, (i + 2 * step) % shards) for i in range...  4.78 us
    pallas_call x1, Pallas kernels, on_device(): pl.pallas_call(lambda *refs: up_kernel(*refs, base_parts=len(parts)), out...  2.73 us
    ppermute x2, starting transfers between devices, neighbour(): return lax.ppermute(value, 'shard', [(i, i ^ 1) for i in range(shards)])  2.03 us
    ppermute x3, waiting for transfers between devices, along_line(): lax.ppermute(value, 'shard', [(i, (i + 2 * step) % shards) for i in range...  1.81 us
  transfers between devices with their start and end apart: 13, of which 4 were waited for; matrix products, arithmetic and copies ran while one was open for 4% of the time, Pallas kernels for 19%

profile of v8, /device:TPU:0, one launch (start us, length us, event | category | flops | bytes accessed | tf_op | source)
XLA Modules:
  0.0 46.2 jit_solution(18293773946999555956)
XLA Ops:
  0.0 0.5 collective-permute-start.3
  0.5 1.0 %broadcast_select_fusion = bf16[64,1536]{1,0:T(8,128)(2,1)S(1)} fusion(pred[]{:T(512)S(6)} %eq.8, bf16[1,64,1536]{2,1,0:T(8,128)(2,1)} %param.9, bf16[1,1536,64]{1,2,0:T(8,128)(2,1)} %param.8), kind=kLoop, calls=%fused_computation | loop fusion | flops 98304 | bytes 589825 | tf_op jit(solution)/shard_map/jit(_where)/select_n | solution.py:280
  1.5 2.6 %collective-permute-start.1 = (bf16[64,1536]{1,0:T(8,128)(2,1)S(1)}, bf16[64,1536]{1,0:T(8,128)(2,1)S(1)}, u32[]{:S(2)}, u32[]{:S(2)}) collective-permute-start(bf16[64,1536]{1,0:T(8,128)(2,1)S(1)} %broadcast_select_fusion), channel_id=1, source_target_pairs={{0,4},{2,6},{4,8},{6,10},{8,12},{10,14},{12,0},{14,2},{1,5},{3,7},... | collective-permute-start | bytes 589832 | tf_op jit(solution)/shard_map/ppermute | solution.py:29
  4.1 2.1 %collective-permute-start.2 = (bf16[64,1536]{1,0:T(8,128)(2,1)S(1)}, bf16[64,1536]{1,0:T(8,128)(2,1)S(1)}, u32[]{:S(2)}, u32[]{:S(2)}) collective-permute-start(bf16[64,1536]{1,0:T(8,128)(2,1)S(1)} %broadcast_select_fusion), channel_id=1, source_target_pairs={{0,12},{2,14},{4,0},{6,2},{8,4},{10,6},{12,8},{14,10},{1,13},{3,15... | collective-permute-start | bytes 589832 | tf_op jit(solution)/shard_map/ppermute | solution.py:29
  6.2 1.7 %collective-permute-start = (bf16[64,1536]{1,0:T(8,128)(2,1)}, bf16[64,1536]{1,0:T(8,128)(2,1)S(1)}, u32[]{:S(2)}, u32[]{:S(2)}) collective-permute-start(bf16[64,1536]{1,0:T(8,128)(2,1)} %bitcast.16), channel_id=1, source_target_pairs={{0,2},{2,0},{4,6},{6,4},{8,10},{10,8},{12,14},{14,12},{1,3},{3,1},... | collective-permute-start | bytes 589832 | tf_op jit(solution)/shard_map/ppermute | solution.py:25
  7.9 0.3 collective-permute-start.7
  8.2 0.8 %copy.9.refs_4_.ids.refs_1_ = s32[512,1]{1,0:T(8,128)S(1)} copy(s32[512,1]{0,1:T(1,128)} %param.6) | data formatting | bytes 4096 | tf_op args[1]
  9.1 0.1 stack.47.refs_0_.info
  9.2 0.0 collective-permute-done.3.refs_2_
  9.2 0.0 copy-start
  9.2 3.7 %copy-done = bf16[3072,1536]{1,0:T(8,128)(2,1)S(1)} copy-done((bf16[3072,1536]{1,0:T(8,128)(2,1)S(1)}, bf16[3072,1536]{1,0:T(8,128)(2,1)}, u32[]{:S(2)}) %copy-start) | copy-done | bytes 9437208
  12.9 0.0 copy-start.1
  12.9 1.4 %copy-done.1 = bf16[512,1536]{1,0:T(8,128)(2,1)S(1)} copy-done((bf16[512,1536]{1,0:T(8,128)(2,1)S(1)}, bf16[512,1536]{1,0:T(8,128)(2,1)}, u32[]{:S(2)}) %copy-start.1) | copy-done | bytes 1572888
  14.3 1.5 %shard_map.55 = (f32[512,256]{1,0:T(8,128)S(1)}, f32[8,128]{1,0:T(8,128)S(1)}) custom-call(s32[10]{0:T(128)S(1)} %stack.47.refs_0_.info, bf16[512,1536]{1,0:T(8,128)(2,1)S(1)} %copy-done.1, bf16[512,1536]{1,0:T(8,128)(2,1)S(1)} %collective-permute-done.3.refs_2_, bf16[3072,1536]{1,0:T(8,128)(2,1)S(1)} %copy-done, s32[512,1]{1,0:T(8,128)S(1)} %copy.9.refs_4_.ids.refs_1_), custom_call_target="tpu_custom_call" | custom-call | flops 1000 | bytes 1000 | tf_op jit(solution)/shard_map/pallas_call | solution.py:208
  15.8 0.0 collective-permute-done.1.refs_0_
  15.8 0.1 collective-permute-start.6
  15.9 0.0 collective-permute-done.2.refs_1_
  15.9 0.0 collective-permute-done.refs_3_.beside
  16.0 1.7 %collective-permute-start.4 = (bf16[128,1536]{1,0:T(8,128)(2,1)S(1)}, bf16[128,1536]{1,0:T(8,128)(2,1)S(1)}, u32[]{:S(2)}, u32[]{:S(2)}) collective-permute-start(bf16[128,1536]{1,0:T(8,128)(2,1)S(1)} %get-tuple-element.23.refs_0_.refs_9_), channel_id=1, source_target_pairs={{0,2},{1,17},{2,0},{3,19},{4,6},{5,21},{6,4},{7,23},{8,10},{9,25},... | collective-permute-start | bytes 1179656 | tf_op jit(solution)/shard_map/ppermute | solution.py:39
  17.7 1.5 %collective-permute-start.5 = (bf16[128,1536]{1,0:T(8,128)(2,1)S(1)}, bf16[128,1536]{1,0:T(8,128)(2,1)S(1)}, u32[]{:S(2)}, u32[]{:S(2)}) collective-permute-start(bf16[128,1536]{1,0:T(8,128)(2,1)S(1)} %get-tuple-element.23.refs_0_.refs_9_), channel_id=1, source_target_pairs={{0,16},{1,3},{2,18},{3,1},{4,20},{5,7},{6,22},{7,5},{8,24},{9,11},... | collective-permute-start | bytes 1179656 | tf_op jit(solution)/shard_map/ppermute | solution.py:39
  19.2 0.0 collective-permute-done.7.refs_5_.refs_8_
  19.2 3.2 %shard_map.58 = (f32[512,768]{1,0:T(8,128)S(1)}, f32[8,128]{1,0:T(8,128)S(1)}) custom-call(s32[10]{0:T(128)S(1)} %stack.47.refs_0_.info, bf16[512,1536]{1,0:T(8,128)(2,1)S(1)} %copy-done.1, bf16[512,1536]{1,0:T(8,128)(2,1)S(1)} %collective-permute-done.3.refs_2_, bf16[3072,1536]{1,0:T(8,128)(2,1)S(1)} %copy-done, f32[8,128]{1,0:T(8,128)S(1)} %get-tuple-element.25.refs_4_, ...), custom_call_target="tpu_custom_call" | custom-call | flops 1000 | bytes 1000 | tf_op jit(solution)/shard_map/pallas_call | solution.py:208
  22.4 1.8 %collective-permute-done.6.refs_0_ = bf16[64,1536]{1,0:T(8,128)(2,1)S(1)} collective-permute-done((bf16[64,1536]{1,0:T(8,128)(2,1)S(1)}, bf16[64,1536]{1,0:T(8,128)(2,1)S(1)}, u32[]{:S(2)}, u32[]{:S(2)}) %collective-permute-start.6) | collective-permute-done | bytes 196640 | tf_op jit(solution)/shard_map/ppermute | solution.py:29
  24.2 1.6 %collective-permute-start.8 = (bf16[64,1536]{1,0:T(8,128)(2,1)S(1)}, bf16[64,1536]{1,0:T(8,128)(2,1)S(1)}, u32[]{:S(2)}, u32[]{:S(2)}) collective-permute-start(bf16[64,1536]{1,0:T(8,128)(2,1)S(1)} %get-tuple-element.27.refs_3_.refs_12_), channel_id=1, source_target_pairs={{0,2},{1,17},{2,0},{3,19},{4,6},{5,21},{6,4},{7,23},{8,10},{9,25},... | collective-permute-start | bytes 589832 | tf_op jit(solution)/shard_map/ppermute | solution.py:39
  25.8 1.5 %collective-permute-start.9 = (bf16[64,1536]{1,0:T(8,128)(2,1)S(1)}, bf16[64,1536]{1,0:T(8,128)(2,1)S(1)}, u32[]{:S(2)}, u32[]{:S(2)}) collective-permute-start(bf16[64,1536]{1,0:T(8,128)(2,1)S(1)} %get-tuple-element.27.refs_3_.refs_12_), channel_id=1, source_target_pairs={{0,16},{1,3},{2,18},{3,1},{4,20},{5,7},{6,22},{7,5},{8,24},{9,11},... | collective-permute-start | bytes 589832 | tf_op jit(solution)/shard_map/ppermute | solution.py:39
  27.3 0.0 copy-start.2
  27.3 2.3 %shard_map.60 = (f32[512,512]{1,0:T(8,128)S(1)}, f32[8,128]{1,0:T(8,128)S(1)}) custom-call(s32[10]{0:T(128)S(1)} %stack.47.refs_0_.info, bf16[512,1536]{1,0:T(8,128)(2,1)S(1)} %copy-done.1, bf16[512,1536]{1,0:T(8,128)(2,1)S(1)} %collective-permute-done.3.refs_2_, bf16[3072,1536]{1,0:T(8,128)(2,1)S(1)} %copy-done, f32[8,128]{1,0:T(8,128)S(1)} %get-tuple-element.28.refs_4_), custom_call_target="tpu_custom_call" | custom-call | flops 1000 | bytes 1000 | tf_op jit(solution)/shard_map/pallas_call | solution.py:208
  29.6 0.0 collective-permute-done.4.refs_0_.refs_1_.refs_10_
  29.6 2.5 %collective-permute-done.8.refs_1_.refs_4_.refs_13_ = bf16[64,1536]{1,0:T(8,128)(2,1)S(1)} collective-permute-done((bf16[64,1536]{1,0:T(8,128)(2,1)S(1)}, bf16[64,1536]{1,0:T(8,128)(2,1)S(1)}, u32[]{:S(2)}, u32[]{:S(2)}) %collective-permute-start.8) | collective-permute-done | bytes 196640 | tf_op jit(solution)/shard_map/ppermute | solution.py:39
  32.2 0.0 collective-permute-done.5.refs_0_.refs_2_.refs_11_
  32.2 0.0 collective-permute-done.9.refs_1_.refs_5_.refs_14_
  32.2 1.6 %collective-permute-start.11 = (bf16[96,1536]{1,0:T(8,128)(2,1)S(1)}, bf16[96,1536]{1,0:T(8,128)(2,1)S(1)}, u32[]{:S(2)}, u32[]{:S(2)}) collective-permute-start(bf16[96,1536]{1,0:T(8,128)(2,1)S(1)} %get-tuple-element.33), channel_id=1, source_target_pairs={{0,2},{1,17},{2,0},{3,19},{4,6},{5,21},{6,4},{7,23},{8,10},{9,25},... | collective-permute-start | bytes 884744 | tf_op jit(solution)/shard_map/ppermute | solution.py:39
  33.8 0.5 %collective-permute-start.10 = (bf16[96,1536]{1,0:T(8,128)(2,1)S(1)}, bf16[96,1536]{1,0:T(8,128)(2,1)S(1)}, u32[]{:S(2)}, u32[]{:S(2)}) collective-permute-start(bf16[96,1536]{1,0:T(8,128)(2,1)S(1)} %get-tuple-element.32), channel_id=1, source_target_pairs={{0,16},{1,3},{2,18},{3,1},{4,20},{5,7},{6,22},{7,5},{8,24},{9,11},... | collective-permute-start | bytes 884744 | tf_op jit(solution)/shard_map/ppermute | solution.py:39
  34.3 0.0 copy-done.2
  34.3 1.7 %shard_map.63.earlier = f32[512,128]{1,0:T(8,128)S(1)} custom-call(s32[10]{0:T(128)S(1)} %stack.47.refs_0_.info, s32[512,1]{1,0:T(8,128)S(1)} %copy.9.refs_4_.ids.refs_1_, bf16[512,1536]{1,0:T(8,128)(2,1)S(1)} %copy-done.1, bf16[64,1536]{1,0:T(8,128)(2,1)S(1)} %bitcast.17, bf16[64,1536]{1,0:T(8,128)(2,1)S(1)} %collective-permute-done.refs_3_.beside, ...), custom_call_target="tpu_custom_call" | custom-call | tf_op jit(solution)/shard_map/pallas_call | solution.py:303
  36.0 0.0 copy-start.3
  36.0 5.2 %collective-permute-done.11.corner_two.refs_16_ = bf16[96,1536]{1,0:T(8,128)(2,1)S(1)} collective-permute-done((bf16[96,1536]{1,0:T(8,128)(2,1)S(1)}, bf16[96,1536]{1,0:T(8,128)(2,1)S(1)}, u32[]{:S(2)}, u32[]{:S(2)}) %collective-permute-start.11) | collective-permute-done | bytes 294944 | tf_op jit(solution)/shard_map/ppermute | solution.py:39
  41.2 0.0 collective-permute-done.10.corner_one.refs_15_
  41.2 0.6 %shard_map.64.refs_2_ = f32[512,128]{1,0:T(8,128)S(1)} custom-call(s32[10]{0:T(128)S(1)} %stack.47.refs_0_.info, s32[512,1]{1,0:T(8,128)S(1)} %copy.9.refs_4_.ids.refs_1_, bf16[512,1536]{1,0:T(8,128)(2,1)S(1)} %copy-done.1, f32[512,128]{1,0:T(8,128)S(1)} %shard_map.63.earlier, bf16[96,1536]{1,0:T(8,128)(2,1)S(1)} %collective-permute-done.10.corner_one.refs_15_, ...), custom_call_target="tpu_custom_call" | custom-call | tf_op jit(solution)/shard_map/pallas_call | solution.py:310
  41.8 0.1 collective-permute-start.12
  41.9 1.5 %collective-permute-done.12.refs_3_ = f32[512,128]{1,0:T(8,128)S(1)} collective-permute-done((f32[512,128]{1,0:T(8,128)S(1)}, f32[512,128]{1,0:T(8,128)S(1)}, u32[]{:S(2)}, u32[]{:S(2)}) %collective-permute-start.12) | collective-permute-done | bytes 262176 | tf_op jit(solution)/shard_map/ppermute | solution.py:21
  43.4 0.0 copy-done.3
  43.4 2.7 %shard_map.65 = bf16[512,1536]{1,0:T(8,128)(2,1)} custom-call(s32[10]{0:T(128)S(1)} %stack.47.refs_0_.info, s32[512,1]{1,0:T(8,128)S(1)} %copy.9.refs_4_.ids.refs_1_, f32[512,128]{1,0:T(8,128)S(1)} %shard_map.64.refs_2_, f32[512,128]{1,0:T(8,128)S(1)} %collective-permute-done.12.refs_3_, f32[512,256]{1,0:T(8,128)S(1)} %get-tuple-element.34.refs_4_, ...), custom_call_target="tpu_custom_call" | custom-call | tf_op jit(solution)/shard_map/pallas_call | solution.py:330
  (5 shorter events, 0.1 us)
Async XLA Ops:
  0.0 9.2 %collective-permute-start.3 = (bf16[512,1536]{1,0:T(8,128)(2,1)}, bf16[512,1536]{1,0:T(8,128)(2,1)S(1)}, u32[]{:S(2)}, u32[]{:S(2)}) collective-permute-start(bf16[512,1536]{1,0:T(8,128)(2,1)} %latent.3), channel_id=1, source_target_pairs={{0,1},{1,0},{2,3},{3,2},{4,5},{5,4},{6,7},{7,6},{8,9},{9,8},{10,11... | collective-permute-start | bytes 4718600 | tf_op jit(solution)/shard_map/ppermute | solution.py:21
  1.5 14.3 %collective-permute-start.1 = (bf16[64,1536]{1,0:T(8,128)(2,1)S(1)}, bf16[64,1536]{1,0:T(8,128)(2,1)S(1)}, u32[]{:S(2)}, u32[]{:S(2)}) collective-permute-start(bf16[64,1536]{1,0:T(8,128)(2,1)S(1)} %broadcast_select_fusion), channel_id=1, source_target_pairs={{0,4},{2,6},{4,8},{6,10},{8,12},{10,14},{12,0},{14,2},{1,5},{3,7},... | collective-permute-start | bytes 589832 | tf_op jit(solution)/shard_map/ppermute | solution.py:29
  4.1 11.8 %collective-permute-start.2 = (bf16[64,1536]{1,0:T(8,128)(2,1)S(1)}, bf16[64,1536]{1,0:T(8,128)(2,1)S(1)}, u32[]{:S(2)}, u32[]{:S(2)}) collective-permute-start(bf16[64,1536]{1,0:T(8,128)(2,1)S(1)} %broadcast_select_fusion), channel_id=1, source_target_pairs={{0,12},{2,14},{4,0},{6,2},{8,4},{10,6},{12,8},{14,10},{1,13},{3,15... | collective-permute-start | bytes 589832 | tf_op jit(solution)/shard_map/ppermute | solution.py:29
  6.2 9.7 %collective-permute-start = (bf16[64,1536]{1,0:T(8,128)(2,1)}, bf16[64,1536]{1,0:T(8,128)(2,1)S(1)}, u32[]{:S(2)}, u32[]{:S(2)}) collective-permute-start(bf16[64,1536]{1,0:T(8,128)(2,1)} %bitcast.16), channel_id=1, source_target_pairs={{0,2},{2,0},{4,6},{6,4},{8,10},{10,8},{12,14},{14,12},{1,3},{3,1},... | collective-permute-start | bytes 589832 | tf_op jit(solution)/shard_map/ppermute | solution.py:25
  7.9 11.3 %collective-permute-start.7 = (bf16[64,1536]{1,0:T(8,128)(2,1)}, bf16[64,1536]{1,0:T(8,128)(2,1)S(1)}, u32[]{:S(2)}, u32[]{:S(2)}) collective-permute-start(bf16[64,1536]{1,0:T(8,128)(2,1)} %bitcast.18), channel_id=1, source_target_pairs={{0,2},{2,0},{4,6},{6,4},{8,10},{10,8},{12,14},{14,12},{1,3},{3,1},... | collective-permute-start | bytes 589832 | tf_op jit(solution)/shard_map/ppermute | solution.py:25
  9.2 3.7 %copy-start = (bf16[3072,1536]{1,0:T(8,128)(2,1)S(1)}, bf16[3072,1536]{1,0:T(8,128)(2,1)}, u32[]{:S(2)}) copy-start(bf16[3072,1536]{1,0:T(8,128)(2,1)} %refs_3_.5) | copy-start | bytes 28311556
  12.9 1.4 %copy-start.1 = (bf16[512,1536]{1,0:T(8,128)(2,1)S(1)}, bf16[512,1536]{1,0:T(8,128)(2,1)}, u32[]{:S(2)}) copy-start(bf16[512,1536]{1,0:T(8,128)(2,1)} %latent.3) | copy-start | bytes 4718596
  15.8 8.3 %collective-permute-start.6 = (bf16[64,1536]{1,0:T(8,128)(2,1)S(1)}, bf16[64,1536]{1,0:T(8,128)(2,1)S(1)}, u32[]{:S(2)}, u32[]{:S(2)}) collective-permute-start(bf16[64,1536]{1,0:T(8,128)(2,1)S(1)} %get-tuple-element.24), channel_id=1, source_target_pairs={{0,4},{2,6},{4,8},{6,10},{8,12},{10,14},{12,0},{14,2},{1,5},{3,7},... | collective-permute-start | bytes 589832 | tf_op jit(solution)/shard_map/ppermute | solution.py:29
  16.0 13.6 %collective-permute-start.4 = (bf16[128,1536]{1,0:T(8,128)(2,1)S(1)}, bf16[128,1536]{1,0:T(8,128)(2,1)S(1)}, u32[]{:S(2)}, u32[]{:S(2)}) collective-permute-start(bf16[128,1536]{1,0:T(8,128)(2,1)S(1)} %get-tuple-element.23.refs_0_.refs_9_), channel_id=1, source_target_pairs={{0,2},{1,17},{2,0},{3,19},{4,6},{5,21},{6,4},{7,23},{8,10},{9,25},... | collective-permute-start | bytes 1179656 | tf_op jit(solution)/shard_map/ppermute | solution.py:39
  17.7 14.5 %collective-permute-start.5 = (bf16[128,1536]{1,0:T(8,128)(2,1)S(1)}, bf16[128,1536]{1,0:T(8,128)(2,1)S(1)}, u32[]{:S(2)}, u32[]{:S(2)}) collective-permute-start(bf16[128,1536]{1,0:T(8,128)(2,1)S(1)} %get-tuple-element.23.refs_0_.refs_9_), channel_id=1, source_target_pairs={{0,16},{1,3},{2,18},{3,1},{4,20},{5,7},{6,22},{7,5},{8,24},{9,11},... | collective-permute-start | bytes 1179656 | tf_op jit(solution)/shard_map/ppermute | solution.py:39
  24.2 8.0 %collective-permute-start.8 = (bf16[64,1536]{1,0:T(8,128)(2,1)S(1)}, bf16[64,1536]{1,0:T(8,128)(2,1)S(1)}, u32[]{:S(2)}, u32[]{:S(2)}) collective-permute-start(bf16[64,1536]{1,0:T(8,128)(2,1)S(1)} %get-tuple-element.27.refs_3_.refs_12_), channel_id=1, source_target_pairs={{0,2},{1,17},{2,0},{3,19},{4,6},{5,21},{6,4},{7,23},{8,10},{9,25},... | collective-permute-start | bytes 589832 | tf_op jit(solution)/shard_map/ppermute | solution.py:39
  25.8 6.4 %collective-permute-start.9 = (bf16[64,1536]{1,0:T(8,128)(2,1)S(1)}, bf16[64,1536]{1,0:T(8,128)(2,1)S(1)}, u32[]{:S(2)}, u32[]{:S(2)}) collective-permute-start(bf16[64,1536]{1,0:T(8,128)(2,1)S(1)} %get-tuple-element.27.refs_3_.refs_12_), channel_id=1, source_target_pairs={{0,16},{1,3},{2,18},{3,1},{4,20},{5,7},{6,22},{7,5},{8,24},{9,11},... | collective-permute-start | bytes 589832 | tf_op jit(solution)/shard_map/ppermute | solution.py:39
  27.3 7.1 %copy-start.2 = (bf16[1,1536,64]{1,2,0:T(8,128)(2,1)S(1)}, bf16[1,1536,64]{1,2,0:T(8,128)(2,1)}, u32[]{:S(2)}) copy-start(bf16[1,1536,64]{1,2,0:T(8,128)(2,1)} %param.8) | copy-start | bytes 589828
  32.2 9.0 %collective-permute-start.11 = (bf16[96,1536]{1,0:T(8,128)(2,1)S(1)}, bf16[96,1536]{1,0:T(8,128)(2,1)S(1)}, u32[]{:S(2)}, u32[]{:S(2)}) collective-permute-start(bf16[96,1536]{1,0:T(8,128)(2,1)S(1)} %get-tuple-element.33), channel_id=1, source_target_pairs={{0,2},{1,17},{2,0},{3,19},{4,6},{5,21},{6,4},{7,23},{8,10},{9,25},... | collective-permute-start | bytes 884744 | tf_op jit(solution)/shard_map/ppermute | solution.py:39
  33.8 7.4 %collective-permute-start.10 = (bf16[96,1536]{1,0:T(8,128)(2,1)S(1)}, bf16[96,1536]{1,0:T(8,128)(2,1)S(1)}, u32[]{:S(2)}, u32[]{:S(2)}) collective-permute-start(bf16[96,1536]{1,0:T(8,128)(2,1)S(1)} %get-tuple-element.32), channel_id=1, source_target_pairs={{0,16},{1,3},{2,18},{3,1},{4,20},{5,7},{6,22},{7,5},{8,24},{9,11},... | collective-permute-start | bytes 884744 | tf_op jit(solution)/shard_map/ppermute | solution.py:39
  36.0 7.4 %copy-start.3 = (bf16[1,64,1536]{2,1,0:T(8,128)(2,1)S(1)}, bf16[1,64,1536]{2,1,0:T(8,128)(2,1)}, u32[]{:S(2)}) copy-start(bf16[1,64,1536]{2,1,0:T(8,128)(2,1)} %param.9) | copy-start | bytes 589828
  41.8 1.6 %collective-permute-start.12 = (f32[512,128]{1,0:T(8,128)S(1)}, f32[512,128]{1,0:T(8,128)S(1)}, u32[]{:S(2)}, u32[]{:S(2)}) collective-permute-start(f32[512,128]{1,0:T(8,128)S(1)} %shard_map.64.refs_2_), channel_id=1, source_target_pairs={{0,1},{1,0},{2,3},{3,2},{4,5},{5,4},{6,7},{7,6},{8,9},{9,8},{10,11... | collective-permute-start | bytes 786440 | tf_op jit(solution)/shard_map/ppermute | solution.py:21

commit v9 on v8

--- a/solution.py
+++ b/solution.py
@@ -90,7 +90,7 @@
 
 
 def fill_here(info, holds, received, stack, top, rank):
-    early, early_first, early_second, late, late_first, late_second, _, _ = received
+    early, early_first, early_second, late, late_first, late_second, *_ = received
 
     def blocks(pair, single):
         return [[(pair, 0, rank)], [(pair, rank, rank)], [(single, 0, rank)]]
@@ -103,8 +103,7 @@
 
 
 def fill_beside(info, holds, received, stack, top, rank, direct=True, corner=True):
-    _, early_first, early_second, _, late_first, late_second, corner_one, corner_two = received
-    half = rank // 2
+    _, early_first, early_second, _, late_first, late_second, *corners = received
     swapped = ((early_first, late_first), (early_second, late_second))
     if direct:
         for core in range(2):
@@ -116,12 +115,8 @@
 
             pl.when(holds & (info[0] == core))(straight)
     if corner:
-
-        def turned():
-            last = [(corner_one, rank, half), (corner_two, rank, half)]
-            put([[(corner_one, 0, rank)], [(corner_two, 0, rank)], last], stack, top, rank)
-
-        pl.when(jnp.logical_not(holds))(turned)
+        blocks = [[(ref, 0, rank)] for ref in corners]
+        pl.when(jnp.logical_not(holds))(lambda: put(blocks, stack, top, rank))
 
 
 def clear(stack, top, rank, count):
@@ -161,15 +156,15 @@
     holds = info[1] == 1
     stack[0:rank, :] = own[...]
     stack[rank : 2 * rank, :] = beside[...]
-    fill_here(info, holds, (*received, None, None), stack, 2 * rank, rank)
-    fill_beside(info, holds, (*received, None, None), stack, 3 * rank, rank, corner=False)
+    fill_here(info, holds, received, stack, 2 * rank, rank)
+    fill_beside(info, holds, received, stack, 3 * rank, rank, corner=False)
     pl.when(jnp.logical_not(holds))(lambda: clear(stack, 3 * rank, rank, 3))
     out[...] = masked_products(info, ids, latent, stack, range(stack.shape[0] // rank), rank)
 
 
-def down_last_kernel(info, ids, latent, earlier, corner_one, corner_two, out, stack):
+def down_last_kernel(info, ids, latent, earlier, *refs):
+    *corners, out, stack = refs
     rank = out.shape[1] // 2
-    half = rank // 2
     holds = info[1] == 1
 
     @pl.when(holds)
@@ -178,10 +173,8 @@
 
     @pl.when(jnp.logical_not(holds))
     def _():
-        stack[0:rank, :] = corner_one[0:rank, :]
-        stack[rank : 2 * rank, :] = corner_two[0:rank, :]
-        stack[2 * rank : 2 * rank + half, :] = corner_one[rank : rank + half, :]
-        stack[2 * rank + half : 3 * rank, :] = corner_two[rank : rank + half, :]
+        for number, corner in enumerate(corners):
+            stack[number * rank : (number + 1) * rank, :] = corner[...]
         stack[3 * rank : 4 * rank, :] = jnp.zeros((rank, stack.shape[1]), stack.dtype)
         pair = masked_products(info, ids, latent, stack, (3, 5, 7, None), rank)
         fold = pair[:, :rank] + pair[:, rank:]
@@ -284,21 +277,23 @@
         parts = []
         part, token = base(info, latent, other, shared_weight, [ids], cuts[0], cuts[1])
         parts.append(part)
-        relay, token = pack([(line[1], 0, rank)], token)
-        line[2] = along_line(relay, shards, 1)
-        early, token = pack([(line[1], 0, rank), (line[3], 0, rank)], token, down_beside)
-        part, token = base(info, latent, other, shared_weight, [token, up_beside], cuts[1], cuts[2])
+        line[2] = along_line(line[1], shards, 1)
+        early, token = pack([(line[1], 0, rank), (line[3], 0, rank)], token, down_beside, up_beside)
+        part, token = base(info, latent, other, shared_weight, [token], cuts[1], cuts[2])
         parts.append(part)
         early_first, early_second = in_plane(early, shards, True), in_plane(early, shards, False)
         late, token = pack([(line[2], 0, rank)], token)
         part, token = base(info, latent, other, shared_weight, [token], cuts[2], cuts[3])
         parts.append(part)
-        late_first, late_second = in_plane(late, shards, True), in_plane(late, shards, False)
-        half = rank // 2
-        turn_one, token = pack([(early_first, 0, rank), (late_first, 0, half)], token)
-        turn_two, token = pack([(early_second, rank, rank), (late_second, half, half)], token)
-        corner_one = in_plane(turn_one, shards, False)
-        corner_two = in_plane(turn_two, shards, True)
+        late_second = in_plane(late, shards, False)
+        turn, token = pack([(early_first, 0, rank)], token)
+        corner_one = in_plane(turn, shards, False)
+        late_first = along_line(turn, shards, 1)
+        turn, token = pack([(early_second, rank, rank)], token)
+        corner_two = in_plane(turn, shards, True)
+        turn, token = pack([(late_second, 0, rank)], token)
+        corner_three = in_plane(turn, shards, True)
+        corners = [corner_one, corner_two, corner_three]
         received = [early, early_first, early_second, late, late_first, late_second]
         mine = call(
             down_first_kernel,
@@ -310,11 +305,11 @@
         mine = call(
             down_last_kernel,
             lowrank,
-            [SMEM] + [VMEM] * 5,
+            [SMEM] + [VMEM] * 6,
             16,
             [pltpu.VMEM((4 * rank, half_width), latent.dtype)],
-        )(info, ids, latent, mine, corner_one, corner_two)
-        up_pieces = [up, up_beside, *received, corner_one, corner_two]
+        )(info, ids, latent, mine, *corners)
+        up_pieces = [up, up_beside, *received, *corners]
     else:
         other = swap(latent, "tensor")
         parts, token = [], ids

time: 46.4 us -> 47.1 us (1.015)
  waiting for transfers between devices: 11.1 us -> 14.3 us
  starting transfers between devices: 15.8 us -> 13.3 us
    ppermute x3 -> x4, waiting for transfers between devices: 1.81 us -> 9.18 us  [along_line(): lax.ppermute(value, 'shard', [(i, (i + 2 * step) % shards) for i in range...]
    ppermute x6, waiting for transfers between devices: 7.75 us -> 2.05 us  [in_plane(): return lax.ppermute(value, AXES, pairs)]
    ppermute x6, starting transfers between devices: 8.43 us -> 5.99 us  [in_plane(): return lax.ppermute(value, AXES, pairs)]
    ppermute x2, waiting for transfers between devices: 0.01 us -> 1.51 us  [neighbour(): return lax.ppermute(value, 'shard', [(i, i ^ 1) for i in range(shards)])]
    ppermute x3 -> x4, starting transfers between devices: 4.78 us -> 4.78 us  [along_line(): lax.ppermute(value, 'shard', [(i, (i + 2 * step) % shards) for i in range...]
  transfers between devices with their start and end apart: 13 -> 14, of which waited for: 4 -> 6; matrix products, arithmetic and copies ran while one was open for 4% -> 4% of each run, Pallas kernels for 19% -> 19%
where the time goes in v9:
time: 47.1 us; the launch traced here: 46.9 us
  waiting for transfers between devices  14.3 us (30%)
  starting transfers between devices  13.3 us (28%)
  Pallas kernels  12.1 us (26%)
  local copies, waits for them, and re-layouts  6.01 us (13%)
  other arithmetic  1.04 us (2%)
    ppermute x4, waiting for transfers between devices, along_line(): lax.ppermute(value, 'shard', [(i, (i + 2 * step) % shards) for i in range...  9.18 us
    pallas_call x3, Pallas kernels, base(): pl.pallas_call(lambda *refs: base_kernel(*refs, skip=skip), out_shape=[ja...  7.01 us
    ppermute x6, starting transfers between devices, in_plane(): return lax.ppermute(value, AXES, pairs)  5.99 us
    unnamed x9, local copies, waits for them, and re-layouts  5.91 us
    ppermute x4, starting transfers between devices, along_line(): lax.ppermute(value, 'shard', [(i, (i + 2 * step) % shards) for i in range...  4.78 us
    pallas_call x1, Pallas kernels, on_device(): pl.pallas_call(lambda *refs: up_kernel(*refs, base_parts=len(parts)), out...  2.73 us
    ppermute x6, waiting for transfers between devices, in_plane(): return lax.ppermute(value, AXES, pairs)  2.05 us
    ppermute x2, starting transfers between devices, neighbour(): return lax.ppermute(value, 'shard', [(i, i ^ 1) for i in range(shards)])  2.03 us
  transfers between devices with their start and end apart: 14, of which 6 were waited for; matrix products, arithmetic and copies ran while one was open for 4% of the time, Pallas kernels for 19%

profile of v9, /device:TPU:0, one launch (start us, length us, event | category | flops | bytes accessed | tf_op | source)
XLA Modules:
  0.0 46.9 jit_solution(10175324294069498297)
XLA Ops:
  0.0 0.5 collective-permute-start.3
  0.5 1.0 %broadcast_select_fusion = bf16[64,1536]{1,0:T(8,128)(2,1)S(1)} fusion(pred[]{:T(512)S(6)} %eq.8, bf16[1,64,1536]{2,1,0:T(8,128)(2,1)} %param.9, bf16[1,1536,64]{1,2,0:T(8,128)(2,1)} %param.8), kind=kLoop, calls=%fused_computation | loop fusion | flops 98304 | bytes 589825 | tf_op jit(solution)/shard_map/jit(_where)/select_n | solution.py:273
  1.5 4.7 %collective-permute-start.2 = (bf16[64,1536]{1,0:T(8,128)(2,1)S(1)}, bf16[64,1536]{1,0:T(8,128)(2,1)S(1)}, u32[]{:S(2)}, u32[]{:S(2)}) collective-permute-start(bf16[64,1536]{1,0:T(8,128)(2,1)S(1)} %broadcast_select_fusion), channel_id=1, source_target_pairs={{0,12},{2,14},{4,0},{6,2},{8,4},{10,6},{12,8},{14,10},{1,13},{3,15... | collective-permute-start | bytes 589832 | tf_op jit(solution)/shard_map/ppermute | solution.py:29
  6.2 0.0 collective-permute-start.1
  6.2 1.5 %collective-permute-start = (bf16[64,1536]{1,0:T(8,128)(2,1)}, bf16[64,1536]{1,0:T(8,128)(2,1)S(1)}, u32[]{:S(2)}, u32[]{:S(2)}) collective-permute-start(bf16[64,1536]{1,0:T(8,128)(2,1)} %bitcast.16), channel_id=1, source_target_pairs={{0,2},{2,0},{4,6},{6,4},{8,10},{10,8},{12,14},{14,12},{1,3},{3,1},... | collective-permute-start | bytes 589832 | tf_op jit(solution)/shard_map/ppermute | solution.py:25
  7.7 0.5 %collective-permute-start.4 = (bf16[64,1536]{1,0:T(8,128)(2,1)}, bf16[64,1536]{1,0:T(8,128)(2,1)S(1)}, u32[]{:S(2)}, u32[]{:S(2)}) collective-permute-start(bf16[64,1536]{1,0:T(8,128)(2,1)} %bitcast.18), channel_id=1, source_target_pairs={{0,2},{2,0},{4,6},{6,4},{8,10},{10,8},{12,14},{14,12},{1,3},{3,1},... | collective-permute-start | bytes 589832 | tf_op jit(solution)/shard_map/ppermute | solution.py:25
  8.2 0.8 %copy.9.refs_4_.ids.refs_1_ = s32[512,1]{1,0:T(8,128)S(1)} copy(s32[512,1]{0,1:T(1,128)} %param.6) | data formatting | bytes 4096 | tf_op args[1]
  9.0 0.1 stack.47.refs_0_.info
  9.1 0.0 collective-permute-done.3.refs_2_
  9.1 0.0 copy-start
  9.1 3.7 %copy-done = bf16[3072,1536]{1,0:T(8,128)(2,1)S(1)} copy-done((bf16[3072,1536]{1,0:T(8,128)(2,1)S(1)}, bf16[3072,1536]{1,0:T(8,128)(2,1)}, u32[]{:S(2)}) %copy-start) | copy-done | bytes 9437208
  12.8 0.0 copy-start.1
  12.8 1.4 %copy-done.1 = bf16[512,1536]{1,0:T(8,128)(2,1)S(1)} copy-done((bf16[512,1536]{1,0:T(8,128)(2,1)S(1)}, bf16[512,1536]{1,0:T(8,128)(2,1)}, u32[]{:S(2)}) %copy-start.1) | copy-done | bytes 1572888
  14.2 1.5 %shard_map.55 = (f32[512,256]{1,0:T(8,128)S(1)}, f32[8,128]{1,0:T(8,128)S(1)}) custom-call(s32[10]{0:T(128)S(1)} %stack.47.refs_0_.info, bf16[512,1536]{1,0:T(8,128)(2,1)S(1)} %copy-done.1, bf16[512,1536]{1,0:T(8,128)(2,1)S(1)} %collective-permute-done.3.refs_2_, bf16[3072,1536]{1,0:T(8,128)(2,1)S(1)} %copy-done, s32[512,1]{1,0:T(8,128)S(1)} %copy.9.refs_4_.ids.refs_1_), custom_call_target="tpu_custom_call" | custom-call | flops 1000 | bytes 1000 | tf_op jit(solution)/shard_map/pallas_call | solution.py:201
  15.7 0.0 collective-permute-done.2.refs_1_
  15.7 0.4 collective-permute-done.1.refs_0_
  16.1 0.0 collective-permute-done.refs_3_.beside
  16.1 1.5 %collective-permute-done.4.refs_4_.refs_8_ = bf16[64,1536]{1,0:T(8,128)(2,1)S(1)} collective-permute-done((bf16[64,1536]{1,0:T(8,128)(2,1)}, bf16[64,1536]{1,0:T(8,128)(2,1)S(1)}, u32[]{:S(2)}, u32[]{:S(2)}) %collective-permute-start.4) | collective-permute-done | bytes 196640 | tf_op jit(solution)/shard_map/ppermute | solution.py:25
  17.6 1.6 %collective-permute-start.5 = (bf16[128,1536]{1,0:T(8,128)(2,1)S(1)}, bf16[128,1536]{1,0:T(8,128)(2,1)S(1)}, u32[]{:S(2)}, u32[]{:S(2)}) collective-permute-start(bf16[128,1536]{1,0:T(8,128)(2,1)S(1)} %get-tuple-element.22.refs_0_.refs_9_), channel_id=1, source_target_pairs={{0,2},{1,17},{2,0},{3,19},{4,6},{5,21},{6,4},{7,23},{8,10},{9,25},... | collective-permute-start | bytes 1179656 | tf_op jit(solution)/shard_map/ppermute | solution.py:39
  19.2 1.5 %collective-permute-start.6 = (bf16[128,1536]{1,0:T(8,128)(2,1)S(1)}, bf16[128,1536]{1,0:T(8,128)(2,1)S(1)}, u32[]{:S(2)}, u32[]{:S(2)}) collective-permute-start(bf16[128,1536]{1,0:T(8,128)(2,1)S(1)} %get-tuple-element.22.refs_0_.refs_9_), channel_id=1, source_target_pairs={{0,16},{1,3},{2,18},{3,1},{4,20},{5,7},{6,22},{7,5},{8,24},{9,11},... | collective-permute-start | bytes 1179656 | tf_op jit(solution)/shard_map/ppermute | solution.py:39
  20.7 0.1 collective-permute-start.7
  20.8 3.2 %shard_map.57 = (f32[512,768]{1,0:T(8,128)S(1)}, f32[8,128]{1,0:T(8,128)S(1)}) custom-call(s32[10]{0:T(128)S(1)} %stack.47.refs_0_.info, bf16[512,1536]{1,0:T(8,128)(2,1)S(1)} %copy-done.1, bf16[512,1536]{1,0:T(8,128)(2,1)S(1)} %collective-permute-done.3.refs_2_, bf16[3072,1536]{1,0:T(8,128)(2,1)S(1)} %copy-done, f32[8,128]{1,0:T(8,128)S(1)} %get-tuple-element.23.refs_4_), custom_call_target="tpu_custom_call" | custom-call | flops 1000 | bytes 1000 | tf_op jit(solution)/shard_map/pallas_call | solution.py:201
  24.0 4.2 %collective-permute-done.7.refs_0_ = bf16[64,1536]{1,0:T(8,128)(2,1)S(1)} collective-permute-done((bf16[64,1536]{1,0:T(8,128)(2,1)S(1)}, bf16[64,1536]{1,0:T(8,128)(2,1)S(1)}, u32[]{:S(2)}, u32[]{:S(2)}) %collective-permute-start.7) | collective-permute-done | bytes 196640 | tf_op jit(solution)/shard_map/ppermute | solution.py:29
  28.2 0.6 %collective-permute-start.9 = (bf16[64,1536]{1,0:T(8,128)(2,1)S(1)}, bf16[64,1536]{1,0:T(8,128)(2,1)S(1)}, u32[]{:S(2)}, u32[]{:S(2)}) collective-permute-start(bf16[64,1536]{1,0:T(8,128)(2,1)S(1)} %get-tuple-element.25.refs_3_.refs_12_), channel_id=1, source_target_pairs={{0,16},{1,3},{2,18},{3,1},{4,20},{5,7},{6,22},{7,5},{8,24},{9,11},... | collective-permute-start | bytes 589832 | tf_op jit(solution)/shard_map/ppermute | solution.py:39
  28.8 0.0 copy-start.2
  28.8 2.3 %shard_map.59 = (f32[512,512]{1,0:T(8,128)S(1)}, f32[8,128]{1,0:T(8,128)S(1)}) custom-call(s32[10]{0:T(128)S(1)} %stack.47.refs_0_.info, bf16[512,1536]{1,0:T(8,128)(2,1)S(1)} %copy-done.1, bf16[512,1536]{1,0:T(8,128)(2,1)S(1)} %collective-permute-done.3.refs_2_, bf16[3072,1536]{1,0:T(8,128)(2,1)S(1)} %copy-done, f32[8,128]{1,0:T(8,128)S(1)} %get-tuple-element.26.refs_4_), custom_call_target="tpu_custom_call" | custom-call | flops 1000 | bytes 1000 | tf_op jit(solution)/shard_map/pallas_call | solution.py:201
  31.1 0.0 collective-permute-done.5.refs_0_.refs_1_.refs_10_
  31.2 1.6 %collective-permute-start.10 = (bf16[64,1536]{1,0:T(8,128)(2,1)S(1)}, bf16[64,1536]{1,0:T(8,128)(2,1)S(1)}, u32[]{:S(2)}, u32[]{:S(2)}) collective-permute-start(bf16[64,1536]{1,0:T(8,128)(2,1)S(1)} %get-tuple-element.28), channel_id=1, source_target_pairs={{0,16},{1,3},{2,18},{3,1},{4,20},{5,7},{6,22},{7,5},{8,24},{9,11},... | collective-permute-start | bytes 589832 | tf_op jit(solution)/shard_map/ppermute | solution.py:39
  32.7 0.0 collective-permute-start.8
  32.7 0.0 collective-permute-done.6.refs_0_.refs_2_.refs_11_
  32.8 0.6 %collective-permute-start.11 = (bf16[64,1536]{1,0:T(8,128)(2,1)S(1)}, bf16[64,1536]{1,0:T(8,128)(2,1)S(1)}, u32[]{:S(2)}, u32[]{:S(2)}) collective-permute-start(bf16[64,1536]{1,0:T(8,128)(2,1)S(1)} %get-tuple-element.32), channel_id=1, source_target_pairs={{0,2},{1,17},{2,0},{3,19},{4,6},{5,21},{6,4},{7,23},{8,10},{9,25},... | collective-permute-start | bytes 589832 | tf_op jit(solution)/shard_map/ppermute | solution.py:39
  33.3 2.0 %collective-permute-done.9.refs_0_.refs_5_.refs_14_ = bf16[64,1536]{1,0:T(8,128)(2,1)S(1)} collective-permute-done((bf16[64,1536]{1,0:T(8,128)(2,1)S(1)}, bf16[64,1536]{1,0:T(8,128)(2,1)S(1)}, u32[]{:S(2)}, u32[]{:S(2)}) %collective-permute-start.9) | collective-permute-done | bytes 196640 | tf_op jit(solution)/shard_map/ppermute | solution.py:39
  35.4 0.2 collective-permute-start.12
  35.6 4.6 %collective-permute-done.8.refs_4_.refs_13_ = bf16[64,1536]{1,0:T(8,128)(2,1)S(1)} collective-permute-done((bf16[64,1536]{1,0:T(8,128)(2,1)S(1)}, bf16[64,1536]{1,0:T(8,128)(2,1)S(1)}, u32[]{:S(2)}, u32[]{:S(2)}) %collective-permute-start.8) | collective-permute-done | bytes 196640 | tf_op jit(solution)/shard_map/ppermute | solution.py:29
  40.2 0.0 copy-done.2
  40.2 1.7 %shard_map.63.earlier = f32[512,128]{1,0:T(8,128)S(1)} custom-call(s32[10]{0:T(128)S(1)} %stack.47.refs_0_.info, s32[512,1]{1,0:T(8,128)S(1)} %copy.9.refs_4_.ids.refs_1_, bf16[512,1536]{1,0:T(8,128)(2,1)S(1)} %copy-done.1, bf16[64,1536]{1,0:T(8,128)(2,1)S(1)} %bitcast.17, bf16[64,1536]{1,0:T(8,128)(2,1)S(1)} %collective-permute-done.refs_3_.beside, ...), custom_call_target="tpu_custom_call" | custom-call | tf_op jit(solution)/shard_map/pallas_call | solution.py:298
  41.9 0.0 copy-start.3
  41.9 0.0 collective-permute-done.11.refs_1_.refs_16_
  41.9 0.0 collective-permute-done.10.refs_0_.refs_15_
  41.9 0.0 collective-permute-done.12.refs_2_.refs_17_
  41.9 0.6 %shard_map.64.refs_2_ = f32[512,128]{1,0:T(8,128)S(1)} custom-call(s32[10]{0:T(128)S(1)} %stack.47.refs_0_.info, s32[512,1]{1,0:T(8,128)S(1)} %copy.9.refs_4_.ids.refs_1_, bf16[512,1536]{1,0:T(8,128)(2,1)S(1)} %copy-done.1, f32[512,128]{1,0:T(8,128)S(1)} %shard_map.63.earlier, bf16[64,1536]{1,0:T(8,128)(2,1)S(1)} %collective-permute-done.10.refs_0_.refs_15_, ...), custom_call_target="tpu_custom_call" | custom-call | tf_op jit(solution)/shard_map/pallas_call | solution.py:305
  42.5 0.1 collective-permute-start.13
  42.6 1.5 %collective-permute-done.13.refs_3_ = f32[512,128]{1,0:T(8,128)S(1)} collective-permute-done((f32[512,128]{1,0:T(8,128)S(1)}, f32[512,128]{1,0:T(8,128)S(1)}, u32[]{:S(2)}, u32[]{:S(2)}) %collective-permute-start.13) | collective-permute-done | bytes 262176 | tf_op jit(solution)/shard_map/ppermute | solution.py:21
  44.1 0.0 copy-done.3
  44.1 2.7 %shard_map.65 = bf16[512,1536]{1,0:T(8,128)(2,1)} custom-call(s32[10]{0:T(128)S(1)} %stack.47.refs_0_.info, s32[512,1]{1,0:T(8,128)S(1)} %copy.9.refs_4_.ids.refs_1_, f32[512,128]{1,0:T(8,128)S(1)} %shard_map.64.refs_2_, f32[512,128]{1,0:T(8,128)S(1)} %collective-permute-done.13.refs_3_, f32[512,256]{1,0:T(8,128)S(1)} %get-tuple-element.34.refs_4_, ...), custom_call_target="tpu_custom_call" | custom-call | tf_op jit(solution)/shard_map/pallas_call | solution.py:325
  (5 shorter events, 0.1 us)
Async XLA Ops:
  0.0 9.1 %collective-permute-start.3 = (bf16[512,1536]{1,0:T(8,128)(2,1)}, bf16[512,1536]{1,0:T(8,128)(2,1)S(1)}, u32[]{:S(2)}, u32[]{:S(2)}) collective-permute-start(bf16[512,1536]{1,0:T(8,128)(2,1)} %latent.3), channel_id=1, source_target_pairs={{0,1},{1,0},{2,3},{3,2},{4,5},{5,4},{6,7},{7,6},{8,9},{9,8},{10,11... | collective-permute-start | bytes 4718600 | tf_op jit(solution)/shard_map/ppermute | solution.py:21
  1.5 14.2 %collective-permute-start.2 = (bf16[64,1536]{1,0:T(8,128)(2,1)S(1)}, bf16[64,1536]{1,0:T(8,128)(2,1)S(1)}, u32[]{:S(2)}, u32[]{:S(2)}) collective-permute-start(bf16[64,1536]{1,0:T(8,128)(2,1)S(1)} %broadcast_select_fusion), channel_id=1, source_target_pairs={{0,12},{2,14},{4,0},{6,2},{8,4},{10,6},{12,8},{14,10},{1,13},{3,15... | collective-permute-start | bytes 589832 | tf_op jit(solution)/shard_map/ppermute | solution.py:29
  6.2 9.9 %collective-permute-start.1 = (bf16[64,1536]{1,0:T(8,128)(2,1)S(1)}, bf16[64,1536]{1,0:T(8,128)(2,1)S(1)}, u32[]{:S(2)}, u32[]{:S(2)}) collective-permute-start(bf16[64,1536]{1,0:T(8,128)(2,1)S(1)} %broadcast_select_fusion), channel_id=1, source_target_pairs={{0,4},{2,6},{4,8},{6,10},{8,12},{10,14},{12,0},{14,2},{1,5},{3,7},... | collective-permute-start | bytes 589832 | tf_op jit(solution)/shard_map/ppermute | solution.py:29
  6.2 9.9 %collective-permute-start = (bf16[64,1536]{1,0:T(8,128)(2,1)}, bf16[64,1536]{1,0:T(8,128)(2,1)S(1)}, u32[]{:S(2)}, u32[]{:S(2)}) collective-permute-start(bf16[64,1536]{1,0:T(8,128)(2,1)} %bitcast.16), channel_id=1, source_target_pairs={{0,2},{2,0},{4,6},{6,4},{8,10},{10,8},{12,14},{14,12},{1,3},{3,1},... | collective-permute-start | bytes 589832 | tf_op jit(solution)/shard_map/ppermute | solution.py:25
  7.7 9.9 %collective-permute-start.4 = (bf16[64,1536]{1,0:T(8,128)(2,1)}, bf16[64,1536]{1,0:T(8,128)(2,1)S(1)}, u32[]{:S(2)}, u32[]{:S(2)}) collective-permute-start(bf16[64,1536]{1,0:T(8,128)(2,1)} %bitcast.18), channel_id=1, source_target_pairs={{0,2},{2,0},{4,6},{6,4},{8,10},{10,8},{12,14},{14,12},{1,3},{3,1},... | collective-permute-start | bytes 589832 | tf_op jit(solution)/shard_map/ppermute | solution.py:25
  9.1 3.7 %copy-start = (bf16[3072,1536]{1,0:T(8,128)(2,1)S(1)}, bf16[3072,1536]{1,0:T(8,128)(2,1)}, u32[]{:S(2)}) copy-start(bf16[3072,1536]{1,0:T(8,128)(2,1)} %refs_3_.5) | copy-start | bytes 28311556
  12.8 1.4 %copy-start.1 = (bf16[512,1536]{1,0:T(8,128)(2,1)S(1)}, bf16[512,1536]{1,0:T(8,128)(2,1)}, u32[]{:S(2)}) copy-start(bf16[512,1536]{1,0:T(8,128)(2,1)} %latent.3) | copy-start | bytes 4718596
  17.6 13.5 %collective-permute-start.5 = (bf16[128,1536]{1,0:T(8,128)(2,1)S(1)}, bf16[128,1536]{1,0:T(8,128)(2,1)S(1)}, u32[]{:S(2)}, u32[]{:S(2)}) collective-permute-start(bf16[128,1536]{1,0:T(8,128)(2,1)S(1)} %get-tuple-element.22.refs_0_.refs_9_), channel_id=1, source_target_pairs={{0,2},{1,17},{2,0},{3,19},{4,6},{5,21},{6,4},{7,23},{8,10},{9,25},... | collective-permute-start | bytes 1179656 | tf_op jit(solution)/shard_map/ppermute | solution.py:39
  19.2 13.5 %collective-permute-start.6 = (bf16[128,1536]{1,0:T(8,128)(2,1)S(1)}, bf16[128,1536]{1,0:T(8,128)(2,1)S(1)}, u32[]{:S(2)}, u32[]{:S(2)}) collective-permute-start(bf16[128,1536]{1,0:T(8,128)(2,1)S(1)} %get-tuple-element.22.refs_0_.refs_9_), channel_id=1, source_target_pairs={{0,16},{1,3},{2,18},{3,1},{4,20},{5,7},{6,22},{7,5},{8,24},{9,11},... | collective-permute-start | bytes 1179656 | tf_op jit(solution)/shard_map/ppermute | solution.py:39
  20.7 7.5 %collective-permute-start.7 = (bf16[64,1536]{1,0:T(8,128)(2,1)S(1)}, bf16[64,1536]{1,0:T(8,128)(2,1)S(1)}, u32[]{:S(2)}, u32[]{:S(2)}) collective-permute-start(bf16[64,1536]{1,0:T(8,128)(2,1)S(1)} %collective-permute-done.1.refs_0_), channel_id=1, source_target_pairs={{0,4},{2,6},{4,8},{6,10},{8,12},{10,14},{12,0},{14,2},{1,5},{3,7},... | collective-permute-start | bytes 589832 | tf_op jit(solution)/shard_map/ppermute | solution.py:29
  28.2 7.2 %collective-permute-start.9 = (bf16[64,1536]{1,0:T(8,128)(2,1)S(1)}, bf16[64,1536]{1,0:T(8,128)(2,1)S(1)}, u32[]{:S(2)}, u32[]{:S(2)}) collective-permute-start(bf16[64,1536]{1,0:T(8,128)(2,1)S(1)} %get-tuple-element.25.refs_3_.refs_12_), channel_id=1, source_target_pairs={{0,16},{1,3},{2,18},{3,1},{4,20},{5,7},{6,22},{7,5},{8,24},{9,11},... | collective-permute-start | bytes 589832 | tf_op jit(solution)/shard_map/ppermute | solution.py:39
  28.8 11.4 %copy-start.2 = (bf16[1,1536,64]{1,2,0:T(8,128)(2,1)S(1)}, bf16[1,1536,64]{1,2,0:T(8,128)(2,1)}, u32[]{:S(2)}) copy-start(bf16[1,1536,64]{1,2,0:T(8,128)(2,1)} %param.8) | copy-start | bytes 589828
  31.2 10.7 %collective-permute-start.10 = (bf16[64,1536]{1,0:T(8,128)(2,1)S(1)}, bf16[64,1536]{1,0:T(8,128)(2,1)S(1)}, u32[]{:S(2)}, u32[]{:S(2)}) collective-permute-start(bf16[64,1536]{1,0:T(8,128)(2,1)S(1)} %get-tuple-element.28), channel_id=1, source_target_pairs={{0,16},{1,3},{2,18},{3,1},{4,20},{5,7},{6,22},{7,5},{8,24},{9,11},... | collective-permute-start | bytes 589832 | tf_op jit(solution)/shard_map/ppermute | solution.py:39
  32.7 7.5 %collective-permute-start.8 = (bf16[64,1536]{1,0:T(8,128)(2,1)S(1)}, bf16[64,1536]{1,0:T(8,128)(2,1)S(1)}, u32[]{:S(2)}, u32[]{:S(2)}) collective-permute-start(bf16[64,1536]{1,0:T(8,128)(2,1)S(1)} %get-tuple-element.28), channel_id=1, source_target_pairs={{0,4},{2,6},{4,8},{6,10},{8,12},{10,14},{12,0},{14,2},{1,5},{3,7},... | collective-permute-start | bytes 589832 | tf_op jit(solution)/shard_map/ppermute | solution.py:29
  32.8 9.1 %collective-permute-start.11 = (bf16[64,1536]{1,0:T(8,128)(2,1)S(1)}, bf16[64,1536]{1,0:T(8,128)(2,1)S(1)}, u32[]{:S(2)}, u32[]{:S(2)}) collective-permute-start(bf16[64,1536]{1,0:T(8,128)(2,1)S(1)} %get-tuple-element.32), channel_id=1, source_target_pairs={{0,2},{1,17},{2,0},{3,19},{4,6},{5,21},{6,4},{7,23},{8,10},{9,25},... | collective-permute-start | bytes 589832 | tf_op jit(solution)/shard_map/ppermute | solution.py:39
  35.4 6.5 %collective-permute-start.12 = (bf16[64,1536]{1,0:T(8,128)(2,1)S(1)}, bf16[64,1536]{1,0:T(8,128)(2,1)S(1)}, u32[]{:S(2)}, u32[]{:S(2)}) collective-permute-start(bf16[64,1536]{1,0:T(8,128)(2,1)S(1)} %get-tuple-element.33), channel_id=1, source_target_pairs={{0,2},{1,17},{2,0},{3,19},{4,6},{5,21},{6,4},{7,23},{8,10},{9,25},... | collective-permute-start | bytes 589832 | tf_op jit(solution)/shard_map/ppermute | solution.py:39
  41.9 2.2 %copy-start.3 = (bf16[1,64,1536]{2,1,0:T(8,128)(2,1)S(1)}, bf16[1,64,1536]{2,1,0:T(8,128)(2,1)}, u32[]{:S(2)}) copy-start(bf16[1,64,1536]{2,1,0:T(8,128)(2,1)} %param.9) | copy-start | bytes 589828
  42.5 1.6 %collective-permute-start.13 = (f32[512,128]{1,0:T(8,128)S(1)}, f32[512,128]{1,0:T(8,128)S(1)}, u32[]{:S(2)}, u32[]{:S(2)}) collective-permute-start(f32[512,128]{1,0:T(8,128)S(1)} %shard_map.64.refs_2_), channel_id=1, source_target_pairs={{0,1},{1,0},{2,3},{3,2},{4,5},{5,4},{6,7},{7,6},{8,9},{9,8},{10,11... | collective-permute-start | bytes 786440 | tf_op jit(solution)/shard_map/ppermute | solution.py:21

commit v10 on v9

--- a/solution.py
+++ b/solution.py
@@ -25,8 +25,14 @@
     return lax.ppermute(value, "shard", [(i, i ^ 1) for i in range(shards)])
 
 
+def ring_step(index, step):
+    plane = index >> 1
+    place = ((plane ^ (plane >> 1)) + step) & 3
+    return ((place ^ (place >> 1)) << 1) | (index & 1)
+
+
 def along_line(value, shards, step):
-    return lax.ppermute(value, "shard", [(i, (i + 2 * step) % shards) for i in range(shards)])
+    return lax.ppermute(value, "shard", [(i, ring_step(i, step)) for i in range(shards)])
 
 
 def in_plane(value, shards, first):
@@ -264,7 +270,7 @@
     routed = routed and half_width == out_width and tiles % 6 == 0
     lowrank = jax.ShapeDtypeStruct((rows, 2 * rank), jnp.float32)
     if routed:
-        sources = [(index - 2 * step) % shards for step in (0, 1, 3, 2)]
+        sources = [ring_step(index, -step) for step in (0, 1, 3, 2)]
         owners = [a for source in sources for a in (source, source ^ 1)]
     else:
         owners = list(range(adapters))

time: 47.1 us -> 45 us (0.955)
  waiting for transfers between devices: 14.3 us -> 9.14 us
  starting transfers between devices: 13.3 us -> 16.3 us
    ppermute x4, waiting for transfers between devices: 9.18 us -> 6.3 us  [along_line(): lax.ppermute(value, 'shard', [(i, ring_step(i, step)) for i in range(shar...]
    ppermute x4, starting transfers between devices: 4.78 us -> 6.39 us  [along_line(): lax.ppermute(value, 'shard', [(i, ring_step(i, step)) for i in range(shar...]
    ppermute x6, starting transfers between devices: 5.99 us -> 7.4 us  [in_plane(): return lax.ppermute(value, AXES, pairs)]
    ppermute x6, waiting for transfers between devices: 2.05 us -> 0.7 us  [in_plane(): return lax.ppermute(value, AXES, pairs)]
    ppermute x2, waiting for transfers between devices: 1.51 us -> 0.61 us  [neighbour(): return lax.ppermute(value, 'shard', [(i, i ^ 1) for i in range(shards)])]
  transfers between devices with their start and end apart: 14 -> 14, of which waited for: 6 -> 6; matrix products, arithmetic and copies ran while one was open for 4% -> 4% of each run, Pallas kernels for 19% -> 20%
where the time goes in v10:
time: 45 us; the launch traced here: 44.7 us
  starting transfers between devices  16.3 us (36%)
  Pallas kernels  12.1 us (27%)
  waiting for transfers between devices  9.14 us (20%)
  local copies, waits for them, and re-layouts  6.01 us (13%)
  other arithmetic  1.04 us (2%)
    ppermute x6, starting transfers between devices, in_plane(): return lax.ppermute(value, AXES, pairs)  7.4 us
    pallas_call x3, Pallas kernels, base(): pl.pallas_call(lambda *refs: base_kernel(*refs, skip=skip), out_shape=[ja...  7.01 us
    ppermute x4, starting transfers between devices, along_line(): lax.ppermute(value, 'shard', [(i, ring_step(i, step)) for i in range(shar...  6.39 us
    ppermute x4, waiting for transfers between devices, along_line(): lax.ppermute(value, 'shard', [(i, ring_step(i, step)) for i in range(shar...  6.3 us
    unnamed x9, local copies, waits for them, and re-layouts  5.91 us
    pallas_call x1, Pallas kernels, on_device(): pl.pallas_call(lambda *refs: up_kernel(*refs, base_parts=len(parts)), out...  2.74 us
    ppermute x2, starting transfers between devices, neighbour(): return lax.ppermute(value, 'shard', [(i, i ^ 1) for i in range(shards)])  2.03 us
    pallas_call x1, Pallas kernels, on_device(): call(down_first_kernel, lowrank, [SMEM] + [VMEM] * 10 + [ANY], 16, [pltpu...  1.68 us
  transfers between devices with their start and end apart: 14, of which 6 were waited for; matrix products, arithmetic and copies ran while one was open for 4% of the time, Pallas kernels for 20%

profile of v10, /device:TPU:0, one launch (start us, length us, event | category | flops | bytes accessed | tf_op | source)
XLA Modules:
  0.0 44.7 jit_solution(9615477982181525594)
XLA Ops:
  0.0 0.5 %collective-permute-start.3 = (bf16[512,1536]{1,0:T(8,128)(2,1)}, bf16[512,1536]{1,0:T(8,128)(2,1)S(1)}, u32[]{:S(2)}, u32[]{:S(2)}) collective-permute-start(bf16[512,1536]{1,0:T(8,128)(2,1)} %latent.3), channel_id=1, source_target_pairs={{0,1},{1,0},{2,3},{3,2},{4,5},{5,4},{6,7},{7,6},{8,9},{9,8},{10,11... | collective-permute-start | bytes 4718600 | tf_op jit(solution)/shard_map/ppermute | solution.py:21
  0.5 1.0 %broadcast_select_fusion = bf16[64,1536]{1,0:T(8,128)(2,1)S(1)} fusion(pred[]{:T(512)S(6)} %eq.3, bf16[1,64,1536]{2,1,0:T(8,128)(2,1)} %param.9, bf16[1,1536,64]{1,2,0:T(8,128)(2,1)} %param.8), kind=kLoop, calls=%fused_computation | loop fusion | flops 98304 | bytes 589825 | tf_op jit(solution)/shard_map/jit(_where)/select_n | solution.py:279
  1.5 3.6 %collective-permute-start.2 = (bf16[64,1536]{1,0:T(8,128)(2,1)S(1)}, bf16[64,1536]{1,0:T(8,128)(2,1)S(1)}, u32[]{:S(2)}, u32[]{:S(2)}) collective-permute-start(bf16[64,1536]{1,0:T(8,128)(2,1)S(1)} %broadcast_select_fusion), channel_id=1, source_target_pairs={{0,8},{2,10},{4,0},{6,2},{8,12},{10,14},{12,4},{14,6},{1,9},{3,11}... | collective-permute-start | bytes 589832 | tf_op jit(solution)/shard_map/ppermute | solution.py:35
  5.1 0.0 collective-permute-start.1
  5.1 1.5 %collective-permute-start = (bf16[64,1536]{1,0:T(8,128)(2,1)}, bf16[64,1536]{1,0:T(8,128)(2,1)S(1)}, u32[]{:S(2)}, u32[]{:S(2)}) collective-permute-start(bf16[64,1536]{1,0:T(8,128)(2,1)} %bitcast.16), channel_id=1, source_target_pairs={{0,2},{2,0},{4,6},{6,4},{8,10},{10,8},{12,14},{14,12},{1,3},{3,1},... | collective-permute-start | bytes 589832 | tf_op jit(solution)/shard_map/ppermute | solution.py:25
  6.7 0.5 %collective-permute-start.4 = (bf16[64,1536]{1,0:T(8,128)(2,1)}, bf16[64,1536]{1,0:T(8,128)(2,1)S(1)}, u32[]{:S(2)}, u32[]{:S(2)}) collective-permute-start(bf16[64,1536]{1,0:T(8,128)(2,1)} %bitcast.18), channel_id=1, source_target_pairs={{0,2},{2,0},{4,6},{6,4},{8,10},{10,8},{12,14},{14,12},{1,3},{3,1},... | collective-permute-start | bytes 589832 | tf_op jit(solution)/shard_map/ppermute | solution.py:25
  7.2 0.8 %copy.9.refs_4_.ids.refs_1_ = s32[512,1]{1,0:T(8,128)S(1)} copy(s32[512,1]{0,1:T(1,128)} %param.6) | data formatting | bytes 4096 | tf_op args[1]
  8.0 0.1 stack.47.refs_0_.info
  8.1 0.0 collective-permute-done.3.refs_2_
  8.1 0.0 copy-start
  8.1 3.7 %copy-done = bf16[3072,1536]{1,0:T(8,128)(2,1)S(1)} copy-done((bf16[3072,1536]{1,0:T(8,128)(2,1)S(1)}, bf16[3072,1536]{1,0:T(8,128)(2,1)}, u32[]{:S(2)}) %copy-start) | copy-done | bytes 9437208
  11.8 0.0 copy-start.1
  11.8 1.4 %copy-done.1 = bf16[512,1536]{1,0:T(8,128)(2,1)S(1)} copy-done((bf16[512,1536]{1,0:T(8,128)(2,1)S(1)}, bf16[512,1536]{1,0:T(8,128)(2,1)}, u32[]{:S(2)}) %copy-start.1) | copy-done | bytes 1572888
  13.2 1.5 %shard_map.55 = (f32[512,256]{1,0:T(8,128)S(1)}, f32[8,128]{1,0:T(8,128)S(1)}) custom-call(s32[10]{0:T(128)S(1)} %stack.47.refs_0_.info, bf16[512,1536]{1,0:T(8,128)(2,1)S(1)} %copy-done.1, bf16[512,1536]{1,0:T(8,128)(2,1)S(1)} %collective-permute-done.3.refs_2_, bf16[3072,1536]{1,0:T(8,128)(2,1)S(1)} %copy-done, s32[512,1]{1,0:T(8,128)S(1)} %copy.9.refs_4_.ids.refs_1_), custom_call_target="tpu_custom_call" | custom-call | flops 1000 | bytes 1000 | tf_op jit(solution)/shard_map/pallas_call | solution.py:207
  14.7 0.0 collective-permute-done.2.refs_1_
  14.7 1.3 %collective-permute-done.1.refs_0_ = bf16[64,1536]{1,0:T(8,128)(2,1)S(1)} collective-permute-done((bf16[64,1536]{1,0:T(8,128)(2,1)S(1)}, bf16[64,1536]{1,0:T(8,128)(2,1)S(1)}, u32[]{:S(2)}, u32[]{:S(2)}) %collective-permute-start.1) | collective-permute-done | bytes 196640 | tf_op jit(solution)/shard_map/ppermute | solution.py:35
  16.0 0.0 collective-permute-done.refs_3_.beside
  16.0 0.6 %collective-permute-done.4.refs_4_.refs_8_ = bf16[64,1536]{1,0:T(8,128)(2,1)S(1)} collective-permute-done((bf16[64,1536]{1,0:T(8,128)(2,1)}, bf16[64,1536]{1,0:T(8,128)(2,1)S(1)}, u32[]{:S(2)}, u32[]{:S(2)}) %collective-permute-start.4) | collective-permute-done | bytes 196640 | tf_op jit(solution)/shard_map/ppermute | solution.py:25
  16.6 1.6 %collective-permute-start.5 = (bf16[128,1536]{1,0:T(8,128)(2,1)S(1)}, bf16[128,1536]{1,0:T(8,128)(2,1)S(1)}, u32[]{:S(2)}, u32[]{:S(2)}) collective-permute-start(bf16[128,1536]{1,0:T(8,128)(2,1)S(1)} %get-tuple-element.22.refs_0_.refs_9_), channel_id=1, source_target_pairs={{0,2},{1,17},{2,0},{3,19},{4,6},{5,21},{6,4},{7,23},{8,10},{9,25},... | collective-permute-start | bytes 1179656 | tf_op jit(solution)/shard_map/ppermute | solution.py:45
  18.2 1.5 %collective-permute-start.6 = (bf16[128,1536]{1,0:T(8,128)(2,1)S(1)}, bf16[128,1536]{1,0:T(8,128)(2,1)S(1)}, u32[]{:S(2)}, u32[]{:S(2)}) collective-permute-start(bf16[128,1536]{1,0:T(8,128)(2,1)S(1)} %get-tuple-element.22.refs_0_.refs_9_), channel_id=1, source_target_pairs={{0,16},{1,3},{2,18},{3,1},{4,20},{5,7},{6,22},{7,5},{8,24},{9,11},... | collective-permute-start | bytes 1179656 | tf_op jit(solution)/shard_map/ppermute | solution.py:45
  19.7 1.6 %collective-permute-start.7 = (bf16[64,1536]{1,0:T(8,128)(2,1)S(1)}, bf16[64,1536]{1,0:T(8,128)(2,1)S(1)}, u32[]{:S(2)}, u32[]{:S(2)}) collective-permute-start(bf16[64,1536]{1,0:T(8,128)(2,1)S(1)} %collective-permute-done.1.refs_0_), channel_id=1, source_target_pairs={{0,4},{2,6},{4,12},{6,14},{8,0},{10,2},{12,8},{14,10},{1,5},{3,7},... | collective-permute-start | bytes 589832 | tf_op jit(solution)/shard_map/ppermute | solution.py:35
  21.3 3.2 %shard_map.57 = (f32[512,768]{1,0:T(8,128)S(1)}, f32[8,128]{1,0:T(8,128)S(1)}) custom-call(s32[10]{0:T(128)S(1)} %stack.47.refs_0_.info, bf16[512,1536]{1,0:T(8,128)(2,1)S(1)} %copy-done.1, bf16[512,1536]{1,0:T(8,128)(2,1)S(1)} %collective-permute-done.3.refs_2_, bf16[3072,1536]{1,0:T(8,128)(2,1)S(1)} %copy-done, f32[8,128]{1,0:T(8,128)S(1)} %get-tuple-element.23.refs_4_), custom_call_target="tpu_custom_call" | custom-call | flops 1000 | bytes 1000 | tf_op jit(solution)/shard_map/pallas_call | solution.py:207
  24.5 1.8 %collective-permute-done.7.refs_0_ = bf16[64,1536]{1,0:T(8,128)(2,1)S(1)} collective-permute-done((bf16[64,1536]{1,0:T(8,128)(2,1)S(1)}, bf16[64,1536]{1,0:T(8,128)(2,1)S(1)}, u32[]{:S(2)}, u32[]{:S(2)}) %collective-permute-start.7) | collective-permute-done | bytes 196640 | tf_op jit(solution)/shard_map/ppermute | solution.py:35
  26.3 0.6 %collective-permute-start.9 = (bf16[64,1536]{1,0:T(8,128)(2,1)S(1)}, bf16[64,1536]{1,0:T(8,128)(2,1)S(1)}, u32[]{:S(2)}, u32[]{:S(2)}) collective-permute-start(bf16[64,1536]{1,0:T(8,128)(2,1)S(1)} %get-tuple-element.25.refs_3_.refs_12_), channel_id=1, source_target_pairs={{0,16},{1,3},{2,18},{3,1},{4,20},{5,7},{6,22},{7,5},{8,24},{9,11},... | collective-permute-start | bytes 589832 | tf_op jit(solution)/shard_map/ppermute | solution.py:45
  26.9 0.0 copy-start.2
  26.9 2.3 %shard_map.59 = (f32[512,512]{1,0:T(8,128)S(1)}, f32[8,128]{1,0:T(8,128)S(1)}) custom-call(s32[10]{0:T(128)S(1)} %stack.47.refs_0_.info, bf16[512,1536]{1,0:T(8,128)(2,1)S(1)} %copy-done.1, bf16[512,1536]{1,0:T(8,128)(2,1)S(1)} %collective-permute-done.3.refs_2_, bf16[3072,1536]{1,0:T(8,128)(2,1)S(1)} %copy-done, f32[8,128]{1,0:T(8,128)S(1)} %get-tuple-element.26.refs_4_), custom_call_target="tpu_custom_call" | custom-call | flops 1000 | bytes 1000 | tf_op jit(solution)/shard_map/pallas_call | solution.py:207
  29.2 0.0 collective-permute-done.5.refs_0_.refs_1_.refs_10_
  29.3 1.6 %collective-permute-start.10 = (bf16[64,1536]{1,0:T(8,128)(2,1)S(1)}, bf16[64,1536]{1,0:T(8,128)(2,1)S(1)}, u32[]{:S(2)}, u32[]{:S(2)}) collective-permute-start(bf16[64,1536]{1,0:T(8,128)(2,1)S(1)} %get-tuple-element.28), channel_id=1, source_target_pairs={{0,16},{1,3},{2,18},{3,1},{4,20},{5,7},{6,22},{7,5},{8,24},{9,11},... | collective-permute-start | bytes 589832 | tf_op jit(solution)/shard_map/ppermute | solution.py:45
  30.9 1.1 %collective-permute-start.8 = (bf16[64,1536]{1,0:T(8,128)(2,1)S(1)}, bf16[64,1536]{1,0:T(8,128)(2,1)S(1)}, u32[]{:S(2)}, u32[]{:S(2)}) collective-permute-start(bf16[64,1536]{1,0:T(8,128)(2,1)S(1)} %get-tuple-element.28), channel_id=1, source_target_pairs={{0,4},{2,6},{4,12},{6,14},{8,0},{10,2},{12,8},{14,10},{1,5},{3,7},... | collective-permute-start | bytes 589832 | tf_op jit(solution)/shard_map/ppermute | solution.py:35
  32.0 0.0 collective-permute-done.6.refs_0_.refs_2_.refs_11_
  32.0 1.6 %collective-permute-start.11 = (bf16[64,1536]{1,0:T(8,128)(2,1)S(1)}, bf16[64,1536]{1,0:T(8,128)(2,1)S(1)}, u32[]{:S(2)}, u32[]{:S(2)}) collective-permute-start(bf16[64,1536]{1,0:T(8,128)(2,1)S(1)} %get-tuple-element.32), channel_id=1, source_target_pairs={{0,2},{1,17},{2,0},{3,19},{4,6},{5,21},{6,4},{7,23},{8,10},{9,25},... | collective-permute-start | bytes 589832 | tf_op jit(solution)/shard_map/ppermute | solution.py:45
  33.6 0.0 collective-permute-done.9.refs_0_.refs_5_.refs_14_
  33.6 0.6 %collective-permute-start.12 = (bf16[64,1536]{1,0:T(8,128)(2,1)S(1)}, bf16[64,1536]{1,0:T(8,128)(2,1)S(1)}, u32[]{:S(2)}, u32[]{:S(2)}) collective-permute-start(bf16[64,1536]{1,0:T(8,128)(2,1)S(1)} %get-tuple-element.33), channel_id=1, source_target_pairs={{0,2},{1,17},{2,0},{3,19},{4,6},{5,21},{6,4},{7,23},{8,10},{9,25},... | collective-permute-start | bytes 589832 | tf_op jit(solution)/shard_map/ppermute | solution.py:45
  34.2 3.3 %collective-permute-done.8.refs_4_.refs_13_ = bf16[64,1536]{1,0:T(8,128)(2,1)S(1)} collective-permute-done((bf16[64,1536]{1,0:T(8,128)(2,1)S(1)}, bf16[64,1536]{1,0:T(8,128)(2,1)S(1)}, u32[]{:S(2)}, u32[]{:S(2)}) %collective-permute-start.8) | collective-permute-done | bytes 196640 | tf_op jit(solution)/shard_map/ppermute | solution.py:35
  37.4 0.0 copy-done.2
  37.4 1.7 %shard_map.63.earlier = f32[512,128]{1,0:T(8,128)S(1)} custom-call(s32[10]{0:T(128)S(1)} %stack.47.refs_0_.info, s32[512,1]{1,0:T(8,128)S(1)} %copy.9.refs_4_.ids.refs_1_, bf16[512,1536]{1,0:T(8,128)(2,1)S(1)} %copy-done.1, bf16[64,1536]{1,0:T(8,128)(2,1)S(1)} %bitcast.17, bf16[64,1536]{1,0:T(8,128)(2,1)S(1)} %collective-permute-done.refs_3_.beside, ...), custom_call_target="tpu_custom_call" | custom-call | tf_op jit(solution)/shard_map/pallas_call | solution.py:304
  39.1 0.0 copy-start.3
  39.1 0.0 collective-permute-done.11.refs_1_.refs_16_
  39.1 0.0 collective-permute-done.10.refs_0_.refs_15_
  39.1 0.7 %collective-permute-done.12.refs_2_.refs_17_ = bf16[64,1536]{1,0:T(8,128)(2,1)S(1)} collective-permute-done((bf16[64,1536]{1,0:T(8,128)(2,1)S(1)}, bf16[64,1536]{1,0:T(8,128)(2,1)S(1)}, u32[]{:S(2)}, u32[]{:S(2)}) %collective-permute-start.12) | collective-permute-done | bytes 196640 | tf_op jit(solution)/shard_map/ppermute | solution.py:45
  39.8 0.6 %shard_map.64.refs_2_ = f32[512,128]{1,0:T(8,128)S(1)} custom-call(s32[10]{0:T(128)S(1)} %stack.47.refs_0_.info, s32[512,1]{1,0:T(8,128)S(1)} %copy.9.refs_4_.ids.refs_1_, bf16[512,1536]{1,0:T(8,128)(2,1)S(1)} %copy-done.1, f32[512,128]{1,0:T(8,128)S(1)} %shard_map.63.earlier, bf16[64,1536]{1,0:T(8,128)(2,1)S(1)} %collective-permute-done.10.refs_0_.refs_15_, ...), custom_call_target="tpu_custom_call" | custom-call | tf_op jit(solution)/shard_map/pallas_call | solution.py:311
  40.4 0.1 collective-permute-start.13
  40.5 1.5 %collective-permute-done.13.refs_3_ = f32[512,128]{1,0:T(8,128)S(1)} collective-permute-done((f32[512,128]{1,0:T(8,128)S(1)}, f32[512,128]{1,0:T(8,128)S(1)}, u32[]{:S(2)}, u32[]{:S(2)}) %collective-permute-start.13) | collective-permute-done | bytes 262176 | tf_op jit(solution)/shard_map/ppermute | solution.py:21
  42.0 0.0 copy-done.3
  42.0 2.7 %shard_map.65 = bf16[512,1536]{1,0:T(8,128)(2,1)} custom-call(s32[10]{0:T(128)S(1)} %stack.47.refs_0_.info, s32[512,1]{1,0:T(8,128)S(1)} %copy.9.refs_4_.ids.refs_1_, f32[512,128]{1,0:T(8,128)S(1)} %shard_map.64.refs_2_, f32[512,128]{1,0:T(8,128)S(1)} %collective-permute-done.13.refs_3_, f32[512,256]{1,0:T(8,128)S(1)} %get-tuple-element.34.refs_4_, ...), custom_call_target="tpu_custom_call" | custom-call | tf_op jit(solution)/shard_map/pallas_call | solution.py:331
  (5 shorter events, 0.1 us)
Async XLA Ops:
  0.0 8.1 %collective-permute-start.3 = (bf16[512,1536]{1,0:T(8,128)(2,1)}, bf16[512,1536]{1,0:T(8,128)(2,1)S(1)}, u32[]{:S(2)}, u32[]{:S(2)}) collective-permute-start(bf16[512,1536]{1,0:T(8,128)(2,1)} %latent.3), channel_id=1, source_target_pairs={{0,1},{1,0},{2,3},{3,2},{4,5},{5,4},{6,7},{7,6},{8,9},{9,8},{10,11... | collective-permute-start | bytes 4718600 | tf_op jit(solution)/shard_map/ppermute | solution.py:21
  1.5 13.2 %collective-permute-start.2 = (bf16[64,1536]{1,0:T(8,128)(2,1)S(1)}, bf16[64,1536]{1,0:T(8,128)(2,1)S(1)}, u32[]{:S(2)}, u32[]{:S(2)}) collective-permute-start(bf16[64,1536]{1,0:T(8,128)(2,1)S(1)} %broadcast_select_fusion), channel_id=1, source_target_pairs={{0,8},{2,10},{4,0},{6,2},{8,12},{10,14},{12,4},{14,6},{1,9},{3,11}... | collective-permute-start | bytes 589832 | tf_op jit(solution)/shard_map/ppermute | solution.py:35
  5.1 10.8 %collective-permute-start.1 = (bf16[64,1536]{1,0:T(8,128)(2,1)S(1)}, bf16[64,1536]{1,0:T(8,128)(2,1)S(1)}, u32[]{:S(2)}, u32[]{:S(2)}) collective-permute-start(bf16[64,1536]{1,0:T(8,128)(2,1)S(1)} %broadcast_select_fusion), channel_id=1, source_target_pairs={{0,4},{2,6},{4,12},{6,14},{8,0},{10,2},{12,8},{14,10},{1,5},{3,7},... | collective-permute-start | bytes 589832 | tf_op jit(solution)/shard_map/ppermute | solution.py:35
  5.1 10.8 %collective-permute-start = (bf16[64,1536]{1,0:T(8,128)(2,1)}, bf16[64,1536]{1,0:T(8,128)(2,1)S(1)}, u32[]{:S(2)}, u32[]{:S(2)}) collective-permute-start(bf16[64,1536]{1,0:T(8,128)(2,1)} %bitcast.16), channel_id=1, source_target_pairs={{0,2},{2,0},{4,6},{6,4},{8,10},{10,8},{12,14},{14,12},{1,3},{3,1},... | collective-permute-start | bytes 589832 | tf_op jit(solution)/shard_map/ppermute | solution.py:25
  6.7 9.9 %collective-permute-start.4 = (bf16[64,1536]{1,0:T(8,128)(2,1)}, bf16[64,1536]{1,0:T(8,128)(2,1)S(1)}, u32[]{:S(2)}, u32[]{:S(2)}) collective-permute-start(bf16[64,1536]{1,0:T(8,128)(2,1)} %bitcast.18), channel_id=1, source_target_pairs={{0,2},{2,0},{4,6},{6,4},{8,10},{10,8},{12,14},{14,12},{1,3},{3,1},... | collective-permute-start | bytes 589832 | tf_op jit(solution)/shard_map/ppermute | solution.py:25
  8.1 3.7 %copy-start = (bf16[3072,1536]{1,0:T(8,128)(2,1)S(1)}, bf16[3072,1536]{1,0:T(8,128)(2,1)}, u32[]{:S(2)}) copy-start(bf16[3072,1536]{1,0:T(8,128)(2,1)} %refs_3_.5) | copy-start | bytes 28311556
  11.8 1.4 %copy-start.1 = (bf16[512,1536]{1,0:T(8,128)(2,1)S(1)}, bf16[512,1536]{1,0:T(8,128)(2,1)}, u32[]{:S(2)}) copy-start(bf16[512,1536]{1,0:T(8,128)(2,1)} %latent.3) | copy-start | bytes 4718596
  16.6 12.6 %collective-permute-start.5 = (bf16[128,1536]{1,0:T(8,128)(2,1)S(1)}, bf16[128,1536]{1,0:T(8,128)(2,1)S(1)}, u32[]{:S(2)}, u32[]{:S(2)}) collective-permute-start(bf16[128,1536]{1,0:T(8,128)(2,1)S(1)} %get-tuple-element.22.refs_0_.refs_9_), channel_id=1, source_target_pairs={{0,2},{1,17},{2,0},{3,19},{4,6},{5,21},{6,4},{7,23},{8,10},{9,25},... | collective-permute-start | bytes 1179656 | tf_op jit(solution)/shard_map/ppermute | solution.py:45
  18.2 13.8 %collective-permute-start.6 = (bf16[128,1536]{1,0:T(8,128)(2,1)S(1)}, bf16[128,1536]{1,0:T(8,128)(2,1)S(1)}, u32[]{:S(2)}, u32[]{:S(2)}) collective-permute-start(bf16[128,1536]{1,0:T(8,128)(2,1)S(1)} %get-tuple-element.22.refs_0_.refs_9_), channel_id=1, source_target_pairs={{0,16},{1,3},{2,18},{3,1},{4,20},{5,7},{6,22},{7,5},{8,24},{9,11},... | collective-permute-start | bytes 1179656 | tf_op jit(solution)/shard_map/ppermute | solution.py:45
  19.7 6.6 %collective-permute-start.7 = (bf16[64,1536]{1,0:T(8,128)(2,1)S(1)}, bf16[64,1536]{1,0:T(8,128)(2,1)S(1)}, u32[]{:S(2)}, u32[]{:S(2)}) collective-permute-start(bf16[64,1536]{1,0:T(8,128)(2,1)S(1)} %collective-permute-done.1.refs_0_), channel_id=1, source_target_pairs={{0,4},{2,6},{4,12},{6,14},{8,0},{10,2},{12,8},{14,10},{1,5},{3,7},... | collective-permute-start | bytes 589832 | tf_op jit(solution)/shard_map/ppermute | solution.py:35
  26.3 7.3 %collective-permute-start.9 = (bf16[64,1536]{1,0:T(8,128)(2,1)S(1)}, bf16[64,1536]{1,0:T(8,128)(2,1)S(1)}, u32[]{:S(2)}, u32[]{:S(2)}) collective-permute-start(bf16[64,1536]{1,0:T(8,128)(2,1)S(1)} %get-tuple-element.25.refs_3_.refs_12_), channel_id=1, source_target_pairs={{0,16},{1,3},{2,18},{3,1},{4,20},{5,7},{6,22},{7,5},{8,24},{9,11},... | collective-permute-start | bytes 589832 | tf_op jit(solution)/shard_map/ppermute | solution.py:45
  26.9 10.5 %copy-start.2 = (bf16[1,1536,64]{1,2,0:T(8,128)(2,1)S(1)}, bf16[1,1536,64]{1,2,0:T(8,128)(2,1)}, u32[]{:S(2)}) copy-start(bf16[1,1536,64]{1,2,0:T(8,128)(2,1)} %param.8) | copy-start | bytes 589828
  29.3 9.9 %collective-permute-start.10 = (bf16[64,1536]{1,0:T(8,128)(2,1)S(1)}, bf16[64,1536]{1,0:T(8,128)(2,1)S(1)}, u32[]{:S(2)}, u32[]{:S(2)}) collective-permute-start(bf16[64,1536]{1,0:T(8,128)(2,1)S(1)} %get-tuple-element.28), channel_id=1, source_target_pairs={{0,16},{1,3},{2,18},{3,1},{4,20},{5,7},{6,22},{7,5},{8,24},{9,11},... | collective-permute-start | bytes 589832 | tf_op jit(solution)/shard_map/ppermute | solution.py:45
  30.9 6.6 %collective-permute-start.8 = (bf16[64,1536]{1,0:T(8,128)(2,1)S(1)}, bf16[64,1536]{1,0:T(8,128)(2,1)S(1)}, u32[]{:S(2)}, u32[]{:S(2)}) collective-permute-start(bf16[64,1536]{1,0:T(8,128)(2,1)S(1)} %get-tuple-element.28), channel_id=1, source_target_pairs={{0,4},{2,6},{4,12},{6,14},{8,0},{10,2},{12,8},{14,10},{1,5},{3,7},... | collective-permute-start | bytes 589832 | tf_op jit(solution)/shard_map/ppermute | solution.py:35
  32.0 7.1 %collective-permute-start.11 = (bf16[64,1536]{1,0:T(8,128)(2,1)S(1)}, bf16[64,1536]{1,0:T(8,128)(2,1)S(1)}, u32[]{:S(2)}, u32[]{:S(2)}) collective-permute-start(bf16[64,1536]{1,0:T(8,128)(2,1)S(1)} %get-tuple-element.32), channel_id=1, source_target_pairs={{0,2},{1,17},{2,0},{3,19},{4,6},{5,21},{6,4},{7,23},{8,10},{9,25},... | collective-permute-start | bytes 589832 | tf_op jit(solution)/shard_map/ppermute | solution.py:45
  33.6 6.2 %collective-permute-start.12 = (bf16[64,1536]{1,0:T(8,128)(2,1)S(1)}, bf16[64,1536]{1,0:T(8,128)(2,1)S(1)}, u32[]{:S(2)}, u32[]{:S(2)}) collective-permute-start(bf16[64,1536]{1,0:T(8,128)(2,1)S(1)} %get-tuple-element.33), channel_id=1, source_target_pairs={{0,2},{1,17},{2,0},{3,19},{4,6},{5,21},{6,4},{7,23},{8,10},{9,25},... | collective-permute-start | bytes 589832 | tf_op jit(solution)/shard_map/ppermute | solution.py:45
  39.1 2.9 %copy-start.3 = (bf16[1,64,1536]{2,1,0:T(8,128)(2,1)S(1)}, bf16[1,64,1536]{2,1,0:T(8,128)(2,1)}, u32[]{:S(2)}) copy-start(bf16[1,64,1536]{2,1,0:T(8,128)(2,1)} %param.9) | copy-start | bytes 589828
  40.4 1.6 %collective-permute-start.13 = (f32[512,128]{1,0:T(8,128)S(1)}, f32[512,128]{1,0:T(8,128)S(1)}, u32[]{:S(2)}, u32[]{:S(2)}) collective-permute-start(f32[512,128]{1,0:T(8,128)S(1)} %shard_map.64.refs_2_), channel_id=1, source_target_pairs={{0,1},{1,0},{2,3},{3,2},{4,5},{5,4},{6,7},{7,6},{8,9},{9,8},{10,11... | collective-permute-start | bytes 786440 | tf_op jit(solution)/shard_map/ppermute | solution.py:21

commit v11 on v10

--- a/solution.py
+++ b/solution.py
@@ -289,8 +289,6 @@
         parts.append(part)
         early_first, early_second = in_plane(early, shards, True), in_plane(early, shards, False)
         late, token = pack([(line[2], 0, rank)], token)
-        part, token = base(info, latent, other, shared_weight, [token], cuts[2], cuts[3])
-        parts.append(part)
         late_second = in_plane(late, shards, False)
         turn, token = pack([(early_first, 0, rank)], token)
         corner_one = in_plane(turn, shards, False)
@@ -299,6 +297,8 @@
         corner_two = in_plane(turn, shards, True)
         turn, token = pack([(late_second, 0, rank)], token)
         corner_three = in_plane(turn, shards, True)
+        part, token = base(info, latent, other, shared_weight, [token], cuts[2], cuts[3])
+        parts.append(part)
         corners = [corner_one, corner_two, corner_three]
         received = [early, early_first, early_second, late, late_first, late_second]
         mine = call(

time: 45 us -> 45 us (level)
  starting transfers between devices: 16.3 us -> 16.9 us
  waiting for transfers between devices: 9.14 us -> 8.56 us
    ppermute x4, waiting for transfers between devices: 6.3 us -> 3.41 us  [along_line(): lax.ppermute(value, 'shard', [(i, ring_step(i, step)) for i in range(shar...]
    ppermute x6, waiting for transfers between devices: 0.7 us -> 3.02 us  [in_plane(): return lax.ppermute(value, AXES, pairs)]
    ppermute x4, starting transfers between devices: 6.39 us -> 6.95 us  [along_line(): lax.ppermute(value, 'shard', [(i, ring_step(i, step)) for i in range(shar...]
  transfers between devices with their start and end apart: 14 -> 14, of which waited for: 6 -> 7; matrix products, arithmetic and copies ran while one was open for 4% -> 4% of each run, Pallas kernels for 20% -> 20%
where the time goes in v11:
time: 45 us; the launch traced here: 44.7 us
  starting transfers between devices  16.9 us (38%)
  Pallas kernels  12.1 us (27%)
  waiting for transfers between devices  8.56 us (19%)
  local copies, waits for them, and re-layouts  6.01 us (13%)
  other arithmetic  1.04 us (2%)
    ppermute x6, starting transfers between devices, in_plane(): return lax.ppermute(value, AXES, pairs)  7.43 us
    pallas_call x3, Pallas kernels, base(): pl.pallas_call(lambda *refs: base_kernel(*refs, skip=skip), out_shape=[ja...  7.01 us
    ppermute x4, starting transfers between devices, along_line(): lax.ppermute(value, 'shard', [(i, ring_step(i, step)) for i in range(shar...  6.95 us
    unnamed x9, local copies, waits for them, and re-layouts  5.91 us
    ppermute x4, waiting for transfers between devices, along_line(): lax.ppermute(value, 'shard', [(i, ring_step(i, step)) for i in range(shar...  3.41 us
    ppermute x6, waiting for transfers between devices, in_plane(): return lax.ppermute(value, AXES, pairs)  3.02 us
    pallas_call x1, Pallas kernels, on_device(): pl.pallas_call(lambda *refs: up_kernel(*refs, base_parts=len(parts)), out...  2.74 us
    ppermute x2, starting transfers between devices, neighbour(): return lax.ppermute(value, 'shard', [(i, i ^ 1) for i in range(shards)])  2.03 us
  transfers between devices with their start and end apart: 14, of which 7 were waited for; matrix products, arithmetic and copies ran while one was open for 4% of the time, Pallas kernels for 20%

profile of v11, /device:TPU:0, one launch (start us, length us, event | category | flops | bytes accessed | tf_op | source)
XLA Modules:
  0.0 44.7 jit_solution(11827288686561944722)
XLA Ops:
  0.0 0.5 %collective-permute-start.3 = (bf16[512,1536]{1,0:T(8,128)(2,1)}, bf16[512,1536]{1,0:T(8,128)(2,1)S(1)}, u32[]{:S(2)}, u32[]{:S(2)}) collective-permute-start(bf16[512,1536]{1,0:T(8,128)(2,1)} %latent.3), channel_id=1, source_target_pairs={{0,1},{1,0},{2,3},{3,2},{4,5},{5,4},{6,7},{7,6},{8,9},{9,8},{10,11... | collective-permute-start | bytes 4718600 | tf_op jit(solution)/shard_map/ppermute | solution.py:21
  0.5 1.0 %broadcast_select_fusion = bf16[64,1536]{1,0:T(8,128)(2,1)S(1)} fusion(pred[]{:T(512)S(6)} %eq.3, bf16[1,64,1536]{2,1,0:T(8,128)(2,1)} %param.9, bf16[1,1536,64]{1,2,0:T(8,128)(2,1)} %param.8), kind=kLoop, calls=%fused_computation | loop fusion | flops 98304 | bytes 589825 | tf_op jit(solution)/shard_map/jit(_where)/select_n | solution.py:279
  1.5 3.6 %collective-permute-start.2 = (bf16[64,1536]{1,0:T(8,128)(2,1)S(1)}, bf16[64,1536]{1,0:T(8,128)(2,1)S(1)}, u32[]{:S(2)}, u32[]{:S(2)}) collective-permute-start(bf16[64,1536]{1,0:T(8,128)(2,1)S(1)} %broadcast_select_fusion), channel_id=1, source_target_pairs={{0,8},{2,10},{4,0},{6,2},{8,12},{10,14},{12,4},{14,6},{1,9},{3,11}... | collective-permute-start | bytes 589832 | tf_op jit(solution)/shard_map/ppermute | solution.py:35
  5.1 0.0 collective-permute-start.1
  5.1 1.5 %collective-permute-start = (bf16[64,1536]{1,0:T(8,128)(2,1)}, bf16[64,1536]{1,0:T(8,128)(2,1)S(1)}, u32[]{:S(2)}, u32[]{:S(2)}) collective-permute-start(bf16[64,1536]{1,0:T(8,128)(2,1)} %bitcast.16), channel_id=1, source_target_pairs={{0,2},{2,0},{4,6},{6,4},{8,10},{10,8},{12,14},{14,12},{1,3},{3,1},... | collective-permute-start | bytes 589832 | tf_op jit(solution)/shard_map/ppermute | solution.py:25
  6.7 0.5 %collective-permute-start.4 = (bf16[64,1536]{1,0:T(8,128)(2,1)}, bf16[64,1536]{1,0:T(8,128)(2,1)S(1)}, u32[]{:S(2)}, u32[]{:S(2)}) collective-permute-start(bf16[64,1536]{1,0:T(8,128)(2,1)} %bitcast.18), channel_id=1, source_target_pairs={{0,2},{2,0},{4,6},{6,4},{8,10},{10,8},{12,14},{14,12},{1,3},{3,1},... | collective-permute-start | bytes 589832 | tf_op jit(solution)/shard_map/ppermute | solution.py:25
  7.2 0.8 %copy.9.refs_4_.ids.refs_1_ = s32[512,1]{1,0:T(8,128)S(1)} copy(s32[512,1]{0,1:T(1,128)} %param.6) | data formatting | bytes 4096 | tf_op args[1]
  8.0 0.1 stack.47.refs_0_.info
  8.1 0.0 collective-permute-done.3.refs_2_
  8.1 0.0 copy-start
  8.1 3.7 %copy-done = bf16[3072,1536]{1,0:T(8,128)(2,1)S(1)} copy-done((bf16[3072,1536]{1,0:T(8,128)(2,1)S(1)}, bf16[3072,1536]{1,0:T(8,128)(2,1)}, u32[]{:S(2)}) %copy-start) | copy-done | bytes 9437208
  11.8 0.0 copy-start.1
  11.8 1.4 %copy-done.1 = bf16[512,1536]{1,0:T(8,128)(2,1)S(1)} copy-done((bf16[512,1536]{1,0:T(8,128)(2,1)S(1)}, bf16[512,1536]{1,0:T(8,128)(2,1)}, u32[]{:S(2)}) %copy-start.1) | copy-done | bytes 1572888
  13.2 1.5 %shard_map.55 = (f32[512,256]{1,0:T(8,128)S(1)}, f32[8,128]{1,0:T(8,128)S(1)}) custom-call(s32[10]{0:T(128)S(1)} %stack.47.refs_0_.info, bf16[512,1536]{1,0:T(8,128)(2,1)S(1)} %copy-done.1, bf16[512,1536]{1,0:T(8,128)(2,1)S(1)} %collective-permute-done.3.refs_2_, bf16[3072,1536]{1,0:T(8,128)(2,1)S(1)} %copy-done, s32[512,1]{1,0:T(8,128)S(1)} %copy.9.refs_4_.ids.refs_1_), custom_call_target="tpu_custom_call" | custom-call | flops 1000 | bytes 1000 | tf_op jit(solution)/shard_map/pallas_call | solution.py:207
  14.7 0.0 collective-permute-done.2.refs_1_
  14.7 1.3 %collective-permute-done.1.refs_0_ = bf16[64,1536]{1,0:T(8,128)(2,1)S(1)} collective-permute-done((bf16[64,1536]{1,0:T(8,128)(2,1)S(1)}, bf16[64,1536]{1,0:T(8,128)(2,1)S(1)}, u32[]{:S(2)}, u32[]{:S(2)}) %collective-permute-start.1) | collective-permute-done | bytes 196640 | tf_op jit(solution)/shard_map/ppermute | solution.py:35
  16.0 0.0 collective-permute-done.refs_3_.beside
  16.0 0.6 %collective-permute-done.4.refs_4_.refs_8_ = bf16[64,1536]{1,0:T(8,128)(2,1)S(1)} collective-permute-done((bf16[64,1536]{1,0:T(8,128)(2,1)}, bf16[64,1536]{1,0:T(8,128)(2,1)S(1)}, u32[]{:S(2)}, u32[]{:S(2)}) %collective-permute-start.4) | collective-permute-done | bytes 196640 | tf_op jit(solution)/shard_map/ppermute | solution.py:25
  16.6 1.6 %collective-permute-start.5 = (bf16[128,1536]{1,0:T(8,128)(2,1)S(1)}, bf16[128,1536]{1,0:T(8,128)(2,1)S(1)}, u32[]{:S(2)}, u32[]{:S(2)}) collective-permute-start(bf16[128,1536]{1,0:T(8,128)(2,1)S(1)} %get-tuple-element.22.refs_0_.refs_9_), channel_id=1, source_target_pairs={{0,2},{1,17},{2,0},{3,19},{4,6},{5,21},{6,4},{7,23},{8,10},{9,25},... | collective-permute-start | bytes 1179656 | tf_op jit(solution)/shard_map/ppermute | solution.py:45
  18.2 1.5 %collective-permute-start.6 = (bf16[128,1536]{1,0:T(8,128)(2,1)S(1)}, bf16[128,1536]{1,0:T(8,128)(2,1)S(1)}, u32[]{:S(2)}, u32[]{:S(2)}) collective-permute-start(bf16[128,1536]{1,0:T(8,128)(2,1)S(1)} %get-tuple-element.22.refs_0_.refs_9_), channel_id=1, source_target_pairs={{0,16},{1,3},{2,18},{3,1},{4,20},{5,7},{6,22},{7,5},{8,24},{9,11},... | collective-permute-start | bytes 1179656 | tf_op jit(solution)/shard_map/ppermute | solution.py:45
  19.7 1.6 %collective-permute-start.7 = (bf16[64,1536]{1,0:T(8,128)(2,1)S(1)}, bf16[64,1536]{1,0:T(8,128)(2,1)S(1)}, u32[]{:S(2)}, u32[]{:S(2)}) collective-permute-start(bf16[64,1536]{1,0:T(8,128)(2,1)S(1)} %collective-permute-done.1.refs_0_), channel_id=1, source_target_pairs={{0,4},{2,6},{4,12},{6,14},{8,0},{10,2},{12,8},{14,10},{1,5},{3,7},... | collective-permute-start | bytes 589832 | tf_op jit(solution)/shard_map/ppermute | solution.py:35
  21.3 3.2 %shard_map.57 = (f32[512,768]{1,0:T(8,128)S(1)}, f32[8,128]{1,0:T(8,128)S(1)}) custom-call(s32[10]{0:T(128)S(1)} %stack.47.refs_0_.info, bf16[512,1536]{1,0:T(8,128)(2,1)S(1)} %copy-done.1, bf16[512,1536]{1,0:T(8,128)(2,1)S(1)} %collective-permute-done.3.refs_2_, bf16[3072,1536]{1,0:T(8,128)(2,1)S(1)} %copy-done, f32[8,128]{1,0:T(8,128)S(1)} %get-tuple-element.23.refs_4_), custom_call_target="tpu_custom_call" | custom-call | flops 1000 | bytes 1000 | tf_op jit(solution)/shard_map/pallas_call | solution.py:207
  24.5 1.8 %collective-permute-done.7.refs_0_ = bf16[64,1536]{1,0:T(8,128)(2,1)S(1)} collective-permute-done((bf16[64,1536]{1,0:T(8,128)(2,1)S(1)}, bf16[64,1536]{1,0:T(8,128)(2,1)S(1)}, u32[]{:S(2)}, u32[]{:S(2)}) %collective-permute-start.7) | collective-permute-done | bytes 196640 | tf_op jit(solution)/shard_map/ppermute | solution.py:35
  26.3 0.6 %collective-permute-start.9 = (bf16[64,1536]{1,0:T(8,128)(2,1)S(1)}, bf16[64,1536]{1,0:T(8,128)(2,1)S(1)}, u32[]{:S(2)}, u32[]{:S(2)}) collective-permute-start(bf16[64,1536]{1,0:T(8,128)(2,1)S(1)} %get-tuple-element.25.refs_3_.refs_12_), channel_id=1, source_target_pairs={{0,16},{1,3},{2,18},{3,1},{4,20},{5,7},{6,22},{7,5},{8,24},{9,11},... | collective-permute-start | bytes 589832 | tf_op jit(solution)/shard_map/ppermute | solution.py:45
  26.9 1.8 %collective-permute-done.5.refs_0_.refs_1_.refs_10_ = bf16[128,1536]{1,0:T(8,128)(2,1)S(1)} collective-permute-done((bf16[128,1536]{1,0:T(8,128)(2,1)S(1)}, bf16[128,1536]{1,0:T(8,128)(2,1)S(1)}, u32[]{:S(2)}, u32[]{:S(2)}) %collective-permute-start.5) | collective-permute-done | bytes 393248 | tf_op jit(solution)/shard_map/ppermute | solution.py:45
  28.7 1.6 %collective-permute-start.10 = (bf16[64,1536]{1,0:T(8,128)(2,1)S(1)}, bf16[64,1536]{1,0:T(8,128)(2,1)S(1)}, u32[]{:S(2)}, u32[]{:S(2)}) collective-permute-start(bf16[64,1536]{1,0:T(8,128)(2,1)S(1)} %get-tuple-element.27), channel_id=1, source_target_pairs={{0,16},{1,3},{2,18},{3,1},{4,20},{5,7},{6,22},{7,5},{8,24},{9,11},... | collective-permute-start | bytes 589832 | tf_op jit(solution)/shard_map/ppermute | solution.py:45
  30.3 1.7 %collective-permute-start.8 = (bf16[64,1536]{1,0:T(8,128)(2,1)S(1)}, bf16[64,1536]{1,0:T(8,128)(2,1)S(1)}, u32[]{:S(2)}, u32[]{:S(2)}) collective-permute-start(bf16[64,1536]{1,0:T(8,128)(2,1)S(1)} %get-tuple-element.27), channel_id=1, source_target_pairs={{0,4},{2,6},{4,12},{6,14},{8,0},{10,2},{12,8},{14,10},{1,5},{3,7},... | collective-permute-start | bytes 589832 | tf_op jit(solution)/shard_map/ppermute | solution.py:35
  32.0 0.0 collective-permute-done.6.refs_0_.refs_2_.refs_11_
  32.0 1.6 %collective-permute-start.11 = (bf16[64,1536]{1,0:T(8,128)(2,1)S(1)}, bf16[64,1536]{1,0:T(8,128)(2,1)S(1)}, u32[]{:S(2)}, u32[]{:S(2)}) collective-permute-start(bf16[64,1536]{1,0:T(8,128)(2,1)S(1)} %get-tuple-element.32), channel_id=1, source_target_pairs={{0,2},{1,17},{2,0},{3,19},{4,6},{5,21},{6,4},{7,23},{8,10},{9,25},... | collective-permute-start | bytes 589832 | tf_op jit(solution)/shard_map/ppermute | solution.py:45
  33.6 0.0 collective-permute-done.9.refs_0_.refs_5_.refs_14_
  33.6 0.6 %collective-permute-start.12 = (bf16[64,1536]{1,0:T(8,128)(2,1)S(1)}, bf16[64,1536]{1,0:T(8,128)(2,1)S(1)}, u32[]{:S(2)}, u32[]{:S(2)}) collective-permute-start(bf16[64,1536]{1,0:T(8,128)(2,1)S(1)} %get-tuple-element.33), channel_id=1, source_target_pairs={{0,2},{1,17},{2,0},{3,19},{4,6},{5,21},{6,4},{7,23},{8,10},{9,25},... | collective-permute-start | bytes 589832 | tf_op jit(solution)/shard_map/ppermute | solution.py:45
  34.2 0.0 copy-start.2
  34.2 2.3 %shard_map.62 = (f32[512,512]{1,0:T(8,128)S(1)}, f32[8,128]{1,0:T(8,128)S(1)}) custom-call(s32[10]{0:T(128)S(1)} %stack.47.refs_0_.info, bf16[512,1536]{1,0:T(8,128)(2,1)S(1)} %copy-done.1, bf16[512,1536]{1,0:T(8,128)(2,1)S(1)} %collective-permute-done.3.refs_2_, bf16[3072,1536]{1,0:T(8,128)(2,1)S(1)} %copy-done, f32[8,128]{1,0:T(8,128)S(1)} %get-tuple-element.30.refs_4_), custom_call_target="tpu_custom_call" | custom-call | flops 1000 | bytes 1000 | tf_op jit(solution)/shard_map/pallas_call | solution.py:207
  36.5 0.4 collective-permute-done.8.refs_4_.refs_13_
  36.9 0.0 copy-done.2
  36.9 1.7 %shard_map.63.earlier = f32[512,128]{1,0:T(8,128)S(1)} custom-call(s32[10]{0:T(128)S(1)} %stack.47.refs_0_.info, s32[512,1]{1,0:T(8,128)S(1)} %copy.9.refs_4_.ids.refs_1_, bf16[512,1536]{1,0:T(8,128)(2,1)S(1)} %copy-done.1, bf16[64,1536]{1,0:T(8,128)(2,1)S(1)} %bitcast.17, bf16[64,1536]{1,0:T(8,128)(2,1)S(1)} %collective-permute-done.refs_3_.beside, ...), custom_call_target="tpu_custom_call" | custom-call | tf_op jit(solution)/shard_map/pallas_call | solution.py:304
  38.6 0.0 copy-start.3
  38.6 0.0 collective-permute-done.11.refs_1_.refs_16_
  38.6 0.0 collective-permute-done.10.refs_0_.refs_15_
  38.6 1.2 %collective-permute-done.12.refs_2_.refs_17_ = bf16[64,1536]{1,0:T(8,128)(2,1)S(1)} collective-permute-done((bf16[64,1536]{1,0:T(8,128)(2,1)S(1)}, bf16[64,1536]{1,0:T(8,128)(2,1)S(1)}, u32[]{:S(2)}, u32[]{:S(2)}) %collective-permute-start.12) | collective-permute-done | bytes 196640 | tf_op jit(solution)/shard_map/ppermute | solution.py:45
  39.8 0.6 %shard_map.64.refs_2_ = f32[512,128]{1,0:T(8,128)S(1)} custom-call(s32[10]{0:T(128)S(1)} %stack.47.refs_0_.info, s32[512,1]{1,0:T(8,128)S(1)} %copy.9.refs_4_.ids.refs_1_, bf16[512,1536]{1,0:T(8,128)(2,1)S(1)} %copy-done.1, f32[512,128]{1,0:T(8,128)S(1)} %shard_map.63.earlier, bf16[64,1536]{1,0:T(8,128)(2,1)S(1)} %collective-permute-done.10.refs_0_.refs_15_, ...), custom_call_target="tpu_custom_call" | custom-call | tf_op jit(solution)/shard_map/pallas_call | solution.py:311
  40.4 0.1 collective-permute-start.13
  40.5 1.5 %collective-permute-done.13.refs_3_ = f32[512,128]{1,0:T(8,128)S(1)} collective-permute-done((f32[512,128]{1,0:T(8,128)S(1)}, f32[512,128]{1,0:T(8,128)S(1)}, u32[]{:S(2)}, u32[]{:S(2)}) %collective-permute-start.13) | collective-permute-done | bytes 262176 | tf_op jit(solution)/shard_map/ppermute | solution.py:21
  42.0 0.0 copy-done.3
  42.0 2.7 %shard_map.65 = bf16[512,1536]{1,0:T(8,128)(2,1)} custom-call(s32[10]{0:T(128)S(1)} %stack.47.refs_0_.info, s32[512,1]{1,0:T(8,128)S(1)} %copy.9.refs_4_.ids.refs_1_, f32[512,128]{1,0:T(8,128)S(1)} %shard_map.64.refs_2_, f32[512,128]{1,0:T(8,128)S(1)} %collective-permute-done.13.refs_3_, f32[512,256]{1,0:T(8,128)S(1)} %get-tuple-element.34.refs_4_, ...), custom_call_target="tpu_custom_call" | custom-call | tf_op jit(solution)/shard_map/pallas_call | solution.py:331
  (5 shorter events, 0.1 us)
Async XLA Ops:
  0.0 8.1 %collective-permute-start.3 = (bf16[512,1536]{1,0:T(8,128)(2,1)}, bf16[512,1536]{1,0:T(8,128)(2,1)S(1)}, u32[]{:S(2)}, u32[]{:S(2)}) collective-permute-start(bf16[512,1536]{1,0:T(8,128)(2,1)} %latent.3), channel_id=1, source_target_pairs={{0,1},{1,0},{2,3},{3,2},{4,5},{5,4},{6,7},{7,6},{8,9},{9,8},{10,11... | collective-permute-start | bytes 4718600 | tf_op jit(solution)/shard_map/ppermute | solution.py:21
  1.5 13.2 %collective-permute-start.2 = (bf16[64,1536]{1,0:T(8,128)(2,1)S(1)}, bf16[64,1536]{1,0:T(8,128)(2,1)S(1)}, u32[]{:S(2)}, u32[]{:S(2)}) collective-permute-start(bf16[64,1536]{1,0:T(8,128)(2,1)S(1)} %broadcast_select_fusion), channel_id=1, source_target_pairs={{0,8},{2,10},{4,0},{6,2},{8,12},{10,14},{12,4},{14,6},{1,9},{3,11}... | collective-permute-start | bytes 589832 | tf_op jit(solution)/shard_map/ppermute | solution.py:35
  5.1 10.8 %collective-permute-start.1 = (bf16[64,1536]{1,0:T(8,128)(2,1)S(1)}, bf16[64,1536]{1,0:T(8,128)(2,1)S(1)}, u32[]{:S(2)}, u32[]{:S(2)}) collective-permute-start(bf16[64,1536]{1,0:T(8,128)(2,1)S(1)} %broadcast_select_fusion), channel_id=1, source_target_pairs={{0,4},{2,6},{4,12},{6,14},{8,0},{10,2},{12,8},{14,10},{1,5},{3,7},... | collective-permute-start | bytes 589832 | tf_op jit(solution)/shard_map/ppermute | solution.py:35
  5.1 10.8 %collective-permute-start = (bf16[64,1536]{1,0:T(8,128)(2,1)}, bf16[64,1536]{1,0:T(8,128)(2,1)S(1)}, u32[]{:S(2)}, u32[]{:S(2)}) collective-permute-start(bf16[64,1536]{1,0:T(8,128)(2,1)} %bitcast.16), channel_id=1, source_target_pairs={{0,2},{2,0},{4,6},{6,4},{8,10},{10,8},{12,14},{14,12},{1,3},{3,1},... | collective-permute-start | bytes 589832 | tf_op jit(solution)/shard_map/ppermute | solution.py:25
  6.7 9.9 %collective-permute-start.4 = (bf16[64,1536]{1,0:T(8,128)(2,1)}, bf16[64,1536]{1,0:T(8,128)(2,1)S(1)}, u32[]{:S(2)}, u32[]{:S(2)}) collective-permute-start(bf16[64,1536]{1,0:T(8,128)(2,1)} %bitcast.18), channel_id=1, source_target_pairs={{0,2},{2,0},{4,6},{6,4},{8,10},{10,8},{12,14},{14,12},{1,3},{3,1},... | collective-permute-start | bytes 589832 | tf_op jit(solution)/shard_map/ppermute | solution.py:25
  8.1 3.7 %copy-start = (bf16[3072,1536]{1,0:T(8,128)(2,1)S(1)}, bf16[3072,1536]{1,0:T(8,128)(2,1)}, u32[]{:S(2)}) copy-start(bf16[3072,1536]{1,0:T(8,128)(2,1)} %refs_3_.5) | copy-start | bytes 28311556
  11.8 1.4 %copy-start.1 = (bf16[512,1536]{1,0:T(8,128)(2,1)S(1)}, bf16[512,1536]{1,0:T(8,128)(2,1)}, u32[]{:S(2)}) copy-start(bf16[512,1536]{1,0:T(8,128)(2,1)} %latent.3) | copy-start | bytes 4718596
  16.6 12.1 %collective-permute-start.5 = (bf16[128,1536]{1,0:T(8,128)(2,1)S(1)}, bf16[128,1536]{1,0:T(8,128)(2,1)S(1)}, u32[]{:S(2)}, u32[]{:S(2)}) collective-permute-start(bf16[128,1536]{1,0:T(8,128)(2,1)S(1)} %get-tuple-element.22.refs_0_.refs_9_), channel_id=1, source_target_pairs={{0,2},{1,17},{2,0},{3,19},{4,6},{5,21},{6,4},{7,23},{8,10},{9,25},... | collective-permute-start | bytes 1179656 | tf_op jit(solution)/shard_map/ppermute | solution.py:45
  18.2 13.8 %collective-permute-start.6 = (bf16[128,1536]{1,0:T(8,128)(2,1)S(1)}, bf16[128,1536]{1,0:T(8,128)(2,1)S(1)}, u32[]{:S(2)}, u32[]{:S(2)}) collective-permute-start(bf16[128,1536]{1,0:T(8,128)(2,1)S(1)} %get-tuple-element.22.refs_0_.refs_9_), channel_id=1, source_target_pairs={{0,16},{1,3},{2,18},{3,1},{4,20},{5,7},{6,22},{7,5},{8,24},{9,11},... | collective-permute-start | bytes 1179656 | tf_op jit(solution)/shard_map/ppermute | solution.py:45
  19.7 6.6 %collective-permute-start.7 = (bf16[64,1536]{1,0:T(8,128)(2,1)S(1)}, bf16[64,1536]{1,0:T(8,128)(2,1)S(1)}, u32[]{:S(2)}, u32[]{:S(2)}) collective-permute-start(bf16[64,1536]{1,0:T(8,128)(2,1)S(1)} %collective-permute-done.1.refs_0_), channel_id=1, source_target_pairs={{0,4},{2,6},{4,12},{6,14},{8,0},{10,2},{12,8},{14,10},{1,5},{3,7},... | collective-permute-start | bytes 589832 | tf_op jit(solution)/shard_map/ppermute | solution.py:35
  26.3 7.3 %collective-permute-start.9 = (bf16[64,1536]{1,0:T(8,128)(2,1)S(1)}, bf16[64,1536]{1,0:T(8,128)(2,1)S(1)}, u32[]{:S(2)}, u32[]{:S(2)}) collective-permute-start(bf16[64,1536]{1,0:T(8,128)(2,1)S(1)} %get-tuple-element.25.refs_3_.refs_12_), channel_id=1, source_target_pairs={{0,16},{1,3},{2,18},{3,1},{4,20},{5,7},{6,22},{7,5},{8,24},{9,11},... | collective-permute-start | bytes 589832 | tf_op jit(solution)/shard_map/ppermute | solution.py:45
  28.7 9.9 %collective-permute-start.10 = (bf16[64,1536]{1,0:T(8,128)(2,1)S(1)}, bf16[64,1536]{1,0:T(8,128)(2,1)S(1)}, u32[]{:S(2)}, u32[]{:S(2)}) collective-permute-start(bf16[64,1536]{1,0:T(8,128)(2,1)S(1)} %get-tuple-element.27), channel_id=1, source_target_pairs={{0,16},{1,3},{2,18},{3,1},{4,20},{5,7},{6,22},{7,5},{8,24},{9,11},... | collective-permute-start | bytes 589832 | tf_op jit(solution)/shard_map/ppermute | solution.py:45
  30.3 6.6 %collective-permute-start.8 = (bf16[64,1536]{1,0:T(8,128)(2,1)S(1)}, bf16[64,1536]{1,0:T(8,128)(2,1)S(1)}, u32[]{:S(2)}, u32[]{:S(2)}) collective-permute-start(bf16[64,1536]{1,0:T(8,128)(2,1)S(1)} %get-tuple-element.27), channel_id=1, source_target_pairs={{0,4},{2,6},{4,12},{6,14},{8,0},{10,2},{12,8},{14,10},{1,5},{3,7},... | collective-permute-start | bytes 589832 | tf_op jit(solution)/shard_map/ppermute | solution.py:35
  32.0 6.6 %collective-permute-start.11 = (bf16[64,1536]{1,0:T(8,128)(2,1)S(1)}, bf16[64,1536]{1,0:T(8,128)(2,1)S(1)}, u32[]{:S(2)}, u32[]{:S(2)}) collective-permute-start(bf16[64,1536]{1,0:T(8,128)(2,1)S(1)} %get-tuple-element.32), channel_id=1, source_target_pairs={{0,2},{1,17},{2,0},{3,19},{4,6},{5,21},{6,4},{7,23},{8,10},{9,25},... | collective-permute-start | bytes 589832 | tf_op jit(solution)/shard_map/ppermute | solution.py:45
  33.6 6.2 %collective-permute-start.12 = (bf16[64,1536]{1,0:T(8,128)(2,1)S(1)}, bf16[64,1536]{1,0:T(8,128)(2,1)S(1)}, u32[]{:S(2)}, u32[]{:S(2)}) collective-permute-start(bf16[64,1536]{1,0:T(8,128)(2,1)S(1)} %get-tuple-element.33), channel_id=1, source_target_pairs={{0,2},{1,17},{2,0},{3,19},{4,6},{5,21},{6,4},{7,23},{8,10},{9,25},... | collective-permute-start | bytes 589832 | tf_op jit(solution)/shard_map/ppermute | solution.py:45
  34.2 2.7 %copy-start.2 = (bf16[1,1536,64]{1,2,0:T(8,128)(2,1)S(1)}, bf16[1,1536,64]{1,2,0:T(8,128)(2,1)}, u32[]{:S(2)}) copy-start(bf16[1,1536,64]{1,2,0:T(8,128)(2,1)} %param.8) | copy-start | bytes 589828
  38.6 3.5 %copy-start.3 = (bf16[1,64,1536]{2,1,0:T(8,128)(2,1)S(1)}, bf16[1,64,1536]{2,1,0:T(8,128)(2,1)}, u32[]{:S(2)}) copy-start(bf16[1,64,1536]{2,1,0:T(8,128)(2,1)} %param.9) | copy-start | bytes 589828
  40.4 1.6 %collective-permute-start.13 = (f32[512,128]{1,0:T(8,128)S(1)}, f32[512,128]{1,0:T(8,128)S(1)}, u32[]{:S(2)}, u32[]{:S(2)}) collective-permute-start(f32[512,128]{1,0:T(8,128)S(1)} %shard_map.64.refs_2_), channel_id=1, source_target_pairs={{0,1},{1,0},{2,3},{3,2},{4,5},{5,4},{6,7},{7,6},{8,9},{9,8},{10,11... | collective-permute-start | bytes 786440 | tf_op jit(solution)/shard_map/ppermute | solution.py:21

commit v12 on v11

--- a/solution.py
+++ b/solution.py
@@ -88,41 +88,26 @@
 
 
 def put(blocks, stack, top, rank):
-    for number, parts in enumerate(blocks):
+    for number, block in enumerate(blocks):
         place = top + 2 * number * rank
-        for ref, begin, rows in parts:
-            stack[place : place + rows, :] = ref[begin : begin + rows, :]
-            place += rows
+        stack[place : place + rank, :] = block[...]
 
 
 def fill_here(info, holds, received, stack, top, rank):
-    early, early_first, early_second, late, late_first, late_second, *_ = received
-
-    def blocks(pair, single):
-        return [[(pair, 0, rank)], [(pair, rank, rank)], [(single, 0, rank)]]
-
-    swapped = ((early_second, late_second), (early_first, late_first))
-    pl.when(holds)(lambda: put(blocks(early, late), stack, top, rank))
-    for core in range(2):
+    here, first, second = received[0:3], received[3:6], received[6:9]
+    pl.when(holds)(lambda: put(here, stack, top, rank))
+    for core, refs in enumerate((second, first)):
         away = jnp.logical_not(holds) & (info[0] == core)
-        pl.when(away)(lambda refs=swapped[core]: put(blocks(*refs), stack, top, rank))
+        pl.when(away)(lambda refs=refs: put(refs, stack, top, rank))
 
 
 def fill_beside(info, holds, received, stack, top, rank, direct=True, corner=True):
-    _, early_first, early_second, _, late_first, late_second, *corners = received
-    swapped = ((early_first, late_first), (early_second, late_second))
     if direct:
-        for core in range(2):
-
-            def straight(refs=swapped[core]):
-                pair, single = refs
-                blocks = [[(pair, 0, rank)], [(pair, rank, rank)], [(single, 0, rank)]]
-                put(blocks, stack, top, rank)
-
-            pl.when(holds & (info[0] == core))(straight)
+        for core, refs in enumerate((received[3:6], received[6:9])):
+            pl.when(holds & (info[0] == core))(lambda refs=refs: put(refs, stack, top, rank))
     if corner:
-        blocks = [[(ref, 0, rank)] for ref in corners]
-        pl.when(jnp.logical_not(holds))(lambda: put(blocks, stack, top, rank))
+        corners = received[9:12]
+        pl.when(jnp.logical_not(holds))(lambda: put(corners, stack, top, rank))
 
 
 def clear(stack, top, rank, count):
@@ -283,28 +268,31 @@
         parts = []
         part, token = base(info, latent, other, shared_weight, [ids], cuts[0], cuts[1])
         parts.append(part)
-        line[2] = along_line(line[1], shards, 1)
-        early, token = pack([(line[1], 0, rank), (line[3], 0, rank)], token, down_beside, up_beside)
+        one, token = pack([(line[1], 0, rank)], token, down_beside)
+        line[2] = along_line(one, shards, 1)
+        one_first, one_second = in_plane(one, shards, True), in_plane(one, shards, False)
+        three, token = pack([(line[3], 0, rank)], token, up_beside)
+        three_first, three_second = in_plane(three, shards, True), in_plane(three, shards, False)
         part, token = base(info, latent, other, shared_weight, [token], cuts[1], cuts[2])
         parts.append(part)
-        early_first, early_second = in_plane(early, shards, True), in_plane(early, shards, False)
-        late, token = pack([(line[2], 0, rank)], token)
-        late_second = in_plane(late, shards, False)
-        turn, token = pack([(early_first, 0, rank)], token)
+        two, token = pack([(line[2], 0, rank)], token)
+        two_second = in_plane(two, shards, False)
+        turn, token = pack([(one_first, 0, rank)], token, one_second)
         corner_one = in_plane(turn, shards, False)
-        late_first = along_line(turn, shards, 1)
-        turn, token = pack([(early_second, rank, rank)], token)
+        two_first = along_line(turn, shards, 1)
+        turn, token = pack([(three_second, 0, rank)], token, three_first)
+        corner_three = in_plane(turn, shards, True)
+        turn, token = pack([(two_second, 0, rank)], token)
         corner_two = in_plane(turn, shards, True)
-        turn, token = pack([(late_second, 0, rank)], token)
-        corner_three = in_plane(turn, shards, True)
         part, token = base(info, latent, other, shared_weight, [token], cuts[2], cuts[3])
         parts.append(part)
-        corners = [corner_one, corner_two, corner_three]
-        received = [early, early_first, early_second, late, late_first, late_second]
+        corners = [corner_one, corner_three, corner_two]
+        received = [one, three, two, one_first, three_first, two_first]
+        received += [one_second, three_second, two_second]
         mine = call(
             down_first_kernel,
             lowrank,
-            [SMEM] + [VMEM] * 10 + [ANY],
+            [SMEM] + [VMEM] * 13 + [ANY],
             16,
             [pltpu.VMEM((columns, half_width), latent.dtype)],
         )(info, ids, latent, down, down_beside, *received, token)

time: 45 us -> 43 us (0.956)
  waiting for transfers between devices: 8.56 us -> 4.04 us
  starting transfers between devices: 16.9 us -> 19.2 us
    ppermute x4, waiting for transfers between devices: 3.41 us -> 0.01 us  [along_line(): lax.ppermute(value, 'shard', [(i, ring_step(i, step)) for i in range(shar...]
    ppermute x4, starting transfers between devices: 6.95 us -> 8.46 us  [along_line(): lax.ppermute(value, 'shard', [(i, ring_step(i, step)) for i in range(shar...]
    ppermute x6 -> x8, starting transfers between devices: 7.43 us -> 8.49 us  [in_plane(): return lax.ppermute(value, AXES, pairs)]
    ppermute x2, waiting for transfers between devices: 0.61 us -> 0.01 us  [neighbour(): return lax.ppermute(value, 'shard', [(i, i ^ 1) for i in range(shards)])]
    ppermute x6 -> x8, waiting for transfers between devices: 3.02 us -> 2.5 us  [in_plane(): return lax.ppermute(value, AXES, pairs)]
  transfers between devices with their start and end apart: 14 -> 16, of which waited for: 7 -> 4; matrix products, arithmetic and copies ran while one was open for 4% -> 5% of each run, Pallas kernels for 20% -> 21%
where the time goes in v12:
time: 43 us; the launch traced here: 42.6 us
  starting transfers between devices  19.2 us (45%)
  Pallas kernels  12.1 us (28%)
  local copies, waits for them, and re-layouts  6 us (14%)
  waiting for transfers between devices  4.04 us (9%)
  other arithmetic  1.04 us (2%)
    ppermute x8, starting transfers between devices, in_plane(): return lax.ppermute(value, AXES, pairs)  8.49 us
    ppermute x4, starting transfers between devices, along_line(): lax.ppermute(value, 'shard', [(i, ring_step(i, step)) for i in range(shar...  8.46 us
    pallas_call x3, Pallas kernels, base(): pl.pallas_call(lambda *refs: base_kernel(*refs, skip=skip), out_shape=[ja...  7.01 us
    unnamed x9, local copies, waits for them, and re-layouts  5.91 us
    pallas_call x1, Pallas kernels, on_device(): pl.pallas_call(lambda *refs: up_kernel(*refs, base_parts=len(parts)), out...  2.74 us
    ppermute x8, waiting for transfers between devices, in_plane(): return lax.ppermute(value, AXES, pairs)  2.5 us
    ppermute x2, starting transfers between devices, neighbour(): return lax.ppermute(value, 'shard', [(i, i ^ 1) for i in range(shards)])  1.77 us
    pallas_call x1, Pallas kernels, on_device(): call(down_first_kernel, lowrank, [SMEM] + [VMEM] * 13 + [ANY], 16, [pltpu...  1.69 us
  transfers between devices with their start and end apart: 16, of which 4 were waited for; matrix products, arithmetic and copies ran while one was open for 5% of the time, Pallas kernels for 21%

profile of v12, /device:TPU:0, one launch (start us, length us, event | category | flops | bytes accessed | tf_op | source)
XLA Modules:
  0.0 42.6 jit_solution(12832844575627334894)
XLA Ops:
  0.0 0.5 %collective-permute-start.2 = (bf16[512,1536]{1,0:T(8,128)(2,1)}, bf16[512,1536]{1,0:T(8,128)(2,1)S(1)}, u32[]{:S(2)}, u32[]{:S(2)}) collective-permute-start(bf16[512,1536]{1,0:T(8,128)(2,1)} %latent.3), channel_id=1, source_target_pairs={{0,1},{1,0},{2,3},{3,2},{4,5},{5,4},{6,7},{7,6},{8,9},{9,8},{10,11... | collective-permute-start | bytes 4718600 | tf_op jit(solution)/shard_map/ppermute | solution.py:21
  0.5 1.0 %broadcast_select_fusion = bf16[64,1536]{1,0:T(8,128)(2,1)S(1)} fusion(pred[]{:T(512)S(6)} %eq.3, bf16[1,64,1536]{2,1,0:T(8,128)(2,1)} %param.9, bf16[1,1536,64]{1,2,0:T(8,128)(2,1)} %param.8), kind=kLoop, calls=%fused_computation | loop fusion | flops 98304 | bytes 589825 | tf_op jit(solution)/shard_map/jit(_where)/select_n | solution.py:264
  1.5 2.6 %collective-permute-start.1 = (bf16[64,1536]{1,0:T(8,128)(2,1)S(1)}, bf16[64,1536]{1,0:T(8,128)(2,1)S(1)}, u32[]{:S(2)}, u32[]{:S(2)}) collective-permute-start(bf16[64,1536]{1,0:T(8,128)(2,1)S(1)} %broadcast_select_fusion), channel_id=1, source_target_pairs={{0,4},{2,6},{4,12},{6,14},{8,0},{10,2},{12,8},{14,10},{1,5},{3,7},... | collective-permute-start | bytes 589832 | tf_op jit(solution)/shard_map/ppermute | solution.py:35
  4.1 1.5 %collective-permute-start = (bf16[64,1536]{1,0:T(8,128)(2,1)}, bf16[64,1536]{1,0:T(8,128)(2,1)S(1)}, u32[]{:S(2)}, u32[]{:S(2)}) collective-permute-start(bf16[64,1536]{1,0:T(8,128)(2,1)} %bitcast.16), channel_id=1, source_target_pairs={{0,2},{2,0},{4,6},{6,4},{8,10},{10,8},{12,14},{14,12},{1,3},{3,1},... | collective-permute-start | bytes 589832 | tf_op jit(solution)/shard_map/ppermute | solution.py:25
  5.6 1.3 %collective-permute-start.3 = (bf16[64,1536]{1,0:T(8,128)(2,1)S(1)}, bf16[64,1536]{1,0:T(8,128)(2,1)S(1)}, u32[]{:S(2)}, u32[]{:S(2)}) collective-permute-start(bf16[64,1536]{1,0:T(8,128)(2,1)S(1)} %broadcast_select_fusion), channel_id=1, source_target_pairs={{0,8},{2,10},{4,0},{6,2},{8,12},{10,14},{12,4},{14,6},{1,9},{3,11}... | collective-permute-start | bytes 589832 | tf_op jit(solution)/shard_map/ppermute | solution.py:35
  7.0 0.2 collective-permute-start.4
  7.2 0.8 %copy.9.refs_4_.ids.refs_1_ = s32[512,1]{1,0:T(8,128)S(1)} copy(s32[512,1]{0,1:T(1,128)} %param.6) | data formatting | bytes 4096 | tf_op args[1]
  8.1 0.1 stack.47.refs_0_.info
  8.2 0.0 collective-permute-done.2.refs_2_
  8.2 0.0 copy-start
  8.2 3.7 %copy-done = bf16[3072,1536]{1,0:T(8,128)(2,1)S(1)} copy-done((bf16[3072,1536]{1,0:T(8,128)(2,1)S(1)}, bf16[3072,1536]{1,0:T(8,128)(2,1)}, u32[]{:S(2)}) %copy-start) | copy-done | bytes 9437208
  11.9 0.0 copy-start.1
  11.9 1.4 %copy-done.1 = bf16[512,1536]{1,0:T(8,128)(2,1)S(1)} copy-done((bf16[512,1536]{1,0:T(8,128)(2,1)S(1)}, bf16[512,1536]{1,0:T(8,128)(2,1)}, u32[]{:S(2)}) %copy-start.1) | copy-done | bytes 1572888
  13.3 1.5 %shard_map.55 = (f32[512,256]{1,0:T(8,128)S(1)}, f32[8,128]{1,0:T(8,128)S(1)}) custom-call(s32[10]{0:T(128)S(1)} %stack.47.refs_0_.info, bf16[512,1536]{1,0:T(8,128)(2,1)S(1)} %copy-done.1, bf16[512,1536]{1,0:T(8,128)(2,1)S(1)} %collective-permute-done.2.refs_2_, bf16[3072,1536]{1,0:T(8,128)(2,1)S(1)} %copy-done, s32[512,1]{1,0:T(8,128)S(1)} %copy.9.refs_4_.ids.refs_1_), custom_call_target="tpu_custom_call" | custom-call | flops 1000 | bytes 1000 | tf_op jit(solution)/shard_map/pallas_call | solution.py:192
  14.8 0.0 collective-permute-done.1.refs_0_
  14.8 0.0 collective-permute-done.refs_2_.beside
  14.8 1.6 %collective-permute-start.5 = (bf16[64,1536]{1,0:T(8,128)(2,1)S(1)}, bf16[64,1536]{1,0:T(8,128)(2,1)S(1)}, u32[]{:S(2)}, u32[]{:S(2)}) collective-permute-start(bf16[64,1536]{1,0:T(8,128)(2,1)S(1)} %get-tuple-element.24.refs_0_.refs_9_), channel_id=1, source_target_pairs={{0,4},{2,6},{4,12},{6,14},{8,0},{10,2},{12,8},{14,10},{1,5},{3,7},... | collective-permute-start | bytes 589832 | tf_op jit(solution)/shard_map/ppermute | solution.py:35
  16.4 1.5 %collective-permute-start.8 = (bf16[64,1536]{1,0:T(8,128)(2,1)S(1)}, bf16[64,1536]{1,0:T(8,128)(2,1)S(1)}, u32[]{:S(2)}, u32[]{:S(2)}) collective-permute-start(bf16[64,1536]{1,0:T(8,128)(2,1)S(1)} %get-tuple-element.24.refs_0_.refs_9_), channel_id=1, source_target_pairs={{0,16},{1,3},{2,18},{3,1},{4,20},{5,7},{6,22},{7,5},{8,24},{9,11},... | collective-permute-start | bytes 589832 | tf_op jit(solution)/shard_map/ppermute | solution.py:45
  17.9 1.5 %collective-permute-start.6 = (bf16[64,1536]{1,0:T(8,128)(2,1)S(1)}, bf16[64,1536]{1,0:T(8,128)(2,1)S(1)}, u32[]{:S(2)}, u32[]{:S(2)}) collective-permute-start(bf16[64,1536]{1,0:T(8,128)(2,1)S(1)} %get-tuple-element.24.refs_0_.refs_9_), channel_id=1, source_target_pairs={{0,2},{1,17},{2,0},{3,19},{4,6},{5,21},{6,4},{7,23},{8,10},{9,25},... | collective-permute-start | bytes 589832 | tf_op jit(solution)/shard_map/ppermute | solution.py:45
  19.4 0.0 collective-permute-done.3.refs_0_
  19.4 0.0 collective-permute-done.4.refs_2_.refs_8_
  19.4 0.6 %collective-permute-start.10 = (bf16[64,1536]{1,0:T(8,128)(2,1)S(1)}, bf16[64,1536]{1,0:T(8,128)(2,1)S(1)}, u32[]{:S(2)}, u32[]{:S(2)}) collective-permute-start(bf16[64,1536]{1,0:T(8,128)(2,1)S(1)} %get-tuple-element.26.refs_1_.refs_10_), channel_id=1, source_target_pairs={{0,16},{1,3},{2,18},{3,1},{4,20},{5,7},{6,22},{7,5},{8,24},{9,11},... | collective-permute-start | bytes 589832 | tf_op jit(solution)/shard_map/ppermute | solution.py:45
  20.0 0.5 %collective-permute-start.7 = (bf16[64,1536]{1,0:T(8,128)(2,1)S(1)}, bf16[64,1536]{1,0:T(8,128)(2,1)S(1)}, u32[]{:S(2)}, u32[]{:S(2)}) collective-permute-start(bf16[64,1536]{1,0:T(8,128)(2,1)S(1)} %get-tuple-element.26.refs_1_.refs_10_), channel_id=1, source_target_pairs={{0,2},{1,17},{2,0},{3,19},{4,6},{5,21},{6,4},{7,23},{8,10},{9,25},... | collective-permute-start | bytes 589832 | tf_op jit(solution)/shard_map/ppermute | solution.py:45
  20.5 3.2 %shard_map.58 = (f32[512,768]{1,0:T(8,128)S(1)}, f32[8,128]{1,0:T(8,128)S(1)}) custom-call(s32[10]{0:T(128)S(1)} %stack.47.refs_0_.info, bf16[512,1536]{1,0:T(8,128)(2,1)S(1)} %copy-done.1, bf16[512,1536]{1,0:T(8,128)(2,1)S(1)} %collective-permute-done.2.refs_2_, bf16[3072,1536]{1,0:T(8,128)(2,1)S(1)} %copy-done, f32[8,128]{1,0:T(8,128)S(1)} %get-tuple-element.27.refs_4_), custom_call_target="tpu_custom_call" | custom-call | flops 1000 | bytes 1000 | tf_op jit(solution)/shard_map/pallas_call | solution.py:192
  23.7 0.0 collective-permute-done.5.refs_0_
  23.7 1.6 %collective-permute-start.11 = (bf16[64,1536]{1,0:T(8,128)(2,1)S(1)}, bf16[64,1536]{1,0:T(8,128)(2,1)S(1)}, u32[]{:S(2)}, u32[]{:S(2)}) collective-permute-start(bf16[64,1536]{1,0:T(8,128)(2,1)S(1)} %get-tuple-element.29.refs_2_.refs_11_), channel_id=1, source_target_pairs={{0,16},{1,3},{2,18},{3,1},{4,20},{5,7},{6,22},{7,5},{8,24},{9,11},... | collective-permute-start | bytes 589832 | tf_op jit(solution)/shard_map/ppermute | solution.py:45
  25.3 0.0 collective-permute-done.8.refs_2_.refs_6_.refs_15_
  25.3 0.3 collective-permute-done.6.refs_0_.refs_3_.refs_12_
  25.6 0.7 %collective-permute-start.12 = (bf16[64,1536]{1,0:T(8,128)(2,1)S(1)}, bf16[64,1536]{1,0:T(8,128)(2,1)S(1)}, u32[]{:S(2)}, u32[]{:S(2)}) collective-permute-start(bf16[64,1536]{1,0:T(8,128)(2,1)S(1)} %get-tuple-element.31), channel_id=1, source_target_pairs={{0,16},{1,3},{2,18},{3,1},{4,20},{5,7},{6,22},{7,5},{8,24},{9,11},... | collective-permute-start | bytes 589832 | tf_op jit(solution)/shard_map/ppermute | solution.py:45
  26.3 2.9 %collective-permute-start.9 = (bf16[64,1536]{1,0:T(8,128)(2,1)S(1)}, bf16[64,1536]{1,0:T(8,128)(2,1)S(1)}, u32[]{:S(2)}, u32[]{:S(2)}) collective-permute-start(bf16[64,1536]{1,0:T(8,128)(2,1)S(1)} %get-tuple-element.31), channel_id=1, source_target_pairs={{0,4},{2,6},{4,12},{6,14},{8,0},{10,2},{12,8},{14,10},{1,5},{3,7},... | collective-permute-start | bytes 589832 | tf_op jit(solution)/shard_map/ppermute | solution.py:35
  29.2 0.0 collective-permute-done.10.refs_0_.refs_7_.refs_16_
  29.2 0.6 %collective-permute-done.7.refs_2_.refs_4_.refs_13_ = bf16[64,1536]{1,0:T(8,128)(2,1)S(1)} collective-permute-done((bf16[64,1536]{1,0:T(8,128)(2,1)S(1)}, bf16[64,1536]{1,0:T(8,128)(2,1)S(1)}, u32[]{:S(2)}, u32[]{:S(2)}) %collective-permute-start.7) | collective-permute-done | bytes 196640 | tf_op jit(solution)/shard_map/ppermute | solution.py:45
  29.8 1.0 %collective-permute-start.13 = (bf16[64,1536]{1,0:T(8,128)(2,1)S(1)}, bf16[64,1536]{1,0:T(8,128)(2,1)S(1)}, u32[]{:S(2)}, u32[]{:S(2)}) collective-permute-start(bf16[64,1536]{1,0:T(8,128)(2,1)S(1)} %get-tuple-element.36), channel_id=1, source_target_pairs={{0,2},{1,17},{2,0},{3,19},{4,6},{5,21},{6,4},{7,23},{8,10},{9,25},... | collective-permute-start | bytes 589832 | tf_op jit(solution)/shard_map/ppermute | solution.py:45
  30.8 0.0 collective-permute-done.11.refs_0_.refs_8_.refs_17_
  30.8 1.2 %collective-permute-start.14 = (bf16[64,1536]{1,0:T(8,128)(2,1)S(1)}, bf16[64,1536]{1,0:T(8,128)(2,1)S(1)}, u32[]{:S(2)}, u32[]{:S(2)}) collective-permute-start(bf16[64,1536]{1,0:T(8,128)(2,1)S(1)} %get-tuple-element.37), channel_id=1, source_target_pairs={{0,2},{1,17},{2,0},{3,19},{4,6},{5,21},{6,4},{7,23},{8,10},{9,25},... | collective-permute-start | bytes 589832 | tf_op jit(solution)/shard_map/ppermute | solution.py:45
  32.0 2.3 %shard_map.63 = (f32[512,512]{1,0:T(8,128)S(1)}, f32[8,128]{1,0:T(8,128)S(1)}) custom-call(s32[10]{0:T(128)S(1)} %stack.47.refs_0_.info, bf16[512,1536]{1,0:T(8,128)(2,1)S(1)} %copy-done.1, bf16[512,1536]{1,0:T(8,128)(2,1)S(1)} %collective-permute-done.2.refs_2_, bf16[3072,1536]{1,0:T(8,128)(2,1)S(1)} %copy-done, f32[8,128]{1,0:T(8,128)S(1)} %get-tuple-element.34.refs_4_), custom_call_target="tpu_custom_call" | custom-call | flops 1000 | bytes 1000 | tf_op jit(solution)/shard_map/pallas_call | solution.py:192
  34.3 0.0 collective-permute-done.9.refs_5_.refs_14_
  34.3 0.0 copy-done.2
  34.4 1.7 %shard_map.64.earlier = f32[512,128]{1,0:T(8,128)S(1)} custom-call(s32[10]{0:T(128)S(1)} %stack.47.refs_0_.info, s32[512,1]{1,0:T(8,128)S(1)} %copy.9.refs_4_.ids.refs_1_, bf16[512,1536]{1,0:T(8,128)(2,1)S(1)} %copy-done.1, bf16[64,1536]{1,0:T(8,128)(2,1)S(1)} %bitcast.17, bf16[64,1536]{1,0:T(8,128)(2,1)S(1)} %collective-permute-done.refs_2_.beside, ...), custom_call_target="tpu_custom_call" | custom-call | tf_op jit(solution)/shard_map/pallas_call | solution.py:292
  36.0 0.0 copy-start.3
  36.1 0.0 collective-permute-done.13.refs_1_.refs_19_
  36.1 0.0 collective-permute-done.12.refs_0_.refs_18_
  36.1 1.6 %collective-permute-done.14.refs_2_.refs_20_ = bf16[64,1536]{1,0:T(8,128)(2,1)S(1)} collective-permute-done((bf16[64,1536]{1,0:T(8,128)(2,1)S(1)}, bf16[64,1536]{1,0:T(8,128)(2,1)S(1)}, u32[]{:S(2)}, u32[]{:S(2)}) %collective-permute-start.14) | collective-permute-done | bytes 196640 | tf_op jit(solution)/shard_map/ppermute | solution.py:45
  37.7 0.6 %shard_map.65.refs_2_ = f32[512,128]{1,0:T(8,128)S(1)} custom-call(s32[10]{0:T(128)S(1)} %stack.47.refs_0_.info, s32[512,1]{1,0:T(8,128)S(1)} %copy.9.refs_4_.ids.refs_1_, bf16[512,1536]{1,0:T(8,128)(2,1)S(1)} %copy-done.1, f32[512,128]{1,0:T(8,128)S(1)} %shard_map.64.earlier, bf16[64,1536]{1,0:T(8,128)(2,1)S(1)} %collective-permute-done.12.refs_0_.refs_18_, ...), custom_call_target="tpu_custom_call" | custom-call | tf_op jit(solution)/shard_map/pallas_call | solution.py:299
  38.2 0.1 collective-permute-start.15
  38.3 1.5 %collective-permute-done.15.refs_3_ = f32[512,128]{1,0:T(8,128)S(1)} collective-permute-done((f32[512,128]{1,0:T(8,128)S(1)}, f32[512,128]{1,0:T(8,128)S(1)}, u32[]{:S(2)}, u32[]{:S(2)}) %collective-permute-start.15) | collective-permute-done | bytes 262176 | tf_op jit(solution)/shard_map/ppermute | solution.py:21
  39.8 0.0 copy-done.3
  39.8 2.7 %shard_map.66 = bf16[512,1536]{1,0:T(8,128)(2,1)} custom-call(s32[10]{0:T(128)S(1)} %stack.47.refs_0_.info, s32[512,1]{1,0:T(8,128)S(1)} %copy.9.refs_4_.ids.refs_1_, f32[512,128]{1,0:T(8,128)S(1)} %shard_map.65.refs_2_, f32[512,128]{1,0:T(8,128)S(1)} %collective-permute-done.15.refs_3_, f32[512,256]{1,0:T(8,128)S(1)} %get-tuple-element.38.refs_4_, ...), custom_call_target="tpu_custom_call" | custom-call | tf_op jit(solution)/shard_map/pallas_call | solution.py:319
  (7 shorter events, 0.1 us)
Async XLA Ops:
  0.0 8.2 %collective-permute-start.2 = (bf16[512,1536]{1,0:T(8,128)(2,1)}, bf16[512,1536]{1,0:T(8,128)(2,1)S(1)}, u32[]{:S(2)}, u32[]{:S(2)}) collective-permute-start(bf16[512,1536]{1,0:T(8,128)(2,1)} %latent.3), channel_id=1, source_target_pairs={{0,1},{1,0},{2,3},{3,2},{4,5},{5,4},{6,7},{7,6},{8,9},{9,8},{10,11... | collective-permute-start | bytes 4718600 | tf_op jit(solution)/shard_map/ppermute | solution.py:21
  1.5 13.3 %collective-permute-start.1 = (bf16[64,1536]{1,0:T(8,128)(2,1)S(1)}, bf16[64,1536]{1,0:T(8,128)(2,1)S(1)}, u32[]{:S(2)}, u32[]{:S(2)}) collective-permute-start(bf16[64,1536]{1,0:T(8,128)(2,1)S(1)} %broadcast_select_fusion), channel_id=1, source_target_pairs={{0,4},{2,6},{4,12},{6,14},{8,0},{10,2},{12,8},{14,10},{1,5},{3,7},... | collective-permute-start | bytes 589832 | tf_op jit(solution)/shard_map/ppermute | solution.py:35
  4.1 10.7 %collective-permute-start = (bf16[64,1536]{1,0:T(8,128)(2,1)}, bf16[64,1536]{1,0:T(8,128)(2,1)S(1)}, u32[]{:S(2)}, u32[]{:S(2)}) collective-permute-start(bf16[64,1536]{1,0:T(8,128)(2,1)} %bitcast.16), channel_id=1, source_target_pairs={{0,2},{2,0},{4,6},{6,4},{8,10},{10,8},{12,14},{14,12},{1,3},{3,1},... | collective-permute-start | bytes 589832 | tf_op jit(solution)/shard_map/ppermute | solution.py:25
  5.6 13.8 %collective-permute-start.3 = (bf16[64,1536]{1,0:T(8,128)(2,1)S(1)}, bf16[64,1536]{1,0:T(8,128)(2,1)S(1)}, u32[]{:S(2)}, u32[]{:S(2)}) collective-permute-start(bf16[64,1536]{1,0:T(8,128)(2,1)S(1)} %broadcast_select_fusion), channel_id=1, source_target_pairs={{0,8},{2,10},{4,0},{6,2},{8,12},{10,14},{12,4},{14,6},{1,9},{3,11}... | collective-permute-start | bytes 589832 | tf_op jit(solution)/shard_map/ppermute | solution.py:35
  7.0 12.4 %collective-permute-start.4 = (bf16[64,1536]{1,0:T(8,128)(2,1)}, bf16[64,1536]{1,0:T(8,128)(2,1)S(1)}, u32[]{:S(2)}, u32[]{:S(2)}) collective-permute-start(bf16[64,1536]{1,0:T(8,128)(2,1)} %bitcast.18), channel_id=1, source_target_pairs={{0,2},{2,0},{4,6},{6,4},{8,10},{10,8},{12,14},{14,12},{1,3},{3,1},... | collective-permute-start | bytes 589832 | tf_op jit(solution)/shard_map/ppermute | solution.py:25
  8.2 3.7 %copy-start = (bf16[3072,1536]{1,0:T(8,128)(2,1)S(1)}, bf16[3072,1536]{1,0:T(8,128)(2,1)}, u32[]{:S(2)}) copy-start(bf16[3072,1536]{1,0:T(8,128)(2,1)} %refs_3_.5) | copy-start | bytes 28311556
  11.9 1.4 %copy-start.1 = (bf16[512,1536]{1,0:T(8,128)(2,1)S(1)}, bf16[512,1536]{1,0:T(8,128)(2,1)}, u32[]{:S(2)}) copy-start(bf16[512,1536]{1,0:T(8,128)(2,1)} %latent.3) | copy-start | bytes 4718596
  14.8 8.9 %collective-permute-start.5 = (bf16[64,1536]{1,0:T(8,128)(2,1)S(1)}, bf16[64,1536]{1,0:T(8,128)(2,1)S(1)}, u32[]{:S(2)}, u32[]{:S(2)}) collective-permute-start(bf16[64,1536]{1,0:T(8,128)(2,1)S(1)} %get-tuple-element.24.refs_0_.refs_9_), channel_id=1, source_target_pairs={{0,4},{2,6},{4,12},{6,14},{8,0},{10,2},{12,8},{14,10},{1,5},{3,7},... | collective-permute-start | bytes 589832 | tf_op jit(solution)/shard_map/ppermute | solution.py:35
  16.4 8.9 %collective-permute-start.8 = (bf16[64,1536]{1,0:T(8,128)(2,1)S(1)}, bf16[64,1536]{1,0:T(8,128)(2,1)S(1)}, u32[]{:S(2)}, u32[]{:S(2)}) collective-permute-start(bf16[64,1536]{1,0:T(8,128)(2,1)S(1)} %get-tuple-element.24.refs_0_.refs_9_), channel_id=1, source_target_pairs={{0,16},{1,3},{2,18},{3,1},{4,20},{5,7},{6,22},{7,5},{8,24},{9,11},... | collective-permute-start | bytes 589832 | tf_op jit(solution)/shard_map/ppermute | solution.py:45
  17.9 7.7 %collective-permute-start.6 = (bf16[64,1536]{1,0:T(8,128)(2,1)S(1)}, bf16[64,1536]{1,0:T(8,128)(2,1)S(1)}, u32[]{:S(2)}, u32[]{:S(2)}) collective-permute-start(bf16[64,1536]{1,0:T(8,128)(2,1)S(1)} %get-tuple-element.24.refs_0_.refs_9_), channel_id=1, source_target_pairs={{0,2},{1,17},{2,0},{3,19},{4,6},{5,21},{6,4},{7,23},{8,10},{9,25},... | collective-permute-start | bytes 589832 | tf_op jit(solution)/shard_map/ppermute | solution.py:45
  19.4 9.8 %collective-permute-start.10 = (bf16[64,1536]{1,0:T(8,128)(2,1)S(1)}, bf16[64,1536]{1,0:T(8,128)(2,1)S(1)}, u32[]{:S(2)}, u32[]{:S(2)}) collective-permute-start(bf16[64,1536]{1,0:T(8,128)(2,1)S(1)} %get-tuple-element.26.refs_1_.refs_10_), channel_id=1, source_target_pairs={{0,16},{1,3},{2,18},{3,1},{4,20},{5,7},{6,22},{7,5},{8,24},{9,11},... | collective-permute-start | bytes 589832 | tf_op jit(solution)/shard_map/ppermute | solution.py:45
  20.0 9.8 %collective-permute-start.7 = (bf16[64,1536]{1,0:T(8,128)(2,1)S(1)}, bf16[64,1536]{1,0:T(8,128)(2,1)S(1)}, u32[]{:S(2)}, u32[]{:S(2)}) collective-permute-start(bf16[64,1536]{1,0:T(8,128)(2,1)S(1)} %get-tuple-element.26.refs_1_.refs_10_), channel_id=1, source_target_pairs={{0,2},{1,17},{2,0},{3,19},{4,6},{5,21},{6,4},{7,23},{8,10},{9,25},... | collective-permute-start | bytes 589832 | tf_op jit(solution)/shard_map/ppermute | solution.py:45
  23.7 7.1 %collective-permute-start.11 = (bf16[64,1536]{1,0:T(8,128)(2,1)S(1)}, bf16[64,1536]{1,0:T(8,128)(2,1)S(1)}, u32[]{:S(2)}, u32[]{:S(2)}) collective-permute-start(bf16[64,1536]{1,0:T(8,128)(2,1)S(1)} %get-tuple-element.29.refs_2_.refs_11_), channel_id=1, source_target_pairs={{0,16},{1,3},{2,18},{3,1},{4,20},{5,7},{6,22},{7,5},{8,24},{9,11},... | collective-permute-start | bytes 589832 | tf_op jit(solution)/shard_map/ppermute | solution.py:45
  25.6 10.5 %collective-permute-start.12 = (bf16[64,1536]{1,0:T(8,128)(2,1)S(1)}, bf16[64,1536]{1,0:T(8,128)(2,1)S(1)}, u32[]{:S(2)}, u32[]{:S(2)}) collective-permute-start(bf16[64,1536]{1,0:T(8,128)(2,1)S(1)} %get-tuple-element.31), channel_id=1, source_target_pairs={{0,16},{1,3},{2,18},{3,1},{4,20},{5,7},{6,22},{7,5},{8,24},{9,11},... | collective-permute-start | bytes 589832 | tf_op jit(solution)/shard_map/ppermute | solution.py:45
  26.3 8.1 %collective-permute-start.9 = (bf16[64,1536]{1,0:T(8,128)(2,1)S(1)}, bf16[64,1536]{1,0:T(8,128)(2,1)S(1)}, u32[]{:S(2)}, u32[]{:S(2)}) collective-permute-start(bf16[64,1536]{1,0:T(8,128)(2,1)S(1)} %get-tuple-element.31), channel_id=1, source_target_pairs={{0,4},{2,6},{4,12},{6,14},{8,0},{10,2},{12,8},{14,10},{1,5},{3,7},... | collective-permute-start | bytes 589832 | tf_op jit(solution)/shard_map/ppermute | solution.py:35
  29.8 6.2 %collective-permute-start.13 = (bf16[64,1536]{1,0:T(8,128)(2,1)S(1)}, bf16[64,1536]{1,0:T(8,128)(2,1)S(1)}, u32[]{:S(2)}, u32[]{:S(2)}) collective-permute-start(bf16[64,1536]{1,0:T(8,128)(2,1)S(1)} %get-tuple-element.36), channel_id=1, source_target_pairs={{0,2},{1,17},{2,0},{3,19},{4,6},{5,21},{6,4},{7,23},{8,10},{9,25},... | collective-permute-start | bytes 589832 | tf_op jit(solution)/shard_map/ppermute | solution.py:45
  30.8 6.8 %collective-permute-start.14 = (bf16[64,1536]{1,0:T(8,128)(2,1)S(1)}, bf16[64,1536]{1,0:T(8,128)(2,1)S(1)}, u32[]{:S(2)}, u32[]{:S(2)}) collective-permute-start(bf16[64,1536]{1,0:T(8,128)(2,1)S(1)} %get-tuple-element.37), channel_id=1, source_target_pairs={{0,2},{1,17},{2,0},{3,19},{4,6},{5,21},{6,4},{7,23},{8,10},{9,25},... | collective-permute-start | bytes 589832 | tf_op jit(solution)/shard_map/ppermute | solution.py:45
  32.0 2.3 %copy-start.2 = (bf16[1,1536,64]{1,2,0:T(8,128)(2,1)S(1)}, bf16[1,1536,64]{1,2,0:T(8,128)(2,1)}, u32[]{:S(2)}) copy-start(bf16[1,1536,64]{1,2,0:T(8,128)(2,1)} %param.8) | copy-start | bytes 589828
  36.0 3.8 %copy-start.3 = (bf16[1,64,1536]{2,1,0:T(8,128)(2,1)S(1)}, bf16[1,64,1536]{2,1,0:T(8,128)(2,1)}, u32[]{:S(2)}) copy-start(bf16[1,64,1536]{2,1,0:T(8,128)(2,1)} %param.9) | copy-start | bytes 589828
  38.2 1.6 %collective-permute-start.15 = (f32[512,128]{1,0:T(8,128)S(1)}, f32[512,128]{1,0:T(8,128)S(1)}, u32[]{:S(2)}, u32[]{:S(2)}) collective-permute-start(f32[512,128]{1,0:T(8,128)S(1)} %shard_map.65.refs_2_), channel_id=1, source_target_pairs={{0,1},{1,0},{2,3},{3,2},{4,5},{5,4},{6,7},{7,6},{8,9},{9,8},{10,11... | collective-permute-start | bytes 786440 | tf_op jit(solution)/shard_map/ppermute | solution.py:21

commit v13 on v12

--- a/solution.py
+++ b/solution.py
@@ -266,11 +266,11 @@
         other = swap(latent, "tensor")
         down_beside, up_beside = neighbour(down, shards), neighbour(up, shards)
         parts = []
-        part, token = base(info, latent, other, shared_weight, [ids], cuts[0], cuts[1])
-        parts.append(part)
-        one, token = pack([(line[1], 0, rank)], token, down_beside)
+        one, token = pack([(line[1], 0, rank)], ids, info, down_beside)
         line[2] = along_line(one, shards, 1)
         one_first, one_second = in_plane(one, shards, True), in_plane(one, shards, False)
+        part, token = base(info, latent, other, shared_weight, [token], cuts[0], cuts[1])
+        parts.append(part)
         three, token = pack([(line[3], 0, rank)], token, up_beside)
         three_first, three_second = in_plane(three, shards, True), in_plane(three, shards, False)
         part, token = base(info, latent, other, shared_weight, [token], cuts[1], cuts[2])

time: 43 us -> 52.8 us (1.23)
  the two profiles are of different devices: /device:TPU:0 before, /device:TPU:11 now
where the time goes in v13:
time: 52.8 us; the launch traced here: 52.5 us
  starting transfers between devices  17.5 us (33%)
  Pallas kernels  15.4 us (29%)
  waiting for transfers between devices  13.2 us (25%)
  local copies, waits for them, and re-layouts  4.61 us (9%)
  other arithmetic  1.72 us (3%)
    pallas_call x3, Pallas kernels, base(): pl.pallas_call(lambda *refs: base_kernel(*refs, skip=skip), out_shape=[ja...  7.02 us
    ppermute x4, waiting for transfers between devices, along_line(): lax.ppermute(value, 'shard', [(i, ring_step(i, step)) for i in range(shar...  6.21 us
    ppermute x8, waiting for transfers between devices, in_plane(): return lax.ppermute(value, AXES, pairs)  5.81 us
    ppermute x4, starting transfers between devices, along_line(): lax.ppermute(value, 'shard', [(i, ring_step(i, step)) for i in range(shar...  5.68 us
    ppermute x8, starting transfers between devices, in_plane(): return lax.ppermute(value, AXES, pairs)  5.33 us
    ppermute x2, starting transfers between devices, swap(): return lax.ppermute(value, axis, [(0, 1), (1, 0)])  5.01 us
    unnamed x11, local copies, waits for them, and re-layouts  4.52 us
    pallas_call x1, Pallas kernels, on_device(): pl.pallas_call(lambda *refs: up_kernel(*refs, base_parts=len(parts)), out...  3.13 us
  transfers between devices with their start and end apart: 16, of which 4 were waited for; matrix products, arithmetic and copies ran while one was open for 5% of the time, Pallas kernels for 22%

profile of v13, /device:TPU:11, one launch (start us, length us, event | category | flops | bytes accessed | tf_op | source)
XLA Modules:
  0.0 52.5 jit_solution(3825004684509640091)
XLA Ops:
  0.0 0.7 %collective-permute-start.3 = (bf16[512,1536]{1,0:T(8,128)(2,1)}, bf16[512,1536]{1,0:T(8,128)(2,1)S(1)}, u32[]{:S(2)}, u32[]{:S(2)}) collective-permute-start(bf16[512,1536]{1,0:T(8,128)(2,1)} %latent.3), channel_id=1, source_target_pairs={{0,1},{1,0},{2,3},{3,2},{4,5},{5,4},{6,7},{7,6},{8,9},{9,8},{10,11... | collective-permute-start | bytes 4718600 | tf_op jit(solution)/shard_map/ppermute | solution.py:21
  0.7 1.7 %broadcast_select_fusion = bf16[64,1536]{1,0:T(8,128)(2,1)} fusion(pred[]{:T(512)S(6)} %eq.3, bf16[1,64,1536]{2,1,0:T(8,128)(2,1)} %param.9, bf16[1,1536,64]{1,2,0:T(8,128)(2,1)} %param.8), kind=kLoop, calls=%fused_computation | loop fusion | flops 98304 | bytes 589825 | tf_op jit(solution)/shard_map/jit(_where)/select_n | solution.py:264
  2.4 2.3 %collective-permute-start.1 = (bf16[64,1536]{1,0:T(8,128)(2,1)}, bf16[64,1536]{1,0:T(8,128)(2,1)}, u32[]{:S(2)}, u32[]{:S(2)}) collective-permute-start(bf16[64,1536]{1,0:T(8,128)(2,1)} %broadcast_select_fusion), channel_id=1, source_target_pairs={{0,4},{2,6},{4,12},{6,14},{8,0},{10,2},{12,8},{14,10},{1,5},{3,7},... | collective-permute-start | bytes 589832 | tf_op jit(solution)/shard_map/ppermute | solution.py:35
  4.7 1.2 %collective-permute-start = (bf16[64,1536]{1,0:T(8,128)(2,1)}, bf16[64,1536]{1,0:T(8,128)(2,1)}, u32[]{:S(2)}, u32[]{:S(2)}) collective-permute-start(bf16[64,1536]{1,0:T(8,128)(2,1)} %bitcast.16), channel_id=1, source_target_pairs={{0,2},{2,0},{4,6},{6,4},{8,10},{10,8},{12,14},{14,12},{1,3},{3,1},... | collective-permute-start | bytes 589832 | tf_op jit(solution)/shard_map/ppermute | solution.py:25
  5.9 0.0 collective-permute-start.2
  6.0 0.2 collective-permute-start.4
  6.2 0.8 %copy.9.refs_1_.ids = s32[512,1]{1,0:T(8,128)S(1)} copy(s32[512,1]{0,1:T(1,128)} %param.6) | data formatting | bytes 4096 | tf_op args[1]
  7.0 0.1 stack.47.refs_2_.refs_0_.info
  7.1 6.2 %collective-permute-done.1.refs_0_ = bf16[64,1536]{1,0:T(8,128)(2,1)} collective-permute-done((bf16[64,1536]{1,0:T(8,128)(2,1)}, bf16[64,1536]{1,0:T(8,128)(2,1)}, u32[]{:S(2)}, u32[]{:S(2)}) %collective-permute-start.1) | collective-permute-done | bytes 196640 | tf_op jit(solution)/shard_map/ppermute | solution.py:35
  13.3 0.0 collective-permute-done.refs_3_.beside
  13.3 0.9 %shard_map.55 = (bf16[64,1536]{1,0:T(8,128)(2,1)S(1)}, f32[8,128]{1,0:T(8,128)S(1)}) custom-call(bf16[64,1536]{1,0:T(8,128)(2,1)} %collective-permute-done.1.refs_0_, s32[512,1]{1,0:T(8,128)S(1)} %copy.9.refs_1_.ids, s32[10]{0:T(128)S(1)} %stack.47.refs_2_.refs_0_.info, bf16[64,1536]{1,0:T(8,128)(2,1)} %collective-permute-done.refs_3_.beside), custom_call_target="tpu_custom_call" | custom-call | tf_op jit(solution)/shard_map/pallas_call | solution.py:82
  14.3 3.3 %collective-permute-start.5 = (bf16[64,1536]{1,0:T(8,128)(2,1)S(1)}, bf16[64,1536]{1,0:T(8,128)(2,1)S(1)}, u32[]{:S(2)}, u32[]{:S(2)}) collective-permute-start(bf16[64,1536]{1,0:T(8,128)(2,1)S(1)} %get-tuple-element.23.refs_0_.refs_9_), channel_id=1, source_target_pairs={{0,4},{2,6},{4,12},{6,14},{8,0},{10,2},{12,8},{14,10},{1,5},{3,7},... | collective-permute-start | bytes 589832 | tf_op jit(solution)/shard_map/ppermute | solution.py:35
  17.5 1.2 %collective-permute-start.8 = (bf16[64,1536]{1,0:T(8,128)(2,1)S(1)}, bf16[64,1536]{1,0:T(8,128)(2,1)S(1)}, u32[]{:S(2)}, u32[]{:S(2)}) collective-permute-start(bf16[64,1536]{1,0:T(8,128)(2,1)S(1)} %get-tuple-element.23.refs_0_.refs_9_), channel_id=1, source_target_pairs={{0,16},{1,3},{2,18},{3,1},{4,20},{5,7},{6,22},{7,5},{8,24},{9,11},... | collective-permute-start | bytes 589832 | tf_op jit(solution)/shard_map/ppermute | solution.py:45
  18.8 0.0 collective-permute-done.3.refs_2_
  18.8 0.3 collective-permute-start.6
  19.0 0.0 copy-done.2
  19.1 3.7 %copy-done = bf16[3072,1536]{1,0:T(8,128)(2,1)S(1)} copy-done((bf16[3072,1536]{1,0:T(8,128)(2,1)S(1)}, bf16[3072,1536]{1,0:T(8,128)(2,1)}, u32[]{:S(2)}) %copy-start) | copy-done | bytes 9437208
  22.7 1.5 %shard_map.56 = (f32[512,256]{1,0:T(8,128)S(1)}, f32[8,128]{1,0:T(8,128)S(1)}) custom-call(s32[10]{0:T(128)S(1)} %stack.47.refs_2_.refs_0_.info, bf16[512,1536]{1,0:T(8,128)(2,1)S(1)} %copy-done.2, bf16[512,1536]{1,0:T(8,128)(2,1)S(1)} %collective-permute-done.3.refs_2_, bf16[3072,1536]{1,0:T(8,128)(2,1)S(1)} %copy-done, f32[8,128]{1,0:T(8,128)S(1)} %get-tuple-element.24.refs_4_), custom_call_target="tpu_custom_call" | custom-call | flops 1000 | bytes 1000 | tf_op jit(solution)/shard_map/pallas_call | solution.py:192
  24.3 0.0 collective-permute-done.2.refs_0_
  24.3 0.0 collective-permute-done.4.refs_2_.refs_8_
  24.3 1.6 %shard_map.57 = (bf16[64,1536]{1,0:T(8,128)(2,1)S(1)}, f32[8,128]{1,0:T(8,128)S(1)}) custom-call(bf16[64,1536]{1,0:T(8,128)(2,1)} %collective-permute-done.2.refs_0_, f32[8,128]{1,0:T(8,128)S(1)} %get-tuple-element.25.refs_1_, bf16[64,1536]{1,0:T(8,128)(2,1)} %collective-permute-done.4.refs_2_.refs_8_), custom_call_target="tpu_custom_call" | custom-call | tf_op jit(solution)/shard_map/pallas_call | solution.py:82
  25.9 0.3 collective-permute-start.10
  26.2 1.2 %collective-permute-start.7 = (bf16[64,1536]{1,0:T(8,128)(2,1)S(1)}, bf16[64,1536]{1,0:T(8,128)(2,1)S(1)}, u32[]{:S(2)}, u32[]{:S(2)}) collective-permute-start(bf16[64,1536]{1,0:T(8,128)(2,1)S(1)} %get-tuple-element.26.refs_1_.refs_10_), channel_id=1, source_target_pairs={{0,2},{1,17},{2,0},{3,19},{4,6},{5,21},{6,4},{7,23},{8,10},{9,25},... | collective-permute-start | bytes 589832 | tf_op jit(solution)/shard_map/ppermute | solution.py:45
  27.4 0.0 copy-done.1
  27.4 3.2 %shard_map.58 = (f32[512,768]{1,0:T(8,128)S(1)}, f32[8,128]{1,0:T(8,128)S(1)}) custom-call(s32[10]{0:T(128)S(1)} %stack.47.refs_2_.refs_0_.info, bf16[512,1536]{1,0:T(8,128)(2,1)S(1)} %copy-done.2, bf16[512,1536]{1,0:T(8,128)(2,1)S(1)} %collective-permute-done.3.refs_2_, bf16[3072,1536]{1,0:T(8,128)(2,1)S(1)} %copy-done.1, ...), custom_call_target="tpu_custom_call" | custom-call | flops 1000 | bytes 1000 | tf_op jit(solution)/shard_map/pallas_call | solution.py:192
  30.5 0.0 collective-permute-done.5.refs_0_
  30.6 1.3 %collective-permute-start.11 = (bf16[64,1536]{1,0:T(8,128)(2,1)S(1)}, bf16[64,1536]{1,0:T(8,128)(2,1)S(1)}, u32[]{:S(2)}, u32[]{:S(2)}) collective-permute-start(bf16[64,1536]{1,0:T(8,128)(2,1)S(1)} %get-tuple-element.29.refs_2_.refs_11_), channel_id=1, source_target_pairs={{0,16},{1,3},{2,18},{3,1},{4,20},{5,7},{6,22},{7,5},{8,24},{9,11},... | collective-permute-start | bytes 589832 | tf_op jit(solution)/shard_map/ppermute | solution.py:45
  31.9 0.0 collective-permute-done.8.refs_2_.refs_6_.refs_15_
  31.9 0.0 collective-permute-done.6.refs_0_.refs_3_.refs_12_
  31.9 0.3 collective-permute-start.12
  32.2 0.1 collective-permute-start.9
  32.3 0.0 collective-permute-done.10.refs_0_.refs_7_.refs_16_
  32.3 0.0 collective-permute-done.7.refs_2_.refs_4_.refs_13_
  32.3 0.4 collective-permute-start.13
  32.7 3.9 %collective-permute-done.11.refs_0_.refs_8_.refs_17_ = bf16[64,1536]{1,0:T(8,128)(2,1)S(1)} collective-permute-done((bf16[64,1536]{1,0:T(8,128)(2,1)S(1)}, bf16[64,1536]{1,0:T(8,128)(2,1)S(1)}, u32[]{:S(2)}, u32[]{:S(2)}) %collective-permute-start.11) | collective-permute-done | bytes 196640 | tf_op jit(solution)/shard_map/ppermute | solution.py:45
  36.6 0.3 collective-permute-start.14
  36.9 2.3 %shard_map.63 = (f32[512,512]{1,0:T(8,128)S(1)}, f32[8,128]{1,0:T(8,128)S(1)}) custom-call(s32[10]{0:T(128)S(1)} %stack.47.refs_2_.refs_0_.info, bf16[512,1536]{1,0:T(8,128)(2,1)S(1)} %copy-done.2, bf16[512,1536]{1,0:T(8,128)(2,1)S(1)} %collective-permute-done.3.refs_2_, bf16[3072,1536]{1,0:T(8,128)(2,1)S(1)} %copy-done.1, ...), custom_call_target="tpu_custom_call" | custom-call | flops 1000 | bytes 1000 | tf_op jit(solution)/shard_map/pallas_call | solution.py:192
  39.3 0.0 collective-permute-done.9.refs_5_.refs_14_
  39.3 0.0 copy-done.3
  39.3 2.1 %shard_map.64.earlier = f32[512,128]{1,0:T(8,128)S(1)} custom-call(s32[10]{0:T(128)S(1)} %stack.47.refs_2_.refs_0_.info, s32[512,1]{1,0:T(8,128)S(1)} %copy.9.refs_1_.ids, bf16[512,1536]{1,0:T(8,128)(2,1)S(1)} %copy-done.2, bf16[64,1536]{1,0:T(8,128)(2,1)S(1)} %bitcast.17, bf16[64,1536]{1,0:T(8,128)(2,1)} %collective-permute-done.refs_3_.beside, ...), custom_call_target="tpu_custom_call" | custom-call | tf_op jit(solution)/shard_map/pallas_call | solution.py:292
  41.4 0.0 copy-start.4
  41.4 0.0 collective-permute-done.12.refs_0_.refs_18_
  41.4 0.0 collective-permute-done.13.refs_1_.refs_19_
  41.4 1.9 %collective-permute-done.14.refs_2_.refs_20_ = bf16[64,1536]{1,0:T(8,128)(2,1)S(1)} collective-permute-done((bf16[64,1536]{1,0:T(8,128)(2,1)S(1)}, bf16[64,1536]{1,0:T(8,128)(2,1)S(1)}, u32[]{:S(2)}, u32[]{:S(2)}) %collective-permute-start.14) | collective-permute-done | bytes 196640 | tf_op jit(solution)/shard_map/ppermute | solution.py:45
  43.3 0.6 %shard_map.65.refs_2_ = f32[512,128]{1,0:T(8,128)S(1)} custom-call(s32[10]{0:T(128)S(1)} %stack.47.refs_2_.refs_0_.info, s32[512,1]{1,0:T(8,128)S(1)} %copy.9.refs_1_.ids, bf16[512,1536]{1,0:T(8,128)(2,1)S(1)} %copy-done.2, f32[512,128]{1,0:T(8,128)S(1)} %shard_map.64.earlier, bf16[64,1536]{1,0:T(8,128)(2,1)S(1)} %collective-permute-done.12.refs_0_.refs_18_, ...), custom_call_target="tpu_custom_call" | custom-call | tf_op jit(solution)/shard_map/pallas_call | solution.py:299
  43.9 4.3 %collective-permute-start.15 = (f32[512,128]{1,0:T(8,128)S(1)}, f32[512,128]{1,0:T(8,128)S(1)}, u32[]{:S(2)}, u32[]{:S(2)}) collective-permute-start(f32[512,128]{1,0:T(8,128)S(1)} %shard_map.65.refs_2_), channel_id=1, source_target_pairs={{0,1},{1,0},{2,3},{3,2},{4,5},{5,4},{6,7},{7,6},{8,9},{9,8},{10,11... | collective-permute-start | bytes 786440 | tf_op jit(solution)/shard_map/ppermute | solution.py:21
  48.2 1.2 %collective-permute-done.15.refs_3_ = f32[512,128]{1,0:T(8,128)S(1)} collective-permute-done((f32[512,128]{1,0:T(8,128)S(1)}, f32[512,128]{1,0:T(8,128)S(1)}, u32[]{:S(2)}, u32[]{:S(2)}) %collective-permute-start.15) | collective-permute-done | bytes 262176 | tf_op jit(solution)/shard_map/ppermute | solution.py:21
  49.4 3.1 %shard_map.66 = bf16[512,1536]{1,0:T(8,128)(2,1)} custom-call(s32[10]{0:T(128)S(1)} %stack.47.refs_2_.refs_0_.info, s32[512,1]{1,0:T(8,128)S(1)} %copy.9.refs_1_.ids, f32[512,128]{1,0:T(8,128)S(1)} %shard_map.65.refs_2_, f32[512,128]{1,0:T(8,128)S(1)} %collective-permute-done.15.refs_3_, f32[512,256]{1,0:T(8,128)S(1)} %get-tuple-element.38.refs_4_, ...), custom_call_target="tpu_custom_call" | custom-call | tf_op jit(solution)/shard_map/pallas_call | solution.py:319
  (9 shorter events, 0.1 us)
Async XLA Ops:
  0.0 19.1 %copy-start.2 = (bf16[512,1536]{1,0:T(8,128)(2,1)S(1)}, bf16[512,1536]{1,0:T(8,128)(2,1)}, u32[]{:S(2)}) copy-start(bf16[512,1536]{1,0:T(8,128)(2,1)} %latent.3) | copy-start | bytes 4718596
  0.0 18.8 %collective-permute-start.3 = (bf16[512,1536]{1,0:T(8,128)(2,1)}, bf16[512,1536]{1,0:T(8,128)(2,1)S(1)}, u32[]{:S(2)}, u32[]{:S(2)}) collective-permute-start(bf16[512,1536]{1,0:T(8,128)(2,1)} %latent.3), channel_id=1, source_target_pairs={{0,1},{1,0},{2,3},{3,2},{4,5},{5,4},{6,7},{7,6},{8,9},{9,8},{10,11... | collective-permute-start | bytes 4718600 | tf_op jit(solution)/shard_map/ppermute | solution.py:21
  2.4 10.9 %collective-permute-start.1 = (bf16[64,1536]{1,0:T(8,128)(2,1)}, bf16[64,1536]{1,0:T(8,128)(2,1)}, u32[]{:S(2)}, u32[]{:S(2)}) collective-permute-start(bf16[64,1536]{1,0:T(8,128)(2,1)} %broadcast_select_fusion), channel_id=1, source_target_pairs={{0,4},{2,6},{4,12},{6,14},{8,0},{10,2},{12,8},{14,10},{1,5},{3,7},... | collective-permute-start | bytes 589832 | tf_op jit(solution)/shard_map/ppermute | solution.py:35
  4.7 8.6 %collective-permute-start = (bf16[64,1536]{1,0:T(8,128)(2,1)}, bf16[64,1536]{1,0:T(8,128)(2,1)}, u32[]{:S(2)}, u32[]{:S(2)}) collective-permute-start(bf16[64,1536]{1,0:T(8,128)(2,1)} %bitcast.16), channel_id=1, source_target_pairs={{0,2},{2,0},{4,6},{6,4},{8,10},{10,8},{12,14},{14,12},{1,3},{3,1},... | collective-permute-start | bytes 589832 | tf_op jit(solution)/shard_map/ppermute | solution.py:25
  5.9 18.3 %collective-permute-start.2 = (bf16[64,1536]{1,0:T(8,128)(2,1)}, bf16[64,1536]{1,0:T(8,128)(2,1)}, u32[]{:S(2)}, u32[]{:S(2)}) collective-permute-start(bf16[64,1536]{1,0:T(8,128)(2,1)} %broadcast_select_fusion), channel_id=1, source_target_pairs={{0,8},{2,10},{4,0},{6,2},{8,12},{10,14},{12,4},{14,6},{1,9},{3,11}... | collective-permute-start | bytes 589832 | tf_op jit(solution)/shard_map/ppermute | solution.py:35
  6.0 18.3 %collective-permute-start.4 = (bf16[64,1536]{1,0:T(8,128)(2,1)}, bf16[64,1536]{1,0:T(8,128)(2,1)}, u32[]{:S(2)}, u32[]{:S(2)}) collective-permute-start(bf16[64,1536]{1,0:T(8,128)(2,1)} %bitcast.18), channel_id=1, source_target_pairs={{0,2},{2,0},{4,6},{6,4},{8,10},{10,8},{12,14},{14,12},{1,3},{3,1},... | collective-permute-start | bytes 589832 | tf_op jit(solution)/shard_map/ppermute | solution.py:25
  14.3 16.3 %collective-permute-start.5 = (bf16[64,1536]{1,0:T(8,128)(2,1)S(1)}, bf16[64,1536]{1,0:T(8,128)(2,1)S(1)}, u32[]{:S(2)}, u32[]{:S(2)}) collective-permute-start(bf16[64,1536]{1,0:T(8,128)(2,1)S(1)} %get-tuple-element.23.refs_0_.refs_9_), channel_id=1, source_target_pairs={{0,4},{2,6},{4,12},{6,14},{8,0},{10,2},{12,8},{14,10},{1,5},{3,7},... | collective-permute-start | bytes 589832 | tf_op jit(solution)/shard_map/ppermute | solution.py:35
  17.5 14.3 %collective-permute-start.8 = (bf16[64,1536]{1,0:T(8,128)(2,1)S(1)}, bf16[64,1536]{1,0:T(8,128)(2,1)S(1)}, u32[]{:S(2)}, u32[]{:S(2)}) collective-permute-start(bf16[64,1536]{1,0:T(8,128)(2,1)S(1)} %get-tuple-element.23.refs_0_.refs_9_), channel_id=1, source_target_pairs={{0,16},{1,3},{2,18},{3,1},{4,20},{5,7},{6,22},{7,5},{8,24},{9,11},... | collective-permute-start | bytes 589832 | tf_op jit(solution)/shard_map/ppermute | solution.py:45
  18.8 13.1 %collective-permute-start.6 = (bf16[64,1536]{1,0:T(8,128)(2,1)S(1)}, bf16[64,1536]{1,0:T(8,128)(2,1)S(1)}, u32[]{:S(2)}, u32[]{:S(2)}) collective-permute-start(bf16[64,1536]{1,0:T(8,128)(2,1)S(1)} %get-tuple-element.23.refs_0_.refs_9_), channel_id=1, source_target_pairs={{0,2},{1,17},{2,0},{3,19},{4,6},{5,21},{6,4},{7,23},{8,10},{9,25},... | collective-permute-start | bytes 589832 | tf_op jit(solution)/shard_map/ppermute | solution.py:45
  19.1 3.7 %copy-start = (bf16[3072,1536]{1,0:T(8,128)(2,1)S(1)}, bf16[3072,1536]{1,0:T(8,128)(2,1)}, u32[]{:S(2)}) copy-start(bf16[3072,1536]{1,0:T(8,128)(2,1)} %refs_3_.5) | copy-start | bytes 28311556
  22.7 4.6 %copy-start.1 = (bf16[3072,1536]{1,0:T(8,128)(2,1)S(1)}, bf16[3072,1536]{1,0:T(8,128)(2,1)}, u32[]{:S(2)}) copy-start(bf16[3072,1536]{1,0:T(8,128)(2,1)} %refs_3_.5) | copy-start | bytes 28311556
  25.9 6.4 %collective-permute-start.10 = (bf16[64,1536]{1,0:T(8,128)(2,1)S(1)}, bf16[64,1536]{1,0:T(8,128)(2,1)S(1)}, u32[]{:S(2)}, u32[]{:S(2)}) collective-permute-start(bf16[64,1536]{1,0:T(8,128)(2,1)S(1)} %get-tuple-element.26.refs_1_.refs_10_), channel_id=1, source_target_pairs={{0,16},{1,3},{2,18},{3,1},{4,20},{5,7},{6,22},{7,5},{8,24},{9,11},... | collective-permute-start | bytes 589832 | tf_op jit(solution)/shard_map/ppermute | solution.py:45
  26.2 6.1 %collective-permute-start.7 = (bf16[64,1536]{1,0:T(8,128)(2,1)S(1)}, bf16[64,1536]{1,0:T(8,128)(2,1)S(1)}, u32[]{:S(2)}, u32[]{:S(2)}) collective-permute-start(bf16[64,1536]{1,0:T(8,128)(2,1)S(1)} %get-tuple-element.26.refs_1_.refs_10_), channel_id=1, source_target_pairs={{0,2},{1,17},{2,0},{3,19},{4,6},{5,21},{6,4},{7,23},{8,10},{9,25},... | collective-permute-start | bytes 589832 | tf_op jit(solution)/shard_map/ppermute | solution.py:45
  30.6 6.0 %collective-permute-start.11 = (bf16[64,1536]{1,0:T(8,128)(2,1)S(1)}, bf16[64,1536]{1,0:T(8,128)(2,1)S(1)}, u32[]{:S(2)}, u32[]{:S(2)}) collective-permute-start(bf16[64,1536]{1,0:T(8,128)(2,1)S(1)} %get-tuple-element.29.refs_2_.refs_11_), channel_id=1, source_target_pairs={{0,16},{1,3},{2,18},{3,1},{4,20},{5,7},{6,22},{7,5},{8,24},{9,11},... | collective-permute-start | bytes 589832 | tf_op jit(solution)/shard_map/ppermute | solution.py:45
  31.9 9.5 %collective-permute-start.12 = (bf16[64,1536]{1,0:T(8,128)(2,1)S(1)}, bf16[64,1536]{1,0:T(8,128)(2,1)S(1)}, u32[]{:S(2)}, u32[]{:S(2)}) collective-permute-start(bf16[64,1536]{1,0:T(8,128)(2,1)S(1)} %get-tuple-element.31), channel_id=1, source_target_pairs={{0,16},{1,3},{2,18},{3,1},{4,20},{5,7},{6,22},{7,5},{8,24},{9,11},... | collective-permute-start | bytes 589832 | tf_op jit(solution)/shard_map/ppermute | solution.py:45
  32.2 7.1 %collective-permute-start.9 = (bf16[64,1536]{1,0:T(8,128)(2,1)S(1)}, bf16[64,1536]{1,0:T(8,128)(2,1)S(1)}, u32[]{:S(2)}, u32[]{:S(2)}) collective-permute-start(bf16[64,1536]{1,0:T(8,128)(2,1)S(1)} %get-tuple-element.31), channel_id=1, source_target_pairs={{0,4},{2,6},{4,12},{6,14},{8,0},{10,2},{12,8},{14,10},{1,5},{3,7},... | collective-permute-start | bytes 589832 | tf_op jit(solution)/shard_map/ppermute | solution.py:35
  32.3 9.1 %collective-permute-start.13 = (bf16[64,1536]{1,0:T(8,128)(2,1)S(1)}, bf16[64,1536]{1,0:T(8,128)(2,1)S(1)}, u32[]{:S(2)}, u32[]{:S(2)}) collective-permute-start(bf16[64,1536]{1,0:T(8,128)(2,1)S(1)} %get-tuple-element.36), channel_id=1, source_target_pairs={{0,2},{1,17},{2,0},{3,19},{4,6},{5,21},{6,4},{7,23},{8,10},{9,25},... | collective-permute-start | bytes 589832 | tf_op jit(solution)/shard_map/ppermute | solution.py:45
  36.6 6.7 %collective-permute-start.14 = (bf16[64,1536]{1,0:T(8,128)(2,1)S(1)}, bf16[64,1536]{1,0:T(8,128)(2,1)S(1)}, u32[]{:S(2)}, u32[]{:S(2)}) collective-permute-start(bf16[64,1536]{1,0:T(8,128)(2,1)S(1)} %get-tuple-element.37), channel_id=1, source_target_pairs={{0,2},{1,17},{2,0},{3,19},{4,6},{5,21},{6,4},{7,23},{8,10},{9,25},... | collective-permute-start | bytes 589832 | tf_op jit(solution)/shard_map/ppermute | solution.py:45
  36.9 2.3 %copy-start.3 = (bf16[1,1536,64]{1,2,0:T(8,128)(2,1)S(1)}, bf16[1,1536,64]{1,2,0:T(8,128)(2,1)}, u32[]{:S(2)}) copy-start(bf16[1,1536,64]{1,2,0:T(8,128)(2,1)} %param.8) | copy-start | bytes 589828
  41.4 8.0 %copy-start.4 = (bf16[1,64,1536]{2,1,0:T(8,128)(2,1)S(1)}, bf16[1,64,1536]{2,1,0:T(8,128)(2,1)}, u32[]{:S(2)}) copy-start(bf16[1,64,1536]{2,1,0:T(8,128)(2,1)} %param.9) | copy-start | bytes 589828
  43.9 5.5 %collective-permute-start.15 = (f32[512,128]{1,0:T(8,128)S(1)}, f32[512,128]{1,0:T(8,128)S(1)}, u32[]{:S(2)}, u32[]{:S(2)}) collective-permute-start(f32[512,128]{1,0:T(8,128)S(1)} %shard_map.65.refs_2_), channel_id=1, source_target_pairs={{0,1},{1,0},{2,3},{3,2},{4,5},{5,4},{6,7},{7,6},{8,9},{9,8},{10,11... | collective-permute-start | bytes 786440 | tf_op jit(solution)/shard_map/ppermute | solution.py:21

commit v14 on v12

--- a/solution.py
+++ b/solution.py
@@ -114,6 +114,13 @@
     for number in range(count):
         place = top + 2 * number * rank
         stack[place : place + rank, :] = jnp.zeros((rank, stack.shape[1]), stack.dtype)
+
+
+def prepare_kernel(weight, row_ids, *refs):
+    spread, token = refs[-2:]
+    wide = jnp.broadcast_to(row_ids[...].astype(jnp.float32), (128, row_ids.shape[1]))
+    spread[...] = wide.T.astype(jnp.int32)
+    token[...] = weight[0:8, 0:128].astype(jnp.float32)
 
 
 def masked_products(info, ids, latent, stack, blocks, rank):
@@ -128,9 +135,9 @@
             preferred_element_type=jnp.float32,
         )
         owners = owner_row(info, blocks[skip // rank : (skip + count) // rank], rank)
-        part = jnp.where(ids[...] == owners, part, 0.0)
         for lane in range(0, count, width):
-            fold = part[:, lane : lane + width]
+            lanes = slice(lane, lane + width)
+            fold = jnp.where(ids[...] == owners[:, lanes], part[:, lanes], 0.0)
             total = fold if total is None else total + fold
     return total
 
@@ -247,10 +254,10 @@
     index, core = lax.axis_index("shard"), lax.axis_index("tensor")
     holds_down = core == lax.axis_index("replica")
     tiles = out_width // TILE
-    cuts = [0, out_width // 6, out_width * 2 // 3, out_width]
+    cuts = [0, out_width // 6, out_width // 2, out_width]
     down = jnp.swapaxes(adapter_down_weight, 1, 2).reshape(local_adapters * rank, half_width)
     up = adapter_up_weight.reshape(local_adapters * rank, out_width)
-    ids = row_adapter_index
+    row_ids = row_adapter_index.reshape(1, rows)
     routed = shards == 8 and local_adapters == 1 and lax.axis_size("replica") == 2
     routed = routed and half_width == out_width and tiles % 6 == 0
     lowrank = jax.ShapeDtypeStruct((rows, 2 * rank), jnp.float32)
@@ -260,32 +267,35 @@
     else:
         owners = list(range(adapters))
     info = jnp.stack([jnp.asarray(v, jnp.int32) for v in (core, holds_down, *owners)])
+    ids, token = call(
+        prepare_kernel,
+        [jax.ShapeDtypeStruct((rows, 2 * rank), jnp.int32), TOKEN],
+        [VMEM, VMEM, ANY],
+        16,
+    )(shared_weight, row_ids, info)
     if routed:
         piece = jnp.where(holds_down, down, up)
         line = {step: along_line(piece, shards, step) for step in (1, 3)}
         other = swap(latent, "tensor")
         down_beside, up_beside = neighbour(down, shards), neighbour(up, shards)
-        parts = []
-        part, token = base(info, latent, other, shared_weight, [ids], cuts[0], cuts[1])
-        parts.append(part)
         one, token = pack([(line[1], 0, rank)], token, down_beside)
         line[2] = along_line(one, shards, 1)
         one_first, one_second = in_plane(one, shards, True), in_plane(one, shards, False)
+        part_one, token = base(info, latent, other, shared_weight, [token], cuts[0], cuts[1])
         three, token = pack([(line[3], 0, rank)], token, up_beside)
         three_first, three_second = in_plane(three, shards, True), in_plane(three, shards, False)
-        part, token = base(info, latent, other, shared_weight, [token], cuts[1], cuts[2])
-        parts.append(part)
         two, token = pack([(line[2], 0, rank)], token)
         two_second = in_plane(two, shards, False)
         turn, token = pack([(one_first, 0, rank)], token, one_second)
         corner_one = in_plane(turn, shards, False)
         two_first = along_line(turn, shards, 1)
+        part_two, token = base(info, latent, other, shared_weight, [token], cuts[1], cuts[2])
         turn, token = pack([(three_second, 0, rank)], token, three_first)
         corner_three = in_plane(turn, shards, True)
         turn, token = pack([(two_second, 0, rank)], token)
         corner_two = in_plane(turn, shards, True)
-        part, token = base(info, latent, other, shared_weight, [token], cuts[2], cuts[3])
-        parts.append(part)
+        part_three, token = base(info, latent, other, shared_weight, [token], cuts[2], cuts[3])
+        parts = [part_one, part_two, part_three]
         corners = [corner_one, corner_three, corner_two]
         received = [one, three, two, one_first, three_first, two_first]
         received += [one_second, three_second, two_second]
@@ -306,7 +316,7 @@
         up_pieces = [up, up_beside, *received, *corners]
     else:
         other = swap(latent, "tensor")
-        parts, token = [], ids
+        parts = []
         for begin, end in zip(cuts[:-1], cuts[1:]):
             part, token = base(info, latent, other, shared_weight, [token], begin, end)
             parts.append(part)

time: 43 us -> 44.6 us (1.037)
  the two profiles are of different devices: /device:TPU:0 before, /device:TPU:11 now
where the time goes in v14:
time: 44.6 us; the launch traced here: 44.4 us
  starting transfers between devices  18.3 us (41%)
  Pallas kernels  12.1 us (27%)
  waiting for transfers between devices  6.93 us (16%)
  local copies, waits for them, and re-layouts  5.87 us (13%)
  other arithmetic  1.04 us (2%)
    pallas_call x3, Pallas kernels, base(): pl.pallas_call(lambda *refs: base_kernel(*refs, skip=skip), out_shape=[ja...  7.02 us
    ppermute x8, starting transfers between devices, in_plane(): return lax.ppermute(value, AXES, pairs)  6.69 us
    ppermute x4, starting transfers between devices, along_line(): lax.ppermute(value, 'shard', [(i, ring_step(i, step)) for i in range(shar...  6.06 us
    unnamed x14, local copies, waits for them, and re-layouts  5.79 us
    ppermute x2, starting transfers between devices, swap(): return lax.ppermute(value, axis, [(0, 1), (1, 0)])  4.06 us
    ppermute x8, waiting for transfers between devices, in_plane(): return lax.ppermute(value, AXES, pairs)  3.37 us
    pallas_call x1, Pallas kernels, on_device(): pl.pallas_call(lambda *refs: up_kernel(*refs, base_parts=len(parts)), out...  2.6 us
    ppermute x4, waiting for transfers between devices, along_line(): lax.ppermute(value, 'shard', [(i, ring_step(i, step)) for i in range(shar...  2.39 us
  transfers between devices with their start and end apart: 16, of which 6 were waited for; matrix products, arithmetic and copies ran while one was open for 3% of the time, Pallas kernels for 20%

profile of v14, /device:TPU:11, one launch (start us, length us, event | category | flops | bytes accessed | tf_op | source)
XLA Modules:
  0.0 44.4 jit_solution(15372969619769536944)
XLA Ops:
  0.0 0.7 %collective-permute-start.3 = (bf16[512,1536]{1,0:T(8,128)(2,1)}, bf16[512,1536]{1,0:T(8,128)(2,1)S(1)}, u32[]{:S(2)}, u32[]{:S(2)}) collective-permute-start(bf16[512,1536]{1,0:T(8,128)(2,1)} %latent.3), channel_id=1, source_target_pairs={{0,1},{1,0},{2,3},{3,2},{4,5},{5,4},{6,7},{7,6},{8,9},{9,8},{10,11... | collective-permute-start | bytes 4718600 | tf_op jit(solution)/shard_map/ppermute | solution.py:21
  0.7 1.0 %broadcast_select_fusion = bf16[64,1536]{1,0:T(8,128)(2,1)S(1)} fusion(pred[]{:T(512)S(6)} %eq.3, bf16[1,64,1536]{2,1,0:T(8,128)(2,1)} %param.9, bf16[1,1536,64]{1,2,0:T(8,128)(2,1)} %param.8), kind=kLoop, calls=%fused_computation | loop fusion | flops 98304 | bytes 589825 | tf_op jit(solution)/shard_map/jit(_where)/select_n | solution.py:277
  1.7 2.4 %collective-permute-start.1 = (bf16[64,1536]{1,0:T(8,128)(2,1)S(1)}, bf16[64,1536]{1,0:T(8,128)(2,1)S(1)}, u32[]{:S(2)}, u32[]{:S(2)}) collective-permute-start(bf16[64,1536]{1,0:T(8,128)(2,1)S(1)} %broadcast_select_fusion), channel_id=1, source_target_pairs={{0,4},{2,6},{4,12},{6,14},{8,0},{10,2},{12,8},{14,10},{1,5},{3,7},... | collective-permute-start | bytes 589832 | tf_op jit(solution)/shard_map/ppermute | solution.py:35
  4.1 1.2 %collective-permute-start = (bf16[64,1536]{1,0:T(8,128)(2,1)}, bf16[64,1536]{1,0:T(8,128)(2,1)S(1)}, u32[]{:S(2)}, u32[]{:S(2)}) collective-permute-start(bf16[64,1536]{1,0:T(8,128)(2,1)} %bitcast.17), channel_id=1, source_target_pairs={{0,2},{2,0},{4,6},{6,4},{8,10},{10,8},{12,14},{14,12},{1,3},{3,1},... | collective-permute-start | bytes 589832 | tf_op jit(solution)/shard_map/ppermute | solution.py:25
  5.3 0.0 collective-permute-start.2
  5.3 0.2 collective-permute-start.4
  5.6 0.1 stack.47.refs_0_.info
  5.6 3.7 %copy-done = bf16[3072,1536]{1,0:T(8,128)(2,1)S(1)} copy-done((bf16[3072,1536]{1,0:T(8,128)(2,1)S(1)}, bf16[3072,1536]{1,0:T(8,128)(2,1)}, u32[]{:S(2)}) %copy-start) | copy-done | bytes 9437208
  9.3 0.7 %copy-done.6 = s32[512,1]{0,1:T(1,128)S(1)} copy-done((s32[512,1]{0,1:T(1,128)S(1)}, s32[512,1]{0,1:T(1,128)}, u32[]{:S(2)}) %copy-start.6) | copy-done | bytes 2072
  10.0 0.1 shard_map.55
  10.1 2.4 %collective-permute-done.1.refs_0_ = bf16[64,1536]{1,0:T(8,128)(2,1)S(1)} collective-permute-done((bf16[64,1536]{1,0:T(8,128)(2,1)S(1)}, bf16[64,1536]{1,0:T(8,128)(2,1)S(1)}, u32[]{:S(2)}, u32[]{:S(2)}) %collective-permute-start.1) | collective-permute-done | bytes 196640 | tf_op jit(solution)/shard_map/ppermute | solution.py:35
  12.5 0.0 collective-permute-done.refs_2_.beside
  12.6 3.3 %collective-permute-start.5 = (bf16[64,1536]{1,0:T(8,128)(2,1)S(1)}, bf16[64,1536]{1,0:T(8,128)(2,1)S(1)}, u32[]{:S(2)}, u32[]{:S(2)}) collective-permute-start(bf16[64,1536]{1,0:T(8,128)(2,1)S(1)} %get-tuple-element.27.refs_0_.refs_9_), channel_id=1, source_target_pairs={{0,4},{2,6},{4,12},{6,14},{8,0},{10,2},{12,8},{14,10},{1,5},{3,7},... | collective-permute-start | bytes 589832 | tf_op jit(solution)/shard_map/ppermute | solution.py:35
  15.8 1.2 %collective-permute-start.8 = (bf16[64,1536]{1,0:T(8,128)(2,1)S(1)}, bf16[64,1536]{1,0:T(8,128)(2,1)S(1)}, u32[]{:S(2)}, u32[]{:S(2)}) collective-permute-start(bf16[64,1536]{1,0:T(8,128)(2,1)S(1)} %get-tuple-element.27.refs_0_.refs_9_), channel_id=1, source_target_pairs={{0,16},{1,3},{2,18},{3,1},{4,20},{5,7},{6,22},{7,5},{8,24},{9,11},... | collective-permute-start | bytes 589832 | tf_op jit(solution)/shard_map/ppermute | solution.py:45
  17.1 0.0 collective-permute-done.3.refs_2_
  17.1 0.3 collective-permute-start.6
  17.4 0.0 copy-done.1
  17.4 1.4 %copy-done.2 = bf16[512,1536]{1,0:T(8,128)(2,1)S(1)} copy-done((bf16[512,1536]{1,0:T(8,128)(2,1)S(1)}, bf16[512,1536]{1,0:T(8,128)(2,1)}, u32[]{:S(2)}) %copy-start.2) | copy-done | bytes 1572888
  18.8 1.5 %shard_map.57 = (f32[512,256]{1,0:T(8,128)S(1)}, f32[8,128]{1,0:T(8,128)S(1)}) custom-call(s32[10]{0:T(128)S(1)} %stack.47.refs_0_.info, bf16[512,1536]{1,0:T(8,128)(2,1)S(1)} %copy-done.2, bf16[512,1536]{1,0:T(8,128)(2,1)S(1)} %collective-permute-done.3.refs_2_, bf16[3072,1536]{1,0:T(8,128)(2,1)S(1)} %copy-done.1, f32[8,128]{1,0:T(8,128)S(1)} %get-tuple-element.28.refs_4_), custom_call_target="tpu_custom_call" | custom-call | flops 1000 | bytes 1000 | tf_op jit(solution)/shard_map/pallas_call | solution.py:199
  20.3 0.0 collective-permute-done.2.refs_0_
  20.3 0.0 collective-permute-done.4.refs_2_.refs_8_
  20.3 0.3 collective-permute-start.10
  20.6 1.2 %collective-permute-start.7 = (bf16[64,1536]{1,0:T(8,128)(2,1)S(1)}, bf16[64,1536]{1,0:T(8,128)(2,1)S(1)}, u32[]{:S(2)}, u32[]{:S(2)}) collective-permute-start(bf16[64,1536]{1,0:T(8,128)(2,1)S(1)} %get-tuple-element.30.refs_1_.refs_10_), channel_id=1, source_target_pairs={{0,2},{1,17},{2,0},{3,19},{4,6},{5,21},{6,4},{7,23},{8,10},{9,25},... | collective-permute-start | bytes 589832 | tf_op jit(solution)/shard_map/ppermute | solution.py:45
  21.8 0.0 collective-permute-done.5.refs_0_
  21.9 1.3 %collective-permute-start.11 = (bf16[64,1536]{1,0:T(8,128)(2,1)S(1)}, bf16[64,1536]{1,0:T(8,128)(2,1)S(1)}, u32[]{:S(2)}, u32[]{:S(2)}) collective-permute-start(bf16[64,1536]{1,0:T(8,128)(2,1)S(1)} %get-tuple-element.32.refs_2_.refs_11_), channel_id=1, source_target_pairs={{0,16},{1,3},{2,18},{3,1},{4,20},{5,7},{6,22},{7,5},{8,24},{9,11},... | collective-permute-start | bytes 589832 | tf_op jit(solution)/shard_map/ppermute | solution.py:45
  23.2 0.0 collective-permute-done.8.refs_2_.refs_6_.refs_15_
  23.2 0.6 %collective-permute-done.6.refs_0_.refs_3_.refs_12_ = bf16[64,1536]{1,0:T(8,128)(2,1)S(1)} collective-permute-done((bf16[64,1536]{1,0:T(8,128)(2,1)S(1)}, bf16[64,1536]{1,0:T(8,128)(2,1)S(1)}, u32[]{:S(2)}, u32[]{:S(2)}) %collective-permute-start.6) | collective-permute-done | bytes 196640 | tf_op jit(solution)/shard_map/ppermute | solution.py:45
  23.8 0.1 collective-permute-start.12
  23.8 0.4 collective-permute-start.9
  24.2 0.0 copy-done.3
  24.2 2.3 %shard_map.61 = (f32[512,512]{1,0:T(8,128)S(1)}, f32[8,128]{1,0:T(8,128)S(1)}) custom-call(s32[10]{0:T(128)S(1)} %stack.47.refs_0_.info, bf16[512,1536]{1,0:T(8,128)(2,1)S(1)} %copy-done.3, bf16[512,1536]{1,0:T(8,128)(2,1)S(1)} %collective-permute-done.3.refs_2_, bf16[3072,1536]{1,0:T(8,128)(2,1)S(1)} %copy-done.1, f32[8,128]{1,0:T(8,128)S(1)} %get-tuple-element.35.refs_4_), custom_call_target="tpu_custom_call" | custom-call | flops 1000 | bytes 1000 | tf_op jit(solution)/shard_map/pallas_call | solution.py:199
  26.6 0.0 collective-permute-done.10.refs_0_.refs_7_.refs_16_
  26.6 0.4 collective-permute-done.7.refs_2_.refs_4_.refs_13_
  27.0 0.9 %collective-permute-done.11.refs_0_.refs_8_.refs_17_ = bf16[64,1536]{1,0:T(8,128)(2,1)S(1)} collective-permute-done((bf16[64,1536]{1,0:T(8,128)(2,1)S(1)}, bf16[64,1536]{1,0:T(8,128)(2,1)S(1)}, u32[]{:S(2)}, u32[]{:S(2)}) %collective-permute-start.11) | collective-permute-done | bytes 196640 | tf_op jit(solution)/shard_map/ppermute | solution.py:45
  27.9 2.2 %collective-permute-start.14 = (bf16[64,1536]{1,0:T(8,128)(2,1)S(1)}, bf16[64,1536]{1,0:T(8,128)(2,1)S(1)}, u32[]{:S(2)}, u32[]{:S(2)}) collective-permute-start(bf16[64,1536]{1,0:T(8,128)(2,1)S(1)} %get-tuple-element.41), channel_id=1, source_target_pairs={{0,2},{1,17},{2,0},{3,19},{4,6},{5,21},{6,4},{7,23},{8,10},{9,25},... | collective-permute-start | bytes 589832 | tf_op jit(solution)/shard_map/ppermute | solution.py:45
  30.1 0.1 collective-permute-start.13
  30.2 3.2 %shard_map.64 = (f32[512,768]{1,0:T(8,128)S(1)}, f32[8,128]{1,0:T(8,128)S(1)}) custom-call(s32[10]{0:T(128)S(1)} %stack.47.refs_0_.info, bf16[512,1536]{1,0:T(8,128)(2,1)S(1)} %copy-done.3, bf16[512,1536]{1,0:T(8,128)(2,1)S(1)} %collective-permute-done.3.refs_2_, bf16[3072,1536]{1,0:T(8,128)(2,1)S(1)} %copy-done.1, f32[8,128]{1,0:T(8,128)S(1)} %get-tuple-element.38.refs_4_), custom_call_target="tpu_custom_call" | custom-call | flops 1000 | bytes 1000 | tf_op jit(solution)/shard_map/pallas_call | solution.py:199
  33.4 0.0 collective-permute-done.9.refs_5_.refs_14_
  33.4 0.0 copy-done.4
  33.4 1.7 %shard_map.65.earlier = f32[512,128]{1,0:T(8,128)S(1)} custom-call(s32[10]{0:T(128)S(1)} %stack.47.refs_0_.info, s32[512,128]{1,0:T(8,128)S(1)} %get-tuple-element.25.ids.refs_1_, bf16[512,1536]{1,0:T(8,128)(2,1)S(1)} %copy-done.3, bf16[64,1536]{1,0:T(8,128)(2,1)S(1)} %bitcast.18, bf16[64,1536]{1,0:T(8,128)(2,1)S(1)} %collective-permute-done.refs_2_.beside, ...), custom_call_target="tpu_custom_call" | custom-call | tf_op jit(solution)/shard_map/pallas_call | solution.py:302
  35.1 0.0 copy-start.5
  35.1 0.0 collective-permute-done.12.refs_0_.refs_18_
  35.1 0.0 collective-permute-done.14.refs_2_.refs_20_
  35.2 1.5 %collective-permute-done.13.refs_1_.refs_19_ = bf16[64,1536]{1,0:T(8,128)(2,1)S(1)} collective-permute-done((bf16[64,1536]{1,0:T(8,128)(2,1)S(1)}, bf16[64,1536]{1,0:T(8,128)(2,1)S(1)}, u32[]{:S(2)}, u32[]{:S(2)}) %collective-permute-start.13) | collective-permute-done | bytes 196640 | tf_op jit(solution)/shard_map/ppermute | solution.py:45
  36.7 0.6 %shard_map.66.refs_2_ = f32[512,128]{1,0:T(8,128)S(1)} custom-call(s32[10]{0:T(128)S(1)} %stack.47.refs_0_.info, s32[512,128]{1,0:T(8,128)S(1)} %get-tuple-element.25.ids.refs_1_, bf16[512,1536]{1,0:T(8,128)(2,1)S(1)} %copy-done.3, f32[512,128]{1,0:T(8,128)S(1)} %shard_map.65.earlier, bf16[64,1536]{1,0:T(8,128)(2,1)S(1)} %collective-permute-done.12.refs_0_.refs_18_, ...), custom_call_target="tpu_custom_call" | custom-call | tf_op jit(solution)/shard_map/pallas_call | solution.py:309
  37.2 3.4 %collective-permute-start.15 = (f32[512,128]{1,0:T(8,128)S(1)}, f32[512,128]{1,0:T(8,128)S(1)}, u32[]{:S(2)}, u32[]{:S(2)}) collective-permute-start(f32[512,128]{1,0:T(8,128)S(1)} %shard_map.66.refs_2_), channel_id=1, source_target_pairs={{0,1},{1,0},{2,3},{3,2},{4,5},{5,4},{6,7},{7,6},{8,9},{9,8},{10,11... | collective-permute-start | bytes 786440 | tf_op jit(solution)/shard_map/ppermute | solution.py:21
  40.6 1.2 %collective-permute-done.15.refs_3_ = f32[512,128]{1,0:T(8,128)S(1)} collective-permute-done((f32[512,128]{1,0:T(8,128)S(1)}, f32[512,128]{1,0:T(8,128)S(1)}, u32[]{:S(2)}, u32[]{:S(2)}) %collective-permute-start.15) | collective-permute-done | bytes 262176 | tf_op jit(solution)/shard_map/ppermute | solution.py:21
  41.8 2.6 %shard_map.67 = bf16[512,1536]{1,0:T(8,128)(2,1)} custom-call(s32[10]{0:T(128)S(1)} %stack.47.refs_0_.info, s32[512,128]{1,0:T(8,128)S(1)} %get-tuple-element.25.ids.refs_1_, f32[512,128]{1,0:T(8,128)S(1)} %shard_map.66.refs_2_, f32[512,128]{1,0:T(8,128)S(1)} %collective-permute-done.15.refs_3_, f32[512,256]{1,0:T(8,128)S(1)} %get-tuple-element.42.refs_4_, ...), custom_call_target="tpu_custom_call" | custom-call | tf_op jit(solution)/shard_map/pallas_call | solution.py:329
  (13 shorter events, 0.1 us)
Async XLA Ops:
  0.0 17.1 %collective-permute-start.3 = (bf16[512,1536]{1,0:T(8,128)(2,1)}, bf16[512,1536]{1,0:T(8,128)(2,1)S(1)}, u32[]{:S(2)}, u32[]{:S(2)}) collective-permute-start(bf16[512,1536]{1,0:T(8,128)(2,1)} %latent.3), channel_id=1, source_target_pairs={{0,1},{1,0},{2,3},{3,2},{4,5},{5,4},{6,7},{7,6},{8,9},{9,8},{10,11... | collective-permute-start | bytes 4718600 | tf_op jit(solution)/shard_map/ppermute | solution.py:21
  1.7 10.8 %collective-permute-start.1 = (bf16[64,1536]{1,0:T(8,128)(2,1)S(1)}, bf16[64,1536]{1,0:T(8,128)(2,1)S(1)}, u32[]{:S(2)}, u32[]{:S(2)}) collective-permute-start(bf16[64,1536]{1,0:T(8,128)(2,1)S(1)} %broadcast_select_fusion), channel_id=1, source_target_pairs={{0,4},{2,6},{4,12},{6,14},{8,0},{10,2},{12,8},{14,10},{1,5},{3,7},... | collective-permute-start | bytes 589832 | tf_op jit(solution)/shard_map/ppermute | solution.py:35
  4.1 8.4 %collective-permute-start = (bf16[64,1536]{1,0:T(8,128)(2,1)}, bf16[64,1536]{1,0:T(8,128)(2,1)S(1)}, u32[]{:S(2)}, u32[]{:S(2)}) collective-permute-start(bf16[64,1536]{1,0:T(8,128)(2,1)} %bitcast.17), channel_id=1, source_target_pairs={{0,2},{2,0},{4,6},{6,4},{8,10},{10,8},{12,14},{14,12},{1,3},{3,1},... | collective-permute-start | bytes 589832 | tf_op jit(solution)/shard_map/ppermute | solution.py:25
  5.3 15.0 %collective-permute-start.2 = (bf16[64,1536]{1,0:T(8,128)(2,1)S(1)}, bf16[64,1536]{1,0:T(8,128)(2,1)S(1)}, u32[]{:S(2)}, u32[]{:S(2)}) collective-permute-start(bf16[64,1536]{1,0:T(8,128)(2,1)S(1)} %broadcast_select_fusion), channel_id=1, source_target_pairs={{0,8},{2,10},{4,0},{6,2},{8,12},{10,14},{12,4},{14,6},{1,9},{3,11}... | collective-permute-start | bytes 589832 | tf_op jit(solution)/shard_map/ppermute | solution.py:35
  5.3 15.0 %collective-permute-start.4 = (bf16[64,1536]{1,0:T(8,128)(2,1)}, bf16[64,1536]{1,0:T(8,128)(2,1)S(1)}, u32[]{:S(2)}, u32[]{:S(2)}) collective-permute-start(bf16[64,1536]{1,0:T(8,128)(2,1)} %bitcast.19), channel_id=1, source_target_pairs={{0,2},{2,0},{4,6},{6,4},{8,10},{10,8},{12,14},{14,12},{1,3},{3,1},... | collective-permute-start | bytes 589832 | tf_op jit(solution)/shard_map/ppermute | solution.py:25
  5.6 3.7 %copy-start = (bf16[3072,1536]{1,0:T(8,128)(2,1)S(1)}, bf16[3072,1536]{1,0:T(8,128)(2,1)}, u32[]{:S(2)}) copy-start(bf16[3072,1536]{1,0:T(8,128)(2,1)} %refs_3_.5) | copy-start | bytes 28311556
  9.3 0.7 %copy-start.6 = (s32[512,1]{0,1:T(1,128)S(1)}, s32[512,1]{0,1:T(1,128)}, u32[]{:S(2)}) copy-start(s32[512,1]{0,1:T(1,128)} %param.6) | copy-start | bytes 6148
  10.0 7.3 %copy-start.1 = (bf16[3072,1536]{1,0:T(8,128)(2,1)S(1)}, bf16[3072,1536]{1,0:T(8,128)(2,1)}, u32[]{:S(2)}) copy-start(bf16[3072,1536]{1,0:T(8,128)(2,1)} %refs_3_.5) | copy-start | bytes 28311556
  12.6 9.3 %collective-permute-start.5 = (bf16[64,1536]{1,0:T(8,128)(2,1)S(1)}, bf16[64,1536]{1,0:T(8,128)(2,1)S(1)}, u32[]{:S(2)}, u32[]{:S(2)}) collective-permute-start(bf16[64,1536]{1,0:T(8,128)(2,1)S(1)} %get-tuple-element.27.refs_0_.refs_9_), channel_id=1, source_target_pairs={{0,4},{2,6},{4,12},{6,14},{8,0},{10,2},{12,8},{14,10},{1,5},{3,7},... | collective-permute-start | bytes 589832 | tf_op jit(solution)/shard_map/ppermute | solution.py:35
  15.8 7.3 %collective-permute-start.8 = (bf16[64,1536]{1,0:T(8,128)(2,1)S(1)}, bf16[64,1536]{1,0:T(8,128)(2,1)S(1)}, u32[]{:S(2)}, u32[]{:S(2)}) collective-permute-start(bf16[64,1536]{1,0:T(8,128)(2,1)S(1)} %get-tuple-element.27.refs_0_.refs_9_), channel_id=1, source_target_pairs={{0,16},{1,3},{2,18},{3,1},{4,20},{5,7},{6,22},{7,5},{8,24},{9,11},... | collective-permute-start | bytes 589832 | tf_op jit(solution)/shard_map/ppermute | solution.py:45
  17.1 6.6 %collective-permute-start.6 = (bf16[64,1536]{1,0:T(8,128)(2,1)S(1)}, bf16[64,1536]{1,0:T(8,128)(2,1)S(1)}, u32[]{:S(2)}, u32[]{:S(2)}) collective-permute-start(bf16[64,1536]{1,0:T(8,128)(2,1)S(1)} %get-tuple-element.27.refs_0_.refs_9_), channel_id=1, source_target_pairs={{0,2},{1,17},{2,0},{3,19},{4,6},{5,21},{6,4},{7,23},{8,10},{9,25},... | collective-permute-start | bytes 589832 | tf_op jit(solution)/shard_map/ppermute | solution.py:45
  17.4 1.4 %copy-start.2 = (bf16[512,1536]{1,0:T(8,128)(2,1)S(1)}, bf16[512,1536]{1,0:T(8,128)(2,1)}, u32[]{:S(2)}) copy-start(bf16[512,1536]{1,0:T(8,128)(2,1)} %latent.3) | copy-start | bytes 4718596
  18.8 5.5 %copy-start.3 = (bf16[512,1536]{1,0:T(8,128)(2,1)S(1)}, bf16[512,1536]{1,0:T(8,128)(2,1)}, u32[]{:S(2)}) copy-start(bf16[512,1536]{1,0:T(8,128)(2,1)} %latent.3) | copy-start | bytes 4718596
  20.3 6.2 %collective-permute-start.10 = (bf16[64,1536]{1,0:T(8,128)(2,1)S(1)}, bf16[64,1536]{1,0:T(8,128)(2,1)S(1)}, u32[]{:S(2)}, u32[]{:S(2)}) collective-permute-start(bf16[64,1536]{1,0:T(8,128)(2,1)S(1)} %get-tuple-element.30.refs_1_.refs_10_), channel_id=1, source_target_pairs={{0,16},{1,3},{2,18},{3,1},{4,20},{5,7},{6,22},{7,5},{8,24},{9,11},... | collective-permute-start | bytes 589832 | tf_op jit(solution)/shard_map/ppermute | solution.py:45
  20.6 6.3 %collective-permute-start.7 = (bf16[64,1536]{1,0:T(8,128)(2,1)S(1)}, bf16[64,1536]{1,0:T(8,128)(2,1)S(1)}, u32[]{:S(2)}, u32[]{:S(2)}) collective-permute-start(bf16[64,1536]{1,0:T(8,128)(2,1)S(1)} %get-tuple-element.30.refs_1_.refs_10_), channel_id=1, source_target_pairs={{0,2},{1,17},{2,0},{3,19},{4,6},{5,21},{6,4},{7,23},{8,10},{9,25},... | collective-permute-start | bytes 589832 | tf_op jit(solution)/shard_map/ppermute | solution.py:45
  21.9 6.0 %collective-permute-start.11 = (bf16[64,1536]{1,0:T(8,128)(2,1)S(1)}, bf16[64,1536]{1,0:T(8,128)(2,1)S(1)}, u32[]{:S(2)}, u32[]{:S(2)}) collective-permute-start(bf16[64,1536]{1,0:T(8,128)(2,1)S(1)} %get-tuple-element.32.refs_2_.refs_11_), channel_id=1, source_target_pairs={{0,16},{1,3},{2,18},{3,1},{4,20},{5,7},{6,22},{7,5},{8,24},{9,11},... | collective-permute-start | bytes 589832 | tf_op jit(solution)/shard_map/ppermute | solution.py:45
  23.8 11.4 %collective-permute-start.12 = (bf16[64,1536]{1,0:T(8,128)(2,1)S(1)}, bf16[64,1536]{1,0:T(8,128)(2,1)S(1)}, u32[]{:S(2)}, u32[]{:S(2)}) collective-permute-start(bf16[64,1536]{1,0:T(8,128)(2,1)S(1)} %get-tuple-element.34), channel_id=1, source_target_pairs={{0,16},{1,3},{2,18},{3,1},{4,20},{5,7},{6,22},{7,5},{8,24},{9,11},... | collective-permute-start | bytes 589832 | tf_op jit(solution)/shard_map/ppermute | solution.py:45
  23.8 9.6 %collective-permute-start.9 = (bf16[64,1536]{1,0:T(8,128)(2,1)S(1)}, bf16[64,1536]{1,0:T(8,128)(2,1)S(1)}, u32[]{:S(2)}, u32[]{:S(2)}) collective-permute-start(bf16[64,1536]{1,0:T(8,128)(2,1)S(1)} %get-tuple-element.34), channel_id=1, source_target_pairs={{0,4},{2,6},{4,12},{6,14},{8,0},{10,2},{12,8},{14,10},{1,5},{3,7},... | collective-permute-start | bytes 589832 | tf_op jit(solution)/shard_map/ppermute | solution.py:35
  27.9 7.2 %collective-permute-start.14 = (bf16[64,1536]{1,0:T(8,128)(2,1)S(1)}, bf16[64,1536]{1,0:T(8,128)(2,1)S(1)}, u32[]{:S(2)}, u32[]{:S(2)}) collective-permute-start(bf16[64,1536]{1,0:T(8,128)(2,1)S(1)} %get-tuple-element.41), channel_id=1, source_target_pairs={{0,2},{1,17},{2,0},{3,19},{4,6},{5,21},{6,4},{7,23},{8,10},{9,25},... | collective-permute-start | bytes 589832 | tf_op jit(solution)/shard_map/ppermute | solution.py:45
  30.1 6.5 %collective-permute-start.13 = (bf16[64,1536]{1,0:T(8,128)(2,1)S(1)}, bf16[64,1536]{1,0:T(8,128)(2,1)S(1)}, u32[]{:S(2)}, u32[]{:S(2)}) collective-permute-start(bf16[64,1536]{1,0:T(8,128)(2,1)S(1)} %get-tuple-element.40), channel_id=1, source_target_pairs={{0,2},{1,17},{2,0},{3,19},{4,6},{5,21},{6,4},{7,23},{8,10},{9,25},... | collective-permute-start | bytes 589832 | tf_op jit(solution)/shard_map/ppermute | solution.py:45
  30.2 3.2 %copy-start.4 = (bf16[1,1536,64]{1,2,0:T(8,128)(2,1)S(1)}, bf16[1,1536,64]{1,2,0:T(8,128)(2,1)}, u32[]{:S(2)}) copy-start(bf16[1,1536,64]{1,2,0:T(8,128)(2,1)} %param.8) | copy-start | bytes 589828
  35.1 6.7 %copy-start.5 = (bf16[1,64,1536]{2,1,0:T(8,128)(2,1)S(1)}, bf16[1,64,1536]{2,1,0:T(8,128)(2,1)}, u32[]{:S(2)}) copy-start(bf16[1,64,1536]{2,1,0:T(8,128)(2,1)} %param.9) | copy-start | bytes 589828
  37.2 4.5 %collective-permute-start.15 = (f32[512,128]{1,0:T(8,128)S(1)}, f32[512,128]{1,0:T(8,128)S(1)}, u32[]{:S(2)}, u32[]{:S(2)}) collective-permute-start(f32[512,128]{1,0:T(8,128)S(1)} %shard_map.66.refs_2_), channel_id=1, source_target_pairs={{0,1},{1,0},{2,3},{3,2},{4,5},{5,4},{6,7},{7,6},{8,9},{9,8},{10,11... | collective-permute-start | bytes 786440 | tf_op jit(solution)/shard_map/ppermute | solution.py:21

commit v15 on v14

--- a/solution.py
+++ b/solution.py
@@ -275,10 +275,13 @@
     )(shared_weight, row_ids, info)
     if routed:
         piece = jnp.where(holds_down, down, up)
-        line = {step: along_line(piece, shards, step) for step in (1, 3)}
+        line = {1: along_line(piece, shards, 1)}
         other = swap(latent, "tensor")
         down_beside, up_beside = neighbour(down, shards), neighbour(up, shards)
+        ready = token
         one, token = pack([(line[1], 0, rank)], token, down_beside)
+        back, _ = pack([(piece, 0, rank)], ready)
+        line[3] = along_line(back, shards, 3)
         line[2] = along_line(one, shards, 1)
         one_first, one_second = in_plane(one, shards, True), in_plane(one, shards, False)
         part_one, token = base(info, latent, other, shared_weight, [token], cuts[0], cuts[1])

time: 44.6 us -> 43.2 us (0.969)
  the two profiles are of different devices: /device:TPU:11 before, /device:TPU:0 now
where the time goes in v15:
time: 43.2 us; the launch traced here: 43 us
  starting transfers between devices  19.4 us (45%)
  Pallas kernels  12.7 us (29%)
  local copies, waits for them, and re-layouts  5.87 us (14%)
  waiting for transfers between devices  3.76 us (9%)
  other arithmetic  1.04 us (2%)
    ppermute x8, starting transfers between devices, in_plane(): return lax.ppermute(value, AXES, pairs)  9.26 us
    ppermute x4, starting transfers between devices, along_line(): lax.ppermute(value, 'shard', [(i, ring_step(i, step)) for i in range(shar...  7.62 us
    pallas_call x3, Pallas kernels, base(): pl.pallas_call(lambda *refs: base_kernel(*refs, skip=skip), out_shape=[ja...  7.02 us
    unnamed x14, local copies, waits for them, and re-layouts  5.79 us
    pallas_call x1, Pallas kernels, on_device(): pl.pallas_call(lambda *refs: up_kernel(*refs, base_parts=len(parts)), out...  2.61 us
    ppermute x2, starting transfers between devices, neighbour(): return lax.ppermute(value, 'shard', [(i, i ^ 1) for i in range(shards)])  2.03 us
    pallas_call x1, Pallas kernels, on_device(): call(down_first_kernel, lowrank, [SMEM] + [VMEM] * 13 + [ANY], 16, [pltpu...  1.68 us
    ppermute x2, waiting for transfers between devices, swap(): return lax.ppermute(value, axis, [(0, 1), (1, 0)])  1.52 us
  transfers between devices with their start and end apart: 16, of which 3 were waited for; matrix products, arithmetic and copies ran while one was open for 3% of the time, Pallas kernels for 22%

profile of v15, /device:TPU:0, one launch (start us, length us, event | category | flops | bytes accessed | tf_op | source)
XLA Modules:
  0.0 43.0 jit_solution(3520239489541962622)
XLA Ops:
  0.0 0.5 %collective-permute-start.3 = (bf16[512,1536]{1,0:T(8,128)(2,1)}, bf16[512,1536]{1,0:T(8,128)(2,1)S(1)}, u32[]{:S(2)}, u32[]{:S(2)}) collective-permute-start(bf16[512,1536]{1,0:T(8,128)(2,1)} %latent.3), channel_id=1, source_target_pairs={{0,1},{1,0},{2,3},{3,2},{4,5},{5,4},{6,7},{7,6},{8,9},{9,8},{10,11... | collective-permute-start | bytes 4718600 | tf_op jit(solution)/shard_map/ppermute | solution.py:21
  0.5 1.0 %broadcast_select_fusion.refs_0_ = bf16[64,1536]{1,0:T(8,128)(2,1)S(1)} fusion(pred[]{:T(512)S(6)} %eq.3, bf16[1,64,1536]{2,1,0:T(8,128)(2,1)} %param.9, bf16[1,1536,64]{1,2,0:T(8,128)(2,1)} %param.8), kind=kLoop, calls=%fused_computation | loop fusion | flops 98304 | bytes 589825 | tf_op jit(solution)/shard_map/jit(_where)/select_n | solution.py:277
  1.5 2.6 %collective-permute-start.1 = (bf16[64,1536]{1,0:T(8,128)(2,1)S(1)}, bf16[64,1536]{1,0:T(8,128)(2,1)S(1)}, u32[]{:S(2)}, u32[]{:S(2)}) collective-permute-start(bf16[64,1536]{1,0:T(8,128)(2,1)S(1)} %broadcast_select_fusion.refs_0_), channel_id=1, source_target_pairs={{0,4},{2,6},{4,12},{6,14},{8,0},{10,2},{12,8},{14,10},{1,5},{3,7},... | collective-permute-start | bytes 589832 | tf_op jit(solution)/shard_map/ppermute | solution.py:35
  4.1 1.5 %collective-permute-start = (bf16[64,1536]{1,0:T(8,128)(2,1)}, bf16[64,1536]{1,0:T(8,128)(2,1)S(1)}, u32[]{:S(2)}, u32[]{:S(2)}) collective-permute-start(bf16[64,1536]{1,0:T(8,128)(2,1)} %bitcast.17), channel_id=1, source_target_pairs={{0,2},{2,0},{4,6},{6,4},{8,10},{10,8},{12,14},{14,12},{1,3},{3,1},... | collective-permute-start | bytes 589832 | tf_op jit(solution)/shard_map/ppermute | solution.py:25
  5.6 0.5 %collective-permute-start.4 = (bf16[64,1536]{1,0:T(8,128)(2,1)}, bf16[64,1536]{1,0:T(8,128)(2,1)S(1)}, u32[]{:S(2)}, u32[]{:S(2)}) collective-permute-start(bf16[64,1536]{1,0:T(8,128)(2,1)} %bitcast.19), channel_id=1, source_target_pairs={{0,2},{2,0},{4,6},{6,4},{8,10},{10,8},{12,14},{14,12},{1,3},{3,1},... | collective-permute-start | bytes 589832 | tf_op jit(solution)/shard_map/ppermute | solution.py:25
  6.2 0.1 stack.47.refs_0_.info
  6.2 3.7 %copy-done = bf16[3072,1536]{1,0:T(8,128)(2,1)S(1)} copy-done((bf16[3072,1536]{1,0:T(8,128)(2,1)S(1)}, bf16[3072,1536]{1,0:T(8,128)(2,1)}, u32[]{:S(2)}) %copy-start) | copy-done | bytes 9437208
  9.9 0.7 %copy-done.6 = s32[512,1]{0,1:T(1,128)S(1)} copy-done((s32[512,1]{0,1:T(1,128)S(1)}, s32[512,1]{0,1:T(1,128)}, u32[]{:S(2)}) %copy-start.6) | copy-done | bytes 2072
  10.6 0.1 shard_map.55
  10.7 0.6 %shard_map.57 = (bf16[64,1536]{1,0:T(8,128)(2,1)S(1)}, f32[8,128]{1,0:T(8,128)}) custom-call(bf16[64,1536]{1,0:T(8,128)(2,1)S(1)} %broadcast_select_fusion.refs_0_, f32[8,128]{1,0:T(8,128)S(1)} %get-tuple-element.27.refs_1_), custom_call_target="tpu_custom_call" | custom-call | tf_op jit(solution)/shard_map/pallas_call | solution.py:82
  11.4 1.1 %collective-permute-start.2 = (bf16[64,1536]{1,0:T(8,128)(2,1)S(1)}, bf16[64,1536]{1,0:T(8,128)(2,1)S(1)}, u32[]{:S(2)}, u32[]{:S(2)}) collective-permute-start(bf16[64,1536]{1,0:T(8,128)(2,1)S(1)} %get-tuple-element.29), channel_id=1, source_target_pairs={{0,8},{2,10},{4,0},{6,2},{8,12},{10,14},{12,4},{14,6},{1,9},{3,11}... | collective-permute-start | bytes 589832 | tf_op jit(solution)/shard_map/ppermute | solution.py:35
  12.4 0.0 collective-permute-done.1.refs_0_
  12.4 0.0 collective-permute-done.refs_2_.beside
  12.5 2.3 %collective-permute-start.5 = (bf16[64,1536]{1,0:T(8,128)(2,1)S(1)}, bf16[64,1536]{1,0:T(8,128)(2,1)S(1)}, u32[]{:S(2)}, u32[]{:S(2)}) collective-permute-start(bf16[64,1536]{1,0:T(8,128)(2,1)S(1)} %get-tuple-element.28.refs_0_.refs_9_), channel_id=1, source_target_pairs={{0,4},{2,6},{4,12},{6,14},{8,0},{10,2},{12,8},{14,10},{1,5},{3,7},... | collective-permute-start | bytes 589832 | tf_op jit(solution)/shard_map/ppermute | solution.py:35
  14.7 1.5 %collective-permute-start.8 = (bf16[64,1536]{1,0:T(8,128)(2,1)S(1)}, bf16[64,1536]{1,0:T(8,128)(2,1)S(1)}, u32[]{:S(2)}, u32[]{:S(2)}) collective-permute-start(bf16[64,1536]{1,0:T(8,128)(2,1)S(1)} %get-tuple-element.28.refs_0_.refs_9_), channel_id=1, source_target_pairs={{0,16},{1,3},{2,18},{3,1},{4,20},{5,7},{6,22},{7,5},{8,24},{9,11},... | collective-permute-start | bytes 589832 | tf_op jit(solution)/shard_map/ppermute | solution.py:45
  16.2 0.0 collective-permute-done.3.refs_2_
  16.2 1.5 %collective-permute-start.6 = (bf16[64,1536]{1,0:T(8,128)(2,1)S(1)}, bf16[64,1536]{1,0:T(8,128)(2,1)S(1)}, u32[]{:S(2)}, u32[]{:S(2)}) collective-permute-start(bf16[64,1536]{1,0:T(8,128)(2,1)S(1)} %get-tuple-element.28.refs_0_.refs_9_), channel_id=1, source_target_pairs={{0,2},{1,17},{2,0},{3,19},{4,6},{5,21},{6,4},{7,23},{8,10},{9,25},... | collective-permute-start | bytes 589832 | tf_op jit(solution)/shard_map/ppermute | solution.py:45
  17.8 0.0 copy-done.1
  17.8 1.4 %copy-done.2 = bf16[512,1536]{1,0:T(8,128)(2,1)S(1)} copy-done((bf16[512,1536]{1,0:T(8,128)(2,1)S(1)}, bf16[512,1536]{1,0:T(8,128)(2,1)}, u32[]{:S(2)}) %copy-start.2) | copy-done | bytes 1572888
  19.2 1.5 %shard_map.58 = (f32[512,256]{1,0:T(8,128)S(1)}, f32[8,128]{1,0:T(8,128)S(1)}) custom-call(s32[10]{0:T(128)S(1)} %stack.47.refs_0_.info, bf16[512,1536]{1,0:T(8,128)(2,1)S(1)} %copy-done.2, bf16[512,1536]{1,0:T(8,128)(2,1)S(1)} %collective-permute-done.3.refs_2_, bf16[3072,1536]{1,0:T(8,128)(2,1)S(1)} %copy-done.1, f32[8,128]{1,0:T(8,128)S(1)} %get-tuple-element.30.refs_4_), custom_call_target="tpu_custom_call" | custom-call | flops 1000 | bytes 1000 | tf_op jit(solution)/shard_map/pallas_call | solution.py:199
  20.7 0.0 collective-permute-done.4.refs_2_.refs_8_
  20.7 0.0 collective-permute-done.2.refs_0_
  20.7 0.6 %collective-permute-start.10 = (bf16[64,1536]{1,0:T(8,128)(2,1)S(1)}, bf16[64,1536]{1,0:T(8,128)(2,1)S(1)}, u32[]{:S(2)}, u32[]{:S(2)}) collective-permute-start(bf16[64,1536]{1,0:T(8,128)(2,1)S(1)} %get-tuple-element.32.refs_1_.refs_10_), channel_id=1, source_target_pairs={{0,16},{1,3},{2,18},{3,1},{4,20},{5,7},{6,22},{7,5},{8,24},{9,11},... | collective-permute-start | bytes 589832 | tf_op jit(solution)/shard_map/ppermute | solution.py:45
  21.3 1.4 %collective-permute-start.7 = (bf16[64,1536]{1,0:T(8,128)(2,1)S(1)}, bf16[64,1536]{1,0:T(8,128)(2,1)S(1)}, u32[]{:S(2)}, u32[]{:S(2)}) collective-permute-start(bf16[64,1536]{1,0:T(8,128)(2,1)S(1)} %get-tuple-element.32.refs_1_.refs_10_), channel_id=1, source_target_pairs={{0,2},{1,17},{2,0},{3,19},{4,6},{5,21},{6,4},{7,23},{8,10},{9,25},... | collective-permute-start | bytes 589832 | tf_op jit(solution)/shard_map/ppermute | solution.py:45
  22.7 1.4 %collective-permute-done.5.refs_0_ = bf16[64,1536]{1,0:T(8,128)(2,1)S(1)} collective-permute-done((bf16[64,1536]{1,0:T(8,128)(2,1)S(1)}, bf16[64,1536]{1,0:T(8,128)(2,1)S(1)}, u32[]{:S(2)}, u32[]{:S(2)}) %collective-permute-start.5) | collective-permute-done | bytes 196640 | tf_op jit(solution)/shard_map/ppermute | solution.py:35
  24.1 1.6 %collective-permute-start.11 = (bf16[64,1536]{1,0:T(8,128)(2,1)S(1)}, bf16[64,1536]{1,0:T(8,128)(2,1)S(1)}, u32[]{:S(2)}, u32[]{:S(2)}) collective-permute-start(bf16[64,1536]{1,0:T(8,128)(2,1)S(1)} %get-tuple-element.34.refs_2_.refs_11_), channel_id=1, source_target_pairs={{0,16},{1,3},{2,18},{3,1},{4,20},{5,7},{6,22},{7,5},{8,24},{9,11},... | collective-permute-start | bytes 589832 | tf_op jit(solution)/shard_map/ppermute | solution.py:45
  25.7 0.0 collective-permute-done.8.refs_2_.refs_6_.refs_15_
  25.7 0.0 collective-permute-done.6.refs_0_.refs_3_.refs_12_
  25.7 0.6 %collective-permute-start.12 = (bf16[64,1536]{1,0:T(8,128)(2,1)S(1)}, bf16[64,1536]{1,0:T(8,128)(2,1)S(1)}, u32[]{:S(2)}, u32[]{:S(2)}) collective-permute-start(bf16[64,1536]{1,0:T(8,128)(2,1)S(1)} %get-tuple-element.36), channel_id=1, source_target_pairs={{0,16},{1,3},{2,18},{3,1},{4,20},{5,7},{6,22},{7,5},{8,24},{9,11},... | collective-permute-start | bytes 589832 | tf_op jit(solution)/shard_map/ppermute | solution.py:45
  26.3 1.6 %collective-permute-start.9 = (bf16[64,1536]{1,0:T(8,128)(2,1)S(1)}, bf16[64,1536]{1,0:T(8,128)(2,1)S(1)}, u32[]{:S(2)}, u32[]{:S(2)}) collective-permute-start(bf16[64,1536]{1,0:T(8,128)(2,1)S(1)} %get-tuple-element.36), channel_id=1, source_target_pairs={{0,4},{2,6},{4,12},{6,14},{8,0},{10,2},{12,8},{14,10},{1,5},{3,7},... | collective-permute-start | bytes 589832 | tf_op jit(solution)/shard_map/ppermute | solution.py:35
  28.0 0.0 copy-done.3
  28.0 2.3 %shard_map.62 = (f32[512,512]{1,0:T(8,128)S(1)}, f32[8,128]{1,0:T(8,128)S(1)}) custom-call(s32[10]{0:T(128)S(1)} %stack.47.refs_0_.info, bf16[512,1536]{1,0:T(8,128)(2,1)S(1)} %copy-done.3, bf16[512,1536]{1,0:T(8,128)(2,1)S(1)} %collective-permute-done.3.refs_2_, bf16[3072,1536]{1,0:T(8,128)(2,1)S(1)} %copy-done.1, f32[8,128]{1,0:T(8,128)S(1)} %get-tuple-element.37.refs_4_), custom_call_target="tpu_custom_call" | custom-call | flops 1000 | bytes 1000 | tf_op jit(solution)/shard_map/pallas_call | solution.py:199
  30.3 0.0 collective-permute-done.10.refs_0_.refs_7_.refs_16_
  30.3 0.0 collective-permute-done.7.refs_2_.refs_4_.refs_13_
  30.3 0.0 collective-permute-done.11.refs_0_.refs_8_.refs_17_
  30.4 1.1 %collective-permute-start.14 = (bf16[64,1536]{1,0:T(8,128)(2,1)S(1)}, bf16[64,1536]{1,0:T(8,128)(2,1)S(1)}, u32[]{:S(2)}, u32[]{:S(2)}) collective-permute-start(bf16[64,1536]{1,0:T(8,128)(2,1)S(1)} %get-tuple-element.43), channel_id=1, source_target_pairs={{0,2},{1,17},{2,0},{3,19},{4,6},{5,21},{6,4},{7,23},{8,10},{9,25},... | collective-permute-start | bytes 589832 | tf_op jit(solution)/shard_map/ppermute | solution.py:45
  31.5 1.0 %collective-permute-start.13 = (bf16[64,1536]{1,0:T(8,128)(2,1)S(1)}, bf16[64,1536]{1,0:T(8,128)(2,1)S(1)}, u32[]{:S(2)}, u32[]{:S(2)}) collective-permute-start(bf16[64,1536]{1,0:T(8,128)(2,1)S(1)} %get-tuple-element.42), channel_id=1, source_target_pairs={{0,2},{1,17},{2,0},{3,19},{4,6},{5,21},{6,4},{7,23},{8,10},{9,25},... | collective-permute-start | bytes 589832 | tf_op jit(solution)/shard_map/ppermute | solution.py:45
  32.5 3.2 %shard_map.65 = (f32[512,768]{1,0:T(8,128)S(1)}, f32[8,128]{1,0:T(8,128)S(1)}) custom-call(s32[10]{0:T(128)S(1)} %stack.47.refs_0_.info, bf16[512,1536]{1,0:T(8,128)(2,1)S(1)} %copy-done.3, bf16[512,1536]{1,0:T(8,128)(2,1)S(1)} %collective-permute-done.3.refs_2_, bf16[3072,1536]{1,0:T(8,128)(2,1)S(1)} %copy-done.1, f32[8,128]{1,0:T(8,128)S(1)} %get-tuple-element.40.refs_4_), custom_call_target="tpu_custom_call" | custom-call | flops 1000 | bytes 1000 | tf_op jit(solution)/shard_map/pallas_call | solution.py:199
  35.6 0.0 collective-permute-done.9.refs_5_.refs_14_
  35.7 1.7 %shard_map.66.earlier = f32[512,128]{1,0:T(8,128)S(1)} custom-call(s32[10]{0:T(128)S(1)} %stack.47.refs_0_.info, s32[512,128]{1,0:T(8,128)S(1)} %get-tuple-element.26.ids.refs_1_, bf16[512,1536]{1,0:T(8,128)(2,1)S(1)} %copy-done.3, bf16[64,1536]{1,0:T(8,128)(2,1)S(1)} %bitcast.18, bf16[64,1536]{1,0:T(8,128)(2,1)S(1)} %collective-permute-done.refs_2_.beside, ...), custom_call_target="tpu_custom_call" | custom-call | tf_op jit(solution)/shard_map/pallas_call | solution.py:305
  37.3 0.0 copy-start.5
  37.4 0.0 collective-permute-done.12.refs_0_.refs_18_
  37.4 0.0 collective-permute-done.14.refs_2_.refs_20_
  37.4 0.8 %collective-permute-done.13.refs_1_.refs_19_ = bf16[64,1536]{1,0:T(8,128)(2,1)S(1)} collective-permute-done((bf16[64,1536]{1,0:T(8,128)(2,1)S(1)}, bf16[64,1536]{1,0:T(8,128)(2,1)S(1)}, u32[]{:S(2)}, u32[]{:S(2)}) %collective-permute-start.13) | collective-permute-done | bytes 196640 | tf_op jit(solution)/shard_map/ppermute | solution.py:45
  38.2 0.6 %shard_map.67.refs_2_ = f32[512,128]{1,0:T(8,128)S(1)} custom-call(s32[10]{0:T(128)S(1)} %stack.47.refs_0_.info, s32[512,128]{1,0:T(8,128)S(1)} %get-tuple-element.26.ids.refs_1_, bf16[512,1536]{1,0:T(8,128)(2,1)S(1)} %copy-done.3, f32[512,128]{1,0:T(8,128)S(1)} %shard_map.66.earlier, bf16[64,1536]{1,0:T(8,128)(2,1)S(1)} %collective-permute-done.12.refs_0_.refs_18_, ...), custom_call_target="tpu_custom_call" | custom-call | tf_op jit(solution)/shard_map/pallas_call | solution.py:312
  38.8 0.1 collective-permute-start.15
  38.9 1.5 %collective-permute-done.15.refs_3_ = f32[512,128]{1,0:T(8,128)S(1)} collective-permute-done((f32[512,128]{1,0:T(8,128)S(1)}, f32[512,128]{1,0:T(8,128)S(1)}, u32[]{:S(2)}, u32[]{:S(2)}) %collective-permute-start.15) | collective-permute-done | bytes 262176 | tf_op jit(solution)/shard_map/ppermute | solution.py:21
  40.4 2.6 %shard_map.68 = bf16[512,1536]{1,0:T(8,128)(2,1)} custom-call(s32[10]{0:T(128)S(1)} %stack.47.refs_0_.info, s32[512,128]{1,0:T(8,128)S(1)} %get-tuple-element.26.ids.refs_1_, f32[512,128]{1,0:T(8,128)S(1)} %shard_map.67.refs_2_, f32[512,128]{1,0:T(8,128)S(1)} %collective-permute-done.15.refs_3_, f32[512,256]{1,0:T(8,128)S(1)} %get-tuple-element.44.refs_4_, ...), custom_call_target="tpu_custom_call" | custom-call | tf_op jit(solution)/shard_map/pallas_call | solution.py:332
  (14 shorter events, 0.1 us)
Async XLA Ops:
  0.0 16.2 %collective-permute-start.3 = (bf16[512,1536]{1,0:T(8,128)(2,1)}, bf16[512,1536]{1,0:T(8,128)(2,1)S(1)}, u32[]{:S(2)}, u32[]{:S(2)}) collective-permute-start(bf16[512,1536]{1,0:T(8,128)(2,1)} %latent.3), channel_id=1, source_target_pairs={{0,1},{1,0},{2,3},{3,2},{4,5},{5,4},{6,7},{7,6},{8,9},{9,8},{10,11... | collective-permute-start | bytes 4718600 | tf_op jit(solution)/shard_map/ppermute | solution.py:21
  1.5 10.9 %collective-permute-start.1 = (bf16[64,1536]{1,0:T(8,128)(2,1)S(1)}, bf16[64,1536]{1,0:T(8,128)(2,1)S(1)}, u32[]{:S(2)}, u32[]{:S(2)}) collective-permute-start(bf16[64,1536]{1,0:T(8,128)(2,1)S(1)} %broadcast_select_fusion.refs_0_), channel_id=1, source_target_pairs={{0,4},{2,6},{4,12},{6,14},{8,0},{10,2},{12,8},{14,10},{1,5},{3,7},... | collective-permute-start | bytes 589832 | tf_op jit(solution)/shard_map/ppermute | solution.py:35
  4.1 8.3 %collective-permute-start = (bf16[64,1536]{1,0:T(8,128)(2,1)}, bf16[64,1536]{1,0:T(8,128)(2,1)S(1)}, u32[]{:S(2)}, u32[]{:S(2)}) collective-permute-start(bf16[64,1536]{1,0:T(8,128)(2,1)} %bitcast.17), channel_id=1, source_target_pairs={{0,2},{2,0},{4,6},{6,4},{8,10},{10,8},{12,14},{14,12},{1,3},{3,1},... | collective-permute-start | bytes 589832 | tf_op jit(solution)/shard_map/ppermute | solution.py:25
  5.6 15.1 %collective-permute-start.4 = (bf16[64,1536]{1,0:T(8,128)(2,1)}, bf16[64,1536]{1,0:T(8,128)(2,1)S(1)}, u32[]{:S(2)}, u32[]{:S(2)}) collective-permute-start(bf16[64,1536]{1,0:T(8,128)(2,1)} %bitcast.19), channel_id=1, source_target_pairs={{0,2},{2,0},{4,6},{6,4},{8,10},{10,8},{12,14},{14,12},{1,3},{3,1},... | collective-permute-start | bytes 589832 | tf_op jit(solution)/shard_map/ppermute | solution.py:25
  6.2 3.7 %copy-start = (bf16[3072,1536]{1,0:T(8,128)(2,1)S(1)}, bf16[3072,1536]{1,0:T(8,128)(2,1)}, u32[]{:S(2)}) copy-start(bf16[3072,1536]{1,0:T(8,128)(2,1)} %refs_3_.5) | copy-start | bytes 28311556
  9.9 0.7 %copy-start.6 = (s32[512,1]{0,1:T(1,128)S(1)}, s32[512,1]{0,1:T(1,128)}, u32[]{:S(2)}) copy-start(s32[512,1]{0,1:T(1,128)} %param.6) | copy-start | bytes 6148
  10.6 7.1 %copy-start.1 = (bf16[3072,1536]{1,0:T(8,128)(2,1)S(1)}, bf16[3072,1536]{1,0:T(8,128)(2,1)}, u32[]{:S(2)}) copy-start(bf16[3072,1536]{1,0:T(8,128)(2,1)} %refs_3_.5) | copy-start | bytes 28311556
  11.4 9.4 %collective-permute-start.2 = (bf16[64,1536]{1,0:T(8,128)(2,1)S(1)}, bf16[64,1536]{1,0:T(8,128)(2,1)S(1)}, u32[]{:S(2)}, u32[]{:S(2)}) collective-permute-start(bf16[64,1536]{1,0:T(8,128)(2,1)S(1)} %get-tuple-element.29), channel_id=1, source_target_pairs={{0,8},{2,10},{4,0},{6,2},{8,12},{10,14},{12,4},{14,6},{1,9},{3,11}... | collective-permute-start | bytes 589832 | tf_op jit(solution)/shard_map/ppermute | solution.py:35
  12.5 11.6 %collective-permute-start.5 = (bf16[64,1536]{1,0:T(8,128)(2,1)S(1)}, bf16[64,1536]{1,0:T(8,128)(2,1)S(1)}, u32[]{:S(2)}, u32[]{:S(2)}) collective-permute-start(bf16[64,1536]{1,0:T(8,128)(2,1)S(1)} %get-tuple-element.28.refs_0_.refs_9_), channel_id=1, source_target_pairs={{0,4},{2,6},{4,12},{6,14},{8,0},{10,2},{12,8},{14,10},{1,5},{3,7},... | collective-permute-start | bytes 589832 | tf_op jit(solution)/shard_map/ppermute | solution.py:35
  14.7 11.0 %collective-permute-start.8 = (bf16[64,1536]{1,0:T(8,128)(2,1)S(1)}, bf16[64,1536]{1,0:T(8,128)(2,1)S(1)}, u32[]{:S(2)}, u32[]{:S(2)}) collective-permute-start(bf16[64,1536]{1,0:T(8,128)(2,1)S(1)} %get-tuple-element.28.refs_0_.refs_9_), channel_id=1, source_target_pairs={{0,16},{1,3},{2,18},{3,1},{4,20},{5,7},{6,22},{7,5},{8,24},{9,11},... | collective-permute-start | bytes 589832 | tf_op jit(solution)/shard_map/ppermute | solution.py:45
  16.2 9.5 %collective-permute-start.6 = (bf16[64,1536]{1,0:T(8,128)(2,1)S(1)}, bf16[64,1536]{1,0:T(8,128)(2,1)S(1)}, u32[]{:S(2)}, u32[]{:S(2)}) collective-permute-start(bf16[64,1536]{1,0:T(8,128)(2,1)S(1)} %get-tuple-element.28.refs_0_.refs_9_), channel_id=1, source_target_pairs={{0,2},{1,17},{2,0},{3,19},{4,6},{5,21},{6,4},{7,23},{8,10},{9,25},... | collective-permute-start | bytes 589832 | tf_op jit(solution)/shard_map/ppermute | solution.py:45
  17.8 1.4 %copy-start.2 = (bf16[512,1536]{1,0:T(8,128)(2,1)S(1)}, bf16[512,1536]{1,0:T(8,128)(2,1)}, u32[]{:S(2)}) copy-start(bf16[512,1536]{1,0:T(8,128)(2,1)} %latent.3) | copy-start | bytes 4718596
  19.2 8.8 %copy-start.3 = (bf16[512,1536]{1,0:T(8,128)(2,1)S(1)}, bf16[512,1536]{1,0:T(8,128)(2,1)}, u32[]{:S(2)}) copy-start(bf16[512,1536]{1,0:T(8,128)(2,1)} %latent.3) | copy-start | bytes 4718596
  20.7 9.6 %collective-permute-start.10 = (bf16[64,1536]{1,0:T(8,128)(2,1)S(1)}, bf16[64,1536]{1,0:T(8,128)(2,1)S(1)}, u32[]{:S(2)}, u32[]{:S(2)}) collective-permute-start(bf16[64,1536]{1,0:T(8,128)(2,1)S(1)} %get-tuple-element.32.refs_1_.refs_10_), channel_id=1, source_target_pairs={{0,16},{1,3},{2,18},{3,1},{4,20},{5,7},{6,22},{7,5},{8,24},{9,11},... | collective-permute-start | bytes 589832 | tf_op jit(solution)/shard_map/ppermute | solution.py:45
  21.3 9.0 %collective-permute-start.7 = (bf16[64,1536]{1,0:T(8,128)(2,1)S(1)}, bf16[64,1536]{1,0:T(8,128)(2,1)S(1)}, u32[]{:S(2)}, u32[]{:S(2)}) collective-permute-start(bf16[64,1536]{1,0:T(8,128)(2,1)S(1)} %get-tuple-element.32.refs_1_.refs_10_), channel_id=1, source_target_pairs={{0,2},{1,17},{2,0},{3,19},{4,6},{5,21},{6,4},{7,23},{8,10},{9,25},... | collective-permute-start | bytes 589832 | tf_op jit(solution)/shard_map/ppermute | solution.py:45
  24.1 6.2 %collective-permute-start.11 = (bf16[64,1536]{1,0:T(8,128)(2,1)S(1)}, bf16[64,1536]{1,0:T(8,128)(2,1)S(1)}, u32[]{:S(2)}, u32[]{:S(2)}) collective-permute-start(bf16[64,1536]{1,0:T(8,128)(2,1)S(1)} %get-tuple-element.34.refs_2_.refs_11_), channel_id=1, source_target_pairs={{0,16},{1,3},{2,18},{3,1},{4,20},{5,7},{6,22},{7,5},{8,24},{9,11},... | collective-permute-start | bytes 589832 | tf_op jit(solution)/shard_map/ppermute | solution.py:45
  25.7 11.7 %collective-permute-start.12 = (bf16[64,1536]{1,0:T(8,128)(2,1)S(1)}, bf16[64,1536]{1,0:T(8,128)(2,1)S(1)}, u32[]{:S(2)}, u32[]{:S(2)}) collective-permute-start(bf16[64,1536]{1,0:T(8,128)(2,1)S(1)} %get-tuple-element.36), channel_id=1, source_target_pairs={{0,16},{1,3},{2,18},{3,1},{4,20},{5,7},{6,22},{7,5},{8,24},{9,11},... | collective-permute-start | bytes 589832 | tf_op jit(solution)/shard_map/ppermute | solution.py:45
  26.3 9.3 %collective-permute-start.9 = (bf16[64,1536]{1,0:T(8,128)(2,1)S(1)}, bf16[64,1536]{1,0:T(8,128)(2,1)S(1)}, u32[]{:S(2)}, u32[]{:S(2)}) collective-permute-start(bf16[64,1536]{1,0:T(8,128)(2,1)S(1)} %get-tuple-element.36), channel_id=1, source_target_pairs={{0,4},{2,6},{4,12},{6,14},{8,0},{10,2},{12,8},{14,10},{1,5},{3,7},... | collective-permute-start | bytes 589832 | tf_op jit(solution)/shard_map/ppermute | solution.py:35
  30.4 7.0 %collective-permute-start.14 = (bf16[64,1536]{1,0:T(8,128)(2,1)S(1)}, bf16[64,1536]{1,0:T(8,128)(2,1)S(1)}, u32[]{:S(2)}, u32[]{:S(2)}) collective-permute-start(bf16[64,1536]{1,0:T(8,128)(2,1)S(1)} %get-tuple-element.43), channel_id=1, source_target_pairs={{0,2},{1,17},{2,0},{3,19},{4,6},{5,21},{6,4},{7,23},{8,10},{9,25},... | collective-permute-start | bytes 589832 | tf_op jit(solution)/shard_map/ppermute | solution.py:45
  31.5 6.7 %collective-permute-start.13 = (bf16[64,1536]{1,0:T(8,128)(2,1)S(1)}, bf16[64,1536]{1,0:T(8,128)(2,1)S(1)}, u32[]{:S(2)}, u32[]{:S(2)}) collective-permute-start(bf16[64,1536]{1,0:T(8,128)(2,1)S(1)} %get-tuple-element.42), channel_id=1, source_target_pairs={{0,2},{1,17},{2,0},{3,19},{4,6},{5,21},{6,4},{7,23},{8,10},{9,25},... | collective-permute-start | bytes 589832 | tf_op jit(solution)/shard_map/ppermute | solution.py:45
  32.5 3.2 %copy-start.4 = (bf16[1,1536,64]{1,2,0:T(8,128)(2,1)S(1)}, bf16[1,1536,64]{1,2,0:T(8,128)(2,1)}, u32[]{:S(2)}) copy-start(bf16[1,1536,64]{1,2,0:T(8,128)(2,1)} %param.8) | copy-start | bytes 589828
  37.3 3.0 %copy-start.5 = (bf16[1,64,1536]{2,1,0:T(8,128)(2,1)S(1)}, bf16[1,64,1536]{2,1,0:T(8,128)(2,1)}, u32[]{:S(2)}) copy-start(bf16[1,64,1536]{2,1,0:T(8,128)(2,1)} %param.9) | copy-start | bytes 589828
  38.8 1.6 %collective-permute-start.15 = (f32[512,128]{1,0:T(8,128)S(1)}, f32[512,128]{1,0:T(8,128)S(1)}, u32[]{:S(2)}, u32[]{:S(2)}) collective-permute-start(f32[512,128]{1,0:T(8,128)S(1)} %shard_map.67.refs_2_), channel_id=1, source_target_pairs={{0,1},{1,0},{2,3},{3,2},{4,5},{5,4},{6,7},{7,6},{8,9},{9,8},{10,11... | collective-permute-start | bytes 786440 | tf_op jit(solution)/shard_map/ppermute | solution.py:21

commit v16 on v15

--- a/solution.py
+++ b/solution.py
@@ -11,6 +11,7 @@
 TILE = 256
 AXES = ("replica", "shard", "tensor")
 FIRST_OWNER = 2
+COPY = 4 * MIB
 SMEM = pl.BlockSpec(memory_space=pltpu.SMEM)
 VMEM = pl.BlockSpec(memory_space=pltpu.VMEM)
 ANY = pl.BlockSpec(memory_space=pl.ANY)
@@ -84,6 +85,7 @@
         [jax.ShapeDtypeStruct((total, width), dtype), TOKEN],
         [VMEM] * count + [ANY] * len(after),
         4,
+        moved=COPY,
     )(*[array for array, _, _ in pieces], *after)
 
 
@@ -116,11 +118,13 @@
         stack[place : place + rank, :] = jnp.zeros((rank, stack.shape[1]), stack.dtype)
 
 
-def prepare_kernel(weight, row_ids, *refs):
-    spread, token = refs[-2:]
+def prepare_kernel(weight, *refs):
+    refs[-1][...] = weight[0:8, 0:128].astype(jnp.float32)
+
+
+def spread_rows(row_ids):
     wide = jnp.broadcast_to(row_ids[...].astype(jnp.float32), (128, row_ids.shape[1]))
-    spread[...] = wide.T.astype(jnp.int32)
-    token[...] = weight[0:8, 0:128].astype(jnp.float32)
+    return wide.T.astype(jnp.int32)
 
 
 def masked_products(info, ids, latent, stack, blocks, rank):
@@ -142,14 +146,16 @@
     return total
 
 
-def down_whole_kernel(info, ids, latent, stack, out):
+def down_whole_kernel(info, row_ids, latent, stack, out, ids):
+    ids[...] = spread_rows(row_ids)
     rank = out.shape[1] // 2
     blocks = range(stack.shape[0] // rank)
     out[...] = masked_products(info, ids, latent, stack, blocks, rank)
 
 
-def down_first_kernel(info, ids, latent, own, beside, *refs):
-    *received, _, out, stack = refs
+def down_first_kernel(info, row_ids, latent, own, beside, *refs):
+    *received, _, out, ids, stack = refs
+    ids[...] = spread_rows(row_ids)
     rank = own.shape[0]
     holds = info[1] == 1
     stack[0:rank, :] = own[...]
@@ -202,7 +208,11 @@
         in_specs=[SMEM, VMEM, VMEM, VMEM] + [ANY] * len(after),
         out_specs=[VMEM, VMEM],
         compiler_params=pltpu.CompilerParams(vmem_limit_bytes=24 * MIB),
-        cost_estimate=pl.CostEstimate(flops=1000, bytes_accessed=1000, transcendentals=0),
+        cost_estimate=pl.CostEstimate(
+            flops=4 * rows * latent.shape[1] * columns,
+            bytes_accessed=4 * rows * columns,
+            transcendentals=0,
+        ),
     )(info, latent, other, weight, *after)
 
 
@@ -254,7 +264,7 @@
     index, core = lax.axis_index("shard"), lax.axis_index("tensor")
     holds_down = core == lax.axis_index("replica")
     tiles = out_width // TILE
-    cuts = [0, out_width // 6, out_width // 2, out_width]
+    cuts = [0, out_width // 6, out_width]
     down = jnp.swapaxes(adapter_down_weight, 1, 2).reshape(local_adapters * rank, half_width)
     up = adapter_up_weight.reshape(local_adapters * rank, out_width)
     row_ids = row_adapter_index.reshape(1, rows)
@@ -267,12 +277,8 @@
     else:
         owners = list(range(adapters))
     info = jnp.stack([jnp.asarray(v, jnp.int32) for v in (core, holds_down, *owners)])
-    ids, token = call(
-        prepare_kernel,
-        [jax.ShapeDtypeStruct((rows, 2 * rank), jnp.int32), TOKEN],
-        [VMEM, VMEM, ANY],
-        16,
-    )(shared_weight, row_ids, info)
+    (token,) = call(prepare_kernel, [TOKEN], [VMEM, ANY], 16, moved=COPY)(shared_weight, info)
+    down_out = [lowrank, jax.ShapeDtypeStruct((rows, 2 * rank), jnp.int32)]
     if routed:
         piece = jnp.where(holds_down, down, up)
         line = {1: along_line(piece, shards, 1)}
@@ -292,23 +298,22 @@
         turn, token = pack([(one_first, 0, rank)], token, one_second)
         corner_one = in_plane(turn, shards, False)
         two_first = along_line(turn, shards, 1)
-        part_two, token = base(info, latent, other, shared_weight, [token], cuts[1], cuts[2])
         turn, token = pack([(three_second, 0, rank)], token, three_first)
         corner_three = in_plane(turn, shards, True)
         turn, token = pack([(two_second, 0, rank)], token)
         corner_two = in_plane(turn, shards, True)
-        part_three, token = base(info, latent, other, shared_weight, [token], cuts[2], cuts[3])
-        parts = [part_one, part_two, part_three]
+        part_two, token = base(info, latent, other, shared_weight, [token], cuts[1], cuts[2])
+        parts = [part_one, part_two]
         corners = [corner_one, corner_three, corner_two]
         received = [one, three, two, one_first, three_first, two_first]
         received += [one_second, three_second, two_second]
-        mine = call(
+        mine, ids = call(
             down_first_kernel,
-            lowrank,
+            down_out,
             [SMEM] + [VMEM] * 13 + [ANY],
             16,
             [pltpu.VMEM((columns, half_width), latent.dtype)],
-        )(info, ids, latent, down, down_beside, *received, token)
+        )(info, row_ids, latent, down, down_beside, *received, token)
         mine = call(
             down_last_kernel,
             lowrank,
@@ -323,8 +328,8 @@
         for begin, end in zip(cuts[:-1], cuts[1:]):
             part, token = base(info, latent, other, shared_weight, [token], begin, end)
             parts.append(part)
-        mine = call(down_whole_kernel, lowrank, [SMEM] + [VMEM] * 3, 48)(
-            info, ids, latent, lax.all_gather(down, "shard", axis=0, tiled=True)
+        mine, ids = call(down_whole_kernel, down_out, [SMEM] + [VMEM] * 3, 48)(
+            info, row_ids, latent, lax.all_gather(down, "shard", axis=0, tiled=True)
         )
         up_pieces = [lax.all_gather(up, "shard", axis=0, tiled=True)]
     theirs = swap(mine, "tensor")

time: 43.2 us -> 42.8 us (level)
  waiting for transfers between devices: 3.76 us -> 6.21 us
  starting transfers between devices: 19.4 us -> 18 us
  Pallas kernels: 12.7 us -> 12 us
  local copies, waits for them, and re-layouts: 5.87 us -> 5.2 us
    ppermute x8, waiting for transfers between devices: 0.85 us -> 2.54 us  [in_plane(): return lax.ppermute(value, AXES, pairs)]
    ppermute x8, starting transfers between devices: 9.26 us -> 8.38 us  [in_plane(): return lax.ppermute(value, AXES, pairs)]
    ppermute x4, waiting for transfers between devices: 1.38 us -> 2.13 us  [along_line(): lax.ppermute(value, 'shard', [(i, ring_step(i, step)) for i in range(shar...]
    pallas_call x3 -> x2, Pallas kernels: 7.02 us -> 6.31 us  [base(): pl.pallas_call(lambda *refs: base_kernel(*refs, skip=skip), out_shape=[ja...]
    unnamed x14, local copies, waits for them, and re-layouts: 5.79 us -> 5.11 us
  transfers between devices with their start and end apart: 16 -> 16, of which waited for: 3 -> 4; matrix products, arithmetic and copies ran while one was open for 3% -> 3% of each run, Pallas kernels for 22% -> 21%
where the time goes in v16:
time: 42.8 us; the launch traced here: 42.6 us
  starting transfers between devices  18 us (42%)
  Pallas kernels  12 us (28%)
  waiting for transfers between devices  6.21 us (15%)
  local copies, waits for them, and re-layouts  5.2 us (12%)
  other arithmetic  1.04 us (2%)
    ppermute x8, starting transfers between devices, in_plane(): return lax.ppermute(value, AXES, pairs)  8.38 us
    ppermute x4, starting transfers between devices, along_line(): lax.ppermute(value, 'shard', [(i, ring_step(i, step)) for i in range(shar...  7.35 us
    pallas_call x2, Pallas kernels, base(): pl.pallas_call(lambda *refs: base_kernel(*refs, skip=skip), out_shape=[ja...  6.31 us
    unnamed x14, local copies, waits for them, and re-layouts  5.11 us
    pallas_call x1, Pallas kernels, on_device(): pl.pallas_call(lambda *refs: up_kernel(*refs, base_parts=len(parts)), out...  2.6 us
    ppermute x8, waiting for transfers between devices, in_plane(): return lax.ppermute(value, AXES, pairs)  2.54 us
    ppermute x4, waiting for transfers between devices, along_line(): lax.ppermute(value, 'shard', [(i, ring_step(i, step)) for i in range(shar...  2.13 us
    pallas_call x1, Pallas kernels, on_device(): call(down_first_kernel, down_out, [SMEM] + [VMEM] * 13 + [ANY], 16, [pltp...  1.78 us
  transfers between devices with their start and end apart: 16, of which 4 were waited for; matrix products, arithmetic and copies ran while one was open for 3% of the time, Pallas kernels for 21%

profile of v16, /device:TPU:0, one launch (start us, length us, event | category | flops | bytes accessed | tf_op | source)
XLA Modules:
  0.0 42.6 jit_solution(17610271618063798485)
XLA Ops:
  0.0 0.5 %collective-permute-start.3 = (bf16[512,1536]{1,0:T(8,128)(2,1)}, bf16[512,1536]{1,0:T(8,128)(2,1)S(1)}, u32[]{:S(2)}, u32[]{:S(2)}) collective-permute-start(bf16[512,1536]{1,0:T(8,128)(2,1)} %latent.3), channel_id=1, source_target_pairs={{0,1},{1,0},{2,3},{3,2},{4,5},{5,4},{6,7},{7,6},{8,9},{9,8},{10,11... | collective-permute-start | bytes 4718600 | tf_op jit(solution)/shard_map/ppermute | solution.py:22
  0.5 1.0 %broadcast_select_fusion.refs_0_ = bf16[64,1536]{1,0:T(8,128)(2,1)S(1)} fusion(pred[]{:T(512)S(6)} %eq.3, bf16[1,64,1536]{2,1,0:T(8,128)(2,1)} %param.9, bf16[1,1536,64]{1,2,0:T(8,128)(2,1)} %param.8), kind=kLoop, calls=%fused_computation | loop fusion | flops 98304 | bytes 589825 | tf_op jit(solution)/shard_map/jit(_where)/select_n | solution.py:283
  1.5 2.6 %collective-permute-start.1 = (bf16[64,1536]{1,0:T(8,128)(2,1)S(1)}, bf16[64,1536]{1,0:T(8,128)(2,1)S(1)}, u32[]{:S(2)}, u32[]{:S(2)}) collective-permute-start(bf16[64,1536]{1,0:T(8,128)(2,1)S(1)} %broadcast_select_fusion.refs_0_), channel_id=1, source_target_pairs={{0,4},{2,6},{4,12},{6,14},{8,0},{10,2},{12,8},{14,10},{1,5},{3,7},... | collective-permute-start | bytes 589832 | tf_op jit(solution)/shard_map/ppermute | solution.py:36
  4.1 1.5 %collective-permute-start = (bf16[64,1536]{1,0:T(8,128)(2,1)}, bf16[64,1536]{1,0:T(8,128)(2,1)S(1)}, u32[]{:S(2)}, u32[]{:S(2)}) collective-permute-start(bf16[64,1536]{1,0:T(8,128)(2,1)} %bitcast.17), channel_id=1, source_target_pairs={{0,2},{2,0},{4,6},{6,4},{8,10},{10,8},{12,14},{14,12},{1,3},{3,1},... | collective-permute-start | bytes 589832 | tf_op jit(solution)/shard_map/ppermute | solution.py:26
  5.6 0.1 stack.47.refs_0_.info
  5.7 3.7 %copy-done = bf16[3072,1536]{1,0:T(8,128)(2,1)S(1)} copy-done((bf16[3072,1536]{1,0:T(8,128)(2,1)S(1)}, bf16[3072,1536]{1,0:T(8,128)(2,1)}, u32[]{:S(2)}) %copy-start) | copy-done | bytes 9437208
  9.4 0.6 %shard_map.57 = (bf16[64,1536]{1,0:T(8,128)(2,1)S(1)}, f32[8,128]{1,0:T(8,128)}) custom-call(bf16[64,1536]{1,0:T(8,128)(2,1)S(1)} %broadcast_select_fusion.refs_0_, f32[8,128]{1,0:T(8,128)S(1)} %shard_map.55.refs_1_), custom_call_target="tpu_custom_call" | custom-call | bytes 4194304 | tf_op jit(solution)/shard_map/pallas_call | solution.py:83
  10.0 1.3 %collective-permute-start.2 = (bf16[64,1536]{1,0:T(8,128)(2,1)S(1)}, bf16[64,1536]{1,0:T(8,128)(2,1)S(1)}, u32[]{:S(2)}, u32[]{:S(2)}) collective-permute-start(bf16[64,1536]{1,0:T(8,128)(2,1)S(1)} %get-tuple-element.25), channel_id=1, source_target_pairs={{0,8},{2,10},{4,0},{6,2},{8,12},{10,14},{12,4},{14,6},{1,9},{3,11}... | collective-permute-start | bytes 589832 | tf_op jit(solution)/shard_map/ppermute | solution.py:36
  11.4 0.0 copy-done.5
  11.4 0.2 collective-permute-start.4
  11.6 0.0 collective-permute-done.1.refs_0_
  11.6 0.0 collective-permute-done.refs_2_.beside
  11.7 2.4 %collective-permute-start.5 = (bf16[64,1536]{1,0:T(8,128)(2,1)S(1)}, bf16[64,1536]{1,0:T(8,128)(2,1)S(1)}, u32[]{:S(2)}, u32[]{:S(2)}) collective-permute-start(bf16[64,1536]{1,0:T(8,128)(2,1)S(1)} %get-tuple-element.24.refs_0_.refs_8_), channel_id=1, source_target_pairs={{0,4},{2,6},{4,12},{6,14},{8,0},{10,2},{12,8},{14,10},{1,5},{3,7},... | collective-permute-start | bytes 589832 | tf_op jit(solution)/shard_map/ppermute | solution.py:36
  14.0 1.5 %collective-permute-start.8 = (bf16[64,1536]{1,0:T(8,128)(2,1)S(1)}, bf16[64,1536]{1,0:T(8,128)(2,1)S(1)}, u32[]{:S(2)}, u32[]{:S(2)}) collective-permute-start(bf16[64,1536]{1,0:T(8,128)(2,1)S(1)} %get-tuple-element.24.refs_0_.refs_8_), channel_id=1, source_target_pairs={{0,16},{1,3},{2,18},{3,1},{4,20},{5,7},{6,22},{7,5},{8,24},{9,11},... | collective-permute-start | bytes 589832 | tf_op jit(solution)/shard_map/ppermute | solution.py:46
  15.5 0.0 collective-permute-done.3.refs_2_
  15.5 1.5 %collective-permute-start.6 = (bf16[64,1536]{1,0:T(8,128)(2,1)S(1)}, bf16[64,1536]{1,0:T(8,128)(2,1)S(1)}, u32[]{:S(2)}, u32[]{:S(2)}) collective-permute-start(bf16[64,1536]{1,0:T(8,128)(2,1)S(1)} %get-tuple-element.24.refs_0_.refs_8_), channel_id=1, source_target_pairs={{0,2},{1,17},{2,0},{3,19},{4,6},{5,21},{6,4},{7,23},{8,10},{9,25},... | collective-permute-start | bytes 589832 | tf_op jit(solution)/shard_map/ppermute | solution.py:46
  17.0 0.0 copy-done.1
  17.1 1.4 %copy-done.2 = bf16[512,1536]{1,0:T(8,128)(2,1)S(1)} copy-done((bf16[512,1536]{1,0:T(8,128)(2,1)S(1)}, bf16[512,1536]{1,0:T(8,128)(2,1)}, u32[]{:S(2)}) %copy-start.2) | copy-done | bytes 1572888
  18.5 1.5 %shard_map.58 = (f32[512,256]{1,0:T(8,128)S(1)}, f32[8,128]{1,0:T(8,128)S(1)}) custom-call(s32[10]{0:T(128)S(1)} %stack.47.refs_0_.info, bf16[512,1536]{1,0:T(8,128)(2,1)S(1)} %copy-done.2, bf16[512,1536]{1,0:T(8,128)(2,1)S(1)} %collective-permute-done.3.refs_2_, bf16[3072,1536]{1,0:T(8,128)(2,1)S(1)} %copy-done.1, f32[8,128]{1,0:T(8,128)S(1)} %get-tuple-element.26.refs_4_), custom_call_target="tpu_custom_call" | custom-call | flops 805306368 | bytes 524288 | tf_op jit(solution)/shard_map/pallas_call | solution.py:205
  20.0 0.0 copy-start.3
  20.0 0.0 collective-permute-done.2.refs_0_
  20.0 0.0 collective-permute-done.4.refs_2_.refs_7_
  20.0 0.7 %collective-permute-start.10 = (bf16[64,1536]{1,0:T(8,128)(2,1)S(1)}, bf16[64,1536]{1,0:T(8,128)(2,1)S(1)}, u32[]{:S(2)}, u32[]{:S(2)}) collective-permute-start(bf16[64,1536]{1,0:T(8,128)(2,1)S(1)} %get-tuple-element.28.refs_1_.refs_9_), channel_id=1, source_target_pairs={{0,16},{1,3},{2,18},{3,1},{4,20},{5,7},{6,22},{7,5},{8,24},{9,11},... | collective-permute-start | bytes 589832 | tf_op jit(solution)/shard_map/ppermute | solution.py:46
  20.8 0.4 collective-permute-start.7
  21.2 2.1 %collective-permute-done.5.refs_0_ = bf16[64,1536]{1,0:T(8,128)(2,1)S(1)} collective-permute-done((bf16[64,1536]{1,0:T(8,128)(2,1)S(1)}, bf16[64,1536]{1,0:T(8,128)(2,1)S(1)}, u32[]{:S(2)}, u32[]{:S(2)}) %collective-permute-start.5) | collective-permute-done | bytes 196640 | tf_op jit(solution)/shard_map/ppermute | solution.py:36
  23.3 1.6 %collective-permute-start.11 = (bf16[64,1536]{1,0:T(8,128)(2,1)S(1)}, bf16[64,1536]{1,0:T(8,128)(2,1)S(1)}, u32[]{:S(2)}, u32[]{:S(2)}) collective-permute-start(bf16[64,1536]{1,0:T(8,128)(2,1)S(1)} %get-tuple-element.30.refs_2_.refs_10_), channel_id=1, source_target_pairs={{0,16},{1,3},{2,18},{3,1},{4,20},{5,7},{6,22},{7,5},{8,24},{9,11},... | collective-permute-start | bytes 589832 | tf_op jit(solution)/shard_map/ppermute | solution.py:46
  24.9 0.0 collective-permute-done.8.refs_2_.refs_6_.refs_14_
  24.9 0.0 collective-permute-done.6.refs_0_.refs_3_.refs_11_
  24.9 0.6 %collective-permute-start.12 = (bf16[64,1536]{1,0:T(8,128)(2,1)S(1)}, bf16[64,1536]{1,0:T(8,128)(2,1)S(1)}, u32[]{:S(2)}, u32[]{:S(2)}) collective-permute-start(bf16[64,1536]{1,0:T(8,128)(2,1)S(1)} %get-tuple-element.32), channel_id=1, source_target_pairs={{0,16},{1,3},{2,18},{3,1},{4,20},{5,7},{6,22},{7,5},{8,24},{9,11},... | collective-permute-start | bytes 589832 | tf_op jit(solution)/shard_map/ppermute | solution.py:46
  25.5 1.0 %collective-permute-start.9 = (bf16[64,1536]{1,0:T(8,128)(2,1)S(1)}, bf16[64,1536]{1,0:T(8,128)(2,1)S(1)}, u32[]{:S(2)}, u32[]{:S(2)}) collective-permute-start(bf16[64,1536]{1,0:T(8,128)(2,1)S(1)} %get-tuple-element.32), channel_id=1, source_target_pairs={{0,4},{2,6},{4,12},{6,14},{8,0},{10,2},{12,8},{14,10},{1,5},{3,7},... | collective-permute-start | bytes 589832 | tf_op jit(solution)/shard_map/ppermute | solution.py:36
  26.5 0.0 collective-permute-done.10.refs_0_.refs_7_.refs_15_
  26.5 1.0 %collective-permute-done.7.refs_2_.refs_4_.refs_12_ = bf16[64,1536]{1,0:T(8,128)(2,1)S(1)} collective-permute-done((bf16[64,1536]{1,0:T(8,128)(2,1)S(1)}, bf16[64,1536]{1,0:T(8,128)(2,1)S(1)}, u32[]{:S(2)}, u32[]{:S(2)}) %collective-permute-start.7) | collective-permute-done | bytes 196640 | tf_op jit(solution)/shard_map/ppermute | solution.py:46
  27.5 1.5 %collective-permute-done.11.refs_0_.refs_8_.refs_16_ = bf16[64,1536]{1,0:T(8,128)(2,1)S(1)} collective-permute-done((bf16[64,1536]{1,0:T(8,128)(2,1)S(1)}, bf16[64,1536]{1,0:T(8,128)(2,1)S(1)}, u32[]{:S(2)}, u32[]{:S(2)}) %collective-permute-start.11) | collective-permute-done | bytes 196640 | tf_op jit(solution)/shard_map/ppermute | solution.py:46
  29.1 1.2 %collective-permute-start.14 = (bf16[64,1536]{1,0:T(8,128)(2,1)S(1)}, bf16[64,1536]{1,0:T(8,128)(2,1)S(1)}, u32[]{:S(2)}, u32[]{:S(2)}) collective-permute-start(bf16[64,1536]{1,0:T(8,128)(2,1)S(1)} %get-tuple-element.40), channel_id=1, source_target_pairs={{0,2},{1,17},{2,0},{3,19},{4,6},{5,21},{6,4},{7,23},{8,10},{9,25},... | collective-permute-start | bytes 589832 | tf_op jit(solution)/shard_map/ppermute | solution.py:46
  30.3 0.9 %collective-permute-start.13 = (bf16[64,1536]{1,0:T(8,128)(2,1)S(1)}, bf16[64,1536]{1,0:T(8,128)(2,1)S(1)}, u32[]{:S(2)}, u32[]{:S(2)}) collective-permute-start(bf16[64,1536]{1,0:T(8,128)(2,1)S(1)} %get-tuple-element.39), channel_id=1, source_target_pairs={{0,2},{1,17},{2,0},{3,19},{4,6},{5,21},{6,4},{7,23},{8,10},{9,25},... | collective-permute-start | bytes 589832 | tf_op jit(solution)/shard_map/ppermute | solution.py:46
  31.2 0.0 copy-done.3
  31.2 4.8 %shard_map.64 = (f32[512,1280]{1,0:T(8,128)S(1)}, f32[8,128]{1,0:T(8,128)S(1)}) custom-call(s32[10]{0:T(128)S(1)} %stack.47.refs_0_.info, bf16[512,1536]{1,0:T(8,128)(2,1)S(1)} %copy-done.3, bf16[512,1536]{1,0:T(8,128)(2,1)S(1)} %collective-permute-done.3.refs_2_, bf16[3072,1536]{1,0:T(8,128)(2,1)S(1)} %copy-done.1, f32[8,128]{1,0:T(8,128)S(1)} %get-tuple-element.35.refs_4_), custom_call_target="tpu_custom_call" | custom-call | flops 4026531840 | bytes 2621440 | tf_op jit(solution)/shard_map/pallas_call | solution.py:205
  36.0 0.0 collective-permute-done.9.refs_5_.refs_13_
  36.0 0.0 copy-done.4
  36.0 0.0 copy-done.6
  36.0 1.8 %shard_map.65 = (f32[512,128]{1,0:T(8,128)S(1)}, s32[512,128]{1,0:T(8,128)S(1)}) custom-call(s32[10]{0:T(128)S(1)} %stack.47.refs_0_.info, s32[1,512]{1,0:T(1,128)S(1)} %bitcast.21, bf16[512,1536]{1,0:T(8,128)(2,1)S(1)} %copy-done.3, bf16[64,1536]{1,0:T(8,128)(2,1)S(1)} %bitcast.18, bf16[64,1536]{1,0:T(8,128)(2,1)S(1)} %collective-permute-done.refs_2_.beside, ...), custom_call_target="tpu_custom_call" | custom-call | tf_op jit(solution)/shard_map/pallas_call | solution.py:310
  37.8 0.0 collective-permute-done.12.refs_0_.refs_17_
  37.8 0.0 collective-permute-done.14.refs_2_.refs_19_
  37.8 0.0 collective-permute-done.13.refs_1_.refs_18_
  37.8 0.6 %shard_map.66.refs_2_ = f32[512,128]{1,0:T(8,128)S(1)} custom-call(s32[10]{0:T(128)S(1)} %stack.47.refs_0_.info, s32[512,128]{1,0:T(8,128)S(1)} %get-tuple-element.37.ids.refs_1_, bf16[512,1536]{1,0:T(8,128)(2,1)S(1)} %copy-done.3, f32[512,128]{1,0:T(8,128)S(1)} %get-tuple-element.38.earlier, bf16[64,1536]{1,0:T(8,128)(2,1)S(1)} %collective-permute-done.12.refs_0_.refs_17_, ...), custom_call_target="tpu_custom_call" | custom-call | tf_op jit(solution)/shard_map/pallas_call | solution.py:317
  38.4 0.1 collective-permute-start.15
  38.5 1.5 %collective-permute-done.15.refs_3_ = f32[512,128]{1,0:T(8,128)S(1)} collective-permute-done((f32[512,128]{1,0:T(8,128)S(1)}, f32[512,128]{1,0:T(8,128)S(1)}, u32[]{:S(2)}, u32[]{:S(2)}) %collective-permute-start.15) | collective-permute-done | bytes 262176 | tf_op jit(solution)/shard_map/ppermute | solution.py:22
  40.0 2.6 %shard_map.67 = bf16[512,1536]{1,0:T(8,128)(2,1)} custom-call(s32[10]{0:T(128)S(1)} %stack.47.refs_0_.info, s32[512,128]{1,0:T(8,128)S(1)} %get-tuple-element.37.ids.refs_1_, f32[512,128]{1,0:T(8,128)S(1)} %shard_map.66.refs_2_, f32[512,128]{1,0:T(8,128)S(1)} %collective-permute-done.15.refs_3_, f32[512,256]{1,0:T(8,128)S(1)} %get-tuple-element.41.refs_4_, ...), custom_call_target="tpu_custom_call" | custom-call | tf_op jit(solution)/shard_map/pallas_call | solution.py:337
  (13 shorter events, 0.1 us)
Async XLA Ops:
  0.0 15.5 %collective-permute-start.3 = (bf16[512,1536]{1,0:T(8,128)(2,1)}, bf16[512,1536]{1,0:T(8,128)(2,1)S(1)}, u32[]{:S(2)}, u32[]{:S(2)}) collective-permute-start(bf16[512,1536]{1,0:T(8,128)(2,1)} %latent.3), channel_id=1, source_target_pairs={{0,1},{1,0},{2,3},{3,2},{4,5},{5,4},{6,7},{7,6},{8,9},{9,8},{10,11... | collective-permute-start | bytes 4718600 | tf_op jit(solution)/shard_map/ppermute | solution.py:22
  1.5 10.1 %collective-permute-start.1 = (bf16[64,1536]{1,0:T(8,128)(2,1)S(1)}, bf16[64,1536]{1,0:T(8,128)(2,1)S(1)}, u32[]{:S(2)}, u32[]{:S(2)}) collective-permute-start(bf16[64,1536]{1,0:T(8,128)(2,1)S(1)} %broadcast_select_fusion.refs_0_), channel_id=1, source_target_pairs={{0,4},{2,6},{4,12},{6,14},{8,0},{10,2},{12,8},{14,10},{1,5},{3,7},... | collective-permute-start | bytes 589832 | tf_op jit(solution)/shard_map/ppermute | solution.py:36
  4.1 7.5 %collective-permute-start = (bf16[64,1536]{1,0:T(8,128)(2,1)}, bf16[64,1536]{1,0:T(8,128)(2,1)S(1)}, u32[]{:S(2)}, u32[]{:S(2)}) collective-permute-start(bf16[64,1536]{1,0:T(8,128)(2,1)} %bitcast.17), channel_id=1, source_target_pairs={{0,2},{2,0},{4,6},{6,4},{8,10},{10,8},{12,14},{14,12},{1,3},{3,1},... | collective-permute-start | bytes 589832 | tf_op jit(solution)/shard_map/ppermute | solution.py:26
  5.7 3.7 %copy-start = (bf16[3072,1536]{1,0:T(8,128)(2,1)S(1)}, bf16[3072,1536]{1,0:T(8,128)(2,1)}, u32[]{:S(2)}) copy-start(bf16[3072,1536]{1,0:T(8,128)(2,1)} %refs_3_.3) | copy-start | bytes 28311556
  9.4 2.0 %copy-start.5 = (bf16[1,64,1536]{2,1,0:T(8,128)(2,1)S(1)}, bf16[1,64,1536]{2,1,0:T(8,128)(2,1)}, u32[]{:S(2)}) copy-start(bf16[1,64,1536]{2,1,0:T(8,128)(2,1)} %param.9) | copy-start | bytes 589828
  9.4 7.6 %copy-start.1 = (bf16[3072,1536]{1,0:T(8,128)(2,1)S(1)}, bf16[3072,1536]{1,0:T(8,128)(2,1)}, u32[]{:S(2)}) copy-start(bf16[3072,1536]{1,0:T(8,128)(2,1)} %refs_3_.3) | copy-start | bytes 28311556
  10.0 10.0 %collective-permute-start.2 = (bf16[64,1536]{1,0:T(8,128)(2,1)S(1)}, bf16[64,1536]{1,0:T(8,128)(2,1)S(1)}, u32[]{:S(2)}, u32[]{:S(2)}) collective-permute-start(bf16[64,1536]{1,0:T(8,128)(2,1)S(1)} %get-tuple-element.25), channel_id=1, source_target_pairs={{0,8},{2,10},{4,0},{6,2},{8,12},{10,14},{12,4},{14,6},{1,9},{3,11}... | collective-permute-start | bytes 589832 | tf_op jit(solution)/shard_map/ppermute | solution.py:36
  11.4 8.6 %collective-permute-start.4 = (bf16[64,1536]{1,0:T(8,128)(2,1)S(1)}, bf16[64,1536]{1,0:T(8,128)(2,1)S(1)}, u32[]{:S(2)}, u32[]{:S(2)}) collective-permute-start(bf16[64,1536]{1,0:T(8,128)(2,1)S(1)} %bitcast.19), channel_id=1, source_target_pairs={{0,2},{2,0},{4,6},{6,4},{8,10},{10,8},{12,14},{14,12},{1,3},{3,1},... | collective-permute-start | bytes 589832 | tf_op jit(solution)/shard_map/ppermute | solution.py:26
  11.7 11.6 %collective-permute-start.5 = (bf16[64,1536]{1,0:T(8,128)(2,1)S(1)}, bf16[64,1536]{1,0:T(8,128)(2,1)S(1)}, u32[]{:S(2)}, u32[]{:S(2)}) collective-permute-start(bf16[64,1536]{1,0:T(8,128)(2,1)S(1)} %get-tuple-element.24.refs_0_.refs_8_), channel_id=1, source_target_pairs={{0,4},{2,6},{4,12},{6,14},{8,0},{10,2},{12,8},{14,10},{1,5},{3,7},... | collective-permute-start | bytes 589832 | tf_op jit(solution)/shard_map/ppermute | solution.py:36
  14.0 10.8 %collective-permute-start.8 = (bf16[64,1536]{1,0:T(8,128)(2,1)S(1)}, bf16[64,1536]{1,0:T(8,128)(2,1)S(1)}, u32[]{:S(2)}, u32[]{:S(2)}) collective-permute-start(bf16[64,1536]{1,0:T(8,128)(2,1)S(1)} %get-tuple-element.24.refs_0_.refs_8_), channel_id=1, source_target_pairs={{0,16},{1,3},{2,18},{3,1},{4,20},{5,7},{6,22},{7,5},{8,24},{9,11},... | collective-permute-start | bytes 589832 | tf_op jit(solution)/shard_map/ppermute | solution.py:46
  15.5 9.3 %collective-permute-start.6 = (bf16[64,1536]{1,0:T(8,128)(2,1)S(1)}, bf16[64,1536]{1,0:T(8,128)(2,1)S(1)}, u32[]{:S(2)}, u32[]{:S(2)}) collective-permute-start(bf16[64,1536]{1,0:T(8,128)(2,1)S(1)} %get-tuple-element.24.refs_0_.refs_8_), channel_id=1, source_target_pairs={{0,2},{1,17},{2,0},{3,19},{4,6},{5,21},{6,4},{7,23},{8,10},{9,25},... | collective-permute-start | bytes 589832 | tf_op jit(solution)/shard_map/ppermute | solution.py:46
  17.1 1.4 %copy-start.2 = (bf16[512,1536]{1,0:T(8,128)(2,1)S(1)}, bf16[512,1536]{1,0:T(8,128)(2,1)}, u32[]{:S(2)}) copy-start(bf16[512,1536]{1,0:T(8,128)(2,1)} %latent.3) | copy-start | bytes 4718596
  20.0 11.2 %copy-start.3 = (bf16[512,1536]{1,0:T(8,128)(2,1)S(1)}, bf16[512,1536]{1,0:T(8,128)(2,1)}, u32[]{:S(2)}) copy-start(bf16[512,1536]{1,0:T(8,128)(2,1)} %latent.3) | copy-start | bytes 4718596
  20.0 6.5 %collective-permute-start.10 = (bf16[64,1536]{1,0:T(8,128)(2,1)S(1)}, bf16[64,1536]{1,0:T(8,128)(2,1)S(1)}, u32[]{:S(2)}, u32[]{:S(2)}) collective-permute-start(bf16[64,1536]{1,0:T(8,128)(2,1)S(1)} %get-tuple-element.28.refs_1_.refs_9_), channel_id=1, source_target_pairs={{0,16},{1,3},{2,18},{3,1},{4,20},{5,7},{6,22},{7,5},{8,24},{9,11},... | collective-permute-start | bytes 589832 | tf_op jit(solution)/shard_map/ppermute | solution.py:46
  20.8 6.7 %collective-permute-start.7 = (bf16[64,1536]{1,0:T(8,128)(2,1)S(1)}, bf16[64,1536]{1,0:T(8,128)(2,1)S(1)}, u32[]{:S(2)}, u32[]{:S(2)}) collective-permute-start(bf16[64,1536]{1,0:T(8,128)(2,1)S(1)} %get-tuple-element.28.refs_1_.refs_9_), channel_id=1, source_target_pairs={{0,2},{1,17},{2,0},{3,19},{4,6},{5,21},{6,4},{7,23},{8,10},{9,25},... | collective-permute-start | bytes 589832 | tf_op jit(solution)/shard_map/ppermute | solution.py:46
  23.3 5.7 %collective-permute-start.11 = (bf16[64,1536]{1,0:T(8,128)(2,1)S(1)}, bf16[64,1536]{1,0:T(8,128)(2,1)S(1)}, u32[]{:S(2)}, u32[]{:S(2)}) collective-permute-start(bf16[64,1536]{1,0:T(8,128)(2,1)S(1)} %get-tuple-element.30.refs_2_.refs_10_), channel_id=1, source_target_pairs={{0,16},{1,3},{2,18},{3,1},{4,20},{5,7},{6,22},{7,5},{8,24},{9,11},... | collective-permute-start | bytes 589832 | tf_op jit(solution)/shard_map/ppermute | solution.py:46
  24.9 12.9 %collective-permute-start.12 = (bf16[64,1536]{1,0:T(8,128)(2,1)S(1)}, bf16[64,1536]{1,0:T(8,128)(2,1)S(1)}, u32[]{:S(2)}, u32[]{:S(2)}) collective-permute-start(bf16[64,1536]{1,0:T(8,128)(2,1)S(1)} %get-tuple-element.32), channel_id=1, source_target_pairs={{0,16},{1,3},{2,18},{3,1},{4,20},{5,7},{6,22},{7,5},{8,24},{9,11},... | collective-permute-start | bytes 589832 | tf_op jit(solution)/shard_map/ppermute | solution.py:46
  25.5 10.5 %collective-permute-start.9 = (bf16[64,1536]{1,0:T(8,128)(2,1)S(1)}, bf16[64,1536]{1,0:T(8,128)(2,1)S(1)}, u32[]{:S(2)}, u32[]{:S(2)}) collective-permute-start(bf16[64,1536]{1,0:T(8,128)(2,1)S(1)} %get-tuple-element.32), channel_id=1, source_target_pairs={{0,4},{2,6},{4,12},{6,14},{8,0},{10,2},{12,8},{14,10},{1,5},{3,7},... | collective-permute-start | bytes 589832 | tf_op jit(solution)/shard_map/ppermute | solution.py:36
  29.1 8.7 %collective-permute-start.14 = (bf16[64,1536]{1,0:T(8,128)(2,1)S(1)}, bf16[64,1536]{1,0:T(8,128)(2,1)S(1)}, u32[]{:S(2)}, u32[]{:S(2)}) collective-permute-start(bf16[64,1536]{1,0:T(8,128)(2,1)S(1)} %get-tuple-element.40), channel_id=1, source_target_pairs={{0,2},{1,17},{2,0},{3,19},{4,6},{5,21},{6,4},{7,23},{8,10},{9,25},... | collective-permute-start | bytes 589832 | tf_op jit(solution)/shard_map/ppermute | solution.py:46
  30.3 7.5 %collective-permute-start.13 = (bf16[64,1536]{1,0:T(8,128)(2,1)S(1)}, bf16[64,1536]{1,0:T(8,128)(2,1)S(1)}, u32[]{:S(2)}, u32[]{:S(2)}) collective-permute-start(bf16[64,1536]{1,0:T(8,128)(2,1)S(1)} %get-tuple-element.39), channel_id=1, source_target_pairs={{0,2},{1,17},{2,0},{3,19},{4,6},{5,21},{6,4},{7,23},{8,10},{9,25},... | collective-permute-start | bytes 589832 | tf_op jit(solution)/shard_map/ppermute | solution.py:46
  31.2 4.8 %copy-start.4 = (bf16[1,1536,64]{1,2,0:T(8,128)(2,1)S(1)}, bf16[1,1536,64]{1,2,0:T(8,128)(2,1)}, u32[]{:S(2)}) copy-start(bf16[1,1536,64]{1,2,0:T(8,128)(2,1)} %param.8) | copy-start | bytes 589828
  31.2 4.8 %copy-start.6 = (s32[512,1]{0,1:T(1,128)S(1)}, s32[512,1]{0,1:T(1,128)}, u32[]{:S(2)}) copy-start(s32[512,1]{0,1:T(1,128)} %param.6) | copy-start | bytes 6148
  38.4 1.6 %collective-permute-start.15 = (f32[512,128]{1,0:T(8,128)S(1)}, f32[512,128]{1,0:T(8,128)S(1)}, u32[]{:S(2)}, u32[]{:S(2)}) collective-permute-start(f32[512,128]{1,0:T(8,128)S(1)} %shard_map.66.refs_2_), channel_id=1, source_target_pairs={{0,1},{1,0},{2,3},{3,2},{4,5},{5,4},{6,7},{7,6},{8,9},{9,8},{10,11... | collective-permute-start | bytes 786440 | tf_op jit(solution)/shard_map/ppermute | solution.py:22

commit v17 on v16

--- a/solution.py
+++ b/solution.py
@@ -11,7 +11,7 @@
 TILE = 256
 AXES = ("replica", "shard", "tensor")
 FIRST_OWNER = 2
-COPY = 4 * MIB
+COPY = 0
 SMEM = pl.BlockSpec(memory_space=pltpu.SMEM)
 VMEM = pl.BlockSpec(memory_space=pltpu.VMEM)
 ANY = pl.BlockSpec(memory_space=pl.ANY)
@@ -209,8 +209,8 @@
         out_specs=[VMEM, VMEM],
         compiler_params=pltpu.CompilerParams(vmem_limit_bytes=24 * MIB),
         cost_estimate=pl.CostEstimate(
-            flops=4 * rows * latent.shape[1] * columns,
-            bytes_accessed=4 * rows * columns,
+            flops=1000,
+            bytes_accessed=1000,
             transcendentals=0,
         ),
     )(info, latent, other, weight, *after)
@@ -264,7 +264,7 @@
     index, core = lax.axis_index("shard"), lax.axis_index("tensor")
     holds_down = core == lax.axis_index("replica")
     tiles = out_width // TILE
-    cuts = [0, out_width // 6, out_width]
+    cuts = [0, out_width // 3, out_width // 2, out_width]
     down = jnp.swapaxes(adapter_down_weight, 1, 2).reshape(local_adapters * rank, half_width)
     up = adapter_up_weight.reshape(local_adapters * rank, out_width)
     row_ids = row_adapter_index.reshape(1, rows)
@@ -285,25 +285,26 @@
         other = swap(latent, "tensor")
         down_beside, up_beside = neighbour(down, shards), neighbour(up, shards)
         ready = token
-        one, token = pack([(line[1], 0, rank)], token, down_beside)
+        one, token = pack([(line[1], 0, rank)], token, down_beside, other)
         back, _ = pack([(piece, 0, rank)], ready)
         line[3] = along_line(back, shards, 3)
         line[2] = along_line(one, shards, 1)
         one_first, one_second = in_plane(one, shards, True), in_plane(one, shards, False)
-        part_one, token = base(info, latent, other, shared_weight, [token], cuts[0], cuts[1])
         three, token = pack([(line[3], 0, rank)], token, up_beside)
         three_first, three_second = in_plane(three, shards, True), in_plane(three, shards, False)
+        part_one, token = base(info, latent, other, shared_weight, [token], cuts[0], cuts[1])
         two, token = pack([(line[2], 0, rank)], token)
         two_second = in_plane(two, shards, False)
         turn, token = pack([(one_first, 0, rank)], token, one_second)
         corner_one = in_plane(turn, shards, False)
         two_first = along_line(turn, shards, 1)
+        part_two, token = base(info, latent, other, shared_weight, [token], cuts[1], cuts[2])
         turn, token = pack([(three_second, 0, rank)], token, three_first)
         corner_three = in_plane(turn, shards, True)
         turn, token = pack([(two_second, 0, rank)], token)
         corner_two = in_plane(turn, shards, True)
-        part_two, token = base(info, latent, other, shared_weight, [token], cuts[1], cuts[2])
-        parts = [part_one, part_two]
+        part_three, token = base(info, latent, other, shared_weight, [token], cuts[2], cuts[3])
+        parts = [part_one, part_two, part_three]
         corners = [corner_one, corner_three, corner_two]
         received = [one, three, two, one_first, three_first, two_first]
         received += [one_second, three_second, two_second]

time: 42.8 us -> 42.4 us (level)
  starting transfers between devices: 18 us -> 20.2 us
  waiting for transfers between devices: 6.21 us -> 4.35 us
  local copies, waits for them, and re-layouts: 5.2 us -> 3.79 us
  Pallas kernels: 12 us -> 12.7 us
    ppermute x8, waiting for transfers between devices: 2.54 us -> 0.66 us  [in_plane(): return lax.ppermute(value, AXES, pairs)]
    unnamed x14 -> x12, local copies, waits for them, and re-layouts: 5.11 us -> 3.7 us
    ppermute x4, starting transfers between devices: 7.35 us -> 8.75 us  [along_line(): lax.ppermute(value, 'shard', [(i, ring_step(i, step)) for i in range(shar...]
    ppermute x2, waiting for transfers between devices: 0.01 us -> 0.85 us  [neighbour(): return lax.ppermute(value, 'shard', [(i, i ^ 1) for i in range(shards)])]
    ppermute x4, waiting for transfers between devices: 2.13 us -> 1.32 us  [along_line(): lax.ppermute(value, 'shard', [(i, ring_step(i, step)) for i in range(shar...]
    ppermute x8, starting transfers between devices: 8.38 us -> 9.12 us  [in_plane(): return lax.ppermute(value, AXES, pairs)]
    pallas_call x2 -> x3, Pallas kernels: 6.31 us -> 7.02 us  [base(): pl.pallas_call(lambda *refs: base_kernel(*refs, skip=skip), out_shape=[ja...]
  transfers between devices with their start and end apart: 16 -> 16, of which waited for: 4 -> 4; matrix products, arithmetic and copies ran while one was open for 3% -> 3% of each run, Pallas kernels for 21% -> 23%
where the time goes in v17:
time: 42.4 us; the launch traced here: 42.2 us
  starting transfers between devices  20.2 us (48%)
  Pallas kernels  12.7 us (30%)
  waiting for transfers between devices  4.35 us (10%)
  local copies, waits for them, and re-layouts  3.79 us (9%)
  other arithmetic  1.04 us (2%)
    ppermute x8, starting transfers between devices, in_plane(): return lax.ppermute(value, AXES, pairs)  9.12 us
    ppermute x4, starting transfers between devices, along_line(): lax.ppermute(value, 'shard', [(i, ring_step(i, step)) for i in range(shar...  8.75 us
    pallas_call x3, Pallas kernels, base(): pl.pallas_call(lambda *refs: base_kernel(*refs, skip=skip), out_shape=[ja...  7.02 us
    unnamed x12, local copies, waits for them, and re-layouts  3.7 us
    pallas_call x1, Pallas kernels, on_device(): pl.pallas_call(lambda *refs: up_kernel(*refs, base_parts=len(parts)), out...  2.61 us
    pallas_call x1, Pallas kernels, on_device(): call(down_first_kernel, down_out, [SMEM] + [VMEM] * 13 + [ANY], 16, [pltp...  1.78 us
    ppermute x2, starting transfers between devices, neighbour(): return lax.ppermute(value, 'shard', [(i, i ^ 1) for i in range(shards)])  1.77 us
    ppermute x2, waiting for transfers between devices, swap(): return lax.ppermute(value, axis, [(0, 1), (1, 0)])  1.52 us
  transfers between devices with their start and end apart: 16, of which 4 were waited for; matrix products, arithmetic and copies ran while one was open for 3% of the time, Pallas kernels for 23%

profile of v17, /device:TPU:0, one launch (start us, length us, event | category | flops | bytes accessed | tf_op | source)
XLA Modules:
  0.0 42.2 jit_solution(3839565917410935201)
XLA Ops:
  0.0 0.5 %collective-permute-start.2 = (bf16[512,1536]{1,0:T(8,128)(2,1)}, bf16[512,1536]{1,0:T(8,128)(2,1)S(1)}, u32[]{:S(2)}, u32[]{:S(2)}) collective-permute-start(bf16[512,1536]{1,0:T(8,128)(2,1)} %latent.3), channel_id=1, source_target_pairs={{0,1},{1,0},{2,3},{3,2},{4,5},{5,4},{6,7},{7,6},{8,9},{9,8},{10,11... | collective-permute-start | bytes 4718600 | tf_op jit(solution)/shard_map/ppermute | solution.py:22
  0.5 1.0 %broadcast_select_fusion.refs_0_ = bf16[64,1536]{1,0:T(8,128)(2,1)S(1)} fusion(pred[]{:T(512)S(6)} %eq.3, bf16[1,64,1536]{2,1,0:T(8,128)(2,1)} %param.9, bf16[1,1536,64]{1,2,0:T(8,128)(2,1)} %param.8), kind=kLoop, calls=%fused_computation | loop fusion | flops 98304 | bytes 589825 | tf_op jit(solution)/shard_map/jit(_where)/select_n | solution.py:283
  1.5 2.6 %collective-permute-start.1 = (bf16[64,1536]{1,0:T(8,128)(2,1)S(1)}, bf16[64,1536]{1,0:T(8,128)(2,1)S(1)}, u32[]{:S(2)}, u32[]{:S(2)}) collective-permute-start(bf16[64,1536]{1,0:T(8,128)(2,1)S(1)} %broadcast_select_fusion.refs_0_), channel_id=1, source_target_pairs={{0,4},{2,6},{4,12},{6,14},{8,0},{10,2},{12,8},{14,10},{1,5},{3,7},... | collective-permute-start | bytes 589832 | tf_op jit(solution)/shard_map/ppermute | solution.py:36
  4.1 1.5 %collective-permute-start = (bf16[64,1536]{1,0:T(8,128)(2,1)}, bf16[64,1536]{1,0:T(8,128)(2,1)S(1)}, u32[]{:S(2)}, u32[]{:S(2)}) collective-permute-start(bf16[64,1536]{1,0:T(8,128)(2,1)} %bitcast.17), channel_id=1, source_target_pairs={{0,2},{2,0},{4,6},{6,4},{8,10},{10,8},{12,14},{14,12},{1,3},{3,1},... | collective-permute-start | bytes 589832 | tf_op jit(solution)/shard_map/ppermute | solution.py:26
  5.6 0.1 stack.47.refs_0_.info
  5.7 0.0 copy-start
  5.7 3.7 %copy-done = bf16[3072,1536]{1,0:T(8,128)(2,1)S(1)} copy-done((bf16[3072,1536]{1,0:T(8,128)(2,1)S(1)}, bf16[3072,1536]{1,0:T(8,128)(2,1)}, u32[]{:S(2)}) %copy-start) | copy-done | bytes 9437208
  9.4 0.6 %shard_map.57 = (bf16[64,1536]{1,0:T(8,128)(2,1)S(1)}, f32[8,128]{1,0:T(8,128)}) custom-call(bf16[64,1536]{1,0:T(8,128)(2,1)S(1)} %broadcast_select_fusion.refs_0_, f32[8,128]{1,0:T(8,128)S(1)} %shard_map.55.refs_1_), custom_call_target="tpu_custom_call" | custom-call | tf_op jit(solution)/shard_map/pallas_call | solution.py:83
  10.0 1.3 %collective-permute-start.3 = (bf16[64,1536]{1,0:T(8,128)(2,1)S(1)}, bf16[64,1536]{1,0:T(8,128)(2,1)S(1)}, u32[]{:S(2)}, u32[]{:S(2)}) collective-permute-start(bf16[64,1536]{1,0:T(8,128)(2,1)S(1)} %get-tuple-element.27), channel_id=1, source_target_pairs={{0,8},{2,10},{4,0},{6,2},{8,12},{10,14},{12,4},{14,6},{1,9},{3,11}... | collective-permute-start | bytes 589832 | tf_op jit(solution)/shard_map/ppermute | solution.py:36
  11.4 0.0 copy-done.4
  11.4 0.2 collective-permute-start.4
  11.6 0.0 collective-permute-done.1.refs_0_
  11.6 0.0 collective-permute-done.refs_2_.beside
  11.6 0.0 collective-permute-done.2.refs_3_.refs_2_
  11.7 2.4 %collective-permute-start.5 = (bf16[64,1536]{1,0:T(8,128)(2,1)S(1)}, bf16[64,1536]{1,0:T(8,128)(2,1)S(1)}, u32[]{:S(2)}, u32[]{:S(2)}) collective-permute-start(bf16[64,1536]{1,0:T(8,128)(2,1)S(1)} %get-tuple-element.26.refs_0_.refs_9_), channel_id=1, source_target_pairs={{0,4},{2,6},{4,12},{6,14},{8,0},{10,2},{12,8},{14,10},{1,5},{3,7},... | collective-permute-start | bytes 589832 | tf_op jit(solution)/shard_map/ppermute | solution.py:36
  14.0 1.5 %collective-permute-start.8 = (bf16[64,1536]{1,0:T(8,128)(2,1)S(1)}, bf16[64,1536]{1,0:T(8,128)(2,1)S(1)}, u32[]{:S(2)}, u32[]{:S(2)}) collective-permute-start(bf16[64,1536]{1,0:T(8,128)(2,1)S(1)} %get-tuple-element.26.refs_0_.refs_9_), channel_id=1, source_target_pairs={{0,16},{1,3},{2,18},{3,1},{4,20},{5,7},{6,22},{7,5},{8,24},{9,11},... | collective-permute-start | bytes 589832 | tf_op jit(solution)/shard_map/ppermute | solution.py:46
  15.5 1.5 %collective-permute-start.6 = (bf16[64,1536]{1,0:T(8,128)(2,1)S(1)}, bf16[64,1536]{1,0:T(8,128)(2,1)S(1)}, u32[]{:S(2)}, u32[]{:S(2)}) collective-permute-start(bf16[64,1536]{1,0:T(8,128)(2,1)S(1)} %get-tuple-element.26.refs_0_.refs_9_), channel_id=1, source_target_pairs={{0,2},{1,17},{2,0},{3,19},{4,6},{5,21},{6,4},{7,23},{8,10},{9,25},... | collective-permute-start | bytes 589832 | tf_op jit(solution)/shard_map/ppermute | solution.py:46
  17.0 1.3 %collective-permute-done.3.refs_0_ = bf16[64,1536]{1,0:T(8,128)(2,1)S(1)} collective-permute-done((bf16[64,1536]{1,0:T(8,128)(2,1)S(1)}, bf16[64,1536]{1,0:T(8,128)(2,1)S(1)}, u32[]{:S(2)}, u32[]{:S(2)}) %collective-permute-start.3) | collective-permute-done | bytes 196640 | tf_op jit(solution)/shard_map/ppermute | solution.py:36
  18.4 0.8 %collective-permute-done.4.refs_2_.refs_8_ = bf16[64,1536]{1,0:T(8,128)(2,1)S(1)} collective-permute-done((bf16[64,1536]{1,0:T(8,128)(2,1)S(1)}, bf16[64,1536]{1,0:T(8,128)(2,1)S(1)}, u32[]{:S(2)}, u32[]{:S(2)}) %collective-permute-start.4) | collective-permute-done | bytes 196640 | tf_op jit(solution)/shard_map/ppermute | solution.py:26
  19.2 1.6 %collective-permute-start.10 = (bf16[64,1536]{1,0:T(8,128)(2,1)S(1)}, bf16[64,1536]{1,0:T(8,128)(2,1)S(1)}, u32[]{:S(2)}, u32[]{:S(2)}) collective-permute-start(bf16[64,1536]{1,0:T(8,128)(2,1)S(1)} %get-tuple-element.29.refs_1_.refs_10_), channel_id=1, source_target_pairs={{0,16},{1,3},{2,18},{3,1},{4,20},{5,7},{6,22},{7,5},{8,24},{9,11},... | collective-permute-start | bytes 589832 | tf_op jit(solution)/shard_map/ppermute | solution.py:46
  20.8 0.2 collective-permute-start.7
  21.0 0.0 copy-done.1
  21.0 0.0 copy-done.2
  21.0 2.3 %shard_map.59 = (f32[512,512]{1,0:T(8,128)S(1)}, f32[8,128]{1,0:T(8,128)S(1)}) custom-call(s32[10]{0:T(128)S(1)} %stack.47.refs_0_.info, bf16[512,1536]{1,0:T(8,128)(2,1)S(1)} %copy-done.2, bf16[512,1536]{1,0:T(8,128)(2,1)S(1)} %collective-permute-done.2.refs_3_.refs_2_, bf16[3072,1536]{1,0:T(8,128)(2,1)S(1)} %copy-done.1, ...), custom_call_target="tpu_custom_call" | custom-call | flops 1000 | bytes 1000 | tf_op jit(solution)/shard_map/pallas_call | solution.py:205
  23.4 0.0 collective-permute-done.5.refs_0_
  23.4 1.5 %collective-permute-start.11 = (bf16[64,1536]{1,0:T(8,128)(2,1)S(1)}, bf16[64,1536]{1,0:T(8,128)(2,1)S(1)}, u32[]{:S(2)}, u32[]{:S(2)}) collective-permute-start(bf16[64,1536]{1,0:T(8,128)(2,1)S(1)} %get-tuple-element.32.refs_2_.refs_11_), channel_id=1, source_target_pairs={{0,16},{1,3},{2,18},{3,1},{4,20},{5,7},{6,22},{7,5},{8,24},{9,11},... | collective-permute-start | bytes 589832 | tf_op jit(solution)/shard_map/ppermute | solution.py:46
  24.9 0.0 collective-permute-done.8.refs_2_.refs_6_.refs_15_
  24.9 0.0 collective-permute-done.6.refs_0_.refs_3_.refs_12_
  24.9 0.7 %collective-permute-start.12 = (bf16[64,1536]{1,0:T(8,128)(2,1)S(1)}, bf16[64,1536]{1,0:T(8,128)(2,1)S(1)}, u32[]{:S(2)}, u32[]{:S(2)}) collective-permute-start(bf16[64,1536]{1,0:T(8,128)(2,1)S(1)} %get-tuple-element.34), channel_id=1, source_target_pairs={{0,16},{1,3},{2,18},{3,1},{4,20},{5,7},{6,22},{7,5},{8,24},{9,11},... | collective-permute-start | bytes 589832 | tf_op jit(solution)/shard_map/ppermute | solution.py:46
  25.6 2.4 %collective-permute-start.9 = (bf16[64,1536]{1,0:T(8,128)(2,1)S(1)}, bf16[64,1536]{1,0:T(8,128)(2,1)S(1)}, u32[]{:S(2)}, u32[]{:S(2)}) collective-permute-start(bf16[64,1536]{1,0:T(8,128)(2,1)S(1)} %get-tuple-element.34), channel_id=1, source_target_pairs={{0,4},{2,6},{4,12},{6,14},{8,0},{10,2},{12,8},{14,10},{1,5},{3,7},... | collective-permute-start | bytes 589832 | tf_op jit(solution)/shard_map/ppermute | solution.py:36
  28.0 1.5 %shard_map.62 = (f32[512,256]{1,0:T(8,128)S(1)}, f32[8,128]{1,0:T(8,128)S(1)}) custom-call(s32[10]{0:T(128)S(1)} %stack.47.refs_0_.info, bf16[512,1536]{1,0:T(8,128)(2,1)S(1)} %copy-done.2, bf16[512,1536]{1,0:T(8,128)(2,1)S(1)} %collective-permute-done.2.refs_3_.refs_2_, bf16[3072,1536]{1,0:T(8,128)(2,1)S(1)} %copy-done.1, ...), custom_call_target="tpu_custom_call" | custom-call | flops 1000 | bytes 1000 | tf_op jit(solution)/shard_map/pallas_call | solution.py:205
  29.5 0.0 collective-permute-done.10.refs_0_.refs_7_.refs_16_
  29.5 0.0 collective-permute-done.7.refs_2_.refs_4_.refs_13_
  29.6 1.5 %collective-permute-start.13 = (bf16[64,1536]{1,0:T(8,128)(2,1)S(1)}, bf16[64,1536]{1,0:T(8,128)(2,1)S(1)}, u32[]{:S(2)}, u32[]{:S(2)}) collective-permute-start(bf16[64,1536]{1,0:T(8,128)(2,1)S(1)} %get-tuple-element.42), channel_id=1, source_target_pairs={{0,2},{1,17},{2,0},{3,19},{4,6},{5,21},{6,4},{7,23},{8,10},{9,25},... | collective-permute-start | bytes 589832 | tf_op jit(solution)/shard_map/ppermute | solution.py:46
  31.1 0.0 collective-permute-done.11.refs_0_.refs_8_.refs_17_
  31.1 0.6 %collective-permute-start.14 = (bf16[64,1536]{1,0:T(8,128)(2,1)S(1)}, bf16[64,1536]{1,0:T(8,128)(2,1)S(1)}, u32[]{:S(2)}, u32[]{:S(2)}) collective-permute-start(bf16[64,1536]{1,0:T(8,128)(2,1)S(1)} %get-tuple-element.43), channel_id=1, source_target_pairs={{0,2},{1,17},{2,0},{3,19},{4,6},{5,21},{6,4},{7,23},{8,10},{9,25},... | collective-permute-start | bytes 589832 | tf_op jit(solution)/shard_map/ppermute | solution.py:46
  31.7 3.2 %shard_map.65 = (f32[512,768]{1,0:T(8,128)S(1)}, f32[8,128]{1,0:T(8,128)S(1)}) custom-call(s32[10]{0:T(128)S(1)} %stack.47.refs_0_.info, bf16[512,1536]{1,0:T(8,128)(2,1)S(1)} %copy-done.2, bf16[512,1536]{1,0:T(8,128)(2,1)S(1)} %collective-permute-done.2.refs_3_.refs_2_, bf16[3072,1536]{1,0:T(8,128)(2,1)S(1)} %copy-done.1, ...), custom_call_target="tpu_custom_call" | custom-call | flops 1000 | bytes 1000 | tf_op jit(solution)/shard_map/pallas_call | solution.py:205
  34.9 0.0 collective-permute-done.9.refs_5_.refs_14_
  34.9 0.0 copy-done.3
  34.9 0.0 copy-done.5
  35.0 1.8 %shard_map.66 = (f32[512,128]{1,0:T(8,128)S(1)}, s32[512,128]{1,0:T(8,128)S(1)}) custom-call(s32[10]{0:T(128)S(1)} %stack.47.refs_0_.info, s32[1,512]{1,0:T(1,128)S(1)} %bitcast.21, bf16[512,1536]{1,0:T(8,128)(2,1)S(1)} %copy-done.2, bf16[64,1536]{1,0:T(8,128)(2,1)S(1)} %bitcast.18, bf16[64,1536]{1,0:T(8,128)(2,1)S(1)} %collective-permute-done.refs_2_.beside, ...), custom_call_target="tpu_custom_call" | custom-call | tf_op jit(solution)/shard_map/pallas_call | solution.py:311
  36.7 0.0 collective-permute-done.12.refs_0_.refs_18_
  36.8 0.0 collective-permute-done.13.refs_1_.refs_19_
  36.8 0.6 %collective-permute-done.14.refs_2_.refs_20_ = bf16[64,1536]{1,0:T(8,128)(2,1)S(1)} collective-permute-done((bf16[64,1536]{1,0:T(8,128)(2,1)S(1)}, bf16[64,1536]{1,0:T(8,128)(2,1)S(1)}, u32[]{:S(2)}, u32[]{:S(2)}) %collective-permute-start.14) | collective-permute-done | bytes 196640 | tf_op jit(solution)/shard_map/ppermute | solution.py:46
  37.4 0.6 %shard_map.67.refs_2_ = f32[512,128]{1,0:T(8,128)S(1)} custom-call(s32[10]{0:T(128)S(1)} %stack.47.refs_0_.info, s32[512,128]{1,0:T(8,128)S(1)} %get-tuple-element.40.ids.refs_1_, bf16[512,1536]{1,0:T(8,128)(2,1)S(1)} %copy-done.2, f32[512,128]{1,0:T(8,128)S(1)} %get-tuple-element.41.earlier, bf16[64,1536]{1,0:T(8,128)(2,1)S(1)} %collective-permute-done.12.refs_0_.refs_18_, ...), custom_call_target="tpu_custom_call" | custom-call | tf_op jit(solution)/shard_map/pallas_call | solution.py:318
  38.0 0.1 collective-permute-start.15
  38.1 1.5 %collective-permute-done.15.refs_3_ = f32[512,128]{1,0:T(8,128)S(1)} collective-permute-done((f32[512,128]{1,0:T(8,128)S(1)}, f32[512,128]{1,0:T(8,128)S(1)}, u32[]{:S(2)}, u32[]{:S(2)}) %collective-permute-start.15) | collective-permute-done | bytes 262176 | tf_op jit(solution)/shard_map/ppermute | solution.py:22
  39.6 2.6 %shard_map.68 = bf16[512,1536]{1,0:T(8,128)(2,1)} custom-call(s32[10]{0:T(128)S(1)} %stack.47.refs_0_.info, s32[512,128]{1,0:T(8,128)S(1)} %get-tuple-element.40.ids.refs_1_, f32[512,128]{1,0:T(8,128)S(1)} %shard_map.67.refs_2_, f32[512,128]{1,0:T(8,128)S(1)} %collective-permute-done.15.refs_3_, f32[512,512]{1,0:T(8,128)S(1)} %get-tuple-element.44.refs_4_, ...), custom_call_target="tpu_custom_call" | custom-call | tf_op jit(solution)/shard_map/pallas_call | solution.py:338
  (12 shorter events, 0.1 us)
Async XLA Ops:
  0.0 11.6 %collective-permute-start.2 = (bf16[512,1536]{1,0:T(8,128)(2,1)}, bf16[512,1536]{1,0:T(8,128)(2,1)S(1)}, u32[]{:S(2)}, u32[]{:S(2)}) collective-permute-start(bf16[512,1536]{1,0:T(8,128)(2,1)} %latent.3), channel_id=1, source_target_pairs={{0,1},{1,0},{2,3},{3,2},{4,5},{5,4},{6,7},{7,6},{8,9},{9,8},{10,11... | collective-permute-start | bytes 4718600 | tf_op jit(solution)/shard_map/ppermute | solution.py:22
  1.5 10.1 %collective-permute-start.1 = (bf16[64,1536]{1,0:T(8,128)(2,1)S(1)}, bf16[64,1536]{1,0:T(8,128)(2,1)S(1)}, u32[]{:S(2)}, u32[]{:S(2)}) collective-permute-start(bf16[64,1536]{1,0:T(8,128)(2,1)S(1)} %broadcast_select_fusion.refs_0_), channel_id=1, source_target_pairs={{0,4},{2,6},{4,12},{6,14},{8,0},{10,2},{12,8},{14,10},{1,5},{3,7},... | collective-permute-start | bytes 589832 | tf_op jit(solution)/shard_map/ppermute | solution.py:36
  4.1 7.5 %collective-permute-start = (bf16[64,1536]{1,0:T(8,128)(2,1)}, bf16[64,1536]{1,0:T(8,128)(2,1)S(1)}, u32[]{:S(2)}, u32[]{:S(2)}) collective-permute-start(bf16[64,1536]{1,0:T(8,128)(2,1)} %bitcast.17), channel_id=1, source_target_pairs={{0,2},{2,0},{4,6},{6,4},{8,10},{10,8},{12,14},{14,12},{1,3},{3,1},... | collective-permute-start | bytes 589832 | tf_op jit(solution)/shard_map/ppermute | solution.py:26
  5.7 3.7 %copy-start = (bf16[3072,1536]{1,0:T(8,128)(2,1)S(1)}, bf16[3072,1536]{1,0:T(8,128)(2,1)}, u32[]{:S(2)}) copy-start(bf16[3072,1536]{1,0:T(8,128)(2,1)} %refs_3_.5) | copy-start | bytes 28311556
  9.4 2.0 %copy-start.4 = (bf16[1,64,1536]{2,1,0:T(8,128)(2,1)S(1)}, bf16[1,64,1536]{2,1,0:T(8,128)(2,1)}, u32[]{:S(2)}) copy-start(bf16[1,64,1536]{2,1,0:T(8,128)(2,1)} %param.9) | copy-start | bytes 589828
  9.4 11.6 %copy-start.1 = (bf16[3072,1536]{1,0:T(8,128)(2,1)S(1)}, bf16[3072,1536]{1,0:T(8,128)(2,1)}, u32[]{:S(2)}) copy-start(bf16[3072,1536]{1,0:T(8,128)(2,1)} %refs_3_.5) | copy-start | bytes 28311556
  9.4 11.6 %copy-start.2 = (bf16[512,1536]{1,0:T(8,128)(2,1)S(1)}, bf16[512,1536]{1,0:T(8,128)(2,1)}, u32[]{:S(2)}) copy-start(bf16[512,1536]{1,0:T(8,128)(2,1)} %latent.3) | copy-start | bytes 4718596
  10.0 8.3 %collective-permute-start.3 = (bf16[64,1536]{1,0:T(8,128)(2,1)S(1)}, bf16[64,1536]{1,0:T(8,128)(2,1)S(1)}, u32[]{:S(2)}, u32[]{:S(2)}) collective-permute-start(bf16[64,1536]{1,0:T(8,128)(2,1)S(1)} %get-tuple-element.27), channel_id=1, source_target_pairs={{0,8},{2,10},{4,0},{6,2},{8,12},{10,14},{12,4},{14,6},{1,9},{3,11}... | collective-permute-start | bytes 589832 | tf_op jit(solution)/shard_map/ppermute | solution.py:36
  11.4 7.8 %collective-permute-start.4 = (bf16[64,1536]{1,0:T(8,128)(2,1)S(1)}, bf16[64,1536]{1,0:T(8,128)(2,1)S(1)}, u32[]{:S(2)}, u32[]{:S(2)}) collective-permute-start(bf16[64,1536]{1,0:T(8,128)(2,1)S(1)} %bitcast.19), channel_id=1, source_target_pairs={{0,2},{2,0},{4,6},{6,4},{8,10},{10,8},{12,14},{14,12},{1,3},{3,1},... | collective-permute-start | bytes 589832 | tf_op jit(solution)/shard_map/ppermute | solution.py:26
  11.7 11.7 %collective-permute-start.5 = (bf16[64,1536]{1,0:T(8,128)(2,1)S(1)}, bf16[64,1536]{1,0:T(8,128)(2,1)S(1)}, u32[]{:S(2)}, u32[]{:S(2)}) collective-permute-start(bf16[64,1536]{1,0:T(8,128)(2,1)S(1)} %get-tuple-element.26.refs_0_.refs_9_), channel_id=1, source_target_pairs={{0,4},{2,6},{4,12},{6,14},{8,0},{10,2},{12,8},{14,10},{1,5},{3,7},... | collective-permute-start | bytes 589832 | tf_op jit(solution)/shard_map/ppermute | solution.py:36
  14.0 10.9 %collective-permute-start.8 = (bf16[64,1536]{1,0:T(8,128)(2,1)S(1)}, bf16[64,1536]{1,0:T(8,128)(2,1)S(1)}, u32[]{:S(2)}, u32[]{:S(2)}) collective-permute-start(bf16[64,1536]{1,0:T(8,128)(2,1)S(1)} %get-tuple-element.26.refs_0_.refs_9_), channel_id=1, source_target_pairs={{0,16},{1,3},{2,18},{3,1},{4,20},{5,7},{6,22},{7,5},{8,24},{9,11},... | collective-permute-start | bytes 589832 | tf_op jit(solution)/shard_map/ppermute | solution.py:46
  15.5 9.4 %collective-permute-start.6 = (bf16[64,1536]{1,0:T(8,128)(2,1)S(1)}, bf16[64,1536]{1,0:T(8,128)(2,1)S(1)}, u32[]{:S(2)}, u32[]{:S(2)}) collective-permute-start(bf16[64,1536]{1,0:T(8,128)(2,1)S(1)} %get-tuple-element.26.refs_0_.refs_9_), channel_id=1, source_target_pairs={{0,2},{1,17},{2,0},{3,19},{4,6},{5,21},{6,4},{7,23},{8,10},{9,25},... | collective-permute-start | bytes 589832 | tf_op jit(solution)/shard_map/ppermute | solution.py:46
  19.2 10.3 %collective-permute-start.10 = (bf16[64,1536]{1,0:T(8,128)(2,1)S(1)}, bf16[64,1536]{1,0:T(8,128)(2,1)S(1)}, u32[]{:S(2)}, u32[]{:S(2)}) collective-permute-start(bf16[64,1536]{1,0:T(8,128)(2,1)S(1)} %get-tuple-element.29.refs_1_.refs_10_), channel_id=1, source_target_pairs={{0,16},{1,3},{2,18},{3,1},{4,20},{5,7},{6,22},{7,5},{8,24},{9,11},... | collective-permute-start | bytes 589832 | tf_op jit(solution)/shard_map/ppermute | solution.py:46
  20.8 8.8 %collective-permute-start.7 = (bf16[64,1536]{1,0:T(8,128)(2,1)S(1)}, bf16[64,1536]{1,0:T(8,128)(2,1)S(1)}, u32[]{:S(2)}, u32[]{:S(2)}) collective-permute-start(bf16[64,1536]{1,0:T(8,128)(2,1)S(1)} %get-tuple-element.29.refs_1_.refs_10_), channel_id=1, source_target_pairs={{0,2},{1,17},{2,0},{3,19},{4,6},{5,21},{6,4},{7,23},{8,10},{9,25},... | collective-permute-start | bytes 589832 | tf_op jit(solution)/shard_map/ppermute | solution.py:46
  23.4 7.7 %collective-permute-start.11 = (bf16[64,1536]{1,0:T(8,128)(2,1)S(1)}, bf16[64,1536]{1,0:T(8,128)(2,1)S(1)}, u32[]{:S(2)}, u32[]{:S(2)}) collective-permute-start(bf16[64,1536]{1,0:T(8,128)(2,1)S(1)} %get-tuple-element.32.refs_2_.refs_11_), channel_id=1, source_target_pairs={{0,16},{1,3},{2,18},{3,1},{4,20},{5,7},{6,22},{7,5},{8,24},{9,11},... | collective-permute-start | bytes 589832 | tf_op jit(solution)/shard_map/ppermute | solution.py:46
  24.9 11.8 %collective-permute-start.12 = (bf16[64,1536]{1,0:T(8,128)(2,1)S(1)}, bf16[64,1536]{1,0:T(8,128)(2,1)S(1)}, u32[]{:S(2)}, u32[]{:S(2)}) collective-permute-start(bf16[64,1536]{1,0:T(8,128)(2,1)S(1)} %get-tuple-element.34), channel_id=1, source_target_pairs={{0,16},{1,3},{2,18},{3,1},{4,20},{5,7},{6,22},{7,5},{8,24},{9,11},... | collective-permute-start | bytes 589832 | tf_op jit(solution)/shard_map/ppermute | solution.py:46
  25.6 9.3 %collective-permute-start.9 = (bf16[64,1536]{1,0:T(8,128)(2,1)S(1)}, bf16[64,1536]{1,0:T(8,128)(2,1)S(1)}, u32[]{:S(2)}, u32[]{:S(2)}) collective-permute-start(bf16[64,1536]{1,0:T(8,128)(2,1)S(1)} %get-tuple-element.34), channel_id=1, source_target_pairs={{0,4},{2,6},{4,12},{6,14},{8,0},{10,2},{12,8},{14,10},{1,5},{3,7},... | collective-permute-start | bytes 589832 | tf_op jit(solution)/shard_map/ppermute | solution.py:36
  29.6 7.2 %collective-permute-start.13 = (bf16[64,1536]{1,0:T(8,128)(2,1)S(1)}, bf16[64,1536]{1,0:T(8,128)(2,1)S(1)}, u32[]{:S(2)}, u32[]{:S(2)}) collective-permute-start(bf16[64,1536]{1,0:T(8,128)(2,1)S(1)} %get-tuple-element.42), channel_id=1, source_target_pairs={{0,2},{1,17},{2,0},{3,19},{4,6},{5,21},{6,4},{7,23},{8,10},{9,25},... | collective-permute-start | bytes 589832 | tf_op jit(solution)/shard_map/ppermute | solution.py:46
  31.1 6.3 %collective-permute-start.14 = (bf16[64,1536]{1,0:T(8,128)(2,1)S(1)}, bf16[64,1536]{1,0:T(8,128)(2,1)S(1)}, u32[]{:S(2)}, u32[]{:S(2)}) collective-permute-start(bf16[64,1536]{1,0:T(8,128)(2,1)S(1)} %get-tuple-element.43), channel_id=1, source_target_pairs={{0,2},{1,17},{2,0},{3,19},{4,6},{5,21},{6,4},{7,23},{8,10},{9,25},... | collective-permute-start | bytes 589832 | tf_op jit(solution)/shard_map/ppermute | solution.py:46
  31.7 3.2 %copy-start.3 = (bf16[1,1536,64]{1,2,0:T(8,128)(2,1)S(1)}, bf16[1,1536,64]{1,2,0:T(8,128)(2,1)}, u32[]{:S(2)}) copy-start(bf16[1,1536,64]{1,2,0:T(8,128)(2,1)} %param.8) | copy-start | bytes 589828
  31.7 3.2 %copy-start.5 = (s32[512,1]{0,1:T(1,128)S(1)}, s32[512,1]{0,1:T(1,128)}, u32[]{:S(2)}) copy-start(s32[512,1]{0,1:T(1,128)} %param.6) | copy-start | bytes 6148
  38.0 1.6 %collective-permute-start.15 = (f32[512,128]{1,0:T(8,128)S(1)}, f32[512,128]{1,0:T(8,128)S(1)}, u32[]{:S(2)}, u32[]{:S(2)}) collective-permute-start(f32[512,128]{1,0:T(8,128)S(1)} %shard_map.67.refs_2_), channel_id=1, source_target_pairs={{0,1},{1,0},{2,3},{3,2},{4,5},{5,4},{6,7},{7,6},{8,9},{9,8},{10,11... | collective-permute-start | bytes 786440 | tf_op jit(solution)/shard_map/ppermute | solution.py:22

commit v18 on v17

--- a/solution.py
+++ b/solution.py
@@ -264,7 +264,7 @@
     index, core = lax.axis_index("shard"), lax.axis_index("tensor")
     holds_down = core == lax.axis_index("replica")
     tiles = out_width // TILE
-    cuts = [0, out_width // 3, out_width // 2, out_width]
+    cuts = [0, out_width // 6, out_width // 2, out_width]
     down = jnp.swapaxes(adapter_down_weight, 1, 2).reshape(local_adapters * rank, half_width)
     up = adapter_up_weight.reshape(local_adapters * rank, out_width)
     row_ids = row_adapter_index.reshape(1, rows)
@@ -290,15 +290,15 @@
         line[3] = along_line(back, shards, 3)
         line[2] = along_line(one, shards, 1)
         one_first, one_second = in_plane(one, shards, True), in_plane(one, shards, False)
-        three, token = pack([(line[3], 0, rank)], token, up_beside)
+        part_one, token = base(info, latent, other, shared_weight, [token], cuts[0], cuts[1])
+        three, token = pack([(line[3], 0, rank)], token)
         three_first, three_second = in_plane(three, shards, True), in_plane(three, shards, False)
-        part_one, token = base(info, latent, other, shared_weight, [token], cuts[0], cuts[1])
+        part_two, token = base(info, latent, other, shared_weight, [token, up_beside], cuts[1], cuts[2])
         two, token = pack([(line[2], 0, rank)], token)
         two_second = in_plane(two, shards, False)
         turn, token = pack([(one_first, 0, rank)], token, one_second)
         corner_one = in_plane(turn, shards, False)
         two_first = along_line(turn, shards, 1)
-        part_two, token = base(info, latent, other, shared_weight, [token], cuts[1], cuts[2])
         turn, token = pack([(three_second, 0, rank)], token, three_first)
         corner_three = in_plane(turn, shards, True)
         turn, token = pack([(two_second, 0, rank)], token)

time: 42.4 us -> 42.2 us (level)
  the two profiles are of different devices: /device:TPU:0 before, /device:TPU:11 now
where the time goes in v18:
time: 42.2 us; the launch traced here: 42.1 us
  starting transfers between devices  15.3 us (36%)
  Pallas kernels  12.7 us (30%)
  waiting for transfers between devices  8.79 us (21%)
  local copies, waits for them, and re-layouts  4.1 us (10%)
  other arithmetic  1.04 us (2%)
    pallas_call x3, Pallas kernels, base(): pl.pallas_call(lambda *refs: base_kernel(*refs, skip=skip), out_shape=[ja...  7.03 us
    ppermute x8, waiting for transfers between devices, in_plane(): return lax.ppermute(value, AXES, pairs)  6.19 us
    ppermute x4, starting transfers between devices, along_line(): lax.ppermute(value, 'shard', [(i, ring_step(i, step)) for i in range(shar...  5.86 us
    ppermute x2, starting transfers between devices, swap(): return lax.ppermute(value, axis, [(0, 1), (1, 0)])  4.24 us
    unnamed x12, local copies, waits for them, and re-layouts  4.01 us
    ppermute x8, starting transfers between devices, in_plane(): return lax.ppermute(value, AXES, pairs)  3.73 us
    pallas_call x1, Pallas kernels, on_device(): pl.pallas_call(lambda *refs: up_kernel(*refs, base_parts=len(parts)), out...  2.61 us
    pallas_call x1, Pallas kernels, on_device(): call(down_first_kernel, down_out, [SMEM] + [VMEM] * 13 + [ANY], 16, [pltp...  1.78 us
  transfers between devices with their start and end apart: 16, of which 6 were waited for; matrix products, arithmetic and copies ran while one was open for 3% of the time, Pallas kernels for 23%

profile of v18, /device:TPU:11, one launch (start us, length us, event | category | flops | bytes accessed | tf_op | source)
XLA Modules:
  0.0 42.1 jit_solution(10689173747790271780)
XLA Ops:
  0.0 0.7 %collective-permute-start.2 = (bf16[512,1536]{1,0:T(8,128)(2,1)}, bf16[512,1536]{1,0:T(8,128)(2,1)S(1)}, u32[]{:S(2)}, u32[]{:S(2)}) collective-permute-start(bf16[512,1536]{1,0:T(8,128)(2,1)} %latent.3), channel_id=1, source_target_pairs={{0,1},{1,0},{2,3},{3,2},{4,5},{5,4},{6,7},{7,6},{8,9},{9,8},{10,11... | collective-permute-start | bytes 4718600 | tf_op jit(solution)/shard_map/ppermute | solution.py:22
  0.7 1.0 %broadcast_select_fusion.refs_0_ = bf16[64,1536]{1,0:T(8,128)(2,1)S(1)} fusion(pred[]{:T(512)S(6)} %eq.3, bf16[1,64,1536]{2,1,0:T(8,128)(2,1)} %param.9, bf16[1,1536,64]{1,2,0:T(8,128)(2,1)} %param.8), kind=kLoop, calls=%fused_computation | loop fusion | flops 98304 | bytes 589825 | tf_op jit(solution)/shard_map/jit(_where)/select_n | solution.py:283
  1.7 2.4 %collective-permute-start.1 = (bf16[64,1536]{1,0:T(8,128)(2,1)S(1)}, bf16[64,1536]{1,0:T(8,128)(2,1)S(1)}, u32[]{:S(2)}, u32[]{:S(2)}) collective-permute-start(bf16[64,1536]{1,0:T(8,128)(2,1)S(1)} %broadcast_select_fusion.refs_0_), channel_id=1, source_target_pairs={{0,4},{2,6},{4,12},{6,14},{8,0},{10,2},{12,8},{14,10},{1,5},{3,7},... | collective-permute-start | bytes 589832 | tf_op jit(solution)/shard_map/ppermute | solution.py:36
  4.1 1.2 %collective-permute-start = (bf16[64,1536]{1,0:T(8,128)(2,1)}, bf16[64,1536]{1,0:T(8,128)(2,1)S(1)}, u32[]{:S(2)}, u32[]{:S(2)}) collective-permute-start(bf16[64,1536]{1,0:T(8,128)(2,1)} %bitcast.17), channel_id=1, source_target_pairs={{0,2},{2,0},{4,6},{6,4},{8,10},{10,8},{12,14},{14,12},{1,3},{3,1},... | collective-permute-start | bytes 589832 | tf_op jit(solution)/shard_map/ppermute | solution.py:26
  5.3 0.1 stack.47.refs_0_.info
  5.4 3.7 %copy-done = bf16[3072,1536]{1,0:T(8,128)(2,1)S(1)} copy-done((bf16[3072,1536]{1,0:T(8,128)(2,1)S(1)}, bf16[3072,1536]{1,0:T(8,128)(2,1)}, u32[]{:S(2)}) %copy-start) | copy-done | bytes 9437208
  9.1 0.6 %shard_map.57 = (bf16[64,1536]{1,0:T(8,128)(2,1)S(1)}, f32[8,128]{1,0:T(8,128)}) custom-call(bf16[64,1536]{1,0:T(8,128)(2,1)S(1)} %broadcast_select_fusion.refs_0_, f32[8,128]{1,0:T(8,128)S(1)} %shard_map.55.refs_1_), custom_call_target="tpu_custom_call" | custom-call | tf_op jit(solution)/shard_map/pallas_call | solution.py:83
  9.7 0.0 collective-permute-start.3
  9.7 0.3 copy-done.4
  10.0 0.2 collective-permute-start.5
  10.3 0.0 collective-permute-done.1.refs_0_
  10.3 0.3 collective-permute-done.refs_2_.beside
  10.5 0.0 collective-permute-done.2.refs_3_.refs_2_
  10.5 1.9 %collective-permute-start.4 = (bf16[64,1536]{1,0:T(8,128)(2,1)S(1)}, bf16[64,1536]{1,0:T(8,128)(2,1)S(1)}, u32[]{:S(2)}, u32[]{:S(2)}) collective-permute-start(bf16[64,1536]{1,0:T(8,128)(2,1)S(1)} %get-tuple-element.26.refs_0_.refs_9_), channel_id=1, source_target_pairs={{0,4},{2,6},{4,12},{6,14},{8,0},{10,2},{12,8},{14,10},{1,5},{3,7},... | collective-permute-start | bytes 589832 | tf_op jit(solution)/shard_map/ppermute | solution.py:36
  12.4 1.2 %collective-permute-start.8 = (bf16[64,1536]{1,0:T(8,128)(2,1)S(1)}, bf16[64,1536]{1,0:T(8,128)(2,1)S(1)}, u32[]{:S(2)}, u32[]{:S(2)}) collective-permute-start(bf16[64,1536]{1,0:T(8,128)(2,1)S(1)} %get-tuple-element.26.refs_0_.refs_9_), channel_id=1, source_target_pairs={{0,16},{1,3},{2,18},{3,1},{4,20},{5,7},{6,22},{7,5},{8,24},{9,11},... | collective-permute-start | bytes 589832 | tf_op jit(solution)/shard_map/ppermute | solution.py:46
  13.6 0.3 collective-permute-start.6
  13.9 0.0 copy-done.1
  13.9 0.0 copy-done.2
  13.9 1.5 %shard_map.58 = (f32[512,256]{1,0:T(8,128)S(1)}, f32[8,128]{1,0:T(8,128)S(1)}) custom-call(s32[10]{0:T(128)S(1)} %stack.47.refs_0_.info, bf16[512,1536]{1,0:T(8,128)(2,1)S(1)} %copy-done.2, bf16[512,1536]{1,0:T(8,128)(2,1)S(1)} %collective-permute-done.2.refs_3_.refs_2_, bf16[3072,1536]{1,0:T(8,128)(2,1)S(1)} %copy-done.1, ...), custom_call_target="tpu_custom_call" | custom-call | flops 1000 | bytes 1000 | tf_op jit(solution)/shard_map/pallas_call | solution.py:205
  15.4 1.2 %collective-permute-done.3.refs_0_ = bf16[64,1536]{1,0:T(8,128)(2,1)S(1)} collective-permute-done((bf16[64,1536]{1,0:T(8,128)(2,1)S(1)}, bf16[64,1536]{1,0:T(8,128)(2,1)S(1)}, u32[]{:S(2)}, u32[]{:S(2)}) %collective-permute-start.3) | collective-permute-done | bytes 196640 | tf_op jit(solution)/shard_map/ppermute | solution.py:36
  16.6 0.2 collective-permute-start.10
  16.9 0.0 collective-permute-done.5.refs_5_.refs_8_
  16.9 0.3 collective-permute-start.7
  17.1 2.3 %shard_map.60 = (f32[512,512]{1,0:T(8,128)S(1)}, f32[8,128]{1,0:T(8,128)S(1)}) custom-call(s32[10]{0:T(128)S(1)} %stack.47.refs_0_.info, bf16[512,1536]{1,0:T(8,128)(2,1)S(1)} %copy-done.2, bf16[512,1536]{1,0:T(8,128)(2,1)S(1)} %collective-permute-done.2.refs_3_.refs_2_, bf16[3072,1536]{1,0:T(8,128)(2,1)S(1)} %copy-done.1, ...), custom_call_target="tpu_custom_call" | custom-call | flops 1000 | bytes 1000 | tf_op jit(solution)/shard_map/pallas_call | solution.py:205
  19.5 0.0 collective-permute-done.4.refs_0_
  19.5 1.4 %collective-permute-start.11 = (bf16[64,1536]{1,0:T(8,128)(2,1)S(1)}, bf16[64,1536]{1,0:T(8,128)(2,1)S(1)}, u32[]{:S(2)}, u32[]{:S(2)}) collective-permute-start(bf16[64,1536]{1,0:T(8,128)(2,1)S(1)} %get-tuple-element.33.refs_2_.refs_11_), channel_id=1, source_target_pairs={{0,16},{1,3},{2,18},{3,1},{4,20},{5,7},{6,22},{7,5},{8,24},{9,11},... | collective-permute-start | bytes 589832 | tf_op jit(solution)/shard_map/ppermute | solution.py:46
  20.8 0.0 collective-permute-done.8.refs_2_.refs_6_.refs_15_
  20.9 0.0 collective-permute-done.6.refs_0_.refs_3_.refs_12_
  20.9 0.2 collective-permute-start.12
  21.1 1.6 %collective-permute-start.9 = (bf16[64,1536]{1,0:T(8,128)(2,1)S(1)}, bf16[64,1536]{1,0:T(8,128)(2,1)S(1)}, u32[]{:S(2)}, u32[]{:S(2)}) collective-permute-start(bf16[64,1536]{1,0:T(8,128)(2,1)S(1)} %get-tuple-element.35), channel_id=1, source_target_pairs={{0,4},{2,6},{4,12},{6,14},{8,0},{10,2},{12,8},{14,10},{1,5},{3,7},... | collective-permute-start | bytes 589832 | tf_op jit(solution)/shard_map/ppermute | solution.py:36
  22.7 1.0 %collective-permute-done.10.refs_0_.refs_7_.refs_16_ = bf16[64,1536]{1,0:T(8,128)(2,1)S(1)} collective-permute-done((bf16[64,1536]{1,0:T(8,128)(2,1)S(1)}, bf16[64,1536]{1,0:T(8,128)(2,1)S(1)}, u32[]{:S(2)}, u32[]{:S(2)}) %collective-permute-start.10) | collective-permute-done | bytes 196640 | tf_op jit(solution)/shard_map/ppermute | solution.py:46
  23.7 0.0 collective-permute-done.7.refs_2_.refs_4_.refs_13_
  23.8 0.1 collective-permute-start.13
  23.8 3.7 %collective-permute-done.11.refs_0_.refs_8_.refs_17_ = bf16[64,1536]{1,0:T(8,128)(2,1)S(1)} collective-permute-done((bf16[64,1536]{1,0:T(8,128)(2,1)S(1)}, bf16[64,1536]{1,0:T(8,128)(2,1)S(1)}, u32[]{:S(2)}, u32[]{:S(2)}) %collective-permute-start.11) | collective-permute-done | bytes 196640 | tf_op jit(solution)/shard_map/ppermute | solution.py:46
  27.5 0.1 collective-permute-start.14
  27.6 0.0 copy-start.3
  27.6 0.0 copy-start.5
  27.6 3.2 %shard_map.65 = (f32[512,768]{1,0:T(8,128)S(1)}, f32[8,128]{1,0:T(8,128)S(1)}) custom-call(s32[10]{0:T(128)S(1)} %stack.47.refs_0_.info, bf16[512,1536]{1,0:T(8,128)(2,1)S(1)} %copy-done.2, bf16[512,1536]{1,0:T(8,128)(2,1)S(1)} %collective-permute-done.2.refs_3_.refs_2_, bf16[3072,1536]{1,0:T(8,128)(2,1)S(1)} %copy-done.1, ...), custom_call_target="tpu_custom_call" | custom-call | flops 1000 | bytes 1000 | tf_op jit(solution)/shard_map/pallas_call | solution.py:205
  30.8 0.0 collective-permute-done.9.refs_5_.refs_14_
  30.8 0.0 copy-done.3
  30.8 1.8 %shard_map.66 = (f32[512,128]{1,0:T(8,128)S(1)}, s32[512,128]{1,0:T(8,128)S(1)}) custom-call(s32[10]{0:T(128)S(1)} %stack.47.refs_0_.info, s32[1,512]{1,0:T(1,128)S(1)} %bitcast.21, bf16[512,1536]{1,0:T(8,128)(2,1)S(1)} %copy-done.2, bf16[64,1536]{1,0:T(8,128)(2,1)S(1)} %bitcast.18, bf16[64,1536]{1,0:T(8,128)(2,1)S(1)} %collective-permute-done.refs_2_.beside, ...), custom_call_target="tpu_custom_call" | custom-call | tf_op jit(solution)/shard_map/pallas_call | solution.py:311
  32.6 0.0 collective-permute-done.13.refs_1_.refs_19_
  32.6 0.0 collective-permute-done.12.refs_0_.refs_18_
  32.6 1.5 %collective-permute-done.14.refs_2_.refs_20_ = bf16[64,1536]{1,0:T(8,128)(2,1)S(1)} collective-permute-done((bf16[64,1536]{1,0:T(8,128)(2,1)S(1)}, bf16[64,1536]{1,0:T(8,128)(2,1)S(1)}, u32[]{:S(2)}, u32[]{:S(2)}) %collective-permute-start.14) | collective-permute-done | bytes 196640 | tf_op jit(solution)/shard_map/ppermute | solution.py:46
  34.2 0.6 %shard_map.67.refs_2_ = f32[512,128]{1,0:T(8,128)S(1)} custom-call(s32[10]{0:T(128)S(1)} %stack.47.refs_0_.info, s32[512,128]{1,0:T(8,128)S(1)} %get-tuple-element.40.ids.refs_1_, bf16[512,1536]{1,0:T(8,128)(2,1)S(1)} %copy-done.2, f32[512,128]{1,0:T(8,128)S(1)} %get-tuple-element.41.earlier, bf16[64,1536]{1,0:T(8,128)(2,1)S(1)} %collective-permute-done.12.refs_0_.refs_18_, ...), custom_call_target="tpu_custom_call" | custom-call | tf_op jit(solution)/shard_map/pallas_call | solution.py:318
  34.7 3.6 %collective-permute-start.15 = (f32[512,128]{1,0:T(8,128)S(1)}, f32[512,128]{1,0:T(8,128)S(1)}, u32[]{:S(2)}, u32[]{:S(2)}) collective-permute-start(f32[512,128]{1,0:T(8,128)S(1)} %shard_map.67.refs_2_), channel_id=1, source_target_pairs={{0,1},{1,0},{2,3},{3,2},{4,5},{5,4},{6,7},{7,6},{8,9},{9,8},{10,11... | collective-permute-start | bytes 786440 | tf_op jit(solution)/shard_map/ppermute | solution.py:22
  38.3 1.2 %collective-permute-done.15.refs_3_ = f32[512,128]{1,0:T(8,128)S(1)} collective-permute-done((f32[512,128]{1,0:T(8,128)S(1)}, f32[512,128]{1,0:T(8,128)S(1)}, u32[]{:S(2)}, u32[]{:S(2)}) %collective-permute-start.15) | collective-permute-done | bytes 262176 | tf_op jit(solution)/shard_map/ppermute | solution.py:22
  39.5 2.6 %shard_map.68 = bf16[512,1536]{1,0:T(8,128)(2,1)} custom-call(s32[10]{0:T(128)S(1)} %stack.47.refs_0_.info, s32[512,128]{1,0:T(8,128)S(1)} %get-tuple-element.40.ids.refs_1_, f32[512,128]{1,0:T(8,128)S(1)} %shard_map.67.refs_2_, f32[512,128]{1,0:T(8,128)S(1)} %collective-permute-done.15.refs_3_, f32[512,256]{1,0:T(8,128)S(1)} %get-tuple-element.44.refs_4_, ...), custom_call_target="tpu_custom_call" | custom-call | tf_op jit(solution)/shard_map/pallas_call | solution.py:338
  (12 shorter events, 0.1 us)
Async XLA Ops:
  0.0 10.5 %collective-permute-start.2 = (bf16[512,1536]{1,0:T(8,128)(2,1)}, bf16[512,1536]{1,0:T(8,128)(2,1)S(1)}, u32[]{:S(2)}, u32[]{:S(2)}) collective-permute-start(bf16[512,1536]{1,0:T(8,128)(2,1)} %latent.3), channel_id=1, source_target_pairs={{0,1},{1,0},{2,3},{3,2},{4,5},{5,4},{6,7},{7,6},{8,9},{9,8},{10,11... | collective-permute-start | bytes 4718600 | tf_op jit(solution)/shard_map/ppermute | solution.py:22
  1.7 8.5 %collective-permute-start.1 = (bf16[64,1536]{1,0:T(8,128)(2,1)S(1)}, bf16[64,1536]{1,0:T(8,128)(2,1)S(1)}, u32[]{:S(2)}, u32[]{:S(2)}) collective-permute-start(bf16[64,1536]{1,0:T(8,128)(2,1)S(1)} %broadcast_select_fusion.refs_0_), channel_id=1, source_target_pairs={{0,4},{2,6},{4,12},{6,14},{8,0},{10,2},{12,8},{14,10},{1,5},{3,7},... | collective-permute-start | bytes 589832 | tf_op jit(solution)/shard_map/ppermute | solution.py:36
  4.1 6.4 %collective-permute-start = (bf16[64,1536]{1,0:T(8,128)(2,1)}, bf16[64,1536]{1,0:T(8,128)(2,1)S(1)}, u32[]{:S(2)}, u32[]{:S(2)}) collective-permute-start(bf16[64,1536]{1,0:T(8,128)(2,1)} %bitcast.17), channel_id=1, source_target_pairs={{0,2},{2,0},{4,6},{6,4},{8,10},{10,8},{12,14},{14,12},{1,3},{3,1},... | collective-permute-start | bytes 589832 | tf_op jit(solution)/shard_map/ppermute | solution.py:26
  5.4 3.7 %copy-start = (bf16[3072,1536]{1,0:T(8,128)(2,1)S(1)}, bf16[3072,1536]{1,0:T(8,128)(2,1)}, u32[]{:S(2)}) copy-start(bf16[3072,1536]{1,0:T(8,128)(2,1)} %refs_3_.5) | copy-start | bytes 28311556
  9.1 0.9 %copy-start.4 = (bf16[1,64,1536]{2,1,0:T(8,128)(2,1)S(1)}, bf16[1,64,1536]{2,1,0:T(8,128)(2,1)}, u32[]{:S(2)}) copy-start(bf16[1,64,1536]{2,1,0:T(8,128)(2,1)} %param.9) | copy-start | bytes 589828
  9.1 4.8 %copy-start.1 = (bf16[3072,1536]{1,0:T(8,128)(2,1)S(1)}, bf16[3072,1536]{1,0:T(8,128)(2,1)}, u32[]{:S(2)}) copy-start(bf16[3072,1536]{1,0:T(8,128)(2,1)} %refs_3_.5) | copy-start | bytes 28311556
  9.1 4.8 %copy-start.2 = (bf16[512,1536]{1,0:T(8,128)(2,1)S(1)}, bf16[512,1536]{1,0:T(8,128)(2,1)}, u32[]{:S(2)}) copy-start(bf16[512,1536]{1,0:T(8,128)(2,1)} %latent.3) | copy-start | bytes 4718596
  9.7 6.9 %collective-permute-start.3 = (bf16[64,1536]{1,0:T(8,128)(2,1)S(1)}, bf16[64,1536]{1,0:T(8,128)(2,1)S(1)}, u32[]{:S(2)}, u32[]{:S(2)}) collective-permute-start(bf16[64,1536]{1,0:T(8,128)(2,1)S(1)} %get-tuple-element.27), channel_id=1, source_target_pairs={{0,8},{2,10},{4,0},{6,2},{8,12},{10,14},{12,4},{14,6},{1,9},{3,11}... | collective-permute-start | bytes 589832 | tf_op jit(solution)/shard_map/ppermute | solution.py:36
  10.0 6.8 %collective-permute-start.5 = (bf16[64,1536]{1,0:T(8,128)(2,1)S(1)}, bf16[64,1536]{1,0:T(8,128)(2,1)S(1)}, u32[]{:S(2)}, u32[]{:S(2)}) collective-permute-start(bf16[64,1536]{1,0:T(8,128)(2,1)S(1)} %bitcast.19), channel_id=1, source_target_pairs={{0,2},{2,0},{4,6},{6,4},{8,10},{10,8},{12,14},{14,12},{1,3},{3,1},... | collective-permute-start | bytes 589832 | tf_op jit(solution)/shard_map/ppermute | solution.py:26
  10.5 8.9 %collective-permute-start.4 = (bf16[64,1536]{1,0:T(8,128)(2,1)S(1)}, bf16[64,1536]{1,0:T(8,128)(2,1)S(1)}, u32[]{:S(2)}, u32[]{:S(2)}) collective-permute-start(bf16[64,1536]{1,0:T(8,128)(2,1)S(1)} %get-tuple-element.26.refs_0_.refs_9_), channel_id=1, source_target_pairs={{0,4},{2,6},{4,12},{6,14},{8,0},{10,2},{12,8},{14,10},{1,5},{3,7},... | collective-permute-start | bytes 589832 | tf_op jit(solution)/shard_map/ppermute | solution.py:36
  12.4 8.5 %collective-permute-start.8 = (bf16[64,1536]{1,0:T(8,128)(2,1)S(1)}, bf16[64,1536]{1,0:T(8,128)(2,1)S(1)}, u32[]{:S(2)}, u32[]{:S(2)}) collective-permute-start(bf16[64,1536]{1,0:T(8,128)(2,1)S(1)} %get-tuple-element.26.refs_0_.refs_9_), channel_id=1, source_target_pairs={{0,16},{1,3},{2,18},{3,1},{4,20},{5,7},{6,22},{7,5},{8,24},{9,11},... | collective-permute-start | bytes 589832 | tf_op jit(solution)/shard_map/ppermute | solution.py:46
  13.6 7.2 %collective-permute-start.6 = (bf16[64,1536]{1,0:T(8,128)(2,1)S(1)}, bf16[64,1536]{1,0:T(8,128)(2,1)S(1)}, u32[]{:S(2)}, u32[]{:S(2)}) collective-permute-start(bf16[64,1536]{1,0:T(8,128)(2,1)S(1)} %get-tuple-element.26.refs_0_.refs_9_), channel_id=1, source_target_pairs={{0,2},{1,17},{2,0},{3,19},{4,6},{5,21},{6,4},{7,23},{8,10},{9,25},... | collective-permute-start | bytes 589832 | tf_op jit(solution)/shard_map/ppermute | solution.py:46
  16.6 7.1 %collective-permute-start.10 = (bf16[64,1536]{1,0:T(8,128)(2,1)S(1)}, bf16[64,1536]{1,0:T(8,128)(2,1)S(1)}, u32[]{:S(2)}, u32[]{:S(2)}) collective-permute-start(bf16[64,1536]{1,0:T(8,128)(2,1)S(1)} %get-tuple-element.30.refs_1_.refs_10_), channel_id=1, source_target_pairs={{0,16},{1,3},{2,18},{3,1},{4,20},{5,7},{6,22},{7,5},{8,24},{9,11},... | collective-permute-start | bytes 589832 | tf_op jit(solution)/shard_map/ppermute | solution.py:46
  16.9 6.9 %collective-permute-start.7 = (bf16[64,1536]{1,0:T(8,128)(2,1)S(1)}, bf16[64,1536]{1,0:T(8,128)(2,1)S(1)}, u32[]{:S(2)}, u32[]{:S(2)}) collective-permute-start(bf16[64,1536]{1,0:T(8,128)(2,1)S(1)} %get-tuple-element.30.refs_1_.refs_10_), channel_id=1, source_target_pairs={{0,2},{1,17},{2,0},{3,19},{4,6},{5,21},{6,4},{7,23},{8,10},{9,25},... | collective-permute-start | bytes 589832 | tf_op jit(solution)/shard_map/ppermute | solution.py:46
  19.5 8.0 %collective-permute-start.11 = (bf16[64,1536]{1,0:T(8,128)(2,1)S(1)}, bf16[64,1536]{1,0:T(8,128)(2,1)S(1)}, u32[]{:S(2)}, u32[]{:S(2)}) collective-permute-start(bf16[64,1536]{1,0:T(8,128)(2,1)S(1)} %get-tuple-element.33.refs_2_.refs_11_), channel_id=1, source_target_pairs={{0,16},{1,3},{2,18},{3,1},{4,20},{5,7},{6,22},{7,5},{8,24},{9,11},... | collective-permute-start | bytes 589832 | tf_op jit(solution)/shard_map/ppermute | solution.py:46
  20.9 11.7 %collective-permute-start.12 = (bf16[64,1536]{1,0:T(8,128)(2,1)S(1)}, bf16[64,1536]{1,0:T(8,128)(2,1)S(1)}, u32[]{:S(2)}, u32[]{:S(2)}) collective-permute-start(bf16[64,1536]{1,0:T(8,128)(2,1)S(1)} %get-tuple-element.35), channel_id=1, source_target_pairs={{0,16},{1,3},{2,18},{3,1},{4,20},{5,7},{6,22},{7,5},{8,24},{9,11},... | collective-permute-start | bytes 589832 | tf_op jit(solution)/shard_map/ppermute | solution.py:46
  21.1 9.7 %collective-permute-start.9 = (bf16[64,1536]{1,0:T(8,128)(2,1)S(1)}, bf16[64,1536]{1,0:T(8,128)(2,1)S(1)}, u32[]{:S(2)}, u32[]{:S(2)}) collective-permute-start(bf16[64,1536]{1,0:T(8,128)(2,1)S(1)} %get-tuple-element.35), channel_id=1, source_target_pairs={{0,4},{2,6},{4,12},{6,14},{8,0},{10,2},{12,8},{14,10},{1,5},{3,7},... | collective-permute-start | bytes 589832 | tf_op jit(solution)/shard_map/ppermute | solution.py:36
  23.8 8.8 %collective-permute-start.13 = (bf16[64,1536]{1,0:T(8,128)(2,1)S(1)}, bf16[64,1536]{1,0:T(8,128)(2,1)S(1)}, u32[]{:S(2)}, u32[]{:S(2)}) collective-permute-start(bf16[64,1536]{1,0:T(8,128)(2,1)S(1)} %get-tuple-element.42), channel_id=1, source_target_pairs={{0,2},{1,17},{2,0},{3,19},{4,6},{5,21},{6,4},{7,23},{8,10},{9,25},... | collective-permute-start | bytes 589832 | tf_op jit(solution)/shard_map/ppermute | solution.py:46
  27.5 6.7 %collective-permute-start.14 = (bf16[64,1536]{1,0:T(8,128)(2,1)S(1)}, bf16[64,1536]{1,0:T(8,128)(2,1)S(1)}, u32[]{:S(2)}, u32[]{:S(2)}) collective-permute-start(bf16[64,1536]{1,0:T(8,128)(2,1)S(1)} %get-tuple-element.43), channel_id=1, source_target_pairs={{0,2},{1,17},{2,0},{3,19},{4,6},{5,21},{6,4},{7,23},{8,10},{9,25},... | collective-permute-start | bytes 589832 | tf_op jit(solution)/shard_map/ppermute | solution.py:46
  27.6 3.2 %copy-start.3 = (bf16[1,1536,64]{1,2,0:T(8,128)(2,1)S(1)}, bf16[1,1536,64]{1,2,0:T(8,128)(2,1)}, u32[]{:S(2)}) copy-start(bf16[1,1536,64]{1,2,0:T(8,128)(2,1)} %param.8) | copy-start | bytes 589828
  27.6 3.2 %copy-start.5 = (s32[512,1]{0,1:T(1,128)S(1)}, s32[512,1]{0,1:T(1,128)}, u32[]{:S(2)}) copy-start(s32[512,1]{0,1:T(1,128)} %param.6) | copy-start | bytes 6148
  34.7 4.7 %collective-permute-start.15 = (f32[512,128]{1,0:T(8,128)S(1)}, f32[512,128]{1,0:T(8,128)S(1)}, u32[]{:S(2)}, u32[]{:S(2)}) collective-permute-start(f32[512,128]{1,0:T(8,128)S(1)} %shard_map.67.refs_2_), channel_id=1, source_target_pairs={{0,1},{1,0},{2,3},{3,2},{4,5},{5,4},{6,7},{7,6},{8,9},{9,8},{10,11... | collective-permute-start | bytes 786440 | tf_op jit(solution)/shard_map/ppermute | solution.py:22

commit v19 on v18

--- a/solution.py
+++ b/solution.py
@@ -285,7 +285,7 @@
         other = swap(latent, "tensor")
         down_beside, up_beside = neighbour(down, shards), neighbour(up, shards)
         ready = token
-        one, token = pack([(line[1], 0, rank)], token, down_beside, other)
+        one, token = pack([(line[1], 0, rank)], token, down_beside, up_beside, other)
         back, _ = pack([(piece, 0, rank)], ready)
         line[3] = along_line(back, shards, 3)
         line[2] = along_line(one, shards, 1)
@@ -293,7 +293,7 @@
         part_one, token = base(info, latent, other, shared_weight, [token], cuts[0], cuts[1])
         three, token = pack([(line[3], 0, rank)], token)
         three_first, three_second = in_plane(three, shards, True), in_plane(three, shards, False)
-        part_two, token = base(info, latent, other, shared_weight, [token, up_beside], cuts[1], cuts[2])
+        part_two, token = base(info, latent, other, shared_weight, [token], cuts[1], cuts[2])
         two, token = pack([(line[2], 0, rank)], token)
         two_second = in_plane(two, shards, False)
         turn, token = pack([(one_first, 0, rank)], token, one_second)

time: 42.2 us -> 45.4 us (1.076)
  the two profiles are of different devices: /device:TPU:11 before, /device:TPU:0 now
where the time goes in v19:
time: 45.4 us; the launch traced here: 45.2 us
  starting transfers between devices  20.3 us (45%)
  Pallas kernels  12.6 us (28%)
  waiting for transfers between devices  7.29 us (16%)
  local copies, waits for them, and re-layouts  3.79 us (8%)
  other arithmetic  1.04 us (2%)
    ppermute x8, starting transfers between devices, in_plane(): return lax.ppermute(value, AXES, pairs)  10.4 us
    ppermute x4, starting transfers between devices, along_line(): lax.ppermute(value, 'shard', [(i, ring_step(i, step)) for i in range(shar...  7.34 us
    pallas_call x3, Pallas kernels, base(): pl.pallas_call(lambda *refs: base_kernel(*refs, skip=skip), out_shape=[ja...  7.02 us
    ppermute x2, waiting for transfers between devices, neighbour(): return lax.ppermute(value, 'shard', [(i, i ^ 1) for i in range(shards)])  3.95 us
    unnamed x12, local copies, waits for them, and re-layouts  3.7 us
    pallas_call x1, Pallas kernels, on_device(): pl.pallas_call(lambda *refs: up_kernel(*refs, base_parts=len(parts)), out...  2.58 us
    ppermute x2, starting transfers between devices, neighbour(): return lax.ppermute(value, 'shard', [(i, i ^ 1) for i in range(shards)])  2.03 us
    ppermute x8, waiting for transfers between devices, in_plane(): return lax.ppermute(value, AXES, pairs)  1.8 us
  transfers between devices with their start and end apart: 16, of which 5 were waited for; matrix products, arithmetic and copies ran while one was open for 2% of the time, Pallas kernels for 21%

profile of v19, /device:TPU:0, one launch (start us, length us, event | category | flops | bytes accessed | tf_op | source)
XLA Modules:
  0.0 45.2 jit_solution(10100737181410697886)
XLA Ops:
  0.0 0.5 %collective-permute-start.3 = (bf16[512,1536]{1,0:T(8,128)(2,1)}, bf16[512,1536]{1,0:T(8,128)(2,1)S(1)}, u32[]{:S(2)}, u32[]{:S(2)}) collective-permute-start(bf16[512,1536]{1,0:T(8,128)(2,1)} %latent.3), channel_id=1, source_target_pairs={{0,1},{1,0},{2,3},{3,2},{4,5},{5,4},{6,7},{7,6},{8,9},{9,8},{10,11... | collective-permute-start | bytes 4718600 | tf_op jit(solution)/shard_map/ppermute | solution.py:22
  0.5 1.0 %broadcast_select_fusion.refs_0_ = bf16[64,1536]{1,0:T(8,128)(2,1)S(1)} fusion(pred[]{:T(512)S(6)} %eq.3, bf16[1,64,1536]{2,1,0:T(8,128)(2,1)} %param.9, bf16[1,1536,64]{1,2,0:T(8,128)(2,1)} %param.8), kind=kLoop, calls=%fused_computation | loop fusion | flops 98304 | bytes 589825 | tf_op jit(solution)/shard_map/jit(_where)/select_n | solution.py:283
  1.5 2.6 %collective-permute-start.1 = (bf16[64,1536]{1,0:T(8,128)(2,1)S(1)}, bf16[64,1536]{1,0:T(8,128)(2,1)S(1)}, u32[]{:S(2)}, u32[]{:S(2)}) collective-permute-start(bf16[64,1536]{1,0:T(8,128)(2,1)S(1)} %broadcast_select_fusion.refs_0_), channel_id=1, source_target_pairs={{0,4},{2,6},{4,12},{6,14},{8,0},{10,2},{12,8},{14,10},{1,5},{3,7},... | collective-permute-start | bytes 589832 | tf_op jit(solution)/shard_map/ppermute | solution.py:36
  4.1 1.5 %collective-permute-start = (bf16[64,1536]{1,0:T(8,128)(2,1)}, bf16[64,1536]{1,0:T(8,128)(2,1)S(1)}, u32[]{:S(2)}, u32[]{:S(2)}) collective-permute-start(bf16[64,1536]{1,0:T(8,128)(2,1)} %bitcast.17), channel_id=1, source_target_pairs={{0,2},{2,0},{4,6},{6,4},{8,10},{10,8},{12,14},{14,12},{1,3},{3,1},... | collective-permute-start | bytes 589832 | tf_op jit(solution)/shard_map/ppermute | solution.py:26
  5.6 0.5 %collective-permute-start.2 = (bf16[64,1536]{1,0:T(8,128)(2,1)}, bf16[64,1536]{1,0:T(8,128)(2,1)S(1)}, u32[]{:S(2)}, u32[]{:S(2)}) collective-permute-start(bf16[64,1536]{1,0:T(8,128)(2,1)} %bitcast.19), channel_id=1, source_target_pairs={{0,2},{2,0},{4,6},{6,4},{8,10},{10,8},{12,14},{14,12},{1,3},{3,1},... | collective-permute-start | bytes 589832 | tf_op jit(solution)/shard_map/ppermute | solution.py:26
  6.2 0.1 stack.47.refs_0_.info
  6.2 3.7 %copy-done = bf16[3072,1536]{1,0:T(8,128)(2,1)S(1)} copy-done((bf16[3072,1536]{1,0:T(8,128)(2,1)S(1)}, bf16[3072,1536]{1,0:T(8,128)(2,1)}, u32[]{:S(2)}) %copy-start) | copy-done | bytes 9437208
  9.9 0.6 %shard_map.57 = (bf16[64,1536]{1,0:T(8,128)(2,1)S(1)}, f32[8,128]{1,0:T(8,128)}) custom-call(bf16[64,1536]{1,0:T(8,128)(2,1)S(1)} %broadcast_select_fusion.refs_0_, f32[8,128]{1,0:T(8,128)S(1)} %shard_map.55.refs_1_), custom_call_target="tpu_custom_call" | custom-call | tf_op jit(solution)/shard_map/pallas_call | solution.py:83
  10.5 1.1 %collective-permute-start.4 = (bf16[64,1536]{1,0:T(8,128)(2,1)S(1)}, bf16[64,1536]{1,0:T(8,128)(2,1)S(1)}, u32[]{:S(2)}, u32[]{:S(2)}) collective-permute-start(bf16[64,1536]{1,0:T(8,128)(2,1)S(1)} %get-tuple-element.27), channel_id=1, source_target_pairs={{0,8},{2,10},{4,0},{6,2},{8,12},{10,14},{12,4},{14,6},{1,9},{3,11}... | collective-permute-start | bytes 589832 | tf_op jit(solution)/shard_map/ppermute | solution.py:36
  11.6 0.0 collective-permute-done.1.refs_0_
  11.6 0.4 collective-permute-done.refs_2_.beside
  12.1 3.5 %collective-permute-done.2.refs_3_.refs_8_ = bf16[64,1536]{1,0:T(8,128)(2,1)S(1)} collective-permute-done((bf16[64,1536]{1,0:T(8,128)(2,1)}, bf16[64,1536]{1,0:T(8,128)(2,1)S(1)}, u32[]{:S(2)}, u32[]{:S(2)}) %collective-permute-start.2) | collective-permute-done | bytes 196640 | tf_op jit(solution)/shard_map/ppermute | solution.py:26
  15.6 0.0 collective-permute-done.3.refs_4_.refs_2_
  15.6 2.6 %collective-permute-start.5 = (bf16[64,1536]{1,0:T(8,128)(2,1)S(1)}, bf16[64,1536]{1,0:T(8,128)(2,1)S(1)}, u32[]{:S(2)}, u32[]{:S(2)}) collective-permute-start(bf16[64,1536]{1,0:T(8,128)(2,1)S(1)} %get-tuple-element.26.refs_0_.refs_9_), channel_id=1, source_target_pairs={{0,4},{2,6},{4,12},{6,14},{8,0},{10,2},{12,8},{14,10},{1,5},{3,7},... | collective-permute-start | bytes 589832 | tf_op jit(solution)/shard_map/ppermute | solution.py:36
  18.2 1.5 %collective-permute-start.8 = (bf16[64,1536]{1,0:T(8,128)(2,1)S(1)}, bf16[64,1536]{1,0:T(8,128)(2,1)S(1)}, u32[]{:S(2)}, u32[]{:S(2)}) collective-permute-start(bf16[64,1536]{1,0:T(8,128)(2,1)S(1)} %get-tuple-element.26.refs_0_.refs_9_), channel_id=1, source_target_pairs={{0,16},{1,3},{2,18},{3,1},{4,20},{5,7},{6,22},{7,5},{8,24},{9,11},... | collective-permute-start | bytes 589832 | tf_op jit(solution)/shard_map/ppermute | solution.py:46
  19.8 1.5 %collective-permute-start.6 = (bf16[64,1536]{1,0:T(8,128)(2,1)S(1)}, bf16[64,1536]{1,0:T(8,128)(2,1)S(1)}, u32[]{:S(2)}, u32[]{:S(2)}) collective-permute-start(bf16[64,1536]{1,0:T(8,128)(2,1)S(1)} %get-tuple-element.26.refs_0_.refs_9_), channel_id=1, source_target_pairs={{0,2},{1,17},{2,0},{3,19},{4,6},{5,21},{6,4},{7,23},{8,10},{9,25},... | collective-permute-start | bytes 589832 | tf_op jit(solution)/shard_map/ppermute | solution.py:46
  21.3 0.0 copy-done.1
  21.3 0.0 copy-done.2
  21.3 1.5 %shard_map.58 = (f32[512,256]{1,0:T(8,128)S(1)}, f32[8,128]{1,0:T(8,128)S(1)}) custom-call(s32[10]{0:T(128)S(1)} %stack.47.refs_0_.info, bf16[512,1536]{1,0:T(8,128)(2,1)S(1)} %copy-done.2, bf16[512,1536]{1,0:T(8,128)(2,1)S(1)} %collective-permute-done.3.refs_4_.refs_2_, bf16[3072,1536]{1,0:T(8,128)(2,1)S(1)} %copy-done.1, ...), custom_call_target="tpu_custom_call" | custom-call | flops 1000 | bytes 1000 | tf_op jit(solution)/shard_map/pallas_call | solution.py:205
  22.8 0.0 collective-permute-done.4.refs_0_
  22.8 0.6 %collective-permute-start.10 = (bf16[64,1536]{1,0:T(8,128)(2,1)S(1)}, bf16[64,1536]{1,0:T(8,128)(2,1)S(1)}, u32[]{:S(2)}, u32[]{:S(2)}) collective-permute-start(bf16[64,1536]{1,0:T(8,128)(2,1)S(1)} %get-tuple-element.30.refs_1_.refs_10_), channel_id=1, source_target_pairs={{0,16},{1,3},{2,18},{3,1},{4,20},{5,7},{6,22},{7,5},{8,24},{9,11},... | collective-permute-start | bytes 589832 | tf_op jit(solution)/shard_map/ppermute | solution.py:46
  23.4 0.5 %collective-permute-start.7 = (bf16[64,1536]{1,0:T(8,128)(2,1)S(1)}, bf16[64,1536]{1,0:T(8,128)(2,1)S(1)}, u32[]{:S(2)}, u32[]{:S(2)}) collective-permute-start(bf16[64,1536]{1,0:T(8,128)(2,1)S(1)} %get-tuple-element.30.refs_1_.refs_10_), channel_id=1, source_target_pairs={{0,2},{1,17},{2,0},{3,19},{4,6},{5,21},{6,4},{7,23},{8,10},{9,25},... | collective-permute-start | bytes 589832 | tf_op jit(solution)/shard_map/ppermute | solution.py:46
  24.0 2.3 %shard_map.60 = (f32[512,512]{1,0:T(8,128)S(1)}, f32[8,128]{1,0:T(8,128)S(1)}) custom-call(s32[10]{0:T(128)S(1)} %stack.47.refs_0_.info, bf16[512,1536]{1,0:T(8,128)(2,1)S(1)} %copy-done.2, bf16[512,1536]{1,0:T(8,128)(2,1)S(1)} %collective-permute-done.3.refs_4_.refs_2_, bf16[3072,1536]{1,0:T(8,128)(2,1)S(1)} %copy-done.1, ...), custom_call_target="tpu_custom_call" | custom-call | flops 1000 | bytes 1000 | tf_op jit(solution)/shard_map/pallas_call | solution.py:205
  26.3 0.0 collective-permute-done.5.refs_0_
  26.3 1.6 %collective-permute-start.11 = (bf16[64,1536]{1,0:T(8,128)(2,1)S(1)}, bf16[64,1536]{1,0:T(8,128)(2,1)S(1)}, u32[]{:S(2)}, u32[]{:S(2)}) collective-permute-start(bf16[64,1536]{1,0:T(8,128)(2,1)S(1)} %get-tuple-element.33.refs_2_.refs_11_), channel_id=1, source_target_pairs={{0,16},{1,3},{2,18},{3,1},{4,20},{5,7},{6,22},{7,5},{8,24},{9,11},... | collective-permute-start | bytes 589832 | tf_op jit(solution)/shard_map/ppermute | solution.py:46
  27.9 0.0 collective-permute-done.8.refs_2_.refs_6_.refs_15_
  27.9 0.0 collective-permute-done.6.refs_0_.refs_3_.refs_12_
  27.9 0.6 %collective-permute-start.12 = (bf16[64,1536]{1,0:T(8,128)(2,1)S(1)}, bf16[64,1536]{1,0:T(8,128)(2,1)S(1)}, u32[]{:S(2)}, u32[]{:S(2)}) collective-permute-start(bf16[64,1536]{1,0:T(8,128)(2,1)S(1)} %get-tuple-element.35), channel_id=1, source_target_pairs={{0,16},{1,3},{2,18},{3,1},{4,20},{5,7},{6,22},{7,5},{8,24},{9,11},... | collective-permute-start | bytes 589832 | tf_op jit(solution)/shard_map/ppermute | solution.py:46
  28.5 1.0 %collective-permute-start.9 = (bf16[64,1536]{1,0:T(8,128)(2,1)S(1)}, bf16[64,1536]{1,0:T(8,128)(2,1)S(1)}, u32[]{:S(2)}, u32[]{:S(2)}) collective-permute-start(bf16[64,1536]{1,0:T(8,128)(2,1)S(1)} %get-tuple-element.35), channel_id=1, source_target_pairs={{0,4},{2,6},{4,12},{6,14},{8,0},{10,2},{12,8},{14,10},{1,5},{3,7},... | collective-permute-start | bytes 589832 | tf_op jit(solution)/shard_map/ppermute | solution.py:36
  29.5 0.2 collective-permute-done.10.refs_0_.refs_7_.refs_16_
  29.6 1.6 %collective-permute-done.7.refs_2_.refs_4_.refs_13_ = bf16[64,1536]{1,0:T(8,128)(2,1)S(1)} collective-permute-done((bf16[64,1536]{1,0:T(8,128)(2,1)S(1)}, bf16[64,1536]{1,0:T(8,128)(2,1)S(1)}, u32[]{:S(2)}, u32[]{:S(2)}) %collective-permute-start.7) | collective-permute-done | bytes 196640 | tf_op jit(solution)/shard_map/ppermute | solution.py:46
  31.3 2.0 %collective-permute-start.13 = (bf16[64,1536]{1,0:T(8,128)(2,1)S(1)}, bf16[64,1536]{1,0:T(8,128)(2,1)S(1)}, u32[]{:S(2)}, u32[]{:S(2)}) collective-permute-start(bf16[64,1536]{1,0:T(8,128)(2,1)S(1)} %get-tuple-element.42), channel_id=1, source_target_pairs={{0,2},{1,17},{2,0},{3,19},{4,6},{5,21},{6,4},{7,23},{8,10},{9,25},... | collective-permute-start | bytes 589832 | tf_op jit(solution)/shard_map/ppermute | solution.py:46
  33.3 0.0 collective-permute-done.11.refs_0_.refs_8_.refs_17_
  33.4 2.1 %collective-permute-start.14 = (bf16[64,1536]{1,0:T(8,128)(2,1)S(1)}, bf16[64,1536]{1,0:T(8,128)(2,1)S(1)}, u32[]{:S(2)}, u32[]{:S(2)}) collective-permute-start(bf16[64,1536]{1,0:T(8,128)(2,1)S(1)} %get-tuple-element.43), channel_id=1, source_target_pairs={{0,2},{1,17},{2,0},{3,19},{4,6},{5,21},{6,4},{7,23},{8,10},{9,25},... | collective-permute-start | bytes 589832 | tf_op jit(solution)/shard_map/ppermute | solution.py:46
  35.4 3.2 %shard_map.65 = (f32[512,768]{1,0:T(8,128)S(1)}, f32[8,128]{1,0:T(8,128)S(1)}) custom-call(s32[10]{0:T(128)S(1)} %stack.47.refs_0_.info, bf16[512,1536]{1,0:T(8,128)(2,1)S(1)} %copy-done.2, bf16[512,1536]{1,0:T(8,128)(2,1)S(1)} %collective-permute-done.3.refs_4_.refs_2_, bf16[3072,1536]{1,0:T(8,128)(2,1)S(1)} %copy-done.1, ...), custom_call_target="tpu_custom_call" | custom-call | flops 1000 | bytes 1000 | tf_op jit(solution)/shard_map/pallas_call | solution.py:205
  38.6 0.0 collective-permute-done.9.refs_5_.refs_14_
  38.6 0.0 copy-done.3
  38.6 0.0 copy-done.5
  38.6 1.8 %shard_map.66 = (f32[512,128]{1,0:T(8,128)S(1)}, s32[512,128]{1,0:T(8,128)S(1)}) custom-call(s32[10]{0:T(128)S(1)} %stack.47.refs_0_.info, s32[1,512]{1,0:T(1,128)S(1)} %bitcast.21, bf16[512,1536]{1,0:T(8,128)(2,1)S(1)} %copy-done.2, bf16[64,1536]{1,0:T(8,128)(2,1)S(1)} %bitcast.18, bf16[64,1536]{1,0:T(8,128)(2,1)S(1)} %collective-permute-done.refs_2_.beside, ...), custom_call_target="tpu_custom_call" | custom-call | tf_op jit(solution)/shard_map/pallas_call | solution.py:311
  40.4 0.0 copy-start.4
  40.4 0.0 collective-permute-done.13.refs_1_.refs_19_
  40.4 0.0 collective-permute-done.12.refs_0_.refs_18_
  40.5 0.0 collective-permute-done.14.refs_2_.refs_20_
  40.5 0.6 %shard_map.67.refs_2_ = f32[512,128]{1,0:T(8,128)S(1)} custom-call(s32[10]{0:T(128)S(1)} %stack.47.refs_0_.info, s32[512,128]{1,0:T(8,128)S(1)} %get-tuple-element.40.ids.refs_1_, bf16[512,1536]{1,0:T(8,128)(2,1)S(1)} %copy-done.2, f32[512,128]{1,0:T(8,128)S(1)} %get-tuple-element.41.earlier, bf16[64,1536]{1,0:T(8,128)(2,1)S(1)} %collective-permute-done.12.refs_0_.refs_18_, ...), custom_call_target="tpu_custom_call" | custom-call | tf_op jit(solution)/shard_map/pallas_call | solution.py:318
  41.0 0.1 collective-permute-start.15
  41.1 1.5 %collective-permute-done.15.refs_3_ = f32[512,128]{1,0:T(8,128)S(1)} collective-permute-done((f32[512,128]{1,0:T(8,128)S(1)}, f32[512,128]{1,0:T(8,128)S(1)}, u32[]{:S(2)}, u32[]{:S(2)}) %collective-permute-start.15) | collective-permute-done | bytes 262176 | tf_op jit(solution)/shard_map/ppermute | solution.py:22
  42.6 0.0 copy-done.4
  42.6 2.6 %shard_map.68 = bf16[512,1536]{1,0:T(8,128)(2,1)} custom-call(s32[10]{0:T(128)S(1)} %stack.47.refs_0_.info, s32[512,128]{1,0:T(8,128)S(1)} %get-tuple-element.40.ids.refs_1_, f32[512,128]{1,0:T(8,128)S(1)} %shard_map.67.refs_2_, f32[512,128]{1,0:T(8,128)S(1)} %collective-permute-done.15.refs_3_, f32[512,256]{1,0:T(8,128)S(1)} %get-tuple-element.44.refs_4_, ...), custom_call_target="tpu_custom_call" | custom-call | tf_op jit(solution)/shard_map/pallas_call | solution.py:338
  (12 shorter events, 0.1 us)
Async XLA Ops:
  0.0 15.6 %collective-permute-start.3 = (bf16[512,1536]{1,0:T(8,128)(2,1)}, bf16[512,1536]{1,0:T(8,128)(2,1)S(1)}, u32[]{:S(2)}, u32[]{:S(2)}) collective-permute-start(bf16[512,1536]{1,0:T(8,128)(2,1)} %latent.3), channel_id=1, source_target_pairs={{0,1},{1,0},{2,3},{3,2},{4,5},{5,4},{6,7},{7,6},{8,9},{9,8},{10,11... | collective-permute-start | bytes 4718600 | tf_op jit(solution)/shard_map/ppermute | solution.py:22
  1.5 10.1 %collective-permute-start.1 = (bf16[64,1536]{1,0:T(8,128)(2,1)S(1)}, bf16[64,1536]{1,0:T(8,128)(2,1)S(1)}, u32[]{:S(2)}, u32[]{:S(2)}) collective-permute-start(bf16[64,1536]{1,0:T(8,128)(2,1)S(1)} %broadcast_select_fusion.refs_0_), channel_id=1, source_target_pairs={{0,4},{2,6},{4,12},{6,14},{8,0},{10,2},{12,8},{14,10},{1,5},{3,7},... | collective-permute-start | bytes 589832 | tf_op jit(solution)/shard_map/ppermute | solution.py:36
  4.1 7.9 %collective-permute-start = (bf16[64,1536]{1,0:T(8,128)(2,1)}, bf16[64,1536]{1,0:T(8,128)(2,1)S(1)}, u32[]{:S(2)}, u32[]{:S(2)}) collective-permute-start(bf16[64,1536]{1,0:T(8,128)(2,1)} %bitcast.17), channel_id=1, source_target_pairs={{0,2},{2,0},{4,6},{6,4},{8,10},{10,8},{12,14},{14,12},{1,3},{3,1},... | collective-permute-start | bytes 589832 | tf_op jit(solution)/shard_map/ppermute | solution.py:26
  5.6 9.9 %collective-permute-start.2 = (bf16[64,1536]{1,0:T(8,128)(2,1)}, bf16[64,1536]{1,0:T(8,128)(2,1)S(1)}, u32[]{:S(2)}, u32[]{:S(2)}) collective-permute-start(bf16[64,1536]{1,0:T(8,128)(2,1)} %bitcast.19), channel_id=1, source_target_pairs={{0,2},{2,0},{4,6},{6,4},{8,10},{10,8},{12,14},{14,12},{1,3},{3,1},... | collective-permute-start | bytes 589832 | tf_op jit(solution)/shard_map/ppermute | solution.py:26
  6.2 3.7 %copy-start = (bf16[3072,1536]{1,0:T(8,128)(2,1)S(1)}, bf16[3072,1536]{1,0:T(8,128)(2,1)}, u32[]{:S(2)}) copy-start(bf16[3072,1536]{1,0:T(8,128)(2,1)} %refs_3_.5) | copy-start | bytes 28311556
  9.9 11.3 %copy-start.1 = (bf16[3072,1536]{1,0:T(8,128)(2,1)S(1)}, bf16[3072,1536]{1,0:T(8,128)(2,1)}, u32[]{:S(2)}) copy-start(bf16[3072,1536]{1,0:T(8,128)(2,1)} %refs_3_.5) | copy-start | bytes 28311556
  9.9 11.3 %copy-start.2 = (bf16[512,1536]{1,0:T(8,128)(2,1)S(1)}, bf16[512,1536]{1,0:T(8,128)(2,1)}, u32[]{:S(2)}) copy-start(bf16[512,1536]{1,0:T(8,128)(2,1)} %latent.3) | copy-start | bytes 4718596
  10.5 12.3 %collective-permute-start.4 = (bf16[64,1536]{1,0:T(8,128)(2,1)S(1)}, bf16[64,1536]{1,0:T(8,128)(2,1)S(1)}, u32[]{:S(2)}, u32[]{:S(2)}) collective-permute-start(bf16[64,1536]{1,0:T(8,128)(2,1)S(1)} %get-tuple-element.27), channel_id=1, source_target_pairs={{0,8},{2,10},{4,0},{6,2},{8,12},{10,14},{12,4},{14,6},{1,9},{3,11}... | collective-permute-start | bytes 589832 | tf_op jit(solution)/shard_map/ppermute | solution.py:36
  15.6 10.7 %collective-permute-start.5 = (bf16[64,1536]{1,0:T(8,128)(2,1)S(1)}, bf16[64,1536]{1,0:T(8,128)(2,1)S(1)}, u32[]{:S(2)}, u32[]{:S(2)}) collective-permute-start(bf16[64,1536]{1,0:T(8,128)(2,1)S(1)} %get-tuple-element.26.refs_0_.refs_9_), channel_id=1, source_target_pairs={{0,4},{2,6},{4,12},{6,14},{8,0},{10,2},{12,8},{14,10},{1,5},{3,7},... | collective-permute-start | bytes 589832 | tf_op jit(solution)/shard_map/ppermute | solution.py:36
  18.2 9.6 %collective-permute-start.8 = (bf16[64,1536]{1,0:T(8,128)(2,1)S(1)}, bf16[64,1536]{1,0:T(8,128)(2,1)S(1)}, u32[]{:S(2)}, u32[]{:S(2)}) collective-permute-start(bf16[64,1536]{1,0:T(8,128)(2,1)S(1)} %get-tuple-element.26.refs_0_.refs_9_), channel_id=1, source_target_pairs={{0,16},{1,3},{2,18},{3,1},{4,20},{5,7},{6,22},{7,5},{8,24},{9,11},... | collective-permute-start | bytes 589832 | tf_op jit(solution)/shard_map/ppermute | solution.py:46
  19.8 8.1 %collective-permute-start.6 = (bf16[64,1536]{1,0:T(8,128)(2,1)S(1)}, bf16[64,1536]{1,0:T(8,128)(2,1)S(1)}, u32[]{:S(2)}, u32[]{:S(2)}) collective-permute-start(bf16[64,1536]{1,0:T(8,128)(2,1)S(1)} %get-tuple-element.26.refs_0_.refs_9_), channel_id=1, source_target_pairs={{0,2},{1,17},{2,0},{3,19},{4,6},{5,21},{6,4},{7,23},{8,10},{9,25},... | collective-permute-start | bytes 589832 | tf_op jit(solution)/shard_map/ppermute | solution.py:46
  22.8 6.8 %collective-permute-start.10 = (bf16[64,1536]{1,0:T(8,128)(2,1)S(1)}, bf16[64,1536]{1,0:T(8,128)(2,1)S(1)}, u32[]{:S(2)}, u32[]{:S(2)}) collective-permute-start(bf16[64,1536]{1,0:T(8,128)(2,1)S(1)} %get-tuple-element.30.refs_1_.refs_10_), channel_id=1, source_target_pairs={{0,16},{1,3},{2,18},{3,1},{4,20},{5,7},{6,22},{7,5},{8,24},{9,11},... | collective-permute-start | bytes 589832 | tf_op jit(solution)/shard_map/ppermute | solution.py:46
  23.4 7.8 %collective-permute-start.7 = (bf16[64,1536]{1,0:T(8,128)(2,1)S(1)}, bf16[64,1536]{1,0:T(8,128)(2,1)S(1)}, u32[]{:S(2)}, u32[]{:S(2)}) collective-permute-start(bf16[64,1536]{1,0:T(8,128)(2,1)S(1)} %get-tuple-element.30.refs_1_.refs_10_), channel_id=1, source_target_pairs={{0,2},{1,17},{2,0},{3,19},{4,6},{5,21},{6,4},{7,23},{8,10},{9,25},... | collective-permute-start | bytes 589832 | tf_op jit(solution)/shard_map/ppermute | solution.py:46
  26.3 7.0 %collective-permute-start.11 = (bf16[64,1536]{1,0:T(8,128)(2,1)S(1)}, bf16[64,1536]{1,0:T(8,128)(2,1)S(1)}, u32[]{:S(2)}, u32[]{:S(2)}) collective-permute-start(bf16[64,1536]{1,0:T(8,128)(2,1)S(1)} %get-tuple-element.33.refs_2_.refs_11_), channel_id=1, source_target_pairs={{0,16},{1,3},{2,18},{3,1},{4,20},{5,7},{6,22},{7,5},{8,24},{9,11},... | collective-permute-start | bytes 589832 | tf_op jit(solution)/shard_map/ppermute | solution.py:46
  27.9 12.5 %collective-permute-start.12 = (bf16[64,1536]{1,0:T(8,128)(2,1)S(1)}, bf16[64,1536]{1,0:T(8,128)(2,1)S(1)}, u32[]{:S(2)}, u32[]{:S(2)}) collective-permute-start(bf16[64,1536]{1,0:T(8,128)(2,1)S(1)} %get-tuple-element.35), channel_id=1, source_target_pairs={{0,16},{1,3},{2,18},{3,1},{4,20},{5,7},{6,22},{7,5},{8,24},{9,11},... | collective-permute-start | bytes 589832 | tf_op jit(solution)/shard_map/ppermute | solution.py:46
  28.5 10.1 %collective-permute-start.9 = (bf16[64,1536]{1,0:T(8,128)(2,1)S(1)}, bf16[64,1536]{1,0:T(8,128)(2,1)S(1)}, u32[]{:S(2)}, u32[]{:S(2)}) collective-permute-start(bf16[64,1536]{1,0:T(8,128)(2,1)S(1)} %get-tuple-element.35), channel_id=1, source_target_pairs={{0,4},{2,6},{4,12},{6,14},{8,0},{10,2},{12,8},{14,10},{1,5},{3,7},... | collective-permute-start | bytes 589832 | tf_op jit(solution)/shard_map/ppermute | solution.py:36
  31.3 9.1 %collective-permute-start.13 = (bf16[64,1536]{1,0:T(8,128)(2,1)S(1)}, bf16[64,1536]{1,0:T(8,128)(2,1)S(1)}, u32[]{:S(2)}, u32[]{:S(2)}) collective-permute-start(bf16[64,1536]{1,0:T(8,128)(2,1)S(1)} %get-tuple-element.42), channel_id=1, source_target_pairs={{0,2},{1,17},{2,0},{3,19},{4,6},{5,21},{6,4},{7,23},{8,10},{9,25},... | collective-permute-start | bytes 589832 | tf_op jit(solution)/shard_map/ppermute | solution.py:46
  33.4 7.1 %collective-permute-start.14 = (bf16[64,1536]{1,0:T(8,128)(2,1)S(1)}, bf16[64,1536]{1,0:T(8,128)(2,1)S(1)}, u32[]{:S(2)}, u32[]{:S(2)}) collective-permute-start(bf16[64,1536]{1,0:T(8,128)(2,1)S(1)} %get-tuple-element.43), channel_id=1, source_target_pairs={{0,2},{1,17},{2,0},{3,19},{4,6},{5,21},{6,4},{7,23},{8,10},{9,25},... | collective-permute-start | bytes 589832 | tf_op jit(solution)/shard_map/ppermute | solution.py:46
  35.4 3.2 %copy-start.3 = (bf16[1,1536,64]{1,2,0:T(8,128)(2,1)S(1)}, bf16[1,1536,64]{1,2,0:T(8,128)(2,1)}, u32[]{:S(2)}) copy-start(bf16[1,1536,64]{1,2,0:T(8,128)(2,1)} %param.8) | copy-start | bytes 589828
  35.4 3.2 %copy-start.5 = (s32[512,1]{0,1:T(1,128)S(1)}, s32[512,1]{0,1:T(1,128)}, u32[]{:S(2)}) copy-start(s32[512,1]{0,1:T(1,128)} %param.6) | copy-start | bytes 6148
  40.4 2.2 %copy-start.4 = (bf16[1,64,1536]{2,1,0:T(8,128)(2,1)S(1)}, bf16[1,64,1536]{2,1,0:T(8,128)(2,1)}, u32[]{:S(2)}) copy-start(bf16[1,64,1536]{2,1,0:T(8,128)(2,1)} %param.9) | copy-start | bytes 589828
  41.0 1.6 %collective-permute-start.15 = (f32[512,128]{1,0:T(8,128)S(1)}, f32[512,128]{1,0:T(8,128)S(1)}, u32[]{:S(2)}, u32[]{:S(2)}) collective-permute-start(f32[512,128]{1,0:T(8,128)S(1)} %shard_map.67.refs_2_), channel_id=1, source_target_pairs={{0,1},{1,0},{2,3},{3,2},{4,5},{5,4},{6,7},{7,6},{8,9},{9,8},{10,11... | collective-permute-start | bytes 786440 | tf_op jit(solution)/shard_map/ppermute | solution.py:22

commit v20 on v19

--- a/solution.py
+++ b/solution.py
@@ -285,13 +285,13 @@
         other = swap(latent, "tensor")
         down_beside, up_beside = neighbour(down, shards), neighbour(up, shards)
         ready = token
-        one, token = pack([(line[1], 0, rank)], token, down_beside, up_beside, other)
-        back, _ = pack([(piece, 0, rank)], ready)
+        one, token = pack([(line[1], 0, rank)], token, down_beside)
+        back, _ = pack([(piece, 0, rank)], ready, other)
         line[3] = along_line(back, shards, 3)
         line[2] = along_line(one, shards, 1)
         one_first, one_second = in_plane(one, shards, True), in_plane(one, shards, False)
         part_one, token = base(info, latent, other, shared_weight, [token], cuts[0], cuts[1])
-        three, token = pack([(line[3], 0, rank)], token)
+        three, token = pack([(line[3], 0, rank)], token, up_beside)
         three_first, three_second = in_plane(three, shards, True), in_plane(three, shards, False)
         part_two, token = base(info, latent, other, shared_weight, [token], cuts[1], cuts[2])
         two, token = pack([(line[2], 0, rank)], token)

time: 45.4 us -> 42.7 us (0.941)
  waiting for transfers between devices: 7.29 us -> 3.92 us
  starting transfers between devices: 20.3 us -> 20.8 us
    ppermute x2, waiting for transfers between devices: 3.95 us -> 0.44 us  [neighbour(): return lax.ppermute(value, 'shard', [(i, i ^ 1) for i in range(shards)])]
    ppermute x4, starting transfers between devices: 7.34 us -> 9.37 us  [along_line(): lax.ppermute(value, 'shard', [(i, ring_step(i, step)) for i in range(shar...]
    ppermute x8, starting transfers between devices: 10.4 us -> 8.88 us  [in_plane(): return lax.ppermute(value, AXES, pairs)]
  transfers between devices with their start and end apart: 16 -> 16, of which waited for: 5 -> 4; matrix products, arithmetic and copies ran while one was open for 2% -> 3% of each run, Pallas kernels for 21% -> 22%
where the time goes in v20:
time: 42.7 us; the launch traced here: 42.4 us
  starting transfers between devices  20.8 us (49%)
  Pallas kernels  12.7 us (30%)
  waiting for transfers between devices  3.92 us (9%)
  local copies, waits for them, and re-layouts  3.79 us (9%)
  other arithmetic  1.04 us (2%)
    ppermute x4, starting transfers between devices, along_line(): lax.ppermute(value, 'shard', [(i, ring_step(i, step)) for i in range(shar...  9.37 us
    ppermute x8, starting transfers between devices, in_plane(): return lax.ppermute(value, AXES, pairs)  8.88 us
    pallas_call x3, Pallas kernels, base(): pl.pallas_call(lambda *refs: base_kernel(*refs, skip=skip), out_shape=[ja...  7.02 us
    unnamed x12, local copies, waits for them, and re-layouts  3.7 us
    pallas_call x1, Pallas kernels, on_device(): pl.pallas_call(lambda *refs: up_kernel(*refs, base_parts=len(parts)), out...  2.61 us
    ppermute x2, starting transfers between devices, neighbour(): return lax.ppermute(value, 'shard', [(i, i ^ 1) for i in range(shards)])  2.03 us
    ppermute x8, waiting for transfers between devices, in_plane(): return lax.ppermute(value, AXES, pairs)  1.95 us
    pallas_call x1, Pallas kernels, on_device(): call(down_first_kernel, down_out, [SMEM] + [VMEM] * 13 + [ANY], 16, [pltp...  1.78 us
  transfers between devices with their start and end apart: 16, of which 4 were waited for; matrix products, arithmetic and copies ran while one was open for 3% of the time, Pallas kernels for 22%

profile of v20, /device:TPU:0, one launch (start us, length us, event | category | flops | bytes accessed | tf_op | source)
XLA Modules:
  0.0 42.4 jit_solution(8477616391581487146)
XLA Ops:
  0.0 0.5 %collective-permute-start.2 = (bf16[512,1536]{1,0:T(8,128)(2,1)}, bf16[512,1536]{1,0:T(8,128)(2,1)S(1)}, u32[]{:S(2)}, u32[]{:S(2)}) collective-permute-start(bf16[512,1536]{1,0:T(8,128)(2,1)} %latent.3), channel_id=1, source_target_pairs={{0,1},{1,0},{2,3},{3,2},{4,5},{5,4},{6,7},{7,6},{8,9},{9,8},{10,11... | collective-permute-start | bytes 4718600 | tf_op jit(solution)/shard_map/ppermute | solution.py:22
  0.5 1.0 %broadcast_select_fusion.refs_0_ = bf16[64,1536]{1,0:T(8,128)(2,1)S(1)} fusion(pred[]{:T(512)S(6)} %eq.3, bf16[1,64,1536]{2,1,0:T(8,128)(2,1)} %param.9, bf16[1,1536,64]{1,2,0:T(8,128)(2,1)} %param.8), kind=kLoop, calls=%fused_computation | loop fusion | flops 98304 | bytes 589825 | tf_op jit(solution)/shard_map/jit(_where)/select_n | solution.py:283
  1.5 2.6 %collective-permute-start.1 = (bf16[64,1536]{1,0:T(8,128)(2,1)S(1)}, bf16[64,1536]{1,0:T(8,128)(2,1)S(1)}, u32[]{:S(2)}, u32[]{:S(2)}) collective-permute-start(bf16[64,1536]{1,0:T(8,128)(2,1)S(1)} %broadcast_select_fusion.refs_0_), channel_id=1, source_target_pairs={{0,4},{2,6},{4,12},{6,14},{8,0},{10,2},{12,8},{14,10},{1,5},{3,7},... | collective-permute-start | bytes 589832 | tf_op jit(solution)/shard_map/ppermute | solution.py:36
  4.1 1.5 %collective-permute-start = (bf16[64,1536]{1,0:T(8,128)(2,1)}, bf16[64,1536]{1,0:T(8,128)(2,1)S(1)}, u32[]{:S(2)}, u32[]{:S(2)}) collective-permute-start(bf16[64,1536]{1,0:T(8,128)(2,1)} %bitcast.17), channel_id=1, source_target_pairs={{0,2},{2,0},{4,6},{6,4},{8,10},{10,8},{12,14},{14,12},{1,3},{3,1},... | collective-permute-start | bytes 589832 | tf_op jit(solution)/shard_map/ppermute | solution.py:26
  5.6 0.5 %collective-permute-start.4 = (bf16[64,1536]{1,0:T(8,128)(2,1)}, bf16[64,1536]{1,0:T(8,128)(2,1)S(1)}, u32[]{:S(2)}, u32[]{:S(2)}) collective-permute-start(bf16[64,1536]{1,0:T(8,128)(2,1)} %bitcast.19), channel_id=1, source_target_pairs={{0,2},{2,0},{4,6},{6,4},{8,10},{10,8},{12,14},{14,12},{1,3},{3,1},... | collective-permute-start | bytes 589832 | tf_op jit(solution)/shard_map/ppermute | solution.py:26
  6.2 0.1 stack.47.refs_0_.info
  6.2 3.7 %copy-done = bf16[3072,1536]{1,0:T(8,128)(2,1)S(1)} copy-done((bf16[3072,1536]{1,0:T(8,128)(2,1)S(1)}, bf16[3072,1536]{1,0:T(8,128)(2,1)}, u32[]{:S(2)}) %copy-start) | copy-done | bytes 9437208
  9.9 0.0 collective-permute-done.2.refs_2_
  9.9 0.6 %shard_map.57 = (bf16[64,1536]{1,0:T(8,128)(2,1)S(1)}, f32[8,128]{1,0:T(8,128)}) custom-call(bf16[64,1536]{1,0:T(8,128)(2,1)S(1)} %broadcast_select_fusion.refs_0_, f32[8,128]{1,0:T(8,128)S(1)} %shard_map.55.refs_1_, bf16[512,1536]{1,0:T(8,128)(2,1)S(1)} %collective-permute-done.2.refs_2_), custom_call_target="tpu_custom_call" | custom-call | tf_op jit(solution)/shard_map/pallas_call | solution.py:83
  10.5 1.1 %collective-permute-start.3 = (bf16[64,1536]{1,0:T(8,128)(2,1)S(1)}, bf16[64,1536]{1,0:T(8,128)(2,1)S(1)}, u32[]{:S(2)}, u32[]{:S(2)}) collective-permute-start(bf16[64,1536]{1,0:T(8,128)(2,1)S(1)} %get-tuple-element.27), channel_id=1, source_target_pairs={{0,8},{2,10},{4,0},{6,2},{8,12},{10,14},{12,4},{14,6},{1,9},{3,11}... | collective-permute-start | bytes 589832 | tf_op jit(solution)/shard_map/ppermute | solution.py:36
  11.6 0.0 collective-permute-done.1.refs_0_
  11.6 0.4 %collective-permute-done.refs_2_.beside = bf16[64,1536]{1,0:T(8,128)(2,1)S(1)} collective-permute-done((bf16[64,1536]{1,0:T(8,128)(2,1)}, bf16[64,1536]{1,0:T(8,128)(2,1)S(1)}, u32[]{:S(2)}, u32[]{:S(2)}) %collective-permute-start) | collective-permute-done | bytes 196640 | tf_op jit(solution)/shard_map/ppermute | solution.py:26
  12.1 2.6 %collective-permute-start.5 = (bf16[64,1536]{1,0:T(8,128)(2,1)S(1)}, bf16[64,1536]{1,0:T(8,128)(2,1)S(1)}, u32[]{:S(2)}, u32[]{:S(2)}) collective-permute-start(bf16[64,1536]{1,0:T(8,128)(2,1)S(1)} %get-tuple-element.26.refs_0_.refs_9_), channel_id=1, source_target_pairs={{0,4},{2,6},{4,12},{6,14},{8,0},{10,2},{12,8},{14,10},{1,5},{3,7},... | collective-permute-start | bytes 589832 | tf_op jit(solution)/shard_map/ppermute | solution.py:36
  14.7 1.5 %collective-permute-start.8 = (bf16[64,1536]{1,0:T(8,128)(2,1)S(1)}, bf16[64,1536]{1,0:T(8,128)(2,1)S(1)}, u32[]{:S(2)}, u32[]{:S(2)}) collective-permute-start(bf16[64,1536]{1,0:T(8,128)(2,1)S(1)} %get-tuple-element.26.refs_0_.refs_9_), channel_id=1, source_target_pairs={{0,16},{1,3},{2,18},{3,1},{4,20},{5,7},{6,22},{7,5},{8,24},{9,11},... | collective-permute-start | bytes 589832 | tf_op jit(solution)/shard_map/ppermute | solution.py:46
  16.2 1.5 %collective-permute-start.6 = (bf16[64,1536]{1,0:T(8,128)(2,1)S(1)}, bf16[64,1536]{1,0:T(8,128)(2,1)S(1)}, u32[]{:S(2)}, u32[]{:S(2)}) collective-permute-start(bf16[64,1536]{1,0:T(8,128)(2,1)S(1)} %get-tuple-element.26.refs_0_.refs_9_), channel_id=1, source_target_pairs={{0,2},{1,17},{2,0},{3,19},{4,6},{5,21},{6,4},{7,23},{8,10},{9,25},... | collective-permute-start | bytes 589832 | tf_op jit(solution)/shard_map/ppermute | solution.py:46
  17.7 0.0 copy-done.1
  17.7 0.0 copy-done.2
  17.8 1.5 %shard_map.58 = (f32[512,256]{1,0:T(8,128)S(1)}, f32[8,128]{1,0:T(8,128)S(1)}) custom-call(s32[10]{0:T(128)S(1)} %stack.47.refs_0_.info, bf16[512,1536]{1,0:T(8,128)(2,1)S(1)} %copy-done.2, bf16[512,1536]{1,0:T(8,128)(2,1)S(1)} %collective-permute-done.2.refs_2_, bf16[3072,1536]{1,0:T(8,128)(2,1)S(1)} %copy-done.1, f32[8,128]{1,0:T(8,128)S(1)} %get-tuple-element.28.refs_4_), custom_call_target="tpu_custom_call" | custom-call | flops 1000 | bytes 1000 | tf_op jit(solution)/shard_map/pallas_call | solution.py:205
  19.3 0.0 collective-permute-done.4.refs_2_.refs_8_
  19.3 0.0 collective-permute-done.3.refs_0_
  19.3 1.1 %collective-permute-start.10 = (bf16[64,1536]{1,0:T(8,128)(2,1)S(1)}, bf16[64,1536]{1,0:T(8,128)(2,1)S(1)}, u32[]{:S(2)}, u32[]{:S(2)}) collective-permute-start(bf16[64,1536]{1,0:T(8,128)(2,1)S(1)} %get-tuple-element.30.refs_1_.refs_10_), channel_id=1, source_target_pairs={{0,16},{1,3},{2,18},{3,1},{4,20},{5,7},{6,22},{7,5},{8,24},{9,11},... | collective-permute-start | bytes 589832 | tf_op jit(solution)/shard_map/ppermute | solution.py:46
  20.4 1.5 %collective-permute-start.7 = (bf16[64,1536]{1,0:T(8,128)(2,1)S(1)}, bf16[64,1536]{1,0:T(8,128)(2,1)S(1)}, u32[]{:S(2)}, u32[]{:S(2)}) collective-permute-start(bf16[64,1536]{1,0:T(8,128)(2,1)S(1)} %get-tuple-element.30.refs_1_.refs_10_), channel_id=1, source_target_pairs={{0,2},{1,17},{2,0},{3,19},{4,6},{5,21},{6,4},{7,23},{8,10},{9,25},... | collective-permute-start | bytes 589832 | tf_op jit(solution)/shard_map/ppermute | solution.py:46
  21.9 2.3 %shard_map.60 = (f32[512,512]{1,0:T(8,128)S(1)}, f32[8,128]{1,0:T(8,128)S(1)}) custom-call(s32[10]{0:T(128)S(1)} %stack.47.refs_0_.info, bf16[512,1536]{1,0:T(8,128)(2,1)S(1)} %copy-done.2, bf16[512,1536]{1,0:T(8,128)(2,1)S(1)} %collective-permute-done.2.refs_2_, bf16[3072,1536]{1,0:T(8,128)(2,1)S(1)} %copy-done.1, f32[8,128]{1,0:T(8,128)S(1)} %get-tuple-element.31.refs_4_), custom_call_target="tpu_custom_call" | custom-call | flops 1000 | bytes 1000 | tf_op jit(solution)/shard_map/pallas_call | solution.py:205
  24.3 0.0 collective-permute-done.5.refs_0_
  24.3 0.6 %collective-permute-start.11 = (bf16[64,1536]{1,0:T(8,128)(2,1)S(1)}, bf16[64,1536]{1,0:T(8,128)(2,1)S(1)}, u32[]{:S(2)}, u32[]{:S(2)}) collective-permute-start(bf16[64,1536]{1,0:T(8,128)(2,1)S(1)} %get-tuple-element.33.refs_2_.refs_11_), channel_id=1, source_target_pairs={{0,16},{1,3},{2,18},{3,1},{4,20},{5,7},{6,22},{7,5},{8,24},{9,11},... | collective-permute-start | bytes 589832 | tf_op jit(solution)/shard_map/ppermute | solution.py:46
  24.9 0.0 collective-permute-done.8.refs_2_.refs_6_.refs_15_
  24.9 0.0 collective-permute-done.6.refs_0_.refs_3_.refs_12_
  24.9 1.6 %collective-permute-start.12 = (bf16[64,1536]{1,0:T(8,128)(2,1)S(1)}, bf16[64,1536]{1,0:T(8,128)(2,1)S(1)}, u32[]{:S(2)}, u32[]{:S(2)}) collective-permute-start(bf16[64,1536]{1,0:T(8,128)(2,1)S(1)} %get-tuple-element.35), channel_id=1, source_target_pairs={{0,16},{1,3},{2,18},{3,1},{4,20},{5,7},{6,22},{7,5},{8,24},{9,11},... | collective-permute-start | bytes 589832 | tf_op jit(solution)/shard_map/ppermute | solution.py:46
  26.5 3.0 %collective-permute-start.9 = (bf16[64,1536]{1,0:T(8,128)(2,1)S(1)}, bf16[64,1536]{1,0:T(8,128)(2,1)S(1)}, u32[]{:S(2)}, u32[]{:S(2)}) collective-permute-start(bf16[64,1536]{1,0:T(8,128)(2,1)S(1)} %get-tuple-element.35), channel_id=1, source_target_pairs={{0,4},{2,6},{4,12},{6,14},{8,0},{10,2},{12,8},{14,10},{1,5},{3,7},... | collective-permute-start | bytes 589832 | tf_op jit(solution)/shard_map/ppermute | solution.py:36
  29.5 0.0 collective-permute-done.10.refs_0_.refs_7_.refs_16_
  29.5 0.0 collective-permute-done.7.refs_2_.refs_4_.refs_13_
  29.5 0.6 %collective-permute-start.13 = (bf16[64,1536]{1,0:T(8,128)(2,1)S(1)}, bf16[64,1536]{1,0:T(8,128)(2,1)S(1)}, u32[]{:S(2)}, u32[]{:S(2)}) collective-permute-start(bf16[64,1536]{1,0:T(8,128)(2,1)S(1)} %get-tuple-element.42), channel_id=1, source_target_pairs={{0,2},{1,17},{2,0},{3,19},{4,6},{5,21},{6,4},{7,23},{8,10},{9,25},... | collective-permute-start | bytes 589832 | tf_op jit(solution)/shard_map/ppermute | solution.py:46
  30.1 1.8 %collective-permute-done.11.refs_0_.refs_8_.refs_17_ = bf16[64,1536]{1,0:T(8,128)(2,1)S(1)} collective-permute-done((bf16[64,1536]{1,0:T(8,128)(2,1)S(1)}, bf16[64,1536]{1,0:T(8,128)(2,1)S(1)}, u32[]{:S(2)}, u32[]{:S(2)}) %collective-permute-start.11) | collective-permute-done | bytes 196640 | tf_op jit(solution)/shard_map/ppermute | solution.py:46
  31.9 0.5 %collective-permute-start.14 = (bf16[64,1536]{1,0:T(8,128)(2,1)S(1)}, bf16[64,1536]{1,0:T(8,128)(2,1)S(1)}, u32[]{:S(2)}, u32[]{:S(2)}) collective-permute-start(bf16[64,1536]{1,0:T(8,128)(2,1)S(1)} %get-tuple-element.43), channel_id=1, source_target_pairs={{0,2},{1,17},{2,0},{3,19},{4,6},{5,21},{6,4},{7,23},{8,10},{9,25},... | collective-permute-start | bytes 589832 | tf_op jit(solution)/shard_map/ppermute | solution.py:46
  32.4 3.2 %shard_map.65 = (f32[512,768]{1,0:T(8,128)S(1)}, f32[8,128]{1,0:T(8,128)S(1)}) custom-call(s32[10]{0:T(128)S(1)} %stack.47.refs_0_.info, bf16[512,1536]{1,0:T(8,128)(2,1)S(1)} %copy-done.2, bf16[512,1536]{1,0:T(8,128)(2,1)S(1)} %collective-permute-done.2.refs_2_, bf16[3072,1536]{1,0:T(8,128)(2,1)S(1)} %copy-done.1, f32[8,128]{1,0:T(8,128)S(1)} %get-tuple-element.38.refs_4_), custom_call_target="tpu_custom_call" | custom-call | flops 1000 | bytes 1000 | tf_op jit(solution)/shard_map/pallas_call | solution.py:205
  35.6 0.0 collective-permute-done.9.refs_5_.refs_14_
  35.6 0.0 copy-done.3
  35.6 0.0 copy-done.5
  35.6 1.8 %shard_map.66 = (f32[512,128]{1,0:T(8,128)S(1)}, s32[512,128]{1,0:T(8,128)S(1)}) custom-call(s32[10]{0:T(128)S(1)} %stack.47.refs_0_.info, s32[1,512]{1,0:T(1,128)S(1)} %bitcast.21, bf16[512,1536]{1,0:T(8,128)(2,1)S(1)} %copy-done.2, bf16[64,1536]{1,0:T(8,128)(2,1)S(1)} %bitcast.18, bf16[64,1536]{1,0:T(8,128)(2,1)S(1)} %collective-permute-done.refs_2_.beside, ...), custom_call_target="tpu_custom_call" | custom-call | tf_op jit(solution)/shard_map/pallas_call | solution.py:311
  37.4 0.0 copy-start.4
  37.4 0.0 collective-permute-done.12.refs_0_.refs_18_
  37.4 0.0 collective-permute-done.13.refs_1_.refs_19_
  37.5 0.2 collective-permute-done.14.refs_2_.refs_20_
  37.6 0.6 %shard_map.67.refs_2_ = f32[512,128]{1,0:T(8,128)S(1)} custom-call(s32[10]{0:T(128)S(1)} %stack.47.refs_0_.info, s32[512,128]{1,0:T(8,128)S(1)} %get-tuple-element.40.ids.refs_1_, bf16[512,1536]{1,0:T(8,128)(2,1)S(1)} %copy-done.2, f32[512,128]{1,0:T(8,128)S(1)} %get-tuple-element.41.earlier, bf16[64,1536]{1,0:T(8,128)(2,1)S(1)} %collective-permute-done.12.refs_0_.refs_18_, ...), custom_call_target="tpu_custom_call" | custom-call | tf_op jit(solution)/shard_map/pallas_call | solution.py:318
  38.2 0.1 collective-permute-start.15
  38.3 1.5 %collective-permute-done.15.refs_3_ = f32[512,128]{1,0:T(8,128)S(1)} collective-permute-done((f32[512,128]{1,0:T(8,128)S(1)}, f32[512,128]{1,0:T(8,128)S(1)}, u32[]{:S(2)}, u32[]{:S(2)}) %collective-permute-start.15) | collective-permute-done | bytes 262176 | tf_op jit(solution)/shard_map/ppermute | solution.py:22
  39.8 0.0 copy-done.4
  39.8 2.6 %shard_map.68 = bf16[512,1536]{1,0:T(8,128)(2,1)} custom-call(s32[10]{0:T(128)S(1)} %stack.47.refs_0_.info, s32[512,128]{1,0:T(8,128)S(1)} %get-tuple-element.40.ids.refs_1_, f32[512,128]{1,0:T(8,128)S(1)} %shard_map.67.refs_2_, f32[512,128]{1,0:T(8,128)S(1)} %collective-permute-done.15.refs_3_, f32[512,256]{1,0:T(8,128)S(1)} %get-tuple-element.44.refs_4_, ...), custom_call_target="tpu_custom_call" | custom-call | tf_op jit(solution)/shard_map/pallas_call | solution.py:338
  (12 shorter events, 0.1 us)
Async XLA Ops:
  0.0 9.9 %collective-permute-start.2 = (bf16[512,1536]{1,0:T(8,128)(2,1)}, bf16[512,1536]{1,0:T(8,128)(2,1)S(1)}, u32[]{:S(2)}, u32[]{:S(2)}) collective-permute-start(bf16[512,1536]{1,0:T(8,128)(2,1)} %latent.3), channel_id=1, source_target_pairs={{0,1},{1,0},{2,3},{3,2},{4,5},{5,4},{6,7},{7,6},{8,9},{9,8},{10,11... | collective-permute-start | bytes 4718600 | tf_op jit(solution)/shard_map/ppermute | solution.py:22
  1.5 10.1 %collective-permute-start.1 = (bf16[64,1536]{1,0:T(8,128)(2,1)S(1)}, bf16[64,1536]{1,0:T(8,128)(2,1)S(1)}, u32[]{:S(2)}, u32[]{:S(2)}) collective-permute-start(bf16[64,1536]{1,0:T(8,128)(2,1)S(1)} %broadcast_select_fusion.refs_0_), channel_id=1, source_target_pairs={{0,4},{2,6},{4,12},{6,14},{8,0},{10,2},{12,8},{14,10},{1,5},{3,7},... | collective-permute-start | bytes 589832 | tf_op jit(solution)/shard_map/ppermute | solution.py:36
  4.1 7.9 %collective-permute-start = (bf16[64,1536]{1,0:T(8,128)(2,1)}, bf16[64,1536]{1,0:T(8,128)(2,1)S(1)}, u32[]{:S(2)}, u32[]{:S(2)}) collective-permute-start(bf16[64,1536]{1,0:T(8,128)(2,1)} %bitcast.17), channel_id=1, source_target_pairs={{0,2},{2,0},{4,6},{6,4},{8,10},{10,8},{12,14},{14,12},{1,3},{3,1},... | collective-permute-start | bytes 589832 | tf_op jit(solution)/shard_map/ppermute | solution.py:26
  5.6 13.6 %collective-permute-start.4 = (bf16[64,1536]{1,0:T(8,128)(2,1)}, bf16[64,1536]{1,0:T(8,128)(2,1)S(1)}, u32[]{:S(2)}, u32[]{:S(2)}) collective-permute-start(bf16[64,1536]{1,0:T(8,128)(2,1)} %bitcast.19), channel_id=1, source_target_pairs={{0,2},{2,0},{4,6},{6,4},{8,10},{10,8},{12,14},{14,12},{1,3},{3,1},... | collective-permute-start | bytes 589832 | tf_op jit(solution)/shard_map/ppermute | solution.py:26
  6.2 3.7 %copy-start = (bf16[3072,1536]{1,0:T(8,128)(2,1)S(1)}, bf16[3072,1536]{1,0:T(8,128)(2,1)}, u32[]{:S(2)}) copy-start(bf16[3072,1536]{1,0:T(8,128)(2,1)} %refs_3_.5) | copy-start | bytes 28311556
  9.9 7.8 %copy-start.1 = (bf16[3072,1536]{1,0:T(8,128)(2,1)S(1)}, bf16[3072,1536]{1,0:T(8,128)(2,1)}, u32[]{:S(2)}) copy-start(bf16[3072,1536]{1,0:T(8,128)(2,1)} %refs_3_.5) | copy-start | bytes 28311556
  9.9 7.8 %copy-start.2 = (bf16[512,1536]{1,0:T(8,128)(2,1)S(1)}, bf16[512,1536]{1,0:T(8,128)(2,1)}, u32[]{:S(2)}) copy-start(bf16[512,1536]{1,0:T(8,128)(2,1)} %latent.3) | copy-start | bytes 4718596
  10.5 8.8 %collective-permute-start.3 = (bf16[64,1536]{1,0:T(8,128)(2,1)S(1)}, bf16[64,1536]{1,0:T(8,128)(2,1)S(1)}, u32[]{:S(2)}, u32[]{:S(2)}) collective-permute-start(bf16[64,1536]{1,0:T(8,128)(2,1)S(1)} %get-tuple-element.27), channel_id=1, source_target_pairs={{0,8},{2,10},{4,0},{6,2},{8,12},{10,14},{12,4},{14,6},{1,9},{3,11}... | collective-permute-start | bytes 589832 | tf_op jit(solution)/shard_map/ppermute | solution.py:36
  12.1 12.2 %collective-permute-start.5 = (bf16[64,1536]{1,0:T(8,128)(2,1)S(1)}, bf16[64,1536]{1,0:T(8,128)(2,1)S(1)}, u32[]{:S(2)}, u32[]{:S(2)}) collective-permute-start(bf16[64,1536]{1,0:T(8,128)(2,1)S(1)} %get-tuple-element.26.refs_0_.refs_9_), channel_id=1, source_target_pairs={{0,4},{2,6},{4,12},{6,14},{8,0},{10,2},{12,8},{14,10},{1,5},{3,7},... | collective-permute-start | bytes 589832 | tf_op jit(solution)/shard_map/ppermute | solution.py:36
  14.7 10.2 %collective-permute-start.8 = (bf16[64,1536]{1,0:T(8,128)(2,1)S(1)}, bf16[64,1536]{1,0:T(8,128)(2,1)S(1)}, u32[]{:S(2)}, u32[]{:S(2)}) collective-permute-start(bf16[64,1536]{1,0:T(8,128)(2,1)S(1)} %get-tuple-element.26.refs_0_.refs_9_), channel_id=1, source_target_pairs={{0,16},{1,3},{2,18},{3,1},{4,20},{5,7},{6,22},{7,5},{8,24},{9,11},... | collective-permute-start | bytes 589832 | tf_op jit(solution)/shard_map/ppermute | solution.py:46
  16.2 8.7 %collective-permute-start.6 = (bf16[64,1536]{1,0:T(8,128)(2,1)S(1)}, bf16[64,1536]{1,0:T(8,128)(2,1)S(1)}, u32[]{:S(2)}, u32[]{:S(2)}) collective-permute-start(bf16[64,1536]{1,0:T(8,128)(2,1)S(1)} %get-tuple-element.26.refs_0_.refs_9_), channel_id=1, source_target_pairs={{0,2},{1,17},{2,0},{3,19},{4,6},{5,21},{6,4},{7,23},{8,10},{9,25},... | collective-permute-start | bytes 589832 | tf_op jit(solution)/shard_map/ppermute | solution.py:46
  19.3 10.2 %collective-permute-start.10 = (bf16[64,1536]{1,0:T(8,128)(2,1)S(1)}, bf16[64,1536]{1,0:T(8,128)(2,1)S(1)}, u32[]{:S(2)}, u32[]{:S(2)}) collective-permute-start(bf16[64,1536]{1,0:T(8,128)(2,1)S(1)} %get-tuple-element.30.refs_1_.refs_10_), channel_id=1, source_target_pairs={{0,16},{1,3},{2,18},{3,1},{4,20},{5,7},{6,22},{7,5},{8,24},{9,11},... | collective-permute-start | bytes 589832 | tf_op jit(solution)/shard_map/ppermute | solution.py:46
  20.4 9.1 %collective-permute-start.7 = (bf16[64,1536]{1,0:T(8,128)(2,1)S(1)}, bf16[64,1536]{1,0:T(8,128)(2,1)S(1)}, u32[]{:S(2)}, u32[]{:S(2)}) collective-permute-start(bf16[64,1536]{1,0:T(8,128)(2,1)S(1)} %get-tuple-element.30.refs_1_.refs_10_), channel_id=1, source_target_pairs={{0,2},{1,17},{2,0},{3,19},{4,6},{5,21},{6,4},{7,23},{8,10},{9,25},... | collective-permute-start | bytes 589832 | tf_op jit(solution)/shard_map/ppermute | solution.py:46
  24.3 7.6 %collective-permute-start.11 = (bf16[64,1536]{1,0:T(8,128)(2,1)S(1)}, bf16[64,1536]{1,0:T(8,128)(2,1)S(1)}, u32[]{:S(2)}, u32[]{:S(2)}) collective-permute-start(bf16[64,1536]{1,0:T(8,128)(2,1)S(1)} %get-tuple-element.33.refs_2_.refs_11_), channel_id=1, source_target_pairs={{0,16},{1,3},{2,18},{3,1},{4,20},{5,7},{6,22},{7,5},{8,24},{9,11},... | collective-permute-start | bytes 589832 | tf_op jit(solution)/shard_map/ppermute | solution.py:46
  24.9 12.5 %collective-permute-start.12 = (bf16[64,1536]{1,0:T(8,128)(2,1)S(1)}, bf16[64,1536]{1,0:T(8,128)(2,1)S(1)}, u32[]{:S(2)}, u32[]{:S(2)}) collective-permute-start(bf16[64,1536]{1,0:T(8,128)(2,1)S(1)} %get-tuple-element.35), channel_id=1, source_target_pairs={{0,16},{1,3},{2,18},{3,1},{4,20},{5,7},{6,22},{7,5},{8,24},{9,11},... | collective-permute-start | bytes 589832 | tf_op jit(solution)/shard_map/ppermute | solution.py:46
  26.5 9.1 %collective-permute-start.9 = (bf16[64,1536]{1,0:T(8,128)(2,1)S(1)}, bf16[64,1536]{1,0:T(8,128)(2,1)S(1)}, u32[]{:S(2)}, u32[]{:S(2)}) collective-permute-start(bf16[64,1536]{1,0:T(8,128)(2,1)S(1)} %get-tuple-element.35), channel_id=1, source_target_pairs={{0,4},{2,6},{4,12},{6,14},{8,0},{10,2},{12,8},{14,10},{1,5},{3,7},... | collective-permute-start | bytes 589832 | tf_op jit(solution)/shard_map/ppermute | solution.py:36
  29.5 7.9 %collective-permute-start.13 = (bf16[64,1536]{1,0:T(8,128)(2,1)S(1)}, bf16[64,1536]{1,0:T(8,128)(2,1)S(1)}, u32[]{:S(2)}, u32[]{:S(2)}) collective-permute-start(bf16[64,1536]{1,0:T(8,128)(2,1)S(1)} %get-tuple-element.42), channel_id=1, source_target_pairs={{0,2},{1,17},{2,0},{3,19},{4,6},{5,21},{6,4},{7,23},{8,10},{9,25},... | collective-permute-start | bytes 589832 | tf_op jit(solution)/shard_map/ppermute | solution.py:46
  31.9 5.7 %collective-permute-start.14 = (bf16[64,1536]{1,0:T(8,128)(2,1)S(1)}, bf16[64,1536]{1,0:T(8,128)(2,1)S(1)}, u32[]{:S(2)}, u32[]{:S(2)}) collective-permute-start(bf16[64,1536]{1,0:T(8,128)(2,1)S(1)} %get-tuple-element.43), channel_id=1, source_target_pairs={{0,2},{1,17},{2,0},{3,19},{4,6},{5,21},{6,4},{7,23},{8,10},{9,25},... | collective-permute-start | bytes 589832 | tf_op jit(solution)/shard_map/ppermute | solution.py:46
  32.4 3.2 %copy-start.3 = (bf16[1,1536,64]{1,2,0:T(8,128)(2,1)S(1)}, bf16[1,1536,64]{1,2,0:T(8,128)(2,1)}, u32[]{:S(2)}) copy-start(bf16[1,1536,64]{1,2,0:T(8,128)(2,1)} %param.8) | copy-start | bytes 589828
  32.4 3.2 %copy-start.5 = (s32[512,1]{0,1:T(1,128)S(1)}, s32[512,1]{0,1:T(1,128)}, u32[]{:S(2)}) copy-start(s32[512,1]{0,1:T(1,128)} %param.6) | copy-start | bytes 6148
  37.4 2.4 %copy-start.4 = (bf16[1,64,1536]{2,1,0:T(8,128)(2,1)S(1)}, bf16[1,64,1536]{2,1,0:T(8,128)(2,1)}, u32[]{:S(2)}) copy-start(bf16[1,64,1536]{2,1,0:T(8,128)(2,1)} %param.9) | copy-start | bytes 589828
  38.2 1.6 %collective-permute-start.15 = (f32[512,128]{1,0:T(8,128)S(1)}, f32[512,128]{1,0:T(8,128)S(1)}, u32[]{:S(2)}, u32[]{:S(2)}) collective-permute-start(f32[512,128]{1,0:T(8,128)S(1)} %shard_map.67.refs_2_), channel_id=1, source_target_pairs={{0,1},{1,0},{2,3},{3,2},{4,5},{5,4},{6,7},{7,6},{8,9},{9,8},{10,11... | collective-permute-start | bytes 786440 | tf_op jit(solution)/shard_map/ppermute | solution.py:22

commit v21 on v18

--- a/solution.py
+++ b/solution.py
@@ -12,7 +12,6 @@
 AXES = ("replica", "shard", "tensor")
 FIRST_OWNER = 2
 COPY = 0
-SMEM = pl.BlockSpec(memory_space=pltpu.SMEM)
 VMEM = pl.BlockSpec(memory_space=pltpu.VMEM)
 ANY = pl.BlockSpec(memory_space=pl.ANY)
 TOKEN = jax.ShapeDtypeStruct((8, 128), jnp.float32)
@@ -56,6 +55,16 @@
         compiler_params=pltpu.CompilerParams(vmem_limit_bytes=limit * MIB),
         cost_estimate=pl.CostEstimate(flops=flops, bytes_accessed=moved, transcendentals=0),
     )
+
+
+def place_of_device(routed, shards, adapters):
+    core, index = lax.axis_index("tensor"), lax.axis_index("shard")
+    holds_down = (core == lax.axis_index("replica")).astype(jnp.int32)
+    owners = range(adapters)
+    if routed:
+        sources = [ring_step(index, -step) for step in (0, 1, 3, 2)]
+        owners = [a for source in sources for a in (source, source ^ 1)]
+    return [core, holds_down, *owners]
 
 
 def owner_row(info, blocks, rank):
@@ -200,12 +209,12 @@
         ) + jnp.dot(other[...], weight[rest, source], preferred_element_type=jnp.float32)
 
 
-def base(info, latent, other, weight, after, skip, end):
+def base(placed, latent, other, weight, after, skip, end):
     rows, columns = latent.shape[0], end - skip
     return pl.pallas_call(
-        lambda *refs: base_kernel(*refs, skip=skip),
+        placed(base_kernel, skip=skip),
         out_shape=[jax.ShapeDtypeStruct((rows, columns), jnp.float32), TOKEN],
-        in_specs=[SMEM, VMEM, VMEM, VMEM] + [ANY] * len(after),
+        in_specs=[VMEM, VMEM, VMEM] + [ANY] * len(after),
         out_specs=[VMEM, VMEM],
         compiler_params=pltpu.CompilerParams(vmem_limit_bytes=24 * MIB),
         cost_estimate=pl.CostEstimate(
@@ -213,7 +222,7 @@
             bytes_accessed=1000,
             transcendentals=0,
         ),
-    )(info, latent, other, weight, *after)
+    )(latent, other, weight, *after)
 
 
 def up_kernel(info, ids, mine, theirs, *refs, base_parts):
@@ -261,8 +270,7 @@
     shards = lax.axis_size("shard")
     adapters = shards * local_adapters
     columns = adapters * rank
-    index, core = lax.axis_index("shard"), lax.axis_index("tensor")
-    holds_down = core == lax.axis_index("replica")
+    holds_down = lax.axis_index("tensor") == lax.axis_index("replica")
     tiles = out_width // TILE
     cuts = [0, out_width // 6, out_width // 2, out_width]
     down = jnp.swapaxes(adapter_down_weight, 1, 2).reshape(local_adapters * rank, half_width)
@@ -271,13 +279,14 @@
     routed = shards == 8 and local_adapters == 1 and lax.axis_size("replica") == 2
     routed = routed and half_width == out_width and tiles % 6 == 0
     lowrank = jax.ShapeDtypeStruct((rows, 2 * rank), jnp.float32)
-    if routed:
-        sources = [ring_step(index, -step) for step in (0, 1, 3, 2)]
-        owners = [a for source in sources for a in (source, source ^ 1)]
-    else:
-        owners = list(range(adapters))
-    info = jnp.stack([jnp.asarray(v, jnp.int32) for v in (core, holds_down, *owners)])
-    (token,) = call(prepare_kernel, [TOKEN], [VMEM, ANY], 16, moved=COPY)(shared_weight, info)
+
+    def placed(kernel, **options):
+        def inner(*refs):
+            return kernel(place_of_device(routed, shards, adapters), *refs, **options)
+
+        return inner
+
+    (token,) = call(prepare_kernel, [TOKEN], [VMEM], 16, moved=COPY)(shared_weight)
     down_out = [lowrank, jax.ShapeDtypeStruct((rows, 2 * rank), jnp.int32)]
     if routed:
         piece = jnp.where(holds_down, down, up)
@@ -290,10 +299,10 @@
         line[3] = along_line(back, shards, 3)
         line[2] = along_line(one, shards, 1)
         one_first, one_second = in_plane(one, shards, True), in_plane(one, shards, False)
-        part_one, token = base(info, latent, other, shared_weight, [token], cuts[0], cuts[1])
+        part_one, token = base(placed, latent, other, shared_weight, [token], cuts[0], cuts[1])
         three, token = pack([(line[3], 0, rank)], token)
         three_first, three_second = in_plane(three, shards, True), in_plane(three, shards, False)
-        part_two, token = base(info, latent, other, shared_weight, [token, up_beside], cuts[1], cuts[2])
+        part_two, token = base(placed, latent, other, shared_weight, [token, up_beside], cuts[1], cuts[2])
         two, token = pack([(line[2], 0, rank)], token)
         two_second = in_plane(two, shards, False)
         turn, token = pack([(one_first, 0, rank)], token, one_second)
@@ -303,42 +312,42 @@
         corner_three = in_plane(turn, shards, True)
         turn, token = pack([(two_second, 0, rank)], token)
         corner_two = in_plane(turn, shards, True)
-        part_three, token = base(info, latent, other, shared_weight, [token], cuts[2], cuts[3])
+        part_three, token = base(placed, latent, other, shared_weight, [token], cuts[2], cuts[3])
         parts = [part_one, part_two, part_three]
         corners = [corner_one, corner_three, corner_two]
         received = [one, three, two, one_first, three_first, two_first]
         received += [one_second, three_second, two_second]
         mine, ids = call(
-            down_first_kernel,
+            placed(down_first_kernel),
             down_out,
-            [SMEM] + [VMEM] * 13 + [ANY],
+            [VMEM] * 13 + [ANY],
             16,
             [pltpu.VMEM((columns, half_width), latent.dtype)],
-        )(info, row_ids, latent, down, down_beside, *received, token)
+        )(row_ids, latent, down, down_beside, *received, token)
         mine = call(
-            down_last_kernel,
+            placed(down_last_kernel),
             lowrank,
-            [SMEM] + [VMEM] * 6,
+            [VMEM] * 6,
             16,
             [pltpu.VMEM((4 * rank, half_width), latent.dtype)],
-        )(info, ids, latent, mine, *corners)
+        )(ids, latent, mine, *corners)
         up_pieces = [up, up_beside, *received, *corners]
     else:
         other = swap(latent, "tensor")
         parts = []
         for begin, end in zip(cuts[:-1], cuts[1:]):
-            part, token = base(info, latent, other, shared_weight, [token], begin, end)
+            part, token = base(placed, latent, other, shared_weight, [token], begin, end)
             parts.append(part)
-        mine, ids = call(down_whole_kernel, down_out, [SMEM] + [VMEM] * 3, 48)(
-            info, row_ids, latent, lax.all_gather(down, "shard", axis=0, tiled=True)
+        mine, ids = call(placed(down_whole_kernel), down_out, [VMEM] * 3, 48)(
+            row_ids, latent, lax.all_gather(down, "shard", axis=0, tiled=True)
         )
         up_pieces = [lax.all_gather(up, "shard", axis=0, tiled=True)]
     theirs = swap(mine, "tensor")
 
     return pl.pallas_call(
-        lambda *refs: up_kernel(*refs, base_parts=len(parts)),
+        placed(up_kernel, base_parts=len(parts)),
         out_shape=jax.ShapeDtypeStruct((rows, out_width), latent.dtype),
-        in_specs=[SMEM] + [VMEM] * (3 + len(parts) + len(up_pieces)),
+        in_specs=[VMEM] * (3 + len(parts) + len(up_pieces)),
         out_specs=ANY,
         scratch_shapes=[
             pltpu.VMEM((columns, out_width), latent.dtype),
@@ -347,7 +356,7 @@
             pltpu.VMEM((tiles, rows, TILE), latent.dtype),
         ],
         compiler_params=pltpu.CompilerParams(vmem_limit_bytes=(24 if routed else 56) * MIB),
-    )(info, ids, mine, theirs, *parts, *up_pieces)
+    )(ids, mine, theirs, *parts, *up_pieces)
 
 
 def solution(mesh):

time: 42.2 us -> 40.1 us (0.950)
  the two profiles are of different devices: /device:TPU:11 before, /device:TPU:0 now
where the time goes in v21:
time: 40.1 us; the launch traced here: 39.9 us
  starting transfers between devices  19.7 us (49%)
  Pallas kernels  9.35 us (23%)
  waiting for transfers between devices  5.93 us (15%)
  local copies, waits for them, and re-layouts  3.7 us (9%)
  other arithmetic  1.04 us (3%)
    ppermute x8, starting transfers between devices, in_plane(): return lax.ppermute(value, AXES, pairs)  9.1 us
    ppermute x4, starting transfers between devices, along_line(): lax.ppermute(value, 'shard', [(i, ring_step(i, step)) for i in range(shar...  8.34 us
    pallas_call x3, Pallas kernels, base(): pl.pallas_call(placed(base_kernel, skip=skip), out_shape=[jax.ShapeDtypeS...  5.36 us
    unnamed x12, local copies, waits for them, and re-layouts  3.7 us
    ppermute x8, waiting for transfers between devices, in_plane(): return lax.ppermute(value, AXES, pairs)  2.58 us
    pallas_call x1, Pallas kernels, on_device(): pl.pallas_call(placed(up_kernel, base_parts=len(parts)), out_shape=jax.Sh...  2.05 us
    ppermute x4, waiting for transfers between devices, along_line(): lax.ppermute(value, 'shard', [(i, ring_step(i, step)) for i in range(shar...  1.82 us
    ppermute x2, starting transfers between devices, neighbour(): return lax.ppermute(value, 'shard', [(i, i ^ 1) for i in range(shards)])  1.77 us
  transfers between devices with their start and end apart: 16, of which 5 were waited for; matrix products, arithmetic and copies ran while one was open for 3% of the time, Pallas kernels for 18%

profile of v21, /device:TPU:0, one launch (start us, length us, event | category | flops | bytes accessed | tf_op | source)
XLA Modules:
  0.0 39.9 jit_solution(5037900045243119951)
XLA Ops:
  0.0 0.5 %collective-permute-start.2 = (bf16[512,1536]{1,0:T(8,128)(2,1)}, bf16[512,1536]{1,0:T(8,128)(2,1)S(1)}, u32[]{:S(2)}, u32[]{:S(2)}) collective-permute-start(bf16[512,1536]{1,0:T(8,128)(2,1)} %refs_1_.3), channel_id=1, source_target_pairs={{0,1},{1,0},{2,3},{3,2},{4,5},{5,4},{6,7},{7,6},{8,9},{9,8},{10,11... | collective-permute-start | bytes 4718600 | tf_op jit(solution)/shard_map/ppermute | solution.py:21
  0.5 1.0 %broadcast_select_fusion.refs_0_ = bf16[64,1536]{1,0:T(8,128)(2,1)S(1)} fusion(pred[]{:T(512)S(6)} %eq.3, bf16[1,64,1536]{2,1,0:T(8,128)(2,1)} %param.9, bf16[1,1536,64]{1,2,0:T(8,128)(2,1)} %param.8), kind=kLoop, calls=%fused_computation | loop fusion | flops 98304 | bytes 589825 | tf_op jit(solution)/shard_map/jit(_where)/select_n | solution.py:292
  1.5 2.6 %collective-permute-start.1 = (bf16[64,1536]{1,0:T(8,128)(2,1)S(1)}, bf16[64,1536]{1,0:T(8,128)(2,1)S(1)}, u32[]{:S(2)}, u32[]{:S(2)}) collective-permute-start(bf16[64,1536]{1,0:T(8,128)(2,1)S(1)} %broadcast_select_fusion.refs_0_), channel_id=1, source_target_pairs={{0,4},{2,6},{4,12},{6,14},{8,0},{10,2},{12,8},{14,10},{1,5},{3,7},... | collective-permute-start | bytes 589832 | tf_op jit(solution)/shard_map/ppermute | solution.py:35
  4.1 1.5 %collective-permute-start = (bf16[64,1536]{1,0:T(8,128)(2,1)}, bf16[64,1536]{1,0:T(8,128)(2,1)S(1)}, u32[]{:S(2)}, u32[]{:S(2)}) collective-permute-start(bf16[64,1536]{1,0:T(8,128)(2,1)} %bitcast.7), channel_id=1, source_target_pairs={{0,2},{2,0},{4,6},{6,4},{8,10},{10,8},{12,14},{14,12},{1,3},{3,1},... | collective-permute-start | bytes 589832 | tf_op jit(solution)/shard_map/ppermute | solution.py:25
  5.6 0.0 copy-start
  5.7 3.7 %copy-done = bf16[3072,1536]{1,0:T(8,128)(2,1)S(1)} copy-done((bf16[3072,1536]{1,0:T(8,128)(2,1)S(1)}, bf16[3072,1536]{1,0:T(8,128)(2,1)}, u32[]{:S(2)}) %copy-start) | copy-done | bytes 9437208
  9.3 0.0 copy-start.4
  9.3 0.0 copy-start.1
  9.3 0.6 %shard_map.57 = (bf16[64,1536]{1,0:T(8,128)(2,1)S(1)}, f32[8,128]{1,0:T(8,128)}) custom-call(bf16[64,1536]{1,0:T(8,128)(2,1)S(1)} %broadcast_select_fusion.refs_0_, f32[8,128]{1,0:T(8,128)S(1)} %shard_map.55.refs_1_), custom_call_target="tpu_custom_call" | custom-call | tf_op jit(solution)/shard_map/pallas_call | solution.py:92
  9.9 1.3 %collective-permute-start.3 = (bf16[64,1536]{1,0:T(8,128)(2,1)S(1)}, bf16[64,1536]{1,0:T(8,128)(2,1)S(1)}, u32[]{:S(2)}, u32[]{:S(2)}) collective-permute-start(bf16[64,1536]{1,0:T(8,128)(2,1)S(1)} %get-tuple-element.27), channel_id=1, source_target_pairs={{0,8},{2,10},{4,0},{6,2},{8,12},{10,14},{12,4},{14,6},{1,9},{3,11}... | collective-permute-start | bytes 589832 | tf_op jit(solution)/shard_map/ppermute | solution.py:35
  11.3 0.0 copy-done.4
  11.3 0.2 collective-permute-start.5
  11.5 0.0 collective-permute-done.1.refs_0_
  11.6 0.0 collective-permute-done.refs_2_.refs_3_
  11.6 0.0 collective-permute-done.2.refs_3_.refs_1_
  11.6 2.5 %collective-permute-start.4 = (bf16[64,1536]{1,0:T(8,128)(2,1)S(1)}, bf16[64,1536]{1,0:T(8,128)(2,1)S(1)}, u32[]{:S(2)}, u32[]{:S(2)}) collective-permute-start(bf16[64,1536]{1,0:T(8,128)(2,1)S(1)} %get-tuple-element.26.refs_4_.refs_8_), channel_id=1, source_target_pairs={{0,4},{2,6},{4,12},{6,14},{8,0},{10,2},{12,8},{14,10},{1,5},{3,7},... | collective-permute-start | bytes 589832 | tf_op jit(solution)/shard_map/ppermute | solution.py:35
  14.0 1.5 %collective-permute-start.8 = (bf16[64,1536]{1,0:T(8,128)(2,1)S(1)}, bf16[64,1536]{1,0:T(8,128)(2,1)S(1)}, u32[]{:S(2)}, u32[]{:S(2)}) collective-permute-start(bf16[64,1536]{1,0:T(8,128)(2,1)S(1)} %get-tuple-element.26.refs_4_.refs_8_), channel_id=1, source_target_pairs={{0,16},{1,3},{2,18},{3,1},{4,20},{5,7},{6,22},{7,5},{8,24},{9,11},... | collective-permute-start | bytes 589832 | tf_op jit(solution)/shard_map/ppermute | solution.py:45
  15.5 1.5 %collective-permute-start.6 = (bf16[64,1536]{1,0:T(8,128)(2,1)S(1)}, bf16[64,1536]{1,0:T(8,128)(2,1)S(1)}, u32[]{:S(2)}, u32[]{:S(2)}) collective-permute-start(bf16[64,1536]{1,0:T(8,128)(2,1)S(1)} %get-tuple-element.26.refs_4_.refs_8_), channel_id=1, source_target_pairs={{0,2},{1,17},{2,0},{3,19},{4,6},{5,21},{6,4},{7,23},{8,10},{9,25},... | collective-permute-start | bytes 589832 | tf_op jit(solution)/shard_map/ppermute | solution.py:45
  17.0 0.0 copy-done.1
  17.1 0.0 copy-done.2
  17.1 1.0 %shard_map.58 = (f32[512,256]{1,0:T(8,128)S(1)}, f32[8,128]{1,0:T(8,128)S(1)}) custom-call(bf16[512,1536]{1,0:T(8,128)(2,1)S(1)} %copy-done.2, bf16[512,1536]{1,0:T(8,128)(2,1)S(1)} %collective-permute-done.2.refs_3_.refs_1_, bf16[3072,1536]{1,0:T(8,128)(2,1)S(1)} %copy-done.1, f32[8,128]{1,0:T(8,128)S(1)} %get-tuple-element.28.refs_3_), custom_call_target="tpu_custom_call" | custom-call | flops 1000 | bytes 1000 | tf_op jit(solution)/shard_map/pallas_call | solution.py:214
  18.0 0.2 collective-permute-done.3.refs_0_
  18.3 1.6 %collective-permute-start.10 = (bf16[64,1536]{1,0:T(8,128)(2,1)S(1)}, bf16[64,1536]{1,0:T(8,128)(2,1)S(1)}, u32[]{:S(2)}, u32[]{:S(2)}) collective-permute-start(bf16[64,1536]{1,0:T(8,128)(2,1)S(1)} %get-tuple-element.30.refs_5_.refs_9_), channel_id=1, source_target_pairs={{0,16},{1,3},{2,18},{3,1},{4,20},{5,7},{6,22},{7,5},{8,24},{9,11},... | collective-permute-start | bytes 589832 | tf_op jit(solution)/shard_map/ppermute | solution.py:45
  19.8 0.0 collective-permute-done.5.refs_4_.refs_7_
  19.8 0.0 collective-permute-start.7
  19.8 1.8 %shard_map.60 = (f32[512,512]{1,0:T(8,128)S(1)}, f32[8,128]{1,0:T(8,128)S(1)}) custom-call(bf16[512,1536]{1,0:T(8,128)(2,1)S(1)} %copy-done.2, bf16[512,1536]{1,0:T(8,128)(2,1)S(1)} %collective-permute-done.2.refs_3_.refs_1_, bf16[3072,1536]{1,0:T(8,128)(2,1)S(1)} %copy-done.1, f32[8,128]{1,0:T(8,128)S(1)} %get-tuple-element.31.refs_3_, ...), custom_call_target="tpu_custom_call" | custom-call | flops 1000 | bytes 1000 | tf_op jit(solution)/shard_map/pallas_call | solution.py:214
  21.6 1.6 %collective-permute-done.4.refs_0_ = bf16[64,1536]{1,0:T(8,128)(2,1)S(1)} collective-permute-done((bf16[64,1536]{1,0:T(8,128)(2,1)S(1)}, bf16[64,1536]{1,0:T(8,128)(2,1)S(1)}, u32[]{:S(2)}, u32[]{:S(2)}) %collective-permute-start.4) | collective-permute-done | bytes 196640 | tf_op jit(solution)/shard_map/ppermute | solution.py:35
  23.2 1.6 %collective-permute-start.11 = (bf16[64,1536]{1,0:T(8,128)(2,1)S(1)}, bf16[64,1536]{1,0:T(8,128)(2,1)S(1)}, u32[]{:S(2)}, u32[]{:S(2)}) collective-permute-start(bf16[64,1536]{1,0:T(8,128)(2,1)S(1)} %get-tuple-element.33.refs_6_.refs_10_), channel_id=1, source_target_pairs={{0,16},{1,3},{2,18},{3,1},{4,20},{5,7},{6,22},{7,5},{8,24},{9,11},... | collective-permute-start | bytes 589832 | tf_op jit(solution)/shard_map/ppermute | solution.py:45
  24.8 0.0 collective-permute-done.8.refs_2_.refs_10_.refs_14_
  24.8 0.0 collective-permute-done.6.refs_0_.refs_7_.refs_11_
  24.8 0.6 %collective-permute-start.12 = (bf16[64,1536]{1,0:T(8,128)(2,1)S(1)}, bf16[64,1536]{1,0:T(8,128)(2,1)S(1)}, u32[]{:S(2)}, u32[]{:S(2)}) collective-permute-start(bf16[64,1536]{1,0:T(8,128)(2,1)S(1)} %get-tuple-element.35), channel_id=1, source_target_pairs={{0,16},{1,3},{2,18},{3,1},{4,20},{5,7},{6,22},{7,5},{8,24},{9,11},... | collective-permute-start | bytes 589832 | tf_op jit(solution)/shard_map/ppermute | solution.py:45
  25.4 1.9 %collective-permute-start.9 = (bf16[64,1536]{1,0:T(8,128)(2,1)S(1)}, bf16[64,1536]{1,0:T(8,128)(2,1)S(1)}, u32[]{:S(2)}, u32[]{:S(2)}) collective-permute-start(bf16[64,1536]{1,0:T(8,128)(2,1)S(1)} %get-tuple-element.35), channel_id=1, source_target_pairs={{0,4},{2,6},{4,12},{6,14},{8,0},{10,2},{12,8},{14,10},{1,5},{3,7},... | collective-permute-start | bytes 589832 | tf_op jit(solution)/shard_map/ppermute | solution.py:35
  27.3 0.0 collective-permute-done.10.refs_0_.refs_11_.refs_15_
  27.3 0.0 collective-permute-done.7.refs_2_.refs_8_.refs_12_
  27.4 1.5 %collective-permute-start.13 = (bf16[64,1536]{1,0:T(8,128)(2,1)S(1)}, bf16[64,1536]{1,0:T(8,128)(2,1)S(1)}, u32[]{:S(2)}, u32[]{:S(2)}) collective-permute-start(bf16[64,1536]{1,0:T(8,128)(2,1)S(1)} %get-tuple-element.42), channel_id=1, source_target_pairs={{0,2},{1,17},{2,0},{3,19},{4,6},{5,21},{6,4},{7,23},{8,10},{9,25},... | collective-permute-start | bytes 589832 | tf_op jit(solution)/shard_map/ppermute | solution.py:45
  28.9 1.5 %collective-permute-done.11.refs_0_.refs_12_.refs_16_ = bf16[64,1536]{1,0:T(8,128)(2,1)S(1)} collective-permute-done((bf16[64,1536]{1,0:T(8,128)(2,1)S(1)}, bf16[64,1536]{1,0:T(8,128)(2,1)S(1)}, u32[]{:S(2)}, u32[]{:S(2)}) %collective-permute-start.11) | collective-permute-done | bytes 196640 | tf_op jit(solution)/shard_map/ppermute | solution.py:45
  30.5 0.8 %collective-permute-start.14 = (bf16[64,1536]{1,0:T(8,128)(2,1)S(1)}, bf16[64,1536]{1,0:T(8,128)(2,1)S(1)}, u32[]{:S(2)}, u32[]{:S(2)}) collective-permute-start(bf16[64,1536]{1,0:T(8,128)(2,1)S(1)} %get-tuple-element.43), channel_id=1, source_target_pairs={{0,2},{1,17},{2,0},{3,19},{4,6},{5,21},{6,4},{7,23},{8,10},{9,25},... | collective-permute-start | bytes 589832 | tf_op jit(solution)/shard_map/ppermute | solution.py:45
  31.3 2.6 %shard_map.65 = (f32[512,768]{1,0:T(8,128)S(1)}, f32[8,128]{1,0:T(8,128)S(1)}) custom-call(bf16[512,1536]{1,0:T(8,128)(2,1)S(1)} %copy-done.2, bf16[512,1536]{1,0:T(8,128)(2,1)S(1)} %collective-permute-done.2.refs_3_.refs_1_, bf16[3072,1536]{1,0:T(8,128)(2,1)S(1)} %copy-done.1, f32[8,128]{1,0:T(8,128)S(1)} %get-tuple-element.38.refs_3_), custom_call_target="tpu_custom_call" | custom-call | flops 1000 | bytes 1000 | tf_op jit(solution)/shard_map/pallas_call | solution.py:214
  33.9 0.0 collective-permute-done.9.refs_9_.refs_13_
  33.9 0.0 copy-done.3
  33.9 0.0 copy-done.5
  33.9 1.2 %shard_map.66 = (f32[512,128]{1,0:T(8,128)S(1)}, s32[512,128]{1,0:T(8,128)S(1)}) custom-call(s32[1,512]{1,0:T(1,128)S(1)} %bitcast.11, bf16[512,1536]{1,0:T(8,128)(2,1)S(1)} %copy-done.2, bf16[64,1536]{1,0:T(8,128)(2,1)S(1)} %bitcast.8, bf16[64,1536]{1,0:T(8,128)(2,1)S(1)} %collective-permute-done.refs_2_.refs_3_, ...), custom_call_target="tpu_custom_call" | custom-call | tf_op jit(solution)/shard_map/pallas_call | solution.py:320
  35.2 0.0 collective-permute-done.13.refs_4_.refs_18_
  35.2 0.0 collective-permute-done.12.refs_3_.refs_17_
  35.2 1.0 %collective-permute-done.14.refs_5_.refs_19_ = bf16[64,1536]{1,0:T(8,128)(2,1)S(1)} collective-permute-done((bf16[64,1536]{1,0:T(8,128)(2,1)S(1)}, bf16[64,1536]{1,0:T(8,128)(2,1)S(1)}, u32[]{:S(2)}, u32[]{:S(2)}) %collective-permute-start.14) | collective-permute-done | bytes 196640 | tf_op jit(solution)/shard_map/ppermute | solution.py:45
  36.2 0.1 collective-permute-start.15
  36.3 1.5 %collective-permute-done.15.refs_2_ = f32[512,128]{1,0:T(8,128)S(1)} collective-permute-done((f32[512,128]{1,0:T(8,128)S(1)}, f32[512,128]{1,0:T(8,128)S(1)}, u32[]{:S(2)}, u32[]{:S(2)}) %collective-permute-start.15) | collective-permute-done | bytes 262176 | tf_op jit(solution)/shard_map/ppermute | solution.py:21
  37.8 2.1 %shard_map.68 = bf16[512,1536]{1,0:T(8,128)(2,1)} custom-call(s32[512,128]{1,0:T(8,128)S(1)} %get-tuple-element.40.refs_0_, f32[512,128]{1,0:T(8,128)S(1)} %shard_map.67.refs_1_, f32[512,128]{1,0:T(8,128)S(1)} %collective-permute-done.15.refs_2_, f32[512,256]{1,0:T(8,128)S(1)} %get-tuple-element.44.refs_3_, f32[512,512]{1,0:T(8,128)S(1)} %get-tuple-element.45.refs_4_, ...), custom_call_target="tpu_custom_call" | custom-call | tf_op jit(solution)/shard_map/pallas_call | solution.py:347
  (11 shorter events, 0.1 us)
Async XLA Ops:
  0.0 11.6 %collective-permute-start.2 = (bf16[512,1536]{1,0:T(8,128)(2,1)}, bf16[512,1536]{1,0:T(8,128)(2,1)S(1)}, u32[]{:S(2)}, u32[]{:S(2)}) collective-permute-start(bf16[512,1536]{1,0:T(8,128)(2,1)} %refs_1_.3), channel_id=1, source_target_pairs={{0,1},{1,0},{2,3},{3,2},{4,5},{5,4},{6,7},{7,6},{8,9},{9,8},{10,11... | collective-permute-start | bytes 4718600 | tf_op jit(solution)/shard_map/ppermute | solution.py:21
  1.5 10.1 %collective-permute-start.1 = (bf16[64,1536]{1,0:T(8,128)(2,1)S(1)}, bf16[64,1536]{1,0:T(8,128)(2,1)S(1)}, u32[]{:S(2)}, u32[]{:S(2)}) collective-permute-start(bf16[64,1536]{1,0:T(8,128)(2,1)S(1)} %broadcast_select_fusion.refs_0_), channel_id=1, source_target_pairs={{0,4},{2,6},{4,12},{6,14},{8,0},{10,2},{12,8},{14,10},{1,5},{3,7},... | collective-permute-start | bytes 589832 | tf_op jit(solution)/shard_map/ppermute | solution.py:35
  4.1 7.4 %collective-permute-start = (bf16[64,1536]{1,0:T(8,128)(2,1)}, bf16[64,1536]{1,0:T(8,128)(2,1)S(1)}, u32[]{:S(2)}, u32[]{:S(2)}) collective-permute-start(bf16[64,1536]{1,0:T(8,128)(2,1)} %bitcast.7), channel_id=1, source_target_pairs={{0,2},{2,0},{4,6},{6,4},{8,10},{10,8},{12,14},{14,12},{1,3},{3,1},... | collective-permute-start | bytes 589832 | tf_op jit(solution)/shard_map/ppermute | solution.py:25
  5.6 3.7 %copy-start = (bf16[3072,1536]{1,0:T(8,128)(2,1)S(1)}, bf16[3072,1536]{1,0:T(8,128)(2,1)}, u32[]{:S(2)}) copy-start(bf16[3072,1536]{1,0:T(8,128)(2,1)} %refs_2_.5) | copy-start | bytes 28311556
  9.3 2.0 %copy-start.4 = (bf16[1,64,1536]{2,1,0:T(8,128)(2,1)S(1)}, bf16[1,64,1536]{2,1,0:T(8,128)(2,1)}, u32[]{:S(2)}) copy-start(bf16[1,64,1536]{2,1,0:T(8,128)(2,1)} %param.9) | copy-start | bytes 589828
  9.3 7.7 %copy-start.1 = (bf16[3072,1536]{1,0:T(8,128)(2,1)S(1)}, bf16[3072,1536]{1,0:T(8,128)(2,1)}, u32[]{:S(2)}) copy-start(bf16[3072,1536]{1,0:T(8,128)(2,1)} %refs_2_.5) | copy-start | bytes 28311556
  9.3 7.7 %copy-start.2 = (bf16[512,1536]{1,0:T(8,128)(2,1)S(1)}, bf16[512,1536]{1,0:T(8,128)(2,1)}, u32[]{:S(2)}) copy-start(bf16[512,1536]{1,0:T(8,128)(2,1)} %refs_1_.3) | copy-start | bytes 4718596
  9.9 8.3 %collective-permute-start.3 = (bf16[64,1536]{1,0:T(8,128)(2,1)S(1)}, bf16[64,1536]{1,0:T(8,128)(2,1)S(1)}, u32[]{:S(2)}, u32[]{:S(2)}) collective-permute-start(bf16[64,1536]{1,0:T(8,128)(2,1)S(1)} %get-tuple-element.27), channel_id=1, source_target_pairs={{0,8},{2,10},{4,0},{6,2},{8,12},{10,14},{12,4},{14,6},{1,9},{3,11}... | collective-permute-start | bytes 589832 | tf_op jit(solution)/shard_map/ppermute | solution.py:35
  11.3 8.5 %collective-permute-start.5 = (bf16[64,1536]{1,0:T(8,128)(2,1)S(1)}, bf16[64,1536]{1,0:T(8,128)(2,1)S(1)}, u32[]{:S(2)}, u32[]{:S(2)}) collective-permute-start(bf16[64,1536]{1,0:T(8,128)(2,1)S(1)} %bitcast.9), channel_id=1, source_target_pairs={{0,2},{2,0},{4,6},{6,4},{8,10},{10,8},{12,14},{14,12},{1,3},{3,1},... | collective-permute-start | bytes 589832 | tf_op jit(solution)/shard_map/ppermute | solution.py:25
  11.6 11.6 %collective-permute-start.4 = (bf16[64,1536]{1,0:T(8,128)(2,1)S(1)}, bf16[64,1536]{1,0:T(8,128)(2,1)S(1)}, u32[]{:S(2)}, u32[]{:S(2)}) collective-permute-start(bf16[64,1536]{1,0:T(8,128)(2,1)S(1)} %get-tuple-element.26.refs_4_.refs_8_), channel_id=1, source_target_pairs={{0,4},{2,6},{4,12},{6,14},{8,0},{10,2},{12,8},{14,10},{1,5},{3,7},... | collective-permute-start | bytes 589832 | tf_op jit(solution)/shard_map/ppermute | solution.py:35
  14.0 10.8 %collective-permute-start.8 = (bf16[64,1536]{1,0:T(8,128)(2,1)S(1)}, bf16[64,1536]{1,0:T(8,128)(2,1)S(1)}, u32[]{:S(2)}, u32[]{:S(2)}) collective-permute-start(bf16[64,1536]{1,0:T(8,128)(2,1)S(1)} %get-tuple-element.26.refs_4_.refs_8_), channel_id=1, source_target_pairs={{0,16},{1,3},{2,18},{3,1},{4,20},{5,7},{6,22},{7,5},{8,24},{9,11},... | collective-permute-start | bytes 589832 | tf_op jit(solution)/shard_map/ppermute | solution.py:45
  15.5 9.3 %collective-permute-start.6 = (bf16[64,1536]{1,0:T(8,128)(2,1)S(1)}, bf16[64,1536]{1,0:T(8,128)(2,1)S(1)}, u32[]{:S(2)}, u32[]{:S(2)}) collective-permute-start(bf16[64,1536]{1,0:T(8,128)(2,1)S(1)} %get-tuple-element.26.refs_4_.refs_8_), channel_id=1, source_target_pairs={{0,2},{1,17},{2,0},{3,19},{4,6},{5,21},{6,4},{7,23},{8,10},{9,25},... | collective-permute-start | bytes 589832 | tf_op jit(solution)/shard_map/ppermute | solution.py:45
  18.3 9.1 %collective-permute-start.10 = (bf16[64,1536]{1,0:T(8,128)(2,1)S(1)}, bf16[64,1536]{1,0:T(8,128)(2,1)S(1)}, u32[]{:S(2)}, u32[]{:S(2)}) collective-permute-start(bf16[64,1536]{1,0:T(8,128)(2,1)S(1)} %get-tuple-element.30.refs_5_.refs_9_), channel_id=1, source_target_pairs={{0,16},{1,3},{2,18},{3,1},{4,20},{5,7},{6,22},{7,5},{8,24},{9,11},... | collective-permute-start | bytes 589832 | tf_op jit(solution)/shard_map/ppermute | solution.py:45
  19.8 7.5 %collective-permute-start.7 = (bf16[64,1536]{1,0:T(8,128)(2,1)S(1)}, bf16[64,1536]{1,0:T(8,128)(2,1)S(1)}, u32[]{:S(2)}, u32[]{:S(2)}) collective-permute-start(bf16[64,1536]{1,0:T(8,128)(2,1)S(1)} %get-tuple-element.30.refs_5_.refs_9_), channel_id=1, source_target_pairs={{0,2},{1,17},{2,0},{3,19},{4,6},{5,21},{6,4},{7,23},{8,10},{9,25},... | collective-permute-start | bytes 589832 | tf_op jit(solution)/shard_map/ppermute | solution.py:45
  23.2 7.2 %collective-permute-start.11 = (bf16[64,1536]{1,0:T(8,128)(2,1)S(1)}, bf16[64,1536]{1,0:T(8,128)(2,1)S(1)}, u32[]{:S(2)}, u32[]{:S(2)}) collective-permute-start(bf16[64,1536]{1,0:T(8,128)(2,1)S(1)} %get-tuple-element.33.refs_6_.refs_10_), channel_id=1, source_target_pairs={{0,16},{1,3},{2,18},{3,1},{4,20},{5,7},{6,22},{7,5},{8,24},{9,11},... | collective-permute-start | bytes 589832 | tf_op jit(solution)/shard_map/ppermute | solution.py:45
  24.8 10.4 %collective-permute-start.12 = (bf16[64,1536]{1,0:T(8,128)(2,1)S(1)}, bf16[64,1536]{1,0:T(8,128)(2,1)S(1)}, u32[]{:S(2)}, u32[]{:S(2)}) collective-permute-start(bf16[64,1536]{1,0:T(8,128)(2,1)S(1)} %get-tuple-element.35), channel_id=1, source_target_pairs={{0,16},{1,3},{2,18},{3,1},{4,20},{5,7},{6,22},{7,5},{8,24},{9,11},... | collective-permute-start | bytes 589832 | tf_op jit(solution)/shard_map/ppermute | solution.py:45
  25.4 8.5 %collective-permute-start.9 = (bf16[64,1536]{1,0:T(8,128)(2,1)S(1)}, bf16[64,1536]{1,0:T(8,128)(2,1)S(1)}, u32[]{:S(2)}, u32[]{:S(2)}) collective-permute-start(bf16[64,1536]{1,0:T(8,128)(2,1)S(1)} %get-tuple-element.35), channel_id=1, source_target_pairs={{0,4},{2,6},{4,12},{6,14},{8,0},{10,2},{12,8},{14,10},{1,5},{3,7},... | collective-permute-start | bytes 589832 | tf_op jit(solution)/shard_map/ppermute | solution.py:35
  27.4 7.8 %collective-permute-start.13 = (bf16[64,1536]{1,0:T(8,128)(2,1)S(1)}, bf16[64,1536]{1,0:T(8,128)(2,1)S(1)}, u32[]{:S(2)}, u32[]{:S(2)}) collective-permute-start(bf16[64,1536]{1,0:T(8,128)(2,1)S(1)} %get-tuple-element.42), channel_id=1, source_target_pairs={{0,2},{1,17},{2,0},{3,19},{4,6},{5,21},{6,4},{7,23},{8,10},{9,25},... | collective-permute-start | bytes 589832 | tf_op jit(solution)/shard_map/ppermute | solution.py:45
  30.5 5.7 %collective-permute-start.14 = (bf16[64,1536]{1,0:T(8,128)(2,1)S(1)}, bf16[64,1536]{1,0:T(8,128)(2,1)S(1)}, u32[]{:S(2)}, u32[]{:S(2)}) collective-permute-start(bf16[64,1536]{1,0:T(8,128)(2,1)S(1)} %get-tuple-element.43), channel_id=1, source_target_pairs={{0,2},{1,17},{2,0},{3,19},{4,6},{5,21},{6,4},{7,23},{8,10},{9,25},... | collective-permute-start | bytes 589832 | tf_op jit(solution)/shard_map/ppermute | solution.py:45
  31.3 2.6 %copy-start.3 = (bf16[1,1536,64]{1,2,0:T(8,128)(2,1)S(1)}, bf16[1,1536,64]{1,2,0:T(8,128)(2,1)}, u32[]{:S(2)}) copy-start(bf16[1,1536,64]{1,2,0:T(8,128)(2,1)} %param.8) | copy-start | bytes 589828
  31.3 2.6 %copy-start.5 = (s32[512,1]{0,1:T(1,128)S(1)}, s32[512,1]{0,1:T(1,128)}, u32[]{:S(2)}) copy-start(s32[512,1]{0,1:T(1,128)} %param.6) | copy-start | bytes 6148
  36.2 1.6 %collective-permute-start.15 = (f32[512,128]{1,0:T(8,128)S(1)}, f32[512,128]{1,0:T(8,128)S(1)}, u32[]{:S(2)}, u32[]{:S(2)}) collective-permute-start(f32[512,128]{1,0:T(8,128)S(1)} %shard_map.67.refs_1_), channel_id=1, source_target_pairs={{0,1},{1,0},{2,3},{3,2},{4,5},{5,4},{6,7},{7,6},{8,9},{9,8},{10,11... | collective-permute-start | bytes 786440 | tf_op jit(solution)/shard_map/ppermute | solution.py:21

commit v22 on v21

--- a/solution.py
+++ b/solution.py
@@ -76,22 +76,23 @@
     return row
 
 
-def pack(pieces, *after):
+def pack(pieces, *after, tokens=1):
     count = len(pieces)
     total = sum(rows for _, _, rows in pieces)
     width, dtype = pieces[0][0].shape[1], pieces[0][0].dtype
 
     def kernel(*refs):
-        out, token = refs[-2:]
+        out = refs[count + len(after)]
         top = 0
         for ref, (_, begin, rows) in zip(refs, pieces):
             out[top : top + rows, :] = ref[begin : begin + rows, :]
             top += rows
-        token[...] = jnp.zeros_like(token)
+        for token in refs[count + len(after) + 1 :]:
+            token[...] = jnp.zeros_like(token)
 
     return call(
         kernel,
-        [jax.ShapeDtypeStruct((total, width), dtype), TOKEN],
+        [jax.ShapeDtypeStruct((total, width), dtype)] + [TOKEN] * tokens,
         [VMEM] * count + [ANY] * len(after),
         4,
         moved=COPY,
@@ -295,7 +296,7 @@
         down_beside, up_beside = neighbour(down, shards), neighbour(up, shards)
         ready = token
         one, token = pack([(line[1], 0, rank)], token, down_beside, other)
-        back, _ = pack([(piece, 0, rank)], ready)
+        (back,) = pack([(piece, 0, rank)], ready, tokens=0)
         line[3] = along_line(back, shards, 3)
         line[2] = along_line(one, shards, 1)
         one_first, one_second = in_plane(one, shards, True), in_plane(one, shards, False)

time: 40.1 us -> 41.3 us (1.030)
  the two profiles are of different devices: /device:TPU:0 before, /device:TPU:11 now
where the time goes in v22:
time: 41.3 us; the launch traced here: 41.2 us
  starting transfers between devices  17.2 us (42%)
  waiting for transfers between devices  9.54 us (23%)
  Pallas kernels  8.76 us (21%)
  local copies, waits for them, and re-layouts  4.52 us (11%)
  other arithmetic  1.04 us (3%)
    ppermute x8, waiting for transfers between devices, in_plane(): return lax.ppermute(value, AXES, pairs)  6.29 us
    ppermute x4, starting transfers between devices, along_line(): lax.ppermute(value, 'shard', [(i, ring_step(i, step)) for i in range(shar...  5.84 us
    ppermute x2, starting transfers between devices, swap(): return lax.ppermute(value, axis, [(0, 1), (1, 0)])  5.62 us
    pallas_call x3, Pallas kernels, base(): pl.pallas_call(placed(base_kernel, skip=skip), out_shape=[jax.ShapeDtypeS...  5.36 us
    unnamed x12, local copies, waits for them, and re-layouts  4.52 us
    ppermute x8, starting transfers between devices, in_plane(): return lax.ppermute(value, AXES, pairs)  4.22 us
    pallas_call x1, Pallas kernels, on_device(): pl.pallas_call(placed(up_kernel, base_parts=len(parts)), out_shape=jax.Sh...  2.06 us
    ppermute x4, waiting for transfers between devices, along_line(): lax.ppermute(value, 'shard', [(i, ring_step(i, step)) for i in range(shar...  1.73 us
  transfers between devices with their start and end apart: 16, of which 5 were waited for; matrix products, arithmetic and copies ran while one was open for 3% of the time, Pallas kernels for 16%

profile of v22, /device:TPU:11, one launch (start us, length us, event | category | flops | bytes accessed | tf_op | source)
XLA Modules:
  0.0 41.2 jit_solution(10258954059161322743)
XLA Ops:
  0.0 0.7 %collective-permute-start.2 = (bf16[512,1536]{1,0:T(8,128)(2,1)}, bf16[512,1536]{1,0:T(8,128)(2,1)S(1)}, u32[]{:S(2)}, u32[]{:S(2)}) collective-permute-start(bf16[512,1536]{1,0:T(8,128)(2,1)} %refs_1_.3), channel_id=1, source_target_pairs={{0,1},{1,0},{2,3},{3,2},{4,5},{5,4},{6,7},{7,6},{8,9},{9,8},{10,11... | collective-permute-start | bytes 4718600 | tf_op jit(solution)/shard_map/ppermute | solution.py:21
  0.7 1.0 %broadcast_select_fusion.refs_0_ = bf16[64,1536]{1,0:T(8,128)(2,1)S(1)} fusion(pred[]{:T(512)S(6)} %eq.3, bf16[1,64,1536]{2,1,0:T(8,128)(2,1)} %param.9, bf16[1,1536,64]{1,2,0:T(8,128)(2,1)} %param.8), kind=kLoop, calls=%fused_computation | loop fusion | flops 98304 | bytes 589825 | tf_op jit(solution)/shard_map/jit(_where)/select_n | solution.py:293
  1.7 2.4 %collective-permute-start.1 = (bf16[64,1536]{1,0:T(8,128)(2,1)S(1)}, bf16[64,1536]{1,0:T(8,128)(2,1)S(1)}, u32[]{:S(2)}, u32[]{:S(2)}) collective-permute-start(bf16[64,1536]{1,0:T(8,128)(2,1)S(1)} %broadcast_select_fusion.refs_0_), channel_id=1, source_target_pairs={{0,4},{2,6},{4,12},{6,14},{8,0},{10,2},{12,8},{14,10},{1,5},{3,7},... | collective-permute-start | bytes 589832 | tf_op jit(solution)/shard_map/ppermute | solution.py:35
  4.1 1.2 %collective-permute-start = (bf16[64,1536]{1,0:T(8,128)(2,1)}, bf16[64,1536]{1,0:T(8,128)(2,1)S(1)}, u32[]{:S(2)}, u32[]{:S(2)}) collective-permute-start(bf16[64,1536]{1,0:T(8,128)(2,1)} %bitcast.7), channel_id=1, source_target_pairs={{0,2},{2,0},{4,6},{6,4},{8,10},{10,8},{12,14},{14,12},{1,3},{3,1},... | collective-permute-start | bytes 589832 | tf_op jit(solution)/shard_map/ppermute | solution.py:25
  5.3 0.0 copy-start
  5.3 3.7 %copy-done = bf16[3072,1536]{1,0:T(8,128)(2,1)S(1)} copy-done((bf16[3072,1536]{1,0:T(8,128)(2,1)S(1)}, bf16[3072,1536]{1,0:T(8,128)(2,1)}, u32[]{:S(2)}) %copy-start) | copy-done | bytes 9437208
  9.0 0.0 copy-start.4
  9.0 0.0 copy-start.1
  9.0 0.0 copy-start.2
  9.0 0.1 collective-permute-start.3
  9.1 0.8 %copy-done.4 = bf16[1,64,1536]{2,1,0:T(8,128)(2,1)S(1)} copy-done((bf16[1,64,1536]{2,1,0:T(8,128)(2,1)S(1)}, bf16[1,64,1536]{2,1,0:T(8,128)(2,1)}, u32[]{:S(2)}) %copy-start.4) | copy-done | bytes 196632
  9.9 0.2 collective-permute-start.5
  10.2 0.0 collective-permute-done.1.refs_0_
  10.2 0.3 collective-permute-done.refs_2_.refs_3_
  10.5 0.0 collective-permute-done.2.refs_3_.refs_1_
  10.5 1.2 %collective-permute-start.4 = (bf16[64,1536]{1,0:T(8,128)(2,1)S(1)}, bf16[64,1536]{1,0:T(8,128)(2,1)S(1)}, u32[]{:S(2)}, u32[]{:S(2)}) collective-permute-start(bf16[64,1536]{1,0:T(8,128)(2,1)S(1)} %get-tuple-element.25.refs_4_.refs_8_), channel_id=1, source_target_pairs={{0,4},{2,6},{4,12},{6,14},{8,0},{10,2},{12,8},{14,10},{1,5},{3,7},... | collective-permute-start | bytes 589832 | tf_op jit(solution)/shard_map/ppermute | solution.py:35
  11.8 1.2 %collective-permute-start.8 = (bf16[64,1536]{1,0:T(8,128)(2,1)S(1)}, bf16[64,1536]{1,0:T(8,128)(2,1)S(1)}, u32[]{:S(2)}, u32[]{:S(2)}) collective-permute-start(bf16[64,1536]{1,0:T(8,128)(2,1)S(1)} %get-tuple-element.25.refs_4_.refs_8_), channel_id=1, source_target_pairs={{0,16},{1,3},{2,18},{3,1},{4,20},{5,7},{6,22},{7,5},{8,24},{9,11},... | collective-permute-start | bytes 589832 | tf_op jit(solution)/shard_map/ppermute | solution.py:45
  13.0 0.3 collective-permute-start.6
  13.3 0.0 copy-done.1
  13.3 0.0 copy-done.2
  13.3 1.0 %shard_map.58 = (f32[512,256]{1,0:T(8,128)S(1)}, f32[8,128]{1,0:T(8,128)S(1)}) custom-call(bf16[512,1536]{1,0:T(8,128)(2,1)S(1)} %copy-done.2, bf16[512,1536]{1,0:T(8,128)(2,1)S(1)} %collective-permute-done.2.refs_3_.refs_1_, bf16[3072,1536]{1,0:T(8,128)(2,1)S(1)} %copy-done.1, f32[8,128]{1,0:T(8,128)S(1)} %get-tuple-element.26.refs_3_), custom_call_target="tpu_custom_call" | custom-call | flops 1000 | bytes 1000 | tf_op jit(solution)/shard_map/pallas_call | solution.py:215
  14.3 1.7 %collective-permute-done.3.refs_0_ = bf16[64,1536]{1,0:T(8,128)(2,1)S(1)} collective-permute-done((bf16[64,1536]{1,0:T(8,128)(2,1)S(1)}, bf16[64,1536]{1,0:T(8,128)(2,1)S(1)}, u32[]{:S(2)}, u32[]{:S(2)}) %collective-permute-start.3) | collective-permute-done | bytes 196640 | tf_op jit(solution)/shard_map/ppermute | solution.py:35
  16.0 0.2 collective-permute-start.10
  16.2 0.0 collective-permute-done.5.refs_4_.refs_7_
  16.2 0.3 collective-permute-start.7
  16.5 1.8 %shard_map.60 = (f32[512,512]{1,0:T(8,128)S(1)}, f32[8,128]{1,0:T(8,128)S(1)}) custom-call(bf16[512,1536]{1,0:T(8,128)(2,1)S(1)} %copy-done.2, bf16[512,1536]{1,0:T(8,128)(2,1)S(1)} %collective-permute-done.2.refs_3_.refs_1_, bf16[3072,1536]{1,0:T(8,128)(2,1)S(1)} %copy-done.1, f32[8,128]{1,0:T(8,128)S(1)} %get-tuple-element.29.refs_3_, ...), custom_call_target="tpu_custom_call" | custom-call | flops 1000 | bytes 1000 | tf_op jit(solution)/shard_map/pallas_call | solution.py:215
  18.3 0.0 collective-permute-done.4.refs_0_
  18.3 1.4 %collective-permute-start.11 = (bf16[64,1536]{1,0:T(8,128)(2,1)S(1)}, bf16[64,1536]{1,0:T(8,128)(2,1)S(1)}, u32[]{:S(2)}, u32[]{:S(2)}) collective-permute-start(bf16[64,1536]{1,0:T(8,128)(2,1)S(1)} %get-tuple-element.31.refs_6_.refs_10_), channel_id=1, source_target_pairs={{0,16},{1,3},{2,18},{3,1},{4,20},{5,7},{6,22},{7,5},{8,24},{9,11},... | collective-permute-start | bytes 589832 | tf_op jit(solution)/shard_map/ppermute | solution.py:45
  19.7 0.0 collective-permute-done.8.refs_2_.refs_10_.refs_14_
  19.7 0.0 collective-permute-done.6.refs_0_.refs_7_.refs_11_
  19.7 0.2 collective-permute-start.12
  19.9 2.2 %collective-permute-start.9 = (bf16[64,1536]{1,0:T(8,128)(2,1)S(1)}, bf16[64,1536]{1,0:T(8,128)(2,1)S(1)}, u32[]{:S(2)}, u32[]{:S(2)}) collective-permute-start(bf16[64,1536]{1,0:T(8,128)(2,1)S(1)} %get-tuple-element.33), channel_id=1, source_target_pairs={{0,4},{2,6},{4,12},{6,14},{8,0},{10,2},{12,8},{14,10},{1,5},{3,7},... | collective-permute-start | bytes 589832 | tf_op jit(solution)/shard_map/ppermute | solution.py:35
  22.1 0.0 collective-permute-done.10.refs_0_.refs_11_.refs_15_
  22.1 0.0 collective-permute-done.7.refs_2_.refs_8_.refs_12_
  22.1 0.3 collective-permute-start.13
  22.5 3.4 %collective-permute-done.11.refs_0_.refs_12_.refs_16_ = bf16[64,1536]{1,0:T(8,128)(2,1)S(1)} collective-permute-done((bf16[64,1536]{1,0:T(8,128)(2,1)S(1)}, bf16[64,1536]{1,0:T(8,128)(2,1)S(1)}, u32[]{:S(2)}, u32[]{:S(2)}) %collective-permute-start.11) | collective-permute-done | bytes 196640 | tf_op jit(solution)/shard_map/ppermute | solution.py:45
  25.9 0.3 collective-permute-start.14
  26.2 2.6 %shard_map.65 = (f32[512,768]{1,0:T(8,128)S(1)}, f32[8,128]{1,0:T(8,128)S(1)}) custom-call(bf16[512,1536]{1,0:T(8,128)(2,1)S(1)} %copy-done.2, bf16[512,1536]{1,0:T(8,128)(2,1)S(1)} %collective-permute-done.2.refs_3_.refs_1_, bf16[3072,1536]{1,0:T(8,128)(2,1)S(1)} %copy-done.1, f32[8,128]{1,0:T(8,128)S(1)} %get-tuple-element.36.refs_3_), custom_call_target="tpu_custom_call" | custom-call | flops 1000 | bytes 1000 | tf_op jit(solution)/shard_map/pallas_call | solution.py:215
  28.8 0.0 collective-permute-done.9.refs_9_.refs_13_
  28.9 0.0 copy-done.3
  28.9 0.0 copy-done.5
  28.9 1.2 %shard_map.66 = (f32[512,128]{1,0:T(8,128)S(1)}, s32[512,128]{1,0:T(8,128)S(1)}) custom-call(s32[1,512]{1,0:T(1,128)S(1)} %bitcast.11, bf16[512,1536]{1,0:T(8,128)(2,1)S(1)} %copy-done.2, bf16[64,1536]{1,0:T(8,128)(2,1)S(1)} %bitcast.8, bf16[64,1536]{1,0:T(8,128)(2,1)S(1)} %collective-permute-done.refs_2_.refs_3_, ...), custom_call_target="tpu_custom_call" | custom-call | tf_op jit(solution)/shard_map/pallas_call | solution.py:321
  30.1 0.0 collective-permute-done.13.refs_4_.refs_18_
  30.1 0.0 collective-permute-done.12.refs_3_.refs_17_
  30.1 2.8 %collective-permute-done.14.refs_5_.refs_19_ = bf16[64,1536]{1,0:T(8,128)(2,1)S(1)} collective-permute-done((bf16[64,1536]{1,0:T(8,128)(2,1)S(1)}, bf16[64,1536]{1,0:T(8,128)(2,1)S(1)}, u32[]{:S(2)}, u32[]{:S(2)}) %collective-permute-start.14) | collective-permute-done | bytes 196640 | tf_op jit(solution)/shard_map/ppermute | solution.py:45
  33.0 4.9 %collective-permute-start.15 = (f32[512,128]{1,0:T(8,128)S(1)}, f32[512,128]{1,0:T(8,128)S(1)}, u32[]{:S(2)}, u32[]{:S(2)}) collective-permute-start(f32[512,128]{1,0:T(8,128)S(1)} %shard_map.67.refs_1_), channel_id=1, source_target_pairs={{0,1},{1,0},{2,3},{3,2},{4,5},{5,4},{6,7},{7,6},{8,9},{9,8},{10,11... | collective-permute-start | bytes 786440 | tf_op jit(solution)/shard_map/ppermute | solution.py:21
  37.9 1.2 %collective-permute-done.15.refs_2_ = f32[512,128]{1,0:T(8,128)S(1)} collective-permute-done((f32[512,128]{1,0:T(8,128)S(1)}, f32[512,128]{1,0:T(8,128)S(1)}, u32[]{:S(2)}, u32[]{:S(2)}) %collective-permute-start.15) | collective-permute-done | bytes 262176 | tf_op jit(solution)/shard_map/ppermute | solution.py:21
  39.1 2.1 %shard_map.68 = bf16[512,1536]{1,0:T(8,128)(2,1)} custom-call(s32[512,128]{1,0:T(8,128)S(1)} %get-tuple-element.38.refs_0_, f32[512,128]{1,0:T(8,128)S(1)} %shard_map.67.refs_1_, f32[512,128]{1,0:T(8,128)S(1)} %collective-permute-done.15.refs_2_, f32[512,256]{1,0:T(8,128)S(1)} %get-tuple-element.42.refs_3_, f32[512,512]{1,0:T(8,128)S(1)} %get-tuple-element.43.refs_4_, ...), custom_call_target="tpu_custom_call" | custom-call | tf_op jit(solution)/shard_map/pallas_call | solution.py:348
  (11 shorter events, 0.1 us)
Async XLA Ops:
  0.0 10.5 %collective-permute-start.2 = (bf16[512,1536]{1,0:T(8,128)(2,1)}, bf16[512,1536]{1,0:T(8,128)(2,1)S(1)}, u32[]{:S(2)}, u32[]{:S(2)}) collective-permute-start(bf16[512,1536]{1,0:T(8,128)(2,1)} %refs_1_.3), channel_id=1, source_target_pairs={{0,1},{1,0},{2,3},{3,2},{4,5},{5,4},{6,7},{7,6},{8,9},{9,8},{10,11... | collective-permute-start | bytes 4718600 | tf_op jit(solution)/shard_map/ppermute | solution.py:21
  1.7 8.4 %collective-permute-start.1 = (bf16[64,1536]{1,0:T(8,128)(2,1)S(1)}, bf16[64,1536]{1,0:T(8,128)(2,1)S(1)}, u32[]{:S(2)}, u32[]{:S(2)}) collective-permute-start(bf16[64,1536]{1,0:T(8,128)(2,1)S(1)} %broadcast_select_fusion.refs_0_), channel_id=1, source_target_pairs={{0,4},{2,6},{4,12},{6,14},{8,0},{10,2},{12,8},{14,10},{1,5},{3,7},... | collective-permute-start | bytes 589832 | tf_op jit(solution)/shard_map/ppermute | solution.py:35
  4.1 6.4 %collective-permute-start = (bf16[64,1536]{1,0:T(8,128)(2,1)}, bf16[64,1536]{1,0:T(8,128)(2,1)S(1)}, u32[]{:S(2)}, u32[]{:S(2)}) collective-permute-start(bf16[64,1536]{1,0:T(8,128)(2,1)} %bitcast.7), channel_id=1, source_target_pairs={{0,2},{2,0},{4,6},{6,4},{8,10},{10,8},{12,14},{14,12},{1,3},{3,1},... | collective-permute-start | bytes 589832 | tf_op jit(solution)/shard_map/ppermute | solution.py:25
  5.3 3.7 %copy-start = (bf16[3072,1536]{1,0:T(8,128)(2,1)S(1)}, bf16[3072,1536]{1,0:T(8,128)(2,1)}, u32[]{:S(2)}) copy-start(bf16[3072,1536]{1,0:T(8,128)(2,1)} %refs_2_.5) | copy-start | bytes 28311556
  9.0 0.9 %copy-start.4 = (bf16[1,64,1536]{2,1,0:T(8,128)(2,1)S(1)}, bf16[1,64,1536]{2,1,0:T(8,128)(2,1)}, u32[]{:S(2)}) copy-start(bf16[1,64,1536]{2,1,0:T(8,128)(2,1)} %param.9) | copy-start | bytes 589828
  9.0 4.3 %copy-start.1 = (bf16[3072,1536]{1,0:T(8,128)(2,1)S(1)}, bf16[3072,1536]{1,0:T(8,128)(2,1)}, u32[]{:S(2)}) copy-start(bf16[3072,1536]{1,0:T(8,128)(2,1)} %refs_2_.5) | copy-start | bytes 28311556
  9.0 4.3 %copy-start.2 = (bf16[512,1536]{1,0:T(8,128)(2,1)S(1)}, bf16[512,1536]{1,0:T(8,128)(2,1)}, u32[]{:S(2)}) copy-start(bf16[512,1536]{1,0:T(8,128)(2,1)} %refs_1_.3) | copy-start | bytes 4718596
  9.0 6.9 %collective-permute-start.3 = (bf16[64,1536]{1,0:T(8,128)(2,1)S(1)}, bf16[64,1536]{1,0:T(8,128)(2,1)S(1)}, u32[]{:S(2)}, u32[]{:S(2)}) collective-permute-start(bf16[64,1536]{1,0:T(8,128)(2,1)S(1)} %shard_map.57), channel_id=1, source_target_pairs={{0,8},{2,10},{4,0},{6,2},{8,12},{10,14},{12,4},{14,6},{1,9},{3,11}... | collective-permute-start | bytes 589832 | tf_op jit(solution)/shard_map/ppermute | solution.py:35
  9.9 6.3 %collective-permute-start.5 = (bf16[64,1536]{1,0:T(8,128)(2,1)S(1)}, bf16[64,1536]{1,0:T(8,128)(2,1)S(1)}, u32[]{:S(2)}, u32[]{:S(2)}) collective-permute-start(bf16[64,1536]{1,0:T(8,128)(2,1)S(1)} %bitcast.9), channel_id=1, source_target_pairs={{0,2},{2,0},{4,6},{6,4},{8,10},{10,8},{12,14},{14,12},{1,3},{3,1},... | collective-permute-start | bytes 589832 | tf_op jit(solution)/shard_map/ppermute | solution.py:25
  10.5 7.8 %collective-permute-start.4 = (bf16[64,1536]{1,0:T(8,128)(2,1)S(1)}, bf16[64,1536]{1,0:T(8,128)(2,1)S(1)}, u32[]{:S(2)}, u32[]{:S(2)}) collective-permute-start(bf16[64,1536]{1,0:T(8,128)(2,1)S(1)} %get-tuple-element.25.refs_4_.refs_8_), channel_id=1, source_target_pairs={{0,4},{2,6},{4,12},{6,14},{8,0},{10,2},{12,8},{14,10},{1,5},{3,7},... | collective-permute-start | bytes 589832 | tf_op jit(solution)/shard_map/ppermute | solution.py:35
  11.8 7.9 %collective-permute-start.8 = (bf16[64,1536]{1,0:T(8,128)(2,1)S(1)}, bf16[64,1536]{1,0:T(8,128)(2,1)S(1)}, u32[]{:S(2)}, u32[]{:S(2)}) collective-permute-start(bf16[64,1536]{1,0:T(8,128)(2,1)S(1)} %get-tuple-element.25.refs_4_.refs_8_), channel_id=1, source_target_pairs={{0,16},{1,3},{2,18},{3,1},{4,20},{5,7},{6,22},{7,5},{8,24},{9,11},... | collective-permute-start | bytes 589832 | tf_op jit(solution)/shard_map/ppermute | solution.py:45
  13.0 6.7 %collective-permute-start.6 = (bf16[64,1536]{1,0:T(8,128)(2,1)S(1)}, bf16[64,1536]{1,0:T(8,128)(2,1)S(1)}, u32[]{:S(2)}, u32[]{:S(2)}) collective-permute-start(bf16[64,1536]{1,0:T(8,128)(2,1)S(1)} %get-tuple-element.25.refs_4_.refs_8_), channel_id=1, source_target_pairs={{0,2},{1,17},{2,0},{3,19},{4,6},{5,21},{6,4},{7,23},{8,10},{9,25},... | collective-permute-start | bytes 589832 | tf_op jit(solution)/shard_map/ppermute | solution.py:45
  16.0 6.1 %collective-permute-start.10 = (bf16[64,1536]{1,0:T(8,128)(2,1)S(1)}, bf16[64,1536]{1,0:T(8,128)(2,1)S(1)}, u32[]{:S(2)}, u32[]{:S(2)}) collective-permute-start(bf16[64,1536]{1,0:T(8,128)(2,1)S(1)} %get-tuple-element.28.refs_5_.refs_9_), channel_id=1, source_target_pairs={{0,16},{1,3},{2,18},{3,1},{4,20},{5,7},{6,22},{7,5},{8,24},{9,11},... | collective-permute-start | bytes 589832 | tf_op jit(solution)/shard_map/ppermute | solution.py:45
  16.2 5.9 %collective-permute-start.7 = (bf16[64,1536]{1,0:T(8,128)(2,1)S(1)}, bf16[64,1536]{1,0:T(8,128)(2,1)S(1)}, u32[]{:S(2)}, u32[]{:S(2)}) collective-permute-start(bf16[64,1536]{1,0:T(8,128)(2,1)S(1)} %get-tuple-element.28.refs_5_.refs_9_), channel_id=1, source_target_pairs={{0,2},{1,17},{2,0},{3,19},{4,6},{5,21},{6,4},{7,23},{8,10},{9,25},... | collective-permute-start | bytes 589832 | tf_op jit(solution)/shard_map/ppermute | solution.py:45
  18.3 7.6 %collective-permute-start.11 = (bf16[64,1536]{1,0:T(8,128)(2,1)S(1)}, bf16[64,1536]{1,0:T(8,128)(2,1)S(1)}, u32[]{:S(2)}, u32[]{:S(2)}) collective-permute-start(bf16[64,1536]{1,0:T(8,128)(2,1)S(1)} %get-tuple-element.31.refs_6_.refs_10_), channel_id=1, source_target_pairs={{0,16},{1,3},{2,18},{3,1},{4,20},{5,7},{6,22},{7,5},{8,24},{9,11},... | collective-permute-start | bytes 589832 | tf_op jit(solution)/shard_map/ppermute | solution.py:45
  19.7 10.4 %collective-permute-start.12 = (bf16[64,1536]{1,0:T(8,128)(2,1)S(1)}, bf16[64,1536]{1,0:T(8,128)(2,1)S(1)}, u32[]{:S(2)}, u32[]{:S(2)}) collective-permute-start(bf16[64,1536]{1,0:T(8,128)(2,1)S(1)} %get-tuple-element.33), channel_id=1, source_target_pairs={{0,16},{1,3},{2,18},{3,1},{4,20},{5,7},{6,22},{7,5},{8,24},{9,11},... | collective-permute-start | bytes 589832 | tf_op jit(solution)/shard_map/ppermute | solution.py:45
  19.9 8.9 %collective-permute-start.9 = (bf16[64,1536]{1,0:T(8,128)(2,1)S(1)}, bf16[64,1536]{1,0:T(8,128)(2,1)S(1)}, u32[]{:S(2)}, u32[]{:S(2)}) collective-permute-start(bf16[64,1536]{1,0:T(8,128)(2,1)S(1)} %get-tuple-element.33), channel_id=1, source_target_pairs={{0,4},{2,6},{4,12},{6,14},{8,0},{10,2},{12,8},{14,10},{1,5},{3,7},... | collective-permute-start | bytes 589832 | tf_op jit(solution)/shard_map/ppermute | solution.py:35
  22.1 8.0 %collective-permute-start.13 = (bf16[64,1536]{1,0:T(8,128)(2,1)S(1)}, bf16[64,1536]{1,0:T(8,128)(2,1)S(1)}, u32[]{:S(2)}, u32[]{:S(2)}) collective-permute-start(bf16[64,1536]{1,0:T(8,128)(2,1)S(1)} %get-tuple-element.40), channel_id=1, source_target_pairs={{0,2},{1,17},{2,0},{3,19},{4,6},{5,21},{6,4},{7,23},{8,10},{9,25},... | collective-permute-start | bytes 589832 | tf_op jit(solution)/shard_map/ppermute | solution.py:45
  25.9 7.0 %collective-permute-start.14 = (bf16[64,1536]{1,0:T(8,128)(2,1)S(1)}, bf16[64,1536]{1,0:T(8,128)(2,1)S(1)}, u32[]{:S(2)}, u32[]{:S(2)}) collective-permute-start(bf16[64,1536]{1,0:T(8,128)(2,1)S(1)} %get-tuple-element.41), channel_id=1, source_target_pairs={{0,2},{1,17},{2,0},{3,19},{4,6},{5,21},{6,4},{7,23},{8,10},{9,25},... | collective-permute-start | bytes 589832 | tf_op jit(solution)/shard_map/ppermute | solution.py:45
  26.2 2.6 %copy-start.3 = (bf16[1,1536,64]{1,2,0:T(8,128)(2,1)S(1)}, bf16[1,1536,64]{1,2,0:T(8,128)(2,1)}, u32[]{:S(2)}) copy-start(bf16[1,1536,64]{1,2,0:T(8,128)(2,1)} %param.8) | copy-start | bytes 589828
  26.2 2.6 %copy-start.5 = (s32[512,1]{0,1:T(1,128)S(1)}, s32[512,1]{0,1:T(1,128)}, u32[]{:S(2)}) copy-start(s32[512,1]{0,1:T(1,128)} %param.6) | copy-start | bytes 6148
  33.0 6.1 %collective-permute-start.15 = (f32[512,128]{1,0:T(8,128)S(1)}, f32[512,128]{1,0:T(8,128)S(1)}, u32[]{:S(2)}, u32[]{:S(2)}) collective-permute-start(f32[512,128]{1,0:T(8,128)S(1)} %shard_map.67.refs_1_), channel_id=1, source_target_pairs={{0,1},{1,0},{2,3},{3,2},{4,5},{5,4},{6,7},{7,6},{8,9},{9,8},{10,11... | collective-permute-start | bytes 786440 | tf_op jit(solution)/shard_map/ppermute | solution.py:21

commit v23 on v21

--- a/solution.py
+++ b/solution.py
@@ -303,11 +303,11 @@
         three, token = pack([(line[3], 0, rank)], token)
         three_first, three_second = in_plane(three, shards, True), in_plane(three, shards, False)
         part_two, token = base(placed, latent, other, shared_weight, [token, up_beside], cuts[1], cuts[2])
-        two, token = pack([(line[2], 0, rank)], token)
-        two_second = in_plane(two, shards, False)
         turn, token = pack([(one_first, 0, rank)], token, one_second)
         corner_one = in_plane(turn, shards, False)
         two_first = along_line(turn, shards, 1)
+        two, token = pack([(line[2], 0, rank)], token)
+        two_second = in_plane(two, shards, False)
         turn, token = pack([(three_second, 0, rank)], token, three_first)
         corner_three = in_plane(turn, shards, True)
         turn, token = pack([(two_second, 0, rank)], token)

time: 40.1 us -> 41 us (1.022)
  waiting for transfers between devices: 5.93 us -> 7.81 us
  starting transfers between devices: 19.7 us -> 18.8 us
    ppermute x8, waiting for transfers between devices: 2.58 us -> 5.77 us  [in_plane(): return lax.ppermute(value, AXES, pairs)]
    ppermute x4, waiting for transfers between devices: 1.82 us -> 0.5 us  [along_line(): lax.ppermute(value, 'shard', [(i, ring_step(i, step)) for i in range(shar...]
    ppermute x4, starting transfers between devices: 8.34 us -> 7.46 us  [along_line(): lax.ppermute(value, 'shard', [(i, ring_step(i, step)) for i in range(shar...]
where the time goes in v23:
time: 41 us; the launch traced here: 40.9 us
  starting transfers between devices  18.8 us (46%)
  Pallas kernels  9.35 us (23%)
  waiting for transfers between devices  7.81 us (19%)
  local copies, waits for them, and re-layouts  3.7 us (9%)
  other arithmetic  1.04 us (3%)
    ppermute x8, starting transfers between devices, in_plane(): return lax.ppermute(value, AXES, pairs)  9.06 us
    ppermute x4, starting transfers between devices, along_line(): lax.ppermute(value, 'shard', [(i, ring_step(i, step)) for i in range(shar...  7.46 us
    ppermute x8, waiting for transfers between devices, in_plane(): return lax.ppermute(value, AXES, pairs)  5.77 us
    pallas_call x3, Pallas kernels, base(): pl.pallas_call(placed(base_kernel, skip=skip), out_shape=[jax.ShapeDtypeS...  5.36 us
    unnamed x12, local copies, waits for them, and re-layouts  3.7 us
    pallas_call x1, Pallas kernels, on_device(): pl.pallas_call(placed(up_kernel, base_parts=len(parts)), out_shape=jax.Sh...  2.06 us
    ppermute x2, starting transfers between devices, neighbour(): return lax.ppermute(value, 'shard', [(i, i ^ 1) for i in range(shards)])  1.77 us
    ppermute x2, waiting for transfers between devices, swap(): return lax.ppermute(value, axis, [(0, 1), (1, 0)])  1.52 us
  transfers between devices with their start and end apart: 16, of which 5 were waited for; matrix products, arithmetic and copies ran while one was open for 3% of the time, Pallas kernels for 18%

profile of v23, /device:TPU:0, one launch (start us, length us, event | category | flops | bytes accessed | tf_op | source)
XLA Modules:
  0.0 40.9 jit_solution(2878658189491063347)
XLA Ops:
  0.0 0.5 %collective-permute-start.2 = (bf16[512,1536]{1,0:T(8,128)(2,1)}, bf16[512,1536]{1,0:T(8,128)(2,1)S(1)}, u32[]{:S(2)}, u32[]{:S(2)}) collective-permute-start(bf16[512,1536]{1,0:T(8,128)(2,1)} %refs_1_.3), channel_id=1, source_target_pairs={{0,1},{1,0},{2,3},{3,2},{4,5},{5,4},{6,7},{7,6},{8,9},{9,8},{10,11... | collective-permute-start | bytes 4718600 | tf_op jit(solution)/shard_map/ppermute | solution.py:21
  0.5 1.0 %broadcast_select_fusion.refs_0_ = bf16[64,1536]{1,0:T(8,128)(2,1)S(1)} fusion(pred[]{:T(512)S(6)} %eq.3, bf16[1,64,1536]{2,1,0:T(8,128)(2,1)} %param.9, bf16[1,1536,64]{1,2,0:T(8,128)(2,1)} %param.8), kind=kLoop, calls=%fused_computation | loop fusion | flops 98304 | bytes 589825 | tf_op jit(solution)/shard_map/jit(_where)/select_n | solution.py:292
  1.5 2.6 %collective-permute-start.1 = (bf16[64,1536]{1,0:T(8,128)(2,1)S(1)}, bf16[64,1536]{1,0:T(8,128)(2,1)S(1)}, u32[]{:S(2)}, u32[]{:S(2)}) collective-permute-start(bf16[64,1536]{1,0:T(8,128)(2,1)S(1)} %broadcast_select_fusion.refs_0_), channel_id=1, source_target_pairs={{0,4},{2,6},{4,12},{6,14},{8,0},{10,2},{12,8},{14,10},{1,5},{3,7},... | collective-permute-start | bytes 589832 | tf_op jit(solution)/shard_map/ppermute | solution.py:35
  4.1 1.5 %collective-permute-start = (bf16[64,1536]{1,0:T(8,128)(2,1)}, bf16[64,1536]{1,0:T(8,128)(2,1)S(1)}, u32[]{:S(2)}, u32[]{:S(2)}) collective-permute-start(bf16[64,1536]{1,0:T(8,128)(2,1)} %bitcast.7), channel_id=1, source_target_pairs={{0,2},{2,0},{4,6},{6,4},{8,10},{10,8},{12,14},{14,12},{1,3},{3,1},... | collective-permute-start | bytes 589832 | tf_op jit(solution)/shard_map/ppermute | solution.py:25
  5.6 0.0 copy-start
  5.7 3.7 %copy-done = bf16[3072,1536]{1,0:T(8,128)(2,1)S(1)} copy-done((bf16[3072,1536]{1,0:T(8,128)(2,1)S(1)}, bf16[3072,1536]{1,0:T(8,128)(2,1)}, u32[]{:S(2)}) %copy-start) | copy-done | bytes 9437208
  9.3 0.0 copy-start.4
  9.3 0.0 copy-start.1
  9.3 0.6 %shard_map.57 = (bf16[64,1536]{1,0:T(8,128)(2,1)S(1)}, f32[8,128]{1,0:T(8,128)}) custom-call(bf16[64,1536]{1,0:T(8,128)(2,1)S(1)} %broadcast_select_fusion.refs_0_, f32[8,128]{1,0:T(8,128)S(1)} %shard_map.55.refs_1_), custom_call_target="tpu_custom_call" | custom-call | tf_op jit(solution)/shard_map/pallas_call | solution.py:92
  9.9 1.3 %collective-permute-start.3 = (bf16[64,1536]{1,0:T(8,128)(2,1)S(1)}, bf16[64,1536]{1,0:T(8,128)(2,1)S(1)}, u32[]{:S(2)}, u32[]{:S(2)}) collective-permute-start(bf16[64,1536]{1,0:T(8,128)(2,1)S(1)} %get-tuple-element.27), channel_id=1, source_target_pairs={{0,8},{2,10},{4,0},{6,2},{8,12},{10,14},{12,4},{14,6},{1,9},{3,11}... | collective-permute-start | bytes 589832 | tf_op jit(solution)/shard_map/ppermute | solution.py:35
  11.3 0.0 copy-done.4
  11.3 0.2 collective-permute-start.6
  11.5 0.0 collective-permute-done.1.refs_0_
  11.6 0.0 collective-permute-done.refs_2_.refs_3_
  11.6 0.0 collective-permute-done.2.refs_3_.refs_1_
  11.6 1.8 %collective-permute-start.7 = (bf16[64,1536]{1,0:T(8,128)(2,1)S(1)}, bf16[64,1536]{1,0:T(8,128)(2,1)S(1)}, u32[]{:S(2)}, u32[]{:S(2)}) collective-permute-start(bf16[64,1536]{1,0:T(8,128)(2,1)S(1)} %get-tuple-element.26.refs_4_.refs_8_), channel_id=1, source_target_pairs={{0,16},{1,3},{2,18},{3,1},{4,20},{5,7},{6,22},{7,5},{8,24},{9,11},... | collective-permute-start | bytes 589832 | tf_op jit(solution)/shard_map/ppermute | solution.py:45
  13.4 1.5 %collective-permute-start.5 = (bf16[64,1536]{1,0:T(8,128)(2,1)S(1)}, bf16[64,1536]{1,0:T(8,128)(2,1)S(1)}, u32[]{:S(2)}, u32[]{:S(2)}) collective-permute-start(bf16[64,1536]{1,0:T(8,128)(2,1)S(1)} %get-tuple-element.26.refs_4_.refs_8_), channel_id=1, source_target_pairs={{0,2},{1,17},{2,0},{3,19},{4,6},{5,21},{6,4},{7,23},{8,10},{9,25},... | collective-permute-start | bytes 589832 | tf_op jit(solution)/shard_map/ppermute | solution.py:45
  14.9 2.1 %collective-permute-start.4 = (bf16[64,1536]{1,0:T(8,128)(2,1)S(1)}, bf16[64,1536]{1,0:T(8,128)(2,1)S(1)}, u32[]{:S(2)}, u32[]{:S(2)}) collective-permute-start(bf16[64,1536]{1,0:T(8,128)(2,1)S(1)} %get-tuple-element.26.refs_4_.refs_8_), channel_id=1, source_target_pairs={{0,4},{2,6},{4,12},{6,14},{8,0},{10,2},{12,8},{14,10},{1,5},{3,7},... | collective-permute-start | bytes 589832 | tf_op jit(solution)/shard_map/ppermute | solution.py:35
  17.1 0.0 copy-done.1
  17.1 0.0 copy-done.2
  17.1 1.0 %shard_map.58 = (f32[512,256]{1,0:T(8,128)S(1)}, f32[8,128]{1,0:T(8,128)S(1)}) custom-call(bf16[512,1536]{1,0:T(8,128)(2,1)S(1)} %copy-done.2, bf16[512,1536]{1,0:T(8,128)(2,1)S(1)} %collective-permute-done.2.refs_3_.refs_1_, bf16[3072,1536]{1,0:T(8,128)(2,1)S(1)} %copy-done.1, f32[8,128]{1,0:T(8,128)S(1)} %get-tuple-element.28.refs_3_), custom_call_target="tpu_custom_call" | custom-call | flops 1000 | bytes 1000 | tf_op jit(solution)/shard_map/pallas_call | solution.py:214
  18.1 0.0 collective-permute-done.3.refs_0_
  18.1 1.1 %collective-permute-start.10 = (bf16[64,1536]{1,0:T(8,128)(2,1)S(1)}, bf16[64,1536]{1,0:T(8,128)(2,1)S(1)}, u32[]{:S(2)}, u32[]{:S(2)}) collective-permute-start(bf16[64,1536]{1,0:T(8,128)(2,1)S(1)} %get-tuple-element.30.refs_5_.refs_9_), channel_id=1, source_target_pairs={{0,16},{1,3},{2,18},{3,1},{4,20},{5,7},{6,22},{7,5},{8,24},{9,11},... | collective-permute-start | bytes 589832 | tf_op jit(solution)/shard_map/ppermute | solution.py:45
  19.2 0.0 collective-permute-done.6.refs_4_.refs_7_
  19.2 0.5 %collective-permute-start.8 = (bf16[64,1536]{1,0:T(8,128)(2,1)S(1)}, bf16[64,1536]{1,0:T(8,128)(2,1)S(1)}, u32[]{:S(2)}, u32[]{:S(2)}) collective-permute-start(bf16[64,1536]{1,0:T(8,128)(2,1)S(1)} %get-tuple-element.30.refs_5_.refs_9_), channel_id=1, source_target_pairs={{0,2},{1,17},{2,0},{3,19},{4,6},{5,21},{6,4},{7,23},{8,10},{9,25},... | collective-permute-start | bytes 589832 | tf_op jit(solution)/shard_map/ppermute | solution.py:45
  19.7 1.8 %shard_map.60 = (f32[512,512]{1,0:T(8,128)S(1)}, f32[8,128]{1,0:T(8,128)S(1)}) custom-call(bf16[512,1536]{1,0:T(8,128)(2,1)S(1)} %copy-done.2, bf16[512,1536]{1,0:T(8,128)(2,1)S(1)} %collective-permute-done.2.refs_3_.refs_1_, bf16[3072,1536]{1,0:T(8,128)(2,1)S(1)} %copy-done.1, f32[8,128]{1,0:T(8,128)S(1)} %get-tuple-element.31.refs_3_, ...), custom_call_target="tpu_custom_call" | custom-call | flops 1000 | bytes 1000 | tf_op jit(solution)/shard_map/pallas_call | solution.py:214
  21.5 0.0 collective-permute-done.7.refs_2_.refs_10_.refs_14_
  21.5 1.8 %collective-permute-done.5.refs_0_.refs_7_.refs_11_ = bf16[64,1536]{1,0:T(8,128)(2,1)S(1)} collective-permute-done((bf16[64,1536]{1,0:T(8,128)(2,1)S(1)}, bf16[64,1536]{1,0:T(8,128)(2,1)S(1)}, u32[]{:S(2)}, u32[]{:S(2)}) %collective-permute-start.5) | collective-permute-done | bytes 196640 | tf_op jit(solution)/shard_map/ppermute | solution.py:45
  23.3 0.5 %collective-permute-done.4.refs_0_ = bf16[64,1536]{1,0:T(8,128)(2,1)S(1)} collective-permute-done((bf16[64,1536]{1,0:T(8,128)(2,1)S(1)}, bf16[64,1536]{1,0:T(8,128)(2,1)S(1)}, u32[]{:S(2)}, u32[]{:S(2)}) %collective-permute-start.4) | collective-permute-done | bytes 196640 | tf_op jit(solution)/shard_map/ppermute | solution.py:35
  23.9 1.6 %collective-permute-start.11 = (bf16[64,1536]{1,0:T(8,128)(2,1)S(1)}, bf16[64,1536]{1,0:T(8,128)(2,1)S(1)}, u32[]{:S(2)}, u32[]{:S(2)}) collective-permute-start(bf16[64,1536]{1,0:T(8,128)(2,1)S(1)} %get-tuple-element.34.refs_6_.refs_10_), channel_id=1, source_target_pairs={{0,16},{1,3},{2,18},{3,1},{4,20},{5,7},{6,22},{7,5},{8,24},{9,11},... | collective-permute-start | bytes 589832 | tf_op jit(solution)/shard_map/ppermute | solution.py:45
  25.4 0.5 %collective-permute-start.12 = (bf16[64,1536]{1,0:T(8,128)(2,1)S(1)}, bf16[64,1536]{1,0:T(8,128)(2,1)S(1)}, u32[]{:S(2)}, u32[]{:S(2)}) collective-permute-start(bf16[64,1536]{1,0:T(8,128)(2,1)S(1)} %get-tuple-element.35), channel_id=1, source_target_pairs={{0,16},{1,3},{2,18},{3,1},{4,20},{5,7},{6,22},{7,5},{8,24},{9,11},... | collective-permute-start | bytes 589832 | tf_op jit(solution)/shard_map/ppermute | solution.py:45
  25.9 1.3 %collective-permute-start.9 = (bf16[64,1536]{1,0:T(8,128)(2,1)S(1)}, bf16[64,1536]{1,0:T(8,128)(2,1)S(1)}, u32[]{:S(2)}, u32[]{:S(2)}) collective-permute-start(bf16[64,1536]{1,0:T(8,128)(2,1)S(1)} %get-tuple-element.35), channel_id=1, source_target_pairs={{0,4},{2,6},{4,12},{6,14},{8,0},{10,2},{12,8},{14,10},{1,5},{3,7},... | collective-permute-start | bytes 589832 | tf_op jit(solution)/shard_map/ppermute | solution.py:35
  27.3 0.0 collective-permute-done.10.refs_0_.refs_11_.refs_15_
  27.3 0.0 collective-permute-done.8.refs_2_.refs_8_.refs_12_
  27.3 1.6 %collective-permute-start.13 = (bf16[64,1536]{1,0:T(8,128)(2,1)S(1)}, bf16[64,1536]{1,0:T(8,128)(2,1)S(1)}, u32[]{:S(2)}, u32[]{:S(2)}) collective-permute-start(bf16[64,1536]{1,0:T(8,128)(2,1)S(1)} %get-tuple-element.42), channel_id=1, source_target_pairs={{0,2},{1,17},{2,0},{3,19},{4,6},{5,21},{6,4},{7,23},{8,10},{9,25},... | collective-permute-start | bytes 589832 | tf_op jit(solution)/shard_map/ppermute | solution.py:45
  28.9 2.5 %collective-permute-done.11.refs_0_.refs_12_.refs_16_ = bf16[64,1536]{1,0:T(8,128)(2,1)S(1)} collective-permute-done((bf16[64,1536]{1,0:T(8,128)(2,1)S(1)}, bf16[64,1536]{1,0:T(8,128)(2,1)S(1)}, u32[]{:S(2)}, u32[]{:S(2)}) %collective-permute-start.11) | collective-permute-done | bytes 196640 | tf_op jit(solution)/shard_map/ppermute | solution.py:45
  31.4 0.4 collective-permute-start.14
  31.9 2.6 %shard_map.65 = (f32[512,768]{1,0:T(8,128)S(1)}, f32[8,128]{1,0:T(8,128)S(1)}) custom-call(bf16[512,1536]{1,0:T(8,128)(2,1)S(1)} %copy-done.2, bf16[512,1536]{1,0:T(8,128)(2,1)S(1)} %collective-permute-done.2.refs_3_.refs_1_, bf16[3072,1536]{1,0:T(8,128)(2,1)S(1)} %copy-done.1, f32[8,128]{1,0:T(8,128)S(1)} %get-tuple-element.38.refs_3_), custom_call_target="tpu_custom_call" | custom-call | flops 1000 | bytes 1000 | tf_op jit(solution)/shard_map/pallas_call | solution.py:214
  34.5 0.0 collective-permute-done.9.refs_9_.refs_13_
  34.5 0.0 copy-done.3
  34.5 0.0 copy-done.5
  34.5 1.2 %shard_map.66 = (f32[512,128]{1,0:T(8,128)S(1)}, s32[512,128]{1,0:T(8,128)S(1)}) custom-call(s32[1,512]{1,0:T(1,128)S(1)} %bitcast.11, bf16[512,1536]{1,0:T(8,128)(2,1)S(1)} %copy-done.2, bf16[64,1536]{1,0:T(8,128)(2,1)S(1)} %bitcast.8, bf16[64,1536]{1,0:T(8,128)(2,1)S(1)} %collective-permute-done.refs_2_.refs_3_, ...), custom_call_target="tpu_custom_call" | custom-call | tf_op jit(solution)/shard_map/pallas_call | solution.py:320
  35.7 0.0 collective-permute-done.13.refs_4_.refs_18_
  35.7 0.0 collective-permute-done.12.refs_3_.refs_17_
  35.7 1.4 %collective-permute-done.14.refs_5_.refs_19_ = bf16[64,1536]{1,0:T(8,128)(2,1)S(1)} collective-permute-done((bf16[64,1536]{1,0:T(8,128)(2,1)S(1)}, bf16[64,1536]{1,0:T(8,128)(2,1)S(1)}, u32[]{:S(2)}, u32[]{:S(2)}) %collective-permute-start.14) | collective-permute-done | bytes 196640 | tf_op jit(solution)/shard_map/ppermute | solution.py:45
  37.2 0.1 collective-permute-start.15
  37.3 1.5 %collective-permute-done.15.refs_2_ = f32[512,128]{1,0:T(8,128)S(1)} collective-permute-done((f32[512,128]{1,0:T(8,128)S(1)}, f32[512,128]{1,0:T(8,128)S(1)}, u32[]{:S(2)}, u32[]{:S(2)}) %collective-permute-start.15) | collective-permute-done | bytes 262176 | tf_op jit(solution)/shard_map/ppermute | solution.py:21
  38.8 2.1 %shard_map.68 = bf16[512,1536]{1,0:T(8,128)(2,1)} custom-call(s32[512,128]{1,0:T(8,128)S(1)} %get-tuple-element.40.refs_0_, f32[512,128]{1,0:T(8,128)S(1)} %shard_map.67.refs_1_, f32[512,128]{1,0:T(8,128)S(1)} %collective-permute-done.15.refs_2_, f32[512,256]{1,0:T(8,128)S(1)} %get-tuple-element.44.refs_3_, f32[512,512]{1,0:T(8,128)S(1)} %get-tuple-element.45.refs_4_, ...), custom_call_target="tpu_custom_call" | custom-call | tf_op jit(solution)/shard_map/pallas_call | solution.py:347
  (11 shorter events, 0.1 us)
Async XLA Ops:
  0.0 11.6 %collective-permute-start.2 = (bf16[512,1536]{1,0:T(8,128)(2,1)}, bf16[512,1536]{1,0:T(8,128)(2,1)S(1)}, u32[]{:S(2)}, u32[]{:S(2)}) collective-permute-start(bf16[512,1536]{1,0:T(8,128)(2,1)} %refs_1_.3), channel_id=1, source_target_pairs={{0,1},{1,0},{2,3},{3,2},{4,5},{5,4},{6,7},{7,6},{8,9},{9,8},{10,11... | collective-permute-start | bytes 4718600 | tf_op jit(solution)/shard_map/ppermute | solution.py:21
  1.5 10.1 %collective-permute-start.1 = (bf16[64,1536]{1,0:T(8,128)(2,1)S(1)}, bf16[64,1536]{1,0:T(8,128)(2,1)S(1)}, u32[]{:S(2)}, u32[]{:S(2)}) collective-permute-start(bf16[64,1536]{1,0:T(8,128)(2,1)S(1)} %broadcast_select_fusion.refs_0_), channel_id=1, source_target_pairs={{0,4},{2,6},{4,12},{6,14},{8,0},{10,2},{12,8},{14,10},{1,5},{3,7},... | collective-permute-start | bytes 589832 | tf_op jit(solution)/shard_map/ppermute | solution.py:35
  4.1 7.4 %collective-permute-start = (bf16[64,1536]{1,0:T(8,128)(2,1)}, bf16[64,1536]{1,0:T(8,128)(2,1)S(1)}, u32[]{:S(2)}, u32[]{:S(2)}) collective-permute-start(bf16[64,1536]{1,0:T(8,128)(2,1)} %bitcast.7), channel_id=1, source_target_pairs={{0,2},{2,0},{4,6},{6,4},{8,10},{10,8},{12,14},{14,12},{1,3},{3,1},... | collective-permute-start | bytes 589832 | tf_op jit(solution)/shard_map/ppermute | solution.py:25
  5.6 3.7 %copy-start = (bf16[3072,1536]{1,0:T(8,128)(2,1)S(1)}, bf16[3072,1536]{1,0:T(8,128)(2,1)}, u32[]{:S(2)}) copy-start(bf16[3072,1536]{1,0:T(8,128)(2,1)} %refs_2_.5) | copy-start | bytes 28311556
  9.3 2.0 %copy-start.4 = (bf16[1,64,1536]{2,1,0:T(8,128)(2,1)S(1)}, bf16[1,64,1536]{2,1,0:T(8,128)(2,1)}, u32[]{:S(2)}) copy-start(bf16[1,64,1536]{2,1,0:T(8,128)(2,1)} %param.9) | copy-start | bytes 589828
  9.3 7.7 %copy-start.1 = (bf16[3072,1536]{1,0:T(8,128)(2,1)S(1)}, bf16[3072,1536]{1,0:T(8,128)(2,1)}, u32[]{:S(2)}) copy-start(bf16[3072,1536]{1,0:T(8,128)(2,1)} %refs_2_.5) | copy-start | bytes 28311556
  9.3 7.7 %copy-start.2 = (bf16[512,1536]{1,0:T(8,128)(2,1)S(1)}, bf16[512,1536]{1,0:T(8,128)(2,1)}, u32[]{:S(2)}) copy-start(bf16[512,1536]{1,0:T(8,128)(2,1)} %refs_1_.3) | copy-start | bytes 4718596
  9.9 8.1 %collective-permute-start.3 = (bf16[64,1536]{1,0:T(8,128)(2,1)S(1)}, bf16[64,1536]{1,0:T(8,128)(2,1)S(1)}, u32[]{:S(2)}, u32[]{:S(2)}) collective-permute-start(bf16[64,1536]{1,0:T(8,128)(2,1)S(1)} %get-tuple-element.27), channel_id=1, source_target_pairs={{0,8},{2,10},{4,0},{6,2},{8,12},{10,14},{12,4},{14,6},{1,9},{3,11}... | collective-permute-start | bytes 589832 | tf_op jit(solution)/shard_map/ppermute | solution.py:35
  11.3 7.9 %collective-permute-start.6 = (bf16[64,1536]{1,0:T(8,128)(2,1)S(1)}, bf16[64,1536]{1,0:T(8,128)(2,1)S(1)}, u32[]{:S(2)}, u32[]{:S(2)}) collective-permute-start(bf16[64,1536]{1,0:T(8,128)(2,1)S(1)} %bitcast.9), channel_id=1, source_target_pairs={{0,2},{2,0},{4,6},{6,4},{8,10},{10,8},{12,14},{14,12},{1,3},{3,1},... | collective-permute-start | bytes 589832 | tf_op jit(solution)/shard_map/ppermute | solution.py:25
  11.6 9.9 %collective-permute-start.7 = (bf16[64,1536]{1,0:T(8,128)(2,1)S(1)}, bf16[64,1536]{1,0:T(8,128)(2,1)S(1)}, u32[]{:S(2)}, u32[]{:S(2)}) collective-permute-start(bf16[64,1536]{1,0:T(8,128)(2,1)S(1)} %get-tuple-element.26.refs_4_.refs_8_), channel_id=1, source_target_pairs={{0,16},{1,3},{2,18},{3,1},{4,20},{5,7},{6,22},{7,5},{8,24},{9,11},... | collective-permute-start | bytes 589832 | tf_op jit(solution)/shard_map/ppermute | solution.py:45
  13.4 9.9 %collective-permute-start.5 = (bf16[64,1536]{1,0:T(8,128)(2,1)S(1)}, bf16[64,1536]{1,0:T(8,128)(2,1)S(1)}, u32[]{:S(2)}, u32[]{:S(2)}) collective-permute-start(bf16[64,1536]{1,0:T(8,128)(2,1)S(1)} %get-tuple-element.26.refs_4_.refs_8_), channel_id=1, source_target_pairs={{0,2},{1,17},{2,0},{3,19},{4,6},{5,21},{6,4},{7,23},{8,10},{9,25},... | collective-permute-start | bytes 589832 | tf_op jit(solution)/shard_map/ppermute | solution.py:45
  14.9 8.9 %collective-permute-start.4 = (bf16[64,1536]{1,0:T(8,128)(2,1)S(1)}, bf16[64,1536]{1,0:T(8,128)(2,1)S(1)}, u32[]{:S(2)}, u32[]{:S(2)}) collective-permute-start(bf16[64,1536]{1,0:T(8,128)(2,1)S(1)} %get-tuple-element.26.refs_4_.refs_8_), channel_id=1, source_target_pairs={{0,4},{2,6},{4,12},{6,14},{8,0},{10,2},{12,8},{14,10},{1,5},{3,7},... | collective-permute-start | bytes 589832 | tf_op jit(solution)/shard_map/ppermute | solution.py:35
  18.1 9.2 %collective-permute-start.10 = (bf16[64,1536]{1,0:T(8,128)(2,1)S(1)}, bf16[64,1536]{1,0:T(8,128)(2,1)S(1)}, u32[]{:S(2)}, u32[]{:S(2)}) collective-permute-start(bf16[64,1536]{1,0:T(8,128)(2,1)S(1)} %get-tuple-element.30.refs_5_.refs_9_), channel_id=1, source_target_pairs={{0,16},{1,3},{2,18},{3,1},{4,20},{5,7},{6,22},{7,5},{8,24},{9,11},... | collective-permute-start | bytes 589832 | tf_op jit(solution)/shard_map/ppermute | solution.py:45
  19.2 8.1 %collective-permute-start.8 = (bf16[64,1536]{1,0:T(8,128)(2,1)S(1)}, bf16[64,1536]{1,0:T(8,128)(2,1)S(1)}, u32[]{:S(2)}, u32[]{:S(2)}) collective-permute-start(bf16[64,1536]{1,0:T(8,128)(2,1)S(1)} %get-tuple-element.30.refs_5_.refs_9_), channel_id=1, source_target_pairs={{0,2},{1,17},{2,0},{3,19},{4,6},{5,21},{6,4},{7,23},{8,10},{9,25},... | collective-permute-start | bytes 589832 | tf_op jit(solution)/shard_map/ppermute | solution.py:45
  23.9 7.6 %collective-permute-start.11 = (bf16[64,1536]{1,0:T(8,128)(2,1)S(1)}, bf16[64,1536]{1,0:T(8,128)(2,1)S(1)}, u32[]{:S(2)}, u32[]{:S(2)}) collective-permute-start(bf16[64,1536]{1,0:T(8,128)(2,1)S(1)} %get-tuple-element.34.refs_6_.refs_10_), channel_id=1, source_target_pairs={{0,16},{1,3},{2,18},{3,1},{4,20},{5,7},{6,22},{7,5},{8,24},{9,11},... | collective-permute-start | bytes 589832 | tf_op jit(solution)/shard_map/ppermute | solution.py:45
  25.4 10.3 %collective-permute-start.12 = (bf16[64,1536]{1,0:T(8,128)(2,1)S(1)}, bf16[64,1536]{1,0:T(8,128)(2,1)S(1)}, u32[]{:S(2)}, u32[]{:S(2)}) collective-permute-start(bf16[64,1536]{1,0:T(8,128)(2,1)S(1)} %get-tuple-element.35), channel_id=1, source_target_pairs={{0,16},{1,3},{2,18},{3,1},{4,20},{5,7},{6,22},{7,5},{8,24},{9,11},... | collective-permute-start | bytes 589832 | tf_op jit(solution)/shard_map/ppermute | solution.py:45
  25.9 8.5 %collective-permute-start.9 = (bf16[64,1536]{1,0:T(8,128)(2,1)S(1)}, bf16[64,1536]{1,0:T(8,128)(2,1)S(1)}, u32[]{:S(2)}, u32[]{:S(2)}) collective-permute-start(bf16[64,1536]{1,0:T(8,128)(2,1)S(1)} %get-tuple-element.35), channel_id=1, source_target_pairs={{0,4},{2,6},{4,12},{6,14},{8,0},{10,2},{12,8},{14,10},{1,5},{3,7},... | collective-permute-start | bytes 589832 | tf_op jit(solution)/shard_map/ppermute | solution.py:35
  27.3 8.4 %collective-permute-start.13 = (bf16[64,1536]{1,0:T(8,128)(2,1)S(1)}, bf16[64,1536]{1,0:T(8,128)(2,1)S(1)}, u32[]{:S(2)}, u32[]{:S(2)}) collective-permute-start(bf16[64,1536]{1,0:T(8,128)(2,1)S(1)} %get-tuple-element.42), channel_id=1, source_target_pairs={{0,2},{1,17},{2,0},{3,19},{4,6},{5,21},{6,4},{7,23},{8,10},{9,25},... | collective-permute-start | bytes 589832 | tf_op jit(solution)/shard_map/ppermute | solution.py:45
  31.4 5.7 %collective-permute-start.14 = (bf16[64,1536]{1,0:T(8,128)(2,1)S(1)}, bf16[64,1536]{1,0:T(8,128)(2,1)S(1)}, u32[]{:S(2)}, u32[]{:S(2)}) collective-permute-start(bf16[64,1536]{1,0:T(8,128)(2,1)S(1)} %get-tuple-element.43), channel_id=1, source_target_pairs={{0,2},{1,17},{2,0},{3,19},{4,6},{5,21},{6,4},{7,23},{8,10},{9,25},... | collective-permute-start | bytes 589832 | tf_op jit(solution)/shard_map/ppermute | solution.py:45
  31.9 2.6 %copy-start.3 = (bf16[1,1536,64]{1,2,0:T(8,128)(2,1)S(1)}, bf16[1,1536,64]{1,2,0:T(8,128)(2,1)}, u32[]{:S(2)}) copy-start(bf16[1,1536,64]{1,2,0:T(8,128)(2,1)} %param.8) | copy-start | bytes 589828
  31.9 2.6 %copy-start.5 = (s32[512,1]{0,1:T(1,128)S(1)}, s32[512,1]{0,1:T(1,128)}, u32[]{:S(2)}) copy-start(s32[512,1]{0,1:T(1,128)} %param.6) | copy-start | bytes 6148
  37.2 1.6 %collective-permute-start.15 = (f32[512,128]{1,0:T(8,128)S(1)}, f32[512,128]{1,0:T(8,128)S(1)}, u32[]{:S(2)}, u32[]{:S(2)}) collective-permute-start(f32[512,128]{1,0:T(8,128)S(1)} %shard_map.67.refs_1_), channel_id=1, source_target_pairs={{0,1},{1,0},{2,3},{3,2},{4,5},{5,4},{6,7},{7,6},{8,9},{9,8},{10,11... | collective-permute-start | bytes 786440 | tf_op jit(solution)/shard_map/ppermute | solution.py:21

commit v24 on v22

--- a/solution.py
+++ b/solution.py
@@ -296,7 +296,7 @@
         down_beside, up_beside = neighbour(down, shards), neighbour(up, shards)
         ready = token
         one, token = pack([(line[1], 0, rank)], token, down_beside, other)
-        (back,) = pack([(piece, 0, rank)], ready, tokens=0)
+        (back,) = pack([(piece, 0, rank)], ready, line[1], tokens=0)
         line[3] = along_line(back, shards, 3)
         line[2] = along_line(one, shards, 1)
         one_first, one_second = in_plane(one, shards, True), in_plane(one, shards, False)

time: 41.3 us -> 42.6 us (1.031)
  the two profiles are of different devices: /device:TPU:11 before, /device:TPU:27 now
where the time goes in v24:
time: 42.6 us; the launch traced here: 42.5 us
  starting transfers between devices  16.1 us (38%)
  waiting for transfers between devices  12.7 us (30%)
  Pallas kernels  8.76 us (21%)
  local copies, waits for them, and re-layouts  3.7 us (9%)
  other arithmetic  1.04 us (2%)
    ppermute x2, starting transfers between devices, swap(): return lax.ppermute(value, axis, [(0, 1), (1, 0)])  7.19 us
    ppermute x8, waiting for transfers between devices, in_plane(): return lax.ppermute(value, AXES, pairs)  6.33 us
    pallas_call x3, Pallas kernels, base(): pl.pallas_call(placed(base_kernel, skip=skip), out_shape=[jax.ShapeDtypeS...  5.37 us
    ppermute x4, waiting for transfers between devices, along_line(): lax.ppermute(value, 'shard', [(i, ring_step(i, step)) for i in range(shar...  5.2 us
    ppermute x8, starting transfers between devices, in_plane(): return lax.ppermute(value, AXES, pairs)  4.58 us
    unnamed x12, local copies, waits for them, and re-layouts  3.7 us
    ppermute x2, starting transfers between devices, neighbour(): return lax.ppermute(value, 'shard', [(i, i ^ 1) for i in range(shards)])  2.54 us
    pallas_call x1, Pallas kernels, on_device(): pl.pallas_call(placed(up_kernel, base_parts=len(parts)), out_shape=jax.Sh...  2.06 us
  transfers between devices with their start and end apart: 16, of which 7 were waited for; matrix products, arithmetic and copies ran while one was open for 2% of the time, Pallas kernels for 16%

profile of v24, /device:TPU:27, one launch (start us, length us, event | category | flops | bytes accessed | tf_op | source)
XLA Modules:
  0.0 42.5 jit_solution(9383513901435495743)
XLA Ops:
  0.0 0.7 %collective-permute-start.2 = (bf16[512,1536]{1,0:T(8,128)(2,1)}, bf16[512,1536]{1,0:T(8,128)(2,1)S(1)}, u32[]{:S(2)}, u32[]{:S(2)}) collective-permute-start(bf16[512,1536]{1,0:T(8,128)(2,1)} %refs_1_.3), channel_id=1, source_target_pairs={{0,1},{1,0},{2,3},{3,2},{4,5},{5,4},{6,7},{7,6},{8,9},{9,8},{10,11... | collective-permute-start | bytes 4718600 | tf_op jit(solution)/shard_map/ppermute | solution.py:21
  0.7 1.0 %broadcast_select_fusion.refs_0_ = bf16[64,1536]{1,0:T(8,128)(2,1)S(1)} fusion(pred[]{:T(512)S(6)} %eq.3, bf16[1,64,1536]{2,1,0:T(8,128)(2,1)} %param.9, bf16[1,1536,64]{1,2,0:T(8,128)(2,1)} %param.8), kind=kLoop, calls=%fused_computation | loop fusion | flops 98304 | bytes 589825 | tf_op jit(solution)/shard_map/jit(_where)/select_n | solution.py:293
  1.7 0.2 collective-permute-start.1
  1.9 1.2 %collective-permute-start = (bf16[64,1536]{1,0:T(8,128)(2,1)}, bf16[64,1536]{1,0:T(8,128)(2,1)S(1)}, u32[]{:S(2)}, u32[]{:S(2)}) collective-permute-start(bf16[64,1536]{1,0:T(8,128)(2,1)} %bitcast.7), channel_id=1, source_target_pairs={{0,2},{2,0},{4,6},{6,4},{8,10},{10,8},{12,14},{14,12},{1,3},{3,1},... | collective-permute-start | bytes 589832 | tf_op jit(solution)/shard_map/ppermute | solution.py:25
  3.2 0.0 copy-start
  3.2 3.7 %copy-done = bf16[3072,1536]{1,0:T(8,128)(2,1)S(1)} copy-done((bf16[3072,1536]{1,0:T(8,128)(2,1)S(1)}, bf16[3072,1536]{1,0:T(8,128)(2,1)}, u32[]{:S(2)}) %copy-start) | copy-done | bytes 9437208
  6.9 0.0 copy-start.4
  6.9 2.3 %collective-permute-done.1.refs_0_.refs_2_ = bf16[64,1536]{1,0:T(8,128)(2,1)S(1)} collective-permute-done((bf16[64,1536]{1,0:T(8,128)(2,1)S(1)}, bf16[64,1536]{1,0:T(8,128)(2,1)S(1)}, u32[]{:S(2)}, u32[]{:S(2)}) %collective-permute-start.1) | collective-permute-done | bytes 196640 | tf_op jit(solution)/shard_map/ppermute | solution.py:35
  9.2 0.1 collective-permute-start.3
  9.3 0.0 copy-done.4
  9.3 1.3 %collective-permute-start.5 = (bf16[64,1536]{1,0:T(8,128)(2,1)S(1)}, bf16[64,1536]{1,0:T(8,128)(2,1)S(1)}, u32[]{:S(2)}, u32[]{:S(2)}) collective-permute-start(bf16[64,1536]{1,0:T(8,128)(2,1)S(1)} %bitcast.9), channel_id=1, source_target_pairs={{0,2},{2,0},{4,6},{6,4},{8,10},{10,8},{12,14},{14,12},{1,3},{3,1},... | collective-permute-start | bytes 589832 | tf_op jit(solution)/shard_map/ppermute | solution.py:25
  10.6 0.0 collective-permute-done.refs_2_.refs_3_
  10.6 0.0 collective-permute-done.2.refs_3_.refs_1_
  10.6 1.4 %collective-permute-start.4 = (bf16[64,1536]{1,0:T(8,128)(2,1)S(1)}, bf16[64,1536]{1,0:T(8,128)(2,1)S(1)}, u32[]{:S(2)}, u32[]{:S(2)}) collective-permute-start(bf16[64,1536]{1,0:T(8,128)(2,1)S(1)} %get-tuple-element.25.refs_4_.refs_8_), channel_id=1, source_target_pairs={{0,4},{2,6},{4,12},{6,14},{8,0},{10,2},{12,8},{14,10},{1,5},{3,7},... | collective-permute-start | bytes 589832 | tf_op jit(solution)/shard_map/ppermute | solution.py:35
  12.1 0.2 collective-permute-start.8
  12.3 0.3 collective-permute-start.6
  12.5 0.0 copy-done.1
  12.6 0.0 copy-done.2
  12.6 1.0 %shard_map.58 = (f32[512,256]{1,0:T(8,128)S(1)}, f32[8,128]{1,0:T(8,128)S(1)}) custom-call(bf16[512,1536]{1,0:T(8,128)(2,1)S(1)} %copy-done.2, bf16[512,1536]{1,0:T(8,128)(2,1)S(1)} %collective-permute-done.2.refs_3_.refs_1_, bf16[3072,1536]{1,0:T(8,128)(2,1)S(1)} %copy-done.1, f32[8,128]{1,0:T(8,128)S(1)} %get-tuple-element.26.refs_3_), custom_call_target="tpu_custom_call" | custom-call | flops 1000 | bytes 1000 | tf_op jit(solution)/shard_map/pallas_call | solution.py:215
  13.5 1.5 %collective-permute-done.3.refs_0_ = bf16[64,1536]{1,0:T(8,128)(2,1)S(1)} collective-permute-done((bf16[64,1536]{1,0:T(8,128)(2,1)S(1)}, bf16[64,1536]{1,0:T(8,128)(2,1)S(1)}, u32[]{:S(2)}, u32[]{:S(2)}) %collective-permute-start.3) | collective-permute-done | bytes 196640 | tf_op jit(solution)/shard_map/ppermute | solution.py:35
  15.0 1.3 %collective-permute-start.10 = (bf16[64,1536]{1,0:T(8,128)(2,1)S(1)}, bf16[64,1536]{1,0:T(8,128)(2,1)S(1)}, u32[]{:S(2)}, u32[]{:S(2)}) collective-permute-start(bf16[64,1536]{1,0:T(8,128)(2,1)S(1)} %get-tuple-element.28.refs_5_.refs_9_), channel_id=1, source_target_pairs={{0,16},{1,3},{2,18},{3,1},{4,20},{5,7},{6,22},{7,5},{8,24},{9,11},... | collective-permute-start | bytes 589832 | tf_op jit(solution)/shard_map/ppermute | solution.py:45
  16.4 0.0 collective-permute-done.5.refs_4_.refs_7_
  16.4 0.3 collective-permute-start.7
  16.6 1.8 %shard_map.60 = (f32[512,512]{1,0:T(8,128)S(1)}, f32[8,128]{1,0:T(8,128)S(1)}) custom-call(bf16[512,1536]{1,0:T(8,128)(2,1)S(1)} %copy-done.2, bf16[512,1536]{1,0:T(8,128)(2,1)S(1)} %collective-permute-done.2.refs_3_.refs_1_, bf16[3072,1536]{1,0:T(8,128)(2,1)S(1)} %copy-done.1, f32[8,128]{1,0:T(8,128)S(1)} %get-tuple-element.29.refs_3_, ...), custom_call_target="tpu_custom_call" | custom-call | flops 1000 | bytes 1000 | tf_op jit(solution)/shard_map/pallas_call | solution.py:215
  18.4 1.4 %collective-permute-done.4.refs_0_ = bf16[64,1536]{1,0:T(8,128)(2,1)S(1)} collective-permute-done((bf16[64,1536]{1,0:T(8,128)(2,1)S(1)}, bf16[64,1536]{1,0:T(8,128)(2,1)S(1)}, u32[]{:S(2)}, u32[]{:S(2)}) %collective-permute-start.4) | collective-permute-done | bytes 196640 | tf_op jit(solution)/shard_map/ppermute | solution.py:35
  19.8 1.8 %collective-permute-start.11 = (bf16[64,1536]{1,0:T(8,128)(2,1)S(1)}, bf16[64,1536]{1,0:T(8,128)(2,1)S(1)}, u32[]{:S(2)}, u32[]{:S(2)}) collective-permute-start(bf16[64,1536]{1,0:T(8,128)(2,1)S(1)} %get-tuple-element.31.refs_6_.refs_10_), channel_id=1, source_target_pairs={{0,16},{1,3},{2,18},{3,1},{4,20},{5,7},{6,22},{7,5},{8,24},{9,11},... | collective-permute-start | bytes 589832 | tf_op jit(solution)/shard_map/ppermute | solution.py:45
  21.6 0.0 collective-permute-done.8.refs_2_.refs_10_.refs_14_
  21.6 0.0 collective-permute-done.6.refs_0_.refs_7_.refs_11_
  21.6 0.1 collective-permute-start.12
  21.7 0.0 collective-permute-start.9
  21.7 0.6 %collective-permute-done.10.refs_0_.refs_11_.refs_15_ = bf16[64,1536]{1,0:T(8,128)(2,1)S(1)} collective-permute-done((bf16[64,1536]{1,0:T(8,128)(2,1)S(1)}, bf16[64,1536]{1,0:T(8,128)(2,1)S(1)}, u32[]{:S(2)}, u32[]{:S(2)}) %collective-permute-start.10) | collective-permute-done | bytes 196640 | tf_op jit(solution)/shard_map/ppermute | solution.py:45
  22.3 0.0 collective-permute-done.7.refs_2_.refs_8_.refs_12_
  22.3 0.6 %collective-permute-start.13 = (bf16[64,1536]{1,0:T(8,128)(2,1)S(1)}, bf16[64,1536]{1,0:T(8,128)(2,1)S(1)}, u32[]{:S(2)}, u32[]{:S(2)}) collective-permute-start(bf16[64,1536]{1,0:T(8,128)(2,1)S(1)} %get-tuple-element.40), channel_id=1, source_target_pairs={{0,2},{1,17},{2,0},{3,19},{4,6},{5,21},{6,4},{7,23},{8,10},{9,25},... | collective-permute-start | bytes 589832 | tf_op jit(solution)/shard_map/ppermute | solution.py:45
  22.9 2.3 %collective-permute-done.11.refs_0_.refs_12_.refs_16_ = bf16[64,1536]{1,0:T(8,128)(2,1)S(1)} collective-permute-done((bf16[64,1536]{1,0:T(8,128)(2,1)S(1)}, bf16[64,1536]{1,0:T(8,128)(2,1)S(1)}, u32[]{:S(2)}, u32[]{:S(2)}) %collective-permute-start.11) | collective-permute-done | bytes 196640 | tf_op jit(solution)/shard_map/ppermute | solution.py:45
  25.2 0.1 collective-permute-start.14
  25.3 0.0 copy-start.3
  25.3 0.0 copy-start.5
  25.3 2.6 %shard_map.65 = (f32[512,768]{1,0:T(8,128)S(1)}, f32[8,128]{1,0:T(8,128)S(1)}) custom-call(bf16[512,1536]{1,0:T(8,128)(2,1)S(1)} %copy-done.2, bf16[512,1536]{1,0:T(8,128)(2,1)S(1)} %collective-permute-done.2.refs_3_.refs_1_, bf16[3072,1536]{1,0:T(8,128)(2,1)S(1)} %copy-done.1, f32[8,128]{1,0:T(8,128)S(1)} %get-tuple-element.36.refs_3_), custom_call_target="tpu_custom_call" | custom-call | flops 1000 | bytes 1000 | tf_op jit(solution)/shard_map/pallas_call | solution.py:215
  27.9 0.0 collective-permute-done.9.refs_9_.refs_13_
  27.9 0.0 copy-done.3
  27.9 0.0 copy-done.5
  27.9 1.2 %shard_map.66 = (f32[512,128]{1,0:T(8,128)S(1)}, s32[512,128]{1,0:T(8,128)S(1)}) custom-call(s32[1,512]{1,0:T(1,128)S(1)} %bitcast.11, bf16[512,1536]{1,0:T(8,128)(2,1)S(1)} %copy-done.2, bf16[64,1536]{1,0:T(8,128)(2,1)S(1)} %bitcast.8, bf16[64,1536]{1,0:T(8,128)(2,1)S(1)} %collective-permute-done.refs_2_.refs_3_, ...), custom_call_target="tpu_custom_call" | custom-call | tf_op jit(solution)/shard_map/pallas_call | solution.py:321
  29.2 0.0 collective-permute-done.13.refs_4_.refs_18_
  29.2 0.0 collective-permute-done.12.refs_3_.refs_17_
  29.2 3.5 %collective-permute-done.14.refs_5_.refs_19_ = bf16[64,1536]{1,0:T(8,128)(2,1)S(1)} collective-permute-done((bf16[64,1536]{1,0:T(8,128)(2,1)S(1)}, bf16[64,1536]{1,0:T(8,128)(2,1)S(1)}, u32[]{:S(2)}, u32[]{:S(2)}) %collective-permute-start.14) | collective-permute-done | bytes 196640 | tf_op jit(solution)/shard_map/ppermute | solution.py:45
  32.7 6.5 %collective-permute-start.15 = (f32[512,128]{1,0:T(8,128)S(1)}, f32[512,128]{1,0:T(8,128)S(1)}, u32[]{:S(2)}, u32[]{:S(2)}) collective-permute-start(f32[512,128]{1,0:T(8,128)S(1)} %shard_map.67.refs_1_), channel_id=1, source_target_pairs={{0,1},{1,0},{2,3},{3,2},{4,5},{5,4},{6,7},{7,6},{8,9},{9,8},{10,11... | collective-permute-start | bytes 786440 | tf_op jit(solution)/shard_map/ppermute | solution.py:21
  39.2 1.2 %collective-permute-done.15.refs_2_ = f32[512,128]{1,0:T(8,128)S(1)} collective-permute-done((f32[512,128]{1,0:T(8,128)S(1)}, f32[512,128]{1,0:T(8,128)S(1)}, u32[]{:S(2)}, u32[]{:S(2)}) %collective-permute-start.15) | collective-permute-done | bytes 262176 | tf_op jit(solution)/shard_map/ppermute | solution.py:21
  40.4 2.1 %shard_map.68 = bf16[512,1536]{1,0:T(8,128)(2,1)} custom-call(s32[512,128]{1,0:T(8,128)S(1)} %get-tuple-element.38.refs_0_, f32[512,128]{1,0:T(8,128)S(1)} %shard_map.67.refs_1_, f32[512,128]{1,0:T(8,128)S(1)} %collective-permute-done.15.refs_2_, f32[512,256]{1,0:T(8,128)S(1)} %get-tuple-element.42.refs_3_, f32[512,512]{1,0:T(8,128)S(1)} %get-tuple-element.43.refs_4_, ...), custom_call_target="tpu_custom_call" | custom-call | tf_op jit(solution)/shard_map/pallas_call | solution.py:348
  (11 shorter events, 0.1 us)
Async XLA Ops:
  0.0 10.6 %collective-permute-start.2 = (bf16[512,1536]{1,0:T(8,128)(2,1)}, bf16[512,1536]{1,0:T(8,128)(2,1)S(1)}, u32[]{:S(2)}, u32[]{:S(2)}) collective-permute-start(bf16[512,1536]{1,0:T(8,128)(2,1)} %refs_1_.3), channel_id=1, source_target_pairs={{0,1},{1,0},{2,3},{3,2},{4,5},{5,4},{6,7},{7,6},{8,9},{9,8},{10,11... | collective-permute-start | bytes 4718600 | tf_op jit(solution)/shard_map/ppermute | solution.py:21
  1.7 7.5 %collective-permute-start.1 = (bf16[64,1536]{1,0:T(8,128)(2,1)S(1)}, bf16[64,1536]{1,0:T(8,128)(2,1)S(1)}, u32[]{:S(2)}, u32[]{:S(2)}) collective-permute-start(bf16[64,1536]{1,0:T(8,128)(2,1)S(1)} %broadcast_select_fusion.refs_0_), channel_id=1, source_target_pairs={{0,4},{2,6},{4,12},{6,14},{8,0},{10,2},{12,8},{14,10},{1,5},{3,7},... | collective-permute-start | bytes 589832 | tf_op jit(solution)/shard_map/ppermute | solution.py:35
  1.9 8.7 %collective-permute-start = (bf16[64,1536]{1,0:T(8,128)(2,1)}, bf16[64,1536]{1,0:T(8,128)(2,1)S(1)}, u32[]{:S(2)}, u32[]{:S(2)}) collective-permute-start(bf16[64,1536]{1,0:T(8,128)(2,1)} %bitcast.7), channel_id=1, source_target_pairs={{0,2},{2,0},{4,6},{6,4},{8,10},{10,8},{12,14},{14,12},{1,3},{3,1},... | collective-permute-start | bytes 589832 | tf_op jit(solution)/shard_map/ppermute | solution.py:25
  3.2 3.7 %copy-start = (bf16[3072,1536]{1,0:T(8,128)(2,1)S(1)}, bf16[3072,1536]{1,0:T(8,128)(2,1)}, u32[]{:S(2)}) copy-start(bf16[3072,1536]{1,0:T(8,128)(2,1)} %refs_2_.5) | copy-start | bytes 28311556
  6.9 2.4 %copy-start.4 = (bf16[1,64,1536]{2,1,0:T(8,128)(2,1)S(1)}, bf16[1,64,1536]{2,1,0:T(8,128)(2,1)}, u32[]{:S(2)}) copy-start(bf16[1,64,1536]{2,1,0:T(8,128)(2,1)} %param.9) | copy-start | bytes 589828
  6.9 5.7 %copy-start.1 = (bf16[3072,1536]{1,0:T(8,128)(2,1)S(1)}, bf16[3072,1536]{1,0:T(8,128)(2,1)}, u32[]{:S(2)}) copy-start(bf16[3072,1536]{1,0:T(8,128)(2,1)} %refs_2_.5) | copy-start | bytes 28311556
  6.9 5.7 %copy-start.2 = (bf16[512,1536]{1,0:T(8,128)(2,1)S(1)}, bf16[512,1536]{1,0:T(8,128)(2,1)}, u32[]{:S(2)}) copy-start(bf16[512,1536]{1,0:T(8,128)(2,1)} %refs_1_.3) | copy-start | bytes 4718596
  9.2 5.8 %collective-permute-start.3 = (bf16[64,1536]{1,0:T(8,128)(2,1)S(1)}, bf16[64,1536]{1,0:T(8,128)(2,1)S(1)}, u32[]{:S(2)}, u32[]{:S(2)}) collective-permute-start(bf16[64,1536]{1,0:T(8,128)(2,1)S(1)} %shard_map.57), channel_id=1, source_target_pairs={{0,8},{2,10},{4,0},{6,2},{8,12},{10,14},{12,4},{14,6},{1,9},{3,11}... | collective-permute-start | bytes 589832 | tf_op jit(solution)/shard_map/ppermute | solution.py:35
  9.3 7.1 %collective-permute-start.5 = (bf16[64,1536]{1,0:T(8,128)(2,1)S(1)}, bf16[64,1536]{1,0:T(8,128)(2,1)S(1)}, u32[]{:S(2)}, u32[]{:S(2)}) collective-permute-start(bf16[64,1536]{1,0:T(8,128)(2,1)S(1)} %bitcast.9), channel_id=1, source_target_pairs={{0,2},{2,0},{4,6},{6,4},{8,10},{10,8},{12,14},{14,12},{1,3},{3,1},... | collective-permute-start | bytes 589832 | tf_op jit(solution)/shard_map/ppermute | solution.py:25
  10.6 9.1 %collective-permute-start.4 = (bf16[64,1536]{1,0:T(8,128)(2,1)S(1)}, bf16[64,1536]{1,0:T(8,128)(2,1)S(1)}, u32[]{:S(2)}, u32[]{:S(2)}) collective-permute-start(bf16[64,1536]{1,0:T(8,128)(2,1)S(1)} %get-tuple-element.25.refs_4_.refs_8_), channel_id=1, source_target_pairs={{0,4},{2,6},{4,12},{6,14},{8,0},{10,2},{12,8},{14,10},{1,5},{3,7},... | collective-permute-start | bytes 589832 | tf_op jit(solution)/shard_map/ppermute | solution.py:35
  12.1 9.5 %collective-permute-start.8 = (bf16[64,1536]{1,0:T(8,128)(2,1)S(1)}, bf16[64,1536]{1,0:T(8,128)(2,1)S(1)}, u32[]{:S(2)}, u32[]{:S(2)}) collective-permute-start(bf16[64,1536]{1,0:T(8,128)(2,1)S(1)} %get-tuple-element.25.refs_4_.refs_8_), channel_id=1, source_target_pairs={{0,16},{1,3},{2,18},{3,1},{4,20},{5,7},{6,22},{7,5},{8,24},{9,11},... | collective-permute-start | bytes 589832 | tf_op jit(solution)/shard_map/ppermute | solution.py:45
  12.3 9.3 %collective-permute-start.6 = (bf16[64,1536]{1,0:T(8,128)(2,1)S(1)}, bf16[64,1536]{1,0:T(8,128)(2,1)S(1)}, u32[]{:S(2)}, u32[]{:S(2)}) collective-permute-start(bf16[64,1536]{1,0:T(8,128)(2,1)S(1)} %get-tuple-element.25.refs_4_.refs_8_), channel_id=1, source_target_pairs={{0,2},{1,17},{2,0},{3,19},{4,6},{5,21},{6,4},{7,23},{8,10},{9,25},... | collective-permute-start | bytes 589832 | tf_op jit(solution)/shard_map/ppermute | solution.py:45
  15.0 7.3 %collective-permute-start.10 = (bf16[64,1536]{1,0:T(8,128)(2,1)S(1)}, bf16[64,1536]{1,0:T(8,128)(2,1)S(1)}, u32[]{:S(2)}, u32[]{:S(2)}) collective-permute-start(bf16[64,1536]{1,0:T(8,128)(2,1)S(1)} %get-tuple-element.28.refs_5_.refs_9_), channel_id=1, source_target_pairs={{0,16},{1,3},{2,18},{3,1},{4,20},{5,7},{6,22},{7,5},{8,24},{9,11},... | collective-permute-start | bytes 589832 | tf_op jit(solution)/shard_map/ppermute | solution.py:45
  16.4 6.0 %collective-permute-start.7 = (bf16[64,1536]{1,0:T(8,128)(2,1)S(1)}, bf16[64,1536]{1,0:T(8,128)(2,1)S(1)}, u32[]{:S(2)}, u32[]{:S(2)}) collective-permute-start(bf16[64,1536]{1,0:T(8,128)(2,1)S(1)} %get-tuple-element.28.refs_5_.refs_9_), channel_id=1, source_target_pairs={{0,2},{1,17},{2,0},{3,19},{4,6},{5,21},{6,4},{7,23},{8,10},{9,25},... | collective-permute-start | bytes 589832 | tf_op jit(solution)/shard_map/ppermute | solution.py:45
  19.8 5.4 %collective-permute-start.11 = (bf16[64,1536]{1,0:T(8,128)(2,1)S(1)}, bf16[64,1536]{1,0:T(8,128)(2,1)S(1)}, u32[]{:S(2)}, u32[]{:S(2)}) collective-permute-start(bf16[64,1536]{1,0:T(8,128)(2,1)S(1)} %get-tuple-element.31.refs_6_.refs_10_), channel_id=1, source_target_pairs={{0,16},{1,3},{2,18},{3,1},{4,20},{5,7},{6,22},{7,5},{8,24},{9,11},... | collective-permute-start | bytes 589832 | tf_op jit(solution)/shard_map/ppermute | solution.py:45
  21.6 7.6 %collective-permute-start.12 = (bf16[64,1536]{1,0:T(8,128)(2,1)S(1)}, bf16[64,1536]{1,0:T(8,128)(2,1)S(1)}, u32[]{:S(2)}, u32[]{:S(2)}) collective-permute-start(bf16[64,1536]{1,0:T(8,128)(2,1)S(1)} %get-tuple-element.33), channel_id=1, source_target_pairs={{0,16},{1,3},{2,18},{3,1},{4,20},{5,7},{6,22},{7,5},{8,24},{9,11},... | collective-permute-start | bytes 589832 | tf_op jit(solution)/shard_map/ppermute | solution.py:45
  21.7 6.2 %collective-permute-start.9 = (bf16[64,1536]{1,0:T(8,128)(2,1)S(1)}, bf16[64,1536]{1,0:T(8,128)(2,1)S(1)}, u32[]{:S(2)}, u32[]{:S(2)}) collective-permute-start(bf16[64,1536]{1,0:T(8,128)(2,1)S(1)} %get-tuple-element.33), channel_id=1, source_target_pairs={{0,4},{2,6},{4,12},{6,14},{8,0},{10,2},{12,8},{14,10},{1,5},{3,7},... | collective-permute-start | bytes 589832 | tf_op jit(solution)/shard_map/ppermute | solution.py:35
  22.3 6.8 %collective-permute-start.13 = (bf16[64,1536]{1,0:T(8,128)(2,1)S(1)}, bf16[64,1536]{1,0:T(8,128)(2,1)S(1)}, u32[]{:S(2)}, u32[]{:S(2)}) collective-permute-start(bf16[64,1536]{1,0:T(8,128)(2,1)S(1)} %get-tuple-element.40), channel_id=1, source_target_pairs={{0,2},{1,17},{2,0},{3,19},{4,6},{5,21},{6,4},{7,23},{8,10},{9,25},... | collective-permute-start | bytes 589832 | tf_op jit(solution)/shard_map/ppermute | solution.py:45
  25.2 7.5 %collective-permute-start.14 = (bf16[64,1536]{1,0:T(8,128)(2,1)S(1)}, bf16[64,1536]{1,0:T(8,128)(2,1)S(1)}, u32[]{:S(2)}, u32[]{:S(2)}) collective-permute-start(bf16[64,1536]{1,0:T(8,128)(2,1)S(1)} %get-tuple-element.41), channel_id=1, source_target_pairs={{0,2},{1,17},{2,0},{3,19},{4,6},{5,21},{6,4},{7,23},{8,10},{9,25},... | collective-permute-start | bytes 589832 | tf_op jit(solution)/shard_map/ppermute | solution.py:45
  25.3 2.6 %copy-start.3 = (bf16[1,1536,64]{1,2,0:T(8,128)(2,1)S(1)}, bf16[1,1536,64]{1,2,0:T(8,128)(2,1)}, u32[]{:S(2)}) copy-start(bf16[1,1536,64]{1,2,0:T(8,128)(2,1)} %param.8) | copy-start | bytes 589828
  25.3 2.6 %copy-start.5 = (s32[512,1]{0,1:T(1,128)S(1)}, s32[512,1]{0,1:T(1,128)}, u32[]{:S(2)}) copy-start(s32[512,1]{0,1:T(1,128)} %param.6) | copy-start | bytes 6148
  32.7 7.7 %collective-permute-start.15 = (f32[512,128]{1,0:T(8,128)S(1)}, f32[512,128]{1,0:T(8,128)S(1)}, u32[]{:S(2)}, u32[]{:S(2)}) collective-permute-start(f32[512,128]{1,0:T(8,128)S(1)} %shard_map.67.refs_1_), channel_id=1, source_target_pairs={{0,1},{1,0},{2,3},{3,2},{4,5},{5,4},{6,7},{7,6},{8,9},{9,8},{10,11... | collective-permute-start | bytes 786440 | tf_op jit(solution)/shard_map/ppermute | solution.py:21

commit v25 on v21

--- a/solution.py
+++ b/solution.py
@@ -272,7 +272,7 @@
     columns = adapters * rank
     holds_down = lax.axis_index("tensor") == lax.axis_index("replica")
     tiles = out_width // TILE
-    cuts = [0, out_width // 6, out_width // 2, out_width]
+    cuts = [0, out_width // 3, out_width // 2, out_width]
     down = jnp.swapaxes(adapter_down_weight, 1, 2).reshape(local_adapters * rank, half_width)
     up = adapter_up_weight.reshape(local_adapters * rank, out_width)
     row_ids = row_adapter_index.reshape(1, rows)

time: 40.1 us -> 40.1 us (level)
  starting transfers between devices: 19.7 us -> 18.1 us
  waiting for transfers between devices: 5.93 us -> 7.51 us
    ppermute x8, waiting for transfers between devices: 2.58 us -> 3.73 us  [in_plane(): return lax.ppermute(value, AXES, pairs)]
    ppermute x4, starting transfers between devices: 8.34 us -> 7.54 us  [along_line(): lax.ppermute(value, 'shard', [(i, ring_step(i, step)) for i in range(shar...]
    ppermute x8, starting transfers between devices: 9.1 us -> 8.31 us  [in_plane(): return lax.ppermute(value, AXES, pairs)]
    ppermute x4, waiting for transfers between devices: 1.82 us -> 2.25 us  [along_line(): lax.ppermute(value, 'shard', [(i, ring_step(i, step)) for i in range(shar...]
where the time goes in v25:
time: 40.1 us; the launch traced here: 39.9 us
  starting transfers between devices  18.1 us (45%)
  Pallas kernels  9.35 us (23%)
  waiting for transfers between devices  7.51 us (19%)
  local copies, waits for them, and re-layouts  3.7 us (9%)
  other arithmetic  1.04 us (3%)
    ppermute x8, starting transfers between devices, in_plane(): return lax.ppermute(value, AXES, pairs)  8.31 us
    ppermute x4, starting transfers between devices, along_line(): lax.ppermute(value, 'shard', [(i, ring_step(i, step)) for i in range(shar...  7.54 us
    pallas_call x3, Pallas kernels, base(): pl.pallas_call(placed(base_kernel, skip=skip), out_shape=[jax.ShapeDtypeS...  5.36 us
    ppermute x8, waiting for transfers between devices, in_plane(): return lax.ppermute(value, AXES, pairs)  3.73 us
    unnamed x12, local copies, waits for them, and re-layouts  3.7 us
    ppermute x4, waiting for transfers between devices, along_line(): lax.ppermute(value, 'shard', [(i, ring_step(i, step)) for i in range(shar...  2.25 us
    pallas_call x1, Pallas kernels, on_device(): pl.pallas_call(placed(up_kernel, base_parts=len(parts)), out_shape=jax.Sh...  2.05 us
    ppermute x2, starting transfers between devices, neighbour(): return lax.ppermute(value, 'shard', [(i, i ^ 1) for i in range(shards)])  1.77 us
  transfers between devices with their start and end apart: 16, of which 5 were waited for; matrix products, arithmetic and copies ran while one was open for 3% of the time, Pallas kernels for 18%

profile of v25, /device:TPU:0, one launch (start us, length us, event | category | flops | bytes accessed | tf_op | source)
XLA Modules:
  0.0 39.9 jit_solution(6574658386338967484)
XLA Ops:
  0.0 0.5 %collective-permute-start.2 = (bf16[512,1536]{1,0:T(8,128)(2,1)}, bf16[512,1536]{1,0:T(8,128)(2,1)S(1)}, u32[]{:S(2)}, u32[]{:S(2)}) collective-permute-start(bf16[512,1536]{1,0:T(8,128)(2,1)} %refs_1_.3), channel_id=1, source_target_pairs={{0,1},{1,0},{2,3},{3,2},{4,5},{5,4},{6,7},{7,6},{8,9},{9,8},{10,11... | collective-permute-start | bytes 4718600 | tf_op jit(solution)/shard_map/ppermute | solution.py:21
  0.5 1.0 %broadcast_select_fusion.refs_0_ = bf16[64,1536]{1,0:T(8,128)(2,1)S(1)} fusion(pred[]{:T(512)S(6)} %eq.3, bf16[1,64,1536]{2,1,0:T(8,128)(2,1)} %param.9, bf16[1,1536,64]{1,2,0:T(8,128)(2,1)} %param.8), kind=kLoop, calls=%fused_computation | loop fusion | flops 98304 | bytes 589825 | tf_op jit(solution)/shard_map/jit(_where)/select_n | solution.py:292
  1.5 2.6 %collective-permute-start.1 = (bf16[64,1536]{1,0:T(8,128)(2,1)S(1)}, bf16[64,1536]{1,0:T(8,128)(2,1)S(1)}, u32[]{:S(2)}, u32[]{:S(2)}) collective-permute-start(bf16[64,1536]{1,0:T(8,128)(2,1)S(1)} %broadcast_select_fusion.refs_0_), channel_id=1, source_target_pairs={{0,4},{2,6},{4,12},{6,14},{8,0},{10,2},{12,8},{14,10},{1,5},{3,7},... | collective-permute-start | bytes 589832 | tf_op jit(solution)/shard_map/ppermute | solution.py:35
  4.1 1.5 %collective-permute-start = (bf16[64,1536]{1,0:T(8,128)(2,1)}, bf16[64,1536]{1,0:T(8,128)(2,1)S(1)}, u32[]{:S(2)}, u32[]{:S(2)}) collective-permute-start(bf16[64,1536]{1,0:T(8,128)(2,1)} %bitcast.7), channel_id=1, source_target_pairs={{0,2},{2,0},{4,6},{6,4},{8,10},{10,8},{12,14},{14,12},{1,3},{3,1},... | collective-permute-start | bytes 589832 | tf_op jit(solution)/shard_map/ppermute | solution.py:25
  5.6 0.0 copy-start
  5.7 3.7 %copy-done = bf16[3072,1536]{1,0:T(8,128)(2,1)S(1)} copy-done((bf16[3072,1536]{1,0:T(8,128)(2,1)S(1)}, bf16[3072,1536]{1,0:T(8,128)(2,1)}, u32[]{:S(2)}) %copy-start) | copy-done | bytes 9437208
  9.3 0.0 copy-start.4
  9.3 0.0 copy-start.1
  9.3 0.6 %shard_map.57 = (bf16[64,1536]{1,0:T(8,128)(2,1)S(1)}, f32[8,128]{1,0:T(8,128)}) custom-call(bf16[64,1536]{1,0:T(8,128)(2,1)S(1)} %broadcast_select_fusion.refs_0_, f32[8,128]{1,0:T(8,128)S(1)} %shard_map.55.refs_1_), custom_call_target="tpu_custom_call" | custom-call | tf_op jit(solution)/shard_map/pallas_call | solution.py:92
  9.9 1.3 %collective-permute-start.3 = (bf16[64,1536]{1,0:T(8,128)(2,1)S(1)}, bf16[64,1536]{1,0:T(8,128)(2,1)S(1)}, u32[]{:S(2)}, u32[]{:S(2)}) collective-permute-start(bf16[64,1536]{1,0:T(8,128)(2,1)S(1)} %get-tuple-element.27), channel_id=1, source_target_pairs={{0,8},{2,10},{4,0},{6,2},{8,12},{10,14},{12,4},{14,6},{1,9},{3,11}... | collective-permute-start | bytes 589832 | tf_op jit(solution)/shard_map/ppermute | solution.py:35
  11.3 0.0 copy-done.4
  11.3 0.2 collective-permute-start.5
  11.5 0.0 collective-permute-done.1.refs_0_
  11.6 0.0 collective-permute-done.refs_2_.refs_3_
  11.6 0.0 collective-permute-done.2.refs_3_.refs_1_
  11.6 2.5 %collective-permute-start.4 = (bf16[64,1536]{1,0:T(8,128)(2,1)S(1)}, bf16[64,1536]{1,0:T(8,128)(2,1)S(1)}, u32[]{:S(2)}, u32[]{:S(2)}) collective-permute-start(bf16[64,1536]{1,0:T(8,128)(2,1)S(1)} %get-tuple-element.26.refs_4_.refs_8_), channel_id=1, source_target_pairs={{0,4},{2,6},{4,12},{6,14},{8,0},{10,2},{12,8},{14,10},{1,5},{3,7},... | collective-permute-start | bytes 589832 | tf_op jit(solution)/shard_map/ppermute | solution.py:35
  14.0 1.5 %collective-permute-start.8 = (bf16[64,1536]{1,0:T(8,128)(2,1)S(1)}, bf16[64,1536]{1,0:T(8,128)(2,1)S(1)}, u32[]{:S(2)}, u32[]{:S(2)}) collective-permute-start(bf16[64,1536]{1,0:T(8,128)(2,1)S(1)} %get-tuple-element.26.refs_4_.refs_8_), channel_id=1, source_target_pairs={{0,16},{1,3},{2,18},{3,1},{4,20},{5,7},{6,22},{7,5},{8,24},{9,11},... | collective-permute-start | bytes 589832 | tf_op jit(solution)/shard_map/ppermute | solution.py:45
  15.5 1.5 %collective-permute-start.6 = (bf16[64,1536]{1,0:T(8,128)(2,1)S(1)}, bf16[64,1536]{1,0:T(8,128)(2,1)S(1)}, u32[]{:S(2)}, u32[]{:S(2)}) collective-permute-start(bf16[64,1536]{1,0:T(8,128)(2,1)S(1)} %get-tuple-element.26.refs_4_.refs_8_), channel_id=1, source_target_pairs={{0,2},{1,17},{2,0},{3,19},{4,6},{5,21},{6,4},{7,23},{8,10},{9,25},... | collective-permute-start | bytes 589832 | tf_op jit(solution)/shard_map/ppermute | solution.py:45
  17.0 0.0 copy-done.1
  17.1 0.0 copy-done.2
  17.1 1.8 %shard_map.58 = (f32[512,512]{1,0:T(8,128)S(1)}, f32[8,128]{1,0:T(8,128)S(1)}) custom-call(bf16[512,1536]{1,0:T(8,128)(2,1)S(1)} %copy-done.2, bf16[512,1536]{1,0:T(8,128)(2,1)S(1)} %collective-permute-done.2.refs_3_.refs_1_, bf16[3072,1536]{1,0:T(8,128)(2,1)S(1)} %copy-done.1, f32[8,128]{1,0:T(8,128)S(1)} %get-tuple-element.28.refs_3_), custom_call_target="tpu_custom_call" | custom-call | flops 1000 | bytes 1000 | tf_op jit(solution)/shard_map/pallas_call | solution.py:214
  18.8 0.0 collective-permute-done.3.refs_0_
  18.9 1.0 %collective-permute-start.10 = (bf16[64,1536]{1,0:T(8,128)(2,1)S(1)}, bf16[64,1536]{1,0:T(8,128)(2,1)S(1)}, u32[]{:S(2)}, u32[]{:S(2)}) collective-permute-start(bf16[64,1536]{1,0:T(8,128)(2,1)S(1)} %get-tuple-element.30.refs_5_.refs_9_), channel_id=1, source_target_pairs={{0,16},{1,3},{2,18},{3,1},{4,20},{5,7},{6,22},{7,5},{8,24},{9,11},... | collective-permute-start | bytes 589832 | tf_op jit(solution)/shard_map/ppermute | solution.py:45
  19.8 0.0 collective-permute-done.5.refs_4_.refs_7_
  19.8 0.2 collective-permute-start.7
  20.0 1.0 %shard_map.60 = (f32[512,256]{1,0:T(8,128)S(1)}, f32[8,128]{1,0:T(8,128)S(1)}) custom-call(bf16[512,1536]{1,0:T(8,128)(2,1)S(1)} %copy-done.2, bf16[512,1536]{1,0:T(8,128)(2,1)S(1)} %collective-permute-done.2.refs_3_.refs_1_, bf16[3072,1536]{1,0:T(8,128)(2,1)S(1)} %copy-done.1, f32[8,128]{1,0:T(8,128)S(1)} %get-tuple-element.31.refs_3_, ...), custom_call_target="tpu_custom_call" | custom-call | flops 1000 | bytes 1000 | tf_op jit(solution)/shard_map/pallas_call | solution.py:214
  21.0 2.2 %collective-permute-done.4.refs_0_ = bf16[64,1536]{1,0:T(8,128)(2,1)S(1)} collective-permute-done((bf16[64,1536]{1,0:T(8,128)(2,1)S(1)}, bf16[64,1536]{1,0:T(8,128)(2,1)S(1)}, u32[]{:S(2)}, u32[]{:S(2)}) %collective-permute-start.4) | collective-permute-done | bytes 196640 | tf_op jit(solution)/shard_map/ppermute | solution.py:35
  23.2 1.6 %collective-permute-start.11 = (bf16[64,1536]{1,0:T(8,128)(2,1)S(1)}, bf16[64,1536]{1,0:T(8,128)(2,1)S(1)}, u32[]{:S(2)}, u32[]{:S(2)}) collective-permute-start(bf16[64,1536]{1,0:T(8,128)(2,1)S(1)} %get-tuple-element.33.refs_6_.refs_10_), channel_id=1, source_target_pairs={{0,16},{1,3},{2,18},{3,1},{4,20},{5,7},{6,22},{7,5},{8,24},{9,11},... | collective-permute-start | bytes 589832 | tf_op jit(solution)/shard_map/ppermute | solution.py:45
  24.8 0.0 collective-permute-done.8.refs_2_.refs_10_.refs_14_
  24.8 0.0 collective-permute-done.6.refs_0_.refs_7_.refs_11_
  24.8 0.6 %collective-permute-start.12 = (bf16[64,1536]{1,0:T(8,128)(2,1)S(1)}, bf16[64,1536]{1,0:T(8,128)(2,1)S(1)}, u32[]{:S(2)}, u32[]{:S(2)}) collective-permute-start(bf16[64,1536]{1,0:T(8,128)(2,1)S(1)} %get-tuple-element.35), channel_id=1, source_target_pairs={{0,16},{1,3},{2,18},{3,1},{4,20},{5,7},{6,22},{7,5},{8,24},{9,11},... | collective-permute-start | bytes 589832 | tf_op jit(solution)/shard_map/ppermute | solution.py:45
  25.4 1.1 %collective-permute-start.9 = (bf16[64,1536]{1,0:T(8,128)(2,1)S(1)}, bf16[64,1536]{1,0:T(8,128)(2,1)S(1)}, u32[]{:S(2)}, u32[]{:S(2)}) collective-permute-start(bf16[64,1536]{1,0:T(8,128)(2,1)S(1)} %get-tuple-element.35), channel_id=1, source_target_pairs={{0,4},{2,6},{4,12},{6,14},{8,0},{10,2},{12,8},{14,10},{1,5},{3,7},... | collective-permute-start | bytes 589832 | tf_op jit(solution)/shard_map/ppermute | solution.py:35
  26.5 0.0 collective-permute-done.10.refs_0_.refs_11_.refs_15_
  26.5 0.5 %collective-permute-done.7.refs_2_.refs_8_.refs_12_ = bf16[64,1536]{1,0:T(8,128)(2,1)S(1)} collective-permute-done((bf16[64,1536]{1,0:T(8,128)(2,1)S(1)}, bf16[64,1536]{1,0:T(8,128)(2,1)S(1)}, u32[]{:S(2)}, u32[]{:S(2)}) %collective-permute-start.7) | collective-permute-done | bytes 196640 | tf_op jit(solution)/shard_map/ppermute | solution.py:45
  27.1 1.0 %collective-permute-start.13 = (bf16[64,1536]{1,0:T(8,128)(2,1)S(1)}, bf16[64,1536]{1,0:T(8,128)(2,1)S(1)}, u32[]{:S(2)}, u32[]{:S(2)}) collective-permute-start(bf16[64,1536]{1,0:T(8,128)(2,1)S(1)} %get-tuple-element.42), channel_id=1, source_target_pairs={{0,2},{1,17},{2,0},{3,19},{4,6},{5,21},{6,4},{7,23},{8,10},{9,25},... | collective-permute-start | bytes 589832 | tf_op jit(solution)/shard_map/ppermute | solution.py:45
  28.1 2.3 %collective-permute-done.11.refs_0_.refs_12_.refs_16_ = bf16[64,1536]{1,0:T(8,128)(2,1)S(1)} collective-permute-done((bf16[64,1536]{1,0:T(8,128)(2,1)S(1)}, bf16[64,1536]{1,0:T(8,128)(2,1)S(1)}, u32[]{:S(2)}, u32[]{:S(2)}) %collective-permute-start.11) | collective-permute-done | bytes 196640 | tf_op jit(solution)/shard_map/ppermute | solution.py:45
  30.5 1.0 %collective-permute-start.14 = (bf16[64,1536]{1,0:T(8,128)(2,1)S(1)}, bf16[64,1536]{1,0:T(8,128)(2,1)S(1)}, u32[]{:S(2)}, u32[]{:S(2)}) collective-permute-start(bf16[64,1536]{1,0:T(8,128)(2,1)S(1)} %get-tuple-element.43), channel_id=1, source_target_pairs={{0,2},{1,17},{2,0},{3,19},{4,6},{5,21},{6,4},{7,23},{8,10},{9,25},... | collective-permute-start | bytes 589832 | tf_op jit(solution)/shard_map/ppermute | solution.py:45
  31.5 2.6 %shard_map.65 = (f32[512,768]{1,0:T(8,128)S(1)}, f32[8,128]{1,0:T(8,128)S(1)}) custom-call(bf16[512,1536]{1,0:T(8,128)(2,1)S(1)} %copy-done.2, bf16[512,1536]{1,0:T(8,128)(2,1)S(1)} %collective-permute-done.2.refs_3_.refs_1_, bf16[3072,1536]{1,0:T(8,128)(2,1)S(1)} %copy-done.1, f32[8,128]{1,0:T(8,128)S(1)} %get-tuple-element.38.refs_3_), custom_call_target="tpu_custom_call" | custom-call | flops 1000 | bytes 1000 | tf_op jit(solution)/shard_map/pallas_call | solution.py:214
  34.1 0.0 collective-permute-done.9.refs_9_.refs_13_
  34.1 0.0 copy-done.3
  34.1 0.0 copy-done.5
  34.1 1.2 %shard_map.66 = (f32[512,128]{1,0:T(8,128)S(1)}, s32[512,128]{1,0:T(8,128)S(1)}) custom-call(s32[1,512]{1,0:T(1,128)S(1)} %bitcast.11, bf16[512,1536]{1,0:T(8,128)(2,1)S(1)} %copy-done.2, bf16[64,1536]{1,0:T(8,128)(2,1)S(1)} %bitcast.8, bf16[64,1536]{1,0:T(8,128)(2,1)S(1)} %collective-permute-done.refs_2_.refs_3_, ...), custom_call_target="tpu_custom_call" | custom-call | tf_op jit(solution)/shard_map/pallas_call | solution.py:320
  35.3 0.0 collective-permute-done.13.refs_4_.refs_18_
  35.4 0.0 collective-permute-done.12.refs_3_.refs_17_
  35.4 0.8 %collective-permute-done.14.refs_5_.refs_19_ = bf16[64,1536]{1,0:T(8,128)(2,1)S(1)} collective-permute-done((bf16[64,1536]{1,0:T(8,128)(2,1)S(1)}, bf16[64,1536]{1,0:T(8,128)(2,1)S(1)}, u32[]{:S(2)}, u32[]{:S(2)}) %collective-permute-start.14) | collective-permute-done | bytes 196640 | tf_op jit(solution)/shard_map/ppermute | solution.py:45
  36.2 0.1 collective-permute-start.15
  36.3 1.5 %collective-permute-done.15.refs_2_ = f32[512,128]{1,0:T(8,128)S(1)} collective-permute-done((f32[512,128]{1,0:T(8,128)S(1)}, f32[512,128]{1,0:T(8,128)S(1)}, u32[]{:S(2)}, u32[]{:S(2)}) %collective-permute-start.15) | collective-permute-done | bytes 262176 | tf_op jit(solution)/shard_map/ppermute | solution.py:21
  37.8 2.1 %shard_map.68 = bf16[512,1536]{1,0:T(8,128)(2,1)} custom-call(s32[512,128]{1,0:T(8,128)S(1)} %get-tuple-element.40.refs_0_, f32[512,128]{1,0:T(8,128)S(1)} %shard_map.67.refs_1_, f32[512,128]{1,0:T(8,128)S(1)} %collective-permute-done.15.refs_2_, f32[512,512]{1,0:T(8,128)S(1)} %get-tuple-element.44.refs_3_, f32[512,256]{1,0:T(8,128)S(1)} %get-tuple-element.45.refs_4_, ...), custom_call_target="tpu_custom_call" | custom-call | tf_op jit(solution)/shard_map/pallas_call | solution.py:347
  (11 shorter events, 0.1 us)
Async XLA Ops:
  0.0 11.6 %collective-permute-start.2 = (bf16[512,1536]{1,0:T(8,128)(2,1)}, bf16[512,1536]{1,0:T(8,128)(2,1)S(1)}, u32[]{:S(2)}, u32[]{:S(2)}) collective-permute-start(bf16[512,1536]{1,0:T(8,128)(2,1)} %refs_1_.3), channel_id=1, source_target_pairs={{0,1},{1,0},{2,3},{3,2},{4,5},{5,4},{6,7},{7,6},{8,9},{9,8},{10,11... | collective-permute-start | bytes 4718600 | tf_op jit(solution)/shard_map/ppermute | solution.py:21
  1.5 10.1 %collective-permute-start.1 = (bf16[64,1536]{1,0:T(8,128)(2,1)S(1)}, bf16[64,1536]{1,0:T(8,128)(2,1)S(1)}, u32[]{:S(2)}, u32[]{:S(2)}) collective-permute-start(bf16[64,1536]{1,0:T(8,128)(2,1)S(1)} %broadcast_select_fusion.refs_0_), channel_id=1, source_target_pairs={{0,4},{2,6},{4,12},{6,14},{8,0},{10,2},{12,8},{14,10},{1,5},{3,7},... | collective-permute-start | bytes 589832 | tf_op jit(solution)/shard_map/ppermute | solution.py:35
  4.1 7.4 %collective-permute-start = (bf16[64,1536]{1,0:T(8,128)(2,1)}, bf16[64,1536]{1,0:T(8,128)(2,1)S(1)}, u32[]{:S(2)}, u32[]{:S(2)}) collective-permute-start(bf16[64,1536]{1,0:T(8,128)(2,1)} %bitcast.7), channel_id=1, source_target_pairs={{0,2},{2,0},{4,6},{6,4},{8,10},{10,8},{12,14},{14,12},{1,3},{3,1},... | collective-permute-start | bytes 589832 | tf_op jit(solution)/shard_map/ppermute | solution.py:25
  5.6 3.7 %copy-start = (bf16[3072,1536]{1,0:T(8,128)(2,1)S(1)}, bf16[3072,1536]{1,0:T(8,128)(2,1)}, u32[]{:S(2)}) copy-start(bf16[3072,1536]{1,0:T(8,128)(2,1)} %refs_2_.5) | copy-start | bytes 28311556
  9.3 2.0 %copy-start.4 = (bf16[1,64,1536]{2,1,0:T(8,128)(2,1)S(1)}, bf16[1,64,1536]{2,1,0:T(8,128)(2,1)}, u32[]{:S(2)}) copy-start(bf16[1,64,1536]{2,1,0:T(8,128)(2,1)} %param.9) | copy-start | bytes 589828
  9.3 7.7 %copy-start.1 = (bf16[3072,1536]{1,0:T(8,128)(2,1)S(1)}, bf16[3072,1536]{1,0:T(8,128)(2,1)}, u32[]{:S(2)}) copy-start(bf16[3072,1536]{1,0:T(8,128)(2,1)} %refs_2_.5) | copy-start | bytes 28311556
  9.3 7.7 %copy-start.2 = (bf16[512,1536]{1,0:T(8,128)(2,1)S(1)}, bf16[512,1536]{1,0:T(8,128)(2,1)}, u32[]{:S(2)}) copy-start(bf16[512,1536]{1,0:T(8,128)(2,1)} %refs_1_.3) | copy-start | bytes 4718596
  9.9 8.9 %collective-permute-start.3 = (bf16[64,1536]{1,0:T(8,128)(2,1)S(1)}, bf16[64,1536]{1,0:T(8,128)(2,1)S(1)}, u32[]{:S(2)}, u32[]{:S(2)}) collective-permute-start(bf16[64,1536]{1,0:T(8,128)(2,1)S(1)} %get-tuple-element.27), channel_id=1, source_target_pairs={{0,8},{2,10},{4,0},{6,2},{8,12},{10,14},{12,4},{14,6},{1,9},{3,11}... | collective-permute-start | bytes 589832 | tf_op jit(solution)/shard_map/ppermute | solution.py:35
  11.3 8.5 %collective-permute-start.5 = (bf16[64,1536]{1,0:T(8,128)(2,1)S(1)}, bf16[64,1536]{1,0:T(8,128)(2,1)S(1)}, u32[]{:S(2)}, u32[]{:S(2)}) collective-permute-start(bf16[64,1536]{1,0:T(8,128)(2,1)S(1)} %bitcast.9), channel_id=1, source_target_pairs={{0,2},{2,0},{4,6},{6,4},{8,10},{10,8},{12,14},{14,12},{1,3},{3,1},... | collective-permute-start | bytes 589832 | tf_op jit(solution)/shard_map/ppermute | solution.py:25
  11.6 11.6 %collective-permute-start.4 = (bf16[64,1536]{1,0:T(8,128)(2,1)S(1)}, bf16[64,1536]{1,0:T(8,128)(2,1)S(1)}, u32[]{:S(2)}, u32[]{:S(2)}) collective-permute-start(bf16[64,1536]{1,0:T(8,128)(2,1)S(1)} %get-tuple-element.26.refs_4_.refs_8_), channel_id=1, source_target_pairs={{0,4},{2,6},{4,12},{6,14},{8,0},{10,2},{12,8},{14,10},{1,5},{3,7},... | collective-permute-start | bytes 589832 | tf_op jit(solution)/shard_map/ppermute | solution.py:35
  14.0 10.8 %collective-permute-start.8 = (bf16[64,1536]{1,0:T(8,128)(2,1)S(1)}, bf16[64,1536]{1,0:T(8,128)(2,1)S(1)}, u32[]{:S(2)}, u32[]{:S(2)}) collective-permute-start(bf16[64,1536]{1,0:T(8,128)(2,1)S(1)} %get-tuple-element.26.refs_4_.refs_8_), channel_id=1, source_target_pairs={{0,16},{1,3},{2,18},{3,1},{4,20},{5,7},{6,22},{7,5},{8,24},{9,11},... | collective-permute-start | bytes 589832 | tf_op jit(solution)/shard_map/ppermute | solution.py:45
  15.5 9.3 %collective-permute-start.6 = (bf16[64,1536]{1,0:T(8,128)(2,1)S(1)}, bf16[64,1536]{1,0:T(8,128)(2,1)S(1)}, u32[]{:S(2)}, u32[]{:S(2)}) collective-permute-start(bf16[64,1536]{1,0:T(8,128)(2,1)S(1)} %get-tuple-element.26.refs_4_.refs_8_), channel_id=1, source_target_pairs={{0,2},{1,17},{2,0},{3,19},{4,6},{5,21},{6,4},{7,23},{8,10},{9,25},... | collective-permute-start | bytes 589832 | tf_op jit(solution)/shard_map/ppermute | solution.py:45
  18.9 7.7 %collective-permute-start.10 = (bf16[64,1536]{1,0:T(8,128)(2,1)S(1)}, bf16[64,1536]{1,0:T(8,128)(2,1)S(1)}, u32[]{:S(2)}, u32[]{:S(2)}) collective-permute-start(bf16[64,1536]{1,0:T(8,128)(2,1)S(1)} %get-tuple-element.30.refs_5_.refs_9_), channel_id=1, source_target_pairs={{0,16},{1,3},{2,18},{3,1},{4,20},{5,7},{6,22},{7,5},{8,24},{9,11},... | collective-permute-start | bytes 589832 | tf_op jit(solution)/shard_map/ppermute | solution.py:45
  19.8 7.2 %collective-permute-start.7 = (bf16[64,1536]{1,0:T(8,128)(2,1)S(1)}, bf16[64,1536]{1,0:T(8,128)(2,1)S(1)}, u32[]{:S(2)}, u32[]{:S(2)}) collective-permute-start(bf16[64,1536]{1,0:T(8,128)(2,1)S(1)} %get-tuple-element.30.refs_5_.refs_9_), channel_id=1, source_target_pairs={{0,2},{1,17},{2,0},{3,19},{4,6},{5,21},{6,4},{7,23},{8,10},{9,25},... | collective-permute-start | bytes 589832 | tf_op jit(solution)/shard_map/ppermute | solution.py:45
  23.2 7.2 %collective-permute-start.11 = (bf16[64,1536]{1,0:T(8,128)(2,1)S(1)}, bf16[64,1536]{1,0:T(8,128)(2,1)S(1)}, u32[]{:S(2)}, u32[]{:S(2)}) collective-permute-start(bf16[64,1536]{1,0:T(8,128)(2,1)S(1)} %get-tuple-element.33.refs_6_.refs_10_), channel_id=1, source_target_pairs={{0,16},{1,3},{2,18},{3,1},{4,20},{5,7},{6,22},{7,5},{8,24},{9,11},... | collective-permute-start | bytes 589832 | tf_op jit(solution)/shard_map/ppermute | solution.py:45
  24.8 10.5 %collective-permute-start.12 = (bf16[64,1536]{1,0:T(8,128)(2,1)S(1)}, bf16[64,1536]{1,0:T(8,128)(2,1)S(1)}, u32[]{:S(2)}, u32[]{:S(2)}) collective-permute-start(bf16[64,1536]{1,0:T(8,128)(2,1)S(1)} %get-tuple-element.35), channel_id=1, source_target_pairs={{0,16},{1,3},{2,18},{3,1},{4,20},{5,7},{6,22},{7,5},{8,24},{9,11},... | collective-permute-start | bytes 589832 | tf_op jit(solution)/shard_map/ppermute | solution.py:45
  25.4 8.7 %collective-permute-start.9 = (bf16[64,1536]{1,0:T(8,128)(2,1)S(1)}, bf16[64,1536]{1,0:T(8,128)(2,1)S(1)}, u32[]{:S(2)}, u32[]{:S(2)}) collective-permute-start(bf16[64,1536]{1,0:T(8,128)(2,1)S(1)} %get-tuple-element.35), channel_id=1, source_target_pairs={{0,4},{2,6},{4,12},{6,14},{8,0},{10,2},{12,8},{14,10},{1,5},{3,7},... | collective-permute-start | bytes 589832 | tf_op jit(solution)/shard_map/ppermute | solution.py:35
  27.1 8.3 %collective-permute-start.13 = (bf16[64,1536]{1,0:T(8,128)(2,1)S(1)}, bf16[64,1536]{1,0:T(8,128)(2,1)S(1)}, u32[]{:S(2)}, u32[]{:S(2)}) collective-permute-start(bf16[64,1536]{1,0:T(8,128)(2,1)S(1)} %get-tuple-element.42), channel_id=1, source_target_pairs={{0,2},{1,17},{2,0},{3,19},{4,6},{5,21},{6,4},{7,23},{8,10},{9,25},... | collective-permute-start | bytes 589832 | tf_op jit(solution)/shard_map/ppermute | solution.py:45
  30.5 5.7 %collective-permute-start.14 = (bf16[64,1536]{1,0:T(8,128)(2,1)S(1)}, bf16[64,1536]{1,0:T(8,128)(2,1)S(1)}, u32[]{:S(2)}, u32[]{:S(2)}) collective-permute-start(bf16[64,1536]{1,0:T(8,128)(2,1)S(1)} %get-tuple-element.43), channel_id=1, source_target_pairs={{0,2},{1,17},{2,0},{3,19},{4,6},{5,21},{6,4},{7,23},{8,10},{9,25},... | collective-permute-start | bytes 589832 | tf_op jit(solution)/shard_map/ppermute | solution.py:45
  31.5 2.6 %copy-start.3 = (bf16[1,1536,64]{1,2,0:T(8,128)(2,1)S(1)}, bf16[1,1536,64]{1,2,0:T(8,128)(2,1)}, u32[]{:S(2)}) copy-start(bf16[1,1536,64]{1,2,0:T(8,128)(2,1)} %param.8) | copy-start | bytes 589828
  31.5 2.6 %copy-start.5 = (s32[512,1]{0,1:T(1,128)S(1)}, s32[512,1]{0,1:T(1,128)}, u32[]{:S(2)}) copy-start(s32[512,1]{0,1:T(1,128)} %param.6) | copy-start | bytes 6148
  36.2 1.6 %collective-permute-start.15 = (f32[512,128]{1,0:T(8,128)S(1)}, f32[512,128]{1,0:T(8,128)S(1)}, u32[]{:S(2)}, u32[]{:S(2)}) collective-permute-start(f32[512,128]{1,0:T(8,128)S(1)} %shard_map.67.refs_1_), channel_id=1, source_target_pairs={{0,1},{1,0},{2,3},{3,2},{4,5},{5,4},{6,7},{7,6},{8,9},{9,8},{10,11... | collective-permute-start | bytes 786440 | tf_op jit(solution)/shard_map/ppermute | solution.py:21

commit v26 on v25

--- a/solution.py
+++ b/solution.py
@@ -302,9 +302,9 @@
         part_one, token = base(placed, latent, other, shared_weight, [token], cuts[0], cuts[1])
         three, token = pack([(line[3], 0, rank)], token)
         three_first, three_second = in_plane(three, shards, True), in_plane(three, shards, False)
-        part_two, token = base(placed, latent, other, shared_weight, [token, up_beside], cuts[1], cuts[2])
         two, token = pack([(line[2], 0, rank)], token)
         two_second = in_plane(two, shards, False)
+        part_two, token = base(placed, latent, other, shared_weight, [token, up_beside], cuts[1], cuts[2])
         turn, token = pack([(one_first, 0, rank)], token, one_second)
         corner_one = in_plane(turn, shards, False)
         two_first = along_line(turn, shards, 1)

time: 40.1 us -> 42.5 us (1.060)
  starting transfers between devices: 18.1 us -> 20.2 us
    ppermute x2, starting transfers between devices: 1.77 us -> 3.04 us  [neighbour(): return lax.ppermute(value, 'shard', [(i, i ^ 1) for i in range(shards)])]
    ppermute x4, waiting for transfers between devices: 2.25 us -> 2.93 us  [along_line(): lax.ppermute(value, 'shard', [(i, ring_step(i, step)) for i in range(shar...]
    ppermute x4, starting transfers between devices: 7.54 us -> 8.12 us  [along_line(): lax.ppermute(value, 'shard', [(i, ring_step(i, step)) for i in range(shar...]
  transfers between devices with their start and end apart: 16 -> 16, of which waited for: 5 -> 5; matrix products, arithmetic and copies ran while one was open for 3% -> 2% of each run, Pallas kernels for 18% -> 17%
where the time goes in v26:
time: 42.5 us; the launch traced here: 42.3 us
  starting transfers between devices  20.2 us (48%)
  Pallas kernels  9.35 us (22%)
  waiting for transfers between devices  7.9 us (19%)
  local copies, waits for them, and re-layouts  3.7 us (9%)
  other arithmetic  1.04 us (2%)
    ppermute x8, starting transfers between devices, in_plane(): return lax.ppermute(value, AXES, pairs)  8.47 us
    ppermute x4, starting transfers between devices, along_line(): lax.ppermute(value, 'shard', [(i, ring_step(i, step)) for i in range(shar...  8.12 us
    pallas_call x3, Pallas kernels, base(): pl.pallas_call(placed(base_kernel, skip=skip), out_shape=[jax.ShapeDtypeS...  5.36 us
    unnamed x12, local copies, waits for them, and re-layouts  3.7 us
    ppermute x8, waiting for transfers between devices, in_plane(): return lax.ppermute(value, AXES, pairs)  3.38 us
    ppermute x2, starting transfers between devices, neighbour(): return lax.ppermute(value, 'shard', [(i, i ^ 1) for i in range(shards)])  3.04 us
    ppermute x4, waiting for transfers between devices, along_line(): lax.ppermute(value, 'shard', [(i, ring_step(i, step)) for i in range(shar...  2.93 us
    pallas_call x1, Pallas kernels, on_device(): pl.pallas_call(placed(up_kernel, base_parts=len(parts)), out_shape=jax.Sh...  2.06 us
  transfers between devices with their start and end apart: 16, of which 5 were waited for; matrix products, arithmetic and copies ran while one was open for 2% of the time, Pallas kernels for 17%

profile of v26, /device:TPU:0, one launch (start us, length us, event | category | flops | bytes accessed | tf_op | source)
XLA Modules:
  0.0 42.3 jit_solution(17288302092899717607)
XLA Ops:
  0.0 0.5 %collective-permute-start.2 = (bf16[512,1536]{1,0:T(8,128)(2,1)}, bf16[512,1536]{1,0:T(8,128)(2,1)S(1)}, u32[]{:S(2)}, u32[]{:S(2)}) collective-permute-start(bf16[512,1536]{1,0:T(8,128)(2,1)} %refs_1_.3), channel_id=1, source_target_pairs={{0,1},{1,0},{2,3},{3,2},{4,5},{5,4},{6,7},{7,6},{8,9},{9,8},{10,11... | collective-permute-start | bytes 4718600 | tf_op jit(solution)/shard_map/ppermute | solution.py:21
  0.5 1.0 %broadcast_select_fusion.refs_0_ = bf16[64,1536]{1,0:T(8,128)(2,1)S(1)} fusion(pred[]{:T(512)S(6)} %eq.3, bf16[1,64,1536]{2,1,0:T(8,128)(2,1)} %param.9, bf16[1,1536,64]{1,2,0:T(8,128)(2,1)} %param.8), kind=kLoop, calls=%fused_computation | loop fusion | flops 98304 | bytes 589825 | tf_op jit(solution)/shard_map/jit(_where)/select_n | solution.py:292
  1.5 2.6 %collective-permute-start.1 = (bf16[64,1536]{1,0:T(8,128)(2,1)S(1)}, bf16[64,1536]{1,0:T(8,128)(2,1)S(1)}, u32[]{:S(2)}, u32[]{:S(2)}) collective-permute-start(bf16[64,1536]{1,0:T(8,128)(2,1)S(1)} %broadcast_select_fusion.refs_0_), channel_id=1, source_target_pairs={{0,4},{2,6},{4,12},{6,14},{8,0},{10,2},{12,8},{14,10},{1,5},{3,7},... | collective-permute-start | bytes 589832 | tf_op jit(solution)/shard_map/ppermute | solution.py:35
  4.1 1.5 %collective-permute-start = (bf16[64,1536]{1,0:T(8,128)(2,1)}, bf16[64,1536]{1,0:T(8,128)(2,1)S(1)}, u32[]{:S(2)}, u32[]{:S(2)}) collective-permute-start(bf16[64,1536]{1,0:T(8,128)(2,1)} %bitcast.7), channel_id=1, source_target_pairs={{0,2},{2,0},{4,6},{6,4},{8,10},{10,8},{12,14},{14,12},{1,3},{3,1},... | collective-permute-start | bytes 589832 | tf_op jit(solution)/shard_map/ppermute | solution.py:25
  5.6 0.0 copy-start
  5.7 3.7 %copy-done = bf16[3072,1536]{1,0:T(8,128)(2,1)S(1)} copy-done((bf16[3072,1536]{1,0:T(8,128)(2,1)S(1)}, bf16[3072,1536]{1,0:T(8,128)(2,1)}, u32[]{:S(2)}) %copy-start) | copy-done | bytes 9437208
  9.3 0.0 copy-start.1
  9.3 0.0 copy-start.4
  9.3 0.6 %shard_map.57 = (bf16[64,1536]{1,0:T(8,128)(2,1)S(1)}, f32[8,128]{1,0:T(8,128)}) custom-call(bf16[64,1536]{1,0:T(8,128)(2,1)S(1)} %broadcast_select_fusion.refs_0_, f32[8,128]{1,0:T(8,128)S(1)} %shard_map.55.refs_1_), custom_call_target="tpu_custom_call" | custom-call | tf_op jit(solution)/shard_map/pallas_call | solution.py:92
  9.9 1.3 %collective-permute-start.3 = (bf16[64,1536]{1,0:T(8,128)(2,1)S(1)}, bf16[64,1536]{1,0:T(8,128)(2,1)S(1)}, u32[]{:S(2)}, u32[]{:S(2)}) collective-permute-start(bf16[64,1536]{1,0:T(8,128)(2,1)S(1)} %get-tuple-element.27), channel_id=1, source_target_pairs={{0,8},{2,10},{4,0},{6,2},{8,12},{10,14},{12,4},{14,6},{1,9},{3,11}... | collective-permute-start | bytes 589832 | tf_op jit(solution)/shard_map/ppermute | solution.py:35
  11.3 0.0 collective-permute-done.1.refs_0_
  11.3 0.1 collective-permute-done.refs_2_.refs_3_
  11.4 0.0 collective-permute-done.2.refs_3_.refs_1_
  11.4 2.6 %collective-permute-start.4 = (bf16[64,1536]{1,0:T(8,128)(2,1)S(1)}, bf16[64,1536]{1,0:T(8,128)(2,1)S(1)}, u32[]{:S(2)}, u32[]{:S(2)}) collective-permute-start(bf16[64,1536]{1,0:T(8,128)(2,1)S(1)} %get-tuple-element.26.refs_4_.refs_8_), channel_id=1, source_target_pairs={{0,4},{2,6},{4,12},{6,14},{8,0},{10,2},{12,8},{14,10},{1,5},{3,7},... | collective-permute-start | bytes 589832 | tf_op jit(solution)/shard_map/ppermute | solution.py:35
  14.0 0.0 copy-done.4
  14.0 1.5 %collective-permute-start.7 = (bf16[64,1536]{1,0:T(8,128)(2,1)S(1)}, bf16[64,1536]{1,0:T(8,128)(2,1)S(1)}, u32[]{:S(2)}, u32[]{:S(2)}) collective-permute-start(bf16[64,1536]{1,0:T(8,128)(2,1)S(1)} %bitcast.9), channel_id=1, source_target_pairs={{0,2},{2,0},{4,6},{6,4},{8,10},{10,8},{12,14},{14,12},{1,3},{3,1},... | collective-permute-start | bytes 589832 | tf_op jit(solution)/shard_map/ppermute | solution.py:25
  15.6 1.5 %collective-permute-start.8 = (bf16[64,1536]{1,0:T(8,128)(2,1)S(1)}, bf16[64,1536]{1,0:T(8,128)(2,1)S(1)}, u32[]{:S(2)}, u32[]{:S(2)}) collective-permute-start(bf16[64,1536]{1,0:T(8,128)(2,1)S(1)} %get-tuple-element.26.refs_4_.refs_8_), channel_id=1, source_target_pairs={{0,16},{1,3},{2,18},{3,1},{4,20},{5,7},{6,22},{7,5},{8,24},{9,11},... | collective-permute-start | bytes 589832 | tf_op jit(solution)/shard_map/ppermute | solution.py:45
  17.1 0.5 %collective-permute-start.5 = (bf16[64,1536]{1,0:T(8,128)(2,1)S(1)}, bf16[64,1536]{1,0:T(8,128)(2,1)S(1)}, u32[]{:S(2)}, u32[]{:S(2)}) collective-permute-start(bf16[64,1536]{1,0:T(8,128)(2,1)S(1)} %get-tuple-element.26.refs_4_.refs_8_), channel_id=1, source_target_pairs={{0,2},{1,17},{2,0},{3,19},{4,6},{5,21},{6,4},{7,23},{8,10},{9,25},... | collective-permute-start | bytes 589832 | tf_op jit(solution)/shard_map/ppermute | solution.py:45
  17.6 0.0 copy-done.1
  17.6 0.0 copy-done.2
  17.6 1.8 %shard_map.58 = (f32[512,512]{1,0:T(8,128)S(1)}, f32[8,128]{1,0:T(8,128)S(1)}) custom-call(bf16[512,1536]{1,0:T(8,128)(2,1)S(1)} %copy-done.2, bf16[512,1536]{1,0:T(8,128)(2,1)S(1)} %collective-permute-done.2.refs_3_.refs_1_, bf16[3072,1536]{1,0:T(8,128)(2,1)S(1)} %copy-done.1, f32[8,128]{1,0:T(8,128)S(1)} %get-tuple-element.28.refs_3_), custom_call_target="tpu_custom_call" | custom-call | flops 1000 | bytes 1000 | tf_op jit(solution)/shard_map/pallas_call | solution.py:214
  19.4 0.0 collective-permute-done.3.refs_0_
  19.4 0.7 %collective-permute-start.10 = (bf16[64,1536]{1,0:T(8,128)(2,1)S(1)}, bf16[64,1536]{1,0:T(8,128)(2,1)S(1)}, u32[]{:S(2)}, u32[]{:S(2)}) collective-permute-start(bf16[64,1536]{1,0:T(8,128)(2,1)S(1)} %get-tuple-element.30.refs_5_.refs_9_), channel_id=1, source_target_pairs={{0,16},{1,3},{2,18},{3,1},{4,20},{5,7},{6,22},{7,5},{8,24},{9,11},... | collective-permute-start | bytes 589832 | tf_op jit(solution)/shard_map/ppermute | solution.py:45
  20.1 2.9 %collective-permute-done.4.refs_0_ = bf16[64,1536]{1,0:T(8,128)(2,1)S(1)} collective-permute-done((bf16[64,1536]{1,0:T(8,128)(2,1)S(1)}, bf16[64,1536]{1,0:T(8,128)(2,1)S(1)}, u32[]{:S(2)}, u32[]{:S(2)}) %collective-permute-start.4) | collective-permute-done | bytes 196640 | tf_op jit(solution)/shard_map/ppermute | solution.py:35
  23.0 1.3 %collective-permute-start.6 = (bf16[64,1536]{1,0:T(8,128)(2,1)S(1)}, bf16[64,1536]{1,0:T(8,128)(2,1)S(1)}, u32[]{:S(2)}, u32[]{:S(2)}) collective-permute-start(bf16[64,1536]{1,0:T(8,128)(2,1)S(1)} %get-tuple-element.30.refs_5_.refs_9_), channel_id=1, source_target_pairs={{0,2},{1,17},{2,0},{3,19},{4,6},{5,21},{6,4},{7,23},{8,10},{9,25},... | collective-permute-start | bytes 589832 | tf_op jit(solution)/shard_map/ppermute | solution.py:45
  24.3 0.0 collective-permute-done.7.refs_4_.refs_7_
  24.3 1.6 %collective-permute-start.11 = (bf16[64,1536]{1,0:T(8,128)(2,1)S(1)}, bf16[64,1536]{1,0:T(8,128)(2,1)S(1)}, u32[]{:S(2)}, u32[]{:S(2)}) collective-permute-start(bf16[64,1536]{1,0:T(8,128)(2,1)S(1)} %get-tuple-element.32.refs_6_.refs_10_), channel_id=1, source_target_pairs={{0,16},{1,3},{2,18},{3,1},{4,20},{5,7},{6,22},{7,5},{8,24},{9,11},... | collective-permute-start | bytes 589832 | tf_op jit(solution)/shard_map/ppermute | solution.py:45
  25.9 1.0 %shard_map.61 = (f32[512,256]{1,0:T(8,128)S(1)}, f32[8,128]{1,0:T(8,128)S(1)}) custom-call(bf16[512,1536]{1,0:T(8,128)(2,1)S(1)} %copy-done.2, bf16[512,1536]{1,0:T(8,128)(2,1)S(1)} %collective-permute-done.2.refs_3_.refs_1_, bf16[3072,1536]{1,0:T(8,128)(2,1)S(1)} %copy-done.1, f32[8,128]{1,0:T(8,128)S(1)} %get-tuple-element.33.refs_3_, ...), custom_call_target="tpu_custom_call" | custom-call | flops 1000 | bytes 1000 | tf_op jit(solution)/shard_map/pallas_call | solution.py:214
  26.9 0.0 collective-permute-done.8.refs_2_.refs_10_.refs_14_
  26.9 0.0 collective-permute-done.5.refs_0_.refs_7_.refs_11_
  26.9 0.8 %collective-permute-start.12 = (bf16[64,1536]{1,0:T(8,128)(2,1)S(1)}, bf16[64,1536]{1,0:T(8,128)(2,1)S(1)}, u32[]{:S(2)}, u32[]{:S(2)}) collective-permute-start(bf16[64,1536]{1,0:T(8,128)(2,1)S(1)} %get-tuple-element.35), channel_id=1, source_target_pairs={{0,16},{1,3},{2,18},{3,1},{4,20},{5,7},{6,22},{7,5},{8,24},{9,11},... | collective-permute-start | bytes 589832 | tf_op jit(solution)/shard_map/ppermute | solution.py:45
  27.7 1.5 %collective-permute-start.9 = (bf16[64,1536]{1,0:T(8,128)(2,1)S(1)}, bf16[64,1536]{1,0:T(8,128)(2,1)S(1)}, u32[]{:S(2)}, u32[]{:S(2)}) collective-permute-start(bf16[64,1536]{1,0:T(8,128)(2,1)S(1)} %get-tuple-element.35), channel_id=1, source_target_pairs={{0,4},{2,6},{4,12},{6,14},{8,0},{10,2},{12,8},{14,10},{1,5},{3,7},... | collective-permute-start | bytes 589832 | tf_op jit(solution)/shard_map/ppermute | solution.py:35
  29.2 0.0 collective-permute-done.10.refs_0_.refs_11_.refs_15_
  29.2 1.6 %collective-permute-done.6.refs_2_.refs_8_.refs_12_ = bf16[64,1536]{1,0:T(8,128)(2,1)S(1)} collective-permute-done((bf16[64,1536]{1,0:T(8,128)(2,1)S(1)}, bf16[64,1536]{1,0:T(8,128)(2,1)S(1)}, u32[]{:S(2)}, u32[]{:S(2)}) %collective-permute-start.6) | collective-permute-done | bytes 196640 | tf_op jit(solution)/shard_map/ppermute | solution.py:45
  30.8 1.1 %collective-permute-start.13 = (bf16[64,1536]{1,0:T(8,128)(2,1)S(1)}, bf16[64,1536]{1,0:T(8,128)(2,1)S(1)}, u32[]{:S(2)}, u32[]{:S(2)}) collective-permute-start(bf16[64,1536]{1,0:T(8,128)(2,1)S(1)} %get-tuple-element.42), channel_id=1, source_target_pairs={{0,2},{1,17},{2,0},{3,19},{4,6},{5,21},{6,4},{7,23},{8,10},{9,25},... | collective-permute-start | bytes 589832 | tf_op jit(solution)/shard_map/ppermute | solution.py:45
  31.9 0.0 collective-permute-done.11.refs_0_.refs_12_.refs_16_
  31.9 1.1 %collective-permute-start.14 = (bf16[64,1536]{1,0:T(8,128)(2,1)S(1)}, bf16[64,1536]{1,0:T(8,128)(2,1)S(1)}, u32[]{:S(2)}, u32[]{:S(2)}) collective-permute-start(bf16[64,1536]{1,0:T(8,128)(2,1)S(1)} %get-tuple-element.43), channel_id=1, source_target_pairs={{0,2},{1,17},{2,0},{3,19},{4,6},{5,21},{6,4},{7,23},{8,10},{9,25},... | collective-permute-start | bytes 589832 | tf_op jit(solution)/shard_map/ppermute | solution.py:45
  33.0 2.6 %shard_map.65 = (f32[512,768]{1,0:T(8,128)S(1)}, f32[8,128]{1,0:T(8,128)S(1)}) custom-call(bf16[512,1536]{1,0:T(8,128)(2,1)S(1)} %copy-done.2, bf16[512,1536]{1,0:T(8,128)(2,1)S(1)} %collective-permute-done.2.refs_3_.refs_1_, bf16[3072,1536]{1,0:T(8,128)(2,1)S(1)} %copy-done.1, f32[8,128]{1,0:T(8,128)S(1)} %get-tuple-element.38.refs_3_), custom_call_target="tpu_custom_call" | custom-call | flops 1000 | bytes 1000 | tf_op jit(solution)/shard_map/pallas_call | solution.py:214
  35.6 0.0 collective-permute-done.9.refs_9_.refs_13_
  35.6 0.0 copy-done.3
  35.6 0.0 copy-done.5
  35.6 1.2 %shard_map.66 = (f32[512,128]{1,0:T(8,128)S(1)}, s32[512,128]{1,0:T(8,128)S(1)}) custom-call(s32[1,512]{1,0:T(1,128)S(1)} %bitcast.11, bf16[512,1536]{1,0:T(8,128)(2,1)S(1)} %copy-done.2, bf16[64,1536]{1,0:T(8,128)(2,1)S(1)} %bitcast.8, bf16[64,1536]{1,0:T(8,128)(2,1)S(1)} %collective-permute-done.refs_2_.refs_3_, ...), custom_call_target="tpu_custom_call" | custom-call | tf_op jit(solution)/shard_map/pallas_call | solution.py:320
  36.8 0.0 collective-permute-done.13.refs_4_.refs_18_
  36.8 0.0 collective-permute-done.12.refs_3_.refs_17_
  36.9 1.8 %collective-permute-done.14.refs_5_.refs_19_ = bf16[64,1536]{1,0:T(8,128)(2,1)S(1)} collective-permute-done((bf16[64,1536]{1,0:T(8,128)(2,1)S(1)}, bf16[64,1536]{1,0:T(8,128)(2,1)S(1)}, u32[]{:S(2)}, u32[]{:S(2)}) %collective-permute-start.14) | collective-permute-done | bytes 196640 | tf_op jit(solution)/shard_map/ppermute | solution.py:45
  38.7 0.1 collective-permute-start.15
  38.7 1.5 %collective-permute-done.15.refs_2_ = f32[512,128]{1,0:T(8,128)S(1)} collective-permute-done((f32[512,128]{1,0:T(8,128)S(1)}, f32[512,128]{1,0:T(8,128)S(1)}, u32[]{:S(2)}, u32[]{:S(2)}) %collective-permute-start.15) | collective-permute-done | bytes 262176 | tf_op jit(solution)/shard_map/ppermute | solution.py:21
  40.3 2.1 %shard_map.68 = bf16[512,1536]{1,0:T(8,128)(2,1)} custom-call(s32[512,128]{1,0:T(8,128)S(1)} %get-tuple-element.40.refs_0_, f32[512,128]{1,0:T(8,128)S(1)} %shard_map.67.refs_1_, f32[512,128]{1,0:T(8,128)S(1)} %collective-permute-done.15.refs_2_, f32[512,512]{1,0:T(8,128)S(1)} %get-tuple-element.44.refs_3_, f32[512,256]{1,0:T(8,128)S(1)} %get-tuple-element.45.refs_4_, ...), custom_call_target="tpu_custom_call" | custom-call | tf_op jit(solution)/shard_map/pallas_call | solution.py:347
  (11 shorter events, 0.1 us)
Async XLA Ops:
  0.0 11.4 %collective-permute-start.2 = (bf16[512,1536]{1,0:T(8,128)(2,1)}, bf16[512,1536]{1,0:T(8,128)(2,1)S(1)}, u32[]{:S(2)}, u32[]{:S(2)}) collective-permute-start(bf16[512,1536]{1,0:T(8,128)(2,1)} %refs_1_.3), channel_id=1, source_target_pairs={{0,1},{1,0},{2,3},{3,2},{4,5},{5,4},{6,7},{7,6},{8,9},{9,8},{10,11... | collective-permute-start | bytes 4718600 | tf_op jit(solution)/shard_map/ppermute | solution.py:21
  1.5 9.8 %collective-permute-start.1 = (bf16[64,1536]{1,0:T(8,128)(2,1)S(1)}, bf16[64,1536]{1,0:T(8,128)(2,1)S(1)}, u32[]{:S(2)}, u32[]{:S(2)}) collective-permute-start(bf16[64,1536]{1,0:T(8,128)(2,1)S(1)} %broadcast_select_fusion.refs_0_), channel_id=1, source_target_pairs={{0,4},{2,6},{4,12},{6,14},{8,0},{10,2},{12,8},{14,10},{1,5},{3,7},... | collective-permute-start | bytes 589832 | tf_op jit(solution)/shard_map/ppermute | solution.py:35
  4.1 7.2 %collective-permute-start = (bf16[64,1536]{1,0:T(8,128)(2,1)}, bf16[64,1536]{1,0:T(8,128)(2,1)S(1)}, u32[]{:S(2)}, u32[]{:S(2)}) collective-permute-start(bf16[64,1536]{1,0:T(8,128)(2,1)} %bitcast.7), channel_id=1, source_target_pairs={{0,2},{2,0},{4,6},{6,4},{8,10},{10,8},{12,14},{14,12},{1,3},{3,1},... | collective-permute-start | bytes 589832 | tf_op jit(solution)/shard_map/ppermute | solution.py:25
  5.6 3.7 %copy-start = (bf16[3072,1536]{1,0:T(8,128)(2,1)S(1)}, bf16[3072,1536]{1,0:T(8,128)(2,1)}, u32[]{:S(2)}) copy-start(bf16[3072,1536]{1,0:T(8,128)(2,1)} %refs_2_.5) | copy-start | bytes 28311556
  9.3 8.2 %copy-start.1 = (bf16[3072,1536]{1,0:T(8,128)(2,1)S(1)}, bf16[3072,1536]{1,0:T(8,128)(2,1)}, u32[]{:S(2)}) copy-start(bf16[3072,1536]{1,0:T(8,128)(2,1)} %refs_2_.5) | copy-start | bytes 28311556
  9.3 4.7 %copy-start.4 = (bf16[1,64,1536]{2,1,0:T(8,128)(2,1)S(1)}, bf16[1,64,1536]{2,1,0:T(8,128)(2,1)}, u32[]{:S(2)}) copy-start(bf16[1,64,1536]{2,1,0:T(8,128)(2,1)} %param.9) | copy-start | bytes 589828
  9.3 8.2 %copy-start.2 = (bf16[512,1536]{1,0:T(8,128)(2,1)S(1)}, bf16[512,1536]{1,0:T(8,128)(2,1)}, u32[]{:S(2)}) copy-start(bf16[512,1536]{1,0:T(8,128)(2,1)} %refs_1_.3) | copy-start | bytes 4718596
  9.9 9.4 %collective-permute-start.3 = (bf16[64,1536]{1,0:T(8,128)(2,1)S(1)}, bf16[64,1536]{1,0:T(8,128)(2,1)S(1)}, u32[]{:S(2)}, u32[]{:S(2)}) collective-permute-start(bf16[64,1536]{1,0:T(8,128)(2,1)S(1)} %get-tuple-element.27), channel_id=1, source_target_pairs={{0,8},{2,10},{4,0},{6,2},{8,12},{10,14},{12,4},{14,6},{1,9},{3,11}... | collective-permute-start | bytes 589832 | tf_op jit(solution)/shard_map/ppermute | solution.py:35
  11.4 11.6 %collective-permute-start.4 = (bf16[64,1536]{1,0:T(8,128)(2,1)S(1)}, bf16[64,1536]{1,0:T(8,128)(2,1)S(1)}, u32[]{:S(2)}, u32[]{:S(2)}) collective-permute-start(bf16[64,1536]{1,0:T(8,128)(2,1)S(1)} %get-tuple-element.26.refs_4_.refs_8_), channel_id=1, source_target_pairs={{0,4},{2,6},{4,12},{6,14},{8,0},{10,2},{12,8},{14,10},{1,5},{3,7},... | collective-permute-start | bytes 589832 | tf_op jit(solution)/shard_map/ppermute | solution.py:35
  14.0 10.3 %collective-permute-start.7 = (bf16[64,1536]{1,0:T(8,128)(2,1)S(1)}, bf16[64,1536]{1,0:T(8,128)(2,1)S(1)}, u32[]{:S(2)}, u32[]{:S(2)}) collective-permute-start(bf16[64,1536]{1,0:T(8,128)(2,1)S(1)} %bitcast.9), channel_id=1, source_target_pairs={{0,2},{2,0},{4,6},{6,4},{8,10},{10,8},{12,14},{14,12},{1,3},{3,1},... | collective-permute-start | bytes 589832 | tf_op jit(solution)/shard_map/ppermute | solution.py:25
  15.6 11.3 %collective-permute-start.8 = (bf16[64,1536]{1,0:T(8,128)(2,1)S(1)}, bf16[64,1536]{1,0:T(8,128)(2,1)S(1)}, u32[]{:S(2)}, u32[]{:S(2)}) collective-permute-start(bf16[64,1536]{1,0:T(8,128)(2,1)S(1)} %get-tuple-element.26.refs_4_.refs_8_), channel_id=1, source_target_pairs={{0,16},{1,3},{2,18},{3,1},{4,20},{5,7},{6,22},{7,5},{8,24},{9,11},... | collective-permute-start | bytes 589832 | tf_op jit(solution)/shard_map/ppermute | solution.py:45
  17.1 9.8 %collective-permute-start.5 = (bf16[64,1536]{1,0:T(8,128)(2,1)S(1)}, bf16[64,1536]{1,0:T(8,128)(2,1)S(1)}, u32[]{:S(2)}, u32[]{:S(2)}) collective-permute-start(bf16[64,1536]{1,0:T(8,128)(2,1)S(1)} %get-tuple-element.26.refs_4_.refs_8_), channel_id=1, source_target_pairs={{0,2},{1,17},{2,0},{3,19},{4,6},{5,21},{6,4},{7,23},{8,10},{9,25},... | collective-permute-start | bytes 589832 | tf_op jit(solution)/shard_map/ppermute | solution.py:45
  19.4 9.8 %collective-permute-start.10 = (bf16[64,1536]{1,0:T(8,128)(2,1)S(1)}, bf16[64,1536]{1,0:T(8,128)(2,1)S(1)}, u32[]{:S(2)}, u32[]{:S(2)}) collective-permute-start(bf16[64,1536]{1,0:T(8,128)(2,1)S(1)} %get-tuple-element.30.refs_5_.refs_9_), channel_id=1, source_target_pairs={{0,16},{1,3},{2,18},{3,1},{4,20},{5,7},{6,22},{7,5},{8,24},{9,11},... | collective-permute-start | bytes 589832 | tf_op jit(solution)/shard_map/ppermute | solution.py:45
  23.0 7.8 %collective-permute-start.6 = (bf16[64,1536]{1,0:T(8,128)(2,1)S(1)}, bf16[64,1536]{1,0:T(8,128)(2,1)S(1)}, u32[]{:S(2)}, u32[]{:S(2)}) collective-permute-start(bf16[64,1536]{1,0:T(8,128)(2,1)S(1)} %get-tuple-element.30.refs_5_.refs_9_), channel_id=1, source_target_pairs={{0,2},{1,17},{2,0},{3,19},{4,6},{5,21},{6,4},{7,23},{8,10},{9,25},... | collective-permute-start | bytes 589832 | tf_op jit(solution)/shard_map/ppermute | solution.py:45
  24.3 7.5 %collective-permute-start.11 = (bf16[64,1536]{1,0:T(8,128)(2,1)S(1)}, bf16[64,1536]{1,0:T(8,128)(2,1)S(1)}, u32[]{:S(2)}, u32[]{:S(2)}) collective-permute-start(bf16[64,1536]{1,0:T(8,128)(2,1)S(1)} %get-tuple-element.32.refs_6_.refs_10_), channel_id=1, source_target_pairs={{0,16},{1,3},{2,18},{3,1},{4,20},{5,7},{6,22},{7,5},{8,24},{9,11},... | collective-permute-start | bytes 589832 | tf_op jit(solution)/shard_map/ppermute | solution.py:45
  26.9 9.9 %collective-permute-start.12 = (bf16[64,1536]{1,0:T(8,128)(2,1)S(1)}, bf16[64,1536]{1,0:T(8,128)(2,1)S(1)}, u32[]{:S(2)}, u32[]{:S(2)}) collective-permute-start(bf16[64,1536]{1,0:T(8,128)(2,1)S(1)} %get-tuple-element.35), channel_id=1, source_target_pairs={{0,16},{1,3},{2,18},{3,1},{4,20},{5,7},{6,22},{7,5},{8,24},{9,11},... | collective-permute-start | bytes 589832 | tf_op jit(solution)/shard_map/ppermute | solution.py:45
  27.7 7.9 %collective-permute-start.9 = (bf16[64,1536]{1,0:T(8,128)(2,1)S(1)}, bf16[64,1536]{1,0:T(8,128)(2,1)S(1)}, u32[]{:S(2)}, u32[]{:S(2)}) collective-permute-start(bf16[64,1536]{1,0:T(8,128)(2,1)S(1)} %get-tuple-element.35), channel_id=1, source_target_pairs={{0,4},{2,6},{4,12},{6,14},{8,0},{10,2},{12,8},{14,10},{1,5},{3,7},... | collective-permute-start | bytes 589832 | tf_op jit(solution)/shard_map/ppermute | solution.py:35
  30.8 6.0 %collective-permute-start.13 = (bf16[64,1536]{1,0:T(8,128)(2,1)S(1)}, bf16[64,1536]{1,0:T(8,128)(2,1)S(1)}, u32[]{:S(2)}, u32[]{:S(2)}) collective-permute-start(bf16[64,1536]{1,0:T(8,128)(2,1)S(1)} %get-tuple-element.42), channel_id=1, source_target_pairs={{0,2},{1,17},{2,0},{3,19},{4,6},{5,21},{6,4},{7,23},{8,10},{9,25},... | collective-permute-start | bytes 589832 | tf_op jit(solution)/shard_map/ppermute | solution.py:45
  31.9 6.8 %collective-permute-start.14 = (bf16[64,1536]{1,0:T(8,128)(2,1)S(1)}, bf16[64,1536]{1,0:T(8,128)(2,1)S(1)}, u32[]{:S(2)}, u32[]{:S(2)}) collective-permute-start(bf16[64,1536]{1,0:T(8,128)(2,1)S(1)} %get-tuple-element.43), channel_id=1, source_target_pairs={{0,2},{1,17},{2,0},{3,19},{4,6},{5,21},{6,4},{7,23},{8,10},{9,25},... | collective-permute-start | bytes 589832 | tf_op jit(solution)/shard_map/ppermute | solution.py:45
  33.0 2.6 %copy-start.3 = (bf16[1,1536,64]{1,2,0:T(8,128)(2,1)S(1)}, bf16[1,1536,64]{1,2,0:T(8,128)(2,1)}, u32[]{:S(2)}) copy-start(bf16[1,1536,64]{1,2,0:T(8,128)(2,1)} %param.8) | copy-start | bytes 589828
  33.0 2.6 %copy-start.5 = (s32[512,1]{0,1:T(1,128)S(1)}, s32[512,1]{0,1:T(1,128)}, u32[]{:S(2)}) copy-start(s32[512,1]{0,1:T(1,128)} %param.6) | copy-start | bytes 6148
  38.7 1.6 %collective-permute-start.15 = (f32[512,128]{1,0:T(8,128)S(1)}, f32[512,128]{1,0:T(8,128)S(1)}, u32[]{:S(2)}, u32[]{:S(2)}) collective-permute-start(f32[512,128]{1,0:T(8,128)S(1)} %shard_map.67.refs_1_), channel_id=1, source_target_pairs={{0,1},{1,0},{2,3},{3,2},{4,5},{5,4},{6,7},{7,6},{8,9},{9,8},{10,11... | collective-permute-start | bytes 786440 | tf_op jit(solution)/shard_map/ppermute | solution.py:21
